TPU v7x, 32 devices: a whole 2x2x4 slice. The times are simulated.
32 devices in a mesh: ctx: 4 (over y, core), fsdp: 8 (over z, x).
Axes of the slice: x: 2, y: 2, z: 4, core: 2. Of those that a mesh axis runs over, the one named last changes fastest.
Arguments:
- tokens: bfloat16 [1024, 6144], P(('ctx', 'fsdp')), may hold values from -6 to 6
- qkv_weight: bfloat16 [3, 6144, 4096], P(None, None, 'fsdp'), may hold values from -0.078125 to 0.078125
- out_weight: bfloat16 [4096, 6144], P('fsdp'), may hold values from -0.09375 to 0.09375
- norm_gain: float32 [4096], P('fsdp'), may hold values from 0.1 to 1.9
- initial_state: float32 [32, 128, 128], P('fsdp'), may hold values from -2400 to 2400
Outputs:
- mixed: bfloat16 [1024, 6144], P(('ctx', 'fsdp'))
All inputs are finite; a program needn't handle non-finite values.
Results may differ from a plain program's by a relative error of at most 0.013.
Values may be sent and summed in bfloat16 or wider, within the bound.
No kernel may reach another device: no remote copies, remote signals or barrier semaphores. Data moves between devices by JAX's collectives and lax.ppermute only.
A program may use at most 128 MiB of HBM per device.

v0:
```python
import jax
import jax.numpy as jnp
from jax import lax
from jax.sharding import PartitionSpec as P


def carried_in(value, axis, join, neutral):
    place = lax.axis_index(axis)
    gathered = lax.all_gather(value.astype(jnp.bfloat16), axis)
    state = jnp.zeros_like(value) + jnp.asarray(neutral, value.dtype)

    def one(turn, state):
        return join(state, lax.dynamic_index_in_dim(gathered, turn, 0, False).astype(value.dtype))

    return lax.fori_loop(0, place, one, state)


def feature_map(projected):
    return jax.nn.elu(projected) + 1.0


def add_states(earlier, later):
    return earlier + later


def per_device(tokens, qkv_weight, out_weight, norm_gain, initial_state):
    heads_here = initial_state.shape[0]
    head_dim = initial_state.shape[1]
    projected = jnp.einsum(
        "td,sdc->tsc",
        lax.all_gather(tokens, "fsdp", axis=0, tiled=True),
        qkv_weight,
        preferred_element_type=jnp.float32,
    )
    stacked = jnp.stack(
        [feature_map(projected[:, 0]), feature_map(projected[:, 1]), projected[:, 2]], axis=1
    )
    features = stacked.astype(jnp.bfloat16)
    block_len = features.shape[0]
    feat_q = features[:, 0].reshape(block_len, heads_here, head_dim)
    feat_k = features[:, 1].reshape(block_len, heads_here, head_dim)
    values = features[:, 2].reshape(block_len, heads_here, head_dim)
    block_state = jnp.einsum("thd,the->hde", feat_k, values, preferred_element_type=jnp.float32)
    empty = jnp.zeros_like(block_state)
    earlier = carried_in(block_state, "ctx", add_states, empty)
    prefix = initial_state + earlier
    causal = jnp.arange(block_len)[:, None] >= jnp.arange(block_len)[None, :]
    scores = jnp.einsum("ihd,jhd->hij", feat_q, feat_k, preferred_element_type=jnp.float32)
    scores = jnp.where(causal[None], scores, 0.0).astype(jnp.bfloat16)
    within = jnp.einsum("hij,jhd->ihd", scores, values, preferred_element_type=jnp.float32)
    carried = jnp.einsum(
        "ihd,hde->ihe", feat_q.astype(jnp.float32), prefix, precision=lax.Precision.HIGHEST
    )
    attended = within + carried
    scale = lax.rsqrt(jnp.mean(attended * attended, axis=-1, keepdims=True) + 1e-06)
    gain_heads = norm_gain.reshape(heads_here, head_dim)
    normalized = (attended * scale * gain_heads[None]).astype(jnp.bfloat16)
    normalized = normalized.reshape(block_len, heads_here * head_dim)
    return lax.psum_scatter(
        jnp.dot(normalized, out_weight, preferred_element_type=jnp.float32).astype(jnp.bfloat16),
        "fsdp",
        scatter_dimension=0,
        tiled=True,
    )


def solution(mesh):
    placed = (
        P(("ctx", "fsdp"), None),
        P(None, None, "fsdp"),
        P("fsdp", None),
        P("fsdp"),
        P("fsdp", None, None),
    )
    return jax.shard_map(
        per_device, mesh=mesh, in_specs=placed, out_specs=P(("ctx", "fsdp"), None), check_vma=False
    )
```

profile of v0, /device:TPU:0, one launch (start us, length us, event | category | flops | bytes accessed | tf_op | source)
XLA Modules:
  0.0 178.2 jit_solution(12880907943008234919)
XLA Ops:
  6.5 0.0 all-gather.3.cloned.1.call-start
  6.5 0.7 all-gather.3.cloned.1.call-update
  7.3 0.0 reduce-scatter.2.cloned.1.call-start
  7.3 65.4 %all-gather.3.cloned.1.call-done = bf16[256,6144]{1,0:T(8,128)(2,1)} async-done(((bf16[32,6144]{1,0:T(8,128)(2,1)}), bf16[256,6144]{1,0:T(8,128)(2,1)}) %all-gather.3.cloned.1.call-update) | async-done | bytes 3145744 | tf_op jit(solution)/shard_map/all_gather | solution.py:31
  72.7 9.9 %fusion = f32[256,3,512]{2,0,1:T(8,128)S(1)} fusion(bf16[3,6144,512]{2,1,0:T(8,128)(2,1)} %param.8, bf16[256,6144]{1,0:T(8,128)(2,1)} %all-gather.3.cloned.1.call-done), kind=kOutput, calls=%fused_computation.2 | convolution fusion | flops 4831838208 | bytes 23592960 | tf_op jit(solution)/shard_map/td,sdc->tsc/dot_general | solution.py:29
  82.6 0.0 copy-start
  82.6 0.0 copy-start.1
  82.6 0.4 fusion.8
  83.1 0.1 copy.17
  83.3 0.1 reshape_squeeze.9
  83.3 0.2 convolution_convert_fusion.1
  83.6 7.2 %all-gather = bf16[16,128,128]{2,1,0:T(8,128)(2,1)S(1)} all-gather(bf16[4,128,128]{2,1,0:T(8,128)(2,1)S(1)} %convolution_convert_fusion.1), channel_id=2, replica_groups=mesh['ctx'=4,'fsdp'=8] {'ctx'}, dimensions={0}, use_global_device_ids=true | all-gather | bytes 655360 | tf_op jit(solution)/shard_map/all_gather | solution.py:9
  90.7 0.1 reshape_squeeze.10
  90.8 0.0 copy-done
  90.8 0.4 fusion.14
  91.2 0.5 multiply_reduce_fusion
  91.7 0.0 copy-done.1
  91.8 0.1 multiply_convert_fusion
  91.9 6.3 %convolution_convert_fusion = bf16[256,6144]{1,0:T(8,128)(2,1)} fusion(bf16[256,512]{0,1:T(8,128)(2,1)S(1)} %bitcast.24, bf16[512,6144]{1,0:T(8,128)(2,1)} %param.9), kind=kOutput, calls=%fused_computation.1 | convolution fusion | flops 1612185600 | bytes 9699328 | tf_op jit(solution)/shard_map/dot_general | solution.py:60
  98.2 0.0 reduce-scatter.2.cloned.1.call-update
  98.2 73.2 %reduce-scatter.2.cloned.1.call-done = bf16[32,6144]{1,0:T(8,128)(2,1)} async-done(((bf16[256,6144]{1,0:T(8,128)(2,1)}), bf16[32,6144]{1,0:T(8,128)(2,1)}) %reduce-scatter.2.cloned.1.call-update) | async-done | bytes 393232 | tf_op jit(solution)/shard_map/reduce_scatter | solution.py:59
  (5 shorter events, 0.1 us)
Async XLA Ops:
  6.5 66.2 %all-gather.3.cloned.1.call-start = ((), (), s32[]{:S(2)}) async-start(), calls=%async_computation.1 | async-start | bytes 3538944 | tf_op jit(solution)/shard_map/all_gather | solution.py:31
  7.3 164.1 %reduce-scatter.2.cloned.1.call-start = ((), (), s32[]{:S(2)}) async-start(), calls=%async_computation.2 | async-start | bytes 3538944 | tf_op jit(solution)/shard_map/reduce_scatter | solution.py:59
  82.6 8.2 %copy-start = (f32[4,128,128]{2,1,0:T(8,128)S(1)}, f32[4,128,128]{2,1,0:T(8,128)}, u32[]{:S(2)}) copy-start(f32[4,128,128]{2,1,0:T(8,128)} %param.11) | copy-start | bytes 786436
  82.6 9.1 %copy-start.1 = (f32[512]{0:T(512)S(1)}, f32[512]{0:T(512)}, u32[]{:S(2)}) copy-start(f32[512]{0:T(512)} %param.10) | copy-start | bytes 6148
Sparse Core Ops, SparseCore 0:
  9.5 63.1 all-gather.2
  98.3 73.0 reduce-scatter.1
where the time goes:
time: 178 us
  waiting for transfers between devices  139 us (78%)
  matrix products  17.3 us (10%)
  between operations  13.5 us (8%)
  blocking collectives  7.15 us (4%)
    reduce_scatter x1, waiting for transfers between devices, per_device(): lax.psum_scatter(jnp.dot(normalized, out_weight, preferred_element_type=j...  73.2 us
    all_gather x1, waiting for transfers between devices, per_device(): lax.all_gather(tokens, 'fsdp', axis=0, tiled=True)  65.4 us
    dot_general x1, matrix products, per_device(): jnp.einsum('td,sdc->tsc', lax.all_gather(tokens, 'fsdp', axis=0, tiled=Tr...  9.88 us
    all_gather x1, blocking collectives, carried_in(): gathered = lax.all_gather(value.astype(jnp.bfloat16), axis)  7.15 us
    dot_general x1, matrix products, per_device(): jnp.dot(normalized, out_weight, preferred_element_type=jnp.float32)  6.27 us
  transfers between devices with their start and end apart: 2, of which 2 were waited for; matrix products, arithmetic and copies ran while one was open for 0% of the time, Pallas kernels for 0%

commit v1 on v0

v1 whole, which is shorter than its diff:
```python
import jax
import jax.numpy as jnp
from jax import lax
from jax.sharding import PartitionSpec as P


def ring_order(size):
    if size % 2:
        return list(range(size))
    return list(range(0, size, 2)) + list(range(size - 1, 0, -2))


def neighbours(size):
    ring = ring_order(size)
    right = [(ring[i], ring[(i + 1) % size]) for i in range(size)]
    left = [(b, a) for a, b in right]
    return right, left


def slots(size):
    far = size // 2
    order = [0]
    for step in range(1, far):
        order += [-step, step]
    return order + [far]


def ring_gather(block, size, right, left):
    half = block.shape[1] // 2
    own = [block[:, :half], block[:, half:]]
    going_right, going_left = list(own), list(own)
    held = [own]
    for _ in range(size // 2 - 1):
        for part in range(2):
            going_right[part] = lax.ppermute(going_right[part], "fsdp", right)
            going_left[part] = lax.ppermute(going_left[part], "fsdp", left)
        held.append(list(going_right))
        held.append(list(going_left))
    held.append([lax.ppermute(going_right[0], "fsdp", right), lax.ppermute(going_left[1], "fsdp", left)])
    return held


def add(a, b):
    return (a.astype(jnp.float32) + b.astype(jnp.float32)).astype(jnp.bfloat16)


def ring_scatter(part_of, size, right, left):
    far = size // 2
    to_right = [lax.ppermute(part_of(far, 0), "fsdp", right), None]
    to_left = [None, lax.ppermute(part_of(far, 1), "fsdp", left)]
    for step in range(far - 1, 0, -1):
        for half in range(2):
            mine = part_of(step, half)
            got = to_right[half]
            to_right[half] = lax.ppermute(mine if got is None else add(mine, got), "fsdp", right)
            mine = part_of(-step, half)
            got = to_left[half]
            to_left[half] = lax.ppermute(mine if got is None else add(mine, got), "fsdp", left)
    done = []
    for half in range(2):
        total = part_of(0, half).astype(jnp.float32)
        for got in (to_right[half], to_left[half]):
            if got is not None:
                total = total + got.astype(jnp.float32)
        done.append(total.astype(jnp.bfloat16))
    return jnp.concatenate(done, axis=1)


def earlier_states(state, size):
    place = lax.axis_index("ctx")
    before = jnp.zeros_like(state)
    total = state
    reach = 1
    while reach < size:
        pairs = [(i, i ^ reach) for i in range(size)]
        other = lax.ppermute(total.astype(jnp.bfloat16), "ctx", pairs).astype(jnp.float32)
        before = before + jnp.where((place & reach) != 0, other, 0.0)
        total = total + other
        reach *= 2
    return before


def feature_map(projected):
    return jax.nn.elu(projected) + 1.0


def per_device(n_ctx, n_fsdp, tokens, qkv_weight, out_weight, norm_gain, initial_state):
    rows = tokens.shape[0]
    heads_here, head_dim = initial_state.shape[:2]
    right, left = neighbours(n_fsdp)
    order = slots(n_fsdp)
    ring = jnp.asarray(ring_order(n_fsdp), jnp.int32)
    spot = jnp.argmax(ring == lax.axis_index("fsdp"))
    held_by = ring[(spot + jnp.asarray(order, jnp.int32)) % n_fsdp]
    position = (held_by[:, None] * rows + jnp.arange(rows)[None, :]).reshape(-1)

    held = ring_gather(tokens, n_fsdp, right, left)
    gathered = jnp.concatenate([jnp.concatenate(pair, axis=1) for pair in held], axis=0)
    projected = jnp.einsum("td,sdc->stc", gathered, qkv_weight, preferred_element_type=jnp.float32)
    block_len = gathered.shape[0]
    shaped = (block_len, heads_here, head_dim)
    feat_q = feature_map(projected[0]).astype(jnp.bfloat16).reshape(shaped)
    feat_k = feature_map(projected[1]).astype(jnp.bfloat16).reshape(shaped)
    values = projected[2].astype(jnp.bfloat16).reshape(shaped)
    block_state = jnp.einsum("thd,the->hde", feat_k, values, preferred_element_type=jnp.float32)
    prefix = initial_state + earlier_states(block_state, n_ctx)
    causal = position[:, None] >= position[None, :]
    scores = jnp.einsum("ihd,jhd->hij", feat_q, feat_k, preferred_element_type=jnp.float32)
    scores = jnp.where(causal[None], scores, 0.0).astype(jnp.bfloat16)
    within = jnp.einsum("hij,jhd->ihd", scores, values, preferred_element_type=jnp.float32)
    carried = jnp.einsum(
        "ihd,hde->ihe", feat_q.astype(jnp.float32), prefix, precision=lax.Precision.HIGHEST
    )
    attended = within + carried
    scale = lax.rsqrt(jnp.mean(attended * attended, axis=-1, keepdims=True) + 1e-06)
    gain_heads = norm_gain.reshape(heads_here, head_dim)
    normalized = (attended * scale * gain_heads[None]).astype(jnp.bfloat16)
    normalized = normalized.reshape(block_len, heads_here * head_dim)
    partial = jnp.dot(normalized, out_weight, preferred_element_type=jnp.float32).astype(jnp.bfloat16)
    half = partial.shape[1] // 2

    def part_of(distance, which):
        place = order.index(distance)
        return partial[place * rows : (place + 1) * rows, which * half : (which + 1) * half]

    return ring_scatter(part_of, n_fsdp, right, left)


def solution(mesh):
    n_ctx, n_fsdp = mesh.shape["ctx"], mesh.shape["fsdp"]

    def body(*args):
        return per_device(n_ctx, n_fsdp, *args)

    placed = (
        P(("ctx", "fsdp"), None),
        P(None, None, "fsdp"),
        P("fsdp", None),
        P("fsdp"),
        P("fsdp", None, None),
    )
    return jax.shard_map(
        body, mesh=mesh, in_specs=placed, out_specs=P(("ctx", "fsdp"), None), check_vma=False
    )
```

time: 178 us -> 118 us (0.66)
  waiting for transfers between devices: 139 us -> 52.9 us
  starting transfers between devices: 0.04 us -> 33.4 us
  between operations: 13.5 us -> 0.21 us
  other arithmetic: 0.6 us -> 9.83 us
  blocking collectives: 7.15 us -> 0 us
  local copies, waits for them, and re-layouts: 0.33 us -> 4.79 us
    reduce_scatter x1 -> x0, waiting for transfers between devices: 73.2 us -> none  [per_device(): lax.psum_scatter(jnp.dot(normalized, out_weight, preferred_element_type=j...]
    all_gather x1 -> x0, waiting for transfers between devices: 65.4 us -> none  [per_device(): lax.all_gather(tokens, 'fsdp', axis=0, tiled=True)]
    ppermute x0 -> x30, waiting for transfers between devices: none -> 52.9 us  [the longest x6 17.6 us: ring_scatter(): lax.ppermute(mine if got is None else add(mine, got), 'fsdp', left)]
    ppermute x0 -> x30, starting transfers between devices: none -> 33.4 us  [the longest x6 12.8 us: ring_gather(): going_right[part] = lax.ppermute(going_right[part], 'fsdp', right)]
    all_gather x1 -> x0, blocking collectives: 7.15 us -> none  [carried_in(): gathered = lax.all_gather(value.astype(jnp.bfloat16), axis)]
    unnamed x0 -> x6, other arithmetic: none -> 4.7 us
  transfers between devices with their start and end apart: 2 -> 30, of which waited for: 2 -> 17; matrix products, arithmetic and copies ran while one was open for 0% -> 10% of each run, Pallas kernels for 0% -> 0%
where the time goes in v1:
time: 118 us; the launch traced here: 117 us
  waiting for transfers between devices  52.9 us (45%)
  starting transfers between devices  33.4 us (28%)
  matrix products  16.3 us (14%)
  other arithmetic  9.83 us (8%)
  local copies, waits for them, and re-layouts  4.79 us (4%)
    ppermute x6, waiting for transfers between devices, ring_scatter(): lax.ppermute(mine if got is None else add(mine, got), 'fsdp', left)  17.6 us
    ppermute x6, waiting for transfers between devices, ring_scatter(): lax.ppermute(mine if got is None else add(mine, got), 'fsdp', right)  13.1 us
    ppermute x6, starting transfers between devices, ring_gather(): going_right[part] = lax.ppermute(going_right[part], 'fsdp', right)  12.8 us
    ppermute x6, starting transfers between devices, ring_scatter(): lax.ppermute(mine if got is None else add(mine, got), 'fsdp', right)  10.1 us
    dot_general x1, matrix products, per_device(): jnp.einsum('td,sdc->stc', gathered, qkv_weight, preferred_element_type=jn...  9.89 us
    ppermute x6, waiting for transfers between devices, ring_gather(): going_left[part] = lax.ppermute(going_left[part], 'fsdp', left)  5.62 us
    unnamed x6, other arithmetic  4.7 us
    dot_general x1, matrix products, per_device(): jnp.dot(normalized, out_weight, preferred_element_type=jnp.float32)  4.61 us
  transfers between devices with their start and end apart: 30, of which 17 were waited for; matrix products, arithmetic and copies ran while one was open for 10% of the time, Pallas kernels for 0%

profile of v1, /device:TPU:0, one launch (start us, length us, event | category | flops | bytes accessed | tf_op | source)
XLA Modules:
  0.0 117.4 jit_solution(2605697116617320221)
XLA Ops:
  0.0 1.0 fusion.39
  1.1 3.1 %collective-permute-start = (bf16[32,3072]{1,0:T(8,128)(2,1)S(1)}, bf16[32,3072]{1,0:T(8,128)(2,1)S(1)}, u32[]{:S(2)}, u32[]{:S(2)}) collective-permute-start(bf16[32,3072]{1,0:T(8,128)(2,1)S(1)} %get-tuple-element.20), channel_id=1, source_target_pairs={{0,2},{2,4},{4,6},{6,7},{7,5},{5,3},{3,1},{1,0},{8,10},{10,12},{12... | collective-permute-start | bytes 589832 | tf_op jit(solution)/shard_map/ppermute | solution.py:35
  4.1 2.0 %collective-permute-start.1 = (bf16[32,3072]{1,0:T(8,128)(2,1)S(1)}, bf16[32,3072]{1,0:T(8,128)(2,1)S(1)}, u32[]{:S(2)}, u32[]{:S(2)}) collective-permute-start(bf16[32,3072]{1,0:T(8,128)(2,1)S(1)} %get-tuple-element.21), channel_id=1, source_target_pairs={{0,2},{2,4},{4,6},{6,7},{7,5},{5,3},{3,1},{1,0},{8,10},{10,12},{12... | collective-permute-start | bytes 589832 | tf_op jit(solution)/shard_map/ppermute | solution.py:35
  6.2 1.8 %constant_dynamic-update-slice_fusion = bf16[256,6144]{1,0:T(8,128)(2,1)} fusion(bf16[32,6144]{1,0:T(8,128)(2,1)} %param.7), kind=kLoop, calls=%fused_computation.59 | loop fusion | bytes 786432
  7.9 1.3 %compare_reduce_fusion = (pred[]{:T(512)}, s32[]{:T(128)}) fusion(s32[8]{0:T(128)} %constant.56.clone, s32[]{:T(128)S(6)} %axis_index.22), kind=kLoop, calls=%fused_computation.67 | loop fusion | flops 57 | bytes 41 | tf_op jit(solution)/shard_map/per_device/reduce | solution.py:93
  9.2 1.3 %compare_select_fusion.4 = s32[8]{0:T(128)S(1)} fusion(s32[8]{0:T(128)} %constant.57.clone, s32[]{:T(128)} %get-tuple-element.6), kind=kLoop, calls=%fused_computation.63 | loop fusion | flops 120 | bytes 68 | tf_op jit(solution)/shard_map/select_n | solution.py:94
  10.5 1.3 %gather_fusion = s32[8]{0:T(128)S(1)} fusion(s32[8]{0:T(128)} %constant.56.clone, s32[1024]{0:T(1024)S(1)} %pad_clamp_fusion), kind=kCustom, calls=%fused_computation | custom fusion | bytes 96 | tf_op jit(solution)/shard_map/gather | solution.py:94
  12.0 2.0 %collective-permute-start.4 = (bf16[32,3072]{1,0:T(8,128)(2,1)S(1)}, bf16[32,3072]{1,0:T(8,128)(2,1)S(1)}, u32[]{:S(2)}, u32[]{:S(2)}) collective-permute-start(bf16[32,3072]{1,0:T(8,128)(2,1)S(1)} %collective-permute-done), channel_id=1, source_target_pairs={{0,2},{2,4},{4,6},{6,7},{7,5},{5,3},{3,1},{1,0},{8,10},{10,12},{12... | collective-permute-start | bytes 589832 | tf_op jit(solution)/shard_map/ppermute | solution.py:35
  14.0 1.6 %collective-permute-start.5 = (bf16[32,3072]{1,0:T(8,128)(2,1)S(1)}, bf16[32,3072]{1,0:T(8,128)(2,1)S(1)}, u32[]{:S(2)}, u32[]{:S(2)}) collective-permute-start(bf16[32,3072]{1,0:T(8,128)(2,1)S(1)} %collective-permute-done.1), channel_id=1, source_target_pairs={{0,2},{2,4},{4,6},{6,7},{7,5},{5,3},{3,1},{1,0},{8,10},{10,12},{12... | collective-permute-start | bytes 589832 | tf_op jit(solution)/shard_map/ppermute | solution.py:35
  16.8 0.9 collective-permute-start.7
  17.7 0.8 maximum_dynamic-update-slice_fusion.5
  18.5 1.4 %collective-permute-done.4 = bf16[32,3072]{1,0:T(8,128)(2,1)S(1)} collective-permute-done((bf16[32,3072]{1,0:T(8,128)(2,1)S(1)}, bf16[32,3072]{1,0:T(8,128)(2,1)S(1)}, u32[]{:S(2)}, u32[]{:S(2)}) %collective-permute-start.4) | collective-permute-done | bytes 196640 | tf_op jit(solution)/shard_map/ppermute | solution.py:35
  19.9 2.0 %collective-permute-start.8 = (bf16[32,3072]{1,0:T(8,128)(2,1)S(1)}, bf16[32,3072]{1,0:T(8,128)(2,1)S(1)}, u32[]{:S(2)}, u32[]{:S(2)}) collective-permute-start(bf16[32,3072]{1,0:T(8,128)(2,1)S(1)} %collective-permute-done.4), channel_id=1, source_target_pairs={{0,2},{2,4},{4,6},{6,7},{7,5},{5,3},{3,1},{1,0},{8,10},{10,12},{12... | collective-permute-start | bytes 589832 | tf_op jit(solution)/shard_map/ppermute | solution.py:35
  21.9 2.2 %collective-permute-done.5 = bf16[32,3072]{1,0:T(8,128)(2,1)S(1)} collective-permute-done((bf16[32,3072]{1,0:T(8,128)(2,1)S(1)}, bf16[32,3072]{1,0:T(8,128)(2,1)S(1)}, u32[]{:S(2)}, u32[]{:S(2)}) %collective-permute-start.5) | collective-permute-done | bytes 196640 | tf_op jit(solution)/shard_map/ppermute | solution.py:35
  24.1 2.0 %collective-permute-start.9 = (bf16[32,3072]{1,0:T(8,128)(2,1)S(1)}, bf16[32,3072]{1,0:T(8,128)(2,1)S(1)}, u32[]{:S(2)}, u32[]{:S(2)}) collective-permute-start(bf16[32,3072]{1,0:T(8,128)(2,1)S(1)} %collective-permute-done.5), channel_id=1, source_target_pairs={{0,2},{2,4},{4,6},{6,7},{7,5},{5,3},{3,1},{1,0},{8,10},{10,12},{12... | collective-permute-start | bytes 589832 | tf_op jit(solution)/shard_map/ppermute | solution.py:35
  26.1 0.8 maximum_dynamic-update-slice_fusion.4
  26.9 1.9 %collective-permute-start.10 = (bf16[32,3072]{1,0:T(8,128)(2,1)S(1)}, bf16[32,3072]{1,0:T(8,128)(2,1)S(1)}, u32[]{:S(2)}, u32[]{:S(2)}) collective-permute-start(bf16[32,3072]{1,0:T(8,128)(2,1)S(1)} %collective-permute-done.6), channel_id=1, source_target_pairs={{2,0},{4,2},{6,4},{7,6},{5,7},{3,5},{1,3},{0,1},{10,8},{12,10},{14... | collective-permute-start | bytes 589832 | tf_op jit(solution)/shard_map/ppermute | solution.py:36
  28.8 0.8 maximum_dynamic-update-slice_fusion.3
  30.3 4.3 %collective-permute-done.11 = bf16[32,3072]{1,0:T(8,128)(2,1)S(1)} collective-permute-done((bf16[32,3072]{1,0:T(8,128)(2,1)S(1)}, bf16[32,3072]{1,0:T(8,128)(2,1)S(1)}, u32[]{:S(2)}, u32[]{:S(2)}) %collective-permute-start.11) | collective-permute-done | bytes 196640 | tf_op jit(solution)/shard_map/ppermute | solution.py:36
  34.6 0.8 maximum_dynamic-update-slice_fusion.2
  35.4 1.3 %collective-permute-done.10 = bf16[32,3072]{1,0:T(8,128)(2,1)S(1)} collective-permute-done((bf16[32,3072]{1,0:T(8,128)(2,1)S(1)}, bf16[32,3072]{1,0:T(8,128)(2,1)S(1)}, u32[]{:S(2)}, u32[]{:S(2)}) %collective-permute-start.10) | collective-permute-done | bytes 196640 | tf_op jit(solution)/shard_map/ppermute | solution.py:36
  36.7 0.8 maximum_dynamic-update-slice_fusion.1
  37.5 2.8 %collective-permute-done.13 = bf16[32,3072]{1,0:T(8,128)(2,1)S(1)} collective-permute-done((bf16[32,3072]{1,0:T(8,128)(2,1)S(1)}, bf16[32,3072]{1,0:T(8,128)(2,1)S(1)}, u32[]{:S(2)}, u32[]{:S(2)}) %collective-permute-start.13) | collective-permute-done | bytes 196640 | tf_op jit(solution)/shard_map/ppermute | solution.py:39
  40.3 0.8 maximum_dynamic-update-slice_fusion
  41.0 9.9 %fusion.2 = f32[3,256,512]{2,1,0:T(8,128)S(1)} fusion(bf16[3,6144,512]{2,1,0:T(8,128)(2,1)} %param.8, bf16[256,6144]{1,0:T(8,128)(2,1)} %maximum_dynamic-update-slice_fusion), kind=kOutput, calls=%fused_computation.8 | convolution fusion | flops 4831838208 | bytes 23592960 | tf_op jit(solution)/shard_map/td,sdc->stc/dot_general | solution.py:99
  52.1 1.0 collective-permute-done.14
  53.2 1.6 %collective-permute-start.15 = (bf16[4,128,128]{2,1,0:T(8,128)(2,1)S(1)}, bf16[4,128,128]{2,1,0:T(8,128)(2,1)S(1)}, u32[]{:S(2)}, u32[]{:S(2)}) collective-permute-start(bf16[4,128,128]{2,1,0:T(8,128)(2,1)S(1)} %fusion.19), channel_id=1, source_target_pairs={{0,16},{8,24},{16,0},{24,8},{1,17},{9,25},{17,1},{25,9},{2,18},{10... | collective-permute-start | bytes 393224 | tf_op jit(solution)/shard_map/ppermute | solution.py:76
  55.5 3.3 %collective-permute-done.15 = bf16[4,128,128]{2,1,0:T(8,128)(2,1)S(1)} collective-permute-done((bf16[4,128,128]{2,1,0:T(8,128)(2,1)S(1)}, bf16[4,128,128]{2,1,0:T(8,128)(2,1)S(1)}, u32[]{:S(2)}, u32[]{:S(2)}) %collective-permute-start.15) | collective-permute-done | bytes 131104 | tf_op jit(solution)/shard_map/ppermute | solution.py:76
  59.6 4.6 %convolution_convert_fusion = bf16[256,6144]{1,0:T(8,128)(2,1)S(1)} fusion(bf16[256,512]{0,1:T(8,128)(2,1)S(1)} %bitcast.14, bf16[512,6144]{1,0:T(8,128)(2,1)} %param.9), kind=kOutput, calls=%fused_computation.1 | convolution fusion | flops 1612185600 | bytes 9699328 | tf_op jit(solution)/shard_map/dot_general | solution.py:119
  64.3 1.6 %collective-permute-start.16 = (bf16[32,3072]{1,0:T(8,128)(2,1)S(1)}, bf16[32,3072]{1,0:T(8,128)(2,1)S(1)}, u32[]{:S(2)}, u32[]{:S(2)}) collective-permute-start(bf16[32,3072]{1,0:T(8,128)(2,1)S(1)} %get-tuple-element.12), channel_id=1, source_target_pairs={{0,2},{2,4},{4,6},{6,7},{7,5},{5,3},{3,1},{1,0},{8,10},{10,12},{12... | collective-permute-start | bytes 589832 | tf_op jit(solution)/shard_map/ppermute | solution.py:49
  65.9 4.5 %collective-permute-done.16 = bf16[32,3072]{1,0:T(8,128)(2,1)S(1)} collective-permute-done((bf16[32,3072]{1,0:T(8,128)(2,1)S(1)}, bf16[32,3072]{1,0:T(8,128)(2,1)S(1)}, u32[]{:S(2)}, u32[]{:S(2)}) %collective-permute-start.16) | collective-permute-done | bytes 196640 | tf_op jit(solution)/shard_map/ppermute | solution.py:49
  70.5 1.6 %collective-permute-start.17 = (bf16[32,3072]{1,0:T(8,128)(2,1)S(1)}, bf16[32,3072]{1,0:T(8,128)(2,1)S(1)}, u32[]{:S(2)}, u32[]{:S(2)}) collective-permute-start(bf16[32,3072]{1,0:T(8,128)(2,1)S(1)} %add_convert_fusion.11), channel_id=1, source_target_pairs={{0,2},{2,4},{4,6},{6,7},{7,5},{5,3},{3,1},{1,0},{8,10},{10,12},{12... | collective-permute-start | bytes 589832 | tf_op jit(solution)/shard_map/ppermute | solution.py:55
  72.6 3.6 %collective-permute-done.17 = bf16[32,3072]{1,0:T(8,128)(2,1)S(1)} collective-permute-done((bf16[32,3072]{1,0:T(8,128)(2,1)S(1)}, bf16[32,3072]{1,0:T(8,128)(2,1)S(1)}, u32[]{:S(2)}, u32[]{:S(2)}) %collective-permute-start.17) | collective-permute-done | bytes 196640 | tf_op jit(solution)/shard_map/ppermute | solution.py:55
  76.3 1.6 %collective-permute-start.18 = (bf16[32,3072]{1,0:T(8,128)(2,1)S(1)}, bf16[32,3072]{1,0:T(8,128)(2,1)S(1)}, u32[]{:S(2)}, u32[]{:S(2)}) collective-permute-start(bf16[32,3072]{1,0:T(8,128)(2,1)S(1)} %add_convert_fusion.10), channel_id=1, source_target_pairs={{0,2},{2,4},{4,6},{6,7},{7,5},{5,3},{3,1},{1,0},{8,10},{10,12},{12... | collective-permute-start | bytes 589832 | tf_op jit(solution)/shard_map/ppermute | solution.py:55
  77.9 4.7 %collective-permute-done.18 = bf16[32,3072]{1,0:T(8,128)(2,1)S(1)} collective-permute-done((bf16[32,3072]{1,0:T(8,128)(2,1)S(1)}, bf16[32,3072]{1,0:T(8,128)(2,1)S(1)}, u32[]{:S(2)}, u32[]{:S(2)}) %collective-permute-start.18) | collective-permute-done | bytes 196640 | tf_op jit(solution)/shard_map/ppermute | solution.py:55
  82.8 2.0 %collective-permute-start.23 = (bf16[32,3072]{1,0:T(8,128)(2,1)S(1)}, bf16[32,3072]{1,0:T(8,128)(2,1)S(1)}, u32[]{:S(2)}, u32[]{:S(2)}) collective-permute-start(bf16[32,3072]{1,0:T(8,128)(2,1)S(1)} %get-tuple-element.14), channel_id=1, source_target_pairs={{0,2},{2,4},{4,6},{6,7},{7,5},{5,3},{3,1},{1,0},{8,10},{10,12},{12... | collective-permute-start | bytes 589832 | tf_op jit(solution)/shard_map/ppermute | solution.py:55
  84.9 2.0 %collective-permute-start.19 = (bf16[32,3072]{1,0:T(8,128)(2,1)S(1)}, bf16[32,3072]{1,0:T(8,128)(2,1)S(1)}, u32[]{:S(2)}, u32[]{:S(2)}) collective-permute-start(bf16[32,3072]{1,0:T(8,128)(2,1)S(1)} %get-tuple-element.10), channel_id=1, source_target_pairs={{0,2},{2,4},{4,6},{6,7},{7,5},{5,3},{3,1},{1,0},{8,10},{10,12},{12... | collective-permute-start | bytes 589832 | tf_op jit(solution)/shard_map/ppermute | solution.py:55
  86.9 2.9 %collective-permute-done.21 = bf16[32,3072]{1,0:T(8,128)(2,1)S(1)} collective-permute-done((bf16[32,3072]{1,0:T(8,128)(2,1)S(1)}, bf16[32,3072]{1,0:T(8,128)(2,1)S(1)}, u32[]{:S(2)}, u32[]{:S(2)}) %collective-permute-start.21) | collective-permute-done | bytes 196640 | tf_op jit(solution)/shard_map/ppermute | solution.py:58
  90.6 1.3 %collective-permute-done.26 = bf16[32,3072]{1,0:T(8,128)(2,1)S(1)} collective-permute-done((bf16[32,3072]{1,0:T(8,128)(2,1)S(1)}, bf16[32,3072]{1,0:T(8,128)(2,1)S(1)}, u32[]{:S(2)}, u32[]{:S(2)}) %collective-permute-start.26) | collective-permute-done | bytes 196640 | tf_op jit(solution)/shard_map/ppermute | solution.py:50
  91.9 5.6 %collective-permute-done.22 = bf16[32,3072]{1,0:T(8,128)(2,1)S(1)} collective-permute-done((bf16[32,3072]{1,0:T(8,128)(2,1)S(1)}, bf16[32,3072]{1,0:T(8,128)(2,1)S(1)}, u32[]{:S(2)}, u32[]{:S(2)}) %collective-permute-start.22) | collective-permute-done | bytes 196640 | tf_op jit(solution)/shard_map/ppermute | solution.py:58
  97.7 1.6 %collective-permute-start.24 = (bf16[32,3072]{1,0:T(8,128)(2,1)S(1)}, bf16[32,3072]{1,0:T(8,128)(2,1)S(1)}, u32[]{:S(2)}, u32[]{:S(2)}) collective-permute-start(bf16[32,3072]{1,0:T(8,128)(2,1)S(1)} %get-tuple-element.9), channel_id=1, source_target_pairs={{0,2},{2,4},{4,6},{6,7},{7,5},{5,3},{3,1},{1,0},{8,10},{10,12},{12... | collective-permute-start | bytes 589832 | tf_op jit(solution)/shard_map/ppermute | solution.py:55
  99.7 4.7 %collective-permute-done.24 = bf16[32,3072]{1,0:T(8,128)(2,1)S(1)} collective-permute-done((bf16[32,3072]{1,0:T(8,128)(2,1)S(1)}, bf16[32,3072]{1,0:T(8,128)(2,1)S(1)}, u32[]{:S(2)}, u32[]{:S(2)}) %collective-permute-start.24) | collective-permute-done | bytes 196640 | tf_op jit(solution)/shard_map/ppermute | solution.py:55
  105.0 0.8 collective-permute-start.28
  105.8 1.3 %collective-permute-start.25 = (bf16[32,3072]{1,0:T(8,128)(2,1)S(1)}, bf16[32,3072]{1,0:T(8,128)(2,1)S(1)}, u32[]{:S(2)}, u32[]{:S(2)}) collective-permute-start(bf16[32,3072]{1,0:T(8,128)(2,1)S(1)} %get-tuple-element.16), channel_id=1, source_target_pairs={{0,2},{2,4},{4,6},{6,7},{7,5},{5,3},{3,1},{1,0},{8,10},{10,12},{12... | collective-permute-start | bytes 589832 | tf_op jit(solution)/shard_map/ppermute | solution.py:55
  107.1 3.6 %collective-permute-done.28 = bf16[32,3072]{1,0:T(8,128)(2,1)S(1)} collective-permute-done((bf16[32,3072]{1,0:T(8,128)(2,1)S(1)}, bf16[32,3072]{1,0:T(8,128)(2,1)S(1)}, u32[]{:S(2)}, u32[]{:S(2)}) %collective-permute-start.28) | collective-permute-done | bytes 196640 | tf_op jit(solution)/shard_map/ppermute | solution.py:58
  110.8 0.8 collective-permute-start.29
  111.6 4.9 %collective-permute-done.29 = bf16[32,3072]{1,0:T(8,128)(2,1)S(1)} collective-permute-done((bf16[32,3072]{1,0:T(8,128)(2,1)S(1)}, bf16[32,3072]{1,0:T(8,128)(2,1)S(1)}, u32[]{:S(2)}, u32[]{:S(2)}) %collective-permute-start.29) | collective-permute-done | bytes 196640 | tf_op jit(solution)/shard_map/ppermute | solution.py:58
  116.6 0.8 pad_maximum_fusion
  (56 shorter events, 7.7 us)
Async XLA Ops:
  1.1 11.0 %collective-permute-start = (bf16[32,3072]{1,0:T(8,128)(2,1)S(1)}, bf16[32,3072]{1,0:T(8,128)(2,1)S(1)}, u32[]{:S(2)}, u32[]{:S(2)}) collective-permute-start(bf16[32,3072]{1,0:T(8,128)(2,1)S(1)} %get-tuple-element.20), channel_id=1, source_target_pairs={{0,2},{2,4},{4,6},{6,7},{7,5},{5,3},{3,1},{1,0},{8,10},{10,12},{12... | collective-permute-start | bytes 589832 | tf_op jit(solution)/shard_map/ppermute | solution.py:35
  4.1 12.3 %collective-permute-start.2 = (bf16[32,3072]{1,0:T(8,128)(2,1)S(1)}, bf16[32,3072]{1,0:T(8,128)(2,1)S(1)}, u32[]{:S(2)}, u32[]{:S(2)}) collective-permute-start(bf16[32,3072]{1,0:T(8,128)(2,1)S(1)} %get-tuple-element.20), channel_id=1, source_target_pairs={{2,0},{4,2},{6,4},{7,6},{5,7},{3,5},{1,3},{0,1},{10,8},{12,10},{14... | collective-permute-start | bytes 589832 | tf_op jit(solution)/shard_map/ppermute | solution.py:36
  4.1 9.9 %collective-permute-start.1 = (bf16[32,3072]{1,0:T(8,128)(2,1)S(1)}, bf16[32,3072]{1,0:T(8,128)(2,1)S(1)}, u32[]{:S(2)}, u32[]{:S(2)}) collective-permute-start(bf16[32,3072]{1,0:T(8,128)(2,1)S(1)} %get-tuple-element.21), channel_id=1, source_target_pairs={{0,2},{2,4},{4,6},{6,7},{7,5},{5,3},{3,1},{1,0},{8,10},{10,12},{12... | collective-permute-start | bytes 589832 | tf_op jit(solution)/shard_map/ppermute | solution.py:35
  6.2 10.7 %collective-permute-start.3 = (bf16[32,3072]{1,0:T(8,128)(2,1)S(1)}, bf16[32,3072]{1,0:T(8,128)(2,1)S(1)}, u32[]{:S(2)}, u32[]{:S(2)}) collective-permute-start(bf16[32,3072]{1,0:T(8,128)(2,1)S(1)} %get-tuple-element.21), channel_id=1, source_target_pairs={{2,0},{4,2},{6,4},{7,6},{5,7},{3,5},{1,3},{0,1},{10,8},{12,10},{14... | collective-permute-start | bytes 589832 | tf_op jit(solution)/shard_map/ppermute | solution.py:36
  12.0 7.9 %collective-permute-start.4 = (bf16[32,3072]{1,0:T(8,128)(2,1)S(1)}, bf16[32,3072]{1,0:T(8,128)(2,1)S(1)}, u32[]{:S(2)}, u32[]{:S(2)}) collective-permute-start(bf16[32,3072]{1,0:T(8,128)(2,1)S(1)} %collective-permute-done), channel_id=1, source_target_pairs={{0,2},{2,4},{4,6},{6,7},{7,5},{5,3},{3,1},{1,0},{8,10},{10,12},{12... | collective-permute-start | bytes 589832 | tf_op jit(solution)/shard_map/ppermute | solution.py:35
  14.0 10.0 %collective-permute-start.5 = (bf16[32,3072]{1,0:T(8,128)(2,1)S(1)}, bf16[32,3072]{1,0:T(8,128)(2,1)S(1)}, u32[]{:S(2)}, u32[]{:S(2)}) collective-permute-start(bf16[32,3072]{1,0:T(8,128)(2,1)S(1)} %collective-permute-done.1), channel_id=1, source_target_pairs={{0,2},{2,4},{4,6},{6,7},{7,5},{5,3},{3,1},{1,0},{8,10},{10,12},{12... | collective-permute-start | bytes 589832 | tf_op jit(solution)/shard_map/ppermute | solution.py:35
  16.4 10.5 %collective-permute-start.6 = (bf16[32,3072]{1,0:T(8,128)(2,1)S(1)}, bf16[32,3072]{1,0:T(8,128)(2,1)S(1)}, u32[]{:S(2)}, u32[]{:S(2)}) collective-permute-start(bf16[32,3072]{1,0:T(8,128)(2,1)S(1)} %collective-permute-done.2), channel_id=1, source_target_pairs={{2,0},{4,2},{6,4},{7,6},{5,7},{3,5},{1,3},{0,1},{10,8},{12,10},{14... | collective-permute-start | bytes 589832 | tf_op jit(solution)/shard_map/ppermute | solution.py:36
  16.8 10.0 %collective-permute-start.7 = (bf16[32,3072]{1,0:T(8,128)(2,1)S(1)}, bf16[32,3072]{1,0:T(8,128)(2,1)S(1)}, u32[]{:S(2)}, u32[]{:S(2)}) collective-permute-start(bf16[32,3072]{1,0:T(8,128)(2,1)S(1)} %collective-permute-done.3), channel_id=1, source_target_pairs={{2,0},{4,2},{6,4},{7,6},{5,7},{3,5},{1,3},{0,1},{10,8},{12,10},{14... | collective-permute-start | bytes 589832 | tf_op jit(solution)/shard_map/ppermute | solution.py:36
  19.9 9.8 %collective-permute-start.8 = (bf16[32,3072]{1,0:T(8,128)(2,1)S(1)}, bf16[32,3072]{1,0:T(8,128)(2,1)S(1)}, u32[]{:S(2)}, u32[]{:S(2)}) collective-permute-start(bf16[32,3072]{1,0:T(8,128)(2,1)S(1)} %collective-permute-done.4), channel_id=1, source_target_pairs={{0,2},{2,4},{4,6},{6,7},{7,5},{5,3},{3,1},{1,0},{8,10},{10,12},{12... | collective-permute-start | bytes 589832 | tf_op jit(solution)/shard_map/ppermute | solution.py:35
  24.1 10.5 %collective-permute-start.9 = (bf16[32,3072]{1,0:T(8,128)(2,1)S(1)}, bf16[32,3072]{1,0:T(8,128)(2,1)S(1)}, u32[]{:S(2)}, u32[]{:S(2)}) collective-permute-start(bf16[32,3072]{1,0:T(8,128)(2,1)S(1)} %collective-permute-done.5), channel_id=1, source_target_pairs={{0,2},{2,4},{4,6},{6,7},{7,5},{5,3},{3,1},{1,0},{8,10},{10,12},{12... | collective-permute-start | bytes 589832 | tf_op jit(solution)/shard_map/ppermute | solution.py:35
  26.9 7.7 %collective-permute-start.11 = (bf16[32,3072]{1,0:T(8,128)(2,1)S(1)}, bf16[32,3072]{1,0:T(8,128)(2,1)S(1)}, u32[]{:S(2)}, u32[]{:S(2)}) collective-permute-start(bf16[32,3072]{1,0:T(8,128)(2,1)S(1)} %collective-permute-done.7), channel_id=1, source_target_pairs={{2,0},{4,2},{6,4},{7,6},{5,7},{3,5},{1,3},{0,1},{10,8},{12,10},{14... | collective-permute-start | bytes 589832 | tf_op jit(solution)/shard_map/ppermute | solution.py:36
  26.9 9.8 %collective-permute-start.10 = (bf16[32,3072]{1,0:T(8,128)(2,1)S(1)}, bf16[32,3072]{1,0:T(8,128)(2,1)S(1)}, u32[]{:S(2)}, u32[]{:S(2)}) collective-permute-start(bf16[32,3072]{1,0:T(8,128)(2,1)S(1)} %collective-permute-done.6), channel_id=1, source_target_pairs={{2,0},{4,2},{6,4},{7,6},{5,7},{3,5},{1,3},{0,1},{10,8},{12,10},{14... | collective-permute-start | bytes 589832 | tf_op jit(solution)/shard_map/ppermute | solution.py:36
  29.6 7.8 %collective-permute-start.12 = (bf16[32,3072]{1,0:T(8,128)(2,1)S(1)}, bf16[32,3072]{1,0:T(8,128)(2,1)S(1)}, u32[]{:S(2)}, u32[]{:S(2)}) collective-permute-start(bf16[32,3072]{1,0:T(8,128)(2,1)S(1)} %collective-permute-done.8), channel_id=1, source_target_pairs={{0,2},{2,4},{4,6},{6,7},{7,5},{5,3},{3,1},{1,0},{8,10},{10,12},{12... | collective-permute-start | bytes 589832 | tf_op jit(solution)/shard_map/ppermute | solution.py:39
  34.6 5.7 %collective-permute-start.13 = (bf16[32,3072]{1,0:T(8,128)(2,1)S(1)}, bf16[32,3072]{1,0:T(8,128)(2,1)S(1)}, u32[]{:S(2)}, u32[]{:S(2)}) collective-permute-start(bf16[32,3072]{1,0:T(8,128)(2,1)S(1)} %collective-permute-done.11), channel_id=1, source_target_pairs={{2,0},{4,2},{6,4},{7,6},{5,7},{3,5},{1,3},{0,1},{10,8},{12,10},{14... | collective-permute-start | bytes 589832 | tf_op jit(solution)/shard_map/ppermute | solution.py:39
  51.3 7.5 %copy-start = (f32[4,128,128]{2,1,0:T(8,128)S(1)}, f32[4,128,128]{2,1,0:T(8,128)}, u32[]{:S(2)}) copy-start(f32[4,128,128]{2,1,0:T(8,128)} %param.11) | copy-start | bytes 786436
  51.7 1.4 %collective-permute-start.14 = (bf16[4,128,128]{2,1,0:T(8,128)(2,1)S(1)}, bf16[4,128,128]{2,1,0:T(8,128)(2,1)S(1)}, u32[]{:S(2)}, u32[]{:S(2)}) collective-permute-start(bf16[4,128,128]{2,1,0:T(8,128)(2,1)S(1)} %get-tuple-element.22), channel_id=1, source_target_pairs={{0,8},{8,0},{16,24},{24,16},{1,9},{9,1},{17,25},{25,17},{2,10},{10... | collective-permute-start | bytes 393224 | tf_op jit(solution)/shard_map/ppermute | solution.py:76
  52.1 7.3 %copy-start.1 = (f32[512]{0:T(512)S(1)}, f32[512]{0:T(512)}, u32[]{:S(2)}) copy-start(f32[512]{0:T(512)} %param.10) | copy-start | bytes 6148
  53.2 5.6 %collective-permute-start.15 = (bf16[4,128,128]{2,1,0:T(8,128)(2,1)S(1)}, bf16[4,128,128]{2,1,0:T(8,128)(2,1)S(1)}, u32[]{:S(2)}, u32[]{:S(2)}) collective-permute-start(bf16[4,128,128]{2,1,0:T(8,128)(2,1)S(1)} %fusion.19), channel_id=1, source_target_pairs={{0,16},{8,24},{16,0},{24,8},{1,17},{9,25},{17,1},{25,9},{2,18},{10... | collective-permute-start | bytes 393224 | tf_op jit(solution)/shard_map/ppermute | solution.py:76
  64.3 6.2 %collective-permute-start.16 = (bf16[32,3072]{1,0:T(8,128)(2,1)S(1)}, bf16[32,3072]{1,0:T(8,128)(2,1)S(1)}, u32[]{:S(2)}, u32[]{:S(2)}) collective-permute-start(bf16[32,3072]{1,0:T(8,128)(2,1)S(1)} %get-tuple-element.12), channel_id=1, source_target_pairs={{0,2},{2,4},{4,6},{6,7},{7,5},{5,3},{3,1},{1,0},{8,10},{10,12},{12... | collective-permute-start | bytes 589832 | tf_op jit(solution)/shard_map/ppermute | solution.py:49
  70.5 5.7 %collective-permute-start.17 = (bf16[32,3072]{1,0:T(8,128)(2,1)S(1)}, bf16[32,3072]{1,0:T(8,128)(2,1)S(1)}, u32[]{:S(2)}, u32[]{:S(2)}) collective-permute-start(bf16[32,3072]{1,0:T(8,128)(2,1)S(1)} %add_convert_fusion.11), channel_id=1, source_target_pairs={{0,2},{2,4},{4,6},{6,7},{7,5},{5,3},{3,1},{1,0},{8,10},{10,12},{12... | collective-permute-start | bytes 589832 | tf_op jit(solution)/shard_map/ppermute | solution.py:55
  72.2 5.8 %collective-permute-start.20 = (bf16[32,3072]{1,0:T(8,128)(2,1)S(1)}, bf16[32,3072]{1,0:T(8,128)(2,1)S(1)}, u32[]{:S(2)}, u32[]{:S(2)}) collective-permute-start(bf16[32,3072]{1,0:T(8,128)(2,1)S(1)} %get-tuple-element.15), channel_id=1, source_target_pairs={{2,0},{4,2},{6,4},{7,6},{5,7},{3,5},{1,3},{0,1},{10,8},{12,10},{14... | collective-permute-start | bytes 589832 | tf_op jit(solution)/shard_map/ppermute | solution.py:58
  76.3 6.4 %collective-permute-start.18 = (bf16[32,3072]{1,0:T(8,128)(2,1)S(1)}, bf16[32,3072]{1,0:T(8,128)(2,1)S(1)}, u32[]{:S(2)}, u32[]{:S(2)}) collective-permute-start(bf16[32,3072]{1,0:T(8,128)(2,1)S(1)} %add_convert_fusion.10), channel_id=1, source_target_pairs={{0,2},{2,4},{4,6},{6,7},{7,5},{5,3},{3,1},{1,0},{8,10},{10,12},{12... | collective-permute-start | bytes 589832 | tf_op jit(solution)/shard_map/ppermute | solution.py:55
  82.8 7.0 %collective-permute-start.21 = (bf16[32,3072]{1,0:T(8,128)(2,1)S(1)}, bf16[32,3072]{1,0:T(8,128)(2,1)S(1)}, u32[]{:S(2)}, u32[]{:S(2)}) collective-permute-start(bf16[32,3072]{1,0:T(8,128)(2,1)S(1)} %get-tuple-element.11), channel_id=1, source_target_pairs={{2,0},{4,2},{6,4},{7,6},{5,7},{3,5},{1,3},{0,1},{10,8},{12,10},{14... | collective-permute-start | bytes 589832 | tf_op jit(solution)/shard_map/ppermute | solution.py:58
  82.8 7.7 %collective-permute-start.23 = (bf16[32,3072]{1,0:T(8,128)(2,1)S(1)}, bf16[32,3072]{1,0:T(8,128)(2,1)S(1)}, u32[]{:S(2)}, u32[]{:S(2)}) collective-permute-start(bf16[32,3072]{1,0:T(8,128)(2,1)S(1)} %get-tuple-element.14), channel_id=1, source_target_pairs={{0,2},{2,4},{4,6},{6,7},{7,5},{5,3},{3,1},{1,0},{8,10},{10,12},{12... | collective-permute-start | bytes 589832 | tf_op jit(solution)/shard_map/ppermute | solution.py:55
  84.8 7.1 %collective-permute-start.26 = (bf16[32,3072]{1,0:T(8,128)(2,1)S(1)}, bf16[32,3072]{1,0:T(8,128)(2,1)S(1)}, u32[]{:S(2)}, u32[]{:S(2)}) collective-permute-start(bf16[32,3072]{1,0:T(8,128)(2,1)S(1)} %get-tuple-element.13), channel_id=1, source_target_pairs={{2,0},{4,2},{6,4},{7,6},{5,7},{3,5},{1,3},{0,1},{10,8},{12,10},{14... | collective-permute-start | bytes 589832 | tf_op jit(solution)/shard_map/ppermute | solution.py:50
  84.9 7.0 %collective-permute-start.19 = (bf16[32,3072]{1,0:T(8,128)(2,1)S(1)}, bf16[32,3072]{1,0:T(8,128)(2,1)S(1)}, u32[]{:S(2)}, u32[]{:S(2)}) collective-permute-start(bf16[32,3072]{1,0:T(8,128)(2,1)S(1)} %get-tuple-element.10), channel_id=1, source_target_pairs={{0,2},{2,4},{4,6},{6,7},{7,5},{5,3},{3,1},{1,0},{8,10},{10,12},{12... | collective-permute-start | bytes 589832 | tf_op jit(solution)/shard_map/ppermute | solution.py:55
  89.8 7.7 %collective-permute-start.22 = (bf16[32,3072]{1,0:T(8,128)(2,1)S(1)}, bf16[32,3072]{1,0:T(8,128)(2,1)S(1)}, u32[]{:S(2)}, u32[]{:S(2)}) collective-permute-start(bf16[32,3072]{1,0:T(8,128)(2,1)S(1)} %add_convert_fusion.7), channel_id=1, source_target_pairs={{2,0},{4,2},{6,4},{7,6},{5,7},{3,5},{1,3},{0,1},{10,8},{12,10},{14... | collective-permute-start | bytes 589832 | tf_op jit(solution)/shard_map/ppermute | solution.py:58
  97.7 6.8 %collective-permute-start.24 = (bf16[32,3072]{1,0:T(8,128)(2,1)S(1)}, bf16[32,3072]{1,0:T(8,128)(2,1)S(1)}, u32[]{:S(2)}, u32[]{:S(2)}) collective-permute-start(bf16[32,3072]{1,0:T(8,128)(2,1)S(1)} %get-tuple-element.9), channel_id=1, source_target_pairs={{0,2},{2,4},{4,6},{6,7},{7,5},{5,3},{3,1},{1,0},{8,10},{10,12},{12... | collective-permute-start | bytes 589832 | tf_op jit(solution)/shard_map/ppermute | solution.py:55
  99.3 5.7 %collective-permute-start.27 = (bf16[32,3072]{1,0:T(8,128)(2,1)S(1)}, bf16[32,3072]{1,0:T(8,128)(2,1)S(1)}, u32[]{:S(2)}, u32[]{:S(2)}) collective-permute-start(bf16[32,3072]{1,0:T(8,128)(2,1)S(1)} %get-tuple-element.8), channel_id=1, source_target_pairs={{2,0},{4,2},{6,4},{7,6},{5,7},{3,5},{1,3},{0,1},{10,8},{12,10},{14... | collective-permute-start | bytes 589832 | tf_op jit(solution)/shard_map/ppermute | solution.py:58
  105.0 5.7 %collective-permute-start.28 = (bf16[32,3072]{1,0:T(8,128)(2,1)S(1)}, bf16[32,3072]{1,0:T(8,128)(2,1)S(1)}, u32[]{:S(2)}, u32[]{:S(2)}) collective-permute-start(bf16[32,3072]{1,0:T(8,128)(2,1)S(1)} %get-tuple-element.17), channel_id=1, source_target_pairs={{2,0},{4,2},{6,4},{7,6},{5,7},{3,5},{1,3},{0,1},{10,8},{12,10},{14... | collective-permute-start | bytes 589832 | tf_op jit(solution)/shard_map/ppermute | solution.py:58
  105.8 5.8 %collective-permute-start.25 = (bf16[32,3072]{1,0:T(8,128)(2,1)S(1)}, bf16[32,3072]{1,0:T(8,128)(2,1)S(1)}, u32[]{:S(2)}, u32[]{:S(2)}) collective-permute-start(bf16[32,3072]{1,0:T(8,128)(2,1)S(1)} %get-tuple-element.16), channel_id=1, source_target_pairs={{0,2},{2,4},{4,6},{6,7},{7,5},{5,3},{3,1},{1,0},{8,10},{10,12},{12... | collective-permute-start | bytes 589832 | tf_op jit(solution)/shard_map/ppermute | solution.py:55
  110.8 5.7 %collective-permute-start.29 = (bf16[32,3072]{1,0:T(8,128)(2,1)S(1)}, bf16[32,3072]{1,0:T(8,128)(2,1)S(1)}, u32[]{:S(2)}, u32[]{:S(2)}) collective-permute-start(bf16[32,3072]{1,0:T(8,128)(2,1)S(1)} %add_convert_fusion.1), channel_id=1, source_target_pairs={{2,0},{4,2},{6,4},{7,6},{5,7},{3,5},{1,3},{0,1},{10,8},{12,10},{14... | collective-permute-start | bytes 589832 | tf_op jit(solution)/shard_map/ppermute | solution.py:58

commit v2 on v1

v2 whole, which is shorter than its diff:
```python
import functools

import jax
import jax.numpy as jnp
from jax import lax
from jax.experimental import pallas as pl
from jax.experimental.pallas import tpu as pltpu
from jax.sharding import PartitionSpec as P

VMEM = pl.BlockSpec(memory_space=pltpu.VMEM)
ANY = pl.BlockSpec(memory_space=pl.ANY)
F32, BF16 = jnp.float32, jnp.bfloat16


def ring_order(size):
    return list(range(0, size, 2)) + list(range(size - 1, 0, -2))


def neighbours(size):
    ring = ring_order(size)
    right = [(ring[i], ring[(i + 1) % size]) for i in range(size)]
    left = [(b, a) for a, b in right]
    return right, left


def slots(size):
    order = [0]
    for step in range(1, size // 2):
        order += [-step, step]
    return order + [size // 2]


def call(body, out_shape, in_specs, out_specs, flops=0, nbytes=0, limit=16 << 20, **more):
    return pl.pallas_call(
        body,
        out_shape=out_shape,
        in_specs=in_specs,
        out_specs=out_specs,
        cost_estimate=pl.CostEstimate(flops=flops, bytes_accessed=nbytes, transcendentals=0),
        compiler_params=pltpu.CompilerParams(vmem_limit_bytes=limit),
        **more,
    )


def fetch(source, index, shape, after):
    def body(source_ref, after_ref, out_ref, sem):
        copy = pltpu.make_async_copy(source_ref.at[index], out_ref, sem)
        copy.start()
        copy.wait()

    return call(
        body,
        jax.ShapeDtypeStruct(shape, source.dtype),
        [ANY, ANY],
        VMEM,
        nbytes=2 * 2 * shape[0] * shape[1],
        scratch_shapes=[pltpu.SemaphoreType.DMA],
        name="fetch",
    )(source, after)


def ring_gather(block, size, right, left):
    half = block.shape[1] // 2
    quarter = half // 2
    going_right = [block[:, :half], block[:, half:]]
    going_left = list(going_right)
    held = [[going_right[0]], [going_right[1]]]
    for _ in range(size // 2 - 1):
        for part in range(2):
            going_right[part] = lax.ppermute(going_right[part], "fsdp", right)
            going_left[part] = lax.ppermute(going_left[part], "fsdp", left)
            held[part] += [going_right[part], going_left[part]]
    for part in range(2):
        held[part].append(lax.ppermute(going_right[part][:, :quarter], "fsdp", right))
        held[part].append(lax.ppermute(going_left[part][:, quarter:], "fsdp", left))
    return held


def assemble(pieces, into):
    rows = pieces[0].shape[0]
    for place, piece in enumerate(pieces[:-2]):
        into[place * rows : (place + 1) * rows, :] = piece[...]
    quarter = pieces[-1].shape[1]
    start = (len(pieces) - 2) * rows
    into[start : start + rows, :quarter] = pieces[-2][...]
    into[start : start + rows, quarter:] = pieces[-1][...]


def first_pass(pieces, weight, n_rows):
    n_out, width, columns = weight.shape
    half = width // 2
    tile = min(columns, 256)
    tiles = columns // tile

    def body(*refs):
        rows = refs[: len(pieces)]
        weight_ref, out_ref, whole = refs[len(pieces) :]
        step = pl.program_id(0)

        @pl.when(step == 0)
        def _():
            assemble(rows, whole)

        start = pl.multiple_of((step % tiles) * tile, tile)
        out_ref[step // tiles, :, pl.ds(start, tile)] = jnp.dot(
            whole[...], weight_ref[...], preferred_element_type=F32
        )

    return call(
        body,
        jax.ShapeDtypeStruct((n_out, n_rows, columns), F32),
        [VMEM] * len(pieces)
        + [pl.BlockSpec((None, half, tile), lambda i: (i // tiles, 0, i % tiles))],
        VMEM,
        flops=2 * n_out * n_rows * half * columns,
        nbytes=2 * n_out * half * columns,
        limit=24 << 20,
        grid=(n_out * tiles,),
        scratch_shapes=[pltpu.VMEM((n_rows, half), BF16)],
        name="first_pass",
    )(*pieces, weight)


def feature_map(projected):
    return jnp.where(projected > 0.0, projected + 1.0, jnp.exp(jnp.minimum(projected, 0.0)))


def keys_and_values(pieces, key_weight, value_weight, first, head_dim):
    _, n_rows, columns = first.shape
    half = key_weight.shape[0]

    def body(*refs):
        rows = refs[: len(pieces)]
        key_ref, value_ref, first_ref, feat_ref, values_ref, state_ref, whole = refs[len(pieces) :]
        assemble(rows, whole)
        tile = min(columns, 256)
        for start in range(0, columns, tile):
            span = slice(start, start + tile)
            projected = first_ref[1, :, span] + jnp.dot(whole[...], key_ref[:, span], preferred_element_type=F32)
            feat = feature_map(projected).astype(BF16)
            feat_ref[:, span] = feat
            projected = first_ref[2, :, span] + jnp.dot(whole[...], value_ref[:, span], preferred_element_type=F32)
            values = projected.astype(BF16)
            values_ref[:, span] = values
            for head in range(start, start + tile, head_dim):
                at = slice(head - start, head - start + head_dim)
                state_ref[head // head_dim] = lax.dot_general(
                    feat[:, at], values[:, at], (((0,), (0,)), ((), ())), preferred_element_type=F32
                ).astype(BF16)

    return call(
        body,
        (
            jax.ShapeDtypeStruct((n_rows, columns), BF16),
            jax.ShapeDtypeStruct((n_rows, columns), BF16),
            jax.ShapeDtypeStruct((columns // head_dim, head_dim, head_dim), BF16),
            jax.ShapeDtypeStruct((n_rows, half), BF16),
        ),
        [VMEM] * (len(pieces) + 3),
        (VMEM,) * 4,
        flops=2 * 2 * n_rows * half * columns,
        nbytes=2 * 2 * half * columns,
        name="keys_and_values",
    )(*pieces, key_weight, value_weight, first)


def queries_within(whole, query_weight, first, feat_k, values, head_dim, size, rows):
    n_rows, columns = feat_k.shape
    order = slots(size)

    def place(shape, axis):
        spot = lax.axis_index("fsdp")
        spot = jnp.where(spot % 2 == 0, spot // 2, size - (spot + 1) // 2)
        row = lax.broadcasted_iota(jnp.int32, shape, axis)
        slot = row // rows
        start = jnp.zeros(shape, jnp.int32)
        for at, distance in enumerate(order):
            there = (spot + distance + size) % size
            holder = jnp.where(there < size // 2, 2 * there, 2 * (size - there) - 1)
            start = jnp.where(slot == at, holder * rows, start)
        return start + row - slot * rows

    def body(whole_ref, weight_ref, first_ref, k_ref, v_ref, feat_ref, within_ref):
        causal = place((n_rows, 1), 0) >= place((1, n_rows), 1)
        tile = min(columns, 256)
        for start in range(0, columns, tile):
            span = slice(start, start + tile)
            projected = first_ref[0, :, span] + jnp.dot(whole_ref[...], weight_ref[:, span], preferred_element_type=F32)
            feat = feature_map(projected).astype(BF16)
            feat_ref[:, span] = feat
            for head in range(start, start + tile, head_dim):
                at = slice(head, head + head_dim)
                scores = lax.dot_general(
                    feat[:, head - start : head - start + head_dim],
                    k_ref[:, at],
                    (((1,), (1,)), ((), ())),
                    preferred_element_type=F32,
                )
                scores = jnp.where(causal, scores, 0.0).astype(BF16)
                within_ref[:, at] = jnp.dot(scores, v_ref[:, at], preferred_element_type=F32)

    half = whole.shape[1]
    return call(
        body,
        (jax.ShapeDtypeStruct((n_rows, columns), BF16), jax.ShapeDtypeStruct((n_rows, columns), F32)),
        [VMEM] * 5,
        (VMEM,) * 2,
        flops=2 * n_rows * half * columns + 4 * n_rows * n_rows * columns,
        nbytes=2 * half * columns,
        limit=24 << 20,
        name="queries_within",
    )(whole, query_weight, first, feat_k, values)


def part_shapes(count, rows, half):
    return [jax.ShapeDtypeStruct((rows, half), BF16)] * (count - 1) + [
        jax.ShapeDtypeStruct((rows, half // 2), BF16)
    ] * 2


def spread(product, start, parts, rows, width):
    for place, part in enumerate(parts[:-2]):
        part[:, start : start + width] = product[place * rows : (place + 1) * rows, :]
    last = product[(len(parts) - 2) * rows :, :]
    quarter = parts[-1].shape[1]
    target = parts[-2] if start < quarter else parts[-1]
    start = start % quarter
    target[:, start : start + width] = last


def project_out(normalized, weight_ref, first_column, parts, rows):
    half = parts[0].shape[1]
    tile = 512 if (half // 2) % 512 == 0 else 128
    for start in range(0, half, tile):
        columns = slice(first_column + start, first_column + start + tile)
        product = jnp.dot(normalized, weight_ref[:, columns], preferred_element_type=F32).astype(BF16)
        spread(product, start, parts, rows, tile)


def attend_and_project(feat_q, within, initial, earlier, gain, out_weight, size, head_dim):
    n_rows, columns = feat_q.shape
    rows = n_rows // size
    half = out_weight.shape[1] // 2
    shapes = part_shapes(size, rows, half)

    def body(q_ref, within_ref, initial_ref, earlier_ref, gain_ref, weight_ref, *refs):
        normalized_ref, parts = refs[0], refs[1:]
        for head in range(columns // head_dim):
            at = slice(head * head_dim, (head + 1) * head_dim)
            prefix = initial_ref[head] + earlier_ref[head]
            high = prefix.astype(BF16)
            low = (prefix - high.astype(F32)).astype(BF16)
            q = q_ref[:, at]
            attended = within_ref[:, at] + jnp.dot(q, high, preferred_element_type=F32)
            attended = attended + jnp.dot(q, low, preferred_element_type=F32)
            scale = lax.rsqrt(jnp.mean(attended * attended, axis=-1, keepdims=True) + 1e-06)
            normalized_ref[:, at] = (attended * scale * gain_ref[:, at]).astype(BF16)
        project_out(normalized_ref[...], weight_ref, 0, parts, rows)

    out = call(
        body,
        [jax.ShapeDtypeStruct((n_rows, columns), BF16)] + shapes,
        [VMEM] * 6,
        [VMEM] * (1 + len(shapes)),
        flops=2 * n_rows * half * columns,
        nbytes=2 * half * columns,
        name="attend_and_project",
    )(feat_q, within, initial, earlier, gain.reshape(1, columns), out_weight)
    return out[0], out[1:]


def project_rest(normalized, out_weight, size):
    n_rows, columns = normalized.shape
    rows = n_rows // size
    half = out_weight.shape[1] // 2
    shapes = part_shapes(size, rows, half)

    def body(normalized_ref, weight_ref, *parts):
        project_out(normalized_ref[...], weight_ref, half, parts, rows)

    return call(
        body,
        shapes,
        [VMEM] * 2,
        [VMEM] * len(shapes),
        flops=2 * n_rows * half * columns,
        nbytes=2 * half * columns,
        name="project_rest",
    )(normalized, out_weight)


def add_step(mine_right, got_right, mine_left, got_left):
    rows, half = mine_right.shape
    partial = got_right.shape[1]

    def body(mr, gr, ml, gl, to_right, to_left):
        if partial < half:
            to_right[:, partial:] = mr[:, partial:]
            to_left[:, : half - partial] = ml[:, : half - partial]
        to_right[:, :partial] = (mr[:, :partial].astype(F32) + gr[...].astype(F32)).astype(BF16)
        to_left[:, half - partial :] = (ml[:, half - partial :].astype(F32) + gl[...].astype(F32)).astype(BF16)

    return call(
        body,
        [jax.ShapeDtypeStruct((rows, half), BF16)] * 2,
        [VMEM] * 4,
        [VMEM] * 2,
        nbytes=12 * rows * half,
        name="add_step",
    )(mine_right, got_right, mine_left, got_left)


def finish(groups):
    rows, half = groups[0][0].shape

    def body(*refs):
        out = refs[-1]
        for part in range(len(groups)):
            mine, got_right, got_left = refs[3 * part : 3 * part + 3]
            total = mine[...].astype(F32) + got_right[...].astype(F32) + got_left[...].astype(F32)
            out[:, part * half : (part + 1) * half] = total.astype(BF16)

    flat = [value for group in groups for value in group]
    return call(
        body,
        jax.ShapeDtypeStruct((rows, half * len(groups)), BF16),
        [VMEM] * len(flat),
        VMEM,
        nbytes=4 * rows * half,
        name="finish",
    )(*flat)


def earlier_states(state, size):
    place = lax.axis_index("ctx")
    before = None
    total = state
    reach = 1
    while reach < size:
        pairs = [(i, i ^ reach) for i in range(size)]
        other = lax.ppermute(total, "ctx", pairs)
        mine = jnp.where((place & reach) != 0, other.astype(F32), 0.0)
        before = mine if before is None else before + mine
        total = (total.astype(F32) + other.astype(F32)).astype(BF16)
        reach *= 2
    return before


def per_device(n_ctx, n_fsdp, tokens, qkv_weight, out_weight, norm_gain, initial_state):
    rows, width = tokens.shape
    heads_here, head_dim = initial_state.shape[:2]
    columns = heads_here * head_dim
    n_rows = rows * n_fsdp
    far = n_fsdp // 2
    right, left = neighbours(n_fsdp)
    order = slots(n_fsdp)

    held = ring_gather(tokens, n_fsdp, right, left)
    half = width // 2
    second = [
        fetch(qkv_weight, (s, pl.ds(half, half)), (half, columns), held[0][1 + at])
        for at, s in enumerate(range(3))
    ]
    fetched_out = fetch(out_weight, (pl.ds(0, columns),), out_weight.shape, held[1][2])

    first = first_pass(held[0], qkv_weight, n_rows)
    feat_k, values, state, whole = keys_and_values(held[1], second[1], second[2], first, head_dim)
    feat_q, within = queries_within(whole, second[0], first, feat_k, values, head_dim, n_fsdp, rows)
    earlier = earlier_states(state, n_ctx)
    normalized, parts_a = attend_and_project(
        feat_q, within, initial_state, earlier, norm_gain, fetched_out, n_fsdp, head_dim
    )
    parts_b = project_rest(normalized, fetched_out, n_fsdp)

    groups = []
    for parts in (parts_a, parts_b):
        got_right = lax.ppermute(parts[-2], "fsdp", right)
        got_left = lax.ppermute(parts[-1], "fsdp", left)
        for step in range(far - 1, 0, -1):
            to_right, to_left = add_step(
                parts[order.index(step)], got_right, parts[order.index(-step)], got_left
            )
            got_right = lax.ppermute(to_right, "fsdp", right)
            got_left = lax.ppermute(to_left, "fsdp", left)
        groups.append((parts[0], got_right, got_left))
    return finish(groups)


def solution(mesh):
    body = functools.partial(per_device, mesh.shape["ctx"], mesh.shape["fsdp"])
    placed = (
        P(("ctx", "fsdp"), None),
        P(None, None, "fsdp"),
        P("fsdp", None),
        P("fsdp"),
        P("fsdp", None, None),
    )
    return jax.shard_map(
        body, mesh=mesh, in_specs=placed, out_specs=P(("ctx", "fsdp"), None), check_vma=False
    )
```

time: 118 us -> 107 us (0.907)
  waiting for transfers between devices: 52.9 us -> 33.2 us
  local copies, waits for them, and re-layouts: 4.79 us -> 22.2 us
  matrix products: 16.3 us -> 0 us
  Pallas kernels: 0 us -> 14 us
  other arithmetic: 9.83 us -> 0.09 us
  starting transfers between devices: 33.4 us -> 36.9 us
    ppermute x18 -> x22, waiting for transfers between devices: 43.7 us -> 20.9 us  [the longest x6 8.71 us: per_device(): got_right = lax.ppermute(to_right, 'fsdp', right)]
    unnamed x5 -> x34, local copies, waits for them, and re-layouts: 1.78 us -> 21.1 us
    dot_general x5 -> x0, matrix products: 16.3 us -> none  [the longest x1 9.89 us: per_device(): jnp.einsum('td,sdc->stc', gathered, qkv_weight, preferred_element_type=jn...]
    pallas_call x0 -> x16, Pallas kernels: none -> 14 us  [the longest x1 4.35 us: first_pass(): call(body, jax.ShapeDtypeStruct((n_out, n_rows, columns), F32), [VMEM] *...]
    ppermute x18 -> x22, starting transfers between devices: 17.4 us -> 23.4 us  [the longest x6 10.6 us: per_device(): got_right = lax.ppermute(to_right, 'fsdp', right)]
    unnamed x6 -> x2, other arithmetic: 4.7 us -> 0.01 us
    ppermute x6, waiting for transfers between devices: 5.62 us -> 8.5 us  [ring_gather(): going_left[part] = lax.ppermute(going_left[part], 'fsdp', left)]
    concatenate x2 -> x0, other arithmetic: 1.54 us -> none  [the longest x1 0.77 us: ring_scatter(): return jnp.concatenate(done, axis=1)]
  transfers between devices with their start and end apart: 30 -> 34, of which waited for: 17 -> 18; matrix products, arithmetic and copies ran while one was open for 10% -> 0% of each run, Pallas kernels for 0% -> 8%
where the time goes in v2:
time: 107 us
  starting transfers between devices  36.9 us (34%)
  waiting for transfers between devices  33.2 us (31%)
  local copies, waits for them, and re-layouts  22.2 us (21%)
  Pallas kernels  14 us (13%)
    unnamed x34, local copies, waits for them, and re-layouts  21.1 us
    ppermute x6, starting transfers between devices, ring_gather(): going_right[part] = lax.ppermute(going_right[part], 'fsdp', right)  11.5 us
    ppermute x6, starting transfers between devices, per_device(): got_right = lax.ppermute(to_right, 'fsdp', right)  10.6 us
    ppermute x6, waiting for transfers between devices, per_device(): got_right = lax.ppermute(to_right, 'fsdp', right)  8.71 us
    ppermute x6, waiting for transfers between devices, ring_gather(): going_left[part] = lax.ppermute(going_left[part], 'fsdp', left)  8.5 us
    ppermute x6, waiting for transfers between devices, per_device(): got_left = lax.ppermute(to_left, 'fsdp', left)  7.72 us
    pallas_call x1, Pallas kernels, first_pass(): call(body, jax.ShapeDtypeStruct((n_out, n_rows, columns), F32), [VMEM] *...  4.35 us
    ppermute x6, waiting for transfers between devices, ring_gather(): going_right[part] = lax.ppermute(going_right[part], 'fsdp', right)  3.8 us
  transfers between devices with their start and end apart: 34, of which 18 were waited for; matrix products, arithmetic and copies ran while one was open for 0% of the time, Pallas kernels for 8%

profile of v2, /device:TPU:0, one launch (start us, length us, event | category | flops | bytes accessed | tf_op | source)
XLA Modules:
  0.0 106.7 jit_solution(7700355576977595637)
XLA Ops:
  0.0 1.0 fusion.2
  1.1 3.1 %collective-permute-start.9 = (bf16[32,3072]{1,0:T(8,128)(2,1)S(1)}, bf16[32,3072]{1,0:T(8,128)(2,1)S(1)}, u32[]{:S(2)}, u32[]{:S(2)}) collective-permute-start(bf16[32,3072]{1,0:T(8,128)(2,1)S(1)} %get-tuple-element.79.refs_0_), channel_id=1, source_target_pairs={{0,2},{2,4},{4,6},{6,7},{7,5},{5,3},{3,1},{1,0},{8,10},{10,12},{12... | collective-permute-start | bytes 589832 | tf_op jit(solution)/shard_map/ppermute | solution.py:70
  4.1 1.9 %collective-permute-start.1 = (bf16[32,3072]{1,0:T(8,128)(2,1)S(1)}, bf16[32,3072]{1,0:T(8,128)(2,1)S(1)}, u32[]{:S(2)}, u32[]{:S(2)}) collective-permute-start(bf16[32,3072]{1,0:T(8,128)(2,1)S(1)} %get-tuple-element.80.refs_0_), channel_id=1, source_target_pairs={{2,0},{4,2},{6,4},{7,6},{5,7},{3,5},{1,3},{0,1},{10,8},{12,10},{14... | collective-permute-start | bytes 589832 | tf_op jit(solution)/shard_map/ppermute | solution.py:71
  6.2 3.6 %collective-permute-done.9.refs_1_.after_ref = bf16[32,3072]{1,0:T(8,128)(2,1)S(1)} collective-permute-done((bf16[32,3072]{1,0:T(8,128)(2,1)S(1)}, bf16[32,3072]{1,0:T(8,128)(2,1)S(1)}, u32[]{:S(2)}, u32[]{:S(2)}) %collective-permute-start.9) | collective-permute-done | bytes 196640 | tf_op jit(solution)/shard_map/ppermute | solution.py:70
  9.8 2.1 %collective-permute-start.10 = (bf16[32,3072]{1,0:T(8,128)(2,1)S(1)}, bf16[32,3072]{1,0:T(8,128)(2,1)S(1)}, u32[]{:S(2)}, u32[]{:S(2)}) collective-permute-start(bf16[32,3072]{1,0:T(8,128)(2,1)S(1)} %collective-permute-done.9.refs_1_.after_ref), channel_id=1, source_target_pairs={{0,2},{2,4},{4,6},{6,7},{7,5},{5,3},{3,1},{1,0},{8,10},{10,12},{12... | collective-permute-start | bytes 589832 | tf_op jit(solution)/shard_map/ppermute | solution.py:70
  12.0 4.2 %collective-permute-done.1.refs_2_.after_ref = bf16[32,3072]{1,0:T(8,128)(2,1)S(1)} collective-permute-done((bf16[32,3072]{1,0:T(8,128)(2,1)S(1)}, bf16[32,3072]{1,0:T(8,128)(2,1)S(1)}, u32[]{:S(2)}, u32[]{:S(2)}) %collective-permute-start.1) | collective-permute-done | bytes 196640 | tf_op jit(solution)/shard_map/ppermute | solution.py:71
  16.2 2.0 %collective-permute-start.2 = (bf16[32,3072]{1,0:T(8,128)(2,1)S(1)}, bf16[32,3072]{1,0:T(8,128)(2,1)S(1)}, u32[]{:S(2)}, u32[]{:S(2)}) collective-permute-start(bf16[32,3072]{1,0:T(8,128)(2,1)S(1)} %collective-permute-done.refs_1_), channel_id=1, source_target_pairs={{0,2},{2,4},{4,6},{6,7},{7,5},{5,3},{3,1},{1,0},{8,10},{10,12},{12... | collective-permute-start | bytes 589832 | tf_op jit(solution)/shard_map/ppermute | solution.py:70
  18.2 2.1 %collective-permute-start.12 = (bf16[32,3072]{1,0:T(8,128)(2,1)S(1)}, bf16[32,3072]{1,0:T(8,128)(2,1)S(1)}, u32[]{:S(2)}, u32[]{:S(2)}) collective-permute-start(bf16[32,3072]{1,0:T(8,128)(2,1)S(1)} %collective-permute-done.10.after_ref.refs_3_), channel_id=1, source_target_pairs={{0,2},{2,4},{4,6},{6,7},{7,5},{5,3},{3,1},{1,0},{8,10},{10,12},{12... | collective-permute-start | bytes 589832 | tf_op jit(solution)/shard_map/ppermute | solution.py:70
  20.4 4.2 %collective-permute-done.3.refs_4_ = bf16[32,3072]{1,0:T(8,128)(2,1)S(1)} collective-permute-done((bf16[32,3072]{1,0:T(8,128)(2,1)S(1)}, bf16[32,3072]{1,0:T(8,128)(2,1)S(1)}, u32[]{:S(2)}, u32[]{:S(2)}) %collective-permute-start.3) | collective-permute-done | bytes 196640 | tf_op jit(solution)/shard_map/ppermute | solution.py:71
  24.6 2.0 %collective-permute-start.4 = (bf16[32,3072]{1,0:T(8,128)(2,1)S(1)}, bf16[32,3072]{1,0:T(8,128)(2,1)S(1)}, u32[]{:S(2)}, u32[]{:S(2)}) collective-permute-start(bf16[32,3072]{1,0:T(8,128)(2,1)S(1)} %collective-permute-done.2.refs_3_), channel_id=1, source_target_pairs={{0,2},{2,4},{4,6},{6,7},{7,5},{5,3},{3,1},{1,0},{8,10},{10,12},{12... | collective-permute-start | bytes 589832 | tf_op jit(solution)/shard_map/ppermute | solution.py:70
  26.8 2.3 %collective-permute-start.14 = (bf16[32,1536]{1,0:T(8,128)(2,1)S(1)}, bf16[32,1536]{1,0:T(8,128)(2,1)S(1)}, u32[]{:S(2)}, u32[]{:S(2)}) collective-permute-start(bf16[32,1536]{1,0:T(8,128)(2,1)S(1)} %slice.26), channel_id=1, source_target_pairs={{0,2},{2,4},{4,6},{6,7},{7,5},{5,3},{3,1},{1,0},{8,10},{10,12},{12... | collective-permute-start | bytes 294920 | tf_op jit(solution)/shard_map/ppermute | solution.py:74
  29.2 6.4 %copy-done = bf16[3,6144,512]{2,1,0:T(8,128)(2,1)S(1)} copy-done((bf16[3,6144,512]{2,1,0:T(8,128)(2,1)S(1)}, bf16[3,6144,512]{2,1,0:T(8,128)(2,1)}, u32[]{:S(2)}) %copy-start) | copy-done | bytes 18874392
  36.1 2.0 %collective-permute-start.7 = (bf16[32,1536]{1,0:T(8,128)(2,1)S(1)}, bf16[32,1536]{1,0:T(8,128)(2,1)S(1)}, u32[]{:S(2)}, u32[]{:S(2)}) collective-permute-start(bf16[32,1536]{1,0:T(8,128)(2,1)S(1)} %slice.25), channel_id=1, source_target_pairs={{2,0},{4,2},{6,4},{7,6},{5,7},{3,5},{1,3},{0,1},{10,8},{12,10},{14... | collective-permute-start | bytes 294920 | tf_op jit(solution)/shard_map/ppermute | solution.py:75
  38.3 0.8 slice-done.1
  39.0 1.2 %slice-done.2 = s8[4194304]{0:T(1024)(128)(4,1)S(1)} async-done(((s8[18874368]{0:T(1024)(128)(4,1)}), s8[4194304]{0:T(1024)(128)(4,1)S(1)}, s32[]{:S(2)}) %slice-start.2) | async-done | bytes 4194328
  40.2 1.3 %slice-done.3 = s8[4194304]{0:T(1024)(128)(4,1)S(1)} async-done(((s8[18874368]{0:T(1024)(128)(4,1)}), s8[4194304]{0:T(1024)(128)(4,1)S(1)}, s32[]{:S(2)}) %slice-start.3) | async-done | bytes 4194328
  42.1 4.3 %first_pass.1.refs_11_.first_ref = f32[3,256,512]{2,1,0:T(8,128)S(1)} custom-call(bf16[32,3072]{1,0:T(8,128)(2,1)S(1)} %get-tuple-element.79.refs_0_, bf16[32,3072]{1,0:T(8,128)(2,1)S(1)} %collective-permute-done.9.refs_1_.after_ref, bf16[32,3072]{1,0:T(8,128)(2,1)S(1)} %collective-permute-done.8.after_ref.refs_2_, ...), custom_call_target="tpu_custom_call" | custom-call | flops 2415919104 | bytes 9437184 | tf_op jit(solution)/shard_map/first_pass/pallas_call | solution.py:109
  46.5 2.3 %keys_and_values.1 = (bf16[256,512]{1,0:T(8,128)(2,1)S(1)}, bf16[256,512]{1,0:T(8,128)(2,1)S(1)}, bf16[4,128,128]{2,1,0:T(8,128)(2,1)S(1)}, bf16[256,3072]{1,0:T(8,128)(2,1)S(1)}) custom-call(bf16[32,3072]{1,0:T(8,128)(2,1)S(1)} %get-tuple-element.80.refs_0_, bf16[32,3072]{1,0:T(8,128)(2,1)S(1)} %collective-permute-done.refs_1_, ...), custom_call_target="tpu_custom_call" | custom-call | flops 1610612736 | bytes 6291456 | tf_op jit(solution)/shard_map/keys_and_values/pallas_call | solution.py:151
  48.8 1.2 %copy-done.4 = bf16[256,3072]{1,0:T(8,128)(2,1)} copy-done((bf16[256,3072]{1,0:T(8,128)(2,1)}, bf16[256,3072]{1,0:T(8,128)(2,1)S(1)}, u32[]{:S(2)}) %copy-start.4) | copy-done | bytes 1572888
  49.9 1.3 %collective-permute-done.16 = bf16[4,128,128]{2,1,0:T(8,128)(2,1)S(1)} collective-permute-done((bf16[4,128,128]{2,1,0:T(8,128)(2,1)S(1)}, bf16[4,128,128]{2,1,0:T(8,128)(2,1)S(1)}, u32[]{:S(2)}, u32[]{:S(2)}) %collective-permute-start.16) | collective-permute-done | bytes 131104 | tf_op jit(solution)/shard_map/ppermute | solution.py:341
  51.3 2.0 %collective-permute-start.17 = (bf16[4,128,128]{2,1,0:T(8,128)(2,1)S(1)}, bf16[4,128,128]{2,1,0:T(8,128)(2,1)S(1)}, u32[]{:S(2)}, u32[]{:S(2)}) collective-permute-start(bf16[4,128,128]{2,1,0:T(8,128)(2,1)S(1)} %fusion.1), channel_id=1, source_target_pairs={{0,16},{8,24},{16,0},{24,8},{1,17},{9,25},{17,1},{25,9},{2,18},{10... | collective-permute-start | bytes 393224 | tf_op jit(solution)/shard_map/ppermute | solution.py:341
  53.3 6.4 %copy-done.1 = bf16[3,6144,512]{2,1,0:T(8,128)(2,1)S(1)} copy-done((bf16[3,6144,512]{2,1,0:T(8,128)(2,1)S(1)}, bf16[3,6144,512]{2,1,0:T(8,128)(2,1)}, u32[]{:S(2)}) %copy-start.1) | copy-done | bytes 18874392
  59.9 1.9 %slice-done.6 = s8[4194304]{0:T(1024)(128)(4,1)S(1)} async-done(((s8[6291456]{0:T(1024)(128)(4,1)}), s8[4194304]{0:T(1024)(128)(4,1)S(1)}, s32[]{:S(2)}) %slice-start.6) | async-done | bytes 4194328
  62.3 1.0 copy-done.3
  63.8 2.6 %queries_within.1 = (bf16[256,512]{1,0:T(8,128)(2,1)S(1)}, f32[256,512]{1,0:T(8,128)S(1)}) custom-call(bf16[256,3072]{1,0:T(8,128)(2,1)S(1)} %copy-done.5, bf16[3072,512]{1,0:T(8,128)(2,1)S(1)} %fetch.6.weight_ref, f32[3,256,512]{2,1,0:T(8,128)S(1)} %copy-done.3, bf16[256,512]{1,0:T(8,128)(2,1)S(1)} %get-tuple-element.43.k_ref, ...), custom_call_target="tpu_custom_call" | custom-call | flops 939524096 | bytes 3145728 | tf_op jit(solution)/shard_map/queries_within/pallas_call | solution.py:203
  66.5 1.3 %attend_and_project.1 = (bf16[256,512]{1,0:T(8,128)(2,1)S(1)}, bf16[32,3072]{1,0:T(8,128)(2,1)S(1)}, bf16[32,3072]{1,0:T(8,128)(2,1)S(1)}, bf16[32,3072]{1,0:T(8...) custom-call(bf16[256,512]{1,0:T(8,128)(2,1)S(1)} %get-tuple-element., ...), custom_call_target="tpu_custom_call" | custom-call | flops 805306368 | bytes 3145728 | tf_op jit(solution)/shard_map/attend_and_project/pallas_call | solution.py:260
  67.8 1.0 project_rest.1
  68.9 1.6 %collective-permute-start.26 = (bf16[32,1536]{1,0:T(8,128)(2,1)S(1)}, bf16[32,1536]{1,0:T(8,128)(2,1)S(1)}, u32[]{:S(2)}, u32[]{:S(2)}) collective-permute-start(bf16[32,1536]{1,0:T(8,128)(2,1)S(1)} %get-tuple-element.68), channel_id=1, source_target_pairs={{0,2},{2,4},{4,6},{6,7},{7,5},{5,3},{3,1},{1,0},{8,10},{10,12},{12... | collective-permute-start | bytes 294920 | tf_op jit(solution)/shard_map/ppermute | solution.py:377
  70.9 1.6 %collective-permute-start.18 = (bf16[32,1536]{1,0:T(8,128)(2,1)S(1)}, bf16[32,1536]{1,0:T(8,128)(2,1)S(1)}, u32[]{:S(2)}, u32[]{:S(2)}) collective-permute-start(bf16[32,1536]{1,0:T(8,128)(2,1)S(1)} %get-tuple-element.52), channel_id=1, source_target_pairs={{0,2},{2,4},{4,6},{6,7},{7,5},{5,3},{3,1},{1,0},{8,10},{10,12},{12... | collective-permute-start | bytes 294920 | tf_op jit(solution)/shard_map/ppermute | solution.py:377
  73.0 1.3 %collective-permute-done.26.gr = bf16[32,1536]{1,0:T(8,128)(2,1)S(1)} collective-permute-done((bf16[32,1536]{1,0:T(8,128)(2,1)S(1)}, bf16[32,1536]{1,0:T(8,128)(2,1)S(1)}, u32[]{:S(2)}, u32[]{:S(2)}) %collective-permute-start.26) | collective-permute-done | bytes 98336 | tf_op jit(solution)/shard_map/ppermute | solution.py:377
  74.3 1.8 %collective-permute-done.27.gl = bf16[32,1536]{1,0:T(8,128)(2,1)S(1)} collective-permute-done((bf16[32,1536]{1,0:T(8,128)(2,1)S(1)}, bf16[32,1536]{1,0:T(8,128)(2,1)S(1)}, u32[]{:S(2)}, u32[]{:S(2)}) %collective-permute-start.27) | collective-permute-done | bytes 98336 | tf_op jit(solution)/shard_map/ppermute | solution.py:378
  76.1 1.6 %collective-permute-start.28 = (bf16[32,3072]{1,0:T(8,128)(2,1)S(1)}, bf16[32,3072]{1,0:T(8,128)(2,1)S(1)}, u32[]{:S(2)}, u32[]{:S(2)}) collective-permute-start(bf16[32,3072]{1,0:T(8,128)(2,1)S(1)} %get-tuple-element.71), channel_id=1, source_target_pairs={{0,2},{2,4},{4,6},{6,7},{7,5},{5,3},{3,1},{1,0},{8,10},{10,12},{12... | collective-permute-start | bytes 589832 | tf_op jit(solution)/shard_map/ppermute | solution.py:383
  78.3 1.6 %collective-permute-start.20 = (bf16[32,3072]{1,0:T(8,128)(2,1)S(1)}, bf16[32,3072]{1,0:T(8,128)(2,1)S(1)}, u32[]{:S(2)}, u32[]{:S(2)}) collective-permute-start(bf16[32,3072]{1,0:T(8,128)(2,1)S(1)} %get-tuple-element.55), channel_id=1, source_target_pairs={{0,2},{2,4},{4,6},{6,7},{7,5},{5,3},{3,1},{1,0},{8,10},{10,12},{12... | collective-permute-start | bytes 589832 | tf_op jit(solution)/shard_map/ppermute | solution.py:383
  80.4 3.2 %collective-permute-done.28.gr = bf16[32,3072]{1,0:T(8,128)(2,1)S(1)} collective-permute-done((bf16[32,3072]{1,0:T(8,128)(2,1)S(1)}, bf16[32,3072]{1,0:T(8,128)(2,1)S(1)}, u32[]{:S(2)}, u32[]{:S(2)}) %collective-permute-start.28) | collective-permute-done | bytes 196640 | tf_op jit(solution)/shard_map/ppermute | solution.py:383
  83.5 1.3 %collective-permute-done.29.gl = bf16[32,3072]{1,0:T(8,128)(2,1)S(1)} collective-permute-done((bf16[32,3072]{1,0:T(8,128)(2,1)S(1)}, bf16[32,3072]{1,0:T(8,128)(2,1)S(1)}, u32[]{:S(2)}, u32[]{:S(2)}) %collective-permute-start.29) | collective-permute-done | bytes 196640 | tf_op jit(solution)/shard_map/ppermute | solution.py:384
  84.9 1.7 %collective-permute-start.30 = (bf16[32,3072]{1,0:T(8,128)(2,1)S(1)}, bf16[32,3072]{1,0:T(8,128)(2,1)S(1)}, u32[]{:S(2)}, u32[]{:S(2)}) collective-permute-start(bf16[32,3072]{1,0:T(8,128)(2,1)S(1)} %get-tuple-element.74), channel_id=1, source_target_pairs={{0,2},{2,4},{4,6},{6,7},{7,5},{5,3},{3,1},{1,0},{8,10},{10,12},{12... | collective-permute-start | bytes 589832 | tf_op jit(solution)/shard_map/ppermute | solution.py:383
  87.0 0.7 collective-permute-done.20.gr
  87.8 1.3 %collective-permute-done.21.gl = bf16[32,3072]{1,0:T(8,128)(2,1)S(1)} collective-permute-done((bf16[32,3072]{1,0:T(8,128)(2,1)S(1)}, bf16[32,3072]{1,0:T(8,128)(2,1)S(1)}, u32[]{:S(2)}, u32[]{:S(2)}) %collective-permute-start.21) | collective-permute-done | bytes 196640 | tf_op jit(solution)/shard_map/ppermute | solution.py:384
  89.1 1.7 %collective-permute-start.22 = (bf16[32,3072]{1,0:T(8,128)(2,1)S(1)}, bf16[32,3072]{1,0:T(8,128)(2,1)S(1)}, u32[]{:S(2)}, u32[]{:S(2)}) collective-permute-start(bf16[32,3072]{1,0:T(8,128)(2,1)S(1)} %get-tuple-element.58), channel_id=1, source_target_pairs={{0,2},{2,4},{4,6},{6,7},{7,5},{5,3},{3,1},{1,0},{8,10},{10,12},{12... | collective-permute-start | bytes 589832 | tf_op jit(solution)/shard_map/ppermute | solution.py:383
  92.0 1.4 %collective-permute-done.31.gl = bf16[32,3072]{1,0:T(8,128)(2,1)S(1)} collective-permute-done((bf16[32,3072]{1,0:T(8,128)(2,1)S(1)}, bf16[32,3072]{1,0:T(8,128)(2,1)S(1)}, u32[]{:S(2)}, u32[]{:S(2)}) %collective-permute-start.31) | collective-permute-done | bytes 196640 | tf_op jit(solution)/shard_map/ppermute | solution.py:384
  93.4 2.4 %collective-permute-start.32 = (bf16[32,3072]{1,0:T(8,128)(2,1)S(1)}, bf16[32,3072]{1,0:T(8,128)(2,1)S(1)}, u32[]{:S(2)}, u32[]{:S(2)}) collective-permute-start(bf16[32,3072]{1,0:T(8,128)(2,1)S(1)} %get-tuple-element.77), channel_id=1, source_target_pairs={{0,2},{2,4},{4,6},{6,7},{7,5},{5,3},{3,1},{1,0},{8,10},{10,12},{12... | collective-permute-start | bytes 589832 | tf_op jit(solution)/shard_map/ppermute | solution.py:383
  95.8 1.2 %collective-permute-done.22.gr = bf16[32,3072]{1,0:T(8,128)(2,1)S(1)} collective-permute-done((bf16[32,3072]{1,0:T(8,128)(2,1)S(1)}, bf16[32,3072]{1,0:T(8,128)(2,1)S(1)}, u32[]{:S(2)}, u32[]{:S(2)}) %collective-permute-start.22) | collective-permute-done | bytes 196640 | tf_op jit(solution)/shard_map/ppermute | solution.py:383
  97.0 1.5 %collective-permute-done.23.gl = bf16[32,3072]{1,0:T(8,128)(2,1)S(1)} collective-permute-done((bf16[32,3072]{1,0:T(8,128)(2,1)S(1)}, bf16[32,3072]{1,0:T(8,128)(2,1)S(1)}, u32[]{:S(2)}, u32[]{:S(2)}) %collective-permute-start.23) | collective-permute-done | bytes 196640 | tf_op jit(solution)/shard_map/ppermute | solution.py:384
  98.6 1.5 %collective-permute-start.24 = (bf16[32,3072]{1,0:T(8,128)(2,1)S(1)}, bf16[32,3072]{1,0:T(8,128)(2,1)S(1)}, u32[]{:S(2)}, u32[]{:S(2)}) collective-permute-start(bf16[32,3072]{1,0:T(8,128)(2,1)S(1)} %get-tuple-element.61), channel_id=1, source_target_pairs={{0,2},{2,4},{4,6},{6,7},{7,5},{5,3},{3,1},{1,0},{8,10},{10,12},{12... | collective-permute-start | bytes 589832 | tf_op jit(solution)/shard_map/ppermute | solution.py:383
  100.7 0.8 collective-permute-done.33.refs_5_
  101.5 2.8 %collective-permute-done.24.refs_1_ = bf16[32,3072]{1,0:T(8,128)(2,1)S(1)} collective-permute-done((bf16[32,3072]{1,0:T(8,128)(2,1)S(1)}, bf16[32,3072]{1,0:T(8,128)(2,1)S(1)}, u32[]{:S(2)}, u32[]{:S(2)}) %collective-permute-start.24) | collective-permute-done | bytes 196640 | tf_op jit(solution)/shard_map/ppermute | solution.py:383
  104.4 1.5 %collective-permute-done.25.refs_2_ = bf16[32,3072]{1,0:T(8,128)(2,1)S(1)} collective-permute-done((bf16[32,3072]{1,0:T(8,128)(2,1)S(1)}, bf16[32,3072]{1,0:T(8,128)(2,1)S(1)}, u32[]{:S(2)}, u32[]{:S(2)}) %collective-permute-start.25) | collective-permute-done | bytes 196640 | tf_op jit(solution)/shard_map/ppermute | solution.py:384
  105.8 0.9 finish.1
  (79 shorter events, 7.3 us)
Async XLA Ops:
  1.1 8.7 %collective-permute-start.9 = (bf16[32,3072]{1,0:T(8,128)(2,1)S(1)}, bf16[32,3072]{1,0:T(8,128)(2,1)S(1)}, u32[]{:S(2)}, u32[]{:S(2)}) collective-permute-start(bf16[32,3072]{1,0:T(8,128)(2,1)S(1)} %get-tuple-element.79.refs_0_), channel_id=1, source_target_pairs={{0,2},{2,4},{4,6},{6,7},{7,5},{5,3},{3,1},{1,0},{8,10},{10,12},{12... | collective-permute-start | bytes 589832 | tf_op jit(solution)/shard_map/ppermute | solution.py:70
  4.1 7.8 %collective-permute-start.8 = (bf16[32,3072]{1,0:T(8,128)(2,1)S(1)}, bf16[32,3072]{1,0:T(8,128)(2,1)S(1)}, u32[]{:S(2)}, u32[]{:S(2)}) collective-permute-start(bf16[32,3072]{1,0:T(8,128)(2,1)S(1)} %get-tuple-element.79.refs_0_), channel_id=1, source_target_pairs={{2,0},{4,2},{6,4},{7,6},{5,7},{3,5},{1,3},{0,1},{10,8},{12,10},{14... | collective-permute-start | bytes 589832 | tf_op jit(solution)/shard_map/ppermute | solution.py:71
  4.1 12.0 %collective-permute-start.1 = (bf16[32,3072]{1,0:T(8,128)(2,1)S(1)}, bf16[32,3072]{1,0:T(8,128)(2,1)S(1)}, u32[]{:S(2)}, u32[]{:S(2)}) collective-permute-start(bf16[32,3072]{1,0:T(8,128)(2,1)S(1)} %get-tuple-element.80.refs_0_), channel_id=1, source_target_pairs={{2,0},{4,2},{6,4},{7,6},{5,7},{3,5},{1,3},{0,1},{10,8},{12,10},{14... | collective-permute-start | bytes 589832 | tf_op jit(solution)/shard_map/ppermute | solution.py:71
  6.1 10.1 %collective-permute-start = (bf16[32,3072]{1,0:T(8,128)(2,1)S(1)}, bf16[32,3072]{1,0:T(8,128)(2,1)S(1)}, u32[]{:S(2)}, u32[]{:S(2)}) collective-permute-start(bf16[32,3072]{1,0:T(8,128)(2,1)S(1)} %get-tuple-element.80.refs_0_), channel_id=1, source_target_pairs={{0,2},{2,4},{4,6},{6,7},{7,5},{5,3},{3,1},{1,0},{8,10},{10,12},{12... | collective-permute-start | bytes 589832 | tf_op jit(solution)/shard_map/ppermute | solution.py:70
  9.8 8.4 %collective-permute-start.10 = (bf16[32,3072]{1,0:T(8,128)(2,1)S(1)}, bf16[32,3072]{1,0:T(8,128)(2,1)S(1)}, u32[]{:S(2)}, u32[]{:S(2)}) collective-permute-start(bf16[32,3072]{1,0:T(8,128)(2,1)S(1)} %collective-permute-done.9.refs_1_.after_ref), channel_id=1, source_target_pairs={{0,2},{2,4},{4,6},{6,7},{7,5},{5,3},{3,1},{1,0},{8,10},{10,12},{12... | collective-permute-start | bytes 589832 | tf_op jit(solution)/shard_map/ppermute | solution.py:70
  12.0 8.4 %collective-permute-start.11 = (bf16[32,3072]{1,0:T(8,128)(2,1)S(1)}, bf16[32,3072]{1,0:T(8,128)(2,1)S(1)}, u32[]{:S(2)}, u32[]{:S(2)}) collective-permute-start(bf16[32,3072]{1,0:T(8,128)(2,1)S(1)} %collective-permute-done.8.after_ref.refs_2_), channel_id=1, source_target_pairs={{2,0},{4,2},{6,4},{7,6},{5,7},{3,5},{1,3},{0,1},{10,8},{12,10},{14... | collective-permute-start | bytes 589832 | tf_op jit(solution)/shard_map/ppermute | solution.py:71
  16.2 8.4 %collective-permute-start.3 = (bf16[32,3072]{1,0:T(8,128)(2,1)S(1)}, bf16[32,3072]{1,0:T(8,128)(2,1)S(1)}, u32[]{:S(2)}, u32[]{:S(2)}) collective-permute-start(bf16[32,3072]{1,0:T(8,128)(2,1)S(1)} %collective-permute-done.1.refs_2_.after_ref), channel_id=1, source_target_pairs={{2,0},{4,2},{6,4},{7,6},{5,7},{3,5},{1,3},{0,1},{10,8},{12,10},{14... | collective-permute-start | bytes 589832 | tf_op jit(solution)/shard_map/ppermute | solution.py:71
  16.2 8.4 %collective-permute-start.2 = (bf16[32,3072]{1,0:T(8,128)(2,1)S(1)}, bf16[32,3072]{1,0:T(8,128)(2,1)S(1)}, u32[]{:S(2)}, u32[]{:S(2)}) collective-permute-start(bf16[32,3072]{1,0:T(8,128)(2,1)S(1)} %collective-permute-done.refs_1_), channel_id=1, source_target_pairs={{0,2},{2,4},{4,6},{6,7},{7,5},{5,3},{3,1},{1,0},{8,10},{10,12},{12... | collective-permute-start | bytes 589832 | tf_op jit(solution)/shard_map/ppermute | solution.py:70
  18.2 8.6 %collective-permute-start.12 = (bf16[32,3072]{1,0:T(8,128)(2,1)S(1)}, bf16[32,3072]{1,0:T(8,128)(2,1)S(1)}, u32[]{:S(2)}, u32[]{:S(2)}) collective-permute-start(bf16[32,3072]{1,0:T(8,128)(2,1)S(1)} %collective-permute-done.10.after_ref.refs_3_), channel_id=1, source_target_pairs={{0,2},{2,4},{4,6},{6,7},{7,5},{5,3},{3,1},{1,0},{8,10},{10,12},{12... | collective-permute-start | bytes 589832 | tf_op jit(solution)/shard_map/ppermute | solution.py:70
  20.4 8.7 %collective-permute-start.13 = (bf16[32,3072]{1,0:T(8,128)(2,1)S(1)}, bf16[32,3072]{1,0:T(8,128)(2,1)S(1)}, u32[]{:S(2)}, u32[]{:S(2)}) collective-permute-start(bf16[32,3072]{1,0:T(8,128)(2,1)S(1)} %collective-permute-done.11.refs_4_), channel_id=1, source_target_pairs={{2,0},{4,2},{6,4},{7,6},{5,7},{3,5},{1,3},{0,1},{10,8},{12,10},{14... | collective-permute-start | bytes 589832 | tf_op jit(solution)/shard_map/ppermute | solution.py:71
  24.6 11.5 %collective-permute-start.5 = (bf16[32,3072]{1,0:T(8,128)(2,1)S(1)}, bf16[32,3072]{1,0:T(8,128)(2,1)S(1)}, u32[]{:S(2)}, u32[]{:S(2)}) collective-permute-start(bf16[32,3072]{1,0:T(8,128)(2,1)S(1)} %collective-permute-done.3.refs_4_), channel_id=1, source_target_pairs={{2,0},{4,2},{6,4},{7,6},{5,7},{3,5},{1,3},{0,1},{10,8},{12,10},{14... | collective-permute-start | bytes 589832 | tf_op jit(solution)/shard_map/ppermute | solution.py:71
  24.6 11.2 %copy-start.7 = (bf16[32,3072]{1,0:T(8,128)(2,1)}, bf16[32,3072]{1,0:T(8,128)(2,1)S(1)}, u32[]{:S(2)}) copy-start(bf16[32,3072]{1,0:T(8,128)(2,1)S(1)} %collective-permute-done.2.refs_3_) | copy-start | bytes 589828
  24.6 13.5 %collective-permute-start.4 = (bf16[32,3072]{1,0:T(8,128)(2,1)S(1)}, bf16[32,3072]{1,0:T(8,128)(2,1)S(1)}, u32[]{:S(2)}, u32[]{:S(2)}) collective-permute-start(bf16[32,3072]{1,0:T(8,128)(2,1)S(1)} %collective-permute-done.2.refs_3_), channel_id=1, source_target_pairs={{0,2},{2,4},{4,6},{6,7},{7,5},{5,3},{3,1},{1,0},{8,10},{10,12},{12... | collective-permute-start | bytes 589832 | tf_op jit(solution)/shard_map/ppermute | solution.py:70
  26.8 11.4 %collective-permute-start.14 = (bf16[32,1536]{1,0:T(8,128)(2,1)S(1)}, bf16[32,1536]{1,0:T(8,128)(2,1)S(1)}, u32[]{:S(2)}, u32[]{:S(2)}) collective-permute-start(bf16[32,1536]{1,0:T(8,128)(2,1)S(1)} %slice.26), channel_id=1, source_target_pairs={{0,2},{2,4},{4,6},{6,7},{7,5},{5,3},{3,1},{1,0},{8,10},{10,12},{12... | collective-permute-start | bytes 294920 | tf_op jit(solution)/shard_map/ppermute | solution.py:74
  29.1 9.1 %collective-permute-start.15 = (bf16[32,1536]{1,0:T(8,128)(2,1)S(1)}, bf16[32,1536]{1,0:T(8,128)(2,1)S(1)}, u32[]{:S(2)}, u32[]{:S(2)}) collective-permute-start(bf16[32,1536]{1,0:T(8,128)(2,1)S(1)} %slice.27), channel_id=1, source_target_pairs={{2,0},{4,2},{6,4},{7,6},{5,7},{3,5},{1,3},{0,1},{10,8},{12,10},{14... | collective-permute-start | bytes 294920 | tf_op jit(solution)/shard_map/ppermute | solution.py:75
  29.2 6.4 %copy-start = (bf16[3,6144,512]{2,1,0:T(8,128)(2,1)S(1)}, bf16[3,6144,512]{2,1,0:T(8,128)(2,1)}, u32[]{:S(2)}) copy-start(bf16[3,6144,512]{2,1,0:T(8,128)(2,1)} %source_ref.6) | copy-start | bytes 56623108
  35.6 2.7 %slice-start = ((s8[18874368]{0:T(1024)(128)(4,1)}), s8[4194304]{0:T(1024)(128)(4,1)S(1)}, s32[]{:S(2)}) async-start(s8[18874368]{0:T(1024)(128)(4,1)} %bitcast.1), calls=%async_computation | async-start | bytes 8388608
  35.6 3.5 %slice-start.1 = ((s8[18874368]{0:T(1024)(128)(4,1)}), s8[4194304]{0:T(1024)(128)(4,1)S(1)}, s32[]{:S(2)}) async-start(s8[18874368]{0:T(1024)(128)(4,1)} %bitcast.1), calls=%async_computation.1 | async-start | bytes 8388608
  35.6 4.7 %slice-start.2 = ((s8[18874368]{0:T(1024)(128)(4,1)}), s8[4194304]{0:T(1024)(128)(4,1)S(1)}, s32[]{:S(2)}) async-start(s8[18874368]{0:T(1024)(128)(4,1)} %bitcast.1), calls=%async_computation.2 | async-start | bytes 8388608
  35.8 5.7 %slice-start.3 = ((s8[18874368]{0:T(1024)(128)(4,1)}), s8[4194304]{0:T(1024)(128)(4,1)S(1)}, s32[]{:S(2)}) async-start(s8[18874368]{0:T(1024)(128)(4,1)} %bitcast.1), calls=%async_computation.3 | async-start | bytes 8388608
  35.8 6.3 %slice-start.4 = ((s8[18874368]{0:T(1024)(128)(4,1)}), s8[2097152]{0:T(1024)(128)(4,1)S(1)}, s32[]{:S(2)}) async-start(s8[18874368]{0:T(1024)(128)(4,1)} %bitcast.1), calls=%async_computation.4 | async-start | bytes 4194304
  36.1 10.4 %collective-permute-start.7 = (bf16[32,1536]{1,0:T(8,128)(2,1)S(1)}, bf16[32,1536]{1,0:T(8,128)(2,1)S(1)}, u32[]{:S(2)}, u32[]{:S(2)}) collective-permute-start(bf16[32,1536]{1,0:T(8,128)(2,1)S(1)} %slice.25), channel_id=1, source_target_pairs={{2,0},{4,2},{6,4},{7,6},{5,7},{3,5},{1,3},{0,1},{10,8},{12,10},{14... | collective-permute-start | bytes 294920 | tf_op jit(solution)/shard_map/ppermute | solution.py:75
  38.1 8.4 %copy-start.8 = (bf16[32,3072]{1,0:T(8,128)(2,1)S(1)}, bf16[32,3072]{1,0:T(8,128)(2,1)}, u32[]{:S(2)}) copy-start(bf16[32,3072]{1,0:T(8,128)(2,1)} %copy-done.7) | copy-start | bytes 589828
  38.1 8.4 %collective-permute-start.6 = (bf16[32,1536]{1,0:T(8,128)(2,1)S(1)}, bf16[32,1536]{1,0:T(8,128)(2,1)S(1)}, u32[]{:S(2)}, u32[]{:S(2)}) collective-permute-start(bf16[32,1536]{1,0:T(8,128)(2,1)S(1)} %slice.24), channel_id=1, source_target_pairs={{0,2},{2,4},{4,6},{6,7},{7,5},{5,3},{3,1},{1,0},{8,10},{10,12},{12... | collective-permute-start | bytes 294920 | tf_op jit(solution)/shard_map/ppermute | solution.py:74
  46.4 2.3 %copy-start.2 = (f32[3,256,512]{2,1,0:T(8,128)}, f32[3,256,512]{2,1,0:T(8,128)S(1)}, u32[]{:S(2)}) copy-start(f32[3,256,512]{2,1,0:T(8,128)S(1)} %first_pass.1.refs_11_.first_ref) | copy-start | bytes 4718596
  46.5 13.5 %slice-start.5 = ((s8[6291456]{0:T(1024)(128)(4,1)}), s8[2097152]{0:T(1024)(128)(4,1)S(1)}, s32[]{:S(2)}) async-start(s8[6291456]{0:T(1024)(128)(4,1)} %bitcast.3), calls=%async_computation.5 | async-start | bytes 4194304
  49.9 1.3 %collective-permute-start.16 = (bf16[4,128,128]{2,1,0:T(8,128)(2,1)S(1)}, bf16[4,128,128]{2,1,0:T(8,128)(2,1)S(1)}, u32[]{:S(2)}, u32[]{:S(2)}) collective-permute-start(bf16[4,128,128]{2,1,0:T(8,128)(2,1)S(1)} %get-tuple-element.47), channel_id=1, source_target_pairs={{0,8},{8,0},{16,24},{24,16},{1,9},{9,1},{17,25},{25,17},{2,10},{10... | collective-permute-start | bytes 393224 | tf_op jit(solution)/shard_map/ppermute | solution.py:341
  51.3 15.1 %collective-permute-start.17 = (bf16[4,128,128]{2,1,0:T(8,128)(2,1)S(1)}, bf16[4,128,128]{2,1,0:T(8,128)(2,1)S(1)}, u32[]{:S(2)}, u32[]{:S(2)}) collective-permute-start(bf16[4,128,128]{2,1,0:T(8,128)(2,1)S(1)} %fusion.1), channel_id=1, source_target_pairs={{0,16},{8,24},{16,0},{24,8},{1,17},{9,25},{17,1},{25,9},{2,18},{10... | collective-permute-start | bytes 393224 | tf_op jit(solution)/shard_map/ppermute | solution.py:341
  53.3 6.4 %copy-start.1 = (bf16[3,6144,512]{2,1,0:T(8,128)(2,1)S(1)}, bf16[3,6144,512]{2,1,0:T(8,128)(2,1)}, u32[]{:S(2)}) copy-start(bf16[3,6144,512]{2,1,0:T(8,128)(2,1)} %source_ref.6) | copy-start | bytes 56623108
  59.7 2.2 %slice-start.6 = ((s8[6291456]{0:T(1024)(128)(4,1)}), s8[4194304]{0:T(1024)(128)(4,1)S(1)}, s32[]{:S(2)}) async-start(s8[6291456]{0:T(1024)(128)(4,1)} %bitcast.3), calls=%async_computation.6 | async-start | bytes 8388608
  63.8 2.7 %copy-start.6 = (f32[4,128,128]{2,1,0:T(8,128)S(1)}, f32[4,128,128]{2,1,0:T(8,128)}, u32[]{:S(2)}) copy-start(f32[4,128,128]{2,1,0:T(8,128)} %initial_ref.1) | copy-start | bytes 786436
  63.8 2.7 %copy-start.9 = (f32[512]{0:T(512)S(1)}, f32[512]{0:T(512)}, u32[]{:S(2)}) copy-start(f32[512]{0:T(512)} %param.8) | copy-start | bytes 6148
  68.9 5.4 %collective-permute-start.26 = (bf16[32,1536]{1,0:T(8,128)(2,1)S(1)}, bf16[32,1536]{1,0:T(8,128)(2,1)S(1)}, u32[]{:S(2)}, u32[]{:S(2)}) collective-permute-start(bf16[32,1536]{1,0:T(8,128)(2,1)S(1)} %get-tuple-element.68), channel_id=1, source_target_pairs={{0,2},{2,4},{4,6},{6,7},{7,5},{5,3},{3,1},{1,0},{8,10},{10,12},{12... | collective-permute-start | bytes 294920 | tf_op jit(solution)/shard_map/ppermute | solution.py:377
  70.5 5.6 %collective-permute-start.27 = (bf16[32,1536]{1,0:T(8,128)(2,1)S(1)}, bf16[32,1536]{1,0:T(8,128)(2,1)S(1)}, u32[]{:S(2)}, u32[]{:S(2)}) collective-permute-start(bf16[32,1536]{1,0:T(8,128)(2,1)S(1)} %get-tuple-element.70), channel_id=1, source_target_pairs={{2,0},{4,2},{6,4},{7,6},{5,7},{3,5},{1,3},{0,1},{10,8},{12,10},{14... | collective-permute-start | bytes 294920 | tf_op jit(solution)/shard_map/ppermute | solution.py:378
  70.9 7.3 %collective-permute-start.18 = (bf16[32,1536]{1,0:T(8,128)(2,1)S(1)}, bf16[32,1536]{1,0:T(8,128)(2,1)S(1)}, u32[]{:S(2)}, u32[]{:S(2)}) collective-permute-start(bf16[32,1536]{1,0:T(8,128)(2,1)S(1)} %get-tuple-element.52), channel_id=1, source_target_pairs={{0,2},{2,4},{4,6},{6,7},{7,5},{5,3},{3,1},{1,0},{8,10},{10,12},{12... | collective-permute-start | bytes 294920 | tf_op jit(solution)/shard_map/ppermute | solution.py:377
  72.5 5.7 %collective-permute-start.19 = (bf16[32,1536]{1,0:T(8,128)(2,1)S(1)}, bf16[32,1536]{1,0:T(8,128)(2,1)S(1)}, u32[]{:S(2)}, u32[]{:S(2)}) collective-permute-start(bf16[32,1536]{1,0:T(8,128)(2,1)S(1)} %get-tuple-element.54), channel_id=1, source_target_pairs={{2,0},{4,2},{6,4},{7,6},{5,7},{3,5},{1,3},{0,1},{10,8},{12,10},{14... | collective-permute-start | bytes 294920 | tf_op jit(solution)/shard_map/ppermute | solution.py:378
  76.1 7.4 %collective-permute-start.28 = (bf16[32,3072]{1,0:T(8,128)(2,1)S(1)}, bf16[32,3072]{1,0:T(8,128)(2,1)S(1)}, u32[]{:S(2)}, u32[]{:S(2)}) collective-permute-start(bf16[32,3072]{1,0:T(8,128)(2,1)S(1)} %get-tuple-element.71), channel_id=1, source_target_pairs={{0,2},{2,4},{4,6},{6,7},{7,5},{5,3},{3,1},{1,0},{8,10},{10,12},{12... | collective-permute-start | bytes 589832 | tf_op jit(solution)/shard_map/ppermute | solution.py:383
  77.8 7.1 %collective-permute-start.29 = (bf16[32,3072]{1,0:T(8,128)(2,1)S(1)}, bf16[32,3072]{1,0:T(8,128)(2,1)S(1)}, u32[]{:S(2)}, u32[]{:S(2)}) collective-permute-start(bf16[32,3072]{1,0:T(8,128)(2,1)S(1)} %get-tuple-element.73), channel_id=1, source_target_pairs={{2,0},{4,2},{6,4},{7,6},{5,7},{3,5},{1,3},{0,1},{10,8},{12,10},{14... | collective-permute-start | bytes 589832 | tf_op jit(solution)/shard_map/ppermute | solution.py:384
  78.3 9.5 %collective-permute-start.20 = (bf16[32,3072]{1,0:T(8,128)(2,1)S(1)}, bf16[32,3072]{1,0:T(8,128)(2,1)S(1)}, u32[]{:S(2)}, u32[]{:S(2)}) collective-permute-start(bf16[32,3072]{1,0:T(8,128)(2,1)S(1)} %get-tuple-element.55), channel_id=1, source_target_pairs={{0,2},{2,4},{4,6},{6,7},{7,5},{5,3},{3,1},{1,0},{8,10},{10,12},{12... | collective-permute-start | bytes 589832 | tf_op jit(solution)/shard_map/ppermute | solution.py:383
  79.9 9.1 %collective-permute-start.21 = (bf16[32,3072]{1,0:T(8,128)(2,1)S(1)}, bf16[32,3072]{1,0:T(8,128)(2,1)S(1)}, u32[]{:S(2)}, u32[]{:S(2)}) collective-permute-start(bf16[32,3072]{1,0:T(8,128)(2,1)S(1)} %get-tuple-element.57), channel_id=1, source_target_pairs={{2,0},{4,2},{6,4},{7,6},{5,7},{3,5},{1,3},{0,1},{10,8},{12,10},{14... | collective-permute-start | bytes 589832 | tf_op jit(solution)/shard_map/ppermute | solution.py:384
  84.9 7.0 %collective-permute-start.30 = (bf16[32,3072]{1,0:T(8,128)(2,1)S(1)}, bf16[32,3072]{1,0:T(8,128)(2,1)S(1)}, u32[]{:S(2)}, u32[]{:S(2)}) collective-permute-start(bf16[32,3072]{1,0:T(8,128)(2,1)S(1)} %get-tuple-element.74), channel_id=1, source_target_pairs={{0,2},{2,4},{4,6},{6,7},{7,5},{5,3},{3,1},{1,0},{8,10},{10,12},{12... | collective-permute-start | bytes 589832 | tf_op jit(solution)/shard_map/ppermute | solution.py:383
  86.7 6.7 %collective-permute-start.31 = (bf16[32,3072]{1,0:T(8,128)(2,1)S(1)}, bf16[32,3072]{1,0:T(8,128)(2,1)S(1)}, u32[]{:S(2)}, u32[]{:S(2)}) collective-permute-start(bf16[32,3072]{1,0:T(8,128)(2,1)S(1)} %get-tuple-element.76), channel_id=1, source_target_pairs={{2,0},{4,2},{6,4},{7,6},{5,7},{3,5},{1,3},{0,1},{10,8},{12,10},{14... | collective-permute-start | bytes 589832 | tf_op jit(solution)/shard_map/ppermute | solution.py:384
  89.1 7.9 %collective-permute-start.22 = (bf16[32,3072]{1,0:T(8,128)(2,1)S(1)}, bf16[32,3072]{1,0:T(8,128)(2,1)S(1)}, u32[]{:S(2)}, u32[]{:S(2)}) collective-permute-start(bf16[32,3072]{1,0:T(8,128)(2,1)S(1)} %get-tuple-element.58), channel_id=1, source_target_pairs={{0,2},{2,4},{4,6},{6,7},{7,5},{5,3},{3,1},{1,0},{8,10},{10,12},{12... | collective-permute-start | bytes 589832 | tf_op jit(solution)/shard_map/ppermute | solution.py:383
  90.9 7.7 %collective-permute-start.23 = (bf16[32,3072]{1,0:T(8,128)(2,1)S(1)}, bf16[32,3072]{1,0:T(8,128)(2,1)S(1)}, u32[]{:S(2)}, u32[]{:S(2)}) collective-permute-start(bf16[32,3072]{1,0:T(8,128)(2,1)S(1)} %get-tuple-element.60), channel_id=1, source_target_pairs={{2,0},{4,2},{6,4},{7,6},{5,7},{3,5},{1,3},{0,1},{10,8},{12,10},{14... | collective-permute-start | bytes 589832 | tf_op jit(solution)/shard_map/ppermute | solution.py:384
  93.4 7.3 %collective-permute-start.32 = (bf16[32,3072]{1,0:T(8,128)(2,1)S(1)}, bf16[32,3072]{1,0:T(8,128)(2,1)S(1)}, u32[]{:S(2)}, u32[]{:S(2)}) collective-permute-start(bf16[32,3072]{1,0:T(8,128)(2,1)S(1)} %get-tuple-element.77), channel_id=1, source_target_pairs={{0,2},{2,4},{4,6},{6,7},{7,5},{5,3},{3,1},{1,0},{8,10},{10,12},{12... | collective-permute-start | bytes 589832 | tf_op jit(solution)/shard_map/ppermute | solution.py:383
  95.8 5.7 %collective-permute-start.33 = (bf16[32,3072]{1,0:T(8,128)(2,1)S(1)}, bf16[32,3072]{1,0:T(8,128)(2,1)S(1)}, u32[]{:S(2)}, u32[]{:S(2)}) collective-permute-start(bf16[32,3072]{1,0:T(8,128)(2,1)S(1)} %get-tuple-element.78), channel_id=1, source_target_pairs={{2,0},{4,2},{6,4},{7,6},{5,7},{3,5},{1,3},{0,1},{10,8},{12,10},{14... | collective-permute-start | bytes 589832 | tf_op jit(solution)/shard_map/ppermute | solution.py:384
  98.6 5.7 %collective-permute-start.24 = (bf16[32,3072]{1,0:T(8,128)(2,1)S(1)}, bf16[32,3072]{1,0:T(8,128)(2,1)S(1)}, u32[]{:S(2)}, u32[]{:S(2)}) collective-permute-start(bf16[32,3072]{1,0:T(8,128)(2,1)S(1)} %get-tuple-element.61), channel_id=1, source_target_pairs={{0,2},{2,4},{4,6},{6,7},{7,5},{5,3},{3,1},{1,0},{8,10},{10,12},{12... | collective-permute-start | bytes 589832 | tf_op jit(solution)/shard_map/ppermute | solution.py:383
  100.1 5.7 %collective-permute-start.25 = (bf16[32,3072]{1,0:T(8,128)(2,1)S(1)}, bf16[32,3072]{1,0:T(8,128)(2,1)S(1)}, u32[]{:S(2)}, u32[]{:S(2)}) collective-permute-start(bf16[32,3072]{1,0:T(8,128)(2,1)S(1)} %get-tuple-element.62), channel_id=1, source_target_pairs={{2,0},{4,2},{6,4},{7,6},{5,7},{3,5},{1,3},{0,1},{10,8},{12,10},{14... | collective-permute-start | bytes 589832 | tf_op jit(solution)/shard_map/ppermute | solution.py:384
  (3 other events, 4.5 us)

commit v3 on v2

--- a/solution.py
+++ b/solution.py
@@ -9,6 +9,7 @@
 
 VMEM = pl.BlockSpec(memory_space=pltpu.VMEM)
 ANY = pl.BlockSpec(memory_space=pl.ANY)
+HBM = pl.BlockSpec(memory_space=pltpu.HBM)
 F32, BF16 = jnp.float32, jnp.bfloat16
 
 
@@ -30,7 +31,11 @@
     return order + [size // 2]
 
 
-def call(body, out_shape, in_specs, out_specs, flops=0, nbytes=0, limit=16 << 20, **more):
+def in_hbm(array):
+    return pltpu.with_memory_space_constraint(array, pltpu.HBM)
+
+
+def call(body, out_shape, in_specs, out_specs, flops=0, nbytes=0, limit=12 << 20, **more):
     return pl.pallas_call(
         body,
         out_shape=out_shape,
@@ -42,24 +47,27 @@
     )
 
 
-def fetch(source, index, shape, after):
-    def body(source_ref, after_ref, out_ref, sem):
+def fetch(source, index, shape, through):
+    def body(source_ref, through_ref, out_ref, passed_ref, sem):
         copy = pltpu.make_async_copy(source_ref.at[index], out_ref, sem)
         copy.start()
         copy.wait()
 
     return call(
         body,
-        jax.ShapeDtypeStruct(shape, source.dtype),
-        [ANY, ANY],
-        VMEM,
+        (jax.ShapeDtypeStruct(shape, source.dtype), jax.ShapeDtypeStruct(through.shape, through.dtype)),
+        [HBM, ANY],
+        (VMEM, ANY),
         nbytes=2 * 2 * shape[0] * shape[1],
         scratch_shapes=[pltpu.SemaphoreType.DMA],
+        input_output_aliases={1: 1},
         name="fetch",
-    )(source, after)
-
-
-def ring_gather(block, size, right, left):
+    )(in_hbm(source), through)
+
+
+def ring_gather(block, size, right, left, fetches):
+    fetches = list(fetches)
+    brought = []
     half = block.shape[1] // 2
     quarter = half // 2
     going_right = [block[:, :half], block[:, half:]]
@@ -69,11 +77,15 @@
         for part in range(2):
             going_right[part] = lax.ppermute(going_right[part], "fsdp", right)
             going_left[part] = lax.ppermute(going_left[part], "fsdp", left)
+            if fetches:
+                source, index, shape = fetches.pop(0)
+                got, going_right[part] = fetch(source, index, shape, going_right[part])
+                brought.append(got)
             held[part] += [going_right[part], going_left[part]]
     for part in range(2):
         held[part].append(lax.ppermute(going_right[part][:, :quarter], "fsdp", right))
         held[part].append(lax.ppermute(going_left[part][:, quarter:], "fsdp", left))
-    return held
+    return held, brought
 
 
 def assemble(pieces, into):
@@ -94,31 +106,40 @@
 
     def body(*refs):
         rows = refs[: len(pieces)]
-        weight_ref, out_ref, whole = refs[len(pieces) :]
-        step = pl.program_id(0)
-
-        @pl.when(step == 0)
-        def _():
-            assemble(rows, whole)
-
-        start = pl.multiple_of((step % tiles) * tile, tile)
-        out_ref[step // tiles, :, pl.ds(start, tile)] = jnp.dot(
-            whole[...], weight_ref[...], preferred_element_type=F32
-        )
+        weight_ref, out_ref, whole, local, sems = refs[len(pieces) :]
+        copies = [
+            pltpu.make_async_copy(
+                weight_ref.at[step // tiles, pl.ds(0, half), pl.ds((step % tiles) * tile, tile)],
+                local.at[step],
+                sems.at[step],
+            )
+            for step in range(n_out * tiles)
+        ]
+        for copy in copies:
+            copy.start()
+        assemble(rows, whole)
+        for step, copy in enumerate(copies):
+            copy.wait()
+            start = (step % tiles) * tile
+            out_ref[step // tiles, :, start : start + tile] = jnp.dot(
+                whole[...], local[step], preferred_element_type=F32
+            )
 
     return call(
         body,
         jax.ShapeDtypeStruct((n_out, n_rows, columns), F32),
-        [VMEM] * len(pieces)
-        + [pl.BlockSpec((None, half, tile), lambda i: (i // tiles, 0, i % tiles))],
+        [VMEM] * len(pieces) + [HBM],
         VMEM,
         flops=2 * n_out * n_rows * half * columns,
         nbytes=2 * n_out * half * columns,
-        limit=24 << 20,
-        grid=(n_out * tiles,),
-        scratch_shapes=[pltpu.VMEM((n_rows, half), BF16)],
+        limit=14 << 20,
+        scratch_shapes=[
+            pltpu.VMEM((n_rows, half), BF16),
+            pltpu.VMEM((n_out * tiles, half, tile), BF16),
+            pltpu.SemaphoreType.DMA((n_out * tiles,)),
+        ],
         name="first_pass",
-    )(*pieces, weight)
+    )(*pieces, in_hbm(weight))
 
 
 def feature_map(projected):
@@ -207,7 +228,7 @@
         (VMEM,) * 2,
         flops=2 * n_rows * half * columns + 4 * n_rows * n_rows * columns,
         nbytes=2 * half * columns,
-        limit=24 << 20,
+        limit=14 << 20,
         name="queries_within",
     )(whole, query_weight, first, feat_k, values)
 
@@ -228,26 +249,29 @@
     target[:, start : start + width] = last
 
 
-def project_out(normalized, weight_ref, first_column, parts, rows):
+def project_out(normalized, weight_ref, parts, rows):
     half = parts[0].shape[1]
     tile = 512 if (half // 2) % 512 == 0 else 128
     for start in range(0, half, tile):
-        columns = slice(first_column + start, first_column + start + tile)
-        product = jnp.dot(normalized, weight_ref[:, columns], preferred_element_type=F32).astype(BF16)
+        product = jnp.dot(normalized, weight_ref[:, start : start + tile], preferred_element_type=F32).astype(BF16)
         spread(product, start, parts, rows, tile)
 
 
-def attend_and_project(feat_q, within, initial, earlier, gain, out_weight, size, head_dim):
+def attend_and_project(feat_q, within, initial, others, gain, out_weight, size, head_dim):
     n_rows, columns = feat_q.shape
     rows = n_rows // size
-    half = out_weight.shape[1] // 2
+    half = out_weight.shape[1]
     shapes = part_shapes(size, rows, half)
 
-    def body(q_ref, within_ref, initial_ref, earlier_ref, gain_ref, weight_ref, *refs):
-        normalized_ref, parts = refs[0], refs[1:]
+    def body(q_ref, within_ref, initial_ref, gain_ref, weight_ref, *refs):
+        other_refs, normalized_ref, parts = refs[: len(others)], refs[len(others)], refs[len(others) + 1 :]
+        place = lax.axis_index("ctx")
         for head in range(columns // head_dim):
             at = slice(head * head_dim, (head + 1) * head_dim)
-            prefix = initial_ref[head] + earlier_ref[head]
+            prefix = initial_ref[head]
+            for bit, other_ref in enumerate(other_refs):
+                later = (place // 2**bit) % 2 == 1
+                prefix = prefix + jnp.where(later, other_ref[head].astype(F32), 0.0)
             high = prefix.astype(BF16)
             low = (prefix - high.astype(F32)).astype(BF16)
             q = q_ref[:, at]
@@ -255,28 +279,28 @@
             attended = attended + jnp.dot(q, low, preferred_element_type=F32)
             scale = lax.rsqrt(jnp.mean(attended * attended, axis=-1, keepdims=True) + 1e-06)
             normalized_ref[:, at] = (attended * scale * gain_ref[:, at]).astype(BF16)
-        project_out(normalized_ref[...], weight_ref, 0, parts, rows)
+        project_out(normalized_ref[...], weight_ref, parts, rows)
 
     out = call(
         body,
         [jax.ShapeDtypeStruct((n_rows, columns), BF16)] + shapes,
-        [VMEM] * 6,
+        [VMEM] * (5 + len(others)),
         [VMEM] * (1 + len(shapes)),
         flops=2 * n_rows * half * columns,
         nbytes=2 * half * columns,
         name="attend_and_project",
-    )(feat_q, within, initial, earlier, gain.reshape(1, columns), out_weight)
+    )(feat_q, within, initial, gain.reshape(1, columns), out_weight, *others)
     return out[0], out[1:]
 
 
 def project_rest(normalized, out_weight, size):
     n_rows, columns = normalized.shape
     rows = n_rows // size
-    half = out_weight.shape[1] // 2
+    half = out_weight.shape[1]
     shapes = part_shapes(size, rows, half)
 
     def body(normalized_ref, weight_ref, *parts):
-        project_out(normalized_ref[...], weight_ref, half, parts, rows)
+        project_out(normalized_ref[...], weight_ref, parts, rows)
 
     return call(
         body,
@@ -331,19 +355,26 @@
     )(*flat)
 
 
-def earlier_states(state, size):
-    place = lax.axis_index("ctx")
-    before = None
+def add_states(one, two):
+    def body(one_ref, two_ref, out_ref):
+        out_ref[...] = (one_ref[...].astype(F32) + two_ref[...].astype(F32)).astype(BF16)
+
+    return call(
+        body, jax.ShapeDtypeStruct(one.shape, BF16), [VMEM] * 2, VMEM, nbytes=6 * one.size, limit=4 << 20, name="add_states"
+    )(one, two)
+
+
+def exchange_states(state, size):
+    others = []
     total = state
     reach = 1
     while reach < size:
         pairs = [(i, i ^ reach) for i in range(size)]
-        other = lax.ppermute(total, "ctx", pairs)
-        mine = jnp.where((place & reach) != 0, other.astype(F32), 0.0)
-        before = mine if before is None else before + mine
-        total = (total.astype(F32) + other.astype(F32)).astype(BF16)
+        others.append(lax.ppermute(total, "ctx", pairs))
         reach *= 2
-    return before
+        if reach < size:
+            total = add_states(total, others[-1])
+    return others
 
 
 def per_device(n_ctx, n_fsdp, tokens, qkv_weight, out_weight, norm_gain, initial_state):
@@ -355,22 +386,20 @@
     right, left = neighbours(n_fsdp)
     order = slots(n_fsdp)
 
-    held = ring_gather(tokens, n_fsdp, right, left)
     half = width // 2
-    second = [
-        fetch(qkv_weight, (s, pl.ds(half, half)), (half, columns), held[0][1 + at])
-        for at, s in enumerate(range(3))
-    ]
-    fetched_out = fetch(out_weight, (pl.ds(0, columns),), out_weight.shape, held[1][2])
+    fetches = [(qkv_weight, (s, pl.ds(half, half)), (half, columns)) for s in (1, 2, 0)]
+    fetches += [(out_weight, (slice(None), pl.ds(h * half, half)), (columns, half)) for h in range(2)]
+    held, brought = ring_gather(tokens, n_fsdp, right, left, fetches)
+    key_weight, value_weight, query_weight, out_first, out_second = brought
 
     first = first_pass(held[0], qkv_weight, n_rows)
-    feat_k, values, state, whole = keys_and_values(held[1], second[1], second[2], first, head_dim)
-    feat_q, within = queries_within(whole, second[0], first, feat_k, values, head_dim, n_fsdp, rows)
-    earlier = earlier_states(state, n_ctx)
+    feat_k, values, state, whole = keys_and_values(held[1], key_weight, value_weight, first, head_dim)
+    feat_q, within = queries_within(whole, query_weight, first, feat_k, values, head_dim, n_fsdp, rows)
+    others = exchange_states(state, n_ctx)
     normalized, parts_a = attend_and_project(
-        feat_q, within, initial_state, earlier, norm_gain, fetched_out, n_fsdp, head_dim
+        feat_q, within, initial_state, others, norm_gain, out_first, n_fsdp, head_dim
     )
-    parts_b = project_rest(normalized, fetched_out, n_fsdp)
+    parts_b = project_rest(normalized, out_second, n_fsdp)
 
     groups = []
     for parts in (parts_a, parts_b):

time: 107 us -> 92.5 us (0.86)
  local copies, waits for them, and re-layouts: 22.2 us -> 1.09 us
  Pallas kernels: 14 us -> 25.3 us
  waiting for transfers between devices: 33.2 us -> 29.5 us
    unnamed x34 -> x4, local copies, waits for them, and re-layouts: 21.1 us -> 0.01 us
    ppermute x6, starting transfers between devices: 1.95 us -> 12.8 us  [ring_gather(): going_left[part] = lax.ppermute(going_left[part], 'fsdp', left)]
    ppermute x6, starting transfers between devices: 11.5 us -> 0.72 us  [ring_gather(): going_right[part] = lax.ppermute(going_right[part], 'fsdp', right)]
    pallas_call x4 -> x6, Pallas kernels: 1.09 us -> 9.52 us  [the longest x5 9.49 us: fetch(): call(body, (jax.ShapeDtypeStruct(shape, source.dtype), jax.ShapeDtypeStru...]
    ppermute x6, waiting for transfers between devices: 8.5 us -> 3.96 us  [ring_gather(): going_left[part] = lax.ppermute(going_left[part], 'fsdp', left)]
    ppermute x6, waiting for transfers between devices: 7.72 us -> 4.2 us  [per_device(): got_left = lax.ppermute(to_left, 'fsdp', left)]
    ppermute x6, waiting for transfers between devices: 8.71 us -> 12.2 us  [per_device(): got_right = lax.ppermute(to_right, 'fsdp', right)]
    pallas_call x1, Pallas kernels: 4.35 us -> 7.21 us  [first_pass(): call(body, jax.ShapeDtypeStruct((n_out, n_rows, columns), F32), [VMEM] *...]
  transfers between devices with their start and end apart: 34 -> 34, of which waited for: 18 -> 22; matrix products, arithmetic and copies ran while one was open for 0% -> 0% of each run, Pallas kernels for 8% -> 21%
where the time goes in v3:
time: 92.5 us; the launch traced here: 92.2 us
  starting transfers between devices  36.1 us (39%)
  waiting for transfers between devices  29.5 us (32%)
  Pallas kernels  25.3 us (27%)
  local copies, waits for them, and re-layouts  1.09 us (1%)
    ppermute x6, starting transfers between devices, ring_gather(): going_left[part] = lax.ppermute(going_left[part], 'fsdp', left)  12.8 us
    ppermute x6, waiting for transfers between devices, per_device(): got_right = lax.ppermute(to_right, 'fsdp', right)  12.2 us
    ppermute x6, starting transfers between devices, per_device(): got_right = lax.ppermute(to_right, 'fsdp', right)  9.74 us
    pallas_call x5, Pallas kernels, fetch(): call(body, (jax.ShapeDtypeStruct(shape, source.dtype), jax.ShapeDtypeStru...  9.49 us
    pallas_call x1, Pallas kernels, first_pass(): call(body, jax.ShapeDtypeStruct((n_out, n_rows, columns), F32), [VMEM] *...  7.21 us
    ppermute x6, waiting for transfers between devices, per_device(): got_left = lax.ppermute(to_left, 'fsdp', left)  4.2 us
    ppermute x2, starting transfers between devices, ring_gather(): held[part].append(lax.ppermute(going_left[part][:, quarter:], 'fsdp', left))  4.1 us
    ppermute x6, waiting for transfers between devices, ring_gather(): going_left[part] = lax.ppermute(going_left[part], 'fsdp', left)  3.96 us
  transfers between devices with their start and end apart: 34, of which 22 were waited for; matrix products, arithmetic and copies ran while one was open for 0% of the time, Pallas kernels for 21%

profile of v3, /device:TPU:0, one launch (start us, length us, event | category | flops | bytes accessed | tf_op | source)
XLA Modules:
  0.0 92.2 jit_solution(2755814696147603166)
XLA Ops:
  0.0 1.0 %fusion = (bf16[32,3072]{1,0:T(8,128)(2,1)S(1)}, bf16[32,3072]{1,0:T(8,128)(2,1)S(1)}) fusion(bf16[32,6144]{1,0:T(8,128)(2,1)} %param.5), kind=kLoop, calls=%fused_computation | loop fusion | bytes 786432 | tf_op jit(solution)/shard_map/slice | solution.py:73
  1.1 3.0 %collective-permute-start.9 = (bf16[32,3072]{1,0:T(8,128)(2,1)S(1)}, bf16[32,3072]{1,0:T(8,128)(2,1)S(1)}, u32[]{:S(2)}, u32[]{:S(2)}) collective-permute-start(bf16[32,3072]{1,0:T(8,128)(2,1)S(1)} %get-tuple-element.99.refs_0_), channel_id=1, source_target_pairs={{2,0},{4,2},{6,4},{7,6},{5,7},{3,5},{1,3},{0,1},{10,8},{12,10},{14... | collective-permute-start | bytes 589832 | tf_op jit(solution)/shard_map/ppermute | solution.py:79
  4.2 1.9 %collective-permute-start.1 = (bf16[32,3072]{1,0:T(8,128)(2,1)S(1)}, bf16[32,3072]{1,0:T(8,128)(2,1)S(1)}, u32[]{:S(2)}, u32[]{:S(2)}) collective-permute-start(bf16[32,3072]{1,0:T(8,128)(2,1)S(1)} %get-tuple-element.100.refs_0_), channel_id=1, source_target_pairs={{2,0},{4,2},{6,4},{7,6},{5,7},{3,5},{1,3},{0,1},{10,8},{12,10},{14... | collective-permute-start | bytes 589832 | tf_op jit(solution)/shard_map/ppermute | solution.py:79
  6.2 3.6 %collective-permute-done.9.refs_2_ = bf16[32,3072]{1,0:T(8,128)(2,1)S(1)} collective-permute-done((bf16[32,3072]{1,0:T(8,128)(2,1)S(1)}, bf16[32,3072]{1,0:T(8,128)(2,1)S(1)}, u32[]{:S(2)}, u32[]{:S(2)}) %collective-permute-start.9) | collective-permute-done | bytes 196640 | tf_op jit(solution)/shard_map/ppermute | solution.py:79
  9.9 2.0 %collective-permute-start.11 = (bf16[32,3072]{1,0:T(8,128)(2,1)S(1)}, bf16[32,3072]{1,0:T(8,128)(2,1)S(1)}, u32[]{:S(2)}, u32[]{:S(2)}) collective-permute-start(bf16[32,3072]{1,0:T(8,128)(2,1)S(1)} %collective-permute-done.9.refs_2_), channel_id=1, source_target_pairs={{2,0},{4,2},{6,4},{7,6},{5,7},{3,5},{1,3},{0,1},{10,8},{12,10},{14... | collective-permute-start | bytes 589832 | tf_op jit(solution)/shard_map/ppermute | solution.py:79
  11.9 1.9 %fetch.7 = (bf16[3072,512]{1,0:T(8,128)(2,1)S(1)}, bf16[32,3072]{1,0:T(8,128)(2,1)S(1)}) custom-call(bf16[3,6144,512]{2,1,0:T(8,128)(2,1)} %refs_9_.1, bf16[32,3072]{1,0:T(8,128)(2,1)S(1)} %collective-permute-done.8.through_ref), custom_call_target="tpu_custom_call", output_to_operand_aliasing={{1}: (1, {})} | custom-call | bytes 6291456 | tf_op jit(solution)/shard_map/fetch/pallas_call | solution.py:56
  14.1 2.0 %collective-permute-start.3 = (bf16[32,3072]{1,0:T(8,128)(2,1)S(1)}, bf16[32,3072]{1,0:T(8,128)(2,1)S(1)}, u32[]{:S(2)}, u32[]{:S(2)}) collective-permute-start(bf16[32,3072]{1,0:T(8,128)(2,1)S(1)} %collective-permute-done.1.refs_2_), channel_id=1, source_target_pairs={{2,0},{4,2},{6,4},{7,6},{5,7},{3,5},{1,3},{0,1},{10,8},{12,10},{14... | collective-permute-start | bytes 589832 | tf_op jit(solution)/shard_map/ppermute | solution.py:79
  16.0 1.9 %fetch.5 = (bf16[3072,512]{1,0:T(8,128)(2,1)S(1)}, bf16[32,3072]{1,0:T(8,128)(2,1)S(1)}) custom-call(bf16[3,6144,512]{2,1,0:T(8,128)(2,1)} %refs_9_.1, bf16[32,3072]{1,0:T(8,128)(2,1)S(1)} %collective-permute-done.through_ref), custom_call_target="tpu_custom_call", output_to_operand_aliasing={{1}: (1, {})} | custom-call | bytes 6291456 | tf_op jit(solution)/shard_map/fetch/pallas_call | solution.py:56
  18.3 2.0 %collective-permute-start.13 = (bf16[32,3072]{1,0:T(8,128)(2,1)S(1)}, bf16[32,3072]{1,0:T(8,128)(2,1)S(1)}, u32[]{:S(2)}, u32[]{:S(2)}) collective-permute-start(bf16[32,3072]{1,0:T(8,128)(2,1)S(1)} %collective-permute-done.11.refs_4_), channel_id=1, source_target_pairs={{2,0},{4,2},{6,4},{7,6},{5,7},{3,5},{1,3},{0,1},{10,8},{12,10},{14... | collective-permute-start | bytes 589832 | tf_op jit(solution)/shard_map/ppermute | solution.py:79
  20.3 0.6 collective-permute-done.10.through_ref
  20.9 1.9 %fetch.8 = (bf16[3072,512]{1,0:T(8,128)(2,1)S(1)}, bf16[32,3072]{1,0:T(8,128)(2,1)S(1)}) custom-call(bf16[3,6144,512]{2,1,0:T(8,128)(2,1)} %refs_9_.1, bf16[32,3072]{1,0:T(8,128)(2,1)S(1)} %collective-permute-done.10.through_ref), custom_call_target="tpu_custom_call", output_to_operand_aliasing={{1}: (1, {})} | custom-call | bytes 6291456 | tf_op jit(solution)/shard_map/fetch/pallas_call | solution.py:56
  22.9 2.0 %collective-permute-start.5 = (bf16[32,3072]{1,0:T(8,128)(2,1)S(1)}, bf16[32,3072]{1,0:T(8,128)(2,1)S(1)}, u32[]{:S(2)}, u32[]{:S(2)}) collective-permute-start(bf16[32,3072]{1,0:T(8,128)(2,1)S(1)} %collective-permute-done.3.refs_4_), channel_id=1, source_target_pairs={{2,0},{4,2},{6,4},{7,6},{5,7},{3,5},{1,3},{0,1},{10,8},{12,10},{14... | collective-permute-start | bytes 589832 | tf_op jit(solution)/shard_map/ppermute | solution.py:79
  25.1 1.9 %fetch.6 = (bf16[512,3072]{1,0:T(8,128)(2,1)S(1)}, bf16[32,3072]{1,0:T(8,128)(2,1)S(1)}) custom-call(bf16[512,6144]{1,0:T(8,128)(2,1)} %source_ref.9, bf16[32,3072]{1,0:T(8,128)(2,1)S(1)} %collective-permute-done.2.through_ref), custom_call_target="tpu_custom_call", output_to_operand_aliasing={{1}: (1, {})} | custom-call | bytes 6291456 | tf_op jit(solution)/shard_map/fetch/pallas_call | solution.py:56
  27.1 2.1 %collective-permute-start.15 = (bf16[32,1536]{1,0:T(8,128)(2,1)S(1)}, bf16[32,1536]{1,0:T(8,128)(2,1)S(1)}, u32[]{:S(2)}, u32[]{:S(2)}) collective-permute-start(bf16[32,1536]{1,0:T(8,128)(2,1)S(1)} %slice.26), channel_id=1, source_target_pairs={{2,0},{4,2},{6,4},{7,6},{5,7},{3,5},{1,3},{0,1},{10,8},{12,10},{14... | collective-permute-start | bytes 294920 | tf_op jit(solution)/shard_map/ppermute | solution.py:87
  29.2 1.3 %collective-permute-done.12.through_ref = bf16[32,3072]{1,0:T(8,128)(2,1)S(1)} collective-permute-done((bf16[32,3072]{1,0:T(8,128)(2,1)S(1)}, bf16[32,3072]{1,0:T(8,128)(2,1)S(1)}, u32[]{:S(2)}, u32[]{:S(2)}) %collective-permute-start.12) | collective-permute-done | bytes 196640 | tf_op jit(solution)/shard_map/ppermute | solution.py:78
  30.5 1.9 %fetch.9 = (bf16[512,3072]{1,0:T(8,128)(2,1)S(1)}, bf16[32,3072]{1,0:T(8,128)(2,1)S(1)}) custom-call(bf16[512,6144]{1,0:T(8,128)(2,1)} %source_ref.9, bf16[32,3072]{1,0:T(8,128)(2,1)S(1)} %collective-permute-done.12.through_ref), custom_call_target="tpu_custom_call", output_to_operand_aliasing={{1}: (1, {})} | custom-call | bytes 6291456 | tf_op jit(solution)/shard_map/fetch/pallas_call | solution.py:56
  32.5 2.1 %collective-permute-start.7 = (bf16[32,1536]{1,0:T(8,128)(2,1)S(1)}, bf16[32,1536]{1,0:T(8,128)(2,1)S(1)}, u32[]{:S(2)}, u32[]{:S(2)}) collective-permute-start(bf16[32,1536]{1,0:T(8,128)(2,1)S(1)} %slice.25), channel_id=1, source_target_pairs={{2,0},{4,2},{6,4},{7,6},{5,7},{3,5},{1,3},{0,1},{10,8},{12,10},{14... | collective-permute-start | bytes 294920 | tf_op jit(solution)/shard_map/ppermute | solution.py:87
  34.7 2.3 %collective-permute-done.14.refs_7_ = bf16[32,1536]{1,0:T(8,128)(2,1)S(1)} collective-permute-done((bf16[32,1536]{1,0:T(8,128)(2,1)S(1)}, bf16[32,1536]{1,0:T(8,128)(2,1)S(1)}, u32[]{:S(2)}, u32[]{:S(2)}) %collective-permute-start.14) | collective-permute-done | bytes 98336 | tf_op jit(solution)/shard_map/ppermute | solution.py:86
  37.1 7.2 %first_pass.1.refs_11_.first_ref = f32[3,256,512]{2,1,0:T(8,128)S(1)} custom-call(bf16[32,3072]{1,0:T(8,128)(2,1)S(1)} %get-tuple-element.99.refs_0_, bf16[32,3072]{1,0:T(8,128)(2,1)S(1)} %get-tuple-element.56.refs_1_, bf16[32,3072]{1,0:T(8,128)(2,1)S(1)} %collective-permute-done.9.refs_2_, bf16[32,3072]{1,0:T(8,128)(2,1)S(1)} %get-tuple-element.57.refs_3_, ...), custom_call_target="tpu_custom_call" | custom-call | flops 2415919104 | bytes 9437184 | tf_op jit(solution)/shard_map/first_pass/pallas_call | solution.py:128
  44.3 2.3 %keys_and_values.1 = (bf16[256,512]{1,0:T(8,128)(2,1)S(1)}, bf16[256,512]{1,0:T(8,128)(2,1)S(1)}, bf16[4,128,128]{2,1,0:T(8,128)(2,1)S(1)}, bf16[256,3072]{1,0:T(8,128)(2,1)S(1)}) custom-call(bf16[32,3072]{1,0:T(8,128)(2,1)S(1)} %get-tuple-element.100.refs_0_, bf16[32,3072]{1,0:T(8,128)(2,1)S(1)} %get-tuple-element.52.refs_1_, ...), custom_call_target="tpu_custom_call" | custom-call | flops 1610612736 | bytes 6291456 | tf_op jit(solution)/shard_map/keys_and_values/pallas_call | solution.py:172
  46.7 1.3 %collective-permute-done.16.two_ref.refs_0_ = bf16[4,128,128]{2,1,0:T(8,128)(2,1)S(1)} collective-permute-done((bf16[4,128,128]{2,1,0:T(8,128)(2,1)S(1)}, bf16[4,128,128]{2,1,0:T(8,128)(2,1)S(1)}, u32[]{:S(2)}, u32[]{:S(2)}) %collective-permute-start.16) | collective-permute-done | bytes 131104 | tf_op jit(solution)/shard_map/ppermute | solution.py:373
  48.0 1.6 %collective-permute-start.17 = (bf16[4,128,128]{2,1,0:T(8,128)(2,1)S(1)}, bf16[4,128,128]{2,1,0:T(8,128)(2,1)S(1)}, u32[]{:S(2)}, u32[]{:S(2)}) collective-permute-start(bf16[4,128,128]{2,1,0:T(8,128)(2,1)S(1)} %add_states.1), channel_id=1, source_target_pairs={{0,16},{8,24},{16,0},{24,8},{1,17},{9,25},{17,1},{25,9},{2,18},{10... | collective-permute-start | bytes 393224 | tf_op jit(solution)/shard_map/ppermute | solution.py:373
  49.6 2.6 %queries_within.1 = (bf16[256,512]{1,0:T(8,128)(2,1)S(1)}, f32[256,512]{1,0:T(8,128)S(1)}) custom-call(bf16[256,3072]{1,0:T(8,128)(2,1)S(1)} %get-tuple-element.59.whole_ref, bf16[3072,512]{1,0:T(8,128)(2,1)S(1)} %get-tuple-element.60.weight_ref, f32[3,256,512]{2,1,0:T(8,128)S(1)} %first_pass.1.refs_11_.first_ref, ...), custom_call_target="tpu_custom_call" | custom-call | flops 939524096 | bytes 3145728 | tf_op jit(solution)/shard_map/queries_within/pallas_call | solution.py:224
  52.3 1.4 %collective-permute-done.17.refs_1_ = bf16[4,128,128]{2,1,0:T(8,128)(2,1)S(1)} collective-permute-done((bf16[4,128,128]{2,1,0:T(8,128)(2,1)S(1)}, bf16[4,128,128]{2,1,0:T(8,128)(2,1)S(1)}, u32[]{:S(2)}, u32[]{:S(2)}) %collective-permute-start.17) | collective-permute-done | bytes 131104 | tf_op jit(solution)/shard_map/ppermute | solution.py:373
  53.6 1.3 %attend_and_project.1 = (bf16[256,512]{1,0:T(8,128)(2,1)S(1)}, bf16[32,3072]{1,0:T(8,128)(2,1)S(1)}, bf16[32,3072]{1,0:T(8,128)(2,1)S(1)}, bf16[32,3072]{1,0:T(8...) custom-call(bf16[256,512]{1,0:T(8,128)(2,1)S(1)} %get-tuple-element., ...), custom_call_target="tpu_custom_call" | custom-call | flops 805306368 | bytes 3145728 | tf_op jit(solution)/shard_map/attend_and_project/pallas_call | solution.py:284
  55.0 1.0 %project_rest.1 = (bf16[32,3072]{1,0:T(8,128)(2,1)S(1)}, bf16[32,3072]{1,0:T(8,128)(2,1)S(1)}, bf16[32,3072]{1,0:T(8,128)(2,1)S(1)}, bf16[32,3072]{1,0:T(8,128)(...) custom-call(bf16[256,512]{1,0:T(8,128)(2,1)S(1)} %get-tuple-element., ...), custom_call_target="tpu_custom_call" | custom-call | flops 805306368 | bytes 3145728 | tf_op jit(solution)/shard_map/project_rest/pallas_call | solution.py:305
  56.4 1.7 %collective-permute-start.27 = (bf16[32,1536]{1,0:T(8,128)(2,1)S(1)}, bf16[32,1536]{1,0:T(8,128)(2,1)S(1)}, u32[]{:S(2)}, u32[]{:S(2)}) collective-permute-start(bf16[32,1536]{1,0:T(8,128)(2,1)S(1)} %get-tuple-element.90), channel_id=1, source_target_pairs={{2,0},{4,2},{6,4},{7,6},{5,7},{3,5},{1,3},{0,1},{10,8},{12,10},{14... | collective-permute-start | bytes 294920 | tf_op jit(solution)/shard_map/ppermute | solution.py:407
  58.4 1.7 %collective-permute-start.19 = (bf16[32,1536]{1,0:T(8,128)(2,1)S(1)}, bf16[32,1536]{1,0:T(8,128)(2,1)S(1)}, u32[]{:S(2)}, u32[]{:S(2)}) collective-permute-start(bf16[32,1536]{1,0:T(8,128)(2,1)S(1)} %get-tuple-element.73), channel_id=1, source_target_pairs={{2,0},{4,2},{6,4},{7,6},{5,7},{3,5},{1,3},{0,1},{10,8},{12,10},{14... | collective-permute-start | bytes 294920 | tf_op jit(solution)/shard_map/ppermute | solution.py:407
  60.1 1.4 %collective-permute-done.26.gr = bf16[32,1536]{1,0:T(8,128)(2,1)S(1)} collective-permute-done((bf16[32,1536]{1,0:T(8,128)(2,1)S(1)}, bf16[32,1536]{1,0:T(8,128)(2,1)S(1)}, u32[]{:S(2)}, u32[]{:S(2)}) %collective-permute-start.26) | collective-permute-done | bytes 98336 | tf_op jit(solution)/shard_map/ppermute | solution.py:406
  62.0 1.5 %collective-permute-start.28 = (bf16[32,3072]{1,0:T(8,128)(2,1)S(1)}, bf16[32,3072]{1,0:T(8,128)(2,1)S(1)}, u32[]{:S(2)}, u32[]{:S(2)}) collective-permute-start(bf16[32,3072]{1,0:T(8,128)(2,1)S(1)} %get-tuple-element.91), channel_id=1, source_target_pairs={{0,2},{2,4},{4,6},{6,7},{7,5},{5,3},{3,1},{1,0},{8,10},{10,12},{12... | collective-permute-start | bytes 589832 | tf_op jit(solution)/shard_map/ppermute | solution.py:412
  63.5 0.5 collective-permute-start.29
  64.1 1.5 %collective-permute-start.20 = (bf16[32,3072]{1,0:T(8,128)(2,1)S(1)}, bf16[32,3072]{1,0:T(8,128)(2,1)S(1)}, u32[]{:S(2)}, u32[]{:S(2)}) collective-permute-start(bf16[32,3072]{1,0:T(8,128)(2,1)S(1)} %get-tuple-element.74), channel_id=1, source_target_pairs={{0,2},{2,4},{4,6},{6,7},{7,5},{5,3},{3,1},{1,0},{8,10},{10,12},{12... | collective-permute-start | bytes 589832 | tf_op jit(solution)/shard_map/ppermute | solution.py:412
  65.7 0.5 collective-permute-start.21
  66.2 3.7 %collective-permute-done.28.gr = bf16[32,3072]{1,0:T(8,128)(2,1)S(1)} collective-permute-done((bf16[32,3072]{1,0:T(8,128)(2,1)S(1)}, bf16[32,3072]{1,0:T(8,128)(2,1)S(1)}, u32[]{:S(2)}, u32[]{:S(2)}) %collective-permute-start.28) | collective-permute-done | bytes 196640 | tf_op jit(solution)/shard_map/ppermute | solution.py:412
  70.2 1.6 %collective-permute-start.30 = (bf16[32,3072]{1,0:T(8,128)(2,1)S(1)}, bf16[32,3072]{1,0:T(8,128)(2,1)S(1)}, u32[]{:S(2)}, u32[]{:S(2)}) collective-permute-start(bf16[32,3072]{1,0:T(8,128)(2,1)S(1)} %get-tuple-element.94), channel_id=1, source_target_pairs={{0,2},{2,4},{4,6},{6,7},{7,5},{5,3},{3,1},{1,0},{8,10},{10,12},{12... | collective-permute-start | bytes 589832 | tf_op jit(solution)/shard_map/ppermute | solution.py:412
  71.8 0.5 collective-permute-start.31
  72.2 1.8 %collective-permute-done.20.gr = bf16[32,3072]{1,0:T(8,128)(2,1)S(1)} collective-permute-done((bf16[32,3072]{1,0:T(8,128)(2,1)S(1)}, bf16[32,3072]{1,0:T(8,128)(2,1)S(1)}, u32[]{:S(2)}, u32[]{:S(2)}) %collective-permute-start.20) | collective-permute-done | bytes 196640 | tf_op jit(solution)/shard_map/ppermute | solution.py:412
  74.4 1.6 %collective-permute-start.22 = (bf16[32,3072]{1,0:T(8,128)(2,1)S(1)}, bf16[32,3072]{1,0:T(8,128)(2,1)S(1)}, u32[]{:S(2)}, u32[]{:S(2)}) collective-permute-start(bf16[32,3072]{1,0:T(8,128)(2,1)S(1)} %get-tuple-element.77), channel_id=1, source_target_pairs={{0,2},{2,4},{4,6},{6,7},{7,5},{5,3},{3,1},{1,0},{8,10},{10,12},{12... | collective-permute-start | bytes 589832 | tf_op jit(solution)/shard_map/ppermute | solution.py:412
  76.0 0.5 collective-permute-start.23
  76.5 1.8 %collective-permute-done.30.gr = bf16[32,3072]{1,0:T(8,128)(2,1)S(1)} collective-permute-done((bf16[32,3072]{1,0:T(8,128)(2,1)S(1)}, bf16[32,3072]{1,0:T(8,128)(2,1)S(1)}, u32[]{:S(2)}, u32[]{:S(2)}) %collective-permute-start.30) | collective-permute-done | bytes 196640 | tf_op jit(solution)/shard_map/ppermute | solution.py:412
  78.6 1.7 %collective-permute-start.32 = (bf16[32,3072]{1,0:T(8,128)(2,1)S(1)}, bf16[32,3072]{1,0:T(8,128)(2,1)S(1)}, u32[]{:S(2)}, u32[]{:S(2)}) collective-permute-start(bf16[32,3072]{1,0:T(8,128)(2,1)S(1)} %get-tuple-element.97), channel_id=1, source_target_pairs={{0,2},{2,4},{4,6},{6,7},{7,5},{5,3},{3,1},{1,0},{8,10},{10,12},{12... | collective-permute-start | bytes 589832 | tf_op jit(solution)/shard_map/ppermute | solution.py:412
  80.7 1.8 %collective-permute-done.22.gr = bf16[32,3072]{1,0:T(8,128)(2,1)S(1)} collective-permute-done((bf16[32,3072]{1,0:T(8,128)(2,1)S(1)}, bf16[32,3072]{1,0:T(8,128)(2,1)S(1)}, u32[]{:S(2)}, u32[]{:S(2)}) %collective-permute-start.22) | collective-permute-done | bytes 196640 | tf_op jit(solution)/shard_map/ppermute | solution.py:412
  82.5 1.3 %collective-permute-done.23.gl = bf16[32,3072]{1,0:T(8,128)(2,1)S(1)} collective-permute-done((bf16[32,3072]{1,0:T(8,128)(2,1)S(1)}, bf16[32,3072]{1,0:T(8,128)(2,1)S(1)}, u32[]{:S(2)}, u32[]{:S(2)}) %collective-permute-start.23) | collective-permute-done | bytes 196640 | tf_op jit(solution)/shard_map/ppermute | solution.py:413
  83.9 1.7 %collective-permute-start.24 = (bf16[32,3072]{1,0:T(8,128)(2,1)S(1)}, bf16[32,3072]{1,0:T(8,128)(2,1)S(1)}, u32[]{:S(2)}, u32[]{:S(2)}) collective-permute-start(bf16[32,3072]{1,0:T(8,128)(2,1)S(1)} %get-tuple-element.80), channel_id=1, source_target_pairs={{0,2},{2,4},{4,6},{6,7},{7,5},{5,3},{3,1},{1,0},{8,10},{10,12},{12... | collective-permute-start | bytes 589832 | tf_op jit(solution)/shard_map/ppermute | solution.py:412
  86.0 0.6 collective-permute-done.33.refs_5_
  86.6 3.1 %collective-permute-done.24.refs_1_ = bf16[32,3072]{1,0:T(8,128)(2,1)S(1)} collective-permute-done((bf16[32,3072]{1,0:T(8,128)(2,1)S(1)}, bf16[32,3072]{1,0:T(8,128)(2,1)S(1)}, u32[]{:S(2)}, u32[]{:S(2)}) %collective-permute-start.24) | collective-permute-done | bytes 196640 | tf_op jit(solution)/shard_map/ppermute | solution.py:412
  89.7 1.7 %collective-permute-done.25.refs_2_ = bf16[32,3072]{1,0:T(8,128)(2,1)S(1)} collective-permute-done((bf16[32,3072]{1,0:T(8,128)(2,1)S(1)}, bf16[32,3072]{1,0:T(8,128)(2,1)S(1)}, u32[]{:S(2)}, u32[]{:S(2)}) %collective-permute-start.25) | collective-permute-done | bytes 196640 | tf_op jit(solution)/shard_map/ppermute | solution.py:413
  91.3 0.9 finish.1
  (47 shorter events, 4.6 us)
Async XLA Ops:
  1.1 8.8 %collective-permute-start.9 = (bf16[32,3072]{1,0:T(8,128)(2,1)S(1)}, bf16[32,3072]{1,0:T(8,128)(2,1)S(1)}, u32[]{:S(2)}, u32[]{:S(2)}) collective-permute-start(bf16[32,3072]{1,0:T(8,128)(2,1)S(1)} %get-tuple-element.99.refs_0_), channel_id=1, source_target_pairs={{2,0},{4,2},{6,4},{7,6},{5,7},{3,5},{1,3},{0,1},{10,8},{12,10},{14... | collective-permute-start | bytes 589832 | tf_op jit(solution)/shard_map/ppermute | solution.py:79
  4.0 7.8 %collective-permute-start.8 = (bf16[32,3072]{1,0:T(8,128)(2,1)S(1)}, bf16[32,3072]{1,0:T(8,128)(2,1)S(1)}, u32[]{:S(2)}, u32[]{:S(2)}) collective-permute-start(bf16[32,3072]{1,0:T(8,128)(2,1)S(1)} %get-tuple-element.99.refs_0_), channel_id=1, source_target_pairs={{0,2},{2,4},{4,6},{6,7},{7,5},{5,3},{3,1},{1,0},{8,10},{10,12},{12... | collective-permute-start | bytes 589832 | tf_op jit(solution)/shard_map/ppermute | solution.py:78
  4.2 9.9 %collective-permute-start.1 = (bf16[32,3072]{1,0:T(8,128)(2,1)S(1)}, bf16[32,3072]{1,0:T(8,128)(2,1)S(1)}, u32[]{:S(2)}, u32[]{:S(2)}) collective-permute-start(bf16[32,3072]{1,0:T(8,128)(2,1)S(1)} %get-tuple-element.100.refs_0_), channel_id=1, source_target_pairs={{2,0},{4,2},{6,4},{7,6},{5,7},{3,5},{1,3},{0,1},{10,8},{12,10},{14... | collective-permute-start | bytes 589832 | tf_op jit(solution)/shard_map/ppermute | solution.py:79
  6.1 10.0 %collective-permute-start = (bf16[32,3072]{1,0:T(8,128)(2,1)S(1)}, bf16[32,3072]{1,0:T(8,128)(2,1)S(1)}, u32[]{:S(2)}, u32[]{:S(2)}) collective-permute-start(bf16[32,3072]{1,0:T(8,128)(2,1)S(1)} %get-tuple-element.100.refs_0_), channel_id=1, source_target_pairs={{0,2},{2,4},{4,6},{6,7},{7,5},{5,3},{3,1},{1,0},{8,10},{10,12},{12... | collective-permute-start | bytes 589832 | tf_op jit(solution)/shard_map/ppermute | solution.py:78
  9.9 8.4 %collective-permute-start.11 = (bf16[32,3072]{1,0:T(8,128)(2,1)S(1)}, bf16[32,3072]{1,0:T(8,128)(2,1)S(1)}, u32[]{:S(2)}, u32[]{:S(2)}) collective-permute-start(bf16[32,3072]{1,0:T(8,128)(2,1)S(1)} %collective-permute-done.9.refs_2_), channel_id=1, source_target_pairs={{2,0},{4,2},{6,4},{7,6},{5,7},{3,5},{1,3},{0,1},{10,8},{12,10},{14... | collective-permute-start | bytes 589832 | tf_op jit(solution)/shard_map/ppermute | solution.py:79
  13.8 7.1 %collective-permute-start.10 = (bf16[32,3072]{1,0:T(8,128)(2,1)S(1)}, bf16[32,3072]{1,0:T(8,128)(2,1)S(1)}, u32[]{:S(2)}, u32[]{:S(2)}) collective-permute-start(bf16[32,3072]{1,0:T(8,128)(2,1)S(1)} %get-tuple-element.56.refs_1_), channel_id=1, source_target_pairs={{0,2},{2,4},{4,6},{6,7},{7,5},{5,3},{3,1},{1,0},{8,10},{10,12},{12... | collective-permute-start | bytes 589832 | tf_op jit(solution)/shard_map/ppermute | solution.py:78
  14.1 8.8 %collective-permute-start.3 = (bf16[32,3072]{1,0:T(8,128)(2,1)S(1)}, bf16[32,3072]{1,0:T(8,128)(2,1)S(1)}, u32[]{:S(2)}, u32[]{:S(2)}) collective-permute-start(bf16[32,3072]{1,0:T(8,128)(2,1)S(1)} %collective-permute-done.1.refs_2_), channel_id=1, source_target_pairs={{2,0},{4,2},{6,4},{7,6},{5,7},{3,5},{1,3},{0,1},{10,8},{12,10},{14... | collective-permute-start | bytes 589832 | tf_op jit(solution)/shard_map/ppermute | solution.py:79
  18.0 7.2 %collective-permute-start.2 = (bf16[32,3072]{1,0:T(8,128)(2,1)S(1)}, bf16[32,3072]{1,0:T(8,128)(2,1)S(1)}, u32[]{:S(2)}, u32[]{:S(2)}) collective-permute-start(bf16[32,3072]{1,0:T(8,128)(2,1)S(1)} %get-tuple-element.52.refs_1_), channel_id=1, source_target_pairs={{0,2},{2,4},{4,6},{6,7},{7,5},{5,3},{3,1},{1,0},{8,10},{10,12},{12... | collective-permute-start | bytes 589832 | tf_op jit(solution)/shard_map/ppermute | solution.py:78
  18.3 8.8 %collective-permute-start.13 = (bf16[32,3072]{1,0:T(8,128)(2,1)S(1)}, bf16[32,3072]{1,0:T(8,128)(2,1)S(1)}, u32[]{:S(2)}, u32[]{:S(2)}) collective-permute-start(bf16[32,3072]{1,0:T(8,128)(2,1)S(1)} %collective-permute-done.11.refs_4_), channel_id=1, source_target_pairs={{2,0},{4,2},{6,4},{7,6},{5,7},{3,5},{1,3},{0,1},{10,8},{12,10},{14... | collective-permute-start | bytes 589832 | tf_op jit(solution)/shard_map/ppermute | solution.py:79
  22.8 7.7 %collective-permute-start.12 = (bf16[32,3072]{1,0:T(8,128)(2,1)S(1)}, bf16[32,3072]{1,0:T(8,128)(2,1)S(1)}, u32[]{:S(2)}, u32[]{:S(2)}) collective-permute-start(bf16[32,3072]{1,0:T(8,128)(2,1)S(1)} %get-tuple-element.57.refs_3_), channel_id=1, source_target_pairs={{0,2},{2,4},{4,6},{6,7},{7,5},{5,3},{3,1},{1,0},{8,10},{10,12},{12... | collective-permute-start | bytes 589832 | tf_op jit(solution)/shard_map/ppermute | solution.py:78
  22.9 9.6 %collective-permute-start.5 = (bf16[32,3072]{1,0:T(8,128)(2,1)S(1)}, bf16[32,3072]{1,0:T(8,128)(2,1)S(1)}, u32[]{:S(2)}, u32[]{:S(2)}) collective-permute-start(bf16[32,3072]{1,0:T(8,128)(2,1)S(1)} %collective-permute-done.3.refs_4_), channel_id=1, source_target_pairs={{2,0},{4,2},{6,4},{7,6},{5,7},{3,5},{1,3},{0,1},{10,8},{12,10},{14... | collective-permute-start | bytes 589832 | tf_op jit(solution)/shard_map/ppermute | solution.py:79
  27.0 7.5 %collective-permute-start.4 = (bf16[32,3072]{1,0:T(8,128)(2,1)S(1)}, bf16[32,3072]{1,0:T(8,128)(2,1)S(1)}, u32[]{:S(2)}, u32[]{:S(2)}) collective-permute-start(bf16[32,3072]{1,0:T(8,128)(2,1)S(1)} %get-tuple-element.53.refs_3_), channel_id=1, source_target_pairs={{0,2},{2,4},{4,6},{6,7},{7,5},{5,3},{3,1},{1,0},{8,10},{10,12},{12... | collective-permute-start | bytes 589832 | tf_op jit(solution)/shard_map/ppermute | solution.py:78
  27.1 7.6 %collective-permute-start.15 = (bf16[32,1536]{1,0:T(8,128)(2,1)S(1)}, bf16[32,1536]{1,0:T(8,128)(2,1)S(1)}, u32[]{:S(2)}, u32[]{:S(2)}) collective-permute-start(bf16[32,1536]{1,0:T(8,128)(2,1)S(1)} %slice.26), channel_id=1, source_target_pairs={{2,0},{4,2},{6,4},{7,6},{5,7},{3,5},{1,3},{0,1},{10,8},{12,10},{14... | collective-permute-start | bytes 294920 | tf_op jit(solution)/shard_map/ppermute | solution.py:87
  32.4 4.7 %collective-permute-start.14 = (bf16[32,1536]{1,0:T(8,128)(2,1)S(1)}, bf16[32,1536]{1,0:T(8,128)(2,1)S(1)}, u32[]{:S(2)}, u32[]{:S(2)}) collective-permute-start(bf16[32,1536]{1,0:T(8,128)(2,1)S(1)} %slice.22), channel_id=1, source_target_pairs={{0,2},{2,4},{4,6},{6,7},{7,5},{5,3},{3,1},{1,0},{8,10},{10,12},{12... | collective-permute-start | bytes 294920 | tf_op jit(solution)/shard_map/ppermute | solution.py:86
  32.5 11.8 %collective-permute-start.7 = (bf16[32,1536]{1,0:T(8,128)(2,1)S(1)}, bf16[32,1536]{1,0:T(8,128)(2,1)S(1)}, u32[]{:S(2)}, u32[]{:S(2)}) collective-permute-start(bf16[32,1536]{1,0:T(8,128)(2,1)S(1)} %slice.25), channel_id=1, source_target_pairs={{2,0},{4,2},{6,4},{7,6},{5,7},{3,5},{1,3},{0,1},{10,8},{12,10},{14... | collective-permute-start | bytes 294920 | tf_op jit(solution)/shard_map/ppermute | solution.py:87
  34.6 9.7 %collective-permute-start.6 = (bf16[32,1536]{1,0:T(8,128)(2,1)S(1)}, bf16[32,1536]{1,0:T(8,128)(2,1)S(1)}, u32[]{:S(2)}, u32[]{:S(2)}) collective-permute-start(bf16[32,1536]{1,0:T(8,128)(2,1)S(1)} %slice.24), channel_id=1, source_target_pairs={{0,2},{2,4},{4,6},{6,7},{7,5},{5,3},{3,1},{1,0},{8,10},{10,12},{12... | collective-permute-start | bytes 294920 | tf_op jit(solution)/shard_map/ppermute | solution.py:86
  46.6 1.4 %collective-permute-start.16 = (bf16[4,128,128]{2,1,0:T(8,128)(2,1)S(1)}, bf16[4,128,128]{2,1,0:T(8,128)(2,1)S(1)}, u32[]{:S(2)}, u32[]{:S(2)}) collective-permute-start(bf16[4,128,128]{2,1,0:T(8,128)(2,1)S(1)} %get-tuple-element.66.one_ref), channel_id=1, source_target_pairs={{0,8},{8,0},{16,24},{24,16},{1,9},{9,1},{17,25},{25,17},{2,10},{10... | collective-permute-start | bytes 393224 | tf_op jit(solution)/shard_map/ppermute | solution.py:373
  48.0 5.6 %collective-permute-start.17 = (bf16[4,128,128]{2,1,0:T(8,128)(2,1)S(1)}, bf16[4,128,128]{2,1,0:T(8,128)(2,1)S(1)}, u32[]{:S(2)}, u32[]{:S(2)}) collective-permute-start(bf16[4,128,128]{2,1,0:T(8,128)(2,1)S(1)} %add_states.1), channel_id=1, source_target_pairs={{0,16},{8,24},{16,0},{24,8},{1,17},{9,25},{17,1},{25,9},{2,18},{10... | collective-permute-start | bytes 393224 | tf_op jit(solution)/shard_map/ppermute | solution.py:373
  49.6 4.0 %copy-start = (f32[4,128,128]{2,1,0:T(8,128)S(1)}, f32[4,128,128]{2,1,0:T(8,128)}, u32[]{:S(2)}) copy-start(f32[4,128,128]{2,1,0:T(8,128)} %initial_ref.1) | copy-start | bytes 786436
  49.6 4.0 %copy-start.1 = (f32[512]{0:T(512)S(1)}, f32[512]{0:T(512)}, u32[]{:S(2)}) copy-start(f32[512]{0:T(512)} %param.8) | copy-start | bytes 6148
  56.0 5.5 %collective-permute-start.26 = (bf16[32,1536]{1,0:T(8,128)(2,1)S(1)}, bf16[32,1536]{1,0:T(8,128)(2,1)S(1)}, u32[]{:S(2)}, u32[]{:S(2)}) collective-permute-start(bf16[32,1536]{1,0:T(8,128)(2,1)S(1)} %get-tuple-element.88), channel_id=1, source_target_pairs={{0,2},{2,4},{4,6},{6,7},{7,5},{5,3},{3,1},{1,0},{8,10},{10,12},{12... | collective-permute-start | bytes 294920 | tf_op jit(solution)/shard_map/ppermute | solution.py:406
  56.4 5.5 %collective-permute-start.27 = (bf16[32,1536]{1,0:T(8,128)(2,1)S(1)}, bf16[32,1536]{1,0:T(8,128)(2,1)S(1)}, u32[]{:S(2)}, u32[]{:S(2)}) collective-permute-start(bf16[32,1536]{1,0:T(8,128)(2,1)S(1)} %get-tuple-element.90), channel_id=1, source_target_pairs={{2,0},{4,2},{6,4},{7,6},{5,7},{3,5},{1,3},{0,1},{10,8},{12,10},{14... | collective-permute-start | bytes 294920 | tf_op jit(solution)/shard_map/ppermute | solution.py:407
  58.1 6.0 %collective-permute-start.18 = (bf16[32,1536]{1,0:T(8,128)(2,1)S(1)}, bf16[32,1536]{1,0:T(8,128)(2,1)S(1)}, u32[]{:S(2)}, u32[]{:S(2)}) collective-permute-start(bf16[32,1536]{1,0:T(8,128)(2,1)S(1)} %get-tuple-element.71), channel_id=1, source_target_pairs={{0,2},{2,4},{4,6},{6,7},{7,5},{5,3},{3,1},{1,0},{8,10},{10,12},{12... | collective-permute-start | bytes 294920 | tf_op jit(solution)/shard_map/ppermute | solution.py:406
  58.4 5.6 %collective-permute-start.19 = (bf16[32,1536]{1,0:T(8,128)(2,1)S(1)}, bf16[32,1536]{1,0:T(8,128)(2,1)S(1)}, u32[]{:S(2)}, u32[]{:S(2)}) collective-permute-start(bf16[32,1536]{1,0:T(8,128)(2,1)S(1)} %get-tuple-element.73), channel_id=1, source_target_pairs={{2,0},{4,2},{6,4},{7,6},{5,7},{3,5},{1,3},{0,1},{10,8},{12,10},{14... | collective-permute-start | bytes 294920 | tf_op jit(solution)/shard_map/ppermute | solution.py:407
  62.0 7.9 %collective-permute-start.28 = (bf16[32,3072]{1,0:T(8,128)(2,1)S(1)}, bf16[32,3072]{1,0:T(8,128)(2,1)S(1)}, u32[]{:S(2)}, u32[]{:S(2)}) collective-permute-start(bf16[32,3072]{1,0:T(8,128)(2,1)S(1)} %get-tuple-element.91), channel_id=1, source_target_pairs={{0,2},{2,4},{4,6},{6,7},{7,5},{5,3},{3,1},{1,0},{8,10},{10,12},{12... | collective-permute-start | bytes 589832 | tf_op jit(solution)/shard_map/ppermute | solution.py:412
  63.5 6.6 %collective-permute-start.29 = (bf16[32,3072]{1,0:T(8,128)(2,1)S(1)}, bf16[32,3072]{1,0:T(8,128)(2,1)S(1)}, u32[]{:S(2)}, u32[]{:S(2)}) collective-permute-start(bf16[32,3072]{1,0:T(8,128)(2,1)S(1)} %get-tuple-element.93), channel_id=1, source_target_pairs={{2,0},{4,2},{6,4},{7,6},{5,7},{3,5},{1,3},{0,1},{10,8},{12,10},{14... | collective-permute-start | bytes 589832 | tf_op jit(solution)/shard_map/ppermute | solution.py:413
  64.1 10.0 %collective-permute-start.20 = (bf16[32,3072]{1,0:T(8,128)(2,1)S(1)}, bf16[32,3072]{1,0:T(8,128)(2,1)S(1)}, u32[]{:S(2)}, u32[]{:S(2)}) collective-permute-start(bf16[32,3072]{1,0:T(8,128)(2,1)S(1)} %get-tuple-element.74), channel_id=1, source_target_pairs={{0,2},{2,4},{4,6},{6,7},{7,5},{5,3},{3,1},{1,0},{8,10},{10,12},{12... | collective-permute-start | bytes 589832 | tf_op jit(solution)/shard_map/ppermute | solution.py:412
  65.7 8.6 %collective-permute-start.21 = (bf16[32,3072]{1,0:T(8,128)(2,1)S(1)}, bf16[32,3072]{1,0:T(8,128)(2,1)S(1)}, u32[]{:S(2)}, u32[]{:S(2)}) collective-permute-start(bf16[32,3072]{1,0:T(8,128)(2,1)S(1)} %get-tuple-element.76), channel_id=1, source_target_pairs={{2,0},{4,2},{6,4},{7,6},{5,7},{3,5},{1,3},{0,1},{10,8},{12,10},{14... | collective-permute-start | bytes 589832 | tf_op jit(solution)/shard_map/ppermute | solution.py:413
  70.2 8.1 %collective-permute-start.30 = (bf16[32,3072]{1,0:T(8,128)(2,1)S(1)}, bf16[32,3072]{1,0:T(8,128)(2,1)S(1)}, u32[]{:S(2)}, u32[]{:S(2)}) collective-permute-start(bf16[32,3072]{1,0:T(8,128)(2,1)S(1)} %get-tuple-element.94), channel_id=1, source_target_pairs={{0,2},{2,4},{4,6},{6,7},{7,5},{5,3},{3,1},{1,0},{8,10},{10,12},{12... | collective-permute-start | bytes 589832 | tf_op jit(solution)/shard_map/ppermute | solution.py:412
  71.8 6.7 %collective-permute-start.31 = (bf16[32,3072]{1,0:T(8,128)(2,1)S(1)}, bf16[32,3072]{1,0:T(8,128)(2,1)S(1)}, u32[]{:S(2)}, u32[]{:S(2)}) collective-permute-start(bf16[32,3072]{1,0:T(8,128)(2,1)S(1)} %get-tuple-element.96), channel_id=1, source_target_pairs={{2,0},{4,2},{6,4},{7,6},{5,7},{3,5},{1,3},{0,1},{10,8},{12,10},{14... | collective-permute-start | bytes 589832 | tf_op jit(solution)/shard_map/ppermute | solution.py:413
  74.4 8.1 %collective-permute-start.22 = (bf16[32,3072]{1,0:T(8,128)(2,1)S(1)}, bf16[32,3072]{1,0:T(8,128)(2,1)S(1)}, u32[]{:S(2)}, u32[]{:S(2)}) collective-permute-start(bf16[32,3072]{1,0:T(8,128)(2,1)S(1)} %get-tuple-element.77), channel_id=1, source_target_pairs={{0,2},{2,4},{4,6},{6,7},{7,5},{5,3},{3,1},{1,0},{8,10},{10,12},{12... | collective-permute-start | bytes 589832 | tf_op jit(solution)/shard_map/ppermute | solution.py:412
  76.0 7.8 %collective-permute-start.23 = (bf16[32,3072]{1,0:T(8,128)(2,1)S(1)}, bf16[32,3072]{1,0:T(8,128)(2,1)S(1)}, u32[]{:S(2)}, u32[]{:S(2)}) collective-permute-start(bf16[32,3072]{1,0:T(8,128)(2,1)S(1)} %get-tuple-element.79), channel_id=1, source_target_pairs={{2,0},{4,2},{6,4},{7,6},{5,7},{3,5},{1,3},{0,1},{10,8},{12,10},{14... | collective-permute-start | bytes 589832 | tf_op jit(solution)/shard_map/ppermute | solution.py:413
  78.6 7.4 %collective-permute-start.32 = (bf16[32,3072]{1,0:T(8,128)(2,1)S(1)}, bf16[32,3072]{1,0:T(8,128)(2,1)S(1)}, u32[]{:S(2)}, u32[]{:S(2)}) collective-permute-start(bf16[32,3072]{1,0:T(8,128)(2,1)S(1)} %get-tuple-element.97), channel_id=1, source_target_pairs={{0,2},{2,4},{4,6},{6,7},{7,5},{5,3},{3,1},{1,0},{8,10},{10,12},{12... | collective-permute-start | bytes 589832 | tf_op jit(solution)/shard_map/ppermute | solution.py:412
  80.3 6.3 %collective-permute-start.33 = (bf16[32,3072]{1,0:T(8,128)(2,1)S(1)}, bf16[32,3072]{1,0:T(8,128)(2,1)S(1)}, u32[]{:S(2)}, u32[]{:S(2)}) collective-permute-start(bf16[32,3072]{1,0:T(8,128)(2,1)S(1)} %get-tuple-element.98), channel_id=1, source_target_pairs={{2,0},{4,2},{6,4},{7,6},{5,7},{3,5},{1,3},{0,1},{10,8},{12,10},{14... | collective-permute-start | bytes 589832 | tf_op jit(solution)/shard_map/ppermute | solution.py:413
  83.9 5.7 %collective-permute-start.24 = (bf16[32,3072]{1,0:T(8,128)(2,1)S(1)}, bf16[32,3072]{1,0:T(8,128)(2,1)S(1)}, u32[]{:S(2)}, u32[]{:S(2)}) collective-permute-start(bf16[32,3072]{1,0:T(8,128)(2,1)S(1)} %get-tuple-element.80), channel_id=1, source_target_pairs={{0,2},{2,4},{4,6},{6,7},{7,5},{5,3},{3,1},{1,0},{8,10},{10,12},{12... | collective-permute-start | bytes 589832 | tf_op jit(solution)/shard_map/ppermute | solution.py:412
  85.6 5.7 %collective-permute-start.25 = (bf16[32,3072]{1,0:T(8,128)(2,1)S(1)}, bf16[32,3072]{1,0:T(8,128)(2,1)S(1)}, u32[]{:S(2)}, u32[]{:S(2)}) collective-permute-start(bf16[32,3072]{1,0:T(8,128)(2,1)S(1)} %get-tuple-element.81), channel_id=1, source_target_pairs={{2,0},{4,2},{6,4},{7,6},{5,7},{3,5},{1,3},{0,1},{10,8},{12,10},{14... | collective-permute-start | bytes 589832 | tf_op jit(solution)/shard_map/ppermute | solution.py:413

commit v4 on v3

v4 whole, which is shorter than its diff:
```python
import functools

import jax
import jax.numpy as jnp
from jax import lax
from jax.experimental import pallas as pl
from jax.experimental.pallas import tpu as pltpu
from jax.sharding import PartitionSpec as P

VMEM = pl.BlockSpec(memory_space=pltpu.VMEM)
ANY = pl.BlockSpec(memory_space=pl.ANY)
HBM = pl.BlockSpec(memory_space=pltpu.HBM)
F32, BF16 = jnp.float32, jnp.bfloat16
HOP_FLOPS = 5 * 10**9


def ring_order(size):
    return list(range(0, size, 2)) + list(range(size - 1, 0, -2))


def neighbours(size):
    ring = ring_order(size)
    right = [(ring[i], ring[(i + 1) % size]) for i in range(size)]
    left = [(b, a) for a, b in right]
    return right, left


def slots(size):
    order = [0]
    for step in range(1, size // 2):
        order += [-step, step]
    return order + [size // 2]


def in_hbm(array):
    return pltpu.with_memory_space_constraint(array, pltpu.HBM)


def call(body, out_shape, in_specs, out_specs, flops=0, nbytes=0, limit=12 << 20, **more):
    return pl.pallas_call(
        body,
        out_shape=out_shape,
        in_specs=in_specs,
        out_specs=out_specs,
        cost_estimate=pl.CostEstimate(flops=flops, bytes_accessed=nbytes, transcendentals=0),
        compiler_params=pltpu.CompilerParams(vmem_limit_bytes=limit),
        **more,
    )


def fetch(source, index, shape, through):
    def body(source_ref, through_ref, out_ref, passed_ref, sem):
        copy = pltpu.make_async_copy(source_ref.at[index], out_ref, sem)
        copy.start()
        copy.wait()

    return call(
        body,
        (jax.ShapeDtypeStruct(shape, source.dtype), jax.ShapeDtypeStruct(through.shape, through.dtype)),
        [HBM, ANY],
        (VMEM, ANY),
        nbytes=2 * 2 * shape[0] * shape[1],
        scratch_shapes=[pltpu.SemaphoreType.DMA],
        input_output_aliases={1: 1},
        name="fetch",
    )(in_hbm(source), through)


def ring_gather(block, size, right, left, fetches):
    fetches = list(fetches)
    brought = []
    half = block.shape[1] // 2
    quarter = half // 2
    going_right = [block[:, :half], block[:, half:]]
    source, index, shape = fetches.pop(0)
    got, going_right[1] = fetch(source, index, shape, going_right[1])
    brought.append(got)
    going_left = list(going_right)
    held = [[going_right[0]], [going_right[1]]]
    for _ in range(size // 2 - 1):
        for part in range(2):
            going_right[part] = lax.ppermute(going_right[part], "fsdp", right)
            going_left[part] = lax.ppermute(going_left[part], "fsdp", left)
            if fetches:
                source, index, shape = fetches.pop(0)
                got, going_right[part] = fetch(source, index, shape, going_right[part])
                brought.append(got)
            held[part] += [going_right[part], going_left[part]]
    for part in range(2):
        held[part].append(lax.ppermute(going_right[part][:, :quarter], "fsdp", right))
        held[part].append(lax.ppermute(going_left[part][:, quarter:], "fsdp", left))
    return held, brought


def assemble(pieces, into):
    rows = pieces[0].shape[0]
    for place, piece in enumerate(pieces[:-2]):
        into[place * rows : (place + 1) * rows, :] = piece[...]
    quarter = pieces[-1].shape[1]
    start = (len(pieces) - 2) * rows
    into[start : start + rows, :quarter] = pieces[-2][...]
    into[start : start + rows, quarter:] = pieces[-1][...]


def first_pass(pieces, weights, n_rows):
    half, columns = weights[0].shape

    def body(*refs):
        rows = refs[: len(pieces)]
        weight_refs = refs[len(pieces) : len(pieces) + len(weights)]
        out_ref, whole = refs[len(pieces) + len(weights) :]
        assemble(rows, whole)
        for place, weight_ref in enumerate(weight_refs):
            out_ref[place] = jnp.dot(whole[...], weight_ref[...], preferred_element_type=F32)

    return call(
        body,
        (
            jax.ShapeDtypeStruct((len(weights), n_rows, columns), F32),
            jax.ShapeDtypeStruct((n_rows, half), BF16),
        ),
        [VMEM] * (len(pieces) + len(weights)),
        (VMEM, VMEM),
        flops=2 * len(weights) * n_rows * half * columns,
        nbytes=2 * len(weights) * half * columns,
        name="first_pass",
    )(*pieces, *weights)


def feature_map(projected):
    return jnp.where(projected > 0.0, projected + 1.0, jnp.exp(jnp.minimum(projected, 0.0)))


def keys_and_values(pieces, key_weight, value_weight, first, head_dim):
    _, n_rows, columns = first.shape
    half = key_weight.shape[0]

    def body(*refs):
        rows = refs[: len(pieces)]
        key_ref, value_ref, first_ref, feat_ref, values_ref, state_ref, whole = refs[len(pieces) :]
        assemble(rows, whole)
        tile = min(columns, 256)
        for start in range(0, columns, tile):
            span = slice(start, start + tile)
            projected = first_ref[0, :, span] + jnp.dot(whole[...], key_ref[:, span], preferred_element_type=F32)
            feat = feature_map(projected).astype(BF16)
            feat_ref[:, span] = feat
            projected = first_ref[1, :, span] + jnp.dot(whole[...], value_ref[:, span], preferred_element_type=F32)
            values = projected.astype(BF16)
            values_ref[:, span] = values
            for head in range(start, start + tile, head_dim):
                at = slice(head - start, head - start + head_dim)
                state_ref[head // head_dim] = lax.dot_general(
                    feat[:, at], values[:, at], (((0,), (0,)), ((), ())), preferred_element_type=F32
                ).astype(BF16)

    return call(
        body,
        (
            jax.ShapeDtypeStruct((n_rows, columns), BF16),
            jax.ShapeDtypeStruct((n_rows, columns), BF16),
            jax.ShapeDtypeStruct((columns // head_dim, head_dim, head_dim), BF16),
            jax.ShapeDtypeStruct((n_rows, half), BF16),
        ),
        [VMEM] * (len(pieces) + 3),
        (VMEM,) * 4,
        flops=2 * 2 * n_rows * half * columns,
        nbytes=2 * 2 * half * columns,
        name="keys_and_values",
    )(*pieces, key_weight, value_weight, first)


def queries_within(halves, qkv_weight, feat_k, values, head_dim, size, rows):
    n_rows, columns = feat_k.shape
    half = halves[0].shape[1]
    order = slots(size)
    pieces = 3
    chunk = half // pieces

    def place(shape, axis):
        spot = lax.axis_index("fsdp")
        spot = jnp.where(spot % 2 == 0, spot // 2, size - (spot + 1) // 2)
        row = lax.broadcasted_iota(jnp.int32, shape, axis)
        slot = row // rows
        start = jnp.zeros(shape, jnp.int32)
        for at, distance in enumerate(order):
            there = (spot + distance + size) % size
            holder = jnp.where(there < size // 2, 2 * there, 2 * (size - there) - 1)
            start = jnp.where(slot == at, holder * rows, start)
        return start + row - slot * rows

    def body(first_ref, second_ref, weight_ref, k_ref, v_ref, feat_ref, within_ref, local, sems):
        copies = [
            pltpu.make_async_copy(
                weight_ref.at[0, pl.ds(at * chunk, chunk)], local.at[pl.ds(at * chunk, chunk)], sems.at[at]
            )
            for at in range(2 * pieces)
        ]
        for copy in copies:
            copy.start()
        causal = place((n_rows, 1), 0) >= place((1, n_rows), 1)
        projected = None
        for at, copy in enumerate(copies):
            rows_ref = (first_ref, second_ref)[at // pieces]
            start = (at % pieces) * chunk
            copy.wait()
            product = jnp.dot(
                rows_ref[:, start : start + chunk],
                local[at * chunk : (at + 1) * chunk, :],
                preferred_element_type=F32,
            )
            projected = product if projected is None else projected + product
        feat_ref[...] = feature_map(projected).astype(BF16)
        for head in range(0, columns, head_dim):
            span = slice(head, head + head_dim)
            scores = lax.dot_general(
                feat_ref[:, span], k_ref[:, span], (((1,), (1,)), ((), ())), preferred_element_type=F32
            )
            scores = jnp.where(causal, scores, 0.0).astype(BF16)
            within_ref[:, span] = jnp.dot(scores, v_ref[:, span], preferred_element_type=F32)

    return call(
        body,
        (jax.ShapeDtypeStruct((n_rows, columns), BF16), jax.ShapeDtypeStruct((n_rows, columns), F32)),
        [VMEM, VMEM, HBM, VMEM, VMEM],
        (VMEM,) * 2,
        flops=4 * n_rows * half * columns + 4 * n_rows * n_rows * columns,
        nbytes=4 * half * columns,
        limit=16 << 20,
        scratch_shapes=[
            pltpu.VMEM((2 * half, columns), BF16),
            pltpu.SemaphoreType.DMA((2 * pieces,)),
        ],
        name="queries_within",
    )(*halves, in_hbm(qkv_weight), feat_k, values)


def project_out(normalized, weight_refs, parts, rows):
    for which, weight_ref in enumerate(weight_refs):
        half = weight_ref.shape[1]
        tile = 512 if half % 512 == 0 else 128
        for start in range(0, half, tile):
            span = slice(start, start + tile)
            product = jnp.dot(normalized, weight_ref[:, span], preferred_element_type=F32).astype(BF16)
            for block in range(len(parts) // 2):
                parts[2 * block + which][:, span] = product[block * rows : (block + 1) * rows, :]


def attend_and_project(feat_q, within, initial, others, gain, out_weights, blocks, rows, head_dim):
    n_rows, columns = feat_q.shape
    half = out_weights[0].shape[1]

    def body(q_ref, within_ref, initial_ref, gain_ref, first_ref, second_ref, *refs):
        other_refs, normalized_ref, parts = refs[: len(others)], refs[len(others)], refs[len(others) + 1 :]
        place = lax.axis_index("ctx")
        for head in range(columns // head_dim):
            at = slice(head * head_dim, (head + 1) * head_dim)
            prefix = initial_ref[head]
            for bit, other_ref in enumerate(other_refs):
                later = (place // 2**bit) % 2 == 1
                prefix = prefix + jnp.where(later, other_ref[head].astype(F32), 0.0)
            high = prefix.astype(BF16)
            low = (prefix - high.astype(F32)).astype(BF16)
            q = q_ref[:, at]
            attended = within_ref[:, at] + jnp.dot(q, high, preferred_element_type=F32)
            attended = attended + jnp.dot(q, low, preferred_element_type=F32)
            scale = lax.rsqrt(jnp.mean(attended * attended, axis=-1, keepdims=True) + 1e-06)
            normalized_ref[:, at] = (attended * scale * gain_ref[:, at]).astype(BF16)
        project_out(normalized_ref[n_rows - blocks * rows :, :], (first_ref, second_ref), parts, rows)

    out = call(
        body,
        [jax.ShapeDtypeStruct((n_rows, columns), BF16)] + [jax.ShapeDtypeStruct((rows, half), BF16)] * (2 * blocks),
        [VMEM] * (6 + len(others)),
        [VMEM] * (1 + 2 * blocks),
        flops=4 * n_rows * half * columns,
        nbytes=4 * half * columns,
        name="attend_and_project",
    )(feat_q, within, initial, gain.reshape(1, columns), *out_weights, *others)
    return out[0], [out[1 + 2 * block : 3 + 2 * block] for block in range(blocks)]


def project_rest(normalized, out_weights, blocks, rows):
    columns = normalized.shape[1]
    half = out_weights[0].shape[1]

    def body(normalized_ref, first_ref, second_ref, *parts):
        project_out(normalized_ref[: blocks * rows, :], (first_ref, second_ref), parts, rows)

    out = call(
        body,
        [jax.ShapeDtypeStruct((rows, half), BF16)] * (2 * blocks),
        [VMEM] * 3,
        [VMEM] * (2 * blocks),
        flops=HOP_FLOPS,
        nbytes=4 * half * columns,
        name="project_rest",
    )(normalized, *out_weights)
    return [out[2 * block : 2 * block + 2] for block in range(blocks)]


def add_step(mine_right, got_right, mine_left, got_left):
    def body(mr, gr, ml, gl, to_right, to_left):
        to_right[...] = (mr[...].astype(F32) + gr[...].astype(F32)).astype(BF16)
        to_left[...] = (ml[...].astype(F32) + gl[...].astype(F32)).astype(BF16)

    return call(
        body,
        [jax.ShapeDtypeStruct(mine_right.shape, BF16)] * 2,
        [VMEM] * 4,
        [VMEM] * 2,
        nbytes=12 * mine_right.size,
        limit=4 << 20,
        name="add_step",
    )(mine_right, got_right, mine_left, got_left)


def add_own(own, trailing):
    def body(first, second, got_first, got_second, out):
        out[0] = first[...].astype(F32) + got_first[...].astype(F32)
        out[1] = second[...].astype(F32) + got_second[...].astype(F32)

    return call(
        body,
        jax.ShapeDtypeStruct((2,) + own[0].shape, F32),
        [VMEM] * 4,
        VMEM,
        flops=HOP_FLOPS,
        nbytes=16 * own[0].size,
        limit=4 << 20,
        name="add_own",
    )(*own, *trailing)


def finish(gathered, leading):
    rows, half = leading[0].shape

    def body(gathered_ref, first, second, out):
        out[:, :half] = (gathered_ref[0] + first[...].astype(F32)).astype(BF16)
        out[:, half:] = (gathered_ref[1] + second[...].astype(F32)).astype(BF16)

    return call(
        body,
        jax.ShapeDtypeStruct((rows, 2 * half), BF16),
        [VMEM] * 3,
        VMEM,
        nbytes=4 * rows * half,
        limit=4 << 20,
        name="finish",
    )(gathered, *leading)


def ring_scatter(parts, order, right, left):
    far = max(order)

    def part(distance, half):
        return parts[order.index(distance)][half]

    def hop(to_right, to_left):
        return lax.ppermute(to_right, "fsdp", right), lax.ppermute(to_left, "fsdp", left)

    leading = hop(part(far, 0), part(far, 1))
    trailing = hop(part(far - 1, 1), part(1 - far, 0))
    for step in range(far - 1, 0, -1):
        leading = hop(*add_step(part(step, 0), leading[0], part(-step, 1), leading[1]))
        if step > 1:
            trailing = hop(*add_step(part(step - 1, 1), trailing[0], part(1 - step, 0), trailing[1]))
    gathered = add_own(parts[0], (trailing[1], trailing[0]))
    return finish(gathered, leading)


def add_states(one, two):
    def body(one_ref, two_ref, out_ref):
        out_ref[...] = (one_ref[...].astype(F32) + two_ref[...].astype(F32)).astype(BF16)

    return call(
        body, jax.ShapeDtypeStruct(one.shape, BF16), [VMEM] * 2, VMEM, nbytes=6 * one.size, limit=4 << 20, name="add_states"
    )(one, two)


def exchange_states(state, size):
    others = []
    total = state
    reach = 1
    while reach < size:
        pairs = [(i, i ^ reach) for i in range(size)]
        others.append(lax.ppermute(total, "ctx", pairs))
        reach *= 2
        if reach < size:
            total = add_states(total, others[-1])
    return others


def per_device(n_ctx, n_fsdp, tokens, qkv_weight, out_weight, norm_gain, initial_state):
    rows, width = tokens.shape
    heads_here, head_dim = initial_state.shape[:2]
    columns = heads_here * head_dim
    n_rows = rows * n_fsdp
    right, left = neighbours(n_fsdp)
    order = slots(n_fsdp)

    half = width // 2
    fetches = [(qkv_weight, (s, pl.ds(part * half, half)), (half, columns)) for part in range(2) for s in (1, 2)]
    fetches += [(out_weight, (slice(None), pl.ds(part * half, half)), (columns, half)) for part in range(2)]
    held, brought = ring_gather(tokens, n_fsdp, right, left, fetches)

    first, first_rows = first_pass(held[0], brought[:2], n_rows)
    feat_k, values, state, second_rows = keys_and_values(held[1], brought[2], brought[3], first, head_dim)
    feat_q, within = queries_within((first_rows, second_rows), qkv_weight, feat_k, values, head_dim, n_fsdp, rows)
    others = exchange_states(state, n_ctx)
    soon = 1
    normalized, parts = attend_and_project(
        feat_q, within, initial_state, others, norm_gain, brought[4:], soon, rows, head_dim
    )
    parts = project_rest(normalized, brought[4:], n_fsdp - soon, rows) + parts
    return ring_scatter(parts, order, right, left)


def solution(mesh):
    body = functools.partial(per_device, mesh.shape["ctx"], mesh.shape["fsdp"])
    placed = (
        P(("ctx", "fsdp"), None),
        P(None, None, "fsdp"),
        P("fsdp", None),
        P("fsdp"),
        P("fsdp", None, None),
    )
    return jax.shard_map(
        body, mesh=mesh, in_specs=placed, out_specs=P(("ctx", "fsdp"), None), check_vma=False
    )
```

time: 92.5 us -> 83.3 us (0.901)
  waiting for transfers between devices: 29.5 us -> 24 us
  starting transfers between devices: 36.1 us -> 33.6 us
  Pallas kernels: 25.3 us -> 24.1 us
    pallas_call x10, Pallas kernels: 10.9 us -> 6.27 us  [the longest x1 1.78 us: first_pass(): call(body, (jax.ShapeDtypeStruct((len(weights), n_rows, columns), F32), j...]
    ppermute x16 -> x14, starting transfers between devices: 16.6 us -> 14.5 us  [the longest x7 9.21 us: hop(): lax.ppermute(to_right, 'fsdp', right)]
    pallas_call x5 -> x6, Pallas kernels: 9.49 us -> 11.4 us  [fetch(): call(body, (jax.ShapeDtypeStruct(shape, source.dtype), jax.ShapeDtypeStru...]
    ppermute x6, waiting for transfers between devices: 2.23 us -> 0.6 us  [ring_gather(): going_right[part] = lax.ppermute(going_right[part], 'fsdp', right)]
    ppermute x16 -> x14, waiting for transfers between devices: 18.2 us -> 16.6 us  [the longest x7 9.58 us: hop(): lax.ppermute(to_right, 'fsdp', right)]
    pallas_call x1, Pallas kernels: 2.63 us -> 4.15 us  [queries_within(): call(body, (jax.ShapeDtypeStruct((n_rows, columns), BF16), jax.ShapeDtype...]
    ppermute x2, waiting for transfers between devices: 2.72 us -> 1.34 us  [exchange_states(): others.append(lax.ppermute(total, 'ctx', pairs))]
    ppermute x6, waiting for transfers between devices: 3.96 us -> 2.6 us  [ring_gather(): going_left[part] = lax.ppermute(going_left[part], 'fsdp', left)]
  transfers between devices with their start and end apart: 34 -> 32, of which waited for: 22 -> 25; matrix products, arithmetic and copies ran while one was open for 0% -> 0% of each run, Pallas kernels for 21% -> 23%
where the time goes in v4:
time: 83.3 us; the launch traced here: 83 us
  starting transfers between devices  33.6 us (40%)
  Pallas kernels  24.1 us (29%)
  waiting for transfers between devices  24 us (29%)
  local copies, waits for them, and re-layouts  1.08 us (1%)
    ppermute x6, starting transfers between devices, ring_gather(): going_left[part] = lax.ppermute(going_left[part], 'fsdp', left)  12.3 us
    pallas_call x6, Pallas kernels, fetch(): call(body, (jax.ShapeDtypeStruct(shape, source.dtype), jax.ShapeDtypeStru...  11.4 us
    ppermute x7, waiting for transfers between devices, hop(): lax.ppermute(to_right, 'fsdp', right)  9.58 us
    ppermute x7, starting transfers between devices, hop(): lax.ppermute(to_right, 'fsdp', right)  9.21 us
    ppermute x7, waiting for transfers between devices, hop(): lax.ppermute(to_left, 'fsdp', left)  7.05 us
    ppermute x7, starting transfers between devices, hop(): lax.ppermute(to_left, 'fsdp', left)  5.31 us
    pallas_call x1, Pallas kernels, queries_within(): call(body, (jax.ShapeDtypeStruct((n_rows, columns), BF16), jax.ShapeDtype...  4.15 us
    ppermute x2, starting transfers between devices, ring_gather(): held[part].append(lax.ppermute(going_left[part][:, quarter:], 'fsdp', left))  3.89 us
  transfers between devices with their start and end apart: 32, of which 25 were waited for; matrix products, arithmetic and copies ran while one was open for 0% of the time, Pallas kernels for 23%

profile of v4, /device:TPU:0, one launch (start us, length us, event | category | flops | bytes accessed | tf_op | source)
XLA Modules:
  0.0 83.0 jit_solution(7693121362095719626)
XLA Ops:
  0.0 1.0 %fusion = (bf16[32,3072]{1,0:T(8,128)(2,1)S(1)}, bf16[32,3072]{1,0:T(8,128)(2,1)S(1)}) fusion(bf16[32,6144]{1,0:T(8,128)(2,1)} %param.5), kind=kLoop, calls=%fused_computation | loop fusion | bytes 786432 | tf_op jit(solution)/shard_map/slice | solution.py:74
  1.1 3.0 %collective-permute-start.1 = (bf16[32,3072]{1,0:T(8,128)(2,1)S(1)}, bf16[32,3072]{1,0:T(8,128)(2,1)S(1)}, u32[]{:S(2)}, u32[]{:S(2)}) collective-permute-start(bf16[32,3072]{1,0:T(8,128)(2,1)S(1)} %get-tuple-element.100.refs_0_), channel_id=1, source_target_pairs={{2,0},{4,2},{6,4},{7,6},{5,7},{3,5},{1,3},{0,1},{10,8},{12,10},{14... | collective-permute-start | bytes 589832 | tf_op jit(solution)/shard_map/ppermute | solution.py:83
  4.2 1.9 %fetch.9 = (bf16[3072,512]{1,0:T(8,128)(2,1)S(1)}, bf16[32,3072]{1,0:T(8,128)(2,1)S(1)}) custom-call(bf16[3,6144,512]{2,1,0:T(8,128)(2,1)} %weight_ref.1, bf16[32,3072]{1,0:T(8,128)(2,1)S(1)} %get-tuple-element.99.through_ref), custom_call_target="tpu_custom_call", output_to_operand_aliasing={{1}: (1, {})} | custom-call | bytes 6291456 | tf_op jit(solution)/shard_map/fetch/pallas_call | solution.py:57
  6.1 1.9 %collective-permute-start.9 = (bf16[32,3072]{1,0:T(8,128)(2,1)S(1)}, bf16[32,3072]{1,0:T(8,128)(2,1)S(1)}, u32[]{:S(2)}, u32[]{:S(2)}) collective-permute-start(bf16[32,3072]{1,0:T(8,128)(2,1)S(1)} %get-tuple-element.58.refs_0_), channel_id=1, source_target_pairs={{2,0},{4,2},{6,4},{7,6},{5,7},{3,5},{1,3},{0,1},{10,8},{12,10},{14... | collective-permute-start | bytes 589832 | tf_op jit(solution)/shard_map/ppermute | solution.py:83
  8.2 1.5 %collective-permute-done.1.refs_2_ = bf16[32,3072]{1,0:T(8,128)(2,1)S(1)} collective-permute-done((bf16[32,3072]{1,0:T(8,128)(2,1)S(1)}, bf16[32,3072]{1,0:T(8,128)(2,1)S(1)}, u32[]{:S(2)}, u32[]{:S(2)}) %collective-permute-start.1) | collective-permute-done | bytes 196640 | tf_op jit(solution)/shard_map/ppermute | solution.py:83
  9.7 1.7 %collective-permute-start.3 = (bf16[32,3072]{1,0:T(8,128)(2,1)S(1)}, bf16[32,3072]{1,0:T(8,128)(2,1)S(1)}, u32[]{:S(2)}, u32[]{:S(2)}) collective-permute-start(bf16[32,3072]{1,0:T(8,128)(2,1)S(1)} %collective-permute-done.1.refs_2_), channel_id=1, source_target_pairs={{2,0},{4,2},{6,4},{7,6},{5,7},{3,5},{1,3},{0,1},{10,8},{12,10},{14... | collective-permute-start | bytes 589832 | tf_op jit(solution)/shard_map/ppermute | solution.py:83
  11.4 1.9 %fetch.6 = (bf16[3072,512]{1,0:T(8,128)(2,1)S(1)}, bf16[32,3072]{1,0:T(8,128)(2,1)S(1)}) custom-call(bf16[3,6144,512]{2,1,0:T(8,128)(2,1)} %weight_ref.1, bf16[32,3072]{1,0:T(8,128)(2,1)S(1)} %collective-permute-done.through_ref), custom_call_target="tpu_custom_call", output_to_operand_aliasing={{1}: (1, {})} | custom-call | bytes 6291456 | tf_op jit(solution)/shard_map/fetch/pallas_call | solution.py:57
  14.0 1.9 %collective-permute-start.11 = (bf16[32,3072]{1,0:T(8,128)(2,1)S(1)}, bf16[32,3072]{1,0:T(8,128)(2,1)S(1)}, u32[]{:S(2)}, u32[]{:S(2)}) collective-permute-start(bf16[32,3072]{1,0:T(8,128)(2,1)S(1)} %collective-permute-done.9.refs_2_), channel_id=1, source_target_pairs={{2,0},{4,2},{6,4},{7,6},{5,7},{3,5},{1,3},{0,1},{10,8},{12,10},{14... | collective-permute-start | bytes 589832 | tf_op jit(solution)/shard_map/ppermute | solution.py:83
  15.9 1.9 %fetch.10 = (bf16[3072,512]{1,0:T(8,128)(2,1)S(1)}, bf16[32,3072]{1,0:T(8,128)(2,1)S(1)}) custom-call(bf16[3,6144,512]{2,1,0:T(8,128)(2,1)} %weight_ref.1, bf16[32,3072]{1,0:T(8,128)(2,1)S(1)} %collective-permute-done.8.through_ref), custom_call_target="tpu_custom_call", output_to_operand_aliasing={{1}: (1, {})} | custom-call | bytes 6291456 | tf_op jit(solution)/shard_map/fetch/pallas_call | solution.py:57
  18.2 1.9 %collective-permute-start.5 = (bf16[32,3072]{1,0:T(8,128)(2,1)S(1)}, bf16[32,3072]{1,0:T(8,128)(2,1)S(1)}, u32[]{:S(2)}, u32[]{:S(2)}) collective-permute-start(bf16[32,3072]{1,0:T(8,128)(2,1)S(1)} %collective-permute-done.3.refs_4_), channel_id=1, source_target_pairs={{2,0},{4,2},{6,4},{7,6},{5,7},{3,5},{1,3},{0,1},{10,8},{12,10},{14... | collective-permute-start | bytes 589832 | tf_op jit(solution)/shard_map/ppermute | solution.py:83
  20.1 1.9 %fetch.7 = (bf16[3072,512]{1,0:T(8,128)(2,1)S(1)}, bf16[32,3072]{1,0:T(8,128)(2,1)S(1)}) custom-call(bf16[3,6144,512]{2,1,0:T(8,128)(2,1)} %weight_ref.1, bf16[32,3072]{1,0:T(8,128)(2,1)S(1)} %collective-permute-done.2.through_ref), custom_call_target="tpu_custom_call", output_to_operand_aliasing={{1}: (1, {})} | custom-call | bytes 6291456 | tf_op jit(solution)/shard_map/fetch/pallas_call | solution.py:57
  22.4 1.9 %collective-permute-start.13 = (bf16[32,3072]{1,0:T(8,128)(2,1)S(1)}, bf16[32,3072]{1,0:T(8,128)(2,1)S(1)}, u32[]{:S(2)}, u32[]{:S(2)}) collective-permute-start(bf16[32,3072]{1,0:T(8,128)(2,1)S(1)} %collective-permute-done.11.refs_4_), channel_id=1, source_target_pairs={{2,0},{4,2},{6,4},{7,6},{5,7},{3,5},{1,3},{0,1},{10,8},{12,10},{14... | collective-permute-start | bytes 589832 | tf_op jit(solution)/shard_map/ppermute | solution.py:83
  24.5 1.9 %fetch.11 = (bf16[512,3072]{1,0:T(8,128)(2,1)S(1)}, bf16[32,3072]{1,0:T(8,128)(2,1)S(1)}) custom-call(bf16[512,6144]{1,0:T(8,128)(2,1)} %source_ref.11, bf16[32,3072]{1,0:T(8,128)(2,1)S(1)} %collective-permute-done.10.through_ref), custom_call_target="tpu_custom_call", output_to_operand_aliasing={{1}: (1, {})} | custom-call | bytes 6291456 | tf_op jit(solution)/shard_map/fetch/pallas_call | solution.py:57
  26.6 1.9 %collective-permute-start.7 = (bf16[32,1536]{1,0:T(8,128)(2,1)S(1)}, bf16[32,1536]{1,0:T(8,128)(2,1)S(1)}, u32[]{:S(2)}, u32[]{:S(2)}) collective-permute-start(bf16[32,1536]{1,0:T(8,128)(2,1)S(1)} %slice.24), channel_id=1, source_target_pairs={{2,0},{4,2},{6,4},{7,6},{5,7},{3,5},{1,3},{0,1},{10,8},{12,10},{14... | collective-permute-start | bytes 294920 | tf_op jit(solution)/shard_map/ppermute | solution.py:91
  28.7 1.9 %fetch.8 = (bf16[512,3072]{1,0:T(8,128)(2,1)S(1)}, bf16[32,3072]{1,0:T(8,128)(2,1)S(1)}) custom-call(bf16[512,6144]{1,0:T(8,128)(2,1)} %source_ref.11, bf16[32,3072]{1,0:T(8,128)(2,1)S(1)} %collective-permute-done.4.through_ref), custom_call_target="tpu_custom_call", output_to_operand_aliasing={{1}: (1, {})} | custom-call | bytes 6291456 | tf_op jit(solution)/shard_map/fetch/pallas_call | solution.py:57
  30.8 1.9 %collective-permute-start.15 = (bf16[32,1536]{1,0:T(8,128)(2,1)S(1)}, bf16[32,1536]{1,0:T(8,128)(2,1)S(1)}, u32[]{:S(2)}, u32[]{:S(2)}) collective-permute-start(bf16[32,1536]{1,0:T(8,128)(2,1)S(1)} %slice.26), channel_id=1, source_target_pairs={{2,0},{4,2},{6,4},{7,6},{5,7},{3,5},{1,3},{0,1},{10,8},{12,10},{14... | collective-permute-start | bytes 294920 | tf_op jit(solution)/shard_map/ppermute | solution.py:91
  33.2 2.2 %collective-permute-done.6.refs_7_ = bf16[32,1536]{1,0:T(8,128)(2,1)S(1)} collective-permute-done((bf16[32,1536]{1,0:T(8,128)(2,1)S(1)}, bf16[32,1536]{1,0:T(8,128)(2,1)S(1)}, u32[]{:S(2)}, u32[]{:S(2)}) %collective-permute-start.6) | collective-permute-done | bytes 98336 | tf_op jit(solution)/shard_map/ppermute | solution.py:90
  35.4 1.8 %first_pass.1 = (f32[2,256,512]{2,1,0:T(8,128)S(1)}, bf16[256,3072]{1,0:T(8,128)(2,1)S(1)}) custom-call(bf16[32,3072]{1,0:T(8,128)(2,1)S(1)} %get-tuple-element.100.refs_0_, bf16[32,3072]{1,0:T(8,128)(2,1)S(1)} %get-tuple-element.52.refs_1_, bf16[32,3072]{1,0:T(8,128)(2,1)S(1)} %collective-permute-done.1.refs_2_, ...), custom_call_target="tpu_custom_call" | custom-call | flops 1610612736 | bytes 6291456 | tf_op jit(solution)/shard_map/first_pass/pallas_call | solution.py:116
  37.2 0.6 collective-permute-done.14.refs_7_
  37.8 2.2 %keys_and_values.1 = (bf16[256,512]{1,0:T(8,128)(2,1)S(1)}, bf16[256,512]{1,0:T(8,128)(2,1)S(1)}, bf16[4,128,128]{2,1,0:T(8,128)(2,1)S(1)}, bf16[256,3072]{1,0:T(8,128)(2,1)S(1)}) custom-call(bf16[32,3072]{1,0:T(8,128)(2,1)S(1)} %get-tuple-element.58.refs_0_, bf16[32,3072]{1,0:T(8,128)(2,1)S(1)} %get-tuple-element.59.refs_1_, ...), custom_call_target="tpu_custom_call" | custom-call | flops 1610612736 | bytes 6291456 | tf_op jit(solution)/shard_map/keys_and_values/pallas_call | solution.py:157
  40.1 1.3 %collective-permute-done.16.two_ref.refs_0_ = bf16[4,128,128]{2,1,0:T(8,128)(2,1)S(1)} collective-permute-done((bf16[4,128,128]{2,1,0:T(8,128)(2,1)S(1)}, bf16[4,128,128]{2,1,0:T(8,128)(2,1)S(1)}, u32[]{:S(2)}, u32[]{:S(2)}) %collective-permute-start.16) | collective-permute-done | bytes 131104 | tf_op jit(solution)/shard_map/ppermute | solution.py:387
  41.5 1.6 %collective-permute-start.17 = (bf16[4,128,128]{2,1,0:T(8,128)(2,1)S(1)}, bf16[4,128,128]{2,1,0:T(8,128)(2,1)S(1)}, u32[]{:S(2)}, u32[]{:S(2)}) collective-permute-start(bf16[4,128,128]{2,1,0:T(8,128)(2,1)S(1)} %add_states.1), channel_id=1, source_target_pairs={{0,16},{8,24},{16,0},{24,8},{1,17},{9,25},{17,1},{25,9},{2,18},{10... | collective-permute-start | bytes 393224 | tf_op jit(solution)/shard_map/ppermute | solution.py:387
  43.1 4.1 %queries_within.1 = (bf16[256,512]{1,0:T(8,128)(2,1)S(1)}, f32[256,512]{1,0:T(8,128)S(1)}) custom-call(bf16[256,3072]{1,0:T(8,128)(2,1)S(1)} %get-tuple-element.57.first_ref, bf16[256,3072]{1,0:T(8,128)(2,1)S(1)} %get-tuple-element.64.second_ref, bf16[3,6144,512]{2,1,0:T(8,128)(2,1)} %weight_ref.1, bf16[256,512]{1,0:T(8,128)(2,1)S(1)} %get-tuple-element.65.k_ref, ...), custom_call_target="tpu_custom_call" | custom-call | flops 1744830464 | bytes 6291456 | tf_op jit(solution)/shard_map/queries_within/pallas_call | solution.py:222
  47.3 1.5 %attend_and_project.1 = (bf16[256,512]{1,0:T(8,128)(2,1)S(1)}, bf16[32,3072]{1,0:T(8,128)(2,1)S(1)}, bf16[32,3072]{1,0:T(8,128)(2,1)S(1)}) custom-call(bf16[256,512]{1,0:T(8,128)(2,1)S(1)} %get-tuple-element.67.q_ref, f32[256,512]{1,0:T(8,128)S(1)} %get-tuple-element.68.within_ref, f32[4,128,128]{2,1,0:T(8,128)S(1)} %copy-done, f32[1,512]{1,0:T(1,128)S(1)} %bitcast.1, ...), custom_call_target="tpu_custom_call" | custom-call | flops 1610612736 | bytes 6291456 | tf_op jit(solution)/shard_map/attend_and_project/pallas_call | solution.py:271
  48.8 0.6 collective-permute-start.24
  49.4 1.5 %collective-permute-start.25 = (bf16[32,3072]{1,0:T(8,128)(2,1)S(1)}, bf16[32,3072]{1,0:T(8,128)(2,1)S(1)}, u32[]{:S(2)}, u32[]{:S(2)}) collective-permute-start(bf16[32,3072]{1,0:T(8,128)(2,1)S(1)} %get-tuple-element.90), channel_id=1, source_target_pairs={{2,0},{4,2},{6,4},{7,6},{5,7},{3,5},{1,3},{0,1},{10,8},{12,10},{14... | collective-permute-start | bytes 589832 | tf_op jit(solution)/shard_map/ppermute | solution.py:360
  50.9 1.6 %project_rest.1 = (bf16[32,3072]{1,0:T(8,128)(2,1)S(1)}, bf16[32,3072]{1,0:T(8,128)(2,1)S(1)}, bf16[32,3072]{1,0:T(8,128)(2,1)S(1)}, bf16[32,3072]{1,0:T(8,128)(...) custom-call(bf16[256,512]{1,0:T(8,128)(2,1)S(1)} %get-tuple-element., ...), custom_call_target="tpu_custom_call" | custom-call | flops 5000000000 | bytes 6291456 | tf_op jit(solution)/shard_map/project_rest/pallas_call | solution.py:290
  52.5 0.6 collective-permute-start.18
  53.1 1.5 %collective-permute-start.19 = (bf16[32,3072]{1,0:T(8,128)(2,1)S(1)}, bf16[32,3072]{1,0:T(8,128)(2,1)S(1)}, u32[]{:S(2)}, u32[]{:S(2)}) collective-permute-start(bf16[32,3072]{1,0:T(8,128)(2,1)S(1)} %get-tuple-element.79), channel_id=1, source_target_pairs={{2,0},{4,2},{6,4},{7,6},{5,7},{3,5},{1,3},{0,1},{10,8},{12,10},{14... | collective-permute-start | bytes 589832 | tf_op jit(solution)/shard_map/ppermute | solution.py:360
  54.6 2.0 %collective-permute-done.24.gr = bf16[32,3072]{1,0:T(8,128)(2,1)S(1)} collective-permute-done((bf16[32,3072]{1,0:T(8,128)(2,1)S(1)}, bf16[32,3072]{1,0:T(8,128)(2,1)S(1)}, u32[]{:S(2)}, u32[]{:S(2)}) %collective-permute-start.24) | collective-permute-done | bytes 196640 | tf_op jit(solution)/shard_map/ppermute | solution.py:360
  56.9 1.6 %collective-permute-start.26 = (bf16[32,3072]{1,0:T(8,128)(2,1)S(1)}, bf16[32,3072]{1,0:T(8,128)(2,1)S(1)}, u32[]{:S(2)}, u32[]{:S(2)}) collective-permute-start(bf16[32,3072]{1,0:T(8,128)(2,1)S(1)} %get-tuple-element.91), channel_id=1, source_target_pairs={{0,2},{2,4},{4,6},{6,7},{7,5},{5,3},{3,1},{1,0},{8,10},{10,12},{12... | collective-permute-start | bytes 589832 | tf_op jit(solution)/shard_map/ppermute | solution.py:360
  59.0 1.8 %collective-permute-done.18.gr = bf16[32,3072]{1,0:T(8,128)(2,1)S(1)} collective-permute-done((bf16[32,3072]{1,0:T(8,128)(2,1)S(1)}, bf16[32,3072]{1,0:T(8,128)(2,1)S(1)}, u32[]{:S(2)}, u32[]{:S(2)}) %collective-permute-start.18) | collective-permute-done | bytes 196640 | tf_op jit(solution)/shard_map/ppermute | solution.py:360
  61.1 1.6 %collective-permute-start.20 = (bf16[32,3072]{1,0:T(8,128)(2,1)S(1)}, bf16[32,3072]{1,0:T(8,128)(2,1)S(1)}, u32[]{:S(2)}, u32[]{:S(2)}) collective-permute-start(bf16[32,3072]{1,0:T(8,128)(2,1)S(1)} %get-tuple-element.80), channel_id=1, source_target_pairs={{0,2},{2,4},{4,6},{6,7},{7,5},{5,3},{3,1},{1,0},{8,10},{10,12},{12... | collective-permute-start | bytes 589832 | tf_op jit(solution)/shard_map/ppermute | solution.py:360
  63.2 1.8 %collective-permute-done.26.gr = bf16[32,3072]{1,0:T(8,128)(2,1)S(1)} collective-permute-done((bf16[32,3072]{1,0:T(8,128)(2,1)S(1)}, bf16[32,3072]{1,0:T(8,128)(2,1)S(1)}, u32[]{:S(2)}, u32[]{:S(2)}) %collective-permute-start.26) | collective-permute-done | bytes 196640 | tf_op jit(solution)/shard_map/ppermute | solution.py:360
  65.4 1.6 %collective-permute-start.28 = (bf16[32,3072]{1,0:T(8,128)(2,1)S(1)}, bf16[32,3072]{1,0:T(8,128)(2,1)S(1)}, u32[]{:S(2)}, u32[]{:S(2)}) collective-permute-start(bf16[32,3072]{1,0:T(8,128)(2,1)S(1)} %get-tuple-element.94), channel_id=1, source_target_pairs={{0,2},{2,4},{4,6},{6,7},{7,5},{5,3},{3,1},{1,0},{8,10},{10,12},{12... | collective-permute-start | bytes 589832 | tf_op jit(solution)/shard_map/ppermute | solution.py:360
  67.0 0.4 collective-permute-start.29
  67.5 1.7 %collective-permute-done.20.gr = bf16[32,3072]{1,0:T(8,128)(2,1)S(1)} collective-permute-done((bf16[32,3072]{1,0:T(8,128)(2,1)S(1)}, bf16[32,3072]{1,0:T(8,128)(2,1)S(1)}, u32[]{:S(2)}, u32[]{:S(2)}) %collective-permute-start.20) | collective-permute-done | bytes 196640 | tf_op jit(solution)/shard_map/ppermute | solution.py:360
  69.2 1.4 %collective-permute-done.21.gl = bf16[32,3072]{1,0:T(8,128)(2,1)S(1)} collective-permute-done((bf16[32,3072]{1,0:T(8,128)(2,1)S(1)}, bf16[32,3072]{1,0:T(8,128)(2,1)S(1)}, u32[]{:S(2)}, u32[]{:S(2)}) %collective-permute-start.21) | collective-permute-done | bytes 196640 | tf_op jit(solution)/shard_map/ppermute | solution.py:360
  70.7 0.5 collective-permute-start.22
  71.2 1.6 %collective-permute-start.23 = (bf16[32,3072]{1,0:T(8,128)(2,1)S(1)}, bf16[32,3072]{1,0:T(8,128)(2,1)S(1)}, u32[]{:S(2)}, u32[]{:S(2)}) collective-permute-start(bf16[32,3072]{1,0:T(8,128)(2,1)S(1)} %get-tuple-element.84), channel_id=1, source_target_pairs={{0,2},{2,4},{4,6},{6,7},{7,5},{5,3},{3,1},{1,0},{8,10},{10,12},{12... | collective-permute-start | bytes 589832 | tf_op jit(solution)/shard_map/ppermute | solution.py:360
  72.8 0.6 collective-permute-done.28.gr
  73.3 1.5 %collective-permute-done.29.gl = bf16[32,3072]{1,0:T(8,128)(2,1)S(1)} collective-permute-done((bf16[32,3072]{1,0:T(8,128)(2,1)S(1)}, bf16[32,3072]{1,0:T(8,128)(2,1)S(1)}, u32[]{:S(2)}, u32[]{:S(2)}) %collective-permute-start.29) | collective-permute-done | bytes 196640 | tf_op jit(solution)/shard_map/ppermute | solution.py:360
  74.9 1.6 %collective-permute-start.30 = (bf16[32,3072]{1,0:T(8,128)(2,1)S(1)}, bf16[32,3072]{1,0:T(8,128)(2,1)S(1)}, u32[]{:S(2)}, u32[]{:S(2)}) collective-permute-start(bf16[32,3072]{1,0:T(8,128)(2,1)S(1)} %get-tuple-element.97), channel_id=1, source_target_pairs={{0,2},{2,4},{4,6},{6,7},{7,5},{5,3},{3,1},{1,0},{8,10},{10,12},{12... | collective-permute-start | bytes 589832 | tf_op jit(solution)/shard_map/ppermute | solution.py:360
  76.5 0.5 collective-permute-start.31
  77.0 2.0 %collective-permute-done.22.got_first = bf16[32,3072]{1,0:T(8,128)(2,1)S(1)} collective-permute-done((bf16[32,3072]{1,0:T(8,128)(2,1)S(1)}, bf16[32,3072]{1,0:T(8,128)(2,1)S(1)}, u32[]{:S(2)}, u32[]{:S(2)}) %collective-permute-start.22) | collective-permute-done | bytes 196640 | tf_op jit(solution)/shard_map/ppermute | solution.py:360
  79.1 1.8 %collective-permute-done.30.first = bf16[32,3072]{1,0:T(8,128)(2,1)S(1)} collective-permute-done((bf16[32,3072]{1,0:T(8,128)(2,1)S(1)}, bf16[32,3072]{1,0:T(8,128)(2,1)S(1)}, u32[]{:S(2)}, u32[]{:S(2)}) %collective-permute-start.30) | collective-permute-done | bytes 196640 | tf_op jit(solution)/shard_map/ppermute | solution.py:360
  80.8 1.3 %collective-permute-done.31.second = bf16[32,3072]{1,0:T(8,128)(2,1)S(1)} collective-permute-done((bf16[32,3072]{1,0:T(8,128)(2,1)S(1)}, bf16[32,3072]{1,0:T(8,128)(2,1)S(1)}, u32[]{:S(2)}, u32[]{:S(2)}) %collective-permute-start.31) | collective-permute-done | bytes 196640 | tf_op jit(solution)/shard_map/ppermute | solution.py:360
  82.1 0.8 finish.1
  (44 shorter events, 5.4 us)
Async XLA Ops:
  1.1 8.6 %collective-permute-start.1 = (bf16[32,3072]{1,0:T(8,128)(2,1)S(1)}, bf16[32,3072]{1,0:T(8,128)(2,1)S(1)}, u32[]{:S(2)}, u32[]{:S(2)}) collective-permute-start(bf16[32,3072]{1,0:T(8,128)(2,1)S(1)} %get-tuple-element.100.refs_0_), channel_id=1, source_target_pairs={{2,0},{4,2},{6,4},{7,6},{5,7},{3,5},{1,3},{0,1},{10,8},{12,10},{14... | collective-permute-start | bytes 589832 | tf_op jit(solution)/shard_map/ppermute | solution.py:83
  4.0 7.4 %collective-permute-start = (bf16[32,3072]{1,0:T(8,128)(2,1)S(1)}, bf16[32,3072]{1,0:T(8,128)(2,1)S(1)}, u32[]{:S(2)}, u32[]{:S(2)}) collective-permute-start(bf16[32,3072]{1,0:T(8,128)(2,1)S(1)} %get-tuple-element.100.refs_0_), channel_id=1, source_target_pairs={{0,2},{2,4},{4,6},{6,7},{7,5},{5,3},{3,1},{1,0},{8,10},{10,12},{12... | collective-permute-start | bytes 589832 | tf_op jit(solution)/shard_map/ppermute | solution.py:82
  6.1 7.9 %collective-permute-start.9 = (bf16[32,3072]{1,0:T(8,128)(2,1)S(1)}, bf16[32,3072]{1,0:T(8,128)(2,1)S(1)}, u32[]{:S(2)}, u32[]{:S(2)}) collective-permute-start(bf16[32,3072]{1,0:T(8,128)(2,1)S(1)} %get-tuple-element.58.refs_0_), channel_id=1, source_target_pairs={{2,0},{4,2},{6,4},{7,6},{5,7},{3,5},{1,3},{0,1},{10,8},{12,10},{14... | collective-permute-start | bytes 589832 | tf_op jit(solution)/shard_map/ppermute | solution.py:83
  8.0 7.8 %collective-permute-start.8 = (bf16[32,3072]{1,0:T(8,128)(2,1)S(1)}, bf16[32,3072]{1,0:T(8,128)(2,1)S(1)}, u32[]{:S(2)}, u32[]{:S(2)}) collective-permute-start(bf16[32,3072]{1,0:T(8,128)(2,1)S(1)} %get-tuple-element.58.refs_0_), channel_id=1, source_target_pairs={{0,2},{2,4},{4,6},{6,7},{7,5},{5,3},{3,1},{1,0},{8,10},{10,12},{12... | collective-permute-start | bytes 589832 | tf_op jit(solution)/shard_map/ppermute | solution.py:82
  9.7 8.5 %collective-permute-start.3 = (bf16[32,3072]{1,0:T(8,128)(2,1)S(1)}, bf16[32,3072]{1,0:T(8,128)(2,1)S(1)}, u32[]{:S(2)}, u32[]{:S(2)}) collective-permute-start(bf16[32,3072]{1,0:T(8,128)(2,1)S(1)} %collective-permute-done.1.refs_2_), channel_id=1, source_target_pairs={{2,0},{4,2},{6,4},{7,6},{5,7},{3,5},{1,3},{0,1},{10,8},{12,10},{14... | collective-permute-start | bytes 589832 | tf_op jit(solution)/shard_map/ppermute | solution.py:83
  13.3 6.8 %collective-permute-start.2 = (bf16[32,3072]{1,0:T(8,128)(2,1)S(1)}, bf16[32,3072]{1,0:T(8,128)(2,1)S(1)}, u32[]{:S(2)}, u32[]{:S(2)}) collective-permute-start(bf16[32,3072]{1,0:T(8,128)(2,1)S(1)} %get-tuple-element.52.refs_1_), channel_id=1, source_target_pairs={{0,2},{2,4},{4,6},{6,7},{7,5},{5,3},{3,1},{1,0},{8,10},{10,12},{12... | collective-permute-start | bytes 589832 | tf_op jit(solution)/shard_map/ppermute | solution.py:82
  14.0 8.4 %collective-permute-start.11 = (bf16[32,3072]{1,0:T(8,128)(2,1)S(1)}, bf16[32,3072]{1,0:T(8,128)(2,1)S(1)}, u32[]{:S(2)}, u32[]{:S(2)}) collective-permute-start(bf16[32,3072]{1,0:T(8,128)(2,1)S(1)} %collective-permute-done.9.refs_2_), channel_id=1, source_target_pairs={{2,0},{4,2},{6,4},{7,6},{5,7},{3,5},{1,3},{0,1},{10,8},{12,10},{14... | collective-permute-start | bytes 589832 | tf_op jit(solution)/shard_map/ppermute | solution.py:83
  17.8 6.7 %collective-permute-start.10 = (bf16[32,3072]{1,0:T(8,128)(2,1)S(1)}, bf16[32,3072]{1,0:T(8,128)(2,1)S(1)}, u32[]{:S(2)}, u32[]{:S(2)}) collective-permute-start(bf16[32,3072]{1,0:T(8,128)(2,1)S(1)} %get-tuple-element.59.refs_1_), channel_id=1, source_target_pairs={{0,2},{2,4},{4,6},{6,7},{7,5},{5,3},{3,1},{1,0},{8,10},{10,12},{12... | collective-permute-start | bytes 589832 | tf_op jit(solution)/shard_map/ppermute | solution.py:82
  18.2 8.4 %collective-permute-start.5 = (bf16[32,3072]{1,0:T(8,128)(2,1)S(1)}, bf16[32,3072]{1,0:T(8,128)(2,1)S(1)}, u32[]{:S(2)}, u32[]{:S(2)}) collective-permute-start(bf16[32,3072]{1,0:T(8,128)(2,1)S(1)} %collective-permute-done.3.refs_4_), channel_id=1, source_target_pairs={{2,0},{4,2},{6,4},{7,6},{5,7},{3,5},{1,3},{0,1},{10,8},{12,10},{14... | collective-permute-start | bytes 589832 | tf_op jit(solution)/shard_map/ppermute | solution.py:83
  22.0 6.7 %collective-permute-start.4 = (bf16[32,3072]{1,0:T(8,128)(2,1)S(1)}, bf16[32,3072]{1,0:T(8,128)(2,1)S(1)}, u32[]{:S(2)}, u32[]{:S(2)}) collective-permute-start(bf16[32,3072]{1,0:T(8,128)(2,1)S(1)} %get-tuple-element.53.refs_3_), channel_id=1, source_target_pairs={{0,2},{2,4},{4,6},{6,7},{7,5},{5,3},{3,1},{1,0},{8,10},{10,12},{12... | collective-permute-start | bytes 589832 | tf_op jit(solution)/shard_map/ppermute | solution.py:82
  22.4 8.4 %collective-permute-start.13 = (bf16[32,3072]{1,0:T(8,128)(2,1)S(1)}, bf16[32,3072]{1,0:T(8,128)(2,1)S(1)}, u32[]{:S(2)}, u32[]{:S(2)}) collective-permute-start(bf16[32,3072]{1,0:T(8,128)(2,1)S(1)} %collective-permute-done.11.refs_4_), channel_id=1, source_target_pairs={{2,0},{4,2},{6,4},{7,6},{5,7},{3,5},{1,3},{0,1},{10,8},{12,10},{14... | collective-permute-start | bytes 589832 | tf_op jit(solution)/shard_map/ppermute | solution.py:83
  26.4 6.8 %collective-permute-start.12 = (bf16[32,3072]{1,0:T(8,128)(2,1)S(1)}, bf16[32,3072]{1,0:T(8,128)(2,1)S(1)}, u32[]{:S(2)}, u32[]{:S(2)}) collective-permute-start(bf16[32,3072]{1,0:T(8,128)(2,1)S(1)} %get-tuple-element.60.refs_3_), channel_id=1, source_target_pairs={{0,2},{2,4},{4,6},{6,7},{7,5},{5,3},{3,1},{1,0},{8,10},{10,12},{12... | collective-permute-start | bytes 589832 | tf_op jit(solution)/shard_map/ppermute | solution.py:82
  26.6 6.6 %collective-permute-start.7 = (bf16[32,1536]{1,0:T(8,128)(2,1)S(1)}, bf16[32,1536]{1,0:T(8,128)(2,1)S(1)}, u32[]{:S(2)}, u32[]{:S(2)}) collective-permute-start(bf16[32,1536]{1,0:T(8,128)(2,1)S(1)} %slice.24), channel_id=1, source_target_pairs={{2,0},{4,2},{6,4},{7,6},{5,7},{3,5},{1,3},{0,1},{10,8},{12,10},{14... | collective-permute-start | bytes 294920 | tf_op jit(solution)/shard_map/ppermute | solution.py:91
  30.6 4.8 %collective-permute-start.6 = (bf16[32,1536]{1,0:T(8,128)(2,1)S(1)}, bf16[32,1536]{1,0:T(8,128)(2,1)S(1)}, u32[]{:S(2)}, u32[]{:S(2)}) collective-permute-start(bf16[32,1536]{1,0:T(8,128)(2,1)S(1)} %slice.19), channel_id=1, source_target_pairs={{0,2},{2,4},{4,6},{6,7},{7,5},{5,3},{3,1},{1,0},{8,10},{10,12},{12... | collective-permute-start | bytes 294920 | tf_op jit(solution)/shard_map/ppermute | solution.py:90
  30.8 6.4 %collective-permute-start.15 = (bf16[32,1536]{1,0:T(8,128)(2,1)S(1)}, bf16[32,1536]{1,0:T(8,128)(2,1)S(1)}, u32[]{:S(2)}, u32[]{:S(2)}) collective-permute-start(bf16[32,1536]{1,0:T(8,128)(2,1)S(1)} %slice.26), channel_id=1, source_target_pairs={{2,0},{4,2},{6,4},{7,6},{5,7},{3,5},{1,3},{0,1},{10,8},{12,10},{14... | collective-permute-start | bytes 294920 | tf_op jit(solution)/shard_map/ppermute | solution.py:91
  33.1 4.7 %collective-permute-start.14 = (bf16[32,1536]{1,0:T(8,128)(2,1)S(1)}, bf16[32,1536]{1,0:T(8,128)(2,1)S(1)}, u32[]{:S(2)}, u32[]{:S(2)}) collective-permute-start(bf16[32,1536]{1,0:T(8,128)(2,1)S(1)} %slice.25), channel_id=1, source_target_pairs={{0,2},{2,4},{4,6},{6,7},{7,5},{5,3},{3,1},{1,0},{8,10},{10,12},{12... | collective-permute-start | bytes 294920 | tf_op jit(solution)/shard_map/ppermute | solution.py:90
  40.1 1.4 %collective-permute-start.16 = (bf16[4,128,128]{2,1,0:T(8,128)(2,1)S(1)}, bf16[4,128,128]{2,1,0:T(8,128)(2,1)S(1)}, u32[]{:S(2)}, u32[]{:S(2)}) collective-permute-start(bf16[4,128,128]{2,1,0:T(8,128)(2,1)S(1)} %get-tuple-element.71.one_ref), channel_id=1, source_target_pairs={{0,8},{8,0},{16,24},{24,16},{1,9},{9,1},{17,25},{25,17},{2,10},{10... | collective-permute-start | bytes 393224 | tf_op jit(solution)/shard_map/ppermute | solution.py:387
  41.5 5.7 %collective-permute-start.17 = (bf16[4,128,128]{2,1,0:T(8,128)(2,1)S(1)}, bf16[4,128,128]{2,1,0:T(8,128)(2,1)S(1)}, u32[]{:S(2)}, u32[]{:S(2)}) collective-permute-start(bf16[4,128,128]{2,1,0:T(8,128)(2,1)S(1)} %add_states.1), channel_id=1, source_target_pairs={{0,16},{8,24},{16,0},{24,8},{1,17},{9,25},{17,1},{25,9},{2,18},{10... | collective-permute-start | bytes 393224 | tf_op jit(solution)/shard_map/ppermute | solution.py:387
  43.1 4.2 %copy-start = (f32[4,128,128]{2,1,0:T(8,128)S(1)}, f32[4,128,128]{2,1,0:T(8,128)}, u32[]{:S(2)}) copy-start(f32[4,128,128]{2,1,0:T(8,128)} %initial_ref.1) | copy-start | bytes 786436
  43.1 4.2 %copy-start.1 = (f32[512]{0:T(512)S(1)}, f32[512]{0:T(512)}, u32[]{:S(2)}) copy-start(f32[512]{0:T(512)} %param.8) | copy-start | bytes 6148
  48.8 7.7 %collective-permute-start.24 = (bf16[32,3072]{1,0:T(8,128)(2,1)S(1)}, bf16[32,3072]{1,0:T(8,128)(2,1)S(1)}, u32[]{:S(2)}, u32[]{:S(2)}) collective-permute-start(bf16[32,3072]{1,0:T(8,128)(2,1)S(1)} %get-tuple-element.88), channel_id=1, source_target_pairs={{0,2},{2,4},{4,6},{6,7},{7,5},{5,3},{3,1},{1,0},{8,10},{10,12},{12... | collective-permute-start | bytes 589832 | tf_op jit(solution)/shard_map/ppermute | solution.py:360
  49.4 7.4 %collective-permute-start.25 = (bf16[32,3072]{1,0:T(8,128)(2,1)S(1)}, bf16[32,3072]{1,0:T(8,128)(2,1)S(1)}, u32[]{:S(2)}, u32[]{:S(2)}) collective-permute-start(bf16[32,3072]{1,0:T(8,128)(2,1)S(1)} %get-tuple-element.90), channel_id=1, source_target_pairs={{2,0},{4,2},{6,4},{7,6},{5,7},{3,5},{1,3},{0,1},{10,8},{12,10},{14... | collective-permute-start | bytes 589832 | tf_op jit(solution)/shard_map/ppermute | solution.py:360
  52.5 8.3 %collective-permute-start.18 = (bf16[32,3072]{1,0:T(8,128)(2,1)S(1)}, bf16[32,3072]{1,0:T(8,128)(2,1)S(1)}, u32[]{:S(2)}, u32[]{:S(2)}) collective-permute-start(bf16[32,3072]{1,0:T(8,128)(2,1)S(1)} %get-tuple-element.77), channel_id=1, source_target_pairs={{0,2},{2,4},{4,6},{6,7},{7,5},{5,3},{3,1},{1,0},{8,10},{10,12},{12... | collective-permute-start | bytes 589832 | tf_op jit(solution)/shard_map/ppermute | solution.py:360
  53.1 7.9 %collective-permute-start.19 = (bf16[32,3072]{1,0:T(8,128)(2,1)S(1)}, bf16[32,3072]{1,0:T(8,128)(2,1)S(1)}, u32[]{:S(2)}, u32[]{:S(2)}) collective-permute-start(bf16[32,3072]{1,0:T(8,128)(2,1)S(1)} %get-tuple-element.79), channel_id=1, source_target_pairs={{2,0},{4,2},{6,4},{7,6},{5,7},{3,5},{1,3},{0,1},{10,8},{12,10},{14... | collective-permute-start | bytes 589832 | tf_op jit(solution)/shard_map/ppermute | solution.py:360
  56.9 8.1 %collective-permute-start.26 = (bf16[32,3072]{1,0:T(8,128)(2,1)S(1)}, bf16[32,3072]{1,0:T(8,128)(2,1)S(1)}, u32[]{:S(2)}, u32[]{:S(2)}) collective-permute-start(bf16[32,3072]{1,0:T(8,128)(2,1)S(1)} %get-tuple-element.91), channel_id=1, source_target_pairs={{0,2},{2,4},{4,6},{6,7},{7,5},{5,3},{3,1},{1,0},{8,10},{10,12},{12... | collective-permute-start | bytes 589832 | tf_op jit(solution)/shard_map/ppermute | solution.py:360
  58.5 6.8 %collective-permute-start.27 = (bf16[32,3072]{1,0:T(8,128)(2,1)S(1)}, bf16[32,3072]{1,0:T(8,128)(2,1)S(1)}, u32[]{:S(2)}, u32[]{:S(2)}) collective-permute-start(bf16[32,3072]{1,0:T(8,128)(2,1)S(1)} %get-tuple-element.93), channel_id=1, source_target_pairs={{2,0},{4,2},{6,4},{7,6},{5,7},{3,5},{1,3},{0,1},{10,8},{12,10},{14... | collective-permute-start | bytes 589832 | tf_op jit(solution)/shard_map/ppermute | solution.py:360
  61.1 8.1 %collective-permute-start.20 = (bf16[32,3072]{1,0:T(8,128)(2,1)S(1)}, bf16[32,3072]{1,0:T(8,128)(2,1)S(1)}, u32[]{:S(2)}, u32[]{:S(2)}) collective-permute-start(bf16[32,3072]{1,0:T(8,128)(2,1)S(1)} %get-tuple-element.80), channel_id=1, source_target_pairs={{0,2},{2,4},{4,6},{6,7},{7,5},{5,3},{3,1},{1,0},{8,10},{10,12},{12... | collective-permute-start | bytes 589832 | tf_op jit(solution)/shard_map/ppermute | solution.py:360
  62.8 7.8 %collective-permute-start.21 = (bf16[32,3072]{1,0:T(8,128)(2,1)S(1)}, bf16[32,3072]{1,0:T(8,128)(2,1)S(1)}, u32[]{:S(2)}, u32[]{:S(2)}) collective-permute-start(bf16[32,3072]{1,0:T(8,128)(2,1)S(1)} %get-tuple-element.82), channel_id=1, source_target_pairs={{2,0},{4,2},{6,4},{7,6},{5,7},{3,5},{1,3},{0,1},{10,8},{12,10},{14... | collective-permute-start | bytes 589832 | tf_op jit(solution)/shard_map/ppermute | solution.py:360
  65.4 7.9 %collective-permute-start.28 = (bf16[32,3072]{1,0:T(8,128)(2,1)S(1)}, bf16[32,3072]{1,0:T(8,128)(2,1)S(1)}, u32[]{:S(2)}, u32[]{:S(2)}) collective-permute-start(bf16[32,3072]{1,0:T(8,128)(2,1)S(1)} %get-tuple-element.94), channel_id=1, source_target_pairs={{0,2},{2,4},{4,6},{6,7},{7,5},{5,3},{3,1},{1,0},{8,10},{10,12},{12... | collective-permute-start | bytes 589832 | tf_op jit(solution)/shard_map/ppermute | solution.py:360
  67.0 7.8 %collective-permute-start.29 = (bf16[32,3072]{1,0:T(8,128)(2,1)S(1)}, bf16[32,3072]{1,0:T(8,128)(2,1)S(1)}, u32[]{:S(2)}, u32[]{:S(2)}) collective-permute-start(bf16[32,3072]{1,0:T(8,128)(2,1)S(1)} %get-tuple-element.96), channel_id=1, source_target_pairs={{2,0},{4,2},{6,4},{7,6},{5,7},{3,5},{1,3},{0,1},{10,8},{12,10},{14... | collective-permute-start | bytes 589832 | tf_op jit(solution)/shard_map/ppermute | solution.py:360
  70.7 8.3 %collective-permute-start.22 = (bf16[32,3072]{1,0:T(8,128)(2,1)S(1)}, bf16[32,3072]{1,0:T(8,128)(2,1)S(1)}, u32[]{:S(2)}, u32[]{:S(2)}) collective-permute-start(bf16[32,3072]{1,0:T(8,128)(2,1)S(1)} %get-tuple-element.83), channel_id=1, source_target_pairs={{2,0},{4,2},{6,4},{7,6},{5,7},{3,5},{1,3},{0,1},{10,8},{12,10},{14... | collective-permute-start | bytes 589832 | tf_op jit(solution)/shard_map/ppermute | solution.py:360
  71.2 7.8 %collective-permute-start.23 = (bf16[32,3072]{1,0:T(8,128)(2,1)S(1)}, bf16[32,3072]{1,0:T(8,128)(2,1)S(1)}, u32[]{:S(2)}, u32[]{:S(2)}) collective-permute-start(bf16[32,3072]{1,0:T(8,128)(2,1)S(1)} %get-tuple-element.84), channel_id=1, source_target_pairs={{0,2},{2,4},{4,6},{6,7},{7,5},{5,3},{3,1},{1,0},{8,10},{10,12},{12... | collective-permute-start | bytes 589832 | tf_op jit(solution)/shard_map/ppermute | solution.py:360
  74.9 5.9 %collective-permute-start.30 = (bf16[32,3072]{1,0:T(8,128)(2,1)S(1)}, bf16[32,3072]{1,0:T(8,128)(2,1)S(1)}, u32[]{:S(2)}, u32[]{:S(2)}) collective-permute-start(bf16[32,3072]{1,0:T(8,128)(2,1)S(1)} %get-tuple-element.97), channel_id=1, source_target_pairs={{0,2},{2,4},{4,6},{6,7},{7,5},{5,3},{3,1},{1,0},{8,10},{10,12},{12... | collective-permute-start | bytes 589832 | tf_op jit(solution)/shard_map/ppermute | solution.py:360
  76.5 5.7 %collective-permute-start.31 = (bf16[32,3072]{1,0:T(8,128)(2,1)S(1)}, bf16[32,3072]{1,0:T(8,128)(2,1)S(1)}, u32[]{:S(2)}, u32[]{:S(2)}) collective-permute-start(bf16[32,3072]{1,0:T(8,128)(2,1)S(1)} %get-tuple-element.98), channel_id=1, source_target_pairs={{2,0},{4,2},{6,4},{7,6},{5,7},{3,5},{1,3},{0,1},{10,8},{12,10},{14... | collective-permute-start | bytes 589832 | tf_op jit(solution)/shard_map/ppermute | solution.py:360

commit v5 on v4

--- a/solution.py
+++ b/solution.py
@@ -48,48 +48,39 @@
     )
 
 
-def fetch(source, index, shape, through):
-    def body(source_ref, through_ref, out_ref, passed_ref, sem):
-        copy = pltpu.make_async_copy(source_ref.at[index], out_ref, sem)
-        copy.start()
-        copy.wait()
-
-    return call(
-        body,
-        (jax.ShapeDtypeStruct(shape, source.dtype), jax.ShapeDtypeStruct(through.shape, through.dtype)),
-        [HBM, ANY],
-        (VMEM, ANY),
-        nbytes=2 * 2 * shape[0] * shape[1],
-        scratch_shapes=[pltpu.SemaphoreType.DMA],
-        input_output_aliases={1: 1},
-        name="fetch",
-    )(in_hbm(source), through)
-
-
-def ring_gather(block, size, right, left, fetches):
-    fetches = list(fetches)
-    brought = []
+def touch(first, second):
+    def body(first_ref, second_ref, first_out, second_out):
+        pass
+
+    return call(
+        body,
+        [jax.ShapeDtypeStruct(first.shape, first.dtype)] * 2,
+        [ANY] * 2,
+        [ANY] * 2,
+        flops=HOP_FLOPS,
+        input_output_aliases={0: 0, 1: 1},
+        limit=1 << 20,
+        name="touch",
+    )(first, second)
+
+
+def ring_gather(block, size, right, left):
     half = block.shape[1] // 2
     quarter = half // 2
     going_right = [block[:, :half], block[:, half:]]
-    source, index, shape = fetches.pop(0)
-    got, going_right[1] = fetch(source, index, shape, going_right[1])
-    brought.append(got)
     going_left = list(going_right)
     held = [[going_right[0]], [going_right[1]]]
-    for _ in range(size // 2 - 1):
+    for hop in range(1, size // 2):
         for part in range(2):
             going_right[part] = lax.ppermute(going_right[part], "fsdp", right)
             going_left[part] = lax.ppermute(going_left[part], "fsdp", left)
-            if fetches:
-                source, index, shape = fetches.pop(0)
-                got, going_right[part] = fetch(source, index, shape, going_right[part])
-                brought.append(got)
+            if hop > 1:
+                going_right[part], going_left[part] = touch(going_right[part], going_left[part])
             held[part] += [going_right[part], going_left[part]]
     for part in range(2):
         held[part].append(lax.ppermute(going_right[part][:, :quarter], "fsdp", right))
         held[part].append(lax.ppermute(going_left[part][:, quarter:], "fsdp", left))
-    return held, brought
+    return held
 
 
 def assemble(pieces, into):
@@ -102,50 +93,49 @@
     into[start : start + rows, quarter:] = pieces[-1][...]
 
 
-def first_pass(pieces, weights, n_rows):
-    half, columns = weights[0].shape
+def first_pass(pieces, weight, n_rows):
+    half, columns = weight.shape[1] // 2, weight.shape[2]
 
     def body(*refs):
         rows = refs[: len(pieces)]
-        weight_refs = refs[len(pieces) : len(pieces) + len(weights)]
-        out_ref, whole = refs[len(pieces) + len(weights) :]
+        weight_ref, out_ref, whole = refs[len(pieces) :]
         assemble(rows, whole)
-        for place, weight_ref in enumerate(weight_refs):
-            out_ref[place] = jnp.dot(whole[...], weight_ref[...], preferred_element_type=F32)
+        for place in range(2):
+            out_ref[place] = jnp.dot(whole[...], weight_ref[1 + place, :half, :], preferred_element_type=F32)
 
     return call(
         body,
         (
-            jax.ShapeDtypeStruct((len(weights), n_rows, columns), F32),
+            jax.ShapeDtypeStruct((2, n_rows, columns), F32),
             jax.ShapeDtypeStruct((n_rows, half), BF16),
         ),
-        [VMEM] * (len(pieces) + len(weights)),
+        [VMEM] * (len(pieces) + 1),
         (VMEM, VMEM),
-        flops=2 * len(weights) * n_rows * half * columns,
-        nbytes=2 * len(weights) * half * columns,
+        flops=4 * n_rows * half * columns,
+        nbytes=4 * half * columns,
         name="first_pass",
-    )(*pieces, *weights)
+    )(*pieces, weight)
 
 
 def feature_map(projected):
     return jnp.where(projected > 0.0, projected + 1.0, jnp.exp(jnp.minimum(projected, 0.0)))
 
 
-def keys_and_values(pieces, key_weight, value_weight, first, head_dim):
+def keys_and_values(pieces, weight, first, head_dim):
     _, n_rows, columns = first.shape
-    half = key_weight.shape[0]
+    half = weight.shape[1] // 2
 
     def body(*refs):
         rows = refs[: len(pieces)]
-        key_ref, value_ref, first_ref, feat_ref, values_ref, state_ref, whole = refs[len(pieces) :]
+        weight_ref, first_ref, feat_ref, values_ref, state_ref, whole = refs[len(pieces) :]
         assemble(rows, whole)
         tile = min(columns, 256)
         for start in range(0, columns, tile):
             span = slice(start, start + tile)
-            projected = first_ref[0, :, span] + jnp.dot(whole[...], key_ref[:, span], preferred_element_type=F32)
+            projected = first_ref[0, :, span] + jnp.dot(whole[...], weight_ref[1, half:, span], preferred_element_type=F32)
             feat = feature_map(projected).astype(BF16)
             feat_ref[:, span] = feat
-            projected = first_ref[1, :, span] + jnp.dot(whole[...], value_ref[:, span], preferred_element_type=F32)
+            projected = first_ref[1, :, span] + jnp.dot(whole[...], weight_ref[2, half:, span], preferred_element_type=F32)
             values = projected.astype(BF16)
             values_ref[:, span] = values
             for head in range(start, start + tile, head_dim):
@@ -162,20 +152,18 @@
             jax.ShapeDtypeStruct((columns // head_dim, head_dim, head_dim), BF16),
             jax.ShapeDtypeStruct((n_rows, half), BF16),
         ),
-        [VMEM] * (len(pieces) + 3),
+        [VMEM] * (len(pieces) + 2),
         (VMEM,) * 4,
         flops=2 * 2 * n_rows * half * columns,
         nbytes=2 * 2 * half * columns,
         name="keys_and_values",
-    )(*pieces, key_weight, value_weight, first)
+    )(*pieces, weight, first)
 
 
 def queries_within(halves, qkv_weight, feat_k, values, head_dim, size, rows):
     n_rows, columns = feat_k.shape
     half = halves[0].shape[1]
     order = slots(size)
-    pieces = 3
-    chunk = half // pieces
 
     def place(shape, axis):
         spot = lax.axis_index("fsdp")
@@ -189,27 +177,10 @@
             start = jnp.where(slot == at, holder * rows, start)
         return start + row - slot * rows
 
-    def body(first_ref, second_ref, weight_ref, k_ref, v_ref, feat_ref, within_ref, local, sems):
-        copies = [
-            pltpu.make_async_copy(
-                weight_ref.at[0, pl.ds(at * chunk, chunk)], local.at[pl.ds(at * chunk, chunk)], sems.at[at]
-            )
-            for at in range(2 * pieces)
-        ]
-        for copy in copies:
-            copy.start()
+    def body(first_ref, second_ref, weight_ref, k_ref, v_ref, feat_ref, within_ref):
         causal = place((n_rows, 1), 0) >= place((1, n_rows), 1)
-        projected = None
-        for at, copy in enumerate(copies):
-            rows_ref = (first_ref, second_ref)[at // pieces]
-            start = (at % pieces) * chunk
-            copy.wait()
-            product = jnp.dot(
-                rows_ref[:, start : start + chunk],
-                local[at * chunk : (at + 1) * chunk, :],
-                preferred_element_type=F32,
-            )
-            projected = product if projected is None else projected + product
+        projected = jnp.dot(first_ref[...], weight_ref[0, :half, :], preferred_element_type=F32)
+        projected += jnp.dot(second_ref[...], weight_ref[0, half:, :], preferred_element_type=F32)
         feat_ref[...] = feature_map(projected).astype(BF16)
         for head in range(0, columns, head_dim):
             span = slice(head, head + head_dim)
@@ -222,35 +193,30 @@
     return call(
         body,
         (jax.ShapeDtypeStruct((n_rows, columns), BF16), jax.ShapeDtypeStruct((n_rows, columns), F32)),
-        [VMEM, VMEM, HBM, VMEM, VMEM],
+        [VMEM] * 5,
         (VMEM,) * 2,
         flops=4 * n_rows * half * columns + 4 * n_rows * n_rows * columns,
         nbytes=4 * half * columns,
-        limit=16 << 20,
-        scratch_shapes=[
-            pltpu.VMEM((2 * half, columns), BF16),
-            pltpu.SemaphoreType.DMA((2 * pieces,)),
-        ],
         name="queries_within",
-    )(*halves, in_hbm(qkv_weight), feat_k, values)
-
-
-def project_out(normalized, weight_refs, parts, rows):
-    for which, weight_ref in enumerate(weight_refs):
-        half = weight_ref.shape[1]
+    )(*halves, qkv_weight, feat_k, values)
+
+
+def project_out(normalized, weight_ref, parts, rows):
+    half = weight_ref.shape[1] // 2
+    for which in range(2):
         tile = 512 if half % 512 == 0 else 128
         for start in range(0, half, tile):
             span = slice(start, start + tile)
-            product = jnp.dot(normalized, weight_ref[:, span], preferred_element_type=F32).astype(BF16)
+            product = jnp.dot(normalized, weight_ref[:, which * half + start : which * half + start + tile], preferred_element_type=F32).astype(BF16)
             for block in range(len(parts) // 2):
                 parts[2 * block + which][:, span] = product[block * rows : (block + 1) * rows, :]
 
 
-def attend_and_project(feat_q, within, initial, others, gain, out_weights, blocks, rows, head_dim):
+def attend_and_project(feat_q, within, initial, others, gain, out_weight, blocks, rows, head_dim):
     n_rows, columns = feat_q.shape
-    half = out_weights[0].shape[1]
-
-    def body(q_ref, within_ref, initial_ref, gain_ref, first_ref, second_ref, *refs):
+    half = out_weight.shape[1] // 2
+
+    def body(q_ref, within_ref, initial_ref, gain_ref, weight_ref, *refs):
         other_refs, normalized_ref, parts = refs[: len(others)], refs[len(others)], refs[len(others) + 1 :]
         place = lax.axis_index("ctx")
         for head in range(columns // head_dim):
@@ -266,36 +232,36 @@
             attended = attended + jnp.dot(q, low, preferred_element_type=F32)
             scale = lax.rsqrt(jnp.mean(attended * attended, axis=-1, keepdims=True) + 1e-06)
             normalized_ref[:, at] = (attended * scale * gain_ref[:, at]).astype(BF16)
-        project_out(normalized_ref[n_rows - blocks * rows :, :], (first_ref, second_ref), parts, rows)
+        project_out(normalized_ref[n_rows - blocks * rows :, :], weight_ref, parts, rows)
 
     out = call(
         body,
         [jax.ShapeDtypeStruct((n_rows, columns), BF16)] + [jax.ShapeDtypeStruct((rows, half), BF16)] * (2 * blocks),
-        [VMEM] * (6 + len(others)),
+        [VMEM] * (5 + len(others)),
         [VMEM] * (1 + 2 * blocks),
         flops=4 * n_rows * half * columns,
         nbytes=4 * half * columns,
         name="attend_and_project",
-    )(feat_q, within, initial, gain.reshape(1, columns), *out_weights, *others)
+    )(feat_q, within, initial, gain.reshape(1, columns), out_weight, *others)
     return out[0], [out[1 + 2 * block : 3 + 2 * block] for block in range(blocks)]
 
 
-def project_rest(normalized, out_weights, blocks, rows):
+def project_rest(normalized, out_weight, blocks, rows):
     columns = normalized.shape[1]
-    half = out_weights[0].shape[1]
-
-    def body(normalized_ref, first_ref, second_ref, *parts):
-        project_out(normalized_ref[: blocks * rows, :], (first_ref, second_ref), parts, rows)
+    half = out_weight.shape[1] // 2
+
+    def body(normalized_ref, weight_ref, *parts):
+        project_out(normalized_ref[: blocks * rows, :], weight_ref, parts, rows)
 
     out = call(
         body,
         [jax.ShapeDtypeStruct((rows, half), BF16)] * (2 * blocks),
-        [VMEM] * 3,
+        [VMEM] * 2,
         [VMEM] * (2 * blocks),
         flops=HOP_FLOPS,
         nbytes=4 * half * columns,
         name="project_rest",
-    )(normalized, *out_weights)
+    )(normalized, out_weight)
     return [out[2 * block : 2 * block + 2] for block in range(blocks)]
 
 
@@ -400,19 +366,17 @@
     order = slots(n_fsdp)
 
     half = width // 2
-    fetches = [(qkv_weight, (s, pl.ds(part * half, half)), (half, columns)) for part in range(2) for s in (1, 2)]
-    fetches += [(out_weight, (slice(None), pl.ds(part * half, half)), (columns, half)) for part in range(2)]
-    held, brought = ring_gather(tokens, n_fsdp, right, left, fetches)
-
-    first, first_rows = first_pass(held[0], brought[:2], n_rows)
-    feat_k, values, state, second_rows = keys_and_values(held[1], brought[2], brought[3], first, head_dim)
+    held = ring_gather(tokens, n_fsdp, right, left)
+
+    first, first_rows = first_pass(held[0], qkv_weight, n_rows)
+    feat_k, values, state, second_rows = keys_and_values(held[1], qkv_weight, first, head_dim)
     feat_q, within = queries_within((first_rows, second_rows), qkv_weight, feat_k, values, head_dim, n_fsdp, rows)
     others = exchange_states(state, n_ctx)
     soon = 1
     normalized, parts = attend_and_project(
-        feat_q, within, initial_state, others, norm_gain, brought[4:], soon, rows, head_dim
+        feat_q, within, initial_state, others, norm_gain, out_weight, soon, rows, head_dim
     )
-    parts = project_rest(normalized, brought[4:], n_fsdp - soon, rows) + parts
+    parts = project_rest(normalized, out_weight, n_fsdp - soon, rows) + parts
     return ring_scatter(parts, order, right, left)
 
 

time: 83.3 us -> 83 us (level)
  Pallas kernels: 24.1 us -> 10.9 us
  waiting for transfers between devices: 24 us -> 37 us
    pallas_call x7 -> x5, Pallas kernels: 13.2 us -> 1.78 us  [the longest x1 1.78 us: first_pass(): call(body, (jax.ShapeDtypeStruct((2, n_rows, columns), F32), jax.ShapeDty...]
    ppermute x6, waiting for transfers between devices: 0.6 us -> 7.92 us  [ring_gather(): going_right[part] = lax.ppermute(going_right[part], 'fsdp', right)]
    ppermute x6, waiting for transfers between devices: 2.6 us -> 7.99 us  [ring_gather(): going_left[part] = lax.ppermute(going_left[part], 'fsdp', left)]
    ppermute x7, starting transfers between devices: 5.31 us -> 8.53 us  [hop(): lax.ppermute(to_left, 'fsdp', left)]
    ppermute x7, starting transfers between devices: 9.21 us -> 5.99 us  [hop(): lax.ppermute(to_right, 'fsdp', right)]
    pallas_call x1, Pallas kernels: 4.15 us -> 2.3 us  [queries_within(): call(body, (jax.ShapeDtypeStruct((n_rows, columns), BF16), jax.ShapeDtype...]
    ppermute x2, waiting for transfers between devices: 1.34 us -> 3.06 us  [exchange_states(): others.append(lax.ppermute(total, 'ctx', pairs))]
    ppermute x7, waiting for transfers between devices: 7.05 us -> 5.9 us  [hop(): lax.ppermute(to_left, 'fsdp', left)]
  transfers between devices with their start and end apart: 32 -> 32, of which waited for: 25 -> 25; matrix products, arithmetic and copies ran while one was open for 0% -> 0% of each run, Pallas kernels for 23% -> 8%
where the time goes in v5:
time: 83 us; the launch traced here: 82.9 us
  waiting for transfers between devices  37 us (45%)
  starting transfers between devices  33.7 us (41%)
  Pallas kernels  10.9 us (13%)
  local copies, waits for them, and re-layouts  1.12 us (1%)
    ppermute x6, starting transfers between devices, ring_gather(): going_left[part] = lax.ppermute(going_left[part], 'fsdp', left)  12.6 us
    ppermute x7, waiting for transfers between devices, hop(): lax.ppermute(to_right, 'fsdp', right)  9.78 us
    ppermute x7, starting transfers between devices, hop(): lax.ppermute(to_left, 'fsdp', left)  8.53 us
    ppermute x6, waiting for transfers between devices, ring_gather(): going_left[part] = lax.ppermute(going_left[part], 'fsdp', left)  7.99 us
    ppermute x6, waiting for transfers between devices, ring_gather(): going_right[part] = lax.ppermute(going_right[part], 'fsdp', right)  7.92 us
    ppermute x7, starting transfers between devices, hop(): lax.ppermute(to_right, 'fsdp', right)  5.99 us
    ppermute x7, waiting for transfers between devices, hop(): lax.ppermute(to_left, 'fsdp', left)  5.9 us
    ppermute x2, starting transfers between devices, ring_gather(): held[part].append(lax.ppermute(going_left[part][:, quarter:], 'fsdp', left))  3.26 us
  transfers between devices with their start and end apart: 32, of which 25 were waited for; matrix products, arithmetic and copies ran while one was open for 0% of the time, Pallas kernels for 8%

profile of v5, /device:TPU:0, one launch (start us, length us, event | category | flops | bytes accessed | tf_op | source)
XLA Modules:
  0.0 82.9 jit_solution(7286324517102847418)
XLA Ops:
  0.0 1.0 %fusion = (bf16[32,3072]{1,0:T(8,128)(2,1)S(1)}, bf16[32,3072]{1,0:T(8,128)(2,1)S(1)}) fusion(bf16[32,6144]{1,0:T(8,128)(2,1)} %param.5), kind=kLoop, calls=%fused_computation | loop fusion | bytes 786432 | tf_op jit(solution)/shard_map/slice | solution.py:70
  1.1 3.0 %collective-permute-start.1 = (bf16[32,3072]{1,0:T(8,128)(2,1)S(1)}, bf16[32,3072]{1,0:T(8,128)(2,1)S(1)}, u32[]{:S(2)}, u32[]{:S(2)}) collective-permute-start(bf16[32,3072]{1,0:T(8,128)(2,1)S(1)} %get-tuple-element.92.refs_0_), channel_id=1, source_target_pairs={{2,0},{4,2},{6,4},{7,6},{5,7},{3,5},{1,3},{0,1},{10,8},{12,10},{14... | collective-permute-start | bytes 589832 | tf_op jit(solution)/shard_map/ppermute | solution.py:76
  4.2 1.9 %collective-permute-start.9 = (bf16[32,3072]{1,0:T(8,128)(2,1)S(1)}, bf16[32,3072]{1,0:T(8,128)(2,1)S(1)}, u32[]{:S(2)}, u32[]{:S(2)}) collective-permute-start(bf16[32,3072]{1,0:T(8,128)(2,1)S(1)} %get-tuple-element.91.refs_0_), channel_id=1, source_target_pairs={{2,0},{4,2},{6,4},{7,6},{5,7},{3,5},{1,3},{0,1},{10,8},{12,10},{14... | collective-permute-start | bytes 589832 | tf_op jit(solution)/shard_map/ppermute | solution.py:76
  6.2 3.6 %collective-permute-done.1.refs_2_ = bf16[32,3072]{1,0:T(8,128)(2,1)S(1)} collective-permute-done((bf16[32,3072]{1,0:T(8,128)(2,1)S(1)}, bf16[32,3072]{1,0:T(8,128)(2,1)S(1)}, u32[]{:S(2)}, u32[]{:S(2)}) %collective-permute-start.1) | collective-permute-done | bytes 196640 | tf_op jit(solution)/shard_map/ppermute | solution.py:76
  9.9 2.0 %collective-permute-start.3 = (bf16[32,3072]{1,0:T(8,128)(2,1)S(1)}, bf16[32,3072]{1,0:T(8,128)(2,1)S(1)}, u32[]{:S(2)}, u32[]{:S(2)}) collective-permute-start(bf16[32,3072]{1,0:T(8,128)(2,1)S(1)} %collective-permute-done.1.refs_2_), channel_id=1, source_target_pairs={{2,0},{4,2},{6,4},{7,6},{5,7},{3,5},{1,3},{0,1},{10,8},{12,10},{14... | collective-permute-start | bytes 589832 | tf_op jit(solution)/shard_map/ppermute | solution.py:76
  12.0 2.1 %collective-permute-done.9.refs_2_ = bf16[32,3072]{1,0:T(8,128)(2,1)S(1)} collective-permute-done((bf16[32,3072]{1,0:T(8,128)(2,1)S(1)}, bf16[32,3072]{1,0:T(8,128)(2,1)S(1)}, u32[]{:S(2)}, u32[]{:S(2)}) %collective-permute-start.9) | collective-permute-done | bytes 196640 | tf_op jit(solution)/shard_map/ppermute | solution.py:76
  14.1 2.0 %collective-permute-start.11 = (bf16[32,3072]{1,0:T(8,128)(2,1)S(1)}, bf16[32,3072]{1,0:T(8,128)(2,1)S(1)}, u32[]{:S(2)}, u32[]{:S(2)}) collective-permute-start(bf16[32,3072]{1,0:T(8,128)(2,1)S(1)} %collective-permute-done.9.refs_2_), channel_id=1, source_target_pairs={{2,0},{4,2},{6,4},{7,6},{5,7},{3,5},{1,3},{0,1},{10,8},{12,10},{14... | collective-permute-start | bytes 589832 | tf_op jit(solution)/shard_map/ppermute | solution.py:76
  16.2 2.1 %collective-permute-done.3.second_ref = bf16[32,3072]{1,0:T(8,128)(2,1)S(1)} collective-permute-done((bf16[32,3072]{1,0:T(8,128)(2,1)S(1)}, bf16[32,3072]{1,0:T(8,128)(2,1)S(1)}, u32[]{:S(2)}, u32[]{:S(2)}) %collective-permute-start.3) | collective-permute-done | bytes 196640 | tf_op jit(solution)/shard_map/ppermute | solution.py:76
  18.3 2.0 %collective-permute-done.2.first_ref = bf16[32,3072]{1,0:T(8,128)(2,1)S(1)} collective-permute-done((bf16[32,3072]{1,0:T(8,128)(2,1)S(1)}, bf16[32,3072]{1,0:T(8,128)(2,1)S(1)}, u32[]{:S(2)}, u32[]{:S(2)}) %collective-permute-start.2) | collective-permute-done | bytes 196640 | tf_op jit(solution)/shard_map/ppermute | solution.py:75
  20.4 1.9 %collective-permute-start.5 = (bf16[32,3072]{1,0:T(8,128)(2,1)S(1)}, bf16[32,3072]{1,0:T(8,128)(2,1)S(1)}, u32[]{:S(2)}, u32[]{:S(2)}) collective-permute-start(bf16[32,3072]{1,0:T(8,128)(2,1)S(1)} %get-tuple-element.49.refs_4_), channel_id=1, source_target_pairs={{2,0},{4,2},{6,4},{7,6},{5,7},{3,5},{1,3},{0,1},{10,8},{12,10},{14... | collective-permute-start | bytes 589832 | tf_op jit(solution)/shard_map/ppermute | solution.py:76
  22.5 2.0 %collective-permute-done.10.first_ref = bf16[32,3072]{1,0:T(8,128)(2,1)S(1)} collective-permute-done((bf16[32,3072]{1,0:T(8,128)(2,1)S(1)}, bf16[32,3072]{1,0:T(8,128)(2,1)S(1)}, u32[]{:S(2)}, u32[]{:S(2)}) %collective-permute-start.10) | collective-permute-done | bytes 196640 | tf_op jit(solution)/shard_map/ppermute | solution.py:75
  24.6 1.9 %collective-permute-start.13 = (bf16[32,3072]{1,0:T(8,128)(2,1)S(1)}, bf16[32,3072]{1,0:T(8,128)(2,1)S(1)}, u32[]{:S(2)}, u32[]{:S(2)}) collective-permute-start(bf16[32,3072]{1,0:T(8,128)(2,1)S(1)} %get-tuple-element.54.refs_4_), channel_id=1, source_target_pairs={{2,0},{4,2},{6,4},{7,6},{5,7},{3,5},{1,3},{0,1},{10,8},{12,10},{14... | collective-permute-start | bytes 589832 | tf_op jit(solution)/shard_map/ppermute | solution.py:76
  26.5 2.2 %collective-permute-done.4.first_ref = bf16[32,3072]{1,0:T(8,128)(2,1)S(1)} collective-permute-done((bf16[32,3072]{1,0:T(8,128)(2,1)S(1)}, bf16[32,3072]{1,0:T(8,128)(2,1)S(1)}, u32[]{:S(2)}, u32[]{:S(2)}) %collective-permute-start.4) | collective-permute-done | bytes 196640 | tf_op jit(solution)/shard_map/ppermute | solution.py:75
  28.8 1.6 %collective-permute-start.7 = (bf16[32,1536]{1,0:T(8,128)(2,1)S(1)}, bf16[32,1536]{1,0:T(8,128)(2,1)S(1)}, u32[]{:S(2)}, u32[]{:S(2)}) collective-permute-start(bf16[32,1536]{1,0:T(8,128)(2,1)S(1)} %slice.20), channel_id=1, source_target_pairs={{2,0},{4,2},{6,4},{7,6},{5,7},{3,5},{1,3},{0,1},{10,8},{12,10},{14... | collective-permute-start | bytes 294920 | tf_op jit(solution)/shard_map/ppermute | solution.py:82
  30.9 1.6 %collective-permute-done.12.first_ref = bf16[32,3072]{1,0:T(8,128)(2,1)S(1)} collective-permute-done((bf16[32,3072]{1,0:T(8,128)(2,1)S(1)}, bf16[32,3072]{1,0:T(8,128)(2,1)S(1)}, u32[]{:S(2)}, u32[]{:S(2)}) %collective-permute-start.12) | collective-permute-done | bytes 196640 | tf_op jit(solution)/shard_map/ppermute | solution.py:75
  32.6 1.6 %collective-permute-start.15 = (bf16[32,1536]{1,0:T(8,128)(2,1)S(1)}, bf16[32,1536]{1,0:T(8,128)(2,1)S(1)}, u32[]{:S(2)}, u32[]{:S(2)}) collective-permute-start(bf16[32,1536]{1,0:T(8,128)(2,1)S(1)} %slice.23), channel_id=1, source_target_pairs={{2,0},{4,2},{6,4},{7,6},{5,7},{3,5},{1,3},{0,1},{10,8},{12,10},{14... | collective-permute-start | bytes 294920 | tf_op jit(solution)/shard_map/ppermute | solution.py:82
  34.6 1.4 %collective-permute-done.6.refs_7_ = bf16[32,1536]{1,0:T(8,128)(2,1)S(1)} collective-permute-done((bf16[32,1536]{1,0:T(8,128)(2,1)S(1)}, bf16[32,1536]{1,0:T(8,128)(2,1)S(1)}, u32[]{:S(2)}, u32[]{:S(2)}) %collective-permute-start.6) | collective-permute-done | bytes 98336 | tf_op jit(solution)/shard_map/ppermute | solution.py:81
  36.0 1.8 %first_pass.1 = (f32[2,256,512]{2,1,0:T(8,128)S(1)}, bf16[256,3072]{1,0:T(8,128)(2,1)S(1)}) custom-call(bf16[32,3072]{1,0:T(8,128)(2,1)S(1)} %get-tuple-element.92.refs_0_, bf16[32,3072]{1,0:T(8,128)(2,1)S(1)} %collective-permute-done.refs_1_, bf16[32,3072]{1,0:T(8,128)(2,1)S(1)} %collective-permute-done.1.refs_2_, ...), custom_call_target="tpu_custom_call" | custom-call | flops 1610612736 | bytes 6291456 | tf_op jit(solution)/shard_map/first_pass/pallas_call | solution.py:106
  37.8 1.0 %collective-permute-done.14.refs_7_ = bf16[32,1536]{1,0:T(8,128)(2,1)S(1)} collective-permute-done((bf16[32,1536]{1,0:T(8,128)(2,1)S(1)}, bf16[32,1536]{1,0:T(8,128)(2,1)S(1)}, u32[]{:S(2)}, u32[]{:S(2)}) %collective-permute-start.14) | collective-permute-done | bytes 98336 | tf_op jit(solution)/shard_map/ppermute | solution.py:81
  38.8 2.2 %keys_and_values.1 = (bf16[256,512]{1,0:T(8,128)(2,1)S(1)}, bf16[256,512]{1,0:T(8,128)(2,1)S(1)}, bf16[4,128,128]{2,1,0:T(8,128)(2,1)S(1)}, bf16[256,3072]{1,0:T(8,128)(2,1)S(1)}) custom-call(bf16[32,3072]{1,0:T(8,128)(2,1)S(1)} %get-tuple-element.91.refs_0_, bf16[32,3072]{1,0:T(8,128)(2,1)S(1)} %collective-permute-done.8.refs_1_, ...), custom_call_target="tpu_custom_call" | custom-call | flops 1610612736 | bytes 6291456 | tf_op jit(solution)/shard_map/keys_and_values/pallas_call | solution.py:147
  41.1 1.3 %collective-permute-done.16.two_ref.refs_0_ = bf16[4,128,128]{2,1,0:T(8,128)(2,1)S(1)} collective-permute-done((bf16[4,128,128]{2,1,0:T(8,128)(2,1)S(1)}, bf16[4,128,128]{2,1,0:T(8,128)(2,1)S(1)}, u32[]{:S(2)}, u32[]{:S(2)}) %collective-permute-start.16) | collective-permute-done | bytes 131104 | tf_op jit(solution)/shard_map/ppermute | solution.py:353
  42.5 1.6 %collective-permute-start.17 = (bf16[4,128,128]{2,1,0:T(8,128)(2,1)S(1)}, bf16[4,128,128]{2,1,0:T(8,128)(2,1)S(1)}, u32[]{:S(2)}, u32[]{:S(2)}) collective-permute-start(bf16[4,128,128]{2,1,0:T(8,128)(2,1)S(1)} %add_states.1), channel_id=1, source_target_pairs={{0,16},{8,24},{16,0},{24,8},{1,17},{9,25},{17,1},{25,9},{2,18},{10... | collective-permute-start | bytes 393224 | tf_op jit(solution)/shard_map/ppermute | solution.py:353
  44.1 2.3 %queries_within.1 = (bf16[256,512]{1,0:T(8,128)(2,1)S(1)}, f32[256,512]{1,0:T(8,128)S(1)}) custom-call(bf16[256,3072]{1,0:T(8,128)(2,1)S(1)} %get-tuple-element.52.first_ref, bf16[256,3072]{1,0:T(8,128)(2,1)S(1)} %get-tuple-element.58.second_ref, bf16[3,6144,512]{2,1,0:T(8,128)(2,1)S(1)} %bitcast.2, bf16[256,512]{1,0:T(8,128)(2,1)S(1)} %get-tuple-element.59.k_ref, ...), custom_call_target="tpu_custom_call" | custom-call | flops 1744830464 | bytes 6291456 | tf_op jit(solution)/shard_map/queries_within/pallas_call | solution.py:193
  46.4 1.7 %collective-permute-done.17.refs_1_ = bf16[4,128,128]{2,1,0:T(8,128)(2,1)S(1)} collective-permute-done((bf16[4,128,128]{2,1,0:T(8,128)(2,1)S(1)}, bf16[4,128,128]{2,1,0:T(8,128)(2,1)S(1)}, u32[]{:S(2)}, u32[]{:S(2)}) %collective-permute-start.17) | collective-permute-done | bytes 131104 | tf_op jit(solution)/shard_map/ppermute | solution.py:353
  48.2 1.6 %attend_and_project.1 = (bf16[256,512]{1,0:T(8,128)(2,1)S(1)}, bf16[32,3072]{1,0:T(8,128)(2,1)S(1)}, bf16[32,3072]{1,0:T(8,128)(2,1)S(1)}) custom-call(bf16[256,512]{1,0:T(8,128)(2,1)S(1)} %get-tuple-element.61.q_ref, f32[256,512]{1,0:T(8,128)S(1)} %get-tuple-element.62.within_ref, f32[4,128,128]{2,1,0:T(8,128)S(1)} %copy-done, f32[1,512]{1,0:T(1,128)S(1)} %bitcast.5, ...), custom_call_target="tpu_custom_call" | custom-call | flops 1610612736 | bytes 6291456 | tf_op jit(solution)/shard_map/attend_and_project/pallas_call | solution.py:237
  50.2 1.6 %collective-permute-start.25 = (bf16[32,3072]{1,0:T(8,128)(2,1)S(1)}, bf16[32,3072]{1,0:T(8,128)(2,1)S(1)}, u32[]{:S(2)}, u32[]{:S(2)}) collective-permute-start(bf16[32,3072]{1,0:T(8,128)(2,1)S(1)} %get-tuple-element.82), channel_id=1, source_target_pairs={{2,0},{4,2},{6,4},{7,6},{5,7},{3,5},{1,3},{0,1},{10,8},{12,10},{14... | collective-permute-start | bytes 589832 | tf_op jit(solution)/shard_map/ppermute | solution.py:326
  51.8 1.6 %project_rest.1 = (bf16[32,3072]{1,0:T(8,128)(2,1)S(1)}, bf16[32,3072]{1,0:T(8,128)(2,1)S(1)}, bf16[32,3072]{1,0:T(8,128)(2,1)S(1)}, bf16[32,3072]{1,0:T(8,128)(...) custom-call(bf16[256,512]{1,0:T(8,128)(2,1)S(1)} %get-tuple-element., ...), custom_call_target="tpu_custom_call" | custom-call | flops 5000000000 | bytes 6291456 | tf_op jit(solution)/shard_map/project_rest/pallas_call | solution.py:256
  53.9 1.6 %collective-permute-start.19 = (bf16[32,3072]{1,0:T(8,128)(2,1)S(1)}, bf16[32,3072]{1,0:T(8,128)(2,1)S(1)}, u32[]{:S(2)}, u32[]{:S(2)}) collective-permute-start(bf16[32,3072]{1,0:T(8,128)(2,1)S(1)} %get-tuple-element.71), channel_id=1, source_target_pairs={{2,0},{4,2},{6,4},{7,6},{5,7},{3,5},{1,3},{0,1},{10,8},{12,10},{14... | collective-permute-start | bytes 589832 | tf_op jit(solution)/shard_map/ppermute | solution.py:326
  55.4 1.4 %collective-permute-done.24.gr = bf16[32,3072]{1,0:T(8,128)(2,1)S(1)} collective-permute-done((bf16[32,3072]{1,0:T(8,128)(2,1)S(1)}, bf16[32,3072]{1,0:T(8,128)(2,1)S(1)}, u32[]{:S(2)}, u32[]{:S(2)}) %collective-permute-start.24) | collective-permute-done | bytes 196640 | tf_op jit(solution)/shard_map/ppermute | solution.py:326
  57.2 0.9 %collective-permute-start.26 = (bf16[32,3072]{1,0:T(8,128)(2,1)S(1)}, bf16[32,3072]{1,0:T(8,128)(2,1)S(1)}, u32[]{:S(2)}, u32[]{:S(2)}) collective-permute-start(bf16[32,3072]{1,0:T(8,128)(2,1)S(1)} %get-tuple-element.83), channel_id=1, source_target_pairs={{0,2},{2,4},{4,6},{6,7},{7,5},{5,3},{3,1},{1,0},{8,10},{10,12},{12... | collective-permute-start | bytes 589832 | tf_op jit(solution)/shard_map/ppermute | solution.py:326
  58.0 1.2 %collective-permute-start.27 = (bf16[32,3072]{1,0:T(8,128)(2,1)S(1)}, bf16[32,3072]{1,0:T(8,128)(2,1)S(1)}, u32[]{:S(2)}, u32[]{:S(2)}) collective-permute-start(bf16[32,3072]{1,0:T(8,128)(2,1)S(1)} %get-tuple-element.85), channel_id=1, source_target_pairs={{2,0},{4,2},{6,4},{7,6},{5,7},{3,5},{1,3},{0,1},{10,8},{12,10},{14... | collective-permute-start | bytes 589832 | tf_op jit(solution)/shard_map/ppermute | solution.py:326
  59.3 2.0 %collective-permute-done.18.gr = bf16[32,3072]{1,0:T(8,128)(2,1)S(1)} collective-permute-done((bf16[32,3072]{1,0:T(8,128)(2,1)S(1)}, bf16[32,3072]{1,0:T(8,128)(2,1)S(1)}, u32[]{:S(2)}, u32[]{:S(2)}) %collective-permute-start.18) | collective-permute-done | bytes 196640 | tf_op jit(solution)/shard_map/ppermute | solution.py:326
  61.8 0.9 %collective-permute-start.20 = (bf16[32,3072]{1,0:T(8,128)(2,1)S(1)}, bf16[32,3072]{1,0:T(8,128)(2,1)S(1)}, u32[]{:S(2)}, u32[]{:S(2)}) collective-permute-start(bf16[32,3072]{1,0:T(8,128)(2,1)S(1)} %get-tuple-element.72), channel_id=1, source_target_pairs={{0,2},{2,4},{4,6},{6,7},{7,5},{5,3},{3,1},{1,0},{8,10},{10,12},{12... | collective-permute-start | bytes 589832 | tf_op jit(solution)/shard_map/ppermute | solution.py:326
  62.7 1.2 %collective-permute-start.21 = (bf16[32,3072]{1,0:T(8,128)(2,1)S(1)}, bf16[32,3072]{1,0:T(8,128)(2,1)S(1)}, u32[]{:S(2)}, u32[]{:S(2)}) collective-permute-start(bf16[32,3072]{1,0:T(8,128)(2,1)S(1)} %get-tuple-element.74), channel_id=1, source_target_pairs={{2,0},{4,2},{6,4},{7,6},{5,7},{3,5},{1,3},{0,1},{10,8},{12,10},{14... | collective-permute-start | bytes 589832 | tf_op jit(solution)/shard_map/ppermute | solution.py:326
  63.9 1.6 %collective-permute-done.26.gr = bf16[32,3072]{1,0:T(8,128)(2,1)S(1)} collective-permute-done((bf16[32,3072]{1,0:T(8,128)(2,1)S(1)}, bf16[32,3072]{1,0:T(8,128)(2,1)S(1)}, u32[]{:S(2)}, u32[]{:S(2)}) %collective-permute-start.26) | collective-permute-done | bytes 196640 | tf_op jit(solution)/shard_map/ppermute | solution.py:326
  66.0 1.1 %collective-permute-start.28 = (bf16[32,3072]{1,0:T(8,128)(2,1)S(1)}, bf16[32,3072]{1,0:T(8,128)(2,1)S(1)}, u32[]{:S(2)}, u32[]{:S(2)}) collective-permute-start(bf16[32,3072]{1,0:T(8,128)(2,1)S(1)} %get-tuple-element.86), channel_id=1, source_target_pairs={{0,2},{2,4},{4,6},{6,7},{7,5},{5,3},{3,1},{1,0},{8,10},{10,12},{12... | collective-permute-start | bytes 589832 | tf_op jit(solution)/shard_map/ppermute | solution.py:326
  67.1 1.0 %collective-permute-start.29 = (bf16[32,3072]{1,0:T(8,128)(2,1)S(1)}, bf16[32,3072]{1,0:T(8,128)(2,1)S(1)}, u32[]{:S(2)}, u32[]{:S(2)}) collective-permute-start(bf16[32,3072]{1,0:T(8,128)(2,1)S(1)} %get-tuple-element.88), channel_id=1, source_target_pairs={{2,0},{4,2},{6,4},{7,6},{5,7},{3,5},{1,3},{0,1},{10,8},{12,10},{14... | collective-permute-start | bytes 589832 | tf_op jit(solution)/shard_map/ppermute | solution.py:326
  68.1 1.6 %collective-permute-done.20.gr = bf16[32,3072]{1,0:T(8,128)(2,1)S(1)} collective-permute-done((bf16[32,3072]{1,0:T(8,128)(2,1)S(1)}, bf16[32,3072]{1,0:T(8,128)(2,1)S(1)}, u32[]{:S(2)}, u32[]{:S(2)}) %collective-permute-start.20) | collective-permute-done | bytes 196640 | tf_op jit(solution)/shard_map/ppermute | solution.py:326
  69.7 0.8 collective-permute-done.21.gl
  70.6 1.3 %collective-permute-start.22 = (bf16[32,3072]{1,0:T(8,128)(2,1)S(1)}, bf16[32,3072]{1,0:T(8,128)(2,1)S(1)}, u32[]{:S(2)}, u32[]{:S(2)}) collective-permute-start(bf16[32,3072]{1,0:T(8,128)(2,1)S(1)} %get-tuple-element.75), channel_id=1, source_target_pairs={{2,0},{4,2},{6,4},{7,6},{5,7},{3,5},{1,3},{0,1},{10,8},{12,10},{14... | collective-permute-start | bytes 589832 | tf_op jit(solution)/shard_map/ppermute | solution.py:326
  71.9 0.8 collective-permute-start.23
  72.7 1.2 %collective-permute-done.28.gr = bf16[32,3072]{1,0:T(8,128)(2,1)S(1)} collective-permute-done((bf16[32,3072]{1,0:T(8,128)(2,1)S(1)}, bf16[32,3072]{1,0:T(8,128)(2,1)S(1)}, u32[]{:S(2)}, u32[]{:S(2)}) %collective-permute-start.28) | collective-permute-done | bytes 196640 | tf_op jit(solution)/shard_map/ppermute | solution.py:326
  73.9 1.0 %collective-permute-done.29.gl = bf16[32,3072]{1,0:T(8,128)(2,1)S(1)} collective-permute-done((bf16[32,3072]{1,0:T(8,128)(2,1)S(1)}, bf16[32,3072]{1,0:T(8,128)(2,1)S(1)}, u32[]{:S(2)}, u32[]{:S(2)}) %collective-permute-start.29) | collective-permute-done | bytes 196640 | tf_op jit(solution)/shard_map/ppermute | solution.py:326
  75.0 1.4 %collective-permute-start.30 = (bf16[32,3072]{1,0:T(8,128)(2,1)S(1)}, bf16[32,3072]{1,0:T(8,128)(2,1)S(1)}, u32[]{:S(2)}, u32[]{:S(2)}) collective-permute-start(bf16[32,3072]{1,0:T(8,128)(2,1)S(1)} %get-tuple-element.89), channel_id=1, source_target_pairs={{0,2},{2,4},{4,6},{6,7},{7,5},{5,3},{3,1},{1,0},{8,10},{10,12},{12... | collective-permute-start | bytes 589832 | tf_op jit(solution)/shard_map/ppermute | solution.py:326
  77.1 2.0 %collective-permute-done.22.got_first = bf16[32,3072]{1,0:T(8,128)(2,1)S(1)} collective-permute-done((bf16[32,3072]{1,0:T(8,128)(2,1)S(1)}, bf16[32,3072]{1,0:T(8,128)(2,1)S(1)}, u32[]{:S(2)}, u32[]{:S(2)}) %collective-permute-start.22) | collective-permute-done | bytes 196640 | tf_op jit(solution)/shard_map/ppermute | solution.py:326
  79.2 1.9 %collective-permute-done.30.first = bf16[32,3072]{1,0:T(8,128)(2,1)S(1)} collective-permute-done((bf16[32,3072]{1,0:T(8,128)(2,1)S(1)}, bf16[32,3072]{1,0:T(8,128)(2,1)S(1)}, u32[]{:S(2)}, u32[]{:S(2)}) %collective-permute-start.30) | collective-permute-done | bytes 196640 | tf_op jit(solution)/shard_map/ppermute | solution.py:326
  81.1 1.0 %collective-permute-done.31.second = bf16[32,3072]{1,0:T(8,128)(2,1)S(1)} collective-permute-done((bf16[32,3072]{1,0:T(8,128)(2,1)S(1)}, bf16[32,3072]{1,0:T(8,128)(2,1)S(1)}, u32[]{:S(2)}, u32[]{:S(2)}) %collective-permute-start.31) | collective-permute-done | bytes 196640 | tf_op jit(solution)/shard_map/ppermute | solution.py:326
  82.1 0.8 finish.1
  (58 shorter events, 5.3 us)
Async XLA Ops:
  1.1 8.8 %collective-permute-start.1 = (bf16[32,3072]{1,0:T(8,128)(2,1)S(1)}, bf16[32,3072]{1,0:T(8,128)(2,1)S(1)}, u32[]{:S(2)}, u32[]{:S(2)}) collective-permute-start(bf16[32,3072]{1,0:T(8,128)(2,1)S(1)} %get-tuple-element.92.refs_0_), channel_id=1, source_target_pairs={{2,0},{4,2},{6,4},{7,6},{5,7},{3,5},{1,3},{0,1},{10,8},{12,10},{14... | collective-permute-start | bytes 589832 | tf_op jit(solution)/shard_map/ppermute | solution.py:76
  4.0 7.8 %collective-permute-start = (bf16[32,3072]{1,0:T(8,128)(2,1)S(1)}, bf16[32,3072]{1,0:T(8,128)(2,1)S(1)}, u32[]{:S(2)}, u32[]{:S(2)}) collective-permute-start(bf16[32,3072]{1,0:T(8,128)(2,1)S(1)} %get-tuple-element.92.refs_0_), channel_id=1, source_target_pairs={{0,2},{2,4},{4,6},{6,7},{7,5},{5,3},{3,1},{1,0},{8,10},{10,12},{12... | collective-permute-start | bytes 589832 | tf_op jit(solution)/shard_map/ppermute | solution.py:75
  4.2 9.9 %collective-permute-start.9 = (bf16[32,3072]{1,0:T(8,128)(2,1)S(1)}, bf16[32,3072]{1,0:T(8,128)(2,1)S(1)}, u32[]{:S(2)}, u32[]{:S(2)}) collective-permute-start(bf16[32,3072]{1,0:T(8,128)(2,1)S(1)} %get-tuple-element.91.refs_0_), channel_id=1, source_target_pairs={{2,0},{4,2},{6,4},{7,6},{5,7},{3,5},{1,3},{0,1},{10,8},{12,10},{14... | collective-permute-start | bytes 589832 | tf_op jit(solution)/shard_map/ppermute | solution.py:76
  6.1 10.0 %collective-permute-start.8 = (bf16[32,3072]{1,0:T(8,128)(2,1)S(1)}, bf16[32,3072]{1,0:T(8,128)(2,1)S(1)}, u32[]{:S(2)}, u32[]{:S(2)}) collective-permute-start(bf16[32,3072]{1,0:T(8,128)(2,1)S(1)} %get-tuple-element.91.refs_0_), channel_id=1, source_target_pairs={{0,2},{2,4},{4,6},{6,7},{7,5},{5,3},{3,1},{1,0},{8,10},{10,12},{12... | collective-permute-start | bytes 589832 | tf_op jit(solution)/shard_map/ppermute | solution.py:75
  9.9 8.4 %collective-permute-start.3 = (bf16[32,3072]{1,0:T(8,128)(2,1)S(1)}, bf16[32,3072]{1,0:T(8,128)(2,1)S(1)}, u32[]{:S(2)}, u32[]{:S(2)}) collective-permute-start(bf16[32,3072]{1,0:T(8,128)(2,1)S(1)} %collective-permute-done.1.refs_2_), channel_id=1, source_target_pairs={{2,0},{4,2},{6,4},{7,6},{5,7},{3,5},{1,3},{0,1},{10,8},{12,10},{14... | collective-permute-start | bytes 589832 | tf_op jit(solution)/shard_map/ppermute | solution.py:76
  11.9 8.4 %collective-permute-start.2 = (bf16[32,3072]{1,0:T(8,128)(2,1)S(1)}, bf16[32,3072]{1,0:T(8,128)(2,1)S(1)}, u32[]{:S(2)}, u32[]{:S(2)}) collective-permute-start(bf16[32,3072]{1,0:T(8,128)(2,1)S(1)} %collective-permute-done.refs_1_), channel_id=1, source_target_pairs={{0,2},{2,4},{4,6},{6,7},{7,5},{5,3},{3,1},{1,0},{8,10},{10,12},{12... | collective-permute-start | bytes 589832 | tf_op jit(solution)/shard_map/ppermute | solution.py:75
  14.1 8.4 %collective-permute-start.11 = (bf16[32,3072]{1,0:T(8,128)(2,1)S(1)}, bf16[32,3072]{1,0:T(8,128)(2,1)S(1)}, u32[]{:S(2)}, u32[]{:S(2)}) collective-permute-start(bf16[32,3072]{1,0:T(8,128)(2,1)S(1)} %collective-permute-done.9.refs_2_), channel_id=1, source_target_pairs={{2,0},{4,2},{6,4},{7,6},{5,7},{3,5},{1,3},{0,1},{10,8},{12,10},{14... | collective-permute-start | bytes 589832 | tf_op jit(solution)/shard_map/ppermute | solution.py:76
  16.1 8.4 %collective-permute-start.10 = (bf16[32,3072]{1,0:T(8,128)(2,1)S(1)}, bf16[32,3072]{1,0:T(8,128)(2,1)S(1)}, u32[]{:S(2)}, u32[]{:S(2)}) collective-permute-start(bf16[32,3072]{1,0:T(8,128)(2,1)S(1)} %collective-permute-done.8.refs_1_), channel_id=1, source_target_pairs={{0,2},{2,4},{4,6},{6,7},{7,5},{5,3},{3,1},{1,0},{8,10},{10,12},{12... | collective-permute-start | bytes 589832 | tf_op jit(solution)/shard_map/ppermute | solution.py:75
  20.3 8.4 %collective-permute-start.4 = (bf16[32,3072]{1,0:T(8,128)(2,1)S(1)}, bf16[32,3072]{1,0:T(8,128)(2,1)S(1)}, u32[]{:S(2)}, u32[]{:S(2)}) collective-permute-start(bf16[32,3072]{1,0:T(8,128)(2,1)S(1)} %get-tuple-element.48.refs_3_), channel_id=1, source_target_pairs={{0,2},{2,4},{4,6},{6,7},{7,5},{5,3},{3,1},{1,0},{8,10},{10,12},{12... | collective-permute-start | bytes 589832 | tf_op jit(solution)/shard_map/ppermute | solution.py:75
  20.4 8.3 %collective-permute-start.5 = (bf16[32,3072]{1,0:T(8,128)(2,1)S(1)}, bf16[32,3072]{1,0:T(8,128)(2,1)S(1)}, u32[]{:S(2)}, u32[]{:S(2)}) collective-permute-start(bf16[32,3072]{1,0:T(8,128)(2,1)S(1)} %get-tuple-element.49.refs_4_), channel_id=1, source_target_pairs={{2,0},{4,2},{6,4},{7,6},{5,7},{3,5},{1,3},{0,1},{10,8},{12,10},{14... | collective-permute-start | bytes 589832 | tf_op jit(solution)/shard_map/ppermute | solution.py:76
  24.5 8.0 %collective-permute-start.12 = (bf16[32,3072]{1,0:T(8,128)(2,1)S(1)}, bf16[32,3072]{1,0:T(8,128)(2,1)S(1)}, u32[]{:S(2)}, u32[]{:S(2)}) collective-permute-start(bf16[32,3072]{1,0:T(8,128)(2,1)S(1)} %get-tuple-element.53.refs_3_), channel_id=1, source_target_pairs={{0,2},{2,4},{4,6},{6,7},{7,5},{5,3},{3,1},{1,0},{8,10},{10,12},{12... | collective-permute-start | bytes 589832 | tf_op jit(solution)/shard_map/ppermute | solution.py:75
  24.6 7.9 %collective-permute-start.13 = (bf16[32,3072]{1,0:T(8,128)(2,1)S(1)}, bf16[32,3072]{1,0:T(8,128)(2,1)S(1)}, u32[]{:S(2)}, u32[]{:S(2)}) collective-permute-start(bf16[32,3072]{1,0:T(8,128)(2,1)S(1)} %get-tuple-element.54.refs_4_), channel_id=1, source_target_pairs={{2,0},{4,2},{6,4},{7,6},{5,7},{3,5},{1,3},{0,1},{10,8},{12,10},{14... | collective-permute-start | bytes 589832 | tf_op jit(solution)/shard_map/ppermute | solution.py:76
  28.7 7.3 %slice-start = ((s8[18874368]{0:T(1024)(128)(4,1)}), s8[4194304]{0:T(1024)(128)(4,1)S(1)}, s32[]{:S(2)}) async-start(s8[18874368]{0:T(1024)(128)(4,1)} %bitcast.1), calls=%async_computation | async-start | bytes 8388608
  28.7 7.3 %slice-start.1 = ((s8[18874368]{0:T(1024)(128)(4,1)}), s8[4194304]{0:T(1024)(128)(4,1)S(1)}, s32[]{:S(2)}) async-start(s8[18874368]{0:T(1024)(128)(4,1)} %bitcast.1), calls=%async_computation.1 | async-start | bytes 8388608
  28.7 7.3 %slice-start.2 = ((s8[18874368]{0:T(1024)(128)(4,1)}), s8[4194304]{0:T(1024)(128)(4,1)S(1)}, s32[]{:S(2)}) async-start(s8[18874368]{0:T(1024)(128)(4,1)} %bitcast.1), calls=%async_computation.2 | async-start | bytes 8388608
  28.8 7.2 %slice-start.3 = ((s8[18874368]{0:T(1024)(128)(4,1)}), s8[4194304]{0:T(1024)(128)(4,1)S(1)}, s32[]{:S(2)}) async-start(s8[18874368]{0:T(1024)(128)(4,1)} %bitcast.1), calls=%async_computation.3 | async-start | bytes 8388608
  28.8 7.2 %slice-start.4 = ((s8[18874368]{0:T(1024)(128)(4,1)}), s8[2097152]{0:T(1024)(128)(4,1)S(1)}, s32[]{:S(2)}) async-start(s8[18874368]{0:T(1024)(128)(4,1)} %bitcast.1), calls=%async_computation.4 | async-start | bytes 4194304
  28.8 5.8 %collective-permute-start.7 = (bf16[32,1536]{1,0:T(8,128)(2,1)S(1)}, bf16[32,1536]{1,0:T(8,128)(2,1)S(1)}, u32[]{:S(2)}, u32[]{:S(2)}) collective-permute-start(bf16[32,1536]{1,0:T(8,128)(2,1)S(1)} %slice.20), channel_id=1, source_target_pairs={{2,0},{4,2},{6,4},{7,6},{5,7},{3,5},{1,3},{0,1},{10,8},{12,10},{14... | collective-permute-start | bytes 294920 | tf_op jit(solution)/shard_map/ppermute | solution.py:82
  30.4 5.6 %collective-permute-start.6 = (bf16[32,1536]{1,0:T(8,128)(2,1)S(1)}, bf16[32,1536]{1,0:T(8,128)(2,1)S(1)}, u32[]{:S(2)}, u32[]{:S(2)}) collective-permute-start(bf16[32,1536]{1,0:T(8,128)(2,1)S(1)} %slice.19), channel_id=1, source_target_pairs={{0,2},{2,4},{4,6},{6,7},{7,5},{5,3},{3,1},{1,0},{8,10},{10,12},{12... | collective-permute-start | bytes 294920 | tf_op jit(solution)/shard_map/ppermute | solution.py:81
  32.6 5.3 %collective-permute-start.15 = (bf16[32,1536]{1,0:T(8,128)(2,1)S(1)}, bf16[32,1536]{1,0:T(8,128)(2,1)S(1)}, u32[]{:S(2)}, u32[]{:S(2)}) collective-permute-start(bf16[32,1536]{1,0:T(8,128)(2,1)S(1)} %slice.23), channel_id=1, source_target_pairs={{2,0},{4,2},{6,4},{7,6},{5,7},{3,5},{1,3},{0,1},{10,8},{12,10},{14... | collective-permute-start | bytes 294920 | tf_op jit(solution)/shard_map/ppermute | solution.py:82
  34.2 4.6 %collective-permute-start.14 = (bf16[32,1536]{1,0:T(8,128)(2,1)S(1)}, bf16[32,1536]{1,0:T(8,128)(2,1)S(1)}, u32[]{:S(2)}, u32[]{:S(2)}) collective-permute-start(bf16[32,1536]{1,0:T(8,128)(2,1)S(1)} %slice.22), channel_id=1, source_target_pairs={{0,2},{2,4},{4,6},{6,7},{7,5},{5,3},{3,1},{1,0},{8,10},{10,12},{12... | collective-permute-start | bytes 294920 | tf_op jit(solution)/shard_map/ppermute | solution.py:81
  38.8 9.3 %slice-start.5 = ((s8[6291456]{0:T(1024)(128)(4,1)}), s8[4194304]{0:T(1024)(128)(4,1)S(1)}, s32[]{:S(2)}) async-start(s8[6291456]{0:T(1024)(128)(4,1)} %bitcast.3), calls=%async_computation.5 | async-start | bytes 8388608
  41.1 1.4 %collective-permute-start.16 = (bf16[4,128,128]{2,1,0:T(8,128)(2,1)S(1)}, bf16[4,128,128]{2,1,0:T(8,128)(2,1)S(1)}, u32[]{:S(2)}, u32[]{:S(2)}) collective-permute-start(bf16[4,128,128]{2,1,0:T(8,128)(2,1)S(1)} %get-tuple-element.63.one_ref), channel_id=1, source_target_pairs={{0,8},{8,0},{16,24},{24,16},{1,9},{9,1},{17,25},{25,17},{2,10},{10... | collective-permute-start | bytes 393224 | tf_op jit(solution)/shard_map/ppermute | solution.py:353
  42.5 5.6 %collective-permute-start.17 = (bf16[4,128,128]{2,1,0:T(8,128)(2,1)S(1)}, bf16[4,128,128]{2,1,0:T(8,128)(2,1)S(1)}, u32[]{:S(2)}, u32[]{:S(2)}) collective-permute-start(bf16[4,128,128]{2,1,0:T(8,128)(2,1)S(1)} %add_states.1), channel_id=1, source_target_pairs={{0,16},{8,24},{16,0},{24,8},{1,17},{9,25},{17,1},{25,9},{2,18},{10... | collective-permute-start | bytes 393224 | tf_op jit(solution)/shard_map/ppermute | solution.py:353
  44.1 4.0 %slice-start.6 = ((s8[6291456]{0:T(1024)(128)(4,1)}), s8[2097152]{0:T(1024)(128)(4,1)S(1)}, s32[]{:S(2)}) async-start(s8[6291456]{0:T(1024)(128)(4,1)} %bitcast.3), calls=%async_computation.6 | async-start | bytes 4194304
  44.1 4.0 %copy-start = (f32[4,128,128]{2,1,0:T(8,128)S(1)}, f32[4,128,128]{2,1,0:T(8,128)}, u32[]{:S(2)}) copy-start(f32[4,128,128]{2,1,0:T(8,128)} %initial_ref.1) | copy-start | bytes 786436
  44.1 4.0 %copy-start.1 = (f32[512]{0:T(512)S(1)}, f32[512]{0:T(512)}, u32[]{:S(2)}) copy-start(f32[512]{0:T(512)} %param.8) | copy-start | bytes 6148
  49.7 7.2 %collective-permute-start.24 = (bf16[32,3072]{1,0:T(8,128)(2,1)S(1)}, bf16[32,3072]{1,0:T(8,128)(2,1)S(1)}, u32[]{:S(2)}, u32[]{:S(2)}) collective-permute-start(bf16[32,3072]{1,0:T(8,128)(2,1)S(1)} %get-tuple-element.80), channel_id=1, source_target_pairs={{0,2},{2,4},{4,6},{6,7},{7,5},{5,3},{3,1},{1,0},{8,10},{10,12},{12... | collective-permute-start | bytes 589832 | tf_op jit(solution)/shard_map/ppermute | solution.py:326
  50.2 6.9 %collective-permute-start.25 = (bf16[32,3072]{1,0:T(8,128)(2,1)S(1)}, bf16[32,3072]{1,0:T(8,128)(2,1)S(1)}, u32[]{:S(2)}, u32[]{:S(2)}) collective-permute-start(bf16[32,3072]{1,0:T(8,128)(2,1)S(1)} %get-tuple-element.82), channel_id=1, source_target_pairs={{2,0},{4,2},{6,4},{7,6},{5,7},{3,5},{1,3},{0,1},{10,8},{12,10},{14... | collective-permute-start | bytes 589832 | tf_op jit(solution)/shard_map/ppermute | solution.py:326
  53.4 7.9 %collective-permute-start.18 = (bf16[32,3072]{1,0:T(8,128)(2,1)S(1)}, bf16[32,3072]{1,0:T(8,128)(2,1)S(1)}, u32[]{:S(2)}, u32[]{:S(2)}) collective-permute-start(bf16[32,3072]{1,0:T(8,128)(2,1)S(1)} %get-tuple-element.69), channel_id=1, source_target_pairs={{0,2},{2,4},{4,6},{6,7},{7,5},{5,3},{3,1},{1,0},{8,10},{10,12},{12... | collective-permute-start | bytes 589832 | tf_op jit(solution)/shard_map/ppermute | solution.py:326
  53.9 7.8 %collective-permute-start.19 = (bf16[32,3072]{1,0:T(8,128)(2,1)S(1)}, bf16[32,3072]{1,0:T(8,128)(2,1)S(1)}, u32[]{:S(2)}, u32[]{:S(2)}) collective-permute-start(bf16[32,3072]{1,0:T(8,128)(2,1)S(1)} %get-tuple-element.71), channel_id=1, source_target_pairs={{2,0},{4,2},{6,4},{7,6},{5,7},{3,5},{1,3},{0,1},{10,8},{12,10},{14... | collective-permute-start | bytes 589832 | tf_op jit(solution)/shard_map/ppermute | solution.py:326
  57.2 8.3 %collective-permute-start.26 = (bf16[32,3072]{1,0:T(8,128)(2,1)S(1)}, bf16[32,3072]{1,0:T(8,128)(2,1)S(1)}, u32[]{:S(2)}, u32[]{:S(2)}) collective-permute-start(bf16[32,3072]{1,0:T(8,128)(2,1)S(1)} %get-tuple-element.83), channel_id=1, source_target_pairs={{0,2},{2,4},{4,6},{6,7},{7,5},{5,3},{3,1},{1,0},{8,10},{10,12},{12... | collective-permute-start | bytes 589832 | tf_op jit(solution)/shard_map/ppermute | solution.py:326
  58.0 7.9 %collective-permute-start.27 = (bf16[32,3072]{1,0:T(8,128)(2,1)S(1)}, bf16[32,3072]{1,0:T(8,128)(2,1)S(1)}, u32[]{:S(2)}, u32[]{:S(2)}) collective-permute-start(bf16[32,3072]{1,0:T(8,128)(2,1)S(1)} %get-tuple-element.85), channel_id=1, source_target_pairs={{2,0},{4,2},{6,4},{7,6},{5,7},{3,5},{1,3},{0,1},{10,8},{12,10},{14... | collective-permute-start | bytes 589832 | tf_op jit(solution)/shard_map/ppermute | solution.py:326
  61.8 7.9 %collective-permute-start.20 = (bf16[32,3072]{1,0:T(8,128)(2,1)S(1)}, bf16[32,3072]{1,0:T(8,128)(2,1)S(1)}, u32[]{:S(2)}, u32[]{:S(2)}) collective-permute-start(bf16[32,3072]{1,0:T(8,128)(2,1)S(1)} %get-tuple-element.72), channel_id=1, source_target_pairs={{0,2},{2,4},{4,6},{6,7},{7,5},{5,3},{3,1},{1,0},{8,10},{10,12},{12... | collective-permute-start | bytes 589832 | tf_op jit(solution)/shard_map/ppermute | solution.py:326
  62.7 7.8 %collective-permute-start.21 = (bf16[32,3072]{1,0:T(8,128)(2,1)S(1)}, bf16[32,3072]{1,0:T(8,128)(2,1)S(1)}, u32[]{:S(2)}, u32[]{:S(2)}) collective-permute-start(bf16[32,3072]{1,0:T(8,128)(2,1)S(1)} %get-tuple-element.74), channel_id=1, source_target_pairs={{2,0},{4,2},{6,4},{7,6},{5,7},{3,5},{1,3},{0,1},{10,8},{12,10},{14... | collective-permute-start | bytes 589832 | tf_op jit(solution)/shard_map/ppermute | solution.py:326
  66.0 7.9 %collective-permute-start.28 = (bf16[32,3072]{1,0:T(8,128)(2,1)S(1)}, bf16[32,3072]{1,0:T(8,128)(2,1)S(1)}, u32[]{:S(2)}, u32[]{:S(2)}) collective-permute-start(bf16[32,3072]{1,0:T(8,128)(2,1)S(1)} %get-tuple-element.86), channel_id=1, source_target_pairs={{0,2},{2,4},{4,6},{6,7},{7,5},{5,3},{3,1},{1,0},{8,10},{10,12},{12... | collective-permute-start | bytes 589832 | tf_op jit(solution)/shard_map/ppermute | solution.py:326
  67.1 7.8 %collective-permute-start.29 = (bf16[32,3072]{1,0:T(8,128)(2,1)S(1)}, bf16[32,3072]{1,0:T(8,128)(2,1)S(1)}, u32[]{:S(2)}, u32[]{:S(2)}) collective-permute-start(bf16[32,3072]{1,0:T(8,128)(2,1)S(1)} %get-tuple-element.88), channel_id=1, source_target_pairs={{2,0},{4,2},{6,4},{7,6},{5,7},{3,5},{1,3},{0,1},{10,8},{12,10},{14... | collective-permute-start | bytes 589832 | tf_op jit(solution)/shard_map/ppermute | solution.py:326
  70.6 8.5 %collective-permute-start.22 = (bf16[32,3072]{1,0:T(8,128)(2,1)S(1)}, bf16[32,3072]{1,0:T(8,128)(2,1)S(1)}, u32[]{:S(2)}, u32[]{:S(2)}) collective-permute-start(bf16[32,3072]{1,0:T(8,128)(2,1)S(1)} %get-tuple-element.75), channel_id=1, source_target_pairs={{2,0},{4,2},{6,4},{7,6},{5,7},{3,5},{1,3},{0,1},{10,8},{12,10},{14... | collective-permute-start | bytes 589832 | tf_op jit(solution)/shard_map/ppermute | solution.py:326
  71.9 7.3 %collective-permute-start.23 = (bf16[32,3072]{1,0:T(8,128)(2,1)S(1)}, bf16[32,3072]{1,0:T(8,128)(2,1)S(1)}, u32[]{:S(2)}, u32[]{:S(2)}) collective-permute-start(bf16[32,3072]{1,0:T(8,128)(2,1)S(1)} %get-tuple-element.76), channel_id=1, source_target_pairs={{0,2},{2,4},{4,6},{6,7},{7,5},{5,3},{3,1},{1,0},{8,10},{10,12},{12... | collective-permute-start | bytes 589832 | tf_op jit(solution)/shard_map/ppermute | solution.py:326
  75.0 6.1 %collective-permute-start.30 = (bf16[32,3072]{1,0:T(8,128)(2,1)S(1)}, bf16[32,3072]{1,0:T(8,128)(2,1)S(1)}, u32[]{:S(2)}, u32[]{:S(2)}) collective-permute-start(bf16[32,3072]{1,0:T(8,128)(2,1)S(1)} %get-tuple-element.89), channel_id=1, source_target_pairs={{0,2},{2,4},{4,6},{6,7},{7,5},{5,3},{3,1},{1,0},{8,10},{10,12},{12... | collective-permute-start | bytes 589832 | tf_op jit(solution)/shard_map/ppermute | solution.py:326
  76.4 5.7 %collective-permute-start.31 = (bf16[32,3072]{1,0:T(8,128)(2,1)S(1)}, bf16[32,3072]{1,0:T(8,128)(2,1)S(1)}, u32[]{:S(2)}, u32[]{:S(2)}) collective-permute-start(bf16[32,3072]{1,0:T(8,128)(2,1)S(1)} %get-tuple-element.90), channel_id=1, source_target_pairs={{2,0},{4,2},{6,4},{7,6},{5,7},{3,5},{1,3},{0,1},{10,8},{12,10},{14... | collective-permute-start | bytes 589832 | tf_op jit(solution)/shard_map/ppermute | solution.py:326

commit v6 on v5

--- a/solution.py
+++ b/solution.py
@@ -48,20 +48,19 @@
     )
 
 
-def touch(first, second):
-    def body(first_ref, second_ref, first_out, second_out):
-        pass
-
-    return call(
-        body,
-        [jax.ShapeDtypeStruct(first.shape, first.dtype)] * 2,
-        [ANY] * 2,
-        [ANY] * 2,
+def mark(arrived):
+    def body(arrived_ref, out_ref):
+        out_ref[...] = jnp.zeros_like(out_ref)
+
+    return call(
+        body,
+        jax.ShapeDtypeStruct((8, 128), F32),
+        [ANY],
+        VMEM,
         flops=HOP_FLOPS,
-        input_output_aliases={0: 0, 1: 1},
         limit=1 << 20,
-        name="touch",
-    )(first, second)
+        name="mark",
+    )(arrived)
 
 
 def ring_gather(block, size, right, left):
@@ -74,8 +73,6 @@
         for part in range(2):
             going_right[part] = lax.ppermute(going_right[part], "fsdp", right)
             going_left[part] = lax.ppermute(going_left[part], "fsdp", left)
-            if hop > 1:
-                going_right[part], going_left[part] = touch(going_right[part], going_left[part])
             held[part] += [going_right[part], going_left[part]]
     for part in range(2):
         held[part].append(lax.ppermute(going_right[part][:, :quarter], "fsdp", right))
@@ -93,12 +90,12 @@
     into[start : start + rows, quarter:] = pieces[-1][...]
 
 
-def first_pass(pieces, weight, n_rows):
+def first_pass(pieces, weight, n_rows, marks):
     half, columns = weight.shape[1] // 2, weight.shape[2]
 
     def body(*refs):
         rows = refs[: len(pieces)]
-        weight_ref, out_ref, whole = refs[len(pieces) :]
+        weight_ref, out_ref, whole = refs[len(pieces)], *refs[-2:]
         assemble(rows, whole)
         for place in range(2):
             out_ref[place] = jnp.dot(whole[...], weight_ref[1 + place, :half, :], preferred_element_type=F32)
@@ -109,60 +106,69 @@
             jax.ShapeDtypeStruct((2, n_rows, columns), F32),
             jax.ShapeDtypeStruct((n_rows, half), BF16),
         ),
-        [VMEM] * (len(pieces) + 1),
+        [VMEM] * (len(pieces) + 1) + [ANY] * len(marks),
         (VMEM, VMEM),
         flops=4 * n_rows * half * columns,
         nbytes=4 * half * columns,
         name="first_pass",
-    )(*pieces, weight)
+    )(*pieces, weight, *marks)
 
 
 def feature_map(projected):
     return jnp.where(projected > 0.0, projected + 1.0, jnp.exp(jnp.minimum(projected, 0.0)))
 
 
-def keys_and_values(pieces, weight, first, head_dim):
-    _, n_rows, columns = first.shape
+def keys_and_values(rows_or_pieces, weight, first, start, count, head_dim):
+    _, n_rows, _ = first.shape
     half = weight.shape[1] // 2
+    columns = count * head_dim
+    whole = not isinstance(rows_or_pieces, list)
+    operands = [rows_or_pieces] if whole else rows_or_pieces
 
     def body(*refs):
-        rows = refs[: len(pieces)]
-        weight_ref, first_ref, feat_ref, values_ref, state_ref, whole = refs[len(pieces) :]
-        assemble(rows, whole)
-        tile = min(columns, 256)
-        for start in range(0, columns, tile):
-            span = slice(start, start + tile)
-            projected = first_ref[0, :, span] + jnp.dot(whole[...], weight_ref[1, half:, span], preferred_element_type=F32)
-            feat = feature_map(projected).astype(BF16)
-            feat_ref[:, span] = feat
-            projected = first_ref[1, :, span] + jnp.dot(whole[...], weight_ref[2, half:, span], preferred_element_type=F32)
-            values = projected.astype(BF16)
-            values_ref[:, span] = values
-            for head in range(start, start + tile, head_dim):
-                at = slice(head - start, head - start + head_dim)
-                state_ref[head // head_dim] = lax.dot_general(
-                    feat[:, at], values[:, at], (((0,), (0,)), ((), ())), preferred_element_type=F32
-                ).astype(BF16)
-
-    return call(
-        body,
-        (
-            jax.ShapeDtypeStruct((n_rows, columns), BF16),
-            jax.ShapeDtypeStruct((n_rows, columns), BF16),
-            jax.ShapeDtypeStruct((columns // head_dim, head_dim, head_dim), BF16),
-            jax.ShapeDtypeStruct((n_rows, half), BF16),
-        ),
-        [VMEM] * (len(pieces) + 2),
-        (VMEM,) * 4,
-        flops=2 * 2 * n_rows * half * columns,
-        nbytes=2 * 2 * half * columns,
+        rows = refs[: len(operands)]
+        weight_ref, first_ref, feat_ref, values_ref, state_ref = refs[len(operands) : len(operands) + 5]
+        if not whole:
+            assemble(rows, refs[-1])
+        rows_ref = rows[0] if whole else refs[-1]
+        span = slice(start * head_dim, start * head_dim + columns)
+        projected = first_ref[0, :, span] + jnp.dot(
+            rows_ref[...], weight_ref[1, half:, span], preferred_element_type=F32
+        )
+        feat_ref[...] = feature_map(projected).astype(BF16)
+        projected = first_ref[1, :, span] + jnp.dot(
+            rows_ref[...], weight_ref[2, half:, span], preferred_element_type=F32
+        )
+        values_ref[...] = projected.astype(BF16)
+        for head in range(count):
+            at = slice(head * head_dim, (head + 1) * head_dim)
+            state_ref[head] = lax.dot_general(
+                feat_ref[:, at], values_ref[:, at], (((0,), (0,)), ((), ())), preferred_element_type=F32
+            ).astype(BF16)
+
+    outs = [
+        jax.ShapeDtypeStruct((n_rows, columns), BF16),
+        jax.ShapeDtypeStruct((n_rows, columns), BF16),
+        jax.ShapeDtypeStruct((count, head_dim, head_dim), BF16),
+    ]
+    if not whole:
+        outs.append(jax.ShapeDtypeStruct((n_rows, half), BF16))
+    out = call(
+        body,
+        outs,
+        [VMEM] * (len(operands) + 2),
+        [VMEM] * len(outs),
+        flops=HOP_FLOPS if whole else 4 * n_rows * half * columns,
+        nbytes=4 * half * columns,
         name="keys_and_values",
-    )(*pieces, weight, first)
-
-
-def queries_within(halves, qkv_weight, feat_k, values, head_dim, size, rows):
-    n_rows, columns = feat_k.shape
-    half = halves[0].shape[1]
+    )(*operands, weight, first)
+    return out if whole else (out[:3], out[3])
+
+
+def queries_within(halves, qkv_weight, groups, head_dim, size, rows):
+    n_rows, half = halves[0].shape
+    columns = qkv_weight.shape[2]
+    per_group = columns // len(groups)
     order = slots(size)
 
     def place(shape, axis):
@@ -177,28 +183,31 @@
             start = jnp.where(slot == at, holder * rows, start)
         return start + row - slot * rows
 
-    def body(first_ref, second_ref, weight_ref, k_ref, v_ref, feat_ref, within_ref):
+    def body(first_ref, second_ref, weight_ref, *refs):
+        group_refs, (feat_ref, within_ref) = refs[:-2], refs[-2:]
         causal = place((n_rows, 1), 0) >= place((1, n_rows), 1)
         projected = jnp.dot(first_ref[...], weight_ref[0, :half, :], preferred_element_type=F32)
         projected += jnp.dot(second_ref[...], weight_ref[0, half:, :], preferred_element_type=F32)
         feat_ref[...] = feature_map(projected).astype(BF16)
         for head in range(0, columns, head_dim):
             span = slice(head, head + head_dim)
+            k_ref, v_ref = group_refs[2 * (head // per_group) : 2 * (head // per_group) + 2]
+            at = slice(head % per_group, head % per_group + head_dim)
             scores = lax.dot_general(
-                feat_ref[:, span], k_ref[:, span], (((1,), (1,)), ((), ())), preferred_element_type=F32
+                feat_ref[:, span], k_ref[:, at], (((1,), (1,)), ((), ())), preferred_element_type=F32
             )
             scores = jnp.where(causal, scores, 0.0).astype(BF16)
-            within_ref[:, span] = jnp.dot(scores, v_ref[:, span], preferred_element_type=F32)
+            within_ref[:, span] = jnp.dot(scores, v_ref[:, at], preferred_element_type=F32)
 
     return call(
         body,
         (jax.ShapeDtypeStruct((n_rows, columns), BF16), jax.ShapeDtypeStruct((n_rows, columns), F32)),
-        [VMEM] * 5,
+        [VMEM] * (3 + 2 * len(groups)),
         (VMEM,) * 2,
         flops=4 * n_rows * half * columns + 4 * n_rows * n_rows * columns,
         nbytes=4 * half * columns,
         name="queries_within",
-    )(*halves, qkv_weight, feat_k, values)
+    )(*halves, qkv_weight, *[array for group in groups for array in group[:2]])
 
 
 def project_out(normalized, weight_ref, parts, rows):
@@ -212,7 +221,10 @@
                 parts[2 * block + which][:, span] = product[block * rows : (block + 1) * rows, :]
 
 
-def attend_and_project(feat_q, within, initial, others, gain, out_weight, blocks, rows, head_dim):
+def attend_and_project(feat_q, within, initial, exchanged, gain, out_weight, blocks, rows, head_dim):
+    per_group = initial.shape[0] // len(exchanged)
+    steps = len(exchanged[0])
+    others = [other for group in exchanged for other in group]
     n_rows, columns = feat_q.shape
     half = out_weight.shape[1] // 2
 
@@ -222,9 +234,10 @@
         for head in range(columns // head_dim):
             at = slice(head * head_dim, (head + 1) * head_dim)
             prefix = initial_ref[head]
-            for bit, other_ref in enumerate(other_refs):
+            group, within_group = divmod(head, per_group)
+            for bit, other_ref in enumerate(other_refs[group * steps : (group + 1) * steps]):
                 later = (place // 2**bit) % 2 == 1
-                prefix = prefix + jnp.where(later, other_ref[head].astype(F32), 0.0)
+                prefix = prefix + jnp.where(later, other_ref[within_group].astype(F32), 0.0)
             high = prefix.astype(BF16)
             low = (prefix - high.astype(F32)).astype(BF16)
             q = q_ref[:, at]
@@ -335,26 +348,36 @@
     return finish(gathered, leading)
 
 
-def add_states(one, two):
-    def body(one_ref, two_ref, out_ref):
-        out_ref[...] = (one_ref[...].astype(F32) + two_ref[...].astype(F32)).astype(BF16)
-
-    return call(
-        body, jax.ShapeDtypeStruct(one.shape, BF16), [VMEM] * 2, VMEM, nbytes=6 * one.size, limit=4 << 20, name="add_states"
-    )(one, two)
-
-
-def exchange_states(state, size):
-    others = []
-    total = state
+def add_states(one, two, after):
+    def body(one_ref, two_ref, *refs):
+        refs[-1][...] = (one_ref[...].astype(F32) + two_ref[...].astype(F32)).astype(BF16)
+
+    return call(
+        body,
+        jax.ShapeDtypeStruct(one.shape, BF16),
+        [VMEM] * 2 + [ANY] * len(after),
+        VMEM,
+        nbytes=6 * one.size,
+        limit=4 << 20,
+        name="add_states",
+    )(one, two, *after)
+
+
+def exchange_states(states, size):
+    received = [[] for _ in states]
+    totals = list(states)
     reach = 1
     while reach < size:
         pairs = [(i, i ^ reach) for i in range(size)]
-        others.append(lax.ppermute(total, "ctx", pairs))
+        for at, total in enumerate(totals):
+            received[at].append(lax.ppermute(total, "ctx", pairs))
         reach *= 2
         if reach < size:
-            total = add_states(total, others[-1])
-    return others
+            after = []
+            for at, total in enumerate(totals):
+                totals[at] = add_states(total, received[at][-1], after)
+                after = [totals[at]]
+    return received
 
 
 def per_device(n_ctx, n_fsdp, tokens, qkv_weight, out_weight, norm_gain, initial_state):
@@ -368,13 +391,17 @@
     half = width // 2
     held = ring_gather(tokens, n_fsdp, right, left)
 
-    first, first_rows = first_pass(held[0], qkv_weight, n_rows)
-    feat_k, values, state, second_rows = keys_and_values(held[1], qkv_weight, first, head_dim)
-    feat_q, within = queries_within((first_rows, second_rows), qkv_weight, feat_k, values, head_dim, n_fsdp, rows)
-    others = exchange_states(state, n_ctx)
+    first, first_rows = first_pass(held[0], qkv_weight, n_rows, [mark(held[1][-6]), mark(held[1][-5])])
+    count = heads_here // 2 if heads_here % 2 == 0 else heads_here
+    group, second_rows = keys_and_values(held[1], qkv_weight, first, 0, count, head_dim)
+    groups = [group]
+    for start in range(count, heads_here, count):
+        groups.append(keys_and_values(second_rows, qkv_weight, first, start, count, head_dim))
+    feat_q, within = queries_within((first_rows, second_rows), qkv_weight, groups, head_dim, n_fsdp, rows)
+    exchanged = exchange_states([group[2] for group in groups], n_ctx)
     soon = 1
     normalized, parts = attend_and_project(
-        feat_q, within, initial_state, others, norm_gain, out_weight, soon, rows, head_dim
+        feat_q, within, initial_state, exchanged, norm_gain, out_weight, soon, rows, head_dim
     )
     parts = project_rest(normalized, out_weight, n_fsdp - soon, rows) + parts
     return ring_scatter(parts, order, right, left)

time: 83 us -> 82.3 us (level)
  waiting for transfers between devices: 37 us -> 34.3 us
  starting transfers between devices: 33.7 us -> 35.5 us
    ppermute x6, waiting for transfers between devices: 7.92 us -> 0.12 us  [ring_gather(): going_right[part] = lax.ppermute(going_right[part], 'fsdp', right)]
    ppermute x6, waiting for transfers between devices: 7.99 us -> 13.9 us  [ring_gather(): going_left[part] = lax.ppermute(going_left[part], 'fsdp', left)]
    ppermute x7, starting transfers between devices: 8.53 us -> 5.38 us  [hop(): lax.ppermute(to_left, 'fsdp', left)]
    ppermute x7, starting transfers between devices: 5.99 us -> 9.14 us  [hop(): lax.ppermute(to_right, 'fsdp', right)]
    ppermute x7, waiting for transfers between devices: 5.9 us -> 8.61 us  [hop(): lax.ppermute(to_left, 'fsdp', left)]
    ppermute x7, waiting for transfers between devices: 9.78 us -> 7.86 us  [hop(): lax.ppermute(to_right, 'fsdp', right)]
    ppermute x2 -> x4, waiting for transfers between devices: 3.06 us -> 1.15 us  [exchange_states(): received[at].append(lax.ppermute(total, 'ctx', pairs))]
    ppermute x2 -> x4, starting transfers between devices: 1.66 us -> 3.08 us  [exchange_states(): received[at].append(lax.ppermute(total, 'ctx', pairs))]
  transfers between devices with their start and end apart: 32 -> 34, of which waited for: 25 -> 22; matrix products, arithmetic and copies ran while one was open for 0% -> 0% of each run, Pallas kernels for 8% -> 9%
where the time goes in v6:
time: 82.3 us; the launch traced here: 82.2 us
  starting transfers between devices  35.5 us (43%)
  waiting for transfers between devices  34.3 us (42%)
  Pallas kernels  11.1 us (13%)
  local copies, waits for them, and re-layouts  1.12 us (1%)
    ppermute x6, waiting for transfers between devices, ring_gather(): going_left[part] = lax.ppermute(going_left[part], 'fsdp', left)  13.9 us
    ppermute x6, starting transfers between devices, ring_gather(): going_left[part] = lax.ppermute(going_left[part], 'fsdp', left)  12.8 us
    ppermute x7, starting transfers between devices, hop(): lax.ppermute(to_right, 'fsdp', right)  9.14 us
    ppermute x7, waiting for transfers between devices, hop(): lax.ppermute(to_left, 'fsdp', left)  8.61 us
    ppermute x7, waiting for transfers between devices, hop(): lax.ppermute(to_right, 'fsdp', right)  7.86 us
    ppermute x7, starting transfers between devices, hop(): lax.ppermute(to_left, 'fsdp', left)  5.38 us
    ppermute x2, starting transfers between devices, ring_gather(): held[part].append(lax.ppermute(going_left[part][:, quarter:], 'fsdp', left))  3.96 us
    ppermute x4, starting transfers between devices, exchange_states(): received[at].append(lax.ppermute(total, 'ctx', pairs))  3.08 us
  transfers between devices with their start and end apart: 34, of which 22 were waited for; matrix products, arithmetic and copies ran while one was open for 0% of the time, Pallas kernels for 9%

profile of v6, /device:TPU:0, one launch (start us, length us, event | category | flops | bytes accessed | tf_op | source)
XLA Modules:
  0.0 82.2 jit_solution(893902459548375321)
XLA Ops:
  0.0 1.0 %fusion = (bf16[32,3072]{1,0:T(8,128)(2,1)S(1)}, bf16[32,3072]{1,0:T(8,128)(2,1)S(1)}) fusion(bf16[32,6144]{1,0:T(8,128)(2,1)} %param.5), kind=kLoop, calls=%fused_computation | loop fusion | bytes 786432 | tf_op jit(solution)/shard_map/slice | solution.py:69
  1.1 3.0 %collective-permute-start.1 = (bf16[32,3072]{1,0:T(8,128)(2,1)S(1)}, bf16[32,3072]{1,0:T(8,128)(2,1)S(1)}, u32[]{:S(2)}, u32[]{:S(2)}) collective-permute-start(bf16[32,3072]{1,0:T(8,128)(2,1)S(1)} %get-tuple-element.82.refs_0_), channel_id=1, source_target_pairs={{2,0},{4,2},{6,4},{7,6},{5,7},{3,5},{1,3},{0,1},{10,8},{12,10},{14... | collective-permute-start | bytes 589832 | tf_op jit(solution)/shard_map/ppermute | solution.py:75
  4.2 1.9 %collective-permute-start.10 = (bf16[32,3072]{1,0:T(8,128)(2,1)S(1)}, bf16[32,3072]{1,0:T(8,128)(2,1)S(1)}, u32[]{:S(2)}, u32[]{:S(2)}) collective-permute-start(bf16[32,3072]{1,0:T(8,128)(2,1)S(1)} %get-tuple-element.81.refs_0_), channel_id=1, source_target_pairs={{2,0},{4,2},{6,4},{7,6},{5,7},{3,5},{1,3},{0,1},{10,8},{12,10},{14... | collective-permute-start | bytes 589832 | tf_op jit(solution)/shard_map/ppermute | solution.py:75
  6.2 3.6 %collective-permute-done.1.refs_2_ = bf16[32,3072]{1,0:T(8,128)(2,1)S(1)} collective-permute-done((bf16[32,3072]{1,0:T(8,128)(2,1)S(1)}, bf16[32,3072]{1,0:T(8,128)(2,1)S(1)}, u32[]{:S(2)}, u32[]{:S(2)}) %collective-permute-start.1) | collective-permute-done | bytes 196640 | tf_op jit(solution)/shard_map/ppermute | solution.py:75
  9.9 2.0 %collective-permute-start.3 = (bf16[32,3072]{1,0:T(8,128)(2,1)S(1)}, bf16[32,3072]{1,0:T(8,128)(2,1)S(1)}, u32[]{:S(2)}, u32[]{:S(2)}) collective-permute-start(bf16[32,3072]{1,0:T(8,128)(2,1)S(1)} %collective-permute-done.1.refs_2_), channel_id=1, source_target_pairs={{2,0},{4,2},{6,4},{7,6},{5,7},{3,5},{1,3},{0,1},{10,8},{12,10},{14... | collective-permute-start | bytes 589832 | tf_op jit(solution)/shard_map/ppermute | solution.py:75
  12.0 2.1 %collective-permute-done.10.refs_2_ = bf16[32,3072]{1,0:T(8,128)(2,1)S(1)} collective-permute-done((bf16[32,3072]{1,0:T(8,128)(2,1)S(1)}, bf16[32,3072]{1,0:T(8,128)(2,1)S(1)}, u32[]{:S(2)}, u32[]{:S(2)}) %collective-permute-start.10) | collective-permute-done | bytes 196640 | tf_op jit(solution)/shard_map/ppermute | solution.py:75
  14.1 2.0 %collective-permute-start.11 = (bf16[32,3072]{1,0:T(8,128)(2,1)S(1)}, bf16[32,3072]{1,0:T(8,128)(2,1)S(1)}, u32[]{:S(2)}, u32[]{:S(2)}) collective-permute-start(bf16[32,3072]{1,0:T(8,128)(2,1)S(1)} %collective-permute-done.10.refs_2_), channel_id=1, source_target_pairs={{2,0},{4,2},{6,4},{7,6},{5,7},{3,5},{1,3},{0,1},{10,8},{12,10},{14... | collective-permute-start | bytes 589832 | tf_op jit(solution)/shard_map/ppermute | solution.py:75
  16.2 2.1 %collective-permute-done.3.refs_4_ = bf16[32,3072]{1,0:T(8,128)(2,1)S(1)} collective-permute-done((bf16[32,3072]{1,0:T(8,128)(2,1)S(1)}, bf16[32,3072]{1,0:T(8,128)(2,1)S(1)}, u32[]{:S(2)}, u32[]{:S(2)}) %collective-permute-start.3) | collective-permute-done | bytes 196640 | tf_op jit(solution)/shard_map/ppermute | solution.py:75
  18.3 2.0 %collective-permute-start.5 = (bf16[32,3072]{1,0:T(8,128)(2,1)S(1)}, bf16[32,3072]{1,0:T(8,128)(2,1)S(1)}, u32[]{:S(2)}, u32[]{:S(2)}) collective-permute-start(bf16[32,3072]{1,0:T(8,128)(2,1)S(1)} %collective-permute-done.3.refs_4_), channel_id=1, source_target_pairs={{2,0},{4,2},{6,4},{7,6},{5,7},{3,5},{1,3},{0,1},{10,8},{12,10},{14... | collective-permute-start | bytes 589832 | tf_op jit(solution)/shard_map/ppermute | solution.py:75
  20.4 2.1 %collective-permute-done.11.arrived_ref.refs_4_ = bf16[32,3072]{1,0:T(8,128)(2,1)S(1)} collective-permute-done((bf16[32,3072]{1,0:T(8,128)(2,1)S(1)}, bf16[32,3072]{1,0:T(8,128)(2,1)S(1)}, u32[]{:S(2)}, u32[]{:S(2)}) %collective-permute-start.11) | collective-permute-done | bytes 196640 | tf_op jit(solution)/shard_map/ppermute | solution.py:75
  22.5 2.0 %collective-permute-start.13 = (bf16[32,3072]{1,0:T(8,128)(2,1)S(1)}, bf16[32,3072]{1,0:T(8,128)(2,1)S(1)}, u32[]{:S(2)}, u32[]{:S(2)}) collective-permute-start(bf16[32,3072]{1,0:T(8,128)(2,1)S(1)} %collective-permute-done.11.arrived_ref.refs_4_), channel_id=1, source_target_pairs={{2,0},{4,2},{6,4},{7,6},{5,7},{3,5},{1,3},{0,1},{10,8},{12,10},{14... | collective-permute-start | bytes 589832 | tf_op jit(solution)/shard_map/ppermute | solution.py:75
  24.7 2.0 %collective-permute-done.5.refs_6_ = bf16[32,3072]{1,0:T(8,128)(2,1)S(1)} collective-permute-done((bf16[32,3072]{1,0:T(8,128)(2,1)S(1)}, bf16[32,3072]{1,0:T(8,128)(2,1)S(1)}, u32[]{:S(2)}, u32[]{:S(2)}) %collective-permute-start.5) | collective-permute-done | bytes 196640 | tf_op jit(solution)/shard_map/ppermute | solution.py:75
  26.7 2.0 %collective-permute-start.7 = (bf16[32,1536]{1,0:T(8,128)(2,1)S(1)}, bf16[32,1536]{1,0:T(8,128)(2,1)S(1)}, u32[]{:S(2)}, u32[]{:S(2)}) collective-permute-start(bf16[32,1536]{1,0:T(8,128)(2,1)S(1)} %slice.25), channel_id=1, source_target_pairs={{2,0},{4,2},{6,4},{7,6},{5,7},{3,5},{1,3},{0,1},{10,8},{12,10},{14... | collective-permute-start | bytes 294920 | tf_op jit(solution)/shard_map/ppermute | solution.py:79
  28.9 2.0 %collective-permute-done.13.refs_6_ = bf16[32,3072]{1,0:T(8,128)(2,1)S(1)} collective-permute-done((bf16[32,3072]{1,0:T(8,128)(2,1)S(1)}, bf16[32,3072]{1,0:T(8,128)(2,1)S(1)}, u32[]{:S(2)}, u32[]{:S(2)}) %collective-permute-start.13) | collective-permute-done | bytes 196640 | tf_op jit(solution)/shard_map/ppermute | solution.py:75
  30.9 1.9 %collective-permute-start.15 = (bf16[32,1536]{1,0:T(8,128)(2,1)S(1)}, bf16[32,1536]{1,0:T(8,128)(2,1)S(1)}, u32[]{:S(2)}, u32[]{:S(2)}) collective-permute-start(bf16[32,1536]{1,0:T(8,128)(2,1)S(1)} %slice.27), channel_id=1, source_target_pairs={{2,0},{4,2},{6,4},{7,6},{5,7},{3,5},{1,3},{0,1},{10,8},{12,10},{14... | collective-permute-start | bytes 294920 | tf_op jit(solution)/shard_map/ppermute | solution.py:79
  33.1 0.8 %collective-permute-done.6.refs_7_ = bf16[32,1536]{1,0:T(8,128)(2,1)S(1)} collective-permute-done((bf16[32,1536]{1,0:T(8,128)(2,1)S(1)}, bf16[32,1536]{1,0:T(8,128)(2,1)S(1)}, u32[]{:S(2)}, u32[]{:S(2)}) %collective-permute-start.6) | collective-permute-done | bytes 98336 | tf_op jit(solution)/shard_map/ppermute | solution.py:78
  34.0 1.8 %first_pass.1 = (f32[2,256,512]{2,1,0:T(8,128)S(1)}, bf16[256,3072]{1,0:T(8,128)(2,1)S(1)}) custom-call(bf16[32,3072]{1,0:T(8,128)(2,1)S(1)} %get-tuple-element.82.refs_0_, bf16[32,3072]{1,0:T(8,128)(2,1)S(1)} %collective-permute-done.refs_1_, bf16[32,3072]{1,0:T(8,128)(2,1)S(1)} %collective-permute-done.1.refs_2_, ...), custom_call_target="tpu_custom_call" | custom-call | flops 1610612736 | bytes 6291456 | tf_op jit(solution)/shard_map/first_pass/pallas_call | solution.py:103
  35.8 1.8 %collective-permute-done.14.refs_7_ = bf16[32,1536]{1,0:T(8,128)(2,1)S(1)} collective-permute-done((bf16[32,1536]{1,0:T(8,128)(2,1)S(1)}, bf16[32,1536]{1,0:T(8,128)(2,1)S(1)}, u32[]{:S(2)}, u32[]{:S(2)}) %collective-permute-start.14) | collective-permute-done | bytes 98336 | tf_op jit(solution)/shard_map/ppermute | solution.py:78
  37.5 1.2 %keys_and_values.2 = (bf16[256,256]{1,0:T(8,128)(2,1)S(1)}, bf16[256,256]{1,0:T(8,128)(2,1)S(1)}, bf16[2,128,128]{2,1,0:T(8,128)(2,1)S(1)}, bf16[256,3072]{1,0:T(8,128)(2,1)S(1)}) custom-call(bf16[32,3072]{1,0:T(8,128)(2,1)S(1)} %get-tuple-element.81.refs_0_, bf16[32,3072]{1,0:T(8,128)(2,1)S(1)} %collective-permute-done.8.refs_1_, ...), custom_call_target="tpu_custom_call" | custom-call | flops 805306368 | bytes 3145728 | tf_op jit(solution)/shard_map/keys_and_values/pallas_call | solution.py:156
  38.9 1.2 %keys_and_values.3 = (bf16[256,256]{1,0:T(8,128)(2,1)S(1)}, bf16[256,256]{1,0:T(8,128)(2,1)S(1)}, bf16[2,128,128]{2,1,0:T(8,128)(2,1)S(1)}) custom-call(bf16[256,3072]{1,0:T(8,128)(2,1)S(1)} %get-tuple-element.45.refs_0_.second_ref, bf16[3,6144,512]{2,1,0:T(8,128)(2,1)S(1)} %bitcast.2, f32[2,256,512]{2,1,0:T(8,128)S(1)} %get-tuple-element.44.refs_10_.refs_2_), custom_call_target="tpu_custom_call" | custom-call | flops 5000000000 | bytes 3145728 | tf_op jit(solution)/shard_map/keys_and_values/pallas_call | solution.py:156
  40.1 0.5 collective-permute-start.18
  40.7 1.6 %collective-permute-start.17 = (bf16[2,128,128]{2,1,0:T(8,128)(2,1)S(1)}, bf16[2,128,128]{2,1,0:T(8,128)(2,1)S(1)}, u32[]{:S(2)}, u32[]{:S(2)}) collective-permute-start(bf16[2,128,128]{2,1,0:T(8,128)(2,1)S(1)} %add_states.2.refs_0_), channel_id=1, source_target_pairs={{0,16},{8,24},{16,0},{24,8},{1,17},{9,25},{17,1},{25,9},{2,18},{10... | collective-permute-start | bytes 196616 | tf_op jit(solution)/shard_map/ppermute | solution.py:373
  42.3 0.9 %collective-permute-start.19 = (bf16[2,128,128]{2,1,0:T(8,128)(2,1)S(1)}, bf16[2,128,128]{2,1,0:T(8,128)(2,1)S(1)}, u32[]{:S(2)}, u32[]{:S(2)}) collective-permute-start(bf16[2,128,128]{2,1,0:T(8,128)(2,1)S(1)} %add_states.3), channel_id=1, source_target_pairs={{0,16},{8,24},{16,0},{24,8},{1,17},{9,25},{17,1},{25,9},{2,18},{10... | collective-permute-start | bytes 196616 | tf_op jit(solution)/shard_map/ppermute | solution.py:373
  43.2 2.3 %queries_within.1 = (bf16[256,512]{1,0:T(8,128)(2,1)S(1)}, f32[256,512]{1,0:T(8,128)S(1)}) custom-call(bf16[256,3072]{1,0:T(8,128)(2,1)S(1)} %get-tuple-element.43.first_ref, bf16[256,3072]{1,0:T(8,128)(2,1)S(1)} %get-tuple-element.45.refs_0_.second_ref, bf16[3,6144,512]{2,1,0:T(8,128)(2,1)S(1)} %bitcast.2, bf16[256,256]{1,0:T(8,128)(2,1)S(1)} %get-tuple-element.46.refs_0_, ...), custom_call_target="tpu_custom_call" | custom-call | flops 1744830464 | bytes 6291456 | tf_op jit(solution)/shard_map/queries_within/pallas_call | solution.py:202
  45.5 1.1 %collective-permute-done.19.refs_3_ = bf16[2,128,128]{2,1,0:T(8,128)(2,1)S(1)} collective-permute-done((bf16[2,128,128]{2,1,0:T(8,128)(2,1)S(1)}, bf16[2,128,128]{2,1,0:T(8,128)(2,1)S(1)}, u32[]{:S(2)}, u32[]{:S(2)}) %collective-permute-start.19) | collective-permute-done | bytes 65568 | tf_op jit(solution)/shard_map/ppermute | solution.py:373
  46.7 1.6 %attend_and_project.1 = (bf16[256,512]{1,0:T(8,128)(2,1)S(1)}, bf16[32,3072]{1,0:T(8,128)(2,1)S(1)}, bf16[32,3072]{1,0:T(8,128)(2,1)S(1)}) custom-call(bf16[256,512]{1,0:T(8,128)(2,1)S(1)} %get-tuple-element.50.q_ref, f32[256,512]{1,0:T(8,128)S(1)} %get-tuple-element.51.within_ref, f32[4,128,128]{2,1,0:T(8,128)S(1)} %copy-done, f32[1,512]{1,0:T(1,128)S(1)} %bitcast.5, ...), custom_call_target="tpu_custom_call" | custom-call | flops 1610612736 | bytes 6291456 | tf_op jit(solution)/shard_map/attend_and_project/pallas_call | solution.py:250
  48.2 0.6 collective-permute-start.26
  48.8 1.5 %collective-permute-start.27 = (bf16[32,3072]{1,0:T(8,128)(2,1)S(1)}, bf16[32,3072]{1,0:T(8,128)(2,1)S(1)}, u32[]{:S(2)}, u32[]{:S(2)}) collective-permute-start(bf16[32,3072]{1,0:T(8,128)(2,1)S(1)} %get-tuple-element.72), channel_id=1, source_target_pairs={{2,0},{4,2},{6,4},{7,6},{5,7},{3,5},{1,3},{0,1},{10,8},{12,10},{14... | collective-permute-start | bytes 589832 | tf_op jit(solution)/shard_map/ppermute | solution.py:339
  50.3 1.6 %project_rest.1 = (bf16[32,3072]{1,0:T(8,128)(2,1)S(1)}, bf16[32,3072]{1,0:T(8,128)(2,1)S(1)}, bf16[32,3072]{1,0:T(8,128)(2,1)S(1)}, bf16[32,3072]{1,0:T(8,128)(...) custom-call(bf16[256,512]{1,0:T(8,128)(2,1)S(1)} %get-tuple-element., ...), custom_call_target="tpu_custom_call" | custom-call | flops 5000000000 | bytes 6291456 | tf_op jit(solution)/shard_map/project_rest/pallas_call | solution.py:269
  51.9 0.6 collective-permute-start.20
  52.4 1.5 %collective-permute-start.21 = (bf16[32,3072]{1,0:T(8,128)(2,1)S(1)}, bf16[32,3072]{1,0:T(8,128)(2,1)S(1)}, u32[]{:S(2)}, u32[]{:S(2)}) collective-permute-start(bf16[32,3072]{1,0:T(8,128)(2,1)S(1)} %get-tuple-element.61), channel_id=1, source_target_pairs={{2,0},{4,2},{6,4},{7,6},{5,7},{3,5},{1,3},{0,1},{10,8},{12,10},{14... | collective-permute-start | bytes 589832 | tf_op jit(solution)/shard_map/ppermute | solution.py:339
  53.9 1.1 %collective-permute-done.26.gr = bf16[32,3072]{1,0:T(8,128)(2,1)S(1)} collective-permute-done((bf16[32,3072]{1,0:T(8,128)(2,1)S(1)}, bf16[32,3072]{1,0:T(8,128)(2,1)S(1)}, u32[]{:S(2)}, u32[]{:S(2)}) %collective-permute-start.26) | collective-permute-done | bytes 196640 | tf_op jit(solution)/shard_map/ppermute | solution.py:339
  55.1 0.7 collective-permute-done.27.gl
  55.8 1.6 %collective-permute-start.28 = (bf16[32,3072]{1,0:T(8,128)(2,1)S(1)}, bf16[32,3072]{1,0:T(8,128)(2,1)S(1)}, u32[]{:S(2)}, u32[]{:S(2)}) collective-permute-start(bf16[32,3072]{1,0:T(8,128)(2,1)S(1)} %get-tuple-element.73), channel_id=1, source_target_pairs={{0,2},{2,4},{4,6},{6,7},{7,5},{5,3},{3,1},{1,0},{8,10},{10,12},{12... | collective-permute-start | bytes 589832 | tf_op jit(solution)/shard_map/ppermute | solution.py:339
  57.9 1.9 %collective-permute-done.20.gr = bf16[32,3072]{1,0:T(8,128)(2,1)S(1)} collective-permute-done((bf16[32,3072]{1,0:T(8,128)(2,1)S(1)}, bf16[32,3072]{1,0:T(8,128)(2,1)S(1)}, u32[]{:S(2)}, u32[]{:S(2)}) %collective-permute-start.20) | collective-permute-done | bytes 196640 | tf_op jit(solution)/shard_map/ppermute | solution.py:339
  60.4 1.6 %collective-permute-start.22 = (bf16[32,3072]{1,0:T(8,128)(2,1)S(1)}, bf16[32,3072]{1,0:T(8,128)(2,1)S(1)}, u32[]{:S(2)}, u32[]{:S(2)}) collective-permute-start(bf16[32,3072]{1,0:T(8,128)(2,1)S(1)} %get-tuple-element.62), channel_id=1, source_target_pairs={{0,2},{2,4},{4,6},{6,7},{7,5},{5,3},{3,1},{1,0},{8,10},{10,12},{12... | collective-permute-start | bytes 589832 | tf_op jit(solution)/shard_map/ppermute | solution.py:339
  62.5 1.5 %collective-permute-done.28.gr = bf16[32,3072]{1,0:T(8,128)(2,1)S(1)} collective-permute-done((bf16[32,3072]{1,0:T(8,128)(2,1)S(1)}, bf16[32,3072]{1,0:T(8,128)(2,1)S(1)}, u32[]{:S(2)}, u32[]{:S(2)}) %collective-permute-start.28) | collective-permute-done | bytes 196640 | tf_op jit(solution)/shard_map/ppermute | solution.py:339
  64.0 1.1 %collective-permute-done.29.gl = bf16[32,3072]{1,0:T(8,128)(2,1)S(1)} collective-permute-done((bf16[32,3072]{1,0:T(8,128)(2,1)S(1)}, bf16[32,3072]{1,0:T(8,128)(2,1)S(1)}, u32[]{:S(2)}, u32[]{:S(2)}) %collective-permute-start.29) | collective-permute-done | bytes 196640 | tf_op jit(solution)/shard_map/ppermute | solution.py:339
  65.2 1.6 %collective-permute-start.30 = (bf16[32,3072]{1,0:T(8,128)(2,1)S(1)}, bf16[32,3072]{1,0:T(8,128)(2,1)S(1)}, u32[]{:S(2)}, u32[]{:S(2)}) collective-permute-start(bf16[32,3072]{1,0:T(8,128)(2,1)S(1)} %get-tuple-element.76), channel_id=1, source_target_pairs={{0,2},{2,4},{4,6},{6,7},{7,5},{5,3},{3,1},{1,0},{8,10},{10,12},{12... | collective-permute-start | bytes 589832 | tf_op jit(solution)/shard_map/ppermute | solution.py:339
  67.3 1.0 %collective-permute-done.22.gr = bf16[32,3072]{1,0:T(8,128)(2,1)S(1)} collective-permute-done((bf16[32,3072]{1,0:T(8,128)(2,1)S(1)}, bf16[32,3072]{1,0:T(8,128)(2,1)S(1)}, u32[]{:S(2)}, u32[]{:S(2)}) %collective-permute-start.22) | collective-permute-done | bytes 196640 | tf_op jit(solution)/shard_map/ppermute | solution.py:339
  68.3 1.6 %collective-permute-done.23.gl = bf16[32,3072]{1,0:T(8,128)(2,1)S(1)} collective-permute-done((bf16[32,3072]{1,0:T(8,128)(2,1)S(1)}, bf16[32,3072]{1,0:T(8,128)(2,1)S(1)}, u32[]{:S(2)}, u32[]{:S(2)}) %collective-permute-start.23) | collective-permute-done | bytes 196640 | tf_op jit(solution)/shard_map/ppermute | solution.py:339
  70.4 1.6 %collective-permute-start.25 = (bf16[32,3072]{1,0:T(8,128)(2,1)S(1)}, bf16[32,3072]{1,0:T(8,128)(2,1)S(1)}, u32[]{:S(2)}, u32[]{:S(2)}) collective-permute-start(bf16[32,3072]{1,0:T(8,128)(2,1)S(1)} %get-tuple-element.66), channel_id=1, source_target_pairs={{0,2},{2,4},{4,6},{6,7},{7,5},{5,3},{3,1},{1,0},{8,10},{10,12},{12... | collective-permute-start | bytes 589832 | tf_op jit(solution)/shard_map/ppermute | solution.py:339
  72.5 1.6 %collective-permute-done.31.gl = bf16[32,3072]{1,0:T(8,128)(2,1)S(1)} collective-permute-done((bf16[32,3072]{1,0:T(8,128)(2,1)S(1)}, bf16[32,3072]{1,0:T(8,128)(2,1)S(1)}, u32[]{:S(2)}, u32[]{:S(2)}) %collective-permute-start.31) | collective-permute-done | bytes 196640 | tf_op jit(solution)/shard_map/ppermute | solution.py:339
  74.2 1.5 %collective-permute-start.32 = (bf16[32,3072]{1,0:T(8,128)(2,1)S(1)}, bf16[32,3072]{1,0:T(8,128)(2,1)S(1)}, u32[]{:S(2)}, u32[]{:S(2)}) collective-permute-start(bf16[32,3072]{1,0:T(8,128)(2,1)S(1)} %get-tuple-element.79), channel_id=1, source_target_pairs={{0,2},{2,4},{4,6},{6,7},{7,5},{5,3},{3,1},{1,0},{8,10},{10,12},{12... | collective-permute-start | bytes 589832 | tf_op jit(solution)/shard_map/ppermute | solution.py:339
  76.2 1.6 %collective-permute-done.24.got_first = bf16[32,3072]{1,0:T(8,128)(2,1)S(1)} collective-permute-done((bf16[32,3072]{1,0:T(8,128)(2,1)S(1)}, bf16[32,3072]{1,0:T(8,128)(2,1)S(1)}, u32[]{:S(2)}, u32[]{:S(2)}) %collective-permute-start.24) | collective-permute-done | bytes 196640 | tf_op jit(solution)/shard_map/ppermute | solution.py:339
  78.0 1.9 %collective-permute-done.32.first = bf16[32,3072]{1,0:T(8,128)(2,1)S(1)} collective-permute-done((bf16[32,3072]{1,0:T(8,128)(2,1)S(1)}, bf16[32,3072]{1,0:T(8,128)(2,1)S(1)}, u32[]{:S(2)}, u32[]{:S(2)}) %collective-permute-start.32) | collective-permute-done | bytes 196640 | tf_op jit(solution)/shard_map/ppermute | solution.py:339
  79.9 1.5 %collective-permute-done.33.second = bf16[32,3072]{1,0:T(8,128)(2,1)S(1)} collective-permute-done((bf16[32,3072]{1,0:T(8,128)(2,1)S(1)}, bf16[32,3072]{1,0:T(8,128)(2,1)S(1)}, u32[]{:S(2)}, u32[]{:S(2)}) %collective-permute-start.33) | collective-permute-done | bytes 196640 | tf_op jit(solution)/shard_map/ppermute | solution.py:339
  81.4 0.8 finish.1
  (62 shorter events, 5.4 us)
Async XLA Ops:
  1.1 8.8 %collective-permute-start.1 = (bf16[32,3072]{1,0:T(8,128)(2,1)S(1)}, bf16[32,3072]{1,0:T(8,128)(2,1)S(1)}, u32[]{:S(2)}, u32[]{:S(2)}) collective-permute-start(bf16[32,3072]{1,0:T(8,128)(2,1)S(1)} %get-tuple-element.82.refs_0_), channel_id=1, source_target_pairs={{2,0},{4,2},{6,4},{7,6},{5,7},{3,5},{1,3},{0,1},{10,8},{12,10},{14... | collective-permute-start | bytes 589832 | tf_op jit(solution)/shard_map/ppermute | solution.py:75
  4.0 7.8 %collective-permute-start = (bf16[32,3072]{1,0:T(8,128)(2,1)S(1)}, bf16[32,3072]{1,0:T(8,128)(2,1)S(1)}, u32[]{:S(2)}, u32[]{:S(2)}) collective-permute-start(bf16[32,3072]{1,0:T(8,128)(2,1)S(1)} %get-tuple-element.82.refs_0_), channel_id=1, source_target_pairs={{0,2},{2,4},{4,6},{6,7},{7,5},{5,3},{3,1},{1,0},{8,10},{10,12},{12... | collective-permute-start | bytes 589832 | tf_op jit(solution)/shard_map/ppermute | solution.py:74
  4.2 9.9 %collective-permute-start.10 = (bf16[32,3072]{1,0:T(8,128)(2,1)S(1)}, bf16[32,3072]{1,0:T(8,128)(2,1)S(1)}, u32[]{:S(2)}, u32[]{:S(2)}) collective-permute-start(bf16[32,3072]{1,0:T(8,128)(2,1)S(1)} %get-tuple-element.81.refs_0_), channel_id=1, source_target_pairs={{2,0},{4,2},{6,4},{7,6},{5,7},{3,5},{1,3},{0,1},{10,8},{12,10},{14... | collective-permute-start | bytes 589832 | tf_op jit(solution)/shard_map/ppermute | solution.py:75
  6.1 10.0 %collective-permute-start.8 = (bf16[32,3072]{1,0:T(8,128)(2,1)S(1)}, bf16[32,3072]{1,0:T(8,128)(2,1)S(1)}, u32[]{:S(2)}, u32[]{:S(2)}) collective-permute-start(bf16[32,3072]{1,0:T(8,128)(2,1)S(1)} %get-tuple-element.81.refs_0_), channel_id=1, source_target_pairs={{0,2},{2,4},{4,6},{6,7},{7,5},{5,3},{3,1},{1,0},{8,10},{10,12},{12... | collective-permute-start | bytes 589832 | tf_op jit(solution)/shard_map/ppermute | solution.py:74
  9.9 8.4 %collective-permute-start.3 = (bf16[32,3072]{1,0:T(8,128)(2,1)S(1)}, bf16[32,3072]{1,0:T(8,128)(2,1)S(1)}, u32[]{:S(2)}, u32[]{:S(2)}) collective-permute-start(bf16[32,3072]{1,0:T(8,128)(2,1)S(1)} %collective-permute-done.1.refs_2_), channel_id=1, source_target_pairs={{2,0},{4,2},{6,4},{7,6},{5,7},{3,5},{1,3},{0,1},{10,8},{12,10},{14... | collective-permute-start | bytes 589832 | tf_op jit(solution)/shard_map/ppermute | solution.py:75
  11.9 8.4 %collective-permute-start.2 = (bf16[32,3072]{1,0:T(8,128)(2,1)S(1)}, bf16[32,3072]{1,0:T(8,128)(2,1)S(1)}, u32[]{:S(2)}, u32[]{:S(2)}) collective-permute-start(bf16[32,3072]{1,0:T(8,128)(2,1)S(1)} %collective-permute-done.refs_1_), channel_id=1, source_target_pairs={{0,2},{2,4},{4,6},{6,7},{7,5},{5,3},{3,1},{1,0},{8,10},{10,12},{12... | collective-permute-start | bytes 589832 | tf_op jit(solution)/shard_map/ppermute | solution.py:74
  14.1 8.4 %collective-permute-start.11 = (bf16[32,3072]{1,0:T(8,128)(2,1)S(1)}, bf16[32,3072]{1,0:T(8,128)(2,1)S(1)}, u32[]{:S(2)}, u32[]{:S(2)}) collective-permute-start(bf16[32,3072]{1,0:T(8,128)(2,1)S(1)} %collective-permute-done.10.refs_2_), channel_id=1, source_target_pairs={{2,0},{4,2},{6,4},{7,6},{5,7},{3,5},{1,3},{0,1},{10,8},{12,10},{14... | collective-permute-start | bytes 589832 | tf_op jit(solution)/shard_map/ppermute | solution.py:75
  16.1 8.5 %collective-permute-start.9 = (bf16[32,3072]{1,0:T(8,128)(2,1)S(1)}, bf16[32,3072]{1,0:T(8,128)(2,1)S(1)}, u32[]{:S(2)}, u32[]{:S(2)}) collective-permute-start(bf16[32,3072]{1,0:T(8,128)(2,1)S(1)} %collective-permute-done.8.refs_1_), channel_id=1, source_target_pairs={{0,2},{2,4},{4,6},{6,7},{7,5},{5,3},{3,1},{1,0},{8,10},{10,12},{12... | collective-permute-start | bytes 589832 | tf_op jit(solution)/shard_map/ppermute | solution.py:74
  18.3 8.4 %collective-permute-start.5 = (bf16[32,3072]{1,0:T(8,128)(2,1)S(1)}, bf16[32,3072]{1,0:T(8,128)(2,1)S(1)}, u32[]{:S(2)}, u32[]{:S(2)}) collective-permute-start(bf16[32,3072]{1,0:T(8,128)(2,1)S(1)} %collective-permute-done.3.refs_4_), channel_id=1, source_target_pairs={{2,0},{4,2},{6,4},{7,6},{5,7},{3,5},{1,3},{0,1},{10,8},{12,10},{14... | collective-permute-start | bytes 589832 | tf_op jit(solution)/shard_map/ppermute | solution.py:75
  20.3 8.5 %collective-permute-start.4 = (bf16[32,3072]{1,0:T(8,128)(2,1)S(1)}, bf16[32,3072]{1,0:T(8,128)(2,1)S(1)}, u32[]{:S(2)}, u32[]{:S(2)}) collective-permute-start(bf16[32,3072]{1,0:T(8,128)(2,1)S(1)} %collective-permute-done.2.refs_3_), channel_id=1, source_target_pairs={{0,2},{2,4},{4,6},{6,7},{7,5},{5,3},{3,1},{1,0},{8,10},{10,12},{12... | collective-permute-start | bytes 589832 | tf_op jit(solution)/shard_map/ppermute | solution.py:74
  22.5 11.4 %slice-start = ((s8[18874368]{0:T(1024)(128)(4,1)}), s8[4194304]{0:T(1024)(128)(4,1)S(1)}, s32[]{:S(2)}) async-start(s8[18874368]{0:T(1024)(128)(4,1)} %bitcast.1), calls=%async_computation | async-start | bytes 8388608
  22.5 11.4 %slice-start.1 = ((s8[18874368]{0:T(1024)(128)(4,1)}), s8[4194304]{0:T(1024)(128)(4,1)S(1)}, s32[]{:S(2)}) async-start(s8[18874368]{0:T(1024)(128)(4,1)} %bitcast.1), calls=%async_computation.1 | async-start | bytes 8388608
  22.5 11.4 %slice-start.2 = ((s8[18874368]{0:T(1024)(128)(4,1)}), s8[4194304]{0:T(1024)(128)(4,1)S(1)}, s32[]{:S(2)}) async-start(s8[18874368]{0:T(1024)(128)(4,1)} %bitcast.1), calls=%async_computation.2 | async-start | bytes 8388608
  22.5 8.4 %collective-permute-start.13 = (bf16[32,3072]{1,0:T(8,128)(2,1)S(1)}, bf16[32,3072]{1,0:T(8,128)(2,1)S(1)}, u32[]{:S(2)}, u32[]{:S(2)}) collective-permute-start(bf16[32,3072]{1,0:T(8,128)(2,1)S(1)} %collective-permute-done.11.arrived_ref.refs_4_), channel_id=1, source_target_pairs={{2,0},{4,2},{6,4},{7,6},{5,7},{3,5},{1,3},{0,1},{10,8},{12,10},{14... | collective-permute-start | bytes 589832 | tf_op jit(solution)/shard_map/ppermute | solution.py:75
  24.5 8.3 %collective-permute-start.12 = (bf16[32,3072]{1,0:T(8,128)(2,1)S(1)}, bf16[32,3072]{1,0:T(8,128)(2,1)S(1)}, u32[]{:S(2)}, u32[]{:S(2)}) collective-permute-start(bf16[32,3072]{1,0:T(8,128)(2,1)S(1)} %collective-permute-done.9.arrived_ref.refs_3_), channel_id=1, source_target_pairs={{0,2},{2,4},{4,6},{6,7},{7,5},{5,3},{3,1},{1,0},{8,10},{10,12},{12... | collective-permute-start | bytes 589832 | tf_op jit(solution)/shard_map/ppermute | solution.py:74
  26.7 6.4 %collective-permute-start.7 = (bf16[32,1536]{1,0:T(8,128)(2,1)S(1)}, bf16[32,1536]{1,0:T(8,128)(2,1)S(1)}, u32[]{:S(2)}, u32[]{:S(2)}) collective-permute-start(bf16[32,1536]{1,0:T(8,128)(2,1)S(1)} %slice.25), channel_id=1, source_target_pairs={{2,0},{4,2},{6,4},{7,6},{5,7},{3,5},{1,3},{0,1},{10,8},{12,10},{14... | collective-permute-start | bytes 294920 | tf_op jit(solution)/shard_map/ppermute | solution.py:79
  28.8 5.2 %slice-start.3 = ((s8[18874368]{0:T(1024)(128)(4,1)}), s8[4194304]{0:T(1024)(128)(4,1)S(1)}, s32[]{:S(2)}) async-start(s8[18874368]{0:T(1024)(128)(4,1)} %bitcast.1), calls=%async_computation.3 | async-start | bytes 8388608
  28.8 5.2 %slice-start.4 = ((s8[18874368]{0:T(1024)(128)(4,1)}), s8[2097152]{0:T(1024)(128)(4,1)S(1)}, s32[]{:S(2)}) async-start(s8[18874368]{0:T(1024)(128)(4,1)} %bitcast.1), calls=%async_computation.4 | async-start | bytes 4194304
  28.8 5.1 %collective-permute-start.6 = (bf16[32,1536]{1,0:T(8,128)(2,1)S(1)}, bf16[32,1536]{1,0:T(8,128)(2,1)S(1)}, u32[]{:S(2)}, u32[]{:S(2)}) collective-permute-start(bf16[32,1536]{1,0:T(8,128)(2,1)S(1)} %slice.24), channel_id=1, source_target_pairs={{0,2},{2,4},{4,6},{6,7},{7,5},{5,3},{3,1},{1,0},{8,10},{10,12},{12... | collective-permute-start | bytes 294920 | tf_op jit(solution)/shard_map/ppermute | solution.py:78
  30.9 4.8 %collective-permute-start.15 = (bf16[32,1536]{1,0:T(8,128)(2,1)S(1)}, bf16[32,1536]{1,0:T(8,128)(2,1)S(1)}, u32[]{:S(2)}, u32[]{:S(2)}) collective-permute-start(bf16[32,1536]{1,0:T(8,128)(2,1)S(1)} %slice.27), channel_id=1, source_target_pairs={{2,0},{4,2},{6,4},{7,6},{5,7},{3,5},{1,3},{0,1},{10,8},{12,10},{14... | collective-permute-start | bytes 294920 | tf_op jit(solution)/shard_map/ppermute | solution.py:79
  32.9 4.7 %collective-permute-start.14 = (bf16[32,1536]{1,0:T(8,128)(2,1)S(1)}, bf16[32,1536]{1,0:T(8,128)(2,1)S(1)}, u32[]{:S(2)}, u32[]{:S(2)}) collective-permute-start(bf16[32,1536]{1,0:T(8,128)(2,1)S(1)} %slice.26), channel_id=1, source_target_pairs={{0,2},{2,4},{4,6},{6,7},{7,5},{5,3},{3,1},{1,0},{8,10},{10,12},{12... | collective-permute-start | bytes 294920 | tf_op jit(solution)/shard_map/ppermute | solution.py:78
  38.8 1.9 %collective-permute-start.16 = (bf16[2,128,128]{2,1,0:T(8,128)(2,1)S(1)}, bf16[2,128,128]{2,1,0:T(8,128)(2,1)S(1)}, u32[]{:S(2)}, u32[]{:S(2)}) collective-permute-start(bf16[2,128,128]{2,1,0:T(8,128)(2,1)S(1)} %get-tuple-element.52.one_ref), channel_id=1, source_target_pairs={{0,8},{8,0},{16,24},{24,16},{1,9},{9,1},{17,25},{25,17},{2,10},{10... | collective-permute-start | bytes 196616 | tf_op jit(solution)/shard_map/ppermute | solution.py:373
  38.9 7.8 %slice-start.5 = ((s8[6291456]{0:T(1024)(128)(4,1)}), s8[4194304]{0:T(1024)(128)(4,1)S(1)}, s32[]{:S(2)}) async-start(s8[6291456]{0:T(1024)(128)(4,1)} %bitcast.3), calls=%async_computation.5 | async-start | bytes 8388608
  40.1 2.2 %collective-permute-start.18 = (bf16[2,128,128]{2,1,0:T(8,128)(2,1)S(1)}, bf16[2,128,128]{2,1,0:T(8,128)(2,1)S(1)}, u32[]{:S(2)}, u32[]{:S(2)}) collective-permute-start(bf16[2,128,128]{2,1,0:T(8,128)(2,1)S(1)} %get-tuple-element.53.one_ref), channel_id=1, source_target_pairs={{0,8},{8,0},{16,24},{24,16},{1,9},{9,1},{17,25},{25,17},{2,10},{10... | collective-permute-start | bytes 196616 | tf_op jit(solution)/shard_map/ppermute | solution.py:373
  40.7 5.9 %collective-permute-start.17 = (bf16[2,128,128]{2,1,0:T(8,128)(2,1)S(1)}, bf16[2,128,128]{2,1,0:T(8,128)(2,1)S(1)}, u32[]{:S(2)}, u32[]{:S(2)}) collective-permute-start(bf16[2,128,128]{2,1,0:T(8,128)(2,1)S(1)} %add_states.2.refs_0_), channel_id=1, source_target_pairs={{0,16},{8,24},{16,0},{24,8},{1,17},{9,25},{17,1},{25,9},{2,18},{10... | collective-permute-start | bytes 196616 | tf_op jit(solution)/shard_map/ppermute | solution.py:373
  42.3 4.3 %collective-permute-start.19 = (bf16[2,128,128]{2,1,0:T(8,128)(2,1)S(1)}, bf16[2,128,128]{2,1,0:T(8,128)(2,1)S(1)}, u32[]{:S(2)}, u32[]{:S(2)}) collective-permute-start(bf16[2,128,128]{2,1,0:T(8,128)(2,1)S(1)} %add_states.3), channel_id=1, source_target_pairs={{0,16},{8,24},{16,0},{24,8},{1,17},{9,25},{17,1},{25,9},{2,18},{10... | collective-permute-start | bytes 196616 | tf_op jit(solution)/shard_map/ppermute | solution.py:373
  43.2 3.5 %slice-start.6 = ((s8[6291456]{0:T(1024)(128)(4,1)}), s8[2097152]{0:T(1024)(128)(4,1)S(1)}, s32[]{:S(2)}) async-start(s8[6291456]{0:T(1024)(128)(4,1)} %bitcast.3), calls=%async_computation.6 | async-start | bytes 4194304
  43.2 3.5 %copy-start = (f32[4,128,128]{2,1,0:T(8,128)S(1)}, f32[4,128,128]{2,1,0:T(8,128)}, u32[]{:S(2)}) copy-start(f32[4,128,128]{2,1,0:T(8,128)} %initial_ref.1) | copy-start | bytes 786436
  43.2 3.5 %copy-start.1 = (f32[512]{0:T(512)S(1)}, f32[512]{0:T(512)}, u32[]{:S(2)}) copy-start(f32[512]{0:T(512)} %param.8) | copy-start | bytes 6148
  48.2 6.9 %collective-permute-start.26 = (bf16[32,3072]{1,0:T(8,128)(2,1)S(1)}, bf16[32,3072]{1,0:T(8,128)(2,1)S(1)}, u32[]{:S(2)}, u32[]{:S(2)}) collective-permute-start(bf16[32,3072]{1,0:T(8,128)(2,1)S(1)} %get-tuple-element.70), channel_id=1, source_target_pairs={{0,2},{2,4},{4,6},{6,7},{7,5},{5,3},{3,1},{1,0},{8,10},{10,12},{12... | collective-permute-start | bytes 589832 | tf_op jit(solution)/shard_map/ppermute | solution.py:339
  48.8 7.0 %collective-permute-start.27 = (bf16[32,3072]{1,0:T(8,128)(2,1)S(1)}, bf16[32,3072]{1,0:T(8,128)(2,1)S(1)}, u32[]{:S(2)}, u32[]{:S(2)}) collective-permute-start(bf16[32,3072]{1,0:T(8,128)(2,1)S(1)} %get-tuple-element.72), channel_id=1, source_target_pairs={{2,0},{4,2},{6,4},{7,6},{5,7},{3,5},{1,3},{0,1},{10,8},{12,10},{14... | collective-permute-start | bytes 589832 | tf_op jit(solution)/shard_map/ppermute | solution.py:339
  51.9 7.9 %collective-permute-start.20 = (bf16[32,3072]{1,0:T(8,128)(2,1)S(1)}, bf16[32,3072]{1,0:T(8,128)(2,1)S(1)}, u32[]{:S(2)}, u32[]{:S(2)}) collective-permute-start(bf16[32,3072]{1,0:T(8,128)(2,1)S(1)} %get-tuple-element.59), channel_id=1, source_target_pairs={{0,2},{2,4},{4,6},{6,7},{7,5},{5,3},{3,1},{1,0},{8,10},{10,12},{12... | collective-permute-start | bytes 589832 | tf_op jit(solution)/shard_map/ppermute | solution.py:339
  52.4 7.8 %collective-permute-start.21 = (bf16[32,3072]{1,0:T(8,128)(2,1)S(1)}, bf16[32,3072]{1,0:T(8,128)(2,1)S(1)}, u32[]{:S(2)}, u32[]{:S(2)}) collective-permute-start(bf16[32,3072]{1,0:T(8,128)(2,1)S(1)} %get-tuple-element.61), channel_id=1, source_target_pairs={{2,0},{4,2},{6,4},{7,6},{5,7},{3,5},{1,3},{0,1},{10,8},{12,10},{14... | collective-permute-start | bytes 589832 | tf_op jit(solution)/shard_map/ppermute | solution.py:339
  55.8 8.1 %collective-permute-start.28 = (bf16[32,3072]{1,0:T(8,128)(2,1)S(1)}, bf16[32,3072]{1,0:T(8,128)(2,1)S(1)}, u32[]{:S(2)}, u32[]{:S(2)}) collective-permute-start(bf16[32,3072]{1,0:T(8,128)(2,1)S(1)} %get-tuple-element.73), channel_id=1, source_target_pairs={{0,2},{2,4},{4,6},{6,7},{7,5},{5,3},{3,1},{1,0},{8,10},{10,12},{12... | collective-permute-start | bytes 589832 | tf_op jit(solution)/shard_map/ppermute | solution.py:339
  57.5 7.6 %collective-permute-start.29 = (bf16[32,3072]{1,0:T(8,128)(2,1)S(1)}, bf16[32,3072]{1,0:T(8,128)(2,1)S(1)}, u32[]{:S(2)}, u32[]{:S(2)}) collective-permute-start(bf16[32,3072]{1,0:T(8,128)(2,1)S(1)} %get-tuple-element.75), channel_id=1, source_target_pairs={{2,0},{4,2},{6,4},{7,6},{5,7},{3,5},{1,3},{0,1},{10,8},{12,10},{14... | collective-permute-start | bytes 589832 | tf_op jit(solution)/shard_map/ppermute | solution.py:339
  60.4 7.9 %collective-permute-start.22 = (bf16[32,3072]{1,0:T(8,128)(2,1)S(1)}, bf16[32,3072]{1,0:T(8,128)(2,1)S(1)}, u32[]{:S(2)}, u32[]{:S(2)}) collective-permute-start(bf16[32,3072]{1,0:T(8,128)(2,1)S(1)} %get-tuple-element.62), channel_id=1, source_target_pairs={{0,2},{2,4},{4,6},{6,7},{7,5},{5,3},{3,1},{1,0},{8,10},{10,12},{12... | collective-permute-start | bytes 589832 | tf_op jit(solution)/shard_map/ppermute | solution.py:339
  62.0 7.8 %collective-permute-start.23 = (bf16[32,3072]{1,0:T(8,128)(2,1)S(1)}, bf16[32,3072]{1,0:T(8,128)(2,1)S(1)}, u32[]{:S(2)}, u32[]{:S(2)}) collective-permute-start(bf16[32,3072]{1,0:T(8,128)(2,1)S(1)} %get-tuple-element.64), channel_id=1, source_target_pairs={{2,0},{4,2},{6,4},{7,6},{5,7},{3,5},{1,3},{0,1},{10,8},{12,10},{14... | collective-permute-start | bytes 589832 | tf_op jit(solution)/shard_map/ppermute | solution.py:339
  65.2 7.3 %collective-permute-start.30 = (bf16[32,3072]{1,0:T(8,128)(2,1)S(1)}, bf16[32,3072]{1,0:T(8,128)(2,1)S(1)}, u32[]{:S(2)}, u32[]{:S(2)}) collective-permute-start(bf16[32,3072]{1,0:T(8,128)(2,1)S(1)} %get-tuple-element.76), channel_id=1, source_target_pairs={{0,2},{2,4},{4,6},{6,7},{7,5},{5,3},{3,1},{1,0},{8,10},{10,12},{12... | collective-permute-start | bytes 589832 | tf_op jit(solution)/shard_map/ppermute | solution.py:339
  66.8 7.2 %collective-permute-start.31 = (bf16[32,3072]{1,0:T(8,128)(2,1)S(1)}, bf16[32,3072]{1,0:T(8,128)(2,1)S(1)}, u32[]{:S(2)}, u32[]{:S(2)}) collective-permute-start(bf16[32,3072]{1,0:T(8,128)(2,1)S(1)} %get-tuple-element.78), channel_id=1, source_target_pairs={{2,0},{4,2},{6,4},{7,6},{5,7},{3,5},{1,3},{0,1},{10,8},{12,10},{14... | collective-permute-start | bytes 589832 | tf_op jit(solution)/shard_map/ppermute | solution.py:339
  69.9 7.9 %collective-permute-start.24 = (bf16[32,3072]{1,0:T(8,128)(2,1)S(1)}, bf16[32,3072]{1,0:T(8,128)(2,1)S(1)}, u32[]{:S(2)}, u32[]{:S(2)}) collective-permute-start(bf16[32,3072]{1,0:T(8,128)(2,1)S(1)} %get-tuple-element.65), channel_id=1, source_target_pairs={{2,0},{4,2},{6,4},{7,6},{5,7},{3,5},{1,3},{0,1},{10,8},{12,10},{14... | collective-permute-start | bytes 589832 | tf_op jit(solution)/shard_map/ppermute | solution.py:339
  70.4 7.4 %collective-permute-start.25 = (bf16[32,3072]{1,0:T(8,128)(2,1)S(1)}, bf16[32,3072]{1,0:T(8,128)(2,1)S(1)}, u32[]{:S(2)}, u32[]{:S(2)}) collective-permute-start(bf16[32,3072]{1,0:T(8,128)(2,1)S(1)} %get-tuple-element.66), channel_id=1, source_target_pairs={{0,2},{2,4},{4,6},{6,7},{7,5},{5,3},{3,1},{1,0},{8,10},{10,12},{12... | collective-permute-start | bytes 589832 | tf_op jit(solution)/shard_map/ppermute | solution.py:339
  74.2 5.7 %collective-permute-start.32 = (bf16[32,3072]{1,0:T(8,128)(2,1)S(1)}, bf16[32,3072]{1,0:T(8,128)(2,1)S(1)}, u32[]{:S(2)}, u32[]{:S(2)}) collective-permute-start(bf16[32,3072]{1,0:T(8,128)(2,1)S(1)} %get-tuple-element.79), channel_id=1, source_target_pairs={{0,2},{2,4},{4,6},{6,7},{7,5},{5,3},{3,1},{1,0},{8,10},{10,12},{12... | collective-permute-start | bytes 589832 | tf_op jit(solution)/shard_map/ppermute | solution.py:339
  75.7 5.7 %collective-permute-start.33 = (bf16[32,3072]{1,0:T(8,128)(2,1)S(1)}, bf16[32,3072]{1,0:T(8,128)(2,1)S(1)}, u32[]{:S(2)}, u32[]{:S(2)}) collective-permute-start(bf16[32,3072]{1,0:T(8,128)(2,1)S(1)} %get-tuple-element.80), channel_id=1, source_target_pairs={{2,0},{4,2},{6,4},{7,6},{5,7},{3,5},{1,3},{0,1},{10,8},{12,10},{14... | collective-permute-start | bytes 589832 | tf_op jit(solution)/shard_map/ppermute | solution.py:339

commit v7 on v6

--- a/solution.py
+++ b/solution.py
@@ -278,20 +278,19 @@
     return [out[2 * block : 2 * block + 2] for block in range(blocks)]
 
 
-def add_step(mine_right, got_right, mine_left, got_left):
-    def body(mr, gr, ml, gl, to_right, to_left):
-        to_right[...] = (mr[...].astype(F32) + gr[...].astype(F32)).astype(BF16)
-        to_left[...] = (ml[...].astype(F32) + gl[...].astype(F32)).astype(BF16)
-
-    return call(
-        body,
-        [jax.ShapeDtypeStruct(mine_right.shape, BF16)] * 2,
-        [VMEM] * 4,
+def add_step(mine, got):
+    def body(mine_ref, got_ref, out_ref):
+        out_ref[...] = (mine_ref[...].astype(F32) + got_ref[...].astype(F32)).astype(BF16)
+
+    return call(
+        body,
+        jax.ShapeDtypeStruct(mine.shape, BF16),
         [VMEM] * 2,
-        nbytes=12 * mine_right.size,
+        VMEM,
+        nbytes=6 * mine.size,
         limit=4 << 20,
         name="add_step",
-    )(mine_right, got_right, mine_left, got_left)
+    )(mine, got)
 
 
 def add_own(own, trailing):
@@ -341,9 +340,11 @@
     leading = hop(part(far, 0), part(far, 1))
     trailing = hop(part(far - 1, 1), part(1 - far, 0))
     for step in range(far - 1, 0, -1):
-        leading = hop(*add_step(part(step, 0), leading[0], part(-step, 1), leading[1]))
+        leading = hop(add_step(part(step, 0), leading[0]), add_step(part(-step, 1), leading[1]))
         if step > 1:
-            trailing = hop(*add_step(part(step - 1, 1), trailing[0], part(1 - step, 0), trailing[1]))
+            trailing = hop(
+                add_step(part(step - 1, 1), trailing[0]), add_step(part(1 - step, 0), trailing[1])
+            )
     gathered = add_own(parts[0], (trailing[1], trailing[0]))
     return finish(gathered, leading)
 

time: 82.3 us -> 80.7 us (0.981)
  waiting for transfers between devices: 34.3 us -> 32.1 us
    ppermute x7, starting transfers between devices: 5.38 us -> 10.2 us  [hop(): lax.ppermute(to_left, 'fsdp', left)]
    ppermute x7, starting transfers between devices: 9.14 us -> 4.83 us  [hop(): lax.ppermute(to_right, 'fsdp', right)]
    ppermute x7, waiting for transfers between devices: 7.86 us -> 4.92 us  [hop(): lax.ppermute(to_right, 'fsdp', right)]
  transfers between devices with their start and end apart: 34 -> 34, of which waited for: 22 -> 19; matrix products, arithmetic and copies ran while one was open for 0% -> 0% of each run, Pallas kernels for 9% -> 9%
where the time goes in v7:
time: 80.7 us; the launch traced here: 80.5 us
  starting transfers between devices  36 us (45%)
  waiting for transfers between devices  32.1 us (40%)
  Pallas kernels  11.1 us (14%)
  local copies, waits for them, and re-layouts  1.12 us (1%)
    ppermute x6, waiting for transfers between devices, ring_gather(): going_left[part] = lax.ppermute(going_left[part], 'fsdp', left)  13.9 us
    ppermute x6, starting transfers between devices, ring_gather(): going_left[part] = lax.ppermute(going_left[part], 'fsdp', left)  12.8 us
    ppermute x7, starting transfers between devices, hop(): lax.ppermute(to_left, 'fsdp', left)  10.2 us
    ppermute x7, waiting for transfers between devices, hop(): lax.ppermute(to_left, 'fsdp', left)  9.36 us
    ppermute x7, waiting for transfers between devices, hop(): lax.ppermute(to_right, 'fsdp', right)  4.92 us
    ppermute x7, starting transfers between devices, hop(): lax.ppermute(to_right, 'fsdp', right)  4.83 us
    ppermute x2, starting transfers between devices, ring_gather(): held[part].append(lax.ppermute(going_left[part][:, quarter:], 'fsdp', left))  3.96 us
    ppermute x4, starting transfers between devices, exchange_states(): received[at].append(lax.ppermute(total, 'ctx', pairs))  3.08 us
  transfers between devices with their start and end apart: 34, of which 19 were waited for; matrix products, arithmetic and copies ran while one was open for 0% of the time, Pallas kernels for 9%

profile of v7, /device:TPU:0, one launch (start us, length us, event | category | flops | bytes accessed | tf_op | source)
XLA Modules:
  0.0 80.5 jit_solution(14358051657122498314)
XLA Ops:
  0.0 1.0 %fusion = (bf16[32,3072]{1,0:T(8,128)(2,1)S(1)}, bf16[32,3072]{1,0:T(8,128)(2,1)S(1)}) fusion(bf16[32,6144]{1,0:T(8,128)(2,1)} %param.5), kind=kLoop, calls=%fused_computation | loop fusion | bytes 786432 | tf_op jit(solution)/shard_map/slice | solution.py:69
  1.1 3.0 %collective-permute-start.1 = (bf16[32,3072]{1,0:T(8,128)(2,1)S(1)}, bf16[32,3072]{1,0:T(8,128)(2,1)S(1)}, u32[]{:S(2)}, u32[]{:S(2)}) collective-permute-start(bf16[32,3072]{1,0:T(8,128)(2,1)S(1)} %get-tuple-element.62.refs_0_), channel_id=1, source_target_pairs={{2,0},{4,2},{6,4},{7,6},{5,7},{3,5},{1,3},{0,1},{10,8},{12,10},{14... | collective-permute-start | bytes 589832 | tf_op jit(solution)/shard_map/ppermute | solution.py:75
  4.2 1.9 %collective-permute-start.10 = (bf16[32,3072]{1,0:T(8,128)(2,1)S(1)}, bf16[32,3072]{1,0:T(8,128)(2,1)S(1)}, u32[]{:S(2)}, u32[]{:S(2)}) collective-permute-start(bf16[32,3072]{1,0:T(8,128)(2,1)S(1)} %get-tuple-element.61.refs_0_), channel_id=1, source_target_pairs={{2,0},{4,2},{6,4},{7,6},{5,7},{3,5},{1,3},{0,1},{10,8},{12,10},{14... | collective-permute-start | bytes 589832 | tf_op jit(solution)/shard_map/ppermute | solution.py:75
  6.2 3.6 %collective-permute-done.1.refs_2_ = bf16[32,3072]{1,0:T(8,128)(2,1)S(1)} collective-permute-done((bf16[32,3072]{1,0:T(8,128)(2,1)S(1)}, bf16[32,3072]{1,0:T(8,128)(2,1)S(1)}, u32[]{:S(2)}, u32[]{:S(2)}) %collective-permute-start.1) | collective-permute-done | bytes 196640 | tf_op jit(solution)/shard_map/ppermute | solution.py:75
  9.9 2.0 %collective-permute-start.3 = (bf16[32,3072]{1,0:T(8,128)(2,1)S(1)}, bf16[32,3072]{1,0:T(8,128)(2,1)S(1)}, u32[]{:S(2)}, u32[]{:S(2)}) collective-permute-start(bf16[32,3072]{1,0:T(8,128)(2,1)S(1)} %collective-permute-done.1.refs_2_), channel_id=1, source_target_pairs={{2,0},{4,2},{6,4},{7,6},{5,7},{3,5},{1,3},{0,1},{10,8},{12,10},{14... | collective-permute-start | bytes 589832 | tf_op jit(solution)/shard_map/ppermute | solution.py:75
  12.0 2.1 %collective-permute-done.10.refs_2_ = bf16[32,3072]{1,0:T(8,128)(2,1)S(1)} collective-permute-done((bf16[32,3072]{1,0:T(8,128)(2,1)S(1)}, bf16[32,3072]{1,0:T(8,128)(2,1)S(1)}, u32[]{:S(2)}, u32[]{:S(2)}) %collective-permute-start.10) | collective-permute-done | bytes 196640 | tf_op jit(solution)/shard_map/ppermute | solution.py:75
  14.1 2.0 %collective-permute-start.11 = (bf16[32,3072]{1,0:T(8,128)(2,1)S(1)}, bf16[32,3072]{1,0:T(8,128)(2,1)S(1)}, u32[]{:S(2)}, u32[]{:S(2)}) collective-permute-start(bf16[32,3072]{1,0:T(8,128)(2,1)S(1)} %collective-permute-done.10.refs_2_), channel_id=1, source_target_pairs={{2,0},{4,2},{6,4},{7,6},{5,7},{3,5},{1,3},{0,1},{10,8},{12,10},{14... | collective-permute-start | bytes 589832 | tf_op jit(solution)/shard_map/ppermute | solution.py:75
  16.2 2.1 %collective-permute-done.3.refs_4_ = bf16[32,3072]{1,0:T(8,128)(2,1)S(1)} collective-permute-done((bf16[32,3072]{1,0:T(8,128)(2,1)S(1)}, bf16[32,3072]{1,0:T(8,128)(2,1)S(1)}, u32[]{:S(2)}, u32[]{:S(2)}) %collective-permute-start.3) | collective-permute-done | bytes 196640 | tf_op jit(solution)/shard_map/ppermute | solution.py:75
  18.3 2.0 %collective-permute-start.5 = (bf16[32,3072]{1,0:T(8,128)(2,1)S(1)}, bf16[32,3072]{1,0:T(8,128)(2,1)S(1)}, u32[]{:S(2)}, u32[]{:S(2)}) collective-permute-start(bf16[32,3072]{1,0:T(8,128)(2,1)S(1)} %collective-permute-done.3.refs_4_), channel_id=1, source_target_pairs={{2,0},{4,2},{6,4},{7,6},{5,7},{3,5},{1,3},{0,1},{10,8},{12,10},{14... | collective-permute-start | bytes 589832 | tf_op jit(solution)/shard_map/ppermute | solution.py:75
  20.4 2.1 %collective-permute-done.11.arrived_ref.refs_4_ = bf16[32,3072]{1,0:T(8,128)(2,1)S(1)} collective-permute-done((bf16[32,3072]{1,0:T(8,128)(2,1)S(1)}, bf16[32,3072]{1,0:T(8,128)(2,1)S(1)}, u32[]{:S(2)}, u32[]{:S(2)}) %collective-permute-start.11) | collective-permute-done | bytes 196640 | tf_op jit(solution)/shard_map/ppermute | solution.py:75
  22.5 2.0 %collective-permute-start.13 = (bf16[32,3072]{1,0:T(8,128)(2,1)S(1)}, bf16[32,3072]{1,0:T(8,128)(2,1)S(1)}, u32[]{:S(2)}, u32[]{:S(2)}) collective-permute-start(bf16[32,3072]{1,0:T(8,128)(2,1)S(1)} %collective-permute-done.11.arrived_ref.refs_4_), channel_id=1, source_target_pairs={{2,0},{4,2},{6,4},{7,6},{5,7},{3,5},{1,3},{0,1},{10,8},{12,10},{14... | collective-permute-start | bytes 589832 | tf_op jit(solution)/shard_map/ppermute | solution.py:75
  24.7 2.0 %collective-permute-done.5.refs_6_ = bf16[32,3072]{1,0:T(8,128)(2,1)S(1)} collective-permute-done((bf16[32,3072]{1,0:T(8,128)(2,1)S(1)}, bf16[32,3072]{1,0:T(8,128)(2,1)S(1)}, u32[]{:S(2)}, u32[]{:S(2)}) %collective-permute-start.5) | collective-permute-done | bytes 196640 | tf_op jit(solution)/shard_map/ppermute | solution.py:75
  26.7 2.0 %collective-permute-start.7 = (bf16[32,1536]{1,0:T(8,128)(2,1)S(1)}, bf16[32,1536]{1,0:T(8,128)(2,1)S(1)}, u32[]{:S(2)}, u32[]{:S(2)}) collective-permute-start(bf16[32,1536]{1,0:T(8,128)(2,1)S(1)} %slice.25), channel_id=1, source_target_pairs={{2,0},{4,2},{6,4},{7,6},{5,7},{3,5},{1,3},{0,1},{10,8},{12,10},{14... | collective-permute-start | bytes 294920 | tf_op jit(solution)/shard_map/ppermute | solution.py:79
  28.9 2.0 %collective-permute-done.13.refs_6_ = bf16[32,3072]{1,0:T(8,128)(2,1)S(1)} collective-permute-done((bf16[32,3072]{1,0:T(8,128)(2,1)S(1)}, bf16[32,3072]{1,0:T(8,128)(2,1)S(1)}, u32[]{:S(2)}, u32[]{:S(2)}) %collective-permute-start.13) | collective-permute-done | bytes 196640 | tf_op jit(solution)/shard_map/ppermute | solution.py:75
  30.9 1.9 %collective-permute-start.15 = (bf16[32,1536]{1,0:T(8,128)(2,1)S(1)}, bf16[32,1536]{1,0:T(8,128)(2,1)S(1)}, u32[]{:S(2)}, u32[]{:S(2)}) collective-permute-start(bf16[32,1536]{1,0:T(8,128)(2,1)S(1)} %slice.27), channel_id=1, source_target_pairs={{2,0},{4,2},{6,4},{7,6},{5,7},{3,5},{1,3},{0,1},{10,8},{12,10},{14... | collective-permute-start | bytes 294920 | tf_op jit(solution)/shard_map/ppermute | solution.py:79
  33.1 0.8 %collective-permute-done.6.refs_7_ = bf16[32,1536]{1,0:T(8,128)(2,1)S(1)} collective-permute-done((bf16[32,1536]{1,0:T(8,128)(2,1)S(1)}, bf16[32,1536]{1,0:T(8,128)(2,1)S(1)}, u32[]{:S(2)}, u32[]{:S(2)}) %collective-permute-start.6) | collective-permute-done | bytes 98336 | tf_op jit(solution)/shard_map/ppermute | solution.py:78
  34.0 1.8 %first_pass.1 = (f32[2,256,512]{2,1,0:T(8,128)S(1)}, bf16[256,3072]{1,0:T(8,128)(2,1)S(1)}) custom-call(bf16[32,3072]{1,0:T(8,128)(2,1)S(1)} %get-tuple-element.62.refs_0_, bf16[32,3072]{1,0:T(8,128)(2,1)S(1)} %collective-permute-done.refs_1_, bf16[32,3072]{1,0:T(8,128)(2,1)S(1)} %collective-permute-done.1.refs_2_, ...), custom_call_target="tpu_custom_call" | custom-call | flops 1610612736 | bytes 6291456 | tf_op jit(solution)/shard_map/first_pass/pallas_call | solution.py:103
  35.8 1.8 %collective-permute-done.14.refs_7_ = bf16[32,1536]{1,0:T(8,128)(2,1)S(1)} collective-permute-done((bf16[32,1536]{1,0:T(8,128)(2,1)S(1)}, bf16[32,1536]{1,0:T(8,128)(2,1)S(1)}, u32[]{:S(2)}, u32[]{:S(2)}) %collective-permute-start.14) | collective-permute-done | bytes 98336 | tf_op jit(solution)/shard_map/ppermute | solution.py:78
  37.5 1.2 %keys_and_values.2 = (bf16[256,256]{1,0:T(8,128)(2,1)S(1)}, bf16[256,256]{1,0:T(8,128)(2,1)S(1)}, bf16[2,128,128]{2,1,0:T(8,128)(2,1)S(1)}, bf16[256,3072]{1,0:T(8,128)(2,1)S(1)}) custom-call(bf16[32,3072]{1,0:T(8,128)(2,1)S(1)} %get-tuple-element.61.refs_0_, bf16[32,3072]{1,0:T(8,128)(2,1)S(1)} %collective-permute-done.8.refs_1_, ...), custom_call_target="tpu_custom_call" | custom-call | flops 805306368 | bytes 3145728 | tf_op jit(solution)/shard_map/keys_and_values/pallas_call | solution.py:156
  38.9 1.2 %keys_and_values.3 = (bf16[256,256]{1,0:T(8,128)(2,1)S(1)}, bf16[256,256]{1,0:T(8,128)(2,1)S(1)}, bf16[2,128,128]{2,1,0:T(8,128)(2,1)S(1)}) custom-call(bf16[256,3072]{1,0:T(8,128)(2,1)S(1)} %get-tuple-element.35.refs_0_.second_ref, bf16[3,6144,512]{2,1,0:T(8,128)(2,1)S(1)} %bitcast.2, f32[2,256,512]{2,1,0:T(8,128)S(1)} %get-tuple-element.34.refs_10_.refs_2_), custom_call_target="tpu_custom_call" | custom-call | flops 5000000000 | bytes 3145728 | tf_op jit(solution)/shard_map/keys_and_values/pallas_call | solution.py:156
  40.1 0.5 collective-permute-start.18
  40.7 1.6 %collective-permute-start.17 = (bf16[2,128,128]{2,1,0:T(8,128)(2,1)S(1)}, bf16[2,128,128]{2,1,0:T(8,128)(2,1)S(1)}, u32[]{:S(2)}, u32[]{:S(2)}) collective-permute-start(bf16[2,128,128]{2,1,0:T(8,128)(2,1)S(1)} %add_states.2.refs_0_), channel_id=1, source_target_pairs={{0,16},{8,24},{16,0},{24,8},{1,17},{9,25},{17,1},{25,9},{2,18},{10... | collective-permute-start | bytes 196616 | tf_op jit(solution)/shard_map/ppermute | solution.py:374
  42.3 0.9 %collective-permute-start.19 = (bf16[2,128,128]{2,1,0:T(8,128)(2,1)S(1)}, bf16[2,128,128]{2,1,0:T(8,128)(2,1)S(1)}, u32[]{:S(2)}, u32[]{:S(2)}) collective-permute-start(bf16[2,128,128]{2,1,0:T(8,128)(2,1)S(1)} %add_states.3), channel_id=1, source_target_pairs={{0,16},{8,24},{16,0},{24,8},{1,17},{9,25},{17,1},{25,9},{2,18},{10... | collective-permute-start | bytes 196616 | tf_op jit(solution)/shard_map/ppermute | solution.py:374
  43.2 2.3 %queries_within.1 = (bf16[256,512]{1,0:T(8,128)(2,1)S(1)}, f32[256,512]{1,0:T(8,128)S(1)}) custom-call(bf16[256,3072]{1,0:T(8,128)(2,1)S(1)} %get-tuple-element.33.first_ref, bf16[256,3072]{1,0:T(8,128)(2,1)S(1)} %get-tuple-element.35.refs_0_.second_ref, bf16[3,6144,512]{2,1,0:T(8,128)(2,1)S(1)} %bitcast.2, bf16[256,256]{1,0:T(8,128)(2,1)S(1)} %get-tuple-element.36.refs_0_, ...), custom_call_target="tpu_custom_call" | custom-call | flops 1744830464 | bytes 6291456 | tf_op jit(solution)/shard_map/queries_within/pallas_call | solution.py:202
  45.5 1.1 %collective-permute-done.19.refs_3_ = bf16[2,128,128]{2,1,0:T(8,128)(2,1)S(1)} collective-permute-done((bf16[2,128,128]{2,1,0:T(8,128)(2,1)S(1)}, bf16[2,128,128]{2,1,0:T(8,128)(2,1)S(1)}, u32[]{:S(2)}, u32[]{:S(2)}) %collective-permute-start.19) | collective-permute-done | bytes 65568 | tf_op jit(solution)/shard_map/ppermute | solution.py:374
  46.7 1.6 %attend_and_project.1 = (bf16[256,512]{1,0:T(8,128)(2,1)S(1)}, bf16[32,3072]{1,0:T(8,128)(2,1)S(1)}, bf16[32,3072]{1,0:T(8,128)(2,1)S(1)}) custom-call(bf16[256,512]{1,0:T(8,128)(2,1)S(1)} %get-tuple-element.40.q_ref, f32[256,512]{1,0:T(8,128)S(1)} %get-tuple-element.41.within_ref, f32[4,128,128]{2,1,0:T(8,128)S(1)} %copy-done, f32[1,512]{1,0:T(1,128)S(1)} %bitcast.5, ...), custom_call_target="tpu_custom_call" | custom-call | flops 1610612736 | bytes 6291456 | tf_op jit(solution)/shard_map/attend_and_project/pallas_call | solution.py:250
  48.2 0.6 collective-permute-start.26
  48.8 1.5 %collective-permute-start.30 = (bf16[32,3072]{1,0:T(8,128)(2,1)S(1)}, bf16[32,3072]{1,0:T(8,128)(2,1)S(1)}, u32[]{:S(2)}, u32[]{:S(2)}) collective-permute-start(bf16[32,3072]{1,0:T(8,128)(2,1)S(1)} %get-tuple-element.60), channel_id=1, source_target_pairs={{2,0},{4,2},{6,4},{7,6},{5,7},{3,5},{1,3},{0,1},{10,8},{12,10},{14... | collective-permute-start | bytes 589832 | tf_op jit(solution)/shard_map/ppermute | solution.py:338
  50.3 1.6 %project_rest.1 = (bf16[32,3072]{1,0:T(8,128)(2,1)S(1)}, bf16[32,3072]{1,0:T(8,128)(2,1)S(1)}, bf16[32,3072]{1,0:T(8,128)(2,1)S(1)}, bf16[32,3072]{1,0:T(8,128)(...) custom-call(bf16[256,512]{1,0:T(8,128)(2,1)S(1)} %get-tuple-element., ...), custom_call_target="tpu_custom_call" | custom-call | flops 5000000000 | bytes 6291456 | tf_op jit(solution)/shard_map/project_rest/pallas_call | solution.py:269
  51.9 1.6 %collective-permute-start.20 = (bf16[32,3072]{1,0:T(8,128)(2,1)S(1)}, bf16[32,3072]{1,0:T(8,128)(2,1)S(1)}, u32[]{:S(2)}, u32[]{:S(2)}) collective-permute-start(bf16[32,3072]{1,0:T(8,128)(2,1)S(1)} %get-tuple-element.49), channel_id=1, source_target_pairs={{2,0},{4,2},{6,4},{7,6},{5,7},{3,5},{1,3},{0,1},{10,8},{12,10},{14... | collective-permute-start | bytes 589832 | tf_op jit(solution)/shard_map/ppermute | solution.py:338
  54.0 0.6 collective-permute-start.27
  54.6 1.4 %collective-permute-done.30.got_ref = bf16[32,3072]{1,0:T(8,128)(2,1)S(1)} collective-permute-done((bf16[32,3072]{1,0:T(8,128)(2,1)S(1)}, bf16[32,3072]{1,0:T(8,128)(2,1)S(1)}, u32[]{:S(2)}, u32[]{:S(2)}) %collective-permute-start.30) | collective-permute-done | bytes 196640 | tf_op jit(solution)/shard_map/ppermute | solution.py:338
  56.1 1.5 %collective-permute-start.31 = (bf16[32,3072]{1,0:T(8,128)(2,1)S(1)}, bf16[32,3072]{1,0:T(8,128)(2,1)S(1)}, u32[]{:S(2)}, u32[]{:S(2)}) collective-permute-start(bf16[32,3072]{1,0:T(8,128)(2,1)S(1)} %add_step.17), channel_id=1, source_target_pairs={{2,0},{4,2},{6,4},{7,6},{5,7},{3,5},{1,3},{0,1},{10,8},{12,10},{14... | collective-permute-start | bytes 589832 | tf_op jit(solution)/shard_map/ppermute | solution.py:338
  57.5 2.7 %collective-permute-done.20.got_ref = bf16[32,3072]{1,0:T(8,128)(2,1)S(1)} collective-permute-done((bf16[32,3072]{1,0:T(8,128)(2,1)S(1)}, bf16[32,3072]{1,0:T(8,128)(2,1)S(1)}, u32[]{:S(2)}, u32[]{:S(2)}) %collective-permute-start.20) | collective-permute-done | bytes 196640 | tf_op jit(solution)/shard_map/ppermute | solution.py:338
  60.3 1.5 %collective-permute-start.21 = (bf16[32,3072]{1,0:T(8,128)(2,1)S(1)}, bf16[32,3072]{1,0:T(8,128)(2,1)S(1)}, u32[]{:S(2)}, u32[]{:S(2)}) collective-permute-start(bf16[32,3072]{1,0:T(8,128)(2,1)S(1)} %add_step.10), channel_id=1, source_target_pairs={{2,0},{4,2},{6,4},{7,6},{5,7},{3,5},{1,3},{0,1},{10,8},{12,10},{14... | collective-permute-start | bytes 589832 | tf_op jit(solution)/shard_map/ppermute | solution.py:338
  61.8 0.8 %collective-permute-start.24 = (bf16[32,3072]{1,0:T(8,128)(2,1)S(1)}, bf16[32,3072]{1,0:T(8,128)(2,1)S(1)}, u32[]{:S(2)}, u32[]{:S(2)}) collective-permute-start(bf16[32,3072]{1,0:T(8,128)(2,1)S(1)} %add_step.12), channel_id=1, source_target_pairs={{0,2},{2,4},{4,6},{6,7},{7,5},{5,3},{3,1},{1,0},{8,10},{10,12},{12... | collective-permute-start | bytes 589832 | tf_op jit(solution)/shard_map/ppermute | solution.py:338
  62.6 1.3 %collective-permute-done.27.got_ref = bf16[32,3072]{1,0:T(8,128)(2,1)S(1)} collective-permute-done((bf16[32,3072]{1,0:T(8,128)(2,1)S(1)}, bf16[32,3072]{1,0:T(8,128)(2,1)S(1)}, u32[]{:S(2)}, u32[]{:S(2)}) %collective-permute-start.27) | collective-permute-done | bytes 196640 | tf_op jit(solution)/shard_map/ppermute | solution.py:338
  64.0 0.8 collective-permute-start.28
  64.8 1.3 %collective-permute-start.32 = (bf16[32,3072]{1,0:T(8,128)(2,1)S(1)}, bf16[32,3072]{1,0:T(8,128)(2,1)S(1)}, u32[]{:S(2)}, u32[]{:S(2)}) collective-permute-start(bf16[32,3072]{1,0:T(8,128)(2,1)S(1)} %add_step.18), channel_id=1, source_target_pairs={{2,0},{4,2},{6,4},{7,6},{5,7},{3,5},{1,3},{0,1},{10,8},{12,10},{14... | collective-permute-start | bytes 589832 | tf_op jit(solution)/shard_map/ppermute | solution.py:338
  66.1 2.5 %collective-permute-done.21.got_ref = bf16[32,3072]{1,0:T(8,128)(2,1)S(1)} collective-permute-done((bf16[32,3072]{1,0:T(8,128)(2,1)S(1)}, bf16[32,3072]{1,0:T(8,128)(2,1)S(1)}, u32[]{:S(2)}, u32[]{:S(2)}) %collective-permute-start.21) | collective-permute-done | bytes 196640 | tf_op jit(solution)/shard_map/ppermute | solution.py:338
  68.7 1.5 %collective-permute-start.22 = (bf16[32,3072]{1,0:T(8,128)(2,1)S(1)}, bf16[32,3072]{1,0:T(8,128)(2,1)S(1)}, u32[]{:S(2)}, u32[]{:S(2)}) collective-permute-start(bf16[32,3072]{1,0:T(8,128)(2,1)S(1)} %add_step.11), channel_id=1, source_target_pairs={{2,0},{4,2},{6,4},{7,6},{5,7},{3,5},{1,3},{0,1},{10,8},{12,10},{14... | collective-permute-start | bytes 589832 | tf_op jit(solution)/shard_map/ppermute | solution.py:338
  70.2 0.8 %collective-permute-start.25 = (bf16[32,3072]{1,0:T(8,128)(2,1)S(1)}, bf16[32,3072]{1,0:T(8,128)(2,1)S(1)}, u32[]{:S(2)}, u32[]{:S(2)}) collective-permute-start(bf16[32,3072]{1,0:T(8,128)(2,1)S(1)} %add_step.13), channel_id=1, source_target_pairs={{0,2},{2,4},{4,6},{6,7},{7,5},{5,3},{3,1},{1,0},{8,10},{10,12},{12... | collective-permute-start | bytes 589832 | tf_op jit(solution)/shard_map/ppermute | solution.py:338
  71.1 1.3 %collective-permute-done.28.got_ref = bf16[32,3072]{1,0:T(8,128)(2,1)S(1)} collective-permute-done((bf16[32,3072]{1,0:T(8,128)(2,1)S(1)}, bf16[32,3072]{1,0:T(8,128)(2,1)S(1)}, u32[]{:S(2)}, u32[]{:S(2)}) %collective-permute-start.28) | collective-permute-done | bytes 196640 | tf_op jit(solution)/shard_map/ppermute | solution.py:338
  72.4 0.8 collective-permute-start.29
  73.2 1.3 %collective-permute-start.33 = (bf16[32,3072]{1,0:T(8,128)(2,1)S(1)}, bf16[32,3072]{1,0:T(8,128)(2,1)S(1)}, u32[]{:S(2)}, u32[]{:S(2)}) collective-permute-start(bf16[32,3072]{1,0:T(8,128)(2,1)S(1)} %add_step.19), channel_id=1, source_target_pairs={{2,0},{4,2},{6,4},{7,6},{5,7},{3,5},{1,3},{0,1},{10,8},{12,10},{14... | collective-permute-start | bytes 589832 | tf_op jit(solution)/shard_map/ppermute | solution.py:338
  74.6 2.5 %collective-permute-done.22.got_first = bf16[32,3072]{1,0:T(8,128)(2,1)S(1)} collective-permute-done((bf16[32,3072]{1,0:T(8,128)(2,1)S(1)}, bf16[32,3072]{1,0:T(8,128)(2,1)S(1)}, u32[]{:S(2)}, u32[]{:S(2)}) %collective-permute-start.22) | collective-permute-done | bytes 196640 | tf_op jit(solution)/shard_map/ppermute | solution.py:338
  77.5 2.0 %collective-permute-done.29.first = bf16[32,3072]{1,0:T(8,128)(2,1)S(1)} collective-permute-done((bf16[32,3072]{1,0:T(8,128)(2,1)S(1)}, bf16[32,3072]{1,0:T(8,128)(2,1)S(1)}, u32[]{:S(2)}, u32[]{:S(2)}) %collective-permute-start.29) | collective-permute-done | bytes 196640 | tf_op jit(solution)/shard_map/ppermute | solution.py:338
  79.7 0.8 %finish.1 = bf16[32,6144]{1,0:T(8,128)(2,1)} custom-call(f32[2,32,3072]{2,1,0:T(8,128)S(1)} %add_own.1.gathered_ref, bf16[32,3072]{1,0:T(8,128)(2,1)S(1)} %collective-permute-done.29.first, bf16[32,3072]{1,0:T(8,128)(2,1)S(1)} %collective-permute-done.33.second), custom_call_target="tpu_custom_call" | custom-call | bytes 393216 | tf_op jit(solution)/shard_map/finish/pallas_call | solution.py:320
  (67 shorter events, 3.1 us)
Async XLA Ops:
  1.1 8.8 %collective-permute-start.1 = (bf16[32,3072]{1,0:T(8,128)(2,1)S(1)}, bf16[32,3072]{1,0:T(8,128)(2,1)S(1)}, u32[]{:S(2)}, u32[]{:S(2)}) collective-permute-start(bf16[32,3072]{1,0:T(8,128)(2,1)S(1)} %get-tuple-element.62.refs_0_), channel_id=1, source_target_pairs={{2,0},{4,2},{6,4},{7,6},{5,7},{3,5},{1,3},{0,1},{10,8},{12,10},{14... | collective-permute-start | bytes 589832 | tf_op jit(solution)/shard_map/ppermute | solution.py:75
  4.0 7.8 %collective-permute-start = (bf16[32,3072]{1,0:T(8,128)(2,1)S(1)}, bf16[32,3072]{1,0:T(8,128)(2,1)S(1)}, u32[]{:S(2)}, u32[]{:S(2)}) collective-permute-start(bf16[32,3072]{1,0:T(8,128)(2,1)S(1)} %get-tuple-element.62.refs_0_), channel_id=1, source_target_pairs={{0,2},{2,4},{4,6},{6,7},{7,5},{5,3},{3,1},{1,0},{8,10},{10,12},{12... | collective-permute-start | bytes 589832 | tf_op jit(solution)/shard_map/ppermute | solution.py:74
  4.2 9.9 %collective-permute-start.10 = (bf16[32,3072]{1,0:T(8,128)(2,1)S(1)}, bf16[32,3072]{1,0:T(8,128)(2,1)S(1)}, u32[]{:S(2)}, u32[]{:S(2)}) collective-permute-start(bf16[32,3072]{1,0:T(8,128)(2,1)S(1)} %get-tuple-element.61.refs_0_), channel_id=1, source_target_pairs={{2,0},{4,2},{6,4},{7,6},{5,7},{3,5},{1,3},{0,1},{10,8},{12,10},{14... | collective-permute-start | bytes 589832 | tf_op jit(solution)/shard_map/ppermute | solution.py:75
  6.1 10.0 %collective-permute-start.8 = (bf16[32,3072]{1,0:T(8,128)(2,1)S(1)}, bf16[32,3072]{1,0:T(8,128)(2,1)S(1)}, u32[]{:S(2)}, u32[]{:S(2)}) collective-permute-start(bf16[32,3072]{1,0:T(8,128)(2,1)S(1)} %get-tuple-element.61.refs_0_), channel_id=1, source_target_pairs={{0,2},{2,4},{4,6},{6,7},{7,5},{5,3},{3,1},{1,0},{8,10},{10,12},{12... | collective-permute-start | bytes 589832 | tf_op jit(solution)/shard_map/ppermute | solution.py:74
  9.9 8.4 %collective-permute-start.3 = (bf16[32,3072]{1,0:T(8,128)(2,1)S(1)}, bf16[32,3072]{1,0:T(8,128)(2,1)S(1)}, u32[]{:S(2)}, u32[]{:S(2)}) collective-permute-start(bf16[32,3072]{1,0:T(8,128)(2,1)S(1)} %collective-permute-done.1.refs_2_), channel_id=1, source_target_pairs={{2,0},{4,2},{6,4},{7,6},{5,7},{3,5},{1,3},{0,1},{10,8},{12,10},{14... | collective-permute-start | bytes 589832 | tf_op jit(solution)/shard_map/ppermute | solution.py:75
  11.9 8.4 %collective-permute-start.2 = (bf16[32,3072]{1,0:T(8,128)(2,1)S(1)}, bf16[32,3072]{1,0:T(8,128)(2,1)S(1)}, u32[]{:S(2)}, u32[]{:S(2)}) collective-permute-start(bf16[32,3072]{1,0:T(8,128)(2,1)S(1)} %collective-permute-done.refs_1_), channel_id=1, source_target_pairs={{0,2},{2,4},{4,6},{6,7},{7,5},{5,3},{3,1},{1,0},{8,10},{10,12},{12... | collective-permute-start | bytes 589832 | tf_op jit(solution)/shard_map/ppermute | solution.py:74
  14.1 8.4 %collective-permute-start.11 = (bf16[32,3072]{1,0:T(8,128)(2,1)S(1)}, bf16[32,3072]{1,0:T(8,128)(2,1)S(1)}, u32[]{:S(2)}, u32[]{:S(2)}) collective-permute-start(bf16[32,3072]{1,0:T(8,128)(2,1)S(1)} %collective-permute-done.10.refs_2_), channel_id=1, source_target_pairs={{2,0},{4,2},{6,4},{7,6},{5,7},{3,5},{1,3},{0,1},{10,8},{12,10},{14... | collective-permute-start | bytes 589832 | tf_op jit(solution)/shard_map/ppermute | solution.py:75
  16.1 8.5 %collective-permute-start.9 = (bf16[32,3072]{1,0:T(8,128)(2,1)S(1)}, bf16[32,3072]{1,0:T(8,128)(2,1)S(1)}, u32[]{:S(2)}, u32[]{:S(2)}) collective-permute-start(bf16[32,3072]{1,0:T(8,128)(2,1)S(1)} %collective-permute-done.8.refs_1_), channel_id=1, source_target_pairs={{0,2},{2,4},{4,6},{6,7},{7,5},{5,3},{3,1},{1,0},{8,10},{10,12},{12... | collective-permute-start | bytes 589832 | tf_op jit(solution)/shard_map/ppermute | solution.py:74
  18.3 8.4 %collective-permute-start.5 = (bf16[32,3072]{1,0:T(8,128)(2,1)S(1)}, bf16[32,3072]{1,0:T(8,128)(2,1)S(1)}, u32[]{:S(2)}, u32[]{:S(2)}) collective-permute-start(bf16[32,3072]{1,0:T(8,128)(2,1)S(1)} %collective-permute-done.3.refs_4_), channel_id=1, source_target_pairs={{2,0},{4,2},{6,4},{7,6},{5,7},{3,5},{1,3},{0,1},{10,8},{12,10},{14... | collective-permute-start | bytes 589832 | tf_op jit(solution)/shard_map/ppermute | solution.py:75
  20.3 8.5 %collective-permute-start.4 = (bf16[32,3072]{1,0:T(8,128)(2,1)S(1)}, bf16[32,3072]{1,0:T(8,128)(2,1)S(1)}, u32[]{:S(2)}, u32[]{:S(2)}) collective-permute-start(bf16[32,3072]{1,0:T(8,128)(2,1)S(1)} %collective-permute-done.2.refs_3_), channel_id=1, source_target_pairs={{0,2},{2,4},{4,6},{6,7},{7,5},{5,3},{3,1},{1,0},{8,10},{10,12},{12... | collective-permute-start | bytes 589832 | tf_op jit(solution)/shard_map/ppermute | solution.py:74
  22.5 11.4 %slice-start = ((s8[18874368]{0:T(1024)(128)(4,1)}), s8[4194304]{0:T(1024)(128)(4,1)S(1)}, s32[]{:S(2)}) async-start(s8[18874368]{0:T(1024)(128)(4,1)} %bitcast.1), calls=%async_computation | async-start | bytes 8388608
  22.5 11.4 %slice-start.1 = ((s8[18874368]{0:T(1024)(128)(4,1)}), s8[4194304]{0:T(1024)(128)(4,1)S(1)}, s32[]{:S(2)}) async-start(s8[18874368]{0:T(1024)(128)(4,1)} %bitcast.1), calls=%async_computation.1 | async-start | bytes 8388608
  22.5 11.4 %slice-start.2 = ((s8[18874368]{0:T(1024)(128)(4,1)}), s8[4194304]{0:T(1024)(128)(4,1)S(1)}, s32[]{:S(2)}) async-start(s8[18874368]{0:T(1024)(128)(4,1)} %bitcast.1), calls=%async_computation.2 | async-start | bytes 8388608
  22.5 8.4 %collective-permute-start.13 = (bf16[32,3072]{1,0:T(8,128)(2,1)S(1)}, bf16[32,3072]{1,0:T(8,128)(2,1)S(1)}, u32[]{:S(2)}, u32[]{:S(2)}) collective-permute-start(bf16[32,3072]{1,0:T(8,128)(2,1)S(1)} %collective-permute-done.11.arrived_ref.refs_4_), channel_id=1, source_target_pairs={{2,0},{4,2},{6,4},{7,6},{5,7},{3,5},{1,3},{0,1},{10,8},{12,10},{14... | collective-permute-start | bytes 589832 | tf_op jit(solution)/shard_map/ppermute | solution.py:75
  24.5 8.3 %collective-permute-start.12 = (bf16[32,3072]{1,0:T(8,128)(2,1)S(1)}, bf16[32,3072]{1,0:T(8,128)(2,1)S(1)}, u32[]{:S(2)}, u32[]{:S(2)}) collective-permute-start(bf16[32,3072]{1,0:T(8,128)(2,1)S(1)} %collective-permute-done.9.arrived_ref.refs_3_), channel_id=1, source_target_pairs={{0,2},{2,4},{4,6},{6,7},{7,5},{5,3},{3,1},{1,0},{8,10},{10,12},{12... | collective-permute-start | bytes 589832 | tf_op jit(solution)/shard_map/ppermute | solution.py:74
  26.7 6.4 %collective-permute-start.7 = (bf16[32,1536]{1,0:T(8,128)(2,1)S(1)}, bf16[32,1536]{1,0:T(8,128)(2,1)S(1)}, u32[]{:S(2)}, u32[]{:S(2)}) collective-permute-start(bf16[32,1536]{1,0:T(8,128)(2,1)S(1)} %slice.25), channel_id=1, source_target_pairs={{2,0},{4,2},{6,4},{7,6},{5,7},{3,5},{1,3},{0,1},{10,8},{12,10},{14... | collective-permute-start | bytes 294920 | tf_op jit(solution)/shard_map/ppermute | solution.py:79
  28.8 5.2 %slice-start.3 = ((s8[18874368]{0:T(1024)(128)(4,1)}), s8[4194304]{0:T(1024)(128)(4,1)S(1)}, s32[]{:S(2)}) async-start(s8[18874368]{0:T(1024)(128)(4,1)} %bitcast.1), calls=%async_computation.3 | async-start | bytes 8388608
  28.8 5.2 %slice-start.4 = ((s8[18874368]{0:T(1024)(128)(4,1)}), s8[2097152]{0:T(1024)(128)(4,1)S(1)}, s32[]{:S(2)}) async-start(s8[18874368]{0:T(1024)(128)(4,1)} %bitcast.1), calls=%async_computation.4 | async-start | bytes 4194304
  28.8 5.1 %collective-permute-start.6 = (bf16[32,1536]{1,0:T(8,128)(2,1)S(1)}, bf16[32,1536]{1,0:T(8,128)(2,1)S(1)}, u32[]{:S(2)}, u32[]{:S(2)}) collective-permute-start(bf16[32,1536]{1,0:T(8,128)(2,1)S(1)} %slice.24), channel_id=1, source_target_pairs={{0,2},{2,4},{4,6},{6,7},{7,5},{5,3},{3,1},{1,0},{8,10},{10,12},{12... | collective-permute-start | bytes 294920 | tf_op jit(solution)/shard_map/ppermute | solution.py:78
  30.9 4.8 %collective-permute-start.15 = (bf16[32,1536]{1,0:T(8,128)(2,1)S(1)}, bf16[32,1536]{1,0:T(8,128)(2,1)S(1)}, u32[]{:S(2)}, u32[]{:S(2)}) collective-permute-start(bf16[32,1536]{1,0:T(8,128)(2,1)S(1)} %slice.27), channel_id=1, source_target_pairs={{2,0},{4,2},{6,4},{7,6},{5,7},{3,5},{1,3},{0,1},{10,8},{12,10},{14... | collective-permute-start | bytes 294920 | tf_op jit(solution)/shard_map/ppermute | solution.py:79
  32.9 4.7 %collective-permute-start.14 = (bf16[32,1536]{1,0:T(8,128)(2,1)S(1)}, bf16[32,1536]{1,0:T(8,128)(2,1)S(1)}, u32[]{:S(2)}, u32[]{:S(2)}) collective-permute-start(bf16[32,1536]{1,0:T(8,128)(2,1)S(1)} %slice.26), channel_id=1, source_target_pairs={{0,2},{2,4},{4,6},{6,7},{7,5},{5,3},{3,1},{1,0},{8,10},{10,12},{12... | collective-permute-start | bytes 294920 | tf_op jit(solution)/shard_map/ppermute | solution.py:78
  38.8 1.9 %collective-permute-start.16 = (bf16[2,128,128]{2,1,0:T(8,128)(2,1)S(1)}, bf16[2,128,128]{2,1,0:T(8,128)(2,1)S(1)}, u32[]{:S(2)}, u32[]{:S(2)}) collective-permute-start(bf16[2,128,128]{2,1,0:T(8,128)(2,1)S(1)} %get-tuple-element.42.one_ref), channel_id=1, source_target_pairs={{0,8},{8,0},{16,24},{24,16},{1,9},{9,1},{17,25},{25,17},{2,10},{10... | collective-permute-start | bytes 196616 | tf_op jit(solution)/shard_map/ppermute | solution.py:374
  38.9 7.8 %slice-start.5 = ((s8[6291456]{0:T(1024)(128)(4,1)}), s8[4194304]{0:T(1024)(128)(4,1)S(1)}, s32[]{:S(2)}) async-start(s8[6291456]{0:T(1024)(128)(4,1)} %bitcast.3), calls=%async_computation.5 | async-start | bytes 8388608
  40.1 2.2 %collective-permute-start.18 = (bf16[2,128,128]{2,1,0:T(8,128)(2,1)S(1)}, bf16[2,128,128]{2,1,0:T(8,128)(2,1)S(1)}, u32[]{:S(2)}, u32[]{:S(2)}) collective-permute-start(bf16[2,128,128]{2,1,0:T(8,128)(2,1)S(1)} %get-tuple-element.43.one_ref), channel_id=1, source_target_pairs={{0,8},{8,0},{16,24},{24,16},{1,9},{9,1},{17,25},{25,17},{2,10},{10... | collective-permute-start | bytes 196616 | tf_op jit(solution)/shard_map/ppermute | solution.py:374
  40.7 5.9 %collective-permute-start.17 = (bf16[2,128,128]{2,1,0:T(8,128)(2,1)S(1)}, bf16[2,128,128]{2,1,0:T(8,128)(2,1)S(1)}, u32[]{:S(2)}, u32[]{:S(2)}) collective-permute-start(bf16[2,128,128]{2,1,0:T(8,128)(2,1)S(1)} %add_states.2.refs_0_), channel_id=1, source_target_pairs={{0,16},{8,24},{16,0},{24,8},{1,17},{9,25},{17,1},{25,9},{2,18},{10... | collective-permute-start | bytes 196616 | tf_op jit(solution)/shard_map/ppermute | solution.py:374
  42.3 4.3 %collective-permute-start.19 = (bf16[2,128,128]{2,1,0:T(8,128)(2,1)S(1)}, bf16[2,128,128]{2,1,0:T(8,128)(2,1)S(1)}, u32[]{:S(2)}, u32[]{:S(2)}) collective-permute-start(bf16[2,128,128]{2,1,0:T(8,128)(2,1)S(1)} %add_states.3), channel_id=1, source_target_pairs={{0,16},{8,24},{16,0},{24,8},{1,17},{9,25},{17,1},{25,9},{2,18},{10... | collective-permute-start | bytes 196616 | tf_op jit(solution)/shard_map/ppermute | solution.py:374
  43.2 3.5 %slice-start.6 = ((s8[6291456]{0:T(1024)(128)(4,1)}), s8[2097152]{0:T(1024)(128)(4,1)S(1)}, s32[]{:S(2)}) async-start(s8[6291456]{0:T(1024)(128)(4,1)} %bitcast.3), calls=%async_computation.6 | async-start | bytes 4194304
  43.2 3.5 %copy-start = (f32[4,128,128]{2,1,0:T(8,128)S(1)}, f32[4,128,128]{2,1,0:T(8,128)}, u32[]{:S(2)}) copy-start(f32[4,128,128]{2,1,0:T(8,128)} %initial_ref.1) | copy-start | bytes 786436
  43.2 3.5 %copy-start.1 = (f32[512]{0:T(512)S(1)}, f32[512]{0:T(512)}, u32[]{:S(2)}) copy-start(f32[512]{0:T(512)} %param.8) | copy-start | bytes 6148
  48.2 5.8 %collective-permute-start.26 = (bf16[32,3072]{1,0:T(8,128)(2,1)S(1)}, bf16[32,3072]{1,0:T(8,128)(2,1)S(1)}, u32[]{:S(2)}, u32[]{:S(2)}) collective-permute-start(bf16[32,3072]{1,0:T(8,128)(2,1)S(1)} %get-tuple-element.56), channel_id=1, source_target_pairs={{0,2},{2,4},{4,6},{6,7},{7,5},{5,3},{3,1},{1,0},{8,10},{10,12},{12... | collective-permute-start | bytes 589832 | tf_op jit(solution)/shard_map/ppermute | solution.py:338
  48.8 7.3 %collective-permute-start.30 = (bf16[32,3072]{1,0:T(8,128)(2,1)S(1)}, bf16[32,3072]{1,0:T(8,128)(2,1)S(1)}, u32[]{:S(2)}, u32[]{:S(2)}) collective-permute-start(bf16[32,3072]{1,0:T(8,128)(2,1)S(1)} %get-tuple-element.60), channel_id=1, source_target_pairs={{2,0},{4,2},{6,4},{7,6},{5,7},{3,5},{1,3},{0,1},{10,8},{12,10},{14... | collective-permute-start | bytes 589832 | tf_op jit(solution)/shard_map/ppermute | solution.py:338
  51.9 8.4 %collective-permute-start.20 = (bf16[32,3072]{1,0:T(8,128)(2,1)S(1)}, bf16[32,3072]{1,0:T(8,128)(2,1)S(1)}, u32[]{:S(2)}, u32[]{:S(2)}) collective-permute-start(bf16[32,3072]{1,0:T(8,128)(2,1)S(1)} %get-tuple-element.49), channel_id=1, source_target_pairs={{2,0},{4,2},{6,4},{7,6},{5,7},{3,5},{1,3},{0,1},{10,8},{12,10},{14... | collective-permute-start | bytes 589832 | tf_op jit(solution)/shard_map/ppermute | solution.py:338
  53.5 8.3 %collective-permute-start.23 = (bf16[32,3072]{1,0:T(8,128)(2,1)S(1)}, bf16[32,3072]{1,0:T(8,128)(2,1)S(1)}, u32[]{:S(2)}, u32[]{:S(2)}) collective-permute-start(bf16[32,3072]{1,0:T(8,128)(2,1)S(1)} %get-tuple-element.52), channel_id=1, source_target_pairs={{0,2},{2,4},{4,6},{6,7},{7,5},{5,3},{3,1},{1,0},{8,10},{10,12},{12... | collective-permute-start | bytes 589832 | tf_op jit(solution)/shard_map/ppermute | solution.py:338
  54.0 9.9 %collective-permute-start.27 = (bf16[32,3072]{1,0:T(8,128)(2,1)S(1)}, bf16[32,3072]{1,0:T(8,128)(2,1)S(1)}, u32[]{:S(2)}, u32[]{:S(2)}) collective-permute-start(bf16[32,3072]{1,0:T(8,128)(2,1)S(1)} %add_step.14), channel_id=1, source_target_pairs={{0,2},{2,4},{4,6},{6,7},{7,5},{5,3},{3,1},{1,0},{8,10},{10,12},{12... | collective-permute-start | bytes 589832 | tf_op jit(solution)/shard_map/ppermute | solution.py:338
  56.1 8.7 %collective-permute-start.31 = (bf16[32,3072]{1,0:T(8,128)(2,1)S(1)}, bf16[32,3072]{1,0:T(8,128)(2,1)S(1)}, u32[]{:S(2)}, u32[]{:S(2)}) collective-permute-start(bf16[32,3072]{1,0:T(8,128)(2,1)S(1)} %add_step.17), channel_id=1, source_target_pairs={{2,0},{4,2},{6,4},{7,6},{5,7},{3,5},{1,3},{0,1},{10,8},{12,10},{14... | collective-permute-start | bytes 589832 | tf_op jit(solution)/shard_map/ppermute | solution.py:338
  60.3 8.4 %collective-permute-start.21 = (bf16[32,3072]{1,0:T(8,128)(2,1)S(1)}, bf16[32,3072]{1,0:T(8,128)(2,1)S(1)}, u32[]{:S(2)}, u32[]{:S(2)}) collective-permute-start(bf16[32,3072]{1,0:T(8,128)(2,1)S(1)} %add_step.10), channel_id=1, source_target_pairs={{2,0},{4,2},{6,4},{7,6},{5,7},{3,5},{1,3},{0,1},{10,8},{12,10},{14... | collective-permute-start | bytes 589832 | tf_op jit(solution)/shard_map/ppermute | solution.py:338
  61.8 8.4 %collective-permute-start.24 = (bf16[32,3072]{1,0:T(8,128)(2,1)S(1)}, bf16[32,3072]{1,0:T(8,128)(2,1)S(1)}, u32[]{:S(2)}, u32[]{:S(2)}) collective-permute-start(bf16[32,3072]{1,0:T(8,128)(2,1)S(1)} %add_step.12), channel_id=1, source_target_pairs={{0,2},{2,4},{4,6},{6,7},{7,5},{5,3},{3,1},{1,0},{8,10},{10,12},{12... | collective-permute-start | bytes 589832 | tf_op jit(solution)/shard_map/ppermute | solution.py:338
  64.0 8.4 %collective-permute-start.28 = (bf16[32,3072]{1,0:T(8,128)(2,1)S(1)}, bf16[32,3072]{1,0:T(8,128)(2,1)S(1)}, u32[]{:S(2)}, u32[]{:S(2)}) collective-permute-start(bf16[32,3072]{1,0:T(8,128)(2,1)S(1)} %add_step.15), channel_id=1, source_target_pairs={{0,2},{2,4},{4,6},{6,7},{7,5},{5,3},{3,1},{1,0},{8,10},{10,12},{12... | collective-permute-start | bytes 589832 | tf_op jit(solution)/shard_map/ppermute | solution.py:338
  64.8 8.4 %collective-permute-start.32 = (bf16[32,3072]{1,0:T(8,128)(2,1)S(1)}, bf16[32,3072]{1,0:T(8,128)(2,1)S(1)}, u32[]{:S(2)}, u32[]{:S(2)}) collective-permute-start(bf16[32,3072]{1,0:T(8,128)(2,1)S(1)} %add_step.18), channel_id=1, source_target_pairs={{2,0},{4,2},{6,4},{7,6},{5,7},{3,5},{1,3},{0,1},{10,8},{12,10},{14... | collective-permute-start | bytes 589832 | tf_op jit(solution)/shard_map/ppermute | solution.py:338
  68.7 8.4 %collective-permute-start.22 = (bf16[32,3072]{1,0:T(8,128)(2,1)S(1)}, bf16[32,3072]{1,0:T(8,128)(2,1)S(1)}, u32[]{:S(2)}, u32[]{:S(2)}) collective-permute-start(bf16[32,3072]{1,0:T(8,128)(2,1)S(1)} %add_step.11), channel_id=1, source_target_pairs={{2,0},{4,2},{6,4},{7,6},{5,7},{3,5},{1,3},{0,1},{10,8},{12,10},{14... | collective-permute-start | bytes 589832 | tf_op jit(solution)/shard_map/ppermute | solution.py:338
  70.2 7.2 %collective-permute-start.25 = (bf16[32,3072]{1,0:T(8,128)(2,1)S(1)}, bf16[32,3072]{1,0:T(8,128)(2,1)S(1)}, u32[]{:S(2)}, u32[]{:S(2)}) collective-permute-start(bf16[32,3072]{1,0:T(8,128)(2,1)S(1)} %add_step.13), channel_id=1, source_target_pairs={{0,2},{2,4},{4,6},{6,7},{7,5},{5,3},{3,1},{1,0},{8,10},{10,12},{12... | collective-permute-start | bytes 589832 | tf_op jit(solution)/shard_map/ppermute | solution.py:338
  72.4 7.1 %collective-permute-start.29 = (bf16[32,3072]{1,0:T(8,128)(2,1)S(1)}, bf16[32,3072]{1,0:T(8,128)(2,1)S(1)}, u32[]{:S(2)}, u32[]{:S(2)}) collective-permute-start(bf16[32,3072]{1,0:T(8,128)(2,1)S(1)} %add_step.16), channel_id=1, source_target_pairs={{0,2},{2,4},{4,6},{6,7},{7,5},{5,3},{3,1},{1,0},{8,10},{10,12},{12... | collective-permute-start | bytes 589832 | tf_op jit(solution)/shard_map/ppermute | solution.py:338
  73.2 6.5 %collective-permute-start.33 = (bf16[32,3072]{1,0:T(8,128)(2,1)S(1)}, bf16[32,3072]{1,0:T(8,128)(2,1)S(1)}, u32[]{:S(2)}, u32[]{:S(2)}) collective-permute-start(bf16[32,3072]{1,0:T(8,128)(2,1)S(1)} %add_step.19), channel_id=1, source_target_pairs={{2,0},{4,2},{6,4},{7,6},{5,7},{3,5},{1,3},{0,1},{10,8},{12,10},{14... | collective-permute-start | bytes 589832 | tf_op jit(solution)/shard_map/ppermute | solution.py:338

commit v8 on v7

--- a/solution.py
+++ b/solution.py
@@ -80,95 +80,134 @@
     return held
 
 
-def assemble(pieces, into):
+def assemble(pieces, into, first_row):
     rows = pieces[0].shape[0]
-    for place, piece in enumerate(pieces[:-2]):
-        into[place * rows : (place + 1) * rows, :] = piece[...]
-    quarter = pieces[-1].shape[1]
-    start = (len(pieces) - 2) * rows
-    into[start : start + rows, :quarter] = pieces[-2][...]
-    into[start : start + rows, quarter:] = pieces[-1][...]
-
-
-def first_pass(pieces, weight, n_rows, marks):
-    half, columns = weight.shape[1] // 2, weight.shape[2]
+    row = first_row
+    column = 0
+    for piece in pieces:
+        width = piece.shape[1]
+        into[row : row + rows, column : column + width] = piece[...]
+        column = (column + width) % into.shape[1]
+        if column == 0:
+            row += rows
+
+
+def feature_map(projected):
+    return jnp.where(projected > 0.0, projected + 1.0, jnp.exp(jnp.minimum(projected, 0.0)))
+
+
+def early_keys(first_pieces, second_pieces, weight, n_rows):
+    _, width, columns = weight.shape
+    half = width // 2
+    count = len(first_pieces)
+    early = count * first_pieces[0].shape[0]
 
     def body(*refs):
-        rows = refs[: len(pieces)]
-        weight_ref, out_ref, whole = refs[len(pieces)], *refs[-2:]
-        assemble(rows, whole)
+        weight_ref, feat_ref, first_ref, second_ref = refs[2 * count :]
+        assemble(refs[:count], first_ref, 0)
+        assemble(refs[count : 2 * count], second_ref, 0)
+        projected = jnp.dot(first_ref[:early, :], weight_ref[1, :half, :], preferred_element_type=F32)
+        projected += jnp.dot(second_ref[:early, :], weight_ref[1, half:, :], preferred_element_type=F32)
+        feat_ref[:early, :] = feature_map(projected).astype(BF16)
+
+    return call(
+        body,
+        [jax.ShapeDtypeStruct((n_rows, columns), BF16)] + [jax.ShapeDtypeStruct((n_rows, half), BF16)] * 2,
+        [VMEM] * (2 * count + 1),
+        [VMEM] * 3,
+        flops=2 * early * width * columns,
+        nbytes=2 * width * columns,
+        name="early_keys",
+    )(*first_pieces, *second_pieces, weight)
+
+
+def early_values(first_rows, second_rows, weight, early):
+    n_rows, half = first_rows.shape
+    columns = weight.shape[2]
+
+    def body(first_ref, second_ref, weight_ref, values_ref):
+        projected = jnp.dot(first_ref[:early, :], weight_ref[2, :half, :], preferred_element_type=F32)
+        projected += jnp.dot(second_ref[:early, :], weight_ref[2, half:, :], preferred_element_type=F32)
+        values_ref[:early, :] = projected.astype(BF16)
+
+    return call(
+        body,
+        jax.ShapeDtypeStruct((n_rows, columns), BF16),
+        [VMEM] * 3,
+        VMEM,
+        flops=4 * early * half * columns,
+        nbytes=4 * half * columns,
+        name="early_values",
+    )(first_rows, second_rows, weight)
+
+
+def first_pass(pieces, first_rows, weight, early, after):
+    n_rows, half = first_rows.shape
+    columns = weight.shape[2]
+    count = len(pieces)
+
+    def body(*refs):
+        weight_ref, (out_ref, whole) = refs[count + 1], refs[-2:]
+        assemble(refs[:count], whole, early)
         for place in range(2):
-            out_ref[place] = jnp.dot(whole[...], weight_ref[1 + place, :half, :], preferred_element_type=F32)
+            out_ref[place] = jnp.dot(whole[early:, :], weight_ref[1 + place, :half, :], preferred_element_type=F32)
 
     return call(
         body,
         (
-            jax.ShapeDtypeStruct((2, n_rows, columns), F32),
+            jax.ShapeDtypeStruct((2, n_rows - early, columns), F32),
             jax.ShapeDtypeStruct((n_rows, half), BF16),
         ),
-        [VMEM] * (len(pieces) + 1) + [ANY] * len(marks),
+        [VMEM] * (count + 2) + [ANY] * len(after),
         (VMEM, VMEM),
-        flops=4 * n_rows * half * columns,
-        nbytes=4 * half * columns,
+        flops=4 * (n_rows - early) * half * columns,
+        nbytes=4 * half * columns,
+        input_output_aliases={count: 1},
         name="first_pass",
-    )(*pieces, weight, *marks)
-
-
-def feature_map(projected):
-    return jnp.where(projected > 0.0, projected + 1.0, jnp.exp(jnp.minimum(projected, 0.0)))
-
-
-def keys_and_values(rows_or_pieces, weight, first, start, count, head_dim):
-    _, n_rows, _ = first.shape
-    half = weight.shape[1] // 2
+    )(*pieces, first_rows, weight, *after)
+
+
+def late_keys_and_values(pieces, second_rows, weight, first, feat_k, values, start, count, head_dim, early):
+    n_rows, half = second_rows.shape
     columns = count * head_dim
-    whole = not isinstance(rows_or_pieces, list)
-    operands = [rows_or_pieces] if whole else rows_or_pieces
+    n_pieces = len(pieces)
+    span = slice(start * head_dim, start * head_dim + columns)
 
     def body(*refs):
-        rows = refs[: len(operands)]
-        weight_ref, first_ref, feat_ref, values_ref, state_ref = refs[len(operands) : len(operands) + 5]
-        if not whole:
-            assemble(rows, refs[-1])
-        rows_ref = rows[0] if whole else refs[-1]
-        span = slice(start * head_dim, start * head_dim + columns)
+        weight_ref, first_ref = refs[n_pieces + 1 : n_pieces + 3]
+        rows_ref, feat_ref, values_ref, state_ref = refs[-4:]
+        if pieces:
+            assemble(refs[:n_pieces], rows_ref, early)
         projected = first_ref[0, :, span] + jnp.dot(
-            rows_ref[...], weight_ref[1, half:, span], preferred_element_type=F32
+            rows_ref[early:, :], weight_ref[1, half:, span], preferred_element_type=F32
         )
-        feat_ref[...] = feature_map(projected).astype(BF16)
+        feat_ref[early:, span] = feature_map(projected).astype(BF16)
         projected = first_ref[1, :, span] + jnp.dot(
-            rows_ref[...], weight_ref[2, half:, span], preferred_element_type=F32
+            rows_ref[early:, :], weight_ref[2, half:, span], preferred_element_type=F32
         )
-        values_ref[...] = projected.astype(BF16)
+        values_ref[early:, span] = projected.astype(BF16)
         for head in range(count):
-            at = slice(head * head_dim, (head + 1) * head_dim)
+            at = slice((start + head) * head_dim, (start + head + 1) * head_dim)
             state_ref[head] = lax.dot_general(
                 feat_ref[:, at], values_ref[:, at], (((0,), (0,)), ((), ())), preferred_element_type=F32
             ).astype(BF16)
 
-    outs = [
-        jax.ShapeDtypeStruct((n_rows, columns), BF16),
-        jax.ShapeDtypeStruct((n_rows, columns), BF16),
-        jax.ShapeDtypeStruct((count, head_dim, head_dim), BF16),
-    ]
-    if not whole:
-        outs.append(jax.ShapeDtypeStruct((n_rows, half), BF16))
-    out = call(
-        body,
-        outs,
-        [VMEM] * (len(operands) + 2),
-        [VMEM] * len(outs),
-        flops=HOP_FLOPS if whole else 4 * n_rows * half * columns,
-        nbytes=4 * half * columns,
-        name="keys_and_values",
-    )(*operands, weight, first)
-    return out if whole else (out[:3], out[3])
-
-
-def queries_within(halves, qkv_weight, groups, head_dim, size, rows):
+    return call(
+        body,
+        [jax.ShapeDtypeStruct(array.shape, BF16) for array in (second_rows, feat_k, values)]
+        + [jax.ShapeDtypeStruct((count, head_dim, head_dim), BF16)],
+        [VMEM] * (n_pieces + 5),
+        [VMEM] * 4,
+        flops=4 * (n_rows - early) * half * columns if pieces else HOP_FLOPS,
+        nbytes=4 * half * columns,
+        input_output_aliases={n_pieces: 0, n_pieces + 3: 1, n_pieces + 4: 2},
+        name="late_keys_and_values",
+    )(*pieces, second_rows, weight, first, feat_k, values)
+
+
+def queries_within(halves, qkv_weight, feat_k, values, head_dim, size, rows):
     n_rows, half = halves[0].shape
     columns = qkv_weight.shape[2]
-    per_group = columns // len(groups)
     order = slots(size)
 
     def place(shape, axis):
@@ -183,31 +222,28 @@
             start = jnp.where(slot == at, holder * rows, start)
         return start + row - slot * rows
 
-    def body(first_ref, second_ref, weight_ref, *refs):
-        group_refs, (feat_ref, within_ref) = refs[:-2], refs[-2:]
+    def body(first_ref, second_ref, weight_ref, k_ref, v_ref, feat_ref, within_ref):
         causal = place((n_rows, 1), 0) >= place((1, n_rows), 1)
         projected = jnp.dot(first_ref[...], weight_ref[0, :half, :], preferred_element_type=F32)
         projected += jnp.dot(second_ref[...], weight_ref[0, half:, :], preferred_element_type=F32)
         feat_ref[...] = feature_map(projected).astype(BF16)
         for head in range(0, columns, head_dim):
             span = slice(head, head + head_dim)
-            k_ref, v_ref = group_refs[2 * (head // per_group) : 2 * (head // per_group) + 2]
-            at = slice(head % per_group, head % per_group + head_dim)
             scores = lax.dot_general(
-                feat_ref[:, span], k_ref[:, at], (((1,), (1,)), ((), ())), preferred_element_type=F32
+                feat_ref[:, span], k_ref[:, span], (((1,), (1,)), ((), ())), preferred_element_type=F32
             )
             scores = jnp.where(causal, scores, 0.0).astype(BF16)
-            within_ref[:, span] = jnp.dot(scores, v_ref[:, at], preferred_element_type=F32)
+            within_ref[:, span] = jnp.dot(scores, v_ref[:, span], preferred_element_type=F32)
 
     return call(
         body,
         (jax.ShapeDtypeStruct((n_rows, columns), BF16), jax.ShapeDtypeStruct((n_rows, columns), F32)),
-        [VMEM] * (3 + 2 * len(groups)),
+        [VMEM] * 5,
         (VMEM,) * 2,
         flops=4 * n_rows * half * columns + 4 * n_rows * n_rows * columns,
         nbytes=4 * half * columns,
         name="queries_within",
-    )(*halves, qkv_weight, *[array for group in groups for array in group[:2]])
+    )(*halves, qkv_weight, feat_k, values)
 
 
 def project_out(normalized, weight_ref, parts, rows):
@@ -392,14 +428,22 @@
     half = width // 2
     held = ring_gather(tokens, n_fsdp, right, left)
 
-    first, first_rows = first_pass(held[0], qkv_weight, n_rows, [mark(held[1][-6]), mark(held[1][-5])])
+    blocks = n_fsdp - 3
+    early = blocks * rows
+    marks = [mark(held[1][1]), mark(held[1][2])]
+    feat_k, first_rows, second_rows = early_keys(held[0][:blocks], held[1][:blocks], qkv_weight, n_rows)
+    values = early_values(first_rows, second_rows, qkv_weight, early)
+    first, first_rows = first_pass(held[0][blocks:], first_rows, qkv_weight, early, [values, feat_k] + marks)
     count = heads_here // 2 if heads_here % 2 == 0 else heads_here
-    group, second_rows = keys_and_values(held[1], qkv_weight, first, 0, count, head_dim)
-    groups = [group]
-    for start in range(count, heads_here, count):
-        groups.append(keys_and_values(second_rows, qkv_weight, first, start, count, head_dim))
-    feat_q, within = queries_within((first_rows, second_rows), qkv_weight, groups, head_dim, n_fsdp, rows)
-    exchanged = exchange_states([group[2] for group in groups], n_ctx)
+    states = []
+    for start in range(0, heads_here, count):
+        pieces = held[1][blocks:] if start == 0 else []
+        second_rows, feat_k, values, state = late_keys_and_values(
+            pieces, second_rows, qkv_weight, first, feat_k, values, start, count, head_dim, early
+        )
+        states.append(state)
+    feat_q, within = queries_within((first_rows, second_rows), qkv_weight, feat_k, values, head_dim, n_fsdp, rows)
+    exchanged = exchange_states(states, n_ctx)
     soon = 1
     normalized, parts = attend_and_project(
         feat_q, within, initial_state, exchanged, norm_gain, out_weight, soon, rows, head_dim

time: 80.7 us -> 81.4 us (level)
  Pallas kernels: 11.1 us -> 12.1 us
    ppermute x6, waiting for transfers between devices: 13.9 us -> 0.16 us  [ring_gather(): going_left[part] = lax.ppermute(going_left[part], 'fsdp', left)]
    ppermute x6, starting transfers between devices: 0.8 us -> 13.7 us  [ring_gather(): going_right[part] = lax.ppermute(going_right[part], 'fsdp', right)]
    ppermute x6, starting transfers between devices: 12.8 us -> 0.02 us  [ring_gather(): going_left[part] = lax.ppermute(going_left[part], 'fsdp', left)]
    ppermute x6, waiting for transfers between devices: 0.12 us -> 12.3 us  [ring_gather(): going_right[part] = lax.ppermute(going_right[part], 'fsdp', right)]
    ppermute x7, starting transfers between devices: 10.2 us -> 3.45 us  [hop(): lax.ppermute(to_left, 'fsdp', left)]
    ppermute x7, starting transfers between devices: 4.83 us -> 11.3 us  [hop(): lax.ppermute(to_right, 'fsdp', right)]
    ppermute x2, starting transfers between devices: 0.36 us -> 4.3 us  [ring_gather(): lax.ppermute(going_right[part][:, :quarter], 'fsdp', right)]
    ppermute x2, starting transfers between devices: 3.96 us -> 0.12 us  [ring_gather(): held[part].append(lax.ppermute(going_left[part][:, quarter:], 'fsdp', left))]
  transfers between devices with their start and end apart: 34 -> 34, of which waited for: 19 -> 18; matrix products, arithmetic and copies ran while one was open for 0% -> 0% of each run, Pallas kernels for 9% -> 11%
where the time goes in v8:
time: 81.4 us; the launch traced here: 81.2 us
  starting transfers between devices  36 us (44%)
  waiting for transfers between devices  31.8 us (39%)
  Pallas kernels  12.1 us (15%)
  local copies, waits for them, and re-layouts  1.11 us (1%)
    ppermute x6, starting transfers between devices, ring_gather(): going_right[part] = lax.ppermute(going_right[part], 'fsdp', right)  13.7 us
    ppermute x7, waiting for transfers between devices, hop(): lax.ppermute(to_left, 'fsdp', left)  12.7 us
    ppermute x6, waiting for transfers between devices, ring_gather(): going_right[part] = lax.ppermute(going_right[part], 'fsdp', right)  12.3 us
    ppermute x7, starting transfers between devices, hop(): lax.ppermute(to_right, 'fsdp', right)  11.3 us
    ppermute x2, starting transfers between devices, ring_gather(): lax.ppermute(going_right[part][:, :quarter], 'fsdp', right)  4.3 us
    ppermute x7, starting transfers between devices, hop(): lax.ppermute(to_left, 'fsdp', left)  3.45 us
    ppermute x7, waiting for transfers between devices, hop(): lax.ppermute(to_right, 'fsdp', right)  3.16 us
    ppermute x4, starting transfers between devices, exchange_states(): received[at].append(lax.ppermute(total, 'ctx', pairs))  3.09 us
  transfers between devices with their start and end apart: 34, of which 18 were waited for; matrix products, arithmetic and copies ran while one was open for 0% of the time, Pallas kernels for 11%

profile of v8, /device:TPU:0, one launch (start us, length us, event | category | flops | bytes accessed | tf_op | source)
XLA Modules:
  0.0 81.2 jit_solution(6746326519703422063)
XLA Ops:
  0.0 1.0 %fusion = (bf16[32,3072]{1,0:T(8,128)(2,1)S(1)}, bf16[32,3072]{1,0:T(8,128)(2,1)S(1)}) fusion(bf16[32,6144]{1,0:T(8,128)(2,1)} %param.5), kind=kLoop, calls=%fused_computation | loop fusion | bytes 786432 | tf_op jit(solution)/shard_map/slice | solution.py:69
  1.1 3.1 %collective-permute-start = (bf16[32,3072]{1,0:T(8,128)(2,1)S(1)}, bf16[32,3072]{1,0:T(8,128)(2,1)S(1)}, u32[]{:S(2)}, u32[]{:S(2)}) collective-permute-start(bf16[32,3072]{1,0:T(8,128)(2,1)S(1)} %get-tuple-element.70.refs_0_), channel_id=1, source_target_pairs={{0,2},{2,4},{4,6},{6,7},{7,5},{5,3},{3,1},{1,0},{8,10},{10,12},{12... | collective-permute-start | bytes 589832 | tf_op jit(solution)/shard_map/ppermute | solution.py:74
  4.1 2.0 %collective-permute-start.8 = (bf16[32,3072]{1,0:T(8,128)(2,1)S(1)}, bf16[32,3072]{1,0:T(8,128)(2,1)S(1)}, u32[]{:S(2)}, u32[]{:S(2)}) collective-permute-start(bf16[32,3072]{1,0:T(8,128)(2,1)S(1)} %get-tuple-element.69.refs_5_), channel_id=1, source_target_pairs={{0,2},{2,4},{4,6},{6,7},{7,5},{5,3},{3,1},{1,0},{8,10},{10,12},{12... | collective-permute-start | bytes 589832 | tf_op jit(solution)/shard_map/ppermute | solution.py:74
  6.2 3.6 %collective-permute-done.refs_1_ = bf16[32,3072]{1,0:T(8,128)(2,1)S(1)} collective-permute-done((bf16[32,3072]{1,0:T(8,128)(2,1)S(1)}, bf16[32,3072]{1,0:T(8,128)(2,1)S(1)}, u32[]{:S(2)}, u32[]{:S(2)}) %collective-permute-start) | collective-permute-done | bytes 196640 | tf_op jit(solution)/shard_map/ppermute | solution.py:74
  9.8 2.1 %collective-permute-start.1 = (bf16[32,3072]{1,0:T(8,128)(2,1)S(1)}, bf16[32,3072]{1,0:T(8,128)(2,1)S(1)}, u32[]{:S(2)}, u32[]{:S(2)}) collective-permute-start(bf16[32,3072]{1,0:T(8,128)(2,1)S(1)} %collective-permute-done.refs_1_), channel_id=1, source_target_pairs={{0,2},{2,4},{4,6},{6,7},{7,5},{5,3},{3,1},{1,0},{8,10},{10,12},{12... | collective-permute-start | bytes 589832 | tf_op jit(solution)/shard_map/ppermute | solution.py:74
  12.0 2.0 %collective-permute-done.8.refs_6_.arrived_ref = bf16[32,3072]{1,0:T(8,128)(2,1)S(1)} collective-permute-done((bf16[32,3072]{1,0:T(8,128)(2,1)S(1)}, bf16[32,3072]{1,0:T(8,128)(2,1)S(1)}, u32[]{:S(2)}, u32[]{:S(2)}) %collective-permute-start.8) | collective-permute-done | bytes 196640 | tf_op jit(solution)/shard_map/ppermute | solution.py:74
  14.0 2.1 %collective-permute-start.10 = (bf16[32,3072]{1,0:T(8,128)(2,1)S(1)}, bf16[32,3072]{1,0:T(8,128)(2,1)S(1)}, u32[]{:S(2)}, u32[]{:S(2)}) collective-permute-start(bf16[32,3072]{1,0:T(8,128)(2,1)S(1)} %collective-permute-done.8.refs_6_.arrived_ref), channel_id=1, source_target_pairs={{0,2},{2,4},{4,6},{6,7},{7,5},{5,3},{3,1},{1,0},{8,10},{10,12},{12... | collective-permute-start | bytes 589832 | tf_op jit(solution)/shard_map/ppermute | solution.py:74
  16.2 2.0 %collective-permute-done.1.refs_3_ = bf16[32,3072]{1,0:T(8,128)(2,1)S(1)} collective-permute-done((bf16[32,3072]{1,0:T(8,128)(2,1)S(1)}, bf16[32,3072]{1,0:T(8,128)(2,1)S(1)}, u32[]{:S(2)}, u32[]{:S(2)}) %collective-permute-start.1) | collective-permute-done | bytes 196640 | tf_op jit(solution)/shard_map/ppermute | solution.py:74
  18.2 2.1 %collective-permute-start.2 = (bf16[32,3072]{1,0:T(8,128)(2,1)S(1)}, bf16[32,3072]{1,0:T(8,128)(2,1)S(1)}, u32[]{:S(2)}, u32[]{:S(2)}) collective-permute-start(bf16[32,3072]{1,0:T(8,128)(2,1)S(1)} %collective-permute-done.1.refs_3_), channel_id=1, source_target_pairs={{0,2},{2,4},{4,6},{6,7},{7,5},{5,3},{3,1},{1,0},{8,10},{10,12},{12... | collective-permute-start | bytes 589832 | tf_op jit(solution)/shard_map/ppermute | solution.py:74
  20.4 2.0 %collective-permute-done.10.refs_8_ = bf16[32,3072]{1,0:T(8,128)(2,1)S(1)} collective-permute-done((bf16[32,3072]{1,0:T(8,128)(2,1)S(1)}, bf16[32,3072]{1,0:T(8,128)(2,1)S(1)}, u32[]{:S(2)}, u32[]{:S(2)}) %collective-permute-start.10) | collective-permute-done | bytes 196640 | tf_op jit(solution)/shard_map/ppermute | solution.py:74
  22.4 2.1 %collective-permute-start.12 = (bf16[32,3072]{1,0:T(8,128)(2,1)S(1)}, bf16[32,3072]{1,0:T(8,128)(2,1)S(1)}, u32[]{:S(2)}, u32[]{:S(2)}) collective-permute-start(bf16[32,3072]{1,0:T(8,128)(2,1)S(1)} %collective-permute-done.10.refs_8_), channel_id=1, source_target_pairs={{0,2},{2,4},{4,6},{6,7},{7,5},{5,3},{3,1},{1,0},{8,10},{10,12},{12... | collective-permute-start | bytes 589832 | tf_op jit(solution)/shard_map/ppermute | solution.py:74
  24.6 2.0 %collective-permute-done.2.refs_0_ = bf16[32,3072]{1,0:T(8,128)(2,1)S(1)} collective-permute-done((bf16[32,3072]{1,0:T(8,128)(2,1)S(1)}, bf16[32,3072]{1,0:T(8,128)(2,1)S(1)}, u32[]{:S(2)}, u32[]{:S(2)}) %collective-permute-start.2) | collective-permute-done | bytes 196640 | tf_op jit(solution)/shard_map/ppermute | solution.py:74
  26.6 2.2 %collective-permute-start.6 = (bf16[32,1536]{1,0:T(8,128)(2,1)S(1)}, bf16[32,1536]{1,0:T(8,128)(2,1)S(1)}, u32[]{:S(2)}, u32[]{:S(2)}) collective-permute-start(bf16[32,1536]{1,0:T(8,128)(2,1)S(1)} %slice.24), channel_id=1, source_target_pairs={{0,2},{2,4},{4,6},{6,7},{7,5},{5,3},{3,1},{1,0},{8,10},{10,12},{12... | collective-permute-start | bytes 294920 | tf_op jit(solution)/shard_map/ppermute | solution.py:78
  29.0 1.2 %early_keys.1 = (bf16[256,512]{1,0:T(8,128)(2,1)S(1)}, bf16[256,3072]{1,0:T(8,128)(2,1)S(1)}, bf16[256,3072]{1,0:T(8,128)(2,1)S(1)}) custom-call(bf16[32,3072]{1,0:T(8,128)(2,1)S(1)} %get-tuple-element.70.refs_0_, bf16[32,3072]{1,0:T(8,128)(2,1)S(1)} %collective-permute-done.refs_1_, bf16[32,3072]{1,0:T(8,128)(2,1)S(1)} %collective-permute-done.3.refs_2_, ...), custom_call_target="tpu_custom_call" | custom-call | flops 1006632960 | bytes 6291456 | tf_op jit(solution)/shard_map/early_keys/pallas_call | solution.py:113
  30.2 0.6 collective-permute-done.12.refs_0_
  30.8 2.1 %collective-permute-start.14 = (bf16[32,1536]{1,0:T(8,128)(2,1)S(1)}, bf16[32,1536]{1,0:T(8,128)(2,1)S(1)}, u32[]{:S(2)}, u32[]{:S(2)}) collective-permute-start(bf16[32,1536]{1,0:T(8,128)(2,1)S(1)} %slice.26), channel_id=1, source_target_pairs={{0,2},{2,4},{4,6},{6,7},{7,5},{5,3},{3,1},{1,0},{8,10},{10,12},{12... | collective-permute-start | bytes 294920 | tf_op jit(solution)/shard_map/ppermute | solution.py:78
  33.0 1.2 %early_values.1.refs_6_.refs_8_ = bf16[256,512]{1,0:T(8,128)(2,1)S(1)} custom-call(bf16[256,3072]{1,0:T(8,128)(2,1)S(1)} %get-tuple-element.37.first_ref.refs_4_, bf16[256,3072]{1,0:T(8,128)(2,1)S(1)} %get-tuple-element.38.second_ref.refs_4_, bf16[3,6144,512]{2,1,0:T(8,128)(2,1)S(1)} %bitcast.2), custom_call_target="tpu_custom_call" | custom-call | flops 1006632960 | bytes 6291456 | tf_op jit(solution)/shard_map/early_values/pallas_call | solution.py:133
  34.2 1.1 %first_pass.1 = (f32[2,96,512]{2,1,0:T(8,128)S(1)}, bf16[256,3072]{1,0:T(8,128)(2,1)S(1)}) custom-call(bf16[32,3072]{1,0:T(8,128)(2,1)S(1)} %collective-permute-done.2.refs_0_, bf16[32,3072]{1,0:T(8,128)(2,1)S(1)} %collective-permute-done.5.refs_1_, bf16[32,1536]{1,0:T(8,128)(2,1)S(1)} %collective-permute-done.6.refs_2_, ...), custom_call_target="tpu_custom_call", output_to_operand_aliasing={{1}: (4, {})} | custom-call | flops 603979776 | bytes 6291456 | tf_op jit(solution)/shard_map/first_pass/pallas_call | solution.py:155
  35.5 2.1 %collective-permute-done.15.refs_3_ = bf16[32,1536]{1,0:T(8,128)(2,1)S(1)} collective-permute-done((bf16[32,1536]{1,0:T(8,128)(2,1)S(1)}, bf16[32,1536]{1,0:T(8,128)(2,1)S(1)}, u32[]{:S(2)}, u32[]{:S(2)}) %collective-permute-start.15) | collective-permute-done | bytes 98336 | tf_op jit(solution)/shard_map/ppermute | solution.py:79
  37.6 0.9 %late_keys_and_values.2 = (bf16[256,3072]{1,0:T(8,128)(2,1)S(1)}, bf16[256,512]{1,0:T(8,128)(2,1)S(1)}, bf16[256,512]{1,0:T(8,128)(2,1)S(1)}, bf16[2,128,128]{2,1,0:T(8,128)(2,1)S(1)}) custom-call(bf16[32,3072]{1,0:T(8,128)(2,1)S(1)} %collective-permute-done.12.refs_0_, ...), custom_call_target="tpu_custom_call", output_to_operand_aliasing={{0}: (4, {}), {1}: (7, {}), {2}: (8, {})} | custom-call | flops 301989888 | bytes 3145728 | tf_op jit(solution)/shard_map/late_keys_and_values/pallas_call | solution.py:195
  38.6 0.9 %late_keys_and_values.3 = (bf16[256,3072]{1,0:T(8,128)(2,1)S(1)}, bf16[256,512]{1,0:T(8,128)(2,1)S(1)}, bf16[256,512]{1,0:T(8,128)(2,1)S(1)}, bf16[2,128,128]{2,1,0:T(8,128)(2,1)S(1)}) custom-call(bf16[256,3072]{1,0:T(8,128)(2,1)S(1)} %get-tuple-element.42.refs_0_, ...), custom_call_target="tpu_custom_call", output_to_operand_aliasing={{0}: (0, {}), {1}: (3, {}), {2}: (4, {})} | custom-call | flops 5000000000 | bytes 3145728 | tf_op jit(solution)/shard_map/late_keys_and_values/pallas_call | solution.py:195
  39.5 0.6 collective-permute-start.18
  40.1 1.6 %collective-permute-start.17 = (bf16[2,128,128]{2,1,0:T(8,128)(2,1)S(1)}, bf16[2,128,128]{2,1,0:T(8,128)(2,1)S(1)}, u32[]{:S(2)}, u32[]{:S(2)}) collective-permute-start(bf16[2,128,128]{2,1,0:T(8,128)(2,1)S(1)} %add_states.2.refs_0_), channel_id=1, source_target_pairs={{0,16},{8,24},{16,0},{24,8},{1,17},{9,25},{17,1},{25,9},{2,18},{10... | collective-permute-start | bytes 196616 | tf_op jit(solution)/shard_map/ppermute | solution.py:410
  41.7 0.9 %collective-permute-start.19 = (bf16[2,128,128]{2,1,0:T(8,128)(2,1)S(1)}, bf16[2,128,128]{2,1,0:T(8,128)(2,1)S(1)}, u32[]{:S(2)}, u32[]{:S(2)}) collective-permute-start(bf16[2,128,128]{2,1,0:T(8,128)(2,1)S(1)} %add_states.3), channel_id=1, source_target_pairs={{0,16},{8,24},{16,0},{24,8},{1,17},{9,25},{17,1},{25,9},{2,18},{10... | collective-permute-start | bytes 196616 | tf_op jit(solution)/shard_map/ppermute | solution.py:410
  42.5 2.3 %queries_within.1 = (bf16[256,512]{1,0:T(8,128)(2,1)S(1)}, f32[256,512]{1,0:T(8,128)S(1)}) custom-call(bf16[256,3072]{1,0:T(8,128)(2,1)S(1)} %get-tuple-element.40.first_ref, bf16[256,3072]{1,0:T(8,128)(2,1)S(1)} %get-tuple-element.45.second_ref, bf16[3,6144,512]{2,1,0:T(8,128)(2,1)S(1)} %bitcast.2, bf16[256,512]{1,0:T(8,128)(2,1)S(1)} %get-tuple-element.46.k_ref, ...), custom_call_target="tpu_custom_call" | custom-call | flops 1744830464 | bytes 6291456 | tf_op jit(solution)/shard_map/queries_within/pallas_call | solution.py:238
  44.9 1.1 %collective-permute-done.19.refs_3_ = bf16[2,128,128]{2,1,0:T(8,128)(2,1)S(1)} collective-permute-done((bf16[2,128,128]{2,1,0:T(8,128)(2,1)S(1)}, bf16[2,128,128]{2,1,0:T(8,128)(2,1)S(1)}, u32[]{:S(2)}, u32[]{:S(2)}) %collective-permute-start.19) | collective-permute-done | bytes 65568 | tf_op jit(solution)/shard_map/ppermute | solution.py:410
  46.0 1.5 %attend_and_project.1 = (bf16[256,512]{1,0:T(8,128)(2,1)S(1)}, bf16[32,3072]{1,0:T(8,128)(2,1)S(1)}, bf16[32,3072]{1,0:T(8,128)(2,1)S(1)}) custom-call(bf16[256,512]{1,0:T(8,128)(2,1)S(1)} %get-tuple-element.48.q_ref, f32[256,512]{1,0:T(8,128)S(1)} %get-tuple-element.49.within_ref, f32[4,128,128]{2,1,0:T(8,128)S(1)} %copy-done, f32[1,512]{1,0:T(1,128)S(1)} %bitcast.5, ...), custom_call_target="tpu_custom_call" | custom-call | flops 1610612736 | bytes 6291456 | tf_op jit(solution)/shard_map/attend_and_project/pallas_call | solution.py:286
  47.6 1.6 %collective-permute-start.26 = (bf16[32,3072]{1,0:T(8,128)(2,1)S(1)}, bf16[32,3072]{1,0:T(8,128)(2,1)S(1)}, u32[]{:S(2)}, u32[]{:S(2)}) collective-permute-start(bf16[32,3072]{1,0:T(8,128)(2,1)S(1)} %get-tuple-element.64), channel_id=1, source_target_pairs={{0,2},{2,4},{4,6},{6,7},{7,5},{5,3},{3,1},{1,0},{8,10},{10,12},{12... | collective-permute-start | bytes 589832 | tf_op jit(solution)/shard_map/ppermute | solution.py:374
  49.6 1.6 %project_rest.1 = (bf16[32,3072]{1,0:T(8,128)(2,1)S(1)}, bf16[32,3072]{1,0:T(8,128)(2,1)S(1)}, bf16[32,3072]{1,0:T(8,128)(2,1)S(1)}, bf16[32,3072]{1,0:T(8,128)(...) custom-call(bf16[256,512]{1,0:T(8,128)(2,1)S(1)} %get-tuple-element., ...), custom_call_target="tpu_custom_call" | custom-call | flops 5000000000 | bytes 6291456 | tf_op jit(solution)/shard_map/project_rest/pallas_call | solution.py:305
  51.2 0.5 collective-permute-start.20
  51.7 1.6 %collective-permute-start.23 = (bf16[32,3072]{1,0:T(8,128)(2,1)S(1)}, bf16[32,3072]{1,0:T(8,128)(2,1)S(1)}, u32[]{:S(2)}, u32[]{:S(2)}) collective-permute-start(bf16[32,3072]{1,0:T(8,128)(2,1)S(1)} %get-tuple-element.60), channel_id=1, source_target_pairs={{0,2},{2,4},{4,6},{6,7},{7,5},{5,3},{3,1},{1,0},{8,10},{10,12},{12... | collective-permute-start | bytes 589832 | tf_op jit(solution)/shard_map/ppermute | solution.py:374
  53.3 1.4 %collective-permute-done.26.got_ref = bf16[32,3072]{1,0:T(8,128)(2,1)S(1)} collective-permute-done((bf16[32,3072]{1,0:T(8,128)(2,1)S(1)}, bf16[32,3072]{1,0:T(8,128)(2,1)S(1)}, u32[]{:S(2)}, u32[]{:S(2)}) %collective-permute-start.26) | collective-permute-done | bytes 196640 | tf_op jit(solution)/shard_map/ppermute | solution.py:374
  54.8 1.6 %collective-permute-start.27 = (bf16[32,3072]{1,0:T(8,128)(2,1)S(1)}, bf16[32,3072]{1,0:T(8,128)(2,1)S(1)}, u32[]{:S(2)}, u32[]{:S(2)}) collective-permute-start(bf16[32,3072]{1,0:T(8,128)(2,1)S(1)} %add_step.14), channel_id=1, source_target_pairs={{0,2},{2,4},{4,6},{6,7},{7,5},{5,3},{3,1},{1,0},{8,10},{10,12},{12... | collective-permute-start | bytes 589832 | tf_op jit(solution)/shard_map/ppermute | solution.py:374
  56.4 0.6 collective-permute-done.30.got_ref
  57.1 0.5 collective-permute-start.31
  57.6 3.7 %collective-permute-done.20.got_ref = bf16[32,3072]{1,0:T(8,128)(2,1)S(1)} collective-permute-done((bf16[32,3072]{1,0:T(8,128)(2,1)S(1)}, bf16[32,3072]{1,0:T(8,128)(2,1)S(1)}, u32[]{:S(2)}, u32[]{:S(2)}) %collective-permute-start.20) | collective-permute-done | bytes 196640 | tf_op jit(solution)/shard_map/ppermute | solution.py:374
  61.3 0.5 collective-permute-start.21
  61.8 1.6 %collective-permute-start.24 = (bf16[32,3072]{1,0:T(8,128)(2,1)S(1)}, bf16[32,3072]{1,0:T(8,128)(2,1)S(1)}, u32[]{:S(2)}, u32[]{:S(2)}) collective-permute-start(bf16[32,3072]{1,0:T(8,128)(2,1)S(1)} %add_step.12), channel_id=1, source_target_pairs={{0,2},{2,4},{4,6},{6,7},{7,5},{5,3},{3,1},{1,0},{8,10},{10,12},{12... | collective-permute-start | bytes 589832 | tf_op jit(solution)/shard_map/ppermute | solution.py:374
  63.8 1.6 %collective-permute-start.28 = (bf16[32,3072]{1,0:T(8,128)(2,1)S(1)}, bf16[32,3072]{1,0:T(8,128)(2,1)S(1)}, u32[]{:S(2)}, u32[]{:S(2)}) collective-permute-start(bf16[32,3072]{1,0:T(8,128)(2,1)S(1)} %add_step.15), channel_id=1, source_target_pairs={{0,2},{2,4},{4,6},{6,7},{7,5},{5,3},{3,1},{1,0},{8,10},{10,12},{12... | collective-permute-start | bytes 589832 | tf_op jit(solution)/shard_map/ppermute | solution.py:374
  65.5 0.5 collective-permute-start.32
  66.0 3.6 %collective-permute-done.21.got_ref = bf16[32,3072]{1,0:T(8,128)(2,1)S(1)} collective-permute-done((bf16[32,3072]{1,0:T(8,128)(2,1)S(1)}, bf16[32,3072]{1,0:T(8,128)(2,1)S(1)}, u32[]{:S(2)}, u32[]{:S(2)}) %collective-permute-start.21) | collective-permute-done | bytes 196640 | tf_op jit(solution)/shard_map/ppermute | solution.py:374
  70.3 1.6 %collective-permute-start.25 = (bf16[32,3072]{1,0:T(8,128)(2,1)S(1)}, bf16[32,3072]{1,0:T(8,128)(2,1)S(1)}, u32[]{:S(2)}, u32[]{:S(2)}) collective-permute-start(bf16[32,3072]{1,0:T(8,128)(2,1)S(1)} %add_step.13), channel_id=1, source_target_pairs={{0,2},{2,4},{4,6},{6,7},{7,5},{5,3},{3,1},{1,0},{8,10},{10,12},{12... | collective-permute-start | bytes 589832 | tf_op jit(solution)/shard_map/ppermute | solution.py:374
  72.4 1.6 %collective-permute-start.29 = (bf16[32,3072]{1,0:T(8,128)(2,1)S(1)}, bf16[32,3072]{1,0:T(8,128)(2,1)S(1)}, u32[]{:S(2)}, u32[]{:S(2)}) collective-permute-start(bf16[32,3072]{1,0:T(8,128)(2,1)S(1)} %add_step.16), channel_id=1, source_target_pairs={{0,2},{2,4},{4,6},{6,7},{7,5},{5,3},{3,1},{1,0},{8,10},{10,12},{12... | collective-permute-start | bytes 589832 | tf_op jit(solution)/shard_map/ppermute | solution.py:374
  74.1 0.5 collective-permute-start.33
  74.6 3.5 %collective-permute-done.22.got_first = bf16[32,3072]{1,0:T(8,128)(2,1)S(1)} collective-permute-done((bf16[32,3072]{1,0:T(8,128)(2,1)S(1)}, bf16[32,3072]{1,0:T(8,128)(2,1)S(1)}, u32[]{:S(2)}, u32[]{:S(2)}) %collective-permute-start.22) | collective-permute-done | bytes 196640 | tf_op jit(solution)/shard_map/ppermute | solution.py:374
  78.2 1.0 %collective-permute-done.29.first = bf16[32,3072]{1,0:T(8,128)(2,1)S(1)} collective-permute-done((bf16[32,3072]{1,0:T(8,128)(2,1)S(1)}, bf16[32,3072]{1,0:T(8,128)(2,1)S(1)}, u32[]{:S(2)}, u32[]{:S(2)}) %collective-permute-start.29) | collective-permute-done | bytes 196640 | tf_op jit(solution)/shard_map/ppermute | solution.py:374
  79.1 1.3 %collective-permute-done.33.second = bf16[32,3072]{1,0:T(8,128)(2,1)S(1)} collective-permute-done((bf16[32,3072]{1,0:T(8,128)(2,1)S(1)}, bf16[32,3072]{1,0:T(8,128)(2,1)S(1)}, u32[]{:S(2)}, u32[]{:S(2)}) %collective-permute-start.33) | collective-permute-done | bytes 196640 | tf_op jit(solution)/shard_map/ppermute | solution.py:374
  80.4 0.8 finish.1
  (69 shorter events, 2.9 us)
Async XLA Ops:
  1.1 8.7 %collective-permute-start = (bf16[32,3072]{1,0:T(8,128)(2,1)S(1)}, bf16[32,3072]{1,0:T(8,128)(2,1)S(1)}, u32[]{:S(2)}, u32[]{:S(2)}) collective-permute-start(bf16[32,3072]{1,0:T(8,128)(2,1)S(1)} %get-tuple-element.70.refs_0_), channel_id=1, source_target_pairs={{0,2},{2,4},{4,6},{6,7},{7,5},{5,3},{3,1},{1,0},{8,10},{10,12},{12... | collective-permute-start | bytes 589832 | tf_op jit(solution)/shard_map/ppermute | solution.py:74
  4.1 7.8 %collective-permute-start.3 = (bf16[32,3072]{1,0:T(8,128)(2,1)S(1)}, bf16[32,3072]{1,0:T(8,128)(2,1)S(1)}, u32[]{:S(2)}, u32[]{:S(2)}) collective-permute-start(bf16[32,3072]{1,0:T(8,128)(2,1)S(1)} %get-tuple-element.70.refs_0_), channel_id=1, source_target_pairs={{2,0},{4,2},{6,4},{7,6},{5,7},{3,5},{1,3},{0,1},{10,8},{12,10},{14... | collective-permute-start | bytes 589832 | tf_op jit(solution)/shard_map/ppermute | solution.py:75
  4.1 9.9 %collective-permute-start.8 = (bf16[32,3072]{1,0:T(8,128)(2,1)S(1)}, bf16[32,3072]{1,0:T(8,128)(2,1)S(1)}, u32[]{:S(2)}, u32[]{:S(2)}) collective-permute-start(bf16[32,3072]{1,0:T(8,128)(2,1)S(1)} %get-tuple-element.69.refs_5_), channel_id=1, source_target_pairs={{0,2},{2,4},{4,6},{6,7},{7,5},{5,3},{3,1},{1,0},{8,10},{10,12},{12... | collective-permute-start | bytes 589832 | tf_op jit(solution)/shard_map/ppermute | solution.py:74
  6.2 10.0 %collective-permute-start.9 = (bf16[32,3072]{1,0:T(8,128)(2,1)S(1)}, bf16[32,3072]{1,0:T(8,128)(2,1)S(1)}, u32[]{:S(2)}, u32[]{:S(2)}) collective-permute-start(bf16[32,3072]{1,0:T(8,128)(2,1)S(1)} %get-tuple-element.69.refs_5_), channel_id=1, source_target_pairs={{2,0},{4,2},{6,4},{7,6},{5,7},{3,5},{1,3},{0,1},{10,8},{12,10},{14... | collective-permute-start | bytes 589832 | tf_op jit(solution)/shard_map/ppermute | solution.py:75
  9.8 8.4 %collective-permute-start.1 = (bf16[32,3072]{1,0:T(8,128)(2,1)S(1)}, bf16[32,3072]{1,0:T(8,128)(2,1)S(1)}, u32[]{:S(2)}, u32[]{:S(2)}) collective-permute-start(bf16[32,3072]{1,0:T(8,128)(2,1)S(1)} %collective-permute-done.refs_1_), channel_id=1, source_target_pairs={{0,2},{2,4},{4,6},{6,7},{7,5},{5,3},{3,1},{1,0},{8,10},{10,12},{12... | collective-permute-start | bytes 589832 | tf_op jit(solution)/shard_map/ppermute | solution.py:74
  12.0 8.4 %collective-permute-start.4 = (bf16[32,3072]{1,0:T(8,128)(2,1)S(1)}, bf16[32,3072]{1,0:T(8,128)(2,1)S(1)}, u32[]{:S(2)}, u32[]{:S(2)}) collective-permute-start(bf16[32,3072]{1,0:T(8,128)(2,1)S(1)} %collective-permute-done.3.refs_2_), channel_id=1, source_target_pairs={{2,0},{4,2},{6,4},{7,6},{5,7},{3,5},{1,3},{0,1},{10,8},{12,10},{14... | collective-permute-start | bytes 589832 | tf_op jit(solution)/shard_map/ppermute | solution.py:75
  14.0 8.4 %collective-permute-start.10 = (bf16[32,3072]{1,0:T(8,128)(2,1)S(1)}, bf16[32,3072]{1,0:T(8,128)(2,1)S(1)}, u32[]{:S(2)}, u32[]{:S(2)}) collective-permute-start(bf16[32,3072]{1,0:T(8,128)(2,1)S(1)} %collective-permute-done.8.refs_6_.arrived_ref), channel_id=1, source_target_pairs={{0,2},{2,4},{4,6},{6,7},{7,5},{5,3},{3,1},{1,0},{8,10},{10,12},{12... | collective-permute-start | bytes 589832 | tf_op jit(solution)/shard_map/ppermute | solution.py:74
  16.2 8.4 %collective-permute-start.11 = (bf16[32,3072]{1,0:T(8,128)(2,1)S(1)}, bf16[32,3072]{1,0:T(8,128)(2,1)S(1)}, u32[]{:S(2)}, u32[]{:S(2)}) collective-permute-start(bf16[32,3072]{1,0:T(8,128)(2,1)S(1)} %collective-permute-done.9.refs_7_.arrived_ref), channel_id=1, source_target_pairs={{2,0},{4,2},{6,4},{7,6},{5,7},{3,5},{1,3},{0,1},{10,8},{12,10},{14... | collective-permute-start | bytes 589832 | tf_op jit(solution)/shard_map/ppermute | solution.py:75
  16.2 12.7 %slice-start = ((s8[18874368]{0:T(1024)(128)(4,1)}), s8[4194304]{0:T(1024)(128)(4,1)S(1)}, s32[]{:S(2)}) async-start(s8[18874368]{0:T(1024)(128)(4,1)} %bitcast.1), calls=%async_computation | async-start | bytes 8388608
  16.2 12.8 %slice-start.1 = ((s8[18874368]{0:T(1024)(128)(4,1)}), s8[4194304]{0:T(1024)(128)(4,1)S(1)}, s32[]{:S(2)}) async-start(s8[18874368]{0:T(1024)(128)(4,1)} %bitcast.1), calls=%async_computation.1 | async-start | bytes 8388608
  16.2 12.8 %slice-start.2 = ((s8[18874368]{0:T(1024)(128)(4,1)}), s8[4194304]{0:T(1024)(128)(4,1)S(1)}, s32[]{:S(2)}) async-start(s8[18874368]{0:T(1024)(128)(4,1)} %bitcast.1), calls=%async_computation.2 | async-start | bytes 8388608
  16.2 12.8 %slice-start.3 = ((s8[18874368]{0:T(1024)(128)(4,1)}), s8[4194304]{0:T(1024)(128)(4,1)S(1)}, s32[]{:S(2)}) async-start(s8[18874368]{0:T(1024)(128)(4,1)} %bitcast.1), calls=%async_computation.3 | async-start | bytes 8388608
  16.2 12.7 %slice-start.4 = ((s8[18874368]{0:T(1024)(128)(4,1)}), s8[2097152]{0:T(1024)(128)(4,1)S(1)}, s32[]{:S(2)}) async-start(s8[18874368]{0:T(1024)(128)(4,1)} %bitcast.1), calls=%async_computation.4 | async-start | bytes 4194304
  18.2 8.4 %collective-permute-start.2 = (bf16[32,3072]{1,0:T(8,128)(2,1)S(1)}, bf16[32,3072]{1,0:T(8,128)(2,1)S(1)}, u32[]{:S(2)}, u32[]{:S(2)}) collective-permute-start(bf16[32,3072]{1,0:T(8,128)(2,1)S(1)} %collective-permute-done.1.refs_3_), channel_id=1, source_target_pairs={{0,2},{2,4},{4,6},{6,7},{7,5},{5,3},{3,1},{1,0},{8,10},{10,12},{12... | collective-permute-start | bytes 589832 | tf_op jit(solution)/shard_map/ppermute | solution.py:74
  20.4 8.5 %collective-permute-start.5 = (bf16[32,3072]{1,0:T(8,128)(2,1)S(1)}, bf16[32,3072]{1,0:T(8,128)(2,1)S(1)}, u32[]{:S(2)}, u32[]{:S(2)}) collective-permute-start(bf16[32,3072]{1,0:T(8,128)(2,1)S(1)} %collective-permute-done.4.refs_4_), channel_id=1, source_target_pairs={{2,0},{4,2},{6,4},{7,6},{5,7},{3,5},{1,3},{0,1},{10,8},{12,10},{14... | collective-permute-start | bytes 589832 | tf_op jit(solution)/shard_map/ppermute | solution.py:75
  22.4 8.4 %collective-permute-start.12 = (bf16[32,3072]{1,0:T(8,128)(2,1)S(1)}, bf16[32,3072]{1,0:T(8,128)(2,1)S(1)}, u32[]{:S(2)}, u32[]{:S(2)}) collective-permute-start(bf16[32,3072]{1,0:T(8,128)(2,1)S(1)} %collective-permute-done.10.refs_8_), channel_id=1, source_target_pairs={{0,2},{2,4},{4,6},{6,7},{7,5},{5,3},{3,1},{1,0},{8,10},{10,12},{12... | collective-permute-start | bytes 589832 | tf_op jit(solution)/shard_map/ppermute | solution.py:74
  24.6 8.4 %collective-permute-start.13 = (bf16[32,3072]{1,0:T(8,128)(2,1)S(1)}, bf16[32,3072]{1,0:T(8,128)(2,1)S(1)}, u32[]{:S(2)}, u32[]{:S(2)}) collective-permute-start(bf16[32,3072]{1,0:T(8,128)(2,1)S(1)} %collective-permute-done.11.refs_9_), channel_id=1, source_target_pairs={{2,0},{4,2},{6,4},{7,6},{5,7},{3,5},{1,3},{0,1},{10,8},{12,10},{14... | collective-permute-start | bytes 589832 | tf_op jit(solution)/shard_map/ppermute | solution.py:75
  26.6 7.6 %collective-permute-start.6 = (bf16[32,1536]{1,0:T(8,128)(2,1)S(1)}, bf16[32,1536]{1,0:T(8,128)(2,1)S(1)}, u32[]{:S(2)}, u32[]{:S(2)}) collective-permute-start(bf16[32,1536]{1,0:T(8,128)(2,1)S(1)} %slice.24), channel_id=1, source_target_pairs={{0,2},{2,4},{4,6},{6,7},{7,5},{5,3},{3,1},{1,0},{8,10},{10,12},{12... | collective-permute-start | bytes 294920 | tf_op jit(solution)/shard_map/ppermute | solution.py:78
  28.8 5.4 %collective-permute-start.7 = (bf16[32,1536]{1,0:T(8,128)(2,1)S(1)}, bf16[32,1536]{1,0:T(8,128)(2,1)S(1)}, u32[]{:S(2)}, u32[]{:S(2)}) collective-permute-start(bf16[32,1536]{1,0:T(8,128)(2,1)S(1)} %slice.25), channel_id=1, source_target_pairs={{2,0},{4,2},{6,4},{7,6},{5,7},{3,5},{1,3},{0,1},{10,8},{12,10},{14... | collective-permute-start | bytes 294920 | tf_op jit(solution)/shard_map/ppermute | solution.py:79
  30.8 4.7 %collective-permute-start.14 = (bf16[32,1536]{1,0:T(8,128)(2,1)S(1)}, bf16[32,1536]{1,0:T(8,128)(2,1)S(1)}, u32[]{:S(2)}, u32[]{:S(2)}) collective-permute-start(bf16[32,1536]{1,0:T(8,128)(2,1)S(1)} %slice.26), channel_id=1, source_target_pairs={{0,2},{2,4},{4,6},{6,7},{7,5},{5,3},{3,1},{1,0},{8,10},{10,12},{12... | collective-permute-start | bytes 294920 | tf_op jit(solution)/shard_map/ppermute | solution.py:78
  33.0 4.7 %collective-permute-start.15 = (bf16[32,1536]{1,0:T(8,128)(2,1)S(1)}, bf16[32,1536]{1,0:T(8,128)(2,1)S(1)}, u32[]{:S(2)}, u32[]{:S(2)}) collective-permute-start(bf16[32,1536]{1,0:T(8,128)(2,1)S(1)} %slice.27), channel_id=1, source_target_pairs={{2,0},{4,2},{6,4},{7,6},{5,7},{3,5},{1,3},{0,1},{10,8},{12,10},{14... | collective-permute-start | bytes 294920 | tf_op jit(solution)/shard_map/ppermute | solution.py:79
  38.5 1.5 %collective-permute-start.16 = (bf16[2,128,128]{2,1,0:T(8,128)(2,1)S(1)}, bf16[2,128,128]{2,1,0:T(8,128)(2,1)S(1)}, u32[]{:S(2)}, u32[]{:S(2)}) collective-permute-start(bf16[2,128,128]{2,1,0:T(8,128)(2,1)S(1)} %get-tuple-element.50.one_ref), channel_id=1, source_target_pairs={{0,8},{8,0},{16,24},{24,16},{1,9},{9,1},{17,25},{25,17},{2,10},{10... | collective-permute-start | bytes 196616 | tf_op jit(solution)/shard_map/ppermute | solution.py:410
  39.5 2.2 %collective-permute-start.18 = (bf16[2,128,128]{2,1,0:T(8,128)(2,1)S(1)}, bf16[2,128,128]{2,1,0:T(8,128)(2,1)S(1)}, u32[]{:S(2)}, u32[]{:S(2)}) collective-permute-start(bf16[2,128,128]{2,1,0:T(8,128)(2,1)S(1)} %get-tuple-element.51.one_ref), channel_id=1, source_target_pairs={{0,8},{8,0},{16,24},{24,16},{1,9},{9,1},{17,25},{25,17},{2,10},{10... | collective-permute-start | bytes 196616 | tf_op jit(solution)/shard_map/ppermute | solution.py:410
  40.1 4.8 %collective-permute-start.17 = (bf16[2,128,128]{2,1,0:T(8,128)(2,1)S(1)}, bf16[2,128,128]{2,1,0:T(8,128)(2,1)S(1)}, u32[]{:S(2)}, u32[]{:S(2)}) collective-permute-start(bf16[2,128,128]{2,1,0:T(8,128)(2,1)S(1)} %add_states.2.refs_0_), channel_id=1, source_target_pairs={{0,16},{8,24},{16,0},{24,8},{1,17},{9,25},{17,1},{25,9},{2,18},{10... | collective-permute-start | bytes 196616 | tf_op jit(solution)/shard_map/ppermute | solution.py:410
  41.7 4.3 %collective-permute-start.19 = (bf16[2,128,128]{2,1,0:T(8,128)(2,1)S(1)}, bf16[2,128,128]{2,1,0:T(8,128)(2,1)S(1)}, u32[]{:S(2)}, u32[]{:S(2)}) collective-permute-start(bf16[2,128,128]{2,1,0:T(8,128)(2,1)S(1)} %add_states.3), channel_id=1, source_target_pairs={{0,16},{8,24},{16,0},{24,8},{1,17},{9,25},{17,1},{25,9},{2,18},{10... | collective-permute-start | bytes 196616 | tf_op jit(solution)/shard_map/ppermute | solution.py:410
  42.5 3.5 %slice-start.5 = ((s8[6291456]{0:T(1024)(128)(4,1)}), s8[4194304]{0:T(1024)(128)(4,1)S(1)}, s32[]{:S(2)}) async-start(s8[6291456]{0:T(1024)(128)(4,1)} %bitcast.3), calls=%async_computation.5 | async-start | bytes 8388608
  42.5 3.5 %slice-start.6 = ((s8[6291456]{0:T(1024)(128)(4,1)}), s8[2097152]{0:T(1024)(128)(4,1)S(1)}, s32[]{:S(2)}) async-start(s8[6291456]{0:T(1024)(128)(4,1)} %bitcast.3), calls=%async_computation.6 | async-start | bytes 4194304
  42.5 3.5 %copy-start = (f32[4,128,128]{2,1,0:T(8,128)S(1)}, f32[4,128,128]{2,1,0:T(8,128)}, u32[]{:S(2)}) copy-start(f32[4,128,128]{2,1,0:T(8,128)} %initial_ref.1) | copy-start | bytes 786436
  42.5 3.5 %copy-start.1 = (f32[512]{0:T(512)S(1)}, f32[512]{0:T(512)}, u32[]{:S(2)}) copy-start(f32[512]{0:T(512)} %param.8) | copy-start | bytes 6148
  47.6 7.2 %collective-permute-start.26 = (bf16[32,3072]{1,0:T(8,128)(2,1)S(1)}, bf16[32,3072]{1,0:T(8,128)(2,1)S(1)}, u32[]{:S(2)}, u32[]{:S(2)}) collective-permute-start(bf16[32,3072]{1,0:T(8,128)(2,1)S(1)} %get-tuple-element.64), channel_id=1, source_target_pairs={{0,2},{2,4},{4,6},{6,7},{7,5},{5,3},{3,1},{1,0},{8,10},{10,12},{12... | collective-permute-start | bytes 589832 | tf_op jit(solution)/shard_map/ppermute | solution.py:374
  49.2 7.8 %collective-permute-start.30 = (bf16[32,3072]{1,0:T(8,128)(2,1)S(1)}, bf16[32,3072]{1,0:T(8,128)(2,1)S(1)}, u32[]{:S(2)}, u32[]{:S(2)}) collective-permute-start(bf16[32,3072]{1,0:T(8,128)(2,1)S(1)} %get-tuple-element.68), channel_id=1, source_target_pairs={{2,0},{4,2},{6,4},{7,6},{5,7},{3,5},{1,3},{0,1},{10,8},{12,10},{14... | collective-permute-start | bytes 589832 | tf_op jit(solution)/shard_map/ppermute | solution.py:374
  51.2 10.0 %collective-permute-start.20 = (bf16[32,3072]{1,0:T(8,128)(2,1)S(1)}, bf16[32,3072]{1,0:T(8,128)(2,1)S(1)}, u32[]{:S(2)}, u32[]{:S(2)}) collective-permute-start(bf16[32,3072]{1,0:T(8,128)(2,1)S(1)} %get-tuple-element.57), channel_id=1, source_target_pairs={{2,0},{4,2},{6,4},{7,6},{5,7},{3,5},{1,3},{0,1},{10,8},{12,10},{14... | collective-permute-start | bytes 589832 | tf_op jit(solution)/shard_map/ppermute | solution.py:374
  51.7 10.0 %collective-permute-start.23 = (bf16[32,3072]{1,0:T(8,128)(2,1)S(1)}, bf16[32,3072]{1,0:T(8,128)(2,1)S(1)}, u32[]{:S(2)}, u32[]{:S(2)}) collective-permute-start(bf16[32,3072]{1,0:T(8,128)(2,1)S(1)} %get-tuple-element.60), channel_id=1, source_target_pairs={{0,2},{2,4},{4,6},{6,7},{7,5},{5,3},{3,1},{1,0},{8,10},{10,12},{12... | collective-permute-start | bytes 589832 | tf_op jit(solution)/shard_map/ppermute | solution.py:374
  54.8 9.0 %collective-permute-start.27 = (bf16[32,3072]{1,0:T(8,128)(2,1)S(1)}, bf16[32,3072]{1,0:T(8,128)(2,1)S(1)}, u32[]{:S(2)}, u32[]{:S(2)}) collective-permute-start(bf16[32,3072]{1,0:T(8,128)(2,1)S(1)} %add_step.14), channel_id=1, source_target_pairs={{0,2},{2,4},{4,6},{6,7},{7,5},{5,3},{3,1},{1,0},{8,10},{10,12},{12... | collective-permute-start | bytes 589832 | tf_op jit(solution)/shard_map/ppermute | solution.py:374
  57.1 8.4 %collective-permute-start.31 = (bf16[32,3072]{1,0:T(8,128)(2,1)S(1)}, bf16[32,3072]{1,0:T(8,128)(2,1)S(1)}, u32[]{:S(2)}, u32[]{:S(2)}) collective-permute-start(bf16[32,3072]{1,0:T(8,128)(2,1)S(1)} %add_step.17), channel_id=1, source_target_pairs={{2,0},{4,2},{6,4},{7,6},{5,7},{3,5},{1,3},{0,1},{10,8},{12,10},{14... | collective-permute-start | bytes 589832 | tf_op jit(solution)/shard_map/ppermute | solution.py:374
  61.3 8.4 %collective-permute-start.21 = (bf16[32,3072]{1,0:T(8,128)(2,1)S(1)}, bf16[32,3072]{1,0:T(8,128)(2,1)S(1)}, u32[]{:S(2)}, u32[]{:S(2)}) collective-permute-start(bf16[32,3072]{1,0:T(8,128)(2,1)S(1)} %add_step.10), channel_id=1, source_target_pairs={{2,0},{4,2},{6,4},{7,6},{5,7},{3,5},{1,3},{0,1},{10,8},{12,10},{14... | collective-permute-start | bytes 589832 | tf_op jit(solution)/shard_map/ppermute | solution.py:374
  61.8 8.4 %collective-permute-start.24 = (bf16[32,3072]{1,0:T(8,128)(2,1)S(1)}, bf16[32,3072]{1,0:T(8,128)(2,1)S(1)}, u32[]{:S(2)}, u32[]{:S(2)}) collective-permute-start(bf16[32,3072]{1,0:T(8,128)(2,1)S(1)} %add_step.12), channel_id=1, source_target_pairs={{0,2},{2,4},{4,6},{6,7},{7,5},{5,3},{3,1},{1,0},{8,10},{10,12},{12... | collective-permute-start | bytes 589832 | tf_op jit(solution)/shard_map/ppermute | solution.py:374
  63.8 8.5 %collective-permute-start.28 = (bf16[32,3072]{1,0:T(8,128)(2,1)S(1)}, bf16[32,3072]{1,0:T(8,128)(2,1)S(1)}, u32[]{:S(2)}, u32[]{:S(2)}) collective-permute-start(bf16[32,3072]{1,0:T(8,128)(2,1)S(1)} %add_step.15), channel_id=1, source_target_pairs={{0,2},{2,4},{4,6},{6,7},{7,5},{5,3},{3,1},{1,0},{8,10},{10,12},{12... | collective-permute-start | bytes 589832 | tf_op jit(solution)/shard_map/ppermute | solution.py:374
  65.5 8.5 %collective-permute-start.32 = (bf16[32,3072]{1,0:T(8,128)(2,1)S(1)}, bf16[32,3072]{1,0:T(8,128)(2,1)S(1)}, u32[]{:S(2)}, u32[]{:S(2)}) collective-permute-start(bf16[32,3072]{1,0:T(8,128)(2,1)S(1)} %add_step.18), channel_id=1, source_target_pairs={{2,0},{4,2},{6,4},{7,6},{5,7},{3,5},{1,3},{0,1},{10,8},{12,10},{14... | collective-permute-start | bytes 589832 | tf_op jit(solution)/shard_map/ppermute | solution.py:374
  69.7 8.4 %collective-permute-start.22 = (bf16[32,3072]{1,0:T(8,128)(2,1)S(1)}, bf16[32,3072]{1,0:T(8,128)(2,1)S(1)}, u32[]{:S(2)}, u32[]{:S(2)}) collective-permute-start(bf16[32,3072]{1,0:T(8,128)(2,1)S(1)} %add_step.11), channel_id=1, source_target_pairs={{2,0},{4,2},{6,4},{7,6},{5,7},{3,5},{1,3},{0,1},{10,8},{12,10},{14... | collective-permute-start | bytes 589832 | tf_op jit(solution)/shard_map/ppermute | solution.py:374
  70.3 7.8 %collective-permute-start.25 = (bf16[32,3072]{1,0:T(8,128)(2,1)S(1)}, bf16[32,3072]{1,0:T(8,128)(2,1)S(1)}, u32[]{:S(2)}, u32[]{:S(2)}) collective-permute-start(bf16[32,3072]{1,0:T(8,128)(2,1)S(1)} %add_step.13), channel_id=1, source_target_pairs={{0,2},{2,4},{4,6},{6,7},{7,5},{5,3},{3,1},{1,0},{8,10},{10,12},{12... | collective-permute-start | bytes 589832 | tf_op jit(solution)/shard_map/ppermute | solution.py:374
  72.4 6.8 %collective-permute-start.29 = (bf16[32,3072]{1,0:T(8,128)(2,1)S(1)}, bf16[32,3072]{1,0:T(8,128)(2,1)S(1)}, u32[]{:S(2)}, u32[]{:S(2)}) collective-permute-start(bf16[32,3072]{1,0:T(8,128)(2,1)S(1)} %add_step.16), channel_id=1, source_target_pairs={{0,2},{2,4},{4,6},{6,7},{7,5},{5,3},{3,1},{1,0},{8,10},{10,12},{12... | collective-permute-start | bytes 589832 | tf_op jit(solution)/shard_map/ppermute | solution.py:374
  74.1 6.4 %collective-permute-start.33 = (bf16[32,3072]{1,0:T(8,128)(2,1)S(1)}, bf16[32,3072]{1,0:T(8,128)(2,1)S(1)}, u32[]{:S(2)}, u32[]{:S(2)}) collective-permute-start(bf16[32,3072]{1,0:T(8,128)(2,1)S(1)} %add_step.19), channel_id=1, source_target_pairs={{2,0},{4,2},{6,4},{7,6},{5,7},{3,5},{1,3},{0,1},{10,8},{12,10},{14... | collective-permute-start | bytes 589832 | tf_op jit(solution)/shard_map/ppermute | solution.py:374

commit v9 on v8

--- a/solution.py
+++ b/solution.py
@@ -449,7 +449,8 @@
         feat_q, within, initial_state, exchanged, norm_gain, out_weight, soon, rows, head_dim
     )
     parts = project_rest(normalized, out_weight, n_fsdp - soon, rows) + parts
-    return ring_scatter(parts, order, right, left)
+    mirrored = [distance if distance == n_fsdp // 2 else -distance for distance in order]
+    return ring_scatter(parts, mirrored, left, right)
 
 
 def solution(mesh):

time: 81.4 us -> 80.3 us (0.986)
  waiting for transfers between devices: 31.8 us -> 30.4 us
    ppermute x7, starting transfers between devices: 3.45 us -> 11.4 us  [hop(): lax.ppermute(to_left, 'fsdp', left)]
    ppermute x7, starting transfers between devices: 11.3 us -> 3.64 us  [hop(): lax.ppermute(to_right, 'fsdp', right)]
    ppermute x7, waiting for transfers between devices: 12.7 us -> 7.37 us  [hop(): lax.ppermute(to_left, 'fsdp', left)]
    ppermute x7, waiting for transfers between devices: 3.16 us -> 7.18 us  [hop(): lax.ppermute(to_right, 'fsdp', right)]
where the time goes in v9:
time: 80.3 us; the launch traced here: 80.2 us
  starting transfers between devices  36.2 us (45%)
  waiting for transfers between devices  30.4 us (38%)
  Pallas kernels  12.1 us (15%)
  local copies, waits for them, and re-layouts  1.11 us (1%)
    ppermute x6, starting transfers between devices, ring_gather(): going_right[part] = lax.ppermute(going_right[part], 'fsdp', right)  13.7 us
    ppermute x6, waiting for transfers between devices, ring_gather(): going_right[part] = lax.ppermute(going_right[part], 'fsdp', right)  12.3 us
    ppermute x7, starting transfers between devices, hop(): lax.ppermute(to_left, 'fsdp', left)  11.4 us
    ppermute x7, waiting for transfers between devices, hop(): lax.ppermute(to_left, 'fsdp', left)  7.37 us
    ppermute x7, waiting for transfers between devices, hop(): lax.ppermute(to_right, 'fsdp', right)  7.18 us
    ppermute x2, starting transfers between devices, ring_gather(): lax.ppermute(going_right[part][:, :quarter], 'fsdp', right)  4.3 us
    ppermute x7, starting transfers between devices, hop(): lax.ppermute(to_right, 'fsdp', right)  3.64 us
    ppermute x4, starting transfers between devices, exchange_states(): received[at].append(lax.ppermute(total, 'ctx', pairs))  3.09 us
  transfers between devices with their start and end apart: 34, of which 18 were waited for; matrix products, arithmetic and copies ran while one was open for 0% of the time, Pallas kernels for 11%

profile of v9, /device:TPU:0, one launch (start us, length us, event | category | flops | bytes accessed | tf_op | source)
XLA Modules:
  0.0 80.2 jit_solution(7359611042020524573)
XLA Ops:
  0.0 1.0 %fusion = (bf16[32,3072]{1,0:T(8,128)(2,1)S(1)}, bf16[32,3072]{1,0:T(8,128)(2,1)S(1)}) fusion(bf16[32,6144]{1,0:T(8,128)(2,1)} %param.5), kind=kLoop, calls=%fused_computation | loop fusion | bytes 786432 | tf_op jit(solution)/shard_map/slice | solution.py:69
  1.1 3.1 %collective-permute-start = (bf16[32,3072]{1,0:T(8,128)(2,1)S(1)}, bf16[32,3072]{1,0:T(8,128)(2,1)S(1)}, u32[]{:S(2)}, u32[]{:S(2)}) collective-permute-start(bf16[32,3072]{1,0:T(8,128)(2,1)S(1)} %get-tuple-element.70.refs_0_), channel_id=1, source_target_pairs={{0,2},{2,4},{4,6},{6,7},{7,5},{5,3},{3,1},{1,0},{8,10},{10,12},{12... | collective-permute-start | bytes 589832 | tf_op jit(solution)/shard_map/ppermute | solution.py:74
  4.1 2.0 %collective-permute-start.8 = (bf16[32,3072]{1,0:T(8,128)(2,1)S(1)}, bf16[32,3072]{1,0:T(8,128)(2,1)S(1)}, u32[]{:S(2)}, u32[]{:S(2)}) collective-permute-start(bf16[32,3072]{1,0:T(8,128)(2,1)S(1)} %get-tuple-element.69.refs_5_), channel_id=1, source_target_pairs={{0,2},{2,4},{4,6},{6,7},{7,5},{5,3},{3,1},{1,0},{8,10},{10,12},{12... | collective-permute-start | bytes 589832 | tf_op jit(solution)/shard_map/ppermute | solution.py:74
  6.2 3.6 %collective-permute-done.refs_1_ = bf16[32,3072]{1,0:T(8,128)(2,1)S(1)} collective-permute-done((bf16[32,3072]{1,0:T(8,128)(2,1)S(1)}, bf16[32,3072]{1,0:T(8,128)(2,1)S(1)}, u32[]{:S(2)}, u32[]{:S(2)}) %collective-permute-start) | collective-permute-done | bytes 196640 | tf_op jit(solution)/shard_map/ppermute | solution.py:74
  9.8 2.1 %collective-permute-start.1 = (bf16[32,3072]{1,0:T(8,128)(2,1)S(1)}, bf16[32,3072]{1,0:T(8,128)(2,1)S(1)}, u32[]{:S(2)}, u32[]{:S(2)}) collective-permute-start(bf16[32,3072]{1,0:T(8,128)(2,1)S(1)} %collective-permute-done.refs_1_), channel_id=1, source_target_pairs={{0,2},{2,4},{4,6},{6,7},{7,5},{5,3},{3,1},{1,0},{8,10},{10,12},{12... | collective-permute-start | bytes 589832 | tf_op jit(solution)/shard_map/ppermute | solution.py:74
  12.0 2.0 %collective-permute-done.8.refs_6_.arrived_ref = bf16[32,3072]{1,0:T(8,128)(2,1)S(1)} collective-permute-done((bf16[32,3072]{1,0:T(8,128)(2,1)S(1)}, bf16[32,3072]{1,0:T(8,128)(2,1)S(1)}, u32[]{:S(2)}, u32[]{:S(2)}) %collective-permute-start.8) | collective-permute-done | bytes 196640 | tf_op jit(solution)/shard_map/ppermute | solution.py:74
  14.0 2.1 %collective-permute-start.10 = (bf16[32,3072]{1,0:T(8,128)(2,1)S(1)}, bf16[32,3072]{1,0:T(8,128)(2,1)S(1)}, u32[]{:S(2)}, u32[]{:S(2)}) collective-permute-start(bf16[32,3072]{1,0:T(8,128)(2,1)S(1)} %collective-permute-done.8.refs_6_.arrived_ref), channel_id=1, source_target_pairs={{0,2},{2,4},{4,6},{6,7},{7,5},{5,3},{3,1},{1,0},{8,10},{10,12},{12... | collective-permute-start | bytes 589832 | tf_op jit(solution)/shard_map/ppermute | solution.py:74
  16.2 2.0 %collective-permute-done.1.refs_3_ = bf16[32,3072]{1,0:T(8,128)(2,1)S(1)} collective-permute-done((bf16[32,3072]{1,0:T(8,128)(2,1)S(1)}, bf16[32,3072]{1,0:T(8,128)(2,1)S(1)}, u32[]{:S(2)}, u32[]{:S(2)}) %collective-permute-start.1) | collective-permute-done | bytes 196640 | tf_op jit(solution)/shard_map/ppermute | solution.py:74
  18.2 2.1 %collective-permute-start.2 = (bf16[32,3072]{1,0:T(8,128)(2,1)S(1)}, bf16[32,3072]{1,0:T(8,128)(2,1)S(1)}, u32[]{:S(2)}, u32[]{:S(2)}) collective-permute-start(bf16[32,3072]{1,0:T(8,128)(2,1)S(1)} %collective-permute-done.1.refs_3_), channel_id=1, source_target_pairs={{0,2},{2,4},{4,6},{6,7},{7,5},{5,3},{3,1},{1,0},{8,10},{10,12},{12... | collective-permute-start | bytes 589832 | tf_op jit(solution)/shard_map/ppermute | solution.py:74
  20.4 2.0 %collective-permute-done.10.refs_8_ = bf16[32,3072]{1,0:T(8,128)(2,1)S(1)} collective-permute-done((bf16[32,3072]{1,0:T(8,128)(2,1)S(1)}, bf16[32,3072]{1,0:T(8,128)(2,1)S(1)}, u32[]{:S(2)}, u32[]{:S(2)}) %collective-permute-start.10) | collective-permute-done | bytes 196640 | tf_op jit(solution)/shard_map/ppermute | solution.py:74
  22.4 2.1 %collective-permute-start.12 = (bf16[32,3072]{1,0:T(8,128)(2,1)S(1)}, bf16[32,3072]{1,0:T(8,128)(2,1)S(1)}, u32[]{:S(2)}, u32[]{:S(2)}) collective-permute-start(bf16[32,3072]{1,0:T(8,128)(2,1)S(1)} %collective-permute-done.10.refs_8_), channel_id=1, source_target_pairs={{0,2},{2,4},{4,6},{6,7},{7,5},{5,3},{3,1},{1,0},{8,10},{10,12},{12... | collective-permute-start | bytes 589832 | tf_op jit(solution)/shard_map/ppermute | solution.py:74
  24.6 2.0 %collective-permute-done.2.refs_0_ = bf16[32,3072]{1,0:T(8,128)(2,1)S(1)} collective-permute-done((bf16[32,3072]{1,0:T(8,128)(2,1)S(1)}, bf16[32,3072]{1,0:T(8,128)(2,1)S(1)}, u32[]{:S(2)}, u32[]{:S(2)}) %collective-permute-start.2) | collective-permute-done | bytes 196640 | tf_op jit(solution)/shard_map/ppermute | solution.py:74
  26.6 2.2 %collective-permute-start.6 = (bf16[32,1536]{1,0:T(8,128)(2,1)S(1)}, bf16[32,1536]{1,0:T(8,128)(2,1)S(1)}, u32[]{:S(2)}, u32[]{:S(2)}) collective-permute-start(bf16[32,1536]{1,0:T(8,128)(2,1)S(1)} %slice.24), channel_id=1, source_target_pairs={{0,2},{2,4},{4,6},{6,7},{7,5},{5,3},{3,1},{1,0},{8,10},{10,12},{12... | collective-permute-start | bytes 294920 | tf_op jit(solution)/shard_map/ppermute | solution.py:78
  29.0 1.2 %early_keys.1 = (bf16[256,512]{1,0:T(8,128)(2,1)S(1)}, bf16[256,3072]{1,0:T(8,128)(2,1)S(1)}, bf16[256,3072]{1,0:T(8,128)(2,1)S(1)}) custom-call(bf16[32,3072]{1,0:T(8,128)(2,1)S(1)} %get-tuple-element.70.refs_0_, bf16[32,3072]{1,0:T(8,128)(2,1)S(1)} %collective-permute-done.refs_1_, bf16[32,3072]{1,0:T(8,128)(2,1)S(1)} %collective-permute-done.3.refs_2_, ...), custom_call_target="tpu_custom_call" | custom-call | flops 1006632960 | bytes 6291456 | tf_op jit(solution)/shard_map/early_keys/pallas_call | solution.py:113
  30.2 0.6 collective-permute-done.12.refs_0_
  30.8 2.1 %collective-permute-start.14 = (bf16[32,1536]{1,0:T(8,128)(2,1)S(1)}, bf16[32,1536]{1,0:T(8,128)(2,1)S(1)}, u32[]{:S(2)}, u32[]{:S(2)}) collective-permute-start(bf16[32,1536]{1,0:T(8,128)(2,1)S(1)} %slice.26), channel_id=1, source_target_pairs={{0,2},{2,4},{4,6},{6,7},{7,5},{5,3},{3,1},{1,0},{8,10},{10,12},{12... | collective-permute-start | bytes 294920 | tf_op jit(solution)/shard_map/ppermute | solution.py:78
  33.0 1.2 %early_values.1.refs_6_.refs_8_ = bf16[256,512]{1,0:T(8,128)(2,1)S(1)} custom-call(bf16[256,3072]{1,0:T(8,128)(2,1)S(1)} %get-tuple-element.37.first_ref.refs_4_, bf16[256,3072]{1,0:T(8,128)(2,1)S(1)} %get-tuple-element.38.second_ref.refs_4_, bf16[3,6144,512]{2,1,0:T(8,128)(2,1)S(1)} %bitcast.2), custom_call_target="tpu_custom_call" | custom-call | flops 1006632960 | bytes 6291456 | tf_op jit(solution)/shard_map/early_values/pallas_call | solution.py:133
  34.2 1.1 %first_pass.1 = (f32[2,96,512]{2,1,0:T(8,128)S(1)}, bf16[256,3072]{1,0:T(8,128)(2,1)S(1)}) custom-call(bf16[32,3072]{1,0:T(8,128)(2,1)S(1)} %collective-permute-done.2.refs_0_, bf16[32,3072]{1,0:T(8,128)(2,1)S(1)} %collective-permute-done.5.refs_1_, bf16[32,1536]{1,0:T(8,128)(2,1)S(1)} %collective-permute-done.6.refs_2_, ...), custom_call_target="tpu_custom_call", output_to_operand_aliasing={{1}: (4, {})} | custom-call | flops 603979776 | bytes 6291456 | tf_op jit(solution)/shard_map/first_pass/pallas_call | solution.py:155
  35.5 2.1 %collective-permute-done.15.refs_3_ = bf16[32,1536]{1,0:T(8,128)(2,1)S(1)} collective-permute-done((bf16[32,1536]{1,0:T(8,128)(2,1)S(1)}, bf16[32,1536]{1,0:T(8,128)(2,1)S(1)}, u32[]{:S(2)}, u32[]{:S(2)}) %collective-permute-start.15) | collective-permute-done | bytes 98336 | tf_op jit(solution)/shard_map/ppermute | solution.py:79
  37.6 0.9 %late_keys_and_values.2 = (bf16[256,3072]{1,0:T(8,128)(2,1)S(1)}, bf16[256,512]{1,0:T(8,128)(2,1)S(1)}, bf16[256,512]{1,0:T(8,128)(2,1)S(1)}, bf16[2,128,128]{2,1,0:T(8,128)(2,1)S(1)}) custom-call(bf16[32,3072]{1,0:T(8,128)(2,1)S(1)} %collective-permute-done.12.refs_0_, ...), custom_call_target="tpu_custom_call", output_to_operand_aliasing={{0}: (4, {}), {1}: (7, {}), {2}: (8, {})} | custom-call | flops 301989888 | bytes 3145728 | tf_op jit(solution)/shard_map/late_keys_and_values/pallas_call | solution.py:195
  38.6 0.9 %late_keys_and_values.3 = (bf16[256,3072]{1,0:T(8,128)(2,1)S(1)}, bf16[256,512]{1,0:T(8,128)(2,1)S(1)}, bf16[256,512]{1,0:T(8,128)(2,1)S(1)}, bf16[2,128,128]{2,1,0:T(8,128)(2,1)S(1)}) custom-call(bf16[256,3072]{1,0:T(8,128)(2,1)S(1)} %get-tuple-element.42.refs_0_, ...), custom_call_target="tpu_custom_call", output_to_operand_aliasing={{0}: (0, {}), {1}: (3, {}), {2}: (4, {})} | custom-call | flops 5000000000 | bytes 3145728 | tf_op jit(solution)/shard_map/late_keys_and_values/pallas_call | solution.py:195
  39.5 0.6 collective-permute-start.18
  40.1 1.6 %collective-permute-start.17 = (bf16[2,128,128]{2,1,0:T(8,128)(2,1)S(1)}, bf16[2,128,128]{2,1,0:T(8,128)(2,1)S(1)}, u32[]{:S(2)}, u32[]{:S(2)}) collective-permute-start(bf16[2,128,128]{2,1,0:T(8,128)(2,1)S(1)} %add_states.2.refs_0_), channel_id=1, source_target_pairs={{0,16},{8,24},{16,0},{24,8},{1,17},{9,25},{17,1},{25,9},{2,18},{10... | collective-permute-start | bytes 196616 | tf_op jit(solution)/shard_map/ppermute | solution.py:410
  41.7 0.9 %collective-permute-start.19 = (bf16[2,128,128]{2,1,0:T(8,128)(2,1)S(1)}, bf16[2,128,128]{2,1,0:T(8,128)(2,1)S(1)}, u32[]{:S(2)}, u32[]{:S(2)}) collective-permute-start(bf16[2,128,128]{2,1,0:T(8,128)(2,1)S(1)} %add_states.3), channel_id=1, source_target_pairs={{0,16},{8,24},{16,0},{24,8},{1,17},{9,25},{17,1},{25,9},{2,18},{10... | collective-permute-start | bytes 196616 | tf_op jit(solution)/shard_map/ppermute | solution.py:410
  42.5 2.3 %queries_within.1 = (bf16[256,512]{1,0:T(8,128)(2,1)S(1)}, f32[256,512]{1,0:T(8,128)S(1)}) custom-call(bf16[256,3072]{1,0:T(8,128)(2,1)S(1)} %get-tuple-element.40.first_ref, bf16[256,3072]{1,0:T(8,128)(2,1)S(1)} %get-tuple-element.45.second_ref, bf16[3,6144,512]{2,1,0:T(8,128)(2,1)S(1)} %bitcast.2, bf16[256,512]{1,0:T(8,128)(2,1)S(1)} %get-tuple-element.46.k_ref, ...), custom_call_target="tpu_custom_call" | custom-call | flops 1744830464 | bytes 6291456 | tf_op jit(solution)/shard_map/queries_within/pallas_call | solution.py:238
  44.9 1.1 %collective-permute-done.19.refs_3_ = bf16[2,128,128]{2,1,0:T(8,128)(2,1)S(1)} collective-permute-done((bf16[2,128,128]{2,1,0:T(8,128)(2,1)S(1)}, bf16[2,128,128]{2,1,0:T(8,128)(2,1)S(1)}, u32[]{:S(2)}, u32[]{:S(2)}) %collective-permute-start.19) | collective-permute-done | bytes 65568 | tf_op jit(solution)/shard_map/ppermute | solution.py:410
  46.0 1.5 %attend_and_project.1 = (bf16[256,512]{1,0:T(8,128)(2,1)S(1)}, bf16[32,3072]{1,0:T(8,128)(2,1)S(1)}, bf16[32,3072]{1,0:T(8,128)(2,1)S(1)}) custom-call(bf16[256,512]{1,0:T(8,128)(2,1)S(1)} %get-tuple-element.48.q_ref, f32[256,512]{1,0:T(8,128)S(1)} %get-tuple-element.49.within_ref, f32[4,128,128]{2,1,0:T(8,128)S(1)} %copy-done, f32[1,512]{1,0:T(1,128)S(1)} %bitcast.5, ...), custom_call_target="tpu_custom_call" | custom-call | flops 1610612736 | bytes 6291456 | tf_op jit(solution)/shard_map/attend_and_project/pallas_call | solution.py:286
  48.0 1.6 %collective-permute-start.30 = (bf16[32,3072]{1,0:T(8,128)(2,1)S(1)}, bf16[32,3072]{1,0:T(8,128)(2,1)S(1)}, u32[]{:S(2)}, u32[]{:S(2)}) collective-permute-start(bf16[32,3072]{1,0:T(8,128)(2,1)S(1)} %get-tuple-element.68), channel_id=1, source_target_pairs={{0,2},{2,4},{4,6},{6,7},{7,5},{5,3},{3,1},{1,0},{8,10},{10,12},{12... | collective-permute-start | bytes 589832 | tf_op jit(solution)/shard_map/ppermute | solution.py:374
  49.6 1.6 %project_rest.1 = (bf16[32,3072]{1,0:T(8,128)(2,1)S(1)}, bf16[32,3072]{1,0:T(8,128)(2,1)S(1)}, bf16[32,3072]{1,0:T(8,128)(2,1)S(1)}, bf16[32,3072]{1,0:T(8,128)(...) custom-call(bf16[256,512]{1,0:T(8,128)(2,1)S(1)} %get-tuple-element., ...), custom_call_target="tpu_custom_call" | custom-call | flops 5000000000 | bytes 6291456 | tf_op jit(solution)/shard_map/project_rest/pallas_call | solution.py:305
  51.2 1.6 %collective-permute-start.20 = (bf16[32,3072]{1,0:T(8,128)(2,1)S(1)}, bf16[32,3072]{1,0:T(8,128)(2,1)S(1)}, u32[]{:S(2)}, u32[]{:S(2)}) collective-permute-start(bf16[32,3072]{1,0:T(8,128)(2,1)S(1)} %get-tuple-element.57), channel_id=1, source_target_pairs={{0,2},{2,4},{4,6},{6,7},{7,5},{5,3},{3,1},{1,0},{8,10},{10,12},{12... | collective-permute-start | bytes 589832 | tf_op jit(solution)/shard_map/ppermute | solution.py:374
  53.3 0.6 collective-permute-done.26.got_ref
  54.4 0.8 %collective-permute-done.30.got_ref = bf16[32,3072]{1,0:T(8,128)(2,1)S(1)} collective-permute-done((bf16[32,3072]{1,0:T(8,128)(2,1)S(1)}, bf16[32,3072]{1,0:T(8,128)(2,1)S(1)}, u32[]{:S(2)}, u32[]{:S(2)}) %collective-permute-start.30) | collective-permute-done | bytes 196640 | tf_op jit(solution)/shard_map/ppermute | solution.py:374
  55.3 1.6 %collective-permute-start.31 = (bf16[32,3072]{1,0:T(8,128)(2,1)S(1)}, bf16[32,3072]{1,0:T(8,128)(2,1)S(1)}, u32[]{:S(2)}, u32[]{:S(2)}) collective-permute-start(bf16[32,3072]{1,0:T(8,128)(2,1)S(1)} %add_step.17), channel_id=1, source_target_pairs={{0,2},{2,4},{4,6},{6,7},{7,5},{5,3},{3,1},{1,0},{8,10},{10,12},{12... | collective-permute-start | bytes 589832 | tf_op jit(solution)/shard_map/ppermute | solution.py:374
  56.9 2.5 %collective-permute-done.20.got_ref = bf16[32,3072]{1,0:T(8,128)(2,1)S(1)} collective-permute-done((bf16[32,3072]{1,0:T(8,128)(2,1)S(1)}, bf16[32,3072]{1,0:T(8,128)(2,1)S(1)}, u32[]{:S(2)}, u32[]{:S(2)}) %collective-permute-start.20) | collective-permute-done | bytes 196640 | tf_op jit(solution)/shard_map/ppermute | solution.py:374
  59.5 1.6 %collective-permute-start.21 = (bf16[32,3072]{1,0:T(8,128)(2,1)S(1)}, bf16[32,3072]{1,0:T(8,128)(2,1)S(1)}, u32[]{:S(2)}, u32[]{:S(2)}) collective-permute-start(bf16[32,3072]{1,0:T(8,128)(2,1)S(1)} %add_step.10), channel_id=1, source_target_pairs={{0,2},{2,4},{4,6},{6,7},{7,5},{5,3},{3,1},{1,0},{8,10},{10,12},{12... | collective-permute-start | bytes 589832 | tf_op jit(solution)/shard_map/ppermute | solution.py:374
  61.2 0.6 collective-permute-start.24
  61.8 1.9 %collective-permute-done.27.got_ref = bf16[32,3072]{1,0:T(8,128)(2,1)S(1)} collective-permute-done((bf16[32,3072]{1,0:T(8,128)(2,1)S(1)}, bf16[32,3072]{1,0:T(8,128)(2,1)S(1)}, u32[]{:S(2)}, u32[]{:S(2)}) %collective-permute-start.27) | collective-permute-done | bytes 196640 | tf_op jit(solution)/shard_map/ppermute | solution.py:374
  63.8 0.5 collective-permute-start.28
  64.3 1.6 %collective-permute-start.32 = (bf16[32,3072]{1,0:T(8,128)(2,1)S(1)}, bf16[32,3072]{1,0:T(8,128)(2,1)S(1)}, u32[]{:S(2)}, u32[]{:S(2)}) collective-permute-start(bf16[32,3072]{1,0:T(8,128)(2,1)S(1)} %add_step.18), channel_id=1, source_target_pairs={{0,2},{2,4},{4,6},{6,7},{7,5},{5,3},{3,1},{1,0},{8,10},{10,12},{12... | collective-permute-start | bytes 589832 | tf_op jit(solution)/shard_map/ppermute | solution.py:374
  65.9 2.0 %collective-permute-done.21.got_ref = bf16[32,3072]{1,0:T(8,128)(2,1)S(1)} collective-permute-done((bf16[32,3072]{1,0:T(8,128)(2,1)S(1)}, bf16[32,3072]{1,0:T(8,128)(2,1)S(1)}, u32[]{:S(2)}, u32[]{:S(2)}) %collective-permute-start.21) | collective-permute-done | bytes 196640 | tf_op jit(solution)/shard_map/ppermute | solution.py:374
  67.9 1.6 %collective-permute-start.22 = (bf16[32,3072]{1,0:T(8,128)(2,1)S(1)}, bf16[32,3072]{1,0:T(8,128)(2,1)S(1)}, u32[]{:S(2)}, u32[]{:S(2)}) collective-permute-start(bf16[32,3072]{1,0:T(8,128)(2,1)S(1)} %add_step.11), channel_id=1, source_target_pairs={{0,2},{2,4},{4,6},{6,7},{7,5},{5,3},{3,1},{1,0},{8,10},{10,12},{12... | collective-permute-start | bytes 589832 | tf_op jit(solution)/shard_map/ppermute | solution.py:374
  69.6 0.6 collective-permute-start.25
  70.2 1.9 %collective-permute-done.28.got_ref = bf16[32,3072]{1,0:T(8,128)(2,1)S(1)} collective-permute-done((bf16[32,3072]{1,0:T(8,128)(2,1)S(1)}, bf16[32,3072]{1,0:T(8,128)(2,1)S(1)}, u32[]{:S(2)}, u32[]{:S(2)}) %collective-permute-start.28) | collective-permute-done | bytes 196640 | tf_op jit(solution)/shard_map/ppermute | solution.py:374
  72.7 1.6 %collective-permute-start.33 = (bf16[32,3072]{1,0:T(8,128)(2,1)S(1)}, bf16[32,3072]{1,0:T(8,128)(2,1)S(1)}, u32[]{:S(2)}, u32[]{:S(2)}) collective-permute-start(bf16[32,3072]{1,0:T(8,128)(2,1)S(1)} %add_step.19), channel_id=1, source_target_pairs={{0,2},{2,4},{4,6},{6,7},{7,5},{5,3},{3,1},{1,0},{8,10},{10,12},{12... | collective-permute-start | bytes 589832 | tf_op jit(solution)/shard_map/ppermute | solution.py:374
  74.4 2.0 %collective-permute-done.22.got_first = bf16[32,3072]{1,0:T(8,128)(2,1)S(1)} collective-permute-done((bf16[32,3072]{1,0:T(8,128)(2,1)S(1)}, bf16[32,3072]{1,0:T(8,128)(2,1)S(1)}, u32[]{:S(2)}, u32[]{:S(2)}) %collective-permute-start.22) | collective-permute-done | bytes 196640 | tf_op jit(solution)/shard_map/ppermute | solution.py:374
  76.4 0.8 %collective-permute-done.25.got_second = bf16[32,3072]{1,0:T(8,128)(2,1)S(1)} collective-permute-done((bf16[32,3072]{1,0:T(8,128)(2,1)S(1)}, bf16[32,3072]{1,0:T(8,128)(2,1)S(1)}, u32[]{:S(2)}, u32[]{:S(2)}) %collective-permute-start.25) | collective-permute-done | bytes 196640 | tf_op jit(solution)/shard_map/ppermute | solution.py:374
  77.3 2.0 %collective-permute-done.29.first = bf16[32,3072]{1,0:T(8,128)(2,1)S(1)} collective-permute-done((bf16[32,3072]{1,0:T(8,128)(2,1)S(1)}, bf16[32,3072]{1,0:T(8,128)(2,1)S(1)}, u32[]{:S(2)}, u32[]{:S(2)}) %collective-permute-start.29) | collective-permute-done | bytes 196640 | tf_op jit(solution)/shard_map/ppermute | solution.py:374
  79.3 0.8 %finish.1 = bf16[32,6144]{1,0:T(8,128)(2,1)} custom-call(f32[2,32,3072]{2,1,0:T(8,128)S(1)} %add_own.1.gathered_ref, bf16[32,3072]{1,0:T(8,128)(2,1)S(1)} %collective-permute-done.29.first, bf16[32,3072]{1,0:T(8,128)(2,1)S(1)} %collective-permute-done.33.second), custom_call_target="tpu_custom_call" | custom-call | bytes 393216 | tf_op jit(solution)/shard_map/finish/pallas_call | solution.py:356
  (69 shorter events, 3.1 us)
Async XLA Ops:
  1.1 8.7 %collective-permute-start = (bf16[32,3072]{1,0:T(8,128)(2,1)S(1)}, bf16[32,3072]{1,0:T(8,128)(2,1)S(1)}, u32[]{:S(2)}, u32[]{:S(2)}) collective-permute-start(bf16[32,3072]{1,0:T(8,128)(2,1)S(1)} %get-tuple-element.70.refs_0_), channel_id=1, source_target_pairs={{0,2},{2,4},{4,6},{6,7},{7,5},{5,3},{3,1},{1,0},{8,10},{10,12},{12... | collective-permute-start | bytes 589832 | tf_op jit(solution)/shard_map/ppermute | solution.py:74
  4.1 7.8 %collective-permute-start.3 = (bf16[32,3072]{1,0:T(8,128)(2,1)S(1)}, bf16[32,3072]{1,0:T(8,128)(2,1)S(1)}, u32[]{:S(2)}, u32[]{:S(2)}) collective-permute-start(bf16[32,3072]{1,0:T(8,128)(2,1)S(1)} %get-tuple-element.70.refs_0_), channel_id=1, source_target_pairs={{2,0},{4,2},{6,4},{7,6},{5,7},{3,5},{1,3},{0,1},{10,8},{12,10},{14... | collective-permute-start | bytes 589832 | tf_op jit(solution)/shard_map/ppermute | solution.py:75
  4.1 9.9 %collective-permute-start.8 = (bf16[32,3072]{1,0:T(8,128)(2,1)S(1)}, bf16[32,3072]{1,0:T(8,128)(2,1)S(1)}, u32[]{:S(2)}, u32[]{:S(2)}) collective-permute-start(bf16[32,3072]{1,0:T(8,128)(2,1)S(1)} %get-tuple-element.69.refs_5_), channel_id=1, source_target_pairs={{0,2},{2,4},{4,6},{6,7},{7,5},{5,3},{3,1},{1,0},{8,10},{10,12},{12... | collective-permute-start | bytes 589832 | tf_op jit(solution)/shard_map/ppermute | solution.py:74
  6.2 10.0 %collective-permute-start.9 = (bf16[32,3072]{1,0:T(8,128)(2,1)S(1)}, bf16[32,3072]{1,0:T(8,128)(2,1)S(1)}, u32[]{:S(2)}, u32[]{:S(2)}) collective-permute-start(bf16[32,3072]{1,0:T(8,128)(2,1)S(1)} %get-tuple-element.69.refs_5_), channel_id=1, source_target_pairs={{2,0},{4,2},{6,4},{7,6},{5,7},{3,5},{1,3},{0,1},{10,8},{12,10},{14... | collective-permute-start | bytes 589832 | tf_op jit(solution)/shard_map/ppermute | solution.py:75
  9.8 8.4 %collective-permute-start.1 = (bf16[32,3072]{1,0:T(8,128)(2,1)S(1)}, bf16[32,3072]{1,0:T(8,128)(2,1)S(1)}, u32[]{:S(2)}, u32[]{:S(2)}) collective-permute-start(bf16[32,3072]{1,0:T(8,128)(2,1)S(1)} %collective-permute-done.refs_1_), channel_id=1, source_target_pairs={{0,2},{2,4},{4,6},{6,7},{7,5},{5,3},{3,1},{1,0},{8,10},{10,12},{12... | collective-permute-start | bytes 589832 | tf_op jit(solution)/shard_map/ppermute | solution.py:74
  12.0 8.4 %collective-permute-start.4 = (bf16[32,3072]{1,0:T(8,128)(2,1)S(1)}, bf16[32,3072]{1,0:T(8,128)(2,1)S(1)}, u32[]{:S(2)}, u32[]{:S(2)}) collective-permute-start(bf16[32,3072]{1,0:T(8,128)(2,1)S(1)} %collective-permute-done.3.refs_2_), channel_id=1, source_target_pairs={{2,0},{4,2},{6,4},{7,6},{5,7},{3,5},{1,3},{0,1},{10,8},{12,10},{14... | collective-permute-start | bytes 589832 | tf_op jit(solution)/shard_map/ppermute | solution.py:75
  14.0 8.4 %collective-permute-start.10 = (bf16[32,3072]{1,0:T(8,128)(2,1)S(1)}, bf16[32,3072]{1,0:T(8,128)(2,1)S(1)}, u32[]{:S(2)}, u32[]{:S(2)}) collective-permute-start(bf16[32,3072]{1,0:T(8,128)(2,1)S(1)} %collective-permute-done.8.refs_6_.arrived_ref), channel_id=1, source_target_pairs={{0,2},{2,4},{4,6},{6,7},{7,5},{5,3},{3,1},{1,0},{8,10},{10,12},{12... | collective-permute-start | bytes 589832 | tf_op jit(solution)/shard_map/ppermute | solution.py:74
  16.2 8.4 %collective-permute-start.11 = (bf16[32,3072]{1,0:T(8,128)(2,1)S(1)}, bf16[32,3072]{1,0:T(8,128)(2,1)S(1)}, u32[]{:S(2)}, u32[]{:S(2)}) collective-permute-start(bf16[32,3072]{1,0:T(8,128)(2,1)S(1)} %collective-permute-done.9.refs_7_.arrived_ref), channel_id=1, source_target_pairs={{2,0},{4,2},{6,4},{7,6},{5,7},{3,5},{1,3},{0,1},{10,8},{12,10},{14... | collective-permute-start | bytes 589832 | tf_op jit(solution)/shard_map/ppermute | solution.py:75
  16.2 12.7 %slice-start = ((s8[18874368]{0:T(1024)(128)(4,1)}), s8[4194304]{0:T(1024)(128)(4,1)S(1)}, s32[]{:S(2)}) async-start(s8[18874368]{0:T(1024)(128)(4,1)} %bitcast.1), calls=%async_computation | async-start | bytes 8388608
  16.2 12.8 %slice-start.1 = ((s8[18874368]{0:T(1024)(128)(4,1)}), s8[4194304]{0:T(1024)(128)(4,1)S(1)}, s32[]{:S(2)}) async-start(s8[18874368]{0:T(1024)(128)(4,1)} %bitcast.1), calls=%async_computation.1 | async-start | bytes 8388608
  16.2 12.8 %slice-start.2 = ((s8[18874368]{0:T(1024)(128)(4,1)}), s8[4194304]{0:T(1024)(128)(4,1)S(1)}, s32[]{:S(2)}) async-start(s8[18874368]{0:T(1024)(128)(4,1)} %bitcast.1), calls=%async_computation.2 | async-start | bytes 8388608
  16.2 12.8 %slice-start.3 = ((s8[18874368]{0:T(1024)(128)(4,1)}), s8[4194304]{0:T(1024)(128)(4,1)S(1)}, s32[]{:S(2)}) async-start(s8[18874368]{0:T(1024)(128)(4,1)} %bitcast.1), calls=%async_computation.3 | async-start | bytes 8388608
  16.2 12.7 %slice-start.4 = ((s8[18874368]{0:T(1024)(128)(4,1)}), s8[2097152]{0:T(1024)(128)(4,1)S(1)}, s32[]{:S(2)}) async-start(s8[18874368]{0:T(1024)(128)(4,1)} %bitcast.1), calls=%async_computation.4 | async-start | bytes 4194304
  18.2 8.4 %collective-permute-start.2 = (bf16[32,3072]{1,0:T(8,128)(2,1)S(1)}, bf16[32,3072]{1,0:T(8,128)(2,1)S(1)}, u32[]{:S(2)}, u32[]{:S(2)}) collective-permute-start(bf16[32,3072]{1,0:T(8,128)(2,1)S(1)} %collective-permute-done.1.refs_3_), channel_id=1, source_target_pairs={{0,2},{2,4},{4,6},{6,7},{7,5},{5,3},{3,1},{1,0},{8,10},{10,12},{12... | collective-permute-start | bytes 589832 | tf_op jit(solution)/shard_map/ppermute | solution.py:74
  20.4 8.5 %collective-permute-start.5 = (bf16[32,3072]{1,0:T(8,128)(2,1)S(1)}, bf16[32,3072]{1,0:T(8,128)(2,1)S(1)}, u32[]{:S(2)}, u32[]{:S(2)}) collective-permute-start(bf16[32,3072]{1,0:T(8,128)(2,1)S(1)} %collective-permute-done.4.refs_4_), channel_id=1, source_target_pairs={{2,0},{4,2},{6,4},{7,6},{5,7},{3,5},{1,3},{0,1},{10,8},{12,10},{14... | collective-permute-start | bytes 589832 | tf_op jit(solution)/shard_map/ppermute | solution.py:75
  22.4 8.4 %collective-permute-start.12 = (bf16[32,3072]{1,0:T(8,128)(2,1)S(1)}, bf16[32,3072]{1,0:T(8,128)(2,1)S(1)}, u32[]{:S(2)}, u32[]{:S(2)}) collective-permute-start(bf16[32,3072]{1,0:T(8,128)(2,1)S(1)} %collective-permute-done.10.refs_8_), channel_id=1, source_target_pairs={{0,2},{2,4},{4,6},{6,7},{7,5},{5,3},{3,1},{1,0},{8,10},{10,12},{12... | collective-permute-start | bytes 589832 | tf_op jit(solution)/shard_map/ppermute | solution.py:74
  24.6 8.4 %collective-permute-start.13 = (bf16[32,3072]{1,0:T(8,128)(2,1)S(1)}, bf16[32,3072]{1,0:T(8,128)(2,1)S(1)}, u32[]{:S(2)}, u32[]{:S(2)}) collective-permute-start(bf16[32,3072]{1,0:T(8,128)(2,1)S(1)} %collective-permute-done.11.refs_9_), channel_id=1, source_target_pairs={{2,0},{4,2},{6,4},{7,6},{5,7},{3,5},{1,3},{0,1},{10,8},{12,10},{14... | collective-permute-start | bytes 589832 | tf_op jit(solution)/shard_map/ppermute | solution.py:75
  26.6 7.6 %collective-permute-start.6 = (bf16[32,1536]{1,0:T(8,128)(2,1)S(1)}, bf16[32,1536]{1,0:T(8,128)(2,1)S(1)}, u32[]{:S(2)}, u32[]{:S(2)}) collective-permute-start(bf16[32,1536]{1,0:T(8,128)(2,1)S(1)} %slice.24), channel_id=1, source_target_pairs={{0,2},{2,4},{4,6},{6,7},{7,5},{5,3},{3,1},{1,0},{8,10},{10,12},{12... | collective-permute-start | bytes 294920 | tf_op jit(solution)/shard_map/ppermute | solution.py:78
  28.8 5.4 %collective-permute-start.7 = (bf16[32,1536]{1,0:T(8,128)(2,1)S(1)}, bf16[32,1536]{1,0:T(8,128)(2,1)S(1)}, u32[]{:S(2)}, u32[]{:S(2)}) collective-permute-start(bf16[32,1536]{1,0:T(8,128)(2,1)S(1)} %slice.25), channel_id=1, source_target_pairs={{2,0},{4,2},{6,4},{7,6},{5,7},{3,5},{1,3},{0,1},{10,8},{12,10},{14... | collective-permute-start | bytes 294920 | tf_op jit(solution)/shard_map/ppermute | solution.py:79
  30.8 4.7 %collective-permute-start.14 = (bf16[32,1536]{1,0:T(8,128)(2,1)S(1)}, bf16[32,1536]{1,0:T(8,128)(2,1)S(1)}, u32[]{:S(2)}, u32[]{:S(2)}) collective-permute-start(bf16[32,1536]{1,0:T(8,128)(2,1)S(1)} %slice.26), channel_id=1, source_target_pairs={{0,2},{2,4},{4,6},{6,7},{7,5},{5,3},{3,1},{1,0},{8,10},{10,12},{12... | collective-permute-start | bytes 294920 | tf_op jit(solution)/shard_map/ppermute | solution.py:78
  33.0 4.7 %collective-permute-start.15 = (bf16[32,1536]{1,0:T(8,128)(2,1)S(1)}, bf16[32,1536]{1,0:T(8,128)(2,1)S(1)}, u32[]{:S(2)}, u32[]{:S(2)}) collective-permute-start(bf16[32,1536]{1,0:T(8,128)(2,1)S(1)} %slice.27), channel_id=1, source_target_pairs={{2,0},{4,2},{6,4},{7,6},{5,7},{3,5},{1,3},{0,1},{10,8},{12,10},{14... | collective-permute-start | bytes 294920 | tf_op jit(solution)/shard_map/ppermute | solution.py:79
  38.5 1.5 %collective-permute-start.16 = (bf16[2,128,128]{2,1,0:T(8,128)(2,1)S(1)}, bf16[2,128,128]{2,1,0:T(8,128)(2,1)S(1)}, u32[]{:S(2)}, u32[]{:S(2)}) collective-permute-start(bf16[2,128,128]{2,1,0:T(8,128)(2,1)S(1)} %get-tuple-element.50.one_ref), channel_id=1, source_target_pairs={{0,8},{8,0},{16,24},{24,16},{1,9},{9,1},{17,25},{25,17},{2,10},{10... | collective-permute-start | bytes 196616 | tf_op jit(solution)/shard_map/ppermute | solution.py:410
  39.5 2.2 %collective-permute-start.18 = (bf16[2,128,128]{2,1,0:T(8,128)(2,1)S(1)}, bf16[2,128,128]{2,1,0:T(8,128)(2,1)S(1)}, u32[]{:S(2)}, u32[]{:S(2)}) collective-permute-start(bf16[2,128,128]{2,1,0:T(8,128)(2,1)S(1)} %get-tuple-element.51.one_ref), channel_id=1, source_target_pairs={{0,8},{8,0},{16,24},{24,16},{1,9},{9,1},{17,25},{25,17},{2,10},{10... | collective-permute-start | bytes 196616 | tf_op jit(solution)/shard_map/ppermute | solution.py:410
  40.1 4.8 %collective-permute-start.17 = (bf16[2,128,128]{2,1,0:T(8,128)(2,1)S(1)}, bf16[2,128,128]{2,1,0:T(8,128)(2,1)S(1)}, u32[]{:S(2)}, u32[]{:S(2)}) collective-permute-start(bf16[2,128,128]{2,1,0:T(8,128)(2,1)S(1)} %add_states.2.refs_0_), channel_id=1, source_target_pairs={{0,16},{8,24},{16,0},{24,8},{1,17},{9,25},{17,1},{25,9},{2,18},{10... | collective-permute-start | bytes 196616 | tf_op jit(solution)/shard_map/ppermute | solution.py:410
  41.7 4.3 %collective-permute-start.19 = (bf16[2,128,128]{2,1,0:T(8,128)(2,1)S(1)}, bf16[2,128,128]{2,1,0:T(8,128)(2,1)S(1)}, u32[]{:S(2)}, u32[]{:S(2)}) collective-permute-start(bf16[2,128,128]{2,1,0:T(8,128)(2,1)S(1)} %add_states.3), channel_id=1, source_target_pairs={{0,16},{8,24},{16,0},{24,8},{1,17},{9,25},{17,1},{25,9},{2,18},{10... | collective-permute-start | bytes 196616 | tf_op jit(solution)/shard_map/ppermute | solution.py:410
  42.5 3.5 %slice-start.5 = ((s8[6291456]{0:T(1024)(128)(4,1)}), s8[4194304]{0:T(1024)(128)(4,1)S(1)}, s32[]{:S(2)}) async-start(s8[6291456]{0:T(1024)(128)(4,1)} %bitcast.3), calls=%async_computation.5 | async-start | bytes 8388608
  42.5 3.5 %slice-start.6 = ((s8[6291456]{0:T(1024)(128)(4,1)}), s8[2097152]{0:T(1024)(128)(4,1)S(1)}, s32[]{:S(2)}) async-start(s8[6291456]{0:T(1024)(128)(4,1)} %bitcast.3), calls=%async_computation.6 | async-start | bytes 4194304
  42.5 3.5 %copy-start = (f32[4,128,128]{2,1,0:T(8,128)S(1)}, f32[4,128,128]{2,1,0:T(8,128)}, u32[]{:S(2)}) copy-start(f32[4,128,128]{2,1,0:T(8,128)} %initial_ref.1) | copy-start | bytes 786436
  42.5 3.5 %copy-start.1 = (f32[512]{0:T(512)S(1)}, f32[512]{0:T(512)}, u32[]{:S(2)}) copy-start(f32[512]{0:T(512)} %param.8) | copy-start | bytes 6148
  47.6 6.3 %collective-permute-start.26 = (bf16[32,3072]{1,0:T(8,128)(2,1)S(1)}, bf16[32,3072]{1,0:T(8,128)(2,1)S(1)}, u32[]{:S(2)}, u32[]{:S(2)}) collective-permute-start(bf16[32,3072]{1,0:T(8,128)(2,1)S(1)} %get-tuple-element.64), channel_id=1, source_target_pairs={{2,0},{4,2},{6,4},{7,6},{5,7},{3,5},{1,3},{0,1},{10,8},{12,10},{14... | collective-permute-start | bytes 589832 | tf_op jit(solution)/shard_map/ppermute | solution.py:374
  48.0 7.2 %collective-permute-start.30 = (bf16[32,3072]{1,0:T(8,128)(2,1)S(1)}, bf16[32,3072]{1,0:T(8,128)(2,1)S(1)}, u32[]{:S(2)}, u32[]{:S(2)}) collective-permute-start(bf16[32,3072]{1,0:T(8,128)(2,1)S(1)} %get-tuple-element.68), channel_id=1, source_target_pairs={{0,2},{2,4},{4,6},{6,7},{7,5},{5,3},{3,1},{1,0},{8,10},{10,12},{12... | collective-permute-start | bytes 589832 | tf_op jit(solution)/shard_map/ppermute | solution.py:374
  51.2 8.2 %collective-permute-start.20 = (bf16[32,3072]{1,0:T(8,128)(2,1)S(1)}, bf16[32,3072]{1,0:T(8,128)(2,1)S(1)}, u32[]{:S(2)}, u32[]{:S(2)}) collective-permute-start(bf16[32,3072]{1,0:T(8,128)(2,1)S(1)} %get-tuple-element.57), channel_id=1, source_target_pairs={{0,2},{2,4},{4,6},{6,7},{7,5},{5,3},{3,1},{1,0},{8,10},{10,12},{12... | collective-permute-start | bytes 589832 | tf_op jit(solution)/shard_map/ppermute | solution.py:374
  52.9 8.3 %collective-permute-start.23 = (bf16[32,3072]{1,0:T(8,128)(2,1)S(1)}, bf16[32,3072]{1,0:T(8,128)(2,1)S(1)}, u32[]{:S(2)}, u32[]{:S(2)}) collective-permute-start(bf16[32,3072]{1,0:T(8,128)(2,1)S(1)} %get-tuple-element.60), channel_id=1, source_target_pairs={{2,0},{4,2},{6,4},{7,6},{5,7},{3,5},{1,3},{0,1},{10,8},{12,10},{14... | collective-permute-start | bytes 589832 | tf_op jit(solution)/shard_map/ppermute | solution.py:374
  53.9 9.8 %collective-permute-start.27 = (bf16[32,3072]{1,0:T(8,128)(2,1)S(1)}, bf16[32,3072]{1,0:T(8,128)(2,1)S(1)}, u32[]{:S(2)}, u32[]{:S(2)}) collective-permute-start(bf16[32,3072]{1,0:T(8,128)(2,1)S(1)} %add_step.14), channel_id=1, source_target_pairs={{2,0},{4,2},{6,4},{7,6},{5,7},{3,5},{1,3},{0,1},{10,8},{12,10},{14... | collective-permute-start | bytes 589832 | tf_op jit(solution)/shard_map/ppermute | solution.py:374
  55.3 9.0 %collective-permute-start.31 = (bf16[32,3072]{1,0:T(8,128)(2,1)S(1)}, bf16[32,3072]{1,0:T(8,128)(2,1)S(1)}, u32[]{:S(2)}, u32[]{:S(2)}) collective-permute-start(bf16[32,3072]{1,0:T(8,128)(2,1)S(1)} %add_step.17), channel_id=1, source_target_pairs={{0,2},{2,4},{4,6},{6,7},{7,5},{5,3},{3,1},{1,0},{8,10},{10,12},{12... | collective-permute-start | bytes 589832 | tf_op jit(solution)/shard_map/ppermute | solution.py:374
  59.5 8.4 %collective-permute-start.21 = (bf16[32,3072]{1,0:T(8,128)(2,1)S(1)}, bf16[32,3072]{1,0:T(8,128)(2,1)S(1)}, u32[]{:S(2)}, u32[]{:S(2)}) collective-permute-start(bf16[32,3072]{1,0:T(8,128)(2,1)S(1)} %add_step.10), channel_id=1, source_target_pairs={{0,2},{2,4},{4,6},{6,7},{7,5},{5,3},{3,1},{1,0},{8,10},{10,12},{12... | collective-permute-start | bytes 589832 | tf_op jit(solution)/shard_map/ppermute | solution.py:374
  61.2 8.4 %collective-permute-start.24 = (bf16[32,3072]{1,0:T(8,128)(2,1)S(1)}, bf16[32,3072]{1,0:T(8,128)(2,1)S(1)}, u32[]{:S(2)}, u32[]{:S(2)}) collective-permute-start(bf16[32,3072]{1,0:T(8,128)(2,1)S(1)} %add_step.12), channel_id=1, source_target_pairs={{2,0},{4,2},{6,4},{7,6},{5,7},{3,5},{1,3},{0,1},{10,8},{12,10},{14... | collective-permute-start | bytes 589832 | tf_op jit(solution)/shard_map/ppermute | solution.py:374
  63.8 8.4 %collective-permute-start.28 = (bf16[32,3072]{1,0:T(8,128)(2,1)S(1)}, bf16[32,3072]{1,0:T(8,128)(2,1)S(1)}, u32[]{:S(2)}, u32[]{:S(2)}) collective-permute-start(bf16[32,3072]{1,0:T(8,128)(2,1)S(1)} %add_step.15), channel_id=1, source_target_pairs={{2,0},{4,2},{6,4},{7,6},{5,7},{3,5},{1,3},{0,1},{10,8},{12,10},{14... | collective-permute-start | bytes 589832 | tf_op jit(solution)/shard_map/ppermute | solution.py:374
  64.3 8.4 %collective-permute-start.32 = (bf16[32,3072]{1,0:T(8,128)(2,1)S(1)}, bf16[32,3072]{1,0:T(8,128)(2,1)S(1)}, u32[]{:S(2)}, u32[]{:S(2)}) collective-permute-start(bf16[32,3072]{1,0:T(8,128)(2,1)S(1)} %add_step.18), channel_id=1, source_target_pairs={{0,2},{2,4},{4,6},{6,7},{7,5},{5,3},{3,1},{1,0},{8,10},{10,12},{12... | collective-permute-start | bytes 589832 | tf_op jit(solution)/shard_map/ppermute | solution.py:374
  67.9 8.5 %collective-permute-start.22 = (bf16[32,3072]{1,0:T(8,128)(2,1)S(1)}, bf16[32,3072]{1,0:T(8,128)(2,1)S(1)}, u32[]{:S(2)}, u32[]{:S(2)}) collective-permute-start(bf16[32,3072]{1,0:T(8,128)(2,1)S(1)} %add_step.11), channel_id=1, source_target_pairs={{0,2},{2,4},{4,6},{6,7},{7,5},{5,3},{3,1},{1,0},{8,10},{10,12},{12... | collective-permute-start | bytes 589832 | tf_op jit(solution)/shard_map/ppermute | solution.py:374
  69.6 7.6 %collective-permute-start.25 = (bf16[32,3072]{1,0:T(8,128)(2,1)S(1)}, bf16[32,3072]{1,0:T(8,128)(2,1)S(1)}, u32[]{:S(2)}, u32[]{:S(2)}) collective-permute-start(bf16[32,3072]{1,0:T(8,128)(2,1)S(1)} %add_step.13), channel_id=1, source_target_pairs={{2,0},{4,2},{6,4},{7,6},{5,7},{3,5},{1,3},{0,1},{10,8},{12,10},{14... | collective-permute-start | bytes 589832 | tf_op jit(solution)/shard_map/ppermute | solution.py:374
  72.2 7.2 %collective-permute-start.29 = (bf16[32,3072]{1,0:T(8,128)(2,1)S(1)}, bf16[32,3072]{1,0:T(8,128)(2,1)S(1)}, u32[]{:S(2)}, u32[]{:S(2)}) collective-permute-start(bf16[32,3072]{1,0:T(8,128)(2,1)S(1)} %add_step.16), channel_id=1, source_target_pairs={{2,0},{4,2},{6,4},{7,6},{5,7},{3,5},{1,3},{0,1},{10,8},{12,10},{14... | collective-permute-start | bytes 589832 | tf_op jit(solution)/shard_map/ppermute | solution.py:374
  72.7 6.6 %collective-permute-start.33 = (bf16[32,3072]{1,0:T(8,128)(2,1)S(1)}, bf16[32,3072]{1,0:T(8,128)(2,1)S(1)}, u32[]{:S(2)}, u32[]{:S(2)}) collective-permute-start(bf16[32,3072]{1,0:T(8,128)(2,1)S(1)} %add_step.19), channel_id=1, source_target_pairs={{0,2},{2,4},{4,6},{6,7},{7,5},{5,3},{3,1},{1,0},{8,10},{10,12},{12... | collective-permute-start | bytes 589832 | tf_op jit(solution)/shard_map/ppermute | solution.py:374

commit v10 on v9

--- a/solution.py
+++ b/solution.py
@@ -65,31 +65,24 @@
 
 def ring_gather(block, size, right, left):
     half = block.shape[1] // 2
-    quarter = half // 2
     going_right = [block[:, :half], block[:, half:]]
     going_left = list(going_right)
     held = [[going_right[0]], [going_right[1]]]
-    for hop in range(1, size // 2):
+    for _ in range(1, size // 2):
         for part in range(2):
             going_right[part] = lax.ppermute(going_right[part], "fsdp", right)
-            going_left[part] = lax.ppermute(going_left[part], "fsdp", left)
+            going_left[1 - part] = lax.ppermute(going_left[1 - part], "fsdp", left)
+        for part in range(2):
             held[part] += [going_right[part], going_left[part]]
-    for part in range(2):
-        held[part].append(lax.ppermute(going_right[part][:, :quarter], "fsdp", right))
-        held[part].append(lax.ppermute(going_left[part][:, quarter:], "fsdp", left))
+    held[0].append(lax.ppermute(going_right[0], "fsdp", right))
+    held[1].append(lax.ppermute(going_left[1], "fsdp", left))
     return held
 
 
 def assemble(pieces, into, first_row):
     rows = pieces[0].shape[0]
-    row = first_row
-    column = 0
-    for piece in pieces:
-        width = piece.shape[1]
-        into[row : row + rows, column : column + width] = piece[...]
-        column = (column + width) % into.shape[1]
-        if column == 0:
-            row += rows
+    for place, piece in enumerate(pieces):
+        into[first_row + place * rows : first_row + (place + 1) * rows, :] = piece[...]
 
 
 def feature_map(projected):
@@ -141,68 +134,61 @@
     )(first_rows, second_rows, weight)
 
 
-def first_pass(pieces, first_rows, weight, early, after):
-    n_rows, half = first_rows.shape
-    columns = weight.shape[2]
-    count = len(pieces)
+def assemble_late(pieces, halves, early, after):
+    count = len(pieces[0])
 
     def body(*refs):
-        weight_ref, (out_ref, whole) = refs[count + 1], refs[-2:]
-        assemble(refs[:count], whole, early)
-        for place in range(2):
-            out_ref[place] = jnp.dot(whole[early:, :], weight_ref[1 + place, :half, :], preferred_element_type=F32)
-
-    return call(
-        body,
-        (
-            jax.ShapeDtypeStruct((2, n_rows - early, columns), F32),
-            jax.ShapeDtypeStruct((n_rows, half), BF16),
-        ),
-        [VMEM] * (count + 2) + [ANY] * len(after),
-        (VMEM, VMEM),
-        flops=4 * (n_rows - early) * half * columns,
-        nbytes=4 * half * columns,
-        input_output_aliases={count: 1},
-        name="first_pass",
-    )(*pieces, first_rows, weight, *after)
-
-
-def late_keys_and_values(pieces, second_rows, weight, first, feat_k, values, start, count, head_dim, early):
-    n_rows, half = second_rows.shape
+        for part in range(2):
+            assemble(refs[part * count : (part + 1) * count], refs[part - 2], early)
+
+    return call(
+        body,
+        [jax.ShapeDtypeStruct(half.shape, BF16) for half in halves],
+        [VMEM] * (2 * count + 2) + [ANY] * len(after),
+        [VMEM] * 2,
+        flops=HOP_FLOPS,
+        limit=4 << 20,
+        input_output_aliases={2 * count: 0, 2 * count + 1: 1},
+        name="assemble_late",
+    )(*pieces[0], *pieces[1], *halves, *after)
+
+
+def late_keys_and_values(far, halves, weight, feat_k, values, start, count, head_dim, early, after):
+    n_rows, half = halves[0].shape
     columns = count * head_dim
-    n_pieces = len(pieces)
+    n_far = len(far)
     span = slice(start * head_dim, start * head_dim + columns)
 
     def body(*refs):
-        weight_ref, first_ref = refs[n_pieces + 1 : n_pieces + 3]
-        rows_ref, feat_ref, values_ref, state_ref = refs[-4:]
-        if pieces:
-            assemble(refs[:n_pieces], rows_ref, early)
-        projected = first_ref[0, :, span] + jnp.dot(
-            rows_ref[early:, :], weight_ref[1, half:, span], preferred_element_type=F32
-        )
-        feat_ref[early:, span] = feature_map(projected).astype(BF16)
-        projected = first_ref[1, :, span] + jnp.dot(
-            rows_ref[early:, :], weight_ref[2, half:, span], preferred_element_type=F32
-        )
-        values_ref[early:, span] = projected.astype(BF16)
+        weight_ref = refs[n_far + 2]
+        rows_refs, (feat_ref, values_ref, state_ref) = refs[-5:-3], refs[-3:]
+        for piece, rows_ref in zip(refs[:n_far], rows_refs):
+            rows_ref[n_rows - piece.shape[0] :, :] = piece[...]
+
+        def product(which):
+            total = jnp.dot(rows_refs[0][early:, :], weight_ref[which, :half, span], preferred_element_type=F32)
+            return total + jnp.dot(rows_refs[1][early:, :], weight_ref[which, half:, span], preferred_element_type=F32)
+
+        feat_ref[early:, span] = feature_map(product(1)).astype(BF16)
+        values_ref[early:, span] = product(2).astype(BF16)
         for head in range(count):
             at = slice((start + head) * head_dim, (start + head + 1) * head_dim)
             state_ref[head] = lax.dot_general(
                 feat_ref[:, at], values_ref[:, at], (((0,), (0,)), ((), ())), preferred_element_type=F32
             ).astype(BF16)
 
-    return call(
-        body,
-        [jax.ShapeDtypeStruct(array.shape, BF16) for array in (second_rows, feat_k, values)]
+    out = call(
+        body,
+        [jax.ShapeDtypeStruct(array.shape, BF16) for array in (*halves, feat_k, values)]
         + [jax.ShapeDtypeStruct((count, head_dim, head_dim), BF16)],
-        [VMEM] * (n_pieces + 5),
-        [VMEM] * 4,
-        flops=4 * (n_rows - early) * half * columns if pieces else HOP_FLOPS,
-        nbytes=4 * half * columns,
-        input_output_aliases={n_pieces: 0, n_pieces + 3: 1, n_pieces + 4: 2},
+        [VMEM] * (n_far + 5) + [ANY] * len(after),
+        [VMEM] * 5,
+        flops=8 * (n_rows - early) * half * columns if far else HOP_FLOPS,
+        nbytes=8 * half * columns,
+        input_output_aliases={n_far: 0, n_far + 1: 1, n_far + 3: 2, n_far + 4: 3},
         name="late_keys_and_values",
-    )(*pieces, second_rows, weight, first, feat_k, values)
+    )(*far, *halves, weight, feat_k, values, *after)
+    return out[:2], *out[2:]
 
 
 def queries_within(halves, qkv_weight, feat_k, values, head_dim, size, rows):
@@ -425,24 +411,23 @@
     right, left = neighbours(n_fsdp)
     order = slots(n_fsdp)
 
-    half = width // 2
     held = ring_gather(tokens, n_fsdp, right, left)
 
     blocks = n_fsdp - 3
     early = blocks * rows
-    marks = [mark(held[1][1]), mark(held[1][2])]
-    feat_k, first_rows, second_rows = early_keys(held[0][:blocks], held[1][:blocks], qkv_weight, n_rows)
-    values = early_values(first_rows, second_rows, qkv_weight, early)
-    first, first_rows = first_pass(held[0][blocks:], first_rows, qkv_weight, early, [values, feat_k] + marks)
+    feat_k, *halves = early_keys(held[0][:blocks], held[1][:blocks], qkv_weight, n_rows)
+    values = early_values(*halves, qkv_weight, early)
+    halves = assemble_late([held[0][blocks:-1], held[1][blocks:-1]], halves, early, [values])
+    marks = [mark(held[0][1]), mark(held[1][2])]
     count = heads_here // 2 if heads_here % 2 == 0 else heads_here
     states = []
     for start in range(0, heads_here, count):
-        pieces = held[1][blocks:] if start == 0 else []
-        second_rows, feat_k, values, state = late_keys_and_values(
-            pieces, second_rows, qkv_weight, first, feat_k, values, start, count, head_dim, early
+        far = [held[0][-1], held[1][-1]] if start == 0 else []
+        halves, feat_k, values, state = late_keys_and_values(
+            far, halves, qkv_weight, feat_k, values, start, count, head_dim, early, marks if start == 0 else []
         )
         states.append(state)
-    feat_q, within = queries_within((first_rows, second_rows), qkv_weight, feat_k, values, head_dim, n_fsdp, rows)
+    feat_q, within = queries_within(halves, qkv_weight, feat_k, values, head_dim, n_fsdp, rows)
     exchanged = exchange_states(states, n_ctx)
     soon = 1
     normalized, parts = attend_and_project(

time: 80.3 us -> 81.1 us (level)
  waiting for transfers between devices: 30.4 us -> 34.1 us
  starting transfers between devices: 36.2 us -> 33.5 us
    ppermute x10 -> x8, waiting for transfers between devices: 2.43 us -> 9.49 us  [the longest x6 6.17 us: ring_gather(): going_left[1 - part] = lax.ppermute(going_left[1 - part], 'fsdp', left)]
    ppermute x7, waiting for transfers between devices: 7.18 us -> 12.7 us  [hop(): lax.ppermute(to_right, 'fsdp', right)]
    ppermute x6, waiting for transfers between devices: 12.3 us -> 7.63 us  [ring_gather(): going_right[part] = lax.ppermute(going_right[part], 'fsdp', right)]
    ppermute x7, waiting for transfers between devices: 7.37 us -> 3.12 us  [hop(): lax.ppermute(to_left, 'fsdp', left)]
    ppermute x10 -> x8, starting transfers between devices: 4.43 us -> 2.09 us  [the longest x1 1.63 us: ring_gather(): held[0].append(lax.ppermute(going_right[0], 'fsdp', right))]
  transfers between devices with their start and end apart: 34 -> 32, of which waited for: 18 -> 17; matrix products, arithmetic and copies ran while one was open for 0% -> 0% of each run, Pallas kernels for 11% -> 10%
where the time goes in v10:
time: 81.1 us; the launch traced here: 81 us
  waiting for transfers between devices  34.1 us (42%)
  starting transfers between devices  33.5 us (41%)
  Pallas kernels  12 us (15%)
  local copies, waits for them, and re-layouts  1.09 us (1%)
    ppermute x6, starting transfers between devices, ring_gather(): going_right[part] = lax.ppermute(going_right[part], 'fsdp', right)  13.6 us
    ppermute x7, waiting for transfers between devices, hop(): lax.ppermute(to_right, 'fsdp', right)  12.7 us
    ppermute x7, starting transfers between devices, hop(): lax.ppermute(to_left, 'fsdp', left)  11.3 us
    ppermute x6, waiting for transfers between devices, ring_gather(): going_right[part] = lax.ppermute(going_right[part], 'fsdp', right)  7.63 us
    ppermute x6, waiting for transfers between devices, ring_gather(): going_left[1 - part] = lax.ppermute(going_left[1 - part], 'fsdp', left)  6.17 us
    ppermute x7, starting transfers between devices, hop(): lax.ppermute(to_right, 'fsdp', right)  3.47 us
    ppermute x7, waiting for transfers between devices, hop(): lax.ppermute(to_left, 'fsdp', left)  3.12 us
    ppermute x4, starting transfers between devices, exchange_states(): received[at].append(lax.ppermute(total, 'ctx', pairs))  3.09 us
  transfers between devices with their start and end apart: 32, of which 17 were waited for; matrix products, arithmetic and copies ran while one was open for 0% of the time, Pallas kernels for 10%

profile of v10, /device:TPU:0, one launch (start us, length us, event | category | flops | bytes accessed | tf_op | source)
XLA Modules:
  0.0 81.0 jit_solution(9341381095839876046)
XLA Ops:
  0.0 1.0 %fusion = (bf16[32,3072]{1,0:T(8,128)(2,1)S(1)}, bf16[32,3072]{1,0:T(8,128)(2,1)S(1)}) fusion(bf16[32,6144]{1,0:T(8,128)(2,1)} %param.5), kind=kLoop, calls=%fused_computation | loop fusion | bytes 786432 | tf_op jit(solution)/shard_map/slice | solution.py:68
  1.1 3.1 %collective-permute-start = (bf16[32,3072]{1,0:T(8,128)(2,1)S(1)}, bf16[32,3072]{1,0:T(8,128)(2,1)S(1)}, u32[]{:S(2)}, u32[]{:S(2)}) collective-permute-start(bf16[32,3072]{1,0:T(8,128)(2,1)S(1)} %get-tuple-element.74.refs_0_), channel_id=1, source_target_pairs={{0,2},{2,4},{4,6},{6,7},{7,5},{5,3},{3,1},{1,0},{8,10},{10,12},{12... | collective-permute-start | bytes 589832 | tf_op jit(solution)/shard_map/ppermute | solution.py:73
  4.1 2.0 %collective-permute-start.11 = (bf16[32,3072]{1,0:T(8,128)(2,1)S(1)}, bf16[32,3072]{1,0:T(8,128)(2,1)S(1)}, u32[]{:S(2)}, u32[]{:S(2)}) collective-permute-start(bf16[32,3072]{1,0:T(8,128)(2,1)S(1)} %get-tuple-element.73.refs_5_), channel_id=1, source_target_pairs={{0,2},{2,4},{4,6},{6,7},{7,5},{5,3},{3,1},{1,0},{8,10},{10,12},{12... | collective-permute-start | bytes 589832 | tf_op jit(solution)/shard_map/ppermute | solution.py:73
  6.2 3.6 %collective-permute-done.refs_1_.arrived_ref = bf16[32,3072]{1,0:T(8,128)(2,1)S(1)} collective-permute-done((bf16[32,3072]{1,0:T(8,128)(2,1)S(1)}, bf16[32,3072]{1,0:T(8,128)(2,1)S(1)}, u32[]{:S(2)}, u32[]{:S(2)}) %collective-permute-start) | collective-permute-done | bytes 196640 | tf_op jit(solution)/shard_map/ppermute | solution.py:73
  9.8 2.1 %collective-permute-start.1 = (bf16[32,3072]{1,0:T(8,128)(2,1)S(1)}, bf16[32,3072]{1,0:T(8,128)(2,1)S(1)}, u32[]{:S(2)}, u32[]{:S(2)}) collective-permute-start(bf16[32,3072]{1,0:T(8,128)(2,1)S(1)} %collective-permute-done.refs_1_.arrived_ref), channel_id=1, source_target_pairs={{0,2},{2,4},{4,6},{6,7},{7,5},{5,3},{3,1},{1,0},{8,10},{10,12},{12... | collective-permute-start | bytes 589832 | tf_op jit(solution)/shard_map/ppermute | solution.py:73
  12.0 2.0 %collective-permute-done.11.refs_6_ = bf16[32,3072]{1,0:T(8,128)(2,1)S(1)} collective-permute-done((bf16[32,3072]{1,0:T(8,128)(2,1)S(1)}, bf16[32,3072]{1,0:T(8,128)(2,1)S(1)}, u32[]{:S(2)}, u32[]{:S(2)}) %collective-permute-start.11) | collective-permute-done | bytes 196640 | tf_op jit(solution)/shard_map/ppermute | solution.py:73
  14.0 2.1 %collective-permute-start.12 = (bf16[32,3072]{1,0:T(8,128)(2,1)S(1)}, bf16[32,3072]{1,0:T(8,128)(2,1)S(1)}, u32[]{:S(2)}, u32[]{:S(2)}) collective-permute-start(bf16[32,3072]{1,0:T(8,128)(2,1)S(1)} %collective-permute-done.11.refs_6_), channel_id=1, source_target_pairs={{0,2},{2,4},{4,6},{6,7},{7,5},{5,3},{3,1},{1,0},{8,10},{10,12},{12... | collective-permute-start | bytes 589832 | tf_op jit(solution)/shard_map/ppermute | solution.py:73
  16.2 2.0 %collective-permute-done.1.refs_3_ = bf16[32,3072]{1,0:T(8,128)(2,1)S(1)} collective-permute-done((bf16[32,3072]{1,0:T(8,128)(2,1)S(1)}, bf16[32,3072]{1,0:T(8,128)(2,1)S(1)}, u32[]{:S(2)}, u32[]{:S(2)}) %collective-permute-start.1) | collective-permute-done | bytes 196640 | tf_op jit(solution)/shard_map/ppermute | solution.py:73
  18.2 2.1 %collective-permute-start.2 = (bf16[32,3072]{1,0:T(8,128)(2,1)S(1)}, bf16[32,3072]{1,0:T(8,128)(2,1)S(1)}, u32[]{:S(2)}, u32[]{:S(2)}) collective-permute-start(bf16[32,3072]{1,0:T(8,128)(2,1)S(1)} %collective-permute-done.1.refs_3_), channel_id=1, source_target_pairs={{0,2},{2,4},{4,6},{6,7},{7,5},{5,3},{3,1},{1,0},{8,10},{10,12},{12... | collective-permute-start | bytes 589832 | tf_op jit(solution)/shard_map/ppermute | solution.py:73
  20.4 4.2 %collective-permute-done.9.refs_4_ = bf16[32,3072]{1,0:T(8,128)(2,1)S(1)} collective-permute-done((bf16[32,3072]{1,0:T(8,128)(2,1)S(1)}, bf16[32,3072]{1,0:T(8,128)(2,1)S(1)}, u32[]{:S(2)}, u32[]{:S(2)}) %collective-permute-start.9) | collective-permute-done | bytes 196640 | tf_op jit(solution)/shard_map/ppermute | solution.py:74
  24.6 2.0 %collective-permute-start.13 = (bf16[32,3072]{1,0:T(8,128)(2,1)S(1)}, bf16[32,3072]{1,0:T(8,128)(2,1)S(1)}, u32[]{:S(2)}, u32[]{:S(2)}) collective-permute-start(bf16[32,3072]{1,0:T(8,128)(2,1)S(1)} %collective-permute-done.12.refs_8_), channel_id=1, source_target_pairs={{0,2},{2,4},{4,6},{6,7},{7,5},{5,3},{3,1},{1,0},{8,10},{10,12},{12... | collective-permute-start | bytes 589832 | tf_op jit(solution)/shard_map/ppermute | solution.py:73
  26.7 1.2 %early_keys.1 = (bf16[256,512]{1,0:T(8,128)(2,1)S(1)}, bf16[256,3072]{1,0:T(8,128)(2,1)S(1)}, bf16[256,3072]{1,0:T(8,128)(2,1)S(1)}) custom-call(bf16[32,3072]{1,0:T(8,128)(2,1)S(1)} %get-tuple-element.74.refs_0_, bf16[32,3072]{1,0:T(8,128)(2,1)S(1)} %collective-permute-done.refs_1_.arrived_ref, bf16[32,3072]{1,0:T(8,128)(2,1)S(1)} %collective-permute-done.8.refs_2_, ...), custom_call_target="tpu_custom_call" | custom-call | flops 1006632960 | bytes 6291456 | tf_op jit(solution)/shard_map/early_keys/pallas_call | solution.py:106
  27.9 1.2 %early_values.1.refs_6_ = bf16[256,512]{1,0:T(8,128)(2,1)S(1)} custom-call(bf16[256,3072]{1,0:T(8,128)(2,1)S(1)} %get-tuple-element.39.first_ref.refs_4_, bf16[256,3072]{1,0:T(8,128)(2,1)S(1)} %get-tuple-element.40.second_ref.refs_5_, bf16[3,6144,512]{2,1,0:T(8,128)(2,1)S(1)} %bitcast.2), custom_call_target="tpu_custom_call" | custom-call | flops 1006632960 | bytes 6291456 | tf_op jit(solution)/shard_map/early_values/pallas_call | solution.py:126
  29.1 1.6 %collective-permute-start.3 = (bf16[32,3072]{1,0:T(8,128)(2,1)S(1)}, bf16[32,3072]{1,0:T(8,128)(2,1)S(1)}, u32[]{:S(2)}, u32[]{:S(2)}) collective-permute-start(bf16[32,3072]{1,0:T(8,128)(2,1)S(1)} %collective-permute-done.2.refs_0_), channel_id=1, source_target_pairs={{0,2},{2,4},{4,6},{6,7},{7,5},{5,3},{3,1},{1,0},{8,10},{10,12},{12... | collective-permute-start | bytes 589832 | tf_op jit(solution)/shard_map/ppermute | solution.py:77
  30.7 0.4 collective-permute-start.7
  31.2 1.8 %collective-permute-done.10.refs_1_ = bf16[32,3072]{1,0:T(8,128)(2,1)S(1)} collective-permute-done((bf16[32,3072]{1,0:T(8,128)(2,1)S(1)}, bf16[32,3072]{1,0:T(8,128)(2,1)S(1)}, u32[]{:S(2)}, u32[]{:S(2)}) %collective-permute-start.10) | collective-permute-done | bytes 196640 | tf_op jit(solution)/shard_map/ppermute | solution.py:74
  33.1 1.7 %collective-permute-done.3.refs_0_ = bf16[32,3072]{1,0:T(8,128)(2,1)S(1)} collective-permute-done((bf16[32,3072]{1,0:T(8,128)(2,1)S(1)}, bf16[32,3072]{1,0:T(8,128)(2,1)S(1)}, u32[]{:S(2)}, u32[]{:S(2)}) %collective-permute-start.3) | collective-permute-done | bytes 196640 | tf_op jit(solution)/shard_map/ppermute | solution.py:77
  34.8 1.6 %collective-permute-done.7.refs_1_ = bf16[32,3072]{1,0:T(8,128)(2,1)S(1)} collective-permute-done((bf16[32,3072]{1,0:T(8,128)(2,1)S(1)}, bf16[32,3072]{1,0:T(8,128)(2,1)S(1)}, u32[]{:S(2)}, u32[]{:S(2)}) %collective-permute-start.7) | collective-permute-done | bytes 196640 | tf_op jit(solution)/shard_map/ppermute | solution.py:78
  36.4 1.4 %late_keys_and_values.2 = (bf16[256,3072]{1,0:T(8,128)(2,1)S(1)}, bf16[256,3072]{1,0:T(8,128)(2,1)S(1)}, bf16[256,512]{1,0:T(8,128)(2,1)S(1)}, bf16[256,512]{1,0:T(8,128)(2,1)S(1)}, bf16[2,128,128]{2,1,0:T(8,128)(2,1)S(1)}) custom-call(bf16[32,3072]{1,0:T(8,128)(2,1)S(1)} %collective-permute-, ...), custom_call_target="tpu_custom_call", output_to_operand_aliasing={{0}: (2, {}), {1}: (3, {}), {2}: (5, {}), {3}: (6, {})} | custom-call | flops 603979776 | bytes 6291456 | tf_op jit(solution)/shard_map/late_keys_and_values/pallas_call | solution.py:180
  37.8 1.4 %late_keys_and_values.3 = (bf16[256,3072]{1,0:T(8,128)(2,1)S(1)}, bf16[256,3072]{1,0:T(8,128)(2,1)S(1)}, bf16[256,512]{1,0:T(8,128)(2,1)S(1)}, bf16[256,512]{1,0:T(8,128)(2,1)S(1)}, bf16[2,128,128]{2,1,0:T(8,128)(2,1)S(1)}) custom-call(bf16[256,3072]{1,0:T(8,128)(2,1)S(1)} %get-tuple-element., ...), custom_call_target="tpu_custom_call", output_to_operand_aliasing={{0}: (0, {}), {1}: (1, {}), {2}: (3, {}), {3}: (4, {})} | custom-call | flops 5000000000 | bytes 6291456 | tf_op jit(solution)/shard_map/late_keys_and_values/pallas_call | solution.py:180
  39.2 0.6 collective-permute-start.16
  39.8 1.6 %collective-permute-start.15 = (bf16[2,128,128]{2,1,0:T(8,128)(2,1)S(1)}, bf16[2,128,128]{2,1,0:T(8,128)(2,1)S(1)}, u32[]{:S(2)}, u32[]{:S(2)}) collective-permute-start(bf16[2,128,128]{2,1,0:T(8,128)(2,1)S(1)} %add_states.2.refs_0_), channel_id=1, source_target_pairs={{0,16},{8,24},{16,0},{24,8},{1,17},{9,25},{17,1},{25,9},{2,18},{10... | collective-permute-start | bytes 196616 | tf_op jit(solution)/shard_map/ppermute | solution.py:396
  41.4 0.9 %collective-permute-start.17 = (bf16[2,128,128]{2,1,0:T(8,128)(2,1)S(1)}, bf16[2,128,128]{2,1,0:T(8,128)(2,1)S(1)}, u32[]{:S(2)}, u32[]{:S(2)}) collective-permute-start(bf16[2,128,128]{2,1,0:T(8,128)(2,1)S(1)} %add_states.3), channel_id=1, source_target_pairs={{0,16},{8,24},{16,0},{24,8},{1,17},{9,25},{17,1},{25,9},{2,18},{10... | collective-permute-start | bytes 196616 | tf_op jit(solution)/shard_map/ppermute | solution.py:396
  42.3 2.3 %queries_within.1 = (bf16[256,512]{1,0:T(8,128)(2,1)S(1)}, f32[256,512]{1,0:T(8,128)S(1)}) custom-call(bf16[256,3072]{1,0:T(8,128)(2,1)S(1)} %get-tuple-element.48.first_ref, bf16[256,3072]{1,0:T(8,128)(2,1)S(1)} %get-tuple-element.49.second_ref, bf16[3,6144,512]{2,1,0:T(8,128)(2,1)S(1)} %bitcast.2, bf16[256,512]{1,0:T(8,128)(2,1)S(1)} %get-tuple-element.50.k_ref, ...), custom_call_target="tpu_custom_call" | custom-call | flops 1744830464 | bytes 6291456 | tf_op jit(solution)/shard_map/queries_within/pallas_call | solution.py:224
  44.6 1.1 %collective-permute-done.17.refs_3_ = bf16[2,128,128]{2,1,0:T(8,128)(2,1)S(1)} collective-permute-done((bf16[2,128,128]{2,1,0:T(8,128)(2,1)S(1)}, bf16[2,128,128]{2,1,0:T(8,128)(2,1)S(1)}, u32[]{:S(2)}, u32[]{:S(2)}) %collective-permute-start.17) | collective-permute-done | bytes 65568 | tf_op jit(solution)/shard_map/ppermute | solution.py:396
  45.8 1.5 %attend_and_project.1 = (bf16[256,512]{1,0:T(8,128)(2,1)S(1)}, bf16[32,3072]{1,0:T(8,128)(2,1)S(1)}, bf16[32,3072]{1,0:T(8,128)(2,1)S(1)}) custom-call(bf16[256,512]{1,0:T(8,128)(2,1)S(1)} %get-tuple-element.52.q_ref, f32[256,512]{1,0:T(8,128)S(1)} %get-tuple-element.53.within_ref, f32[4,128,128]{2,1,0:T(8,128)S(1)} %copy-done, f32[1,512]{1,0:T(1,128)S(1)} %bitcast.5, ...), custom_call_target="tpu_custom_call" | custom-call | flops 1610612736 | bytes 6291456 | tf_op jit(solution)/shard_map/attend_and_project/pallas_call | solution.py:272
  47.3 1.6 %collective-permute-start.28 = (bf16[32,3072]{1,0:T(8,128)(2,1)S(1)}, bf16[32,3072]{1,0:T(8,128)(2,1)S(1)}, u32[]{:S(2)}, u32[]{:S(2)}) collective-permute-start(bf16[32,3072]{1,0:T(8,128)(2,1)S(1)} %get-tuple-element.72), channel_id=1, source_target_pairs={{0,2},{2,4},{4,6},{6,7},{7,5},{5,3},{3,1},{1,0},{8,10},{10,12},{12... | collective-permute-start | bytes 589832 | tf_op jit(solution)/shard_map/ppermute | solution.py:360
  49.4 1.6 %project_rest.1 = (bf16[32,3072]{1,0:T(8,128)(2,1)S(1)}, bf16[32,3072]{1,0:T(8,128)(2,1)S(1)}, bf16[32,3072]{1,0:T(8,128)(2,1)S(1)}, bf16[32,3072]{1,0:T(8,128)(...) custom-call(bf16[256,512]{1,0:T(8,128)(2,1)S(1)} %get-tuple-element., ...), custom_call_target="tpu_custom_call" | custom-call | flops 5000000000 | bytes 6291456 | tf_op jit(solution)/shard_map/project_rest/pallas_call | solution.py:291
  51.0 0.5 collective-permute-start.21
  51.5 1.6 %collective-permute-start.18 = (bf16[32,3072]{1,0:T(8,128)(2,1)S(1)}, bf16[32,3072]{1,0:T(8,128)(2,1)S(1)}, u32[]{:S(2)}, u32[]{:S(2)}) collective-permute-start(bf16[32,3072]{1,0:T(8,128)(2,1)S(1)} %get-tuple-element.61), channel_id=1, source_target_pairs={{0,2},{2,4},{4,6},{6,7},{7,5},{5,3},{3,1},{1,0},{8,10},{10,12},{12... | collective-permute-start | bytes 589832 | tf_op jit(solution)/shard_map/ppermute | solution.py:360
  53.0 1.4 %collective-permute-done.28.got_ref = bf16[32,3072]{1,0:T(8,128)(2,1)S(1)} collective-permute-done((bf16[32,3072]{1,0:T(8,128)(2,1)S(1)}, bf16[32,3072]{1,0:T(8,128)(2,1)S(1)}, u32[]{:S(2)}, u32[]{:S(2)}) %collective-permute-start.28) | collective-permute-done | bytes 196640 | tf_op jit(solution)/shard_map/ppermute | solution.py:360
  54.5 1.6 %collective-permute-start.29 = (bf16[32,3072]{1,0:T(8,128)(2,1)S(1)}, bf16[32,3072]{1,0:T(8,128)(2,1)S(1)}, u32[]{:S(2)}, u32[]{:S(2)}) collective-permute-start(bf16[32,3072]{1,0:T(8,128)(2,1)S(1)} %add_step.17), channel_id=1, source_target_pairs={{0,2},{2,4},{4,6},{6,7},{7,5},{5,3},{3,1},{1,0},{8,10},{10,12},{12... | collective-permute-start | bytes 589832 | tf_op jit(solution)/shard_map/ppermute | solution.py:360
  56.1 0.6 collective-permute-done.24.got_ref
  56.8 0.5 collective-permute-start.25
  57.3 3.7 %collective-permute-done.21.got_ref = bf16[32,3072]{1,0:T(8,128)(2,1)S(1)} collective-permute-done((bf16[32,3072]{1,0:T(8,128)(2,1)S(1)}, bf16[32,3072]{1,0:T(8,128)(2,1)S(1)}, u32[]{:S(2)}, u32[]{:S(2)}) %collective-permute-start.21) | collective-permute-done | bytes 196640 | tf_op jit(solution)/shard_map/ppermute | solution.py:360
  61.0 0.5 collective-permute-start.22
  61.6 1.6 %collective-permute-start.19 = (bf16[32,3072]{1,0:T(8,128)(2,1)S(1)}, bf16[32,3072]{1,0:T(8,128)(2,1)S(1)}, u32[]{:S(2)}, u32[]{:S(2)}) collective-permute-start(bf16[32,3072]{1,0:T(8,128)(2,1)S(1)} %add_step.10), channel_id=1, source_target_pairs={{0,2},{2,4},{4,6},{6,7},{7,5},{5,3},{3,1},{1,0},{8,10},{10,12},{12... | collective-permute-start | bytes 589832 | tf_op jit(solution)/shard_map/ppermute | solution.py:360
  63.6 1.6 %collective-permute-start.30 = (bf16[32,3072]{1,0:T(8,128)(2,1)S(1)}, bf16[32,3072]{1,0:T(8,128)(2,1)S(1)}, u32[]{:S(2)}, u32[]{:S(2)}) collective-permute-start(bf16[32,3072]{1,0:T(8,128)(2,1)S(1)} %add_step.18), channel_id=1, source_target_pairs={{0,2},{2,4},{4,6},{6,7},{7,5},{5,3},{3,1},{1,0},{8,10},{10,12},{12... | collective-permute-start | bytes 589832 | tf_op jit(solution)/shard_map/ppermute | solution.py:360
  65.3 0.5 collective-permute-start.26
  65.8 3.6 %collective-permute-done.22.got_ref = bf16[32,3072]{1,0:T(8,128)(2,1)S(1)} collective-permute-done((bf16[32,3072]{1,0:T(8,128)(2,1)S(1)}, bf16[32,3072]{1,0:T(8,128)(2,1)S(1)}, u32[]{:S(2)}, u32[]{:S(2)}) %collective-permute-start.22) | collective-permute-done | bytes 196640 | tf_op jit(solution)/shard_map/ppermute | solution.py:360
  69.4 0.5 collective-permute-start.23
  70.0 1.6 %collective-permute-start.20 = (bf16[32,3072]{1,0:T(8,128)(2,1)S(1)}, bf16[32,3072]{1,0:T(8,128)(2,1)S(1)}, u32[]{:S(2)}, u32[]{:S(2)}) collective-permute-start(bf16[32,3072]{1,0:T(8,128)(2,1)S(1)} %add_step.11), channel_id=1, source_target_pairs={{0,2},{2,4},{4,6},{6,7},{7,5},{5,3},{3,1},{1,0},{8,10},{10,12},{12... | collective-permute-start | bytes 589832 | tf_op jit(solution)/shard_map/ppermute | solution.py:360
  72.1 1.6 %collective-permute-start.31 = (bf16[32,3072]{1,0:T(8,128)(2,1)S(1)}, bf16[32,3072]{1,0:T(8,128)(2,1)S(1)}, u32[]{:S(2)}, u32[]{:S(2)}) collective-permute-start(bf16[32,3072]{1,0:T(8,128)(2,1)S(1)} %add_step.19), channel_id=1, source_target_pairs={{0,2},{2,4},{4,6},{6,7},{7,5},{5,3},{3,1},{1,0},{8,10},{10,12},{12... | collective-permute-start | bytes 589832 | tf_op jit(solution)/shard_map/ppermute | solution.py:360
  73.8 0.5 collective-permute-start.27
  74.3 3.5 %collective-permute-done.23.got_second = bf16[32,3072]{1,0:T(8,128)(2,1)S(1)} collective-permute-done((bf16[32,3072]{1,0:T(8,128)(2,1)S(1)}, bf16[32,3072]{1,0:T(8,128)(2,1)S(1)}, u32[]{:S(2)}, u32[]{:S(2)}) %collective-permute-start.23) | collective-permute-done | bytes 196640 | tf_op jit(solution)/shard_map/ppermute | solution.py:360
  77.9 1.0 %collective-permute-done.31.second = bf16[32,3072]{1,0:T(8,128)(2,1)S(1)} collective-permute-done((bf16[32,3072]{1,0:T(8,128)(2,1)S(1)}, bf16[32,3072]{1,0:T(8,128)(2,1)S(1)}, u32[]{:S(2)}, u32[]{:S(2)}) %collective-permute-start.31) | collective-permute-done | bytes 196640 | tf_op jit(solution)/shard_map/ppermute | solution.py:360
  78.9 1.3 %collective-permute-done.27.first = bf16[32,3072]{1,0:T(8,128)(2,1)S(1)} collective-permute-done((bf16[32,3072]{1,0:T(8,128)(2,1)S(1)}, bf16[32,3072]{1,0:T(8,128)(2,1)S(1)}, u32[]{:S(2)}, u32[]{:S(2)}) %collective-permute-start.27) | collective-permute-done | bytes 196640 | tf_op jit(solution)/shard_map/ppermute | solution.py:360
  80.2 0.8 %finish.1 = bf16[32,6144]{1,0:T(8,128)(2,1)} custom-call(f32[2,32,3072]{2,1,0:T(8,128)S(1)} %add_own.1.gathered_ref, bf16[32,3072]{1,0:T(8,128)(2,1)S(1)} %collective-permute-done.27.first, bf16[32,3072]{1,0:T(8,128)(2,1)S(1)} %collective-permute-done.31.second), custom_call_target="tpu_custom_call" | custom-call | bytes 393216 | tf_op jit(solution)/shard_map/finish/pallas_call | solution.py:342
  (61 shorter events, 2.1 us)
Async XLA Ops:
  1.1 8.7 %collective-permute-start = (bf16[32,3072]{1,0:T(8,128)(2,1)S(1)}, bf16[32,3072]{1,0:T(8,128)(2,1)S(1)}, u32[]{:S(2)}, u32[]{:S(2)}) collective-permute-start(bf16[32,3072]{1,0:T(8,128)(2,1)S(1)} %get-tuple-element.74.refs_0_), channel_id=1, source_target_pairs={{0,2},{2,4},{4,6},{6,7},{7,5},{5,3},{3,1},{1,0},{8,10},{10,12},{12... | collective-permute-start | bytes 589832 | tf_op jit(solution)/shard_map/ppermute | solution.py:73
  4.1 7.8 %collective-permute-start.4 = (bf16[32,3072]{1,0:T(8,128)(2,1)S(1)}, bf16[32,3072]{1,0:T(8,128)(2,1)S(1)}, u32[]{:S(2)}, u32[]{:S(2)}) collective-permute-start(bf16[32,3072]{1,0:T(8,128)(2,1)S(1)} %get-tuple-element.73.refs_5_), channel_id=1, source_target_pairs={{2,0},{4,2},{6,4},{7,6},{5,7},{3,5},{1,3},{0,1},{10,8},{12,10},{14... | collective-permute-start | bytes 589832 | tf_op jit(solution)/shard_map/ppermute | solution.py:74
  4.1 9.9 %collective-permute-start.11 = (bf16[32,3072]{1,0:T(8,128)(2,1)S(1)}, bf16[32,3072]{1,0:T(8,128)(2,1)S(1)}, u32[]{:S(2)}, u32[]{:S(2)}) collective-permute-start(bf16[32,3072]{1,0:T(8,128)(2,1)S(1)} %get-tuple-element.73.refs_5_), channel_id=1, source_target_pairs={{0,2},{2,4},{4,6},{6,7},{7,5},{5,3},{3,1},{1,0},{8,10},{10,12},{12... | collective-permute-start | bytes 589832 | tf_op jit(solution)/shard_map/ppermute | solution.py:73
  6.2 10.0 %collective-permute-start.8 = (bf16[32,3072]{1,0:T(8,128)(2,1)S(1)}, bf16[32,3072]{1,0:T(8,128)(2,1)S(1)}, u32[]{:S(2)}, u32[]{:S(2)}) collective-permute-start(bf16[32,3072]{1,0:T(8,128)(2,1)S(1)} %get-tuple-element.74.refs_0_), channel_id=1, source_target_pairs={{2,0},{4,2},{6,4},{7,6},{5,7},{3,5},{1,3},{0,1},{10,8},{12,10},{14... | collective-permute-start | bytes 589832 | tf_op jit(solution)/shard_map/ppermute | solution.py:74
  9.8 8.4 %collective-permute-start.1 = (bf16[32,3072]{1,0:T(8,128)(2,1)S(1)}, bf16[32,3072]{1,0:T(8,128)(2,1)S(1)}, u32[]{:S(2)}, u32[]{:S(2)}) collective-permute-start(bf16[32,3072]{1,0:T(8,128)(2,1)S(1)} %collective-permute-done.refs_1_.arrived_ref), channel_id=1, source_target_pairs={{0,2},{2,4},{4,6},{6,7},{7,5},{5,3},{3,1},{1,0},{8,10},{10,12},{12... | collective-permute-start | bytes 589832 | tf_op jit(solution)/shard_map/ppermute | solution.py:73
  12.0 8.4 %collective-permute-start.5 = (bf16[32,3072]{1,0:T(8,128)(2,1)S(1)}, bf16[32,3072]{1,0:T(8,128)(2,1)S(1)}, u32[]{:S(2)}, u32[]{:S(2)}) collective-permute-start(bf16[32,3072]{1,0:T(8,128)(2,1)S(1)} %collective-permute-done.4.refs_7_.arrived_ref), channel_id=1, source_target_pairs={{2,0},{4,2},{6,4},{7,6},{5,7},{3,5},{1,3},{0,1},{10,8},{12,10},{14... | collective-permute-start | bytes 589832 | tf_op jit(solution)/shard_map/ppermute | solution.py:74
  14.0 10.6 %collective-permute-start.12 = (bf16[32,3072]{1,0:T(8,128)(2,1)S(1)}, bf16[32,3072]{1,0:T(8,128)(2,1)S(1)}, u32[]{:S(2)}, u32[]{:S(2)}) collective-permute-start(bf16[32,3072]{1,0:T(8,128)(2,1)S(1)} %collective-permute-done.11.refs_6_), channel_id=1, source_target_pairs={{0,2},{2,4},{4,6},{6,7},{7,5},{5,3},{3,1},{1,0},{8,10},{10,12},{12... | collective-permute-start | bytes 589832 | tf_op jit(solution)/shard_map/ppermute | solution.py:73
  16.2 8.4 %collective-permute-start.9 = (bf16[32,3072]{1,0:T(8,128)(2,1)S(1)}, bf16[32,3072]{1,0:T(8,128)(2,1)S(1)}, u32[]{:S(2)}, u32[]{:S(2)}) collective-permute-start(bf16[32,3072]{1,0:T(8,128)(2,1)S(1)} %collective-permute-done.8.refs_2_), channel_id=1, source_target_pairs={{2,0},{4,2},{6,4},{7,6},{5,7},{3,5},{1,3},{0,1},{10,8},{12,10},{14... | collective-permute-start | bytes 589832 | tf_op jit(solution)/shard_map/ppermute | solution.py:74
  16.2 10.5 %slice-start = ((s8[18874368]{0:T(1024)(128)(4,1)}), s8[4194304]{0:T(1024)(128)(4,1)S(1)}, s32[]{:S(2)}) async-start(s8[18874368]{0:T(1024)(128)(4,1)} %bitcast.1), calls=%async_computation | async-start | bytes 8388608
  16.2 10.5 %slice-start.1 = ((s8[18874368]{0:T(1024)(128)(4,1)}), s8[4194304]{0:T(1024)(128)(4,1)S(1)}, s32[]{:S(2)}) async-start(s8[18874368]{0:T(1024)(128)(4,1)} %bitcast.1), calls=%async_computation.1 | async-start | bytes 8388608
  16.2 10.5 %slice-start.2 = ((s8[18874368]{0:T(1024)(128)(4,1)}), s8[4194304]{0:T(1024)(128)(4,1)S(1)}, s32[]{:S(2)}) async-start(s8[18874368]{0:T(1024)(128)(4,1)} %bitcast.1), calls=%async_computation.2 | async-start | bytes 8388608
  16.2 10.4 %slice-start.3 = ((s8[18874368]{0:T(1024)(128)(4,1)}), s8[4194304]{0:T(1024)(128)(4,1)S(1)}, s32[]{:S(2)}) async-start(s8[18874368]{0:T(1024)(128)(4,1)} %bitcast.1), calls=%async_computation.3 | async-start | bytes 8388608
  16.2 10.4 %slice-start.4 = ((s8[18874368]{0:T(1024)(128)(4,1)}), s8[2097152]{0:T(1024)(128)(4,1)S(1)}, s32[]{:S(2)}) async-start(s8[18874368]{0:T(1024)(128)(4,1)} %bitcast.1), calls=%async_computation.4 | async-start | bytes 4194304
  18.2 10.9 %collective-permute-start.2 = (bf16[32,3072]{1,0:T(8,128)(2,1)S(1)}, bf16[32,3072]{1,0:T(8,128)(2,1)S(1)}, u32[]{:S(2)}, u32[]{:S(2)}) collective-permute-start(bf16[32,3072]{1,0:T(8,128)(2,1)S(1)} %collective-permute-done.1.refs_3_), channel_id=1, source_target_pairs={{0,2},{2,4},{4,6},{6,7},{7,5},{5,3},{3,1},{1,0},{8,10},{10,12},{12... | collective-permute-start | bytes 589832 | tf_op jit(solution)/shard_map/ppermute | solution.py:73
  20.4 10.3 %collective-permute-start.6 = (bf16[32,3072]{1,0:T(8,128)(2,1)S(1)}, bf16[32,3072]{1,0:T(8,128)(2,1)S(1)}, u32[]{:S(2)}, u32[]{:S(2)}) collective-permute-start(bf16[32,3072]{1,0:T(8,128)(2,1)S(1)} %collective-permute-done.5.refs_9_), channel_id=1, source_target_pairs={{2,0},{4,2},{6,4},{7,6},{5,7},{3,5},{1,3},{0,1},{10,8},{12,10},{14... | collective-permute-start | bytes 589832 | tf_op jit(solution)/shard_map/ppermute | solution.py:74
  24.6 8.4 %collective-permute-start.10 = (bf16[32,3072]{1,0:T(8,128)(2,1)S(1)}, bf16[32,3072]{1,0:T(8,128)(2,1)S(1)}, u32[]{:S(2)}, u32[]{:S(2)}) collective-permute-start(bf16[32,3072]{1,0:T(8,128)(2,1)S(1)} %collective-permute-done.9.refs_4_), channel_id=1, source_target_pairs={{2,0},{4,2},{6,4},{7,6},{5,7},{3,5},{1,3},{0,1},{10,8},{12,10},{14... | collective-permute-start | bytes 589832 | tf_op jit(solution)/shard_map/ppermute | solution.py:74
  24.6 8.4 %collective-permute-start.13 = (bf16[32,3072]{1,0:T(8,128)(2,1)S(1)}, bf16[32,3072]{1,0:T(8,128)(2,1)S(1)}, u32[]{:S(2)}, u32[]{:S(2)}) collective-permute-start(bf16[32,3072]{1,0:T(8,128)(2,1)S(1)} %collective-permute-done.12.refs_8_), channel_id=1, source_target_pairs={{0,2},{2,4},{4,6},{6,7},{7,5},{5,3},{3,1},{1,0},{8,10},{10,12},{12... | collective-permute-start | bytes 589832 | tf_op jit(solution)/shard_map/ppermute | solution.py:73
  29.1 5.7 %collective-permute-start.3 = (bf16[32,3072]{1,0:T(8,128)(2,1)S(1)}, bf16[32,3072]{1,0:T(8,128)(2,1)S(1)}, u32[]{:S(2)}, u32[]{:S(2)}) collective-permute-start(bf16[32,3072]{1,0:T(8,128)(2,1)S(1)} %collective-permute-done.2.refs_0_), channel_id=1, source_target_pairs={{0,2},{2,4},{4,6},{6,7},{7,5},{5,3},{3,1},{1,0},{8,10},{10,12},{12... | collective-permute-start | bytes 589832 | tf_op jit(solution)/shard_map/ppermute | solution.py:77
  30.7 5.7 %collective-permute-start.7 = (bf16[32,3072]{1,0:T(8,128)(2,1)S(1)}, bf16[32,3072]{1,0:T(8,128)(2,1)S(1)}, u32[]{:S(2)}, u32[]{:S(2)}) collective-permute-start(bf16[32,3072]{1,0:T(8,128)(2,1)S(1)} %collective-permute-done.6.refs_3_), channel_id=1, source_target_pairs={{2,0},{4,2},{6,4},{7,6},{5,7},{3,5},{1,3},{0,1},{10,8},{12,10},{14... | collective-permute-start | bytes 589832 | tf_op jit(solution)/shard_map/ppermute | solution.py:78
  37.8 2.0 %collective-permute-start.14 = (bf16[2,128,128]{2,1,0:T(8,128)(2,1)S(1)}, bf16[2,128,128]{2,1,0:T(8,128)(2,1)S(1)}, u32[]{:S(2)}, u32[]{:S(2)}) collective-permute-start(bf16[2,128,128]{2,1,0:T(8,128)(2,1)S(1)} %get-tuple-element.54.one_ref), channel_id=1, source_target_pairs={{0,8},{8,0},{16,24},{24,16},{1,9},{9,1},{17,25},{25,17},{2,10},{10... | collective-permute-start | bytes 196616 | tf_op jit(solution)/shard_map/ppermute | solution.py:396
  39.2 2.2 %collective-permute-start.16 = (bf16[2,128,128]{2,1,0:T(8,128)(2,1)S(1)}, bf16[2,128,128]{2,1,0:T(8,128)(2,1)S(1)}, u32[]{:S(2)}, u32[]{:S(2)}) collective-permute-start(bf16[2,128,128]{2,1,0:T(8,128)(2,1)S(1)} %get-tuple-element.55.one_ref), channel_id=1, source_target_pairs={{0,8},{8,0},{16,24},{24,16},{1,9},{9,1},{17,25},{25,17},{2,10},{10... | collective-permute-start | bytes 196616 | tf_op jit(solution)/shard_map/ppermute | solution.py:396
  39.8 5.9 %collective-permute-start.15 = (bf16[2,128,128]{2,1,0:T(8,128)(2,1)S(1)}, bf16[2,128,128]{2,1,0:T(8,128)(2,1)S(1)}, u32[]{:S(2)}, u32[]{:S(2)}) collective-permute-start(bf16[2,128,128]{2,1,0:T(8,128)(2,1)S(1)} %add_states.2.refs_0_), channel_id=1, source_target_pairs={{0,16},{8,24},{16,0},{24,8},{1,17},{9,25},{17,1},{25,9},{2,18},{10... | collective-permute-start | bytes 196616 | tf_op jit(solution)/shard_map/ppermute | solution.py:396
  41.4 4.3 %collective-permute-start.17 = (bf16[2,128,128]{2,1,0:T(8,128)(2,1)S(1)}, bf16[2,128,128]{2,1,0:T(8,128)(2,1)S(1)}, u32[]{:S(2)}, u32[]{:S(2)}) collective-permute-start(bf16[2,128,128]{2,1,0:T(8,128)(2,1)S(1)} %add_states.3), channel_id=1, source_target_pairs={{0,16},{8,24},{16,0},{24,8},{1,17},{9,25},{17,1},{25,9},{2,18},{10... | collective-permute-start | bytes 196616 | tf_op jit(solution)/shard_map/ppermute | solution.py:396
  42.3 3.5 %slice-start.5 = ((s8[6291456]{0:T(1024)(128)(4,1)}), s8[4194304]{0:T(1024)(128)(4,1)S(1)}, s32[]{:S(2)}) async-start(s8[6291456]{0:T(1024)(128)(4,1)} %bitcast.3), calls=%async_computation.5 | async-start | bytes 8388608
  42.3 3.5 %slice-start.6 = ((s8[6291456]{0:T(1024)(128)(4,1)}), s8[2097152]{0:T(1024)(128)(4,1)S(1)}, s32[]{:S(2)}) async-start(s8[6291456]{0:T(1024)(128)(4,1)} %bitcast.3), calls=%async_computation.6 | async-start | bytes 4194304
  42.3 3.5 %copy-start = (f32[4,128,128]{2,1,0:T(8,128)S(1)}, f32[4,128,128]{2,1,0:T(8,128)}, u32[]{:S(2)}) copy-start(f32[4,128,128]{2,1,0:T(8,128)} %initial_ref.1) | copy-start | bytes 786436
  42.3 3.5 %copy-start.1 = (f32[512]{0:T(512)S(1)}, f32[512]{0:T(512)}, u32[]{:S(2)}) copy-start(f32[512]{0:T(512)} %param.8) | copy-start | bytes 6148
  47.3 7.1 %collective-permute-start.28 = (bf16[32,3072]{1,0:T(8,128)(2,1)S(1)}, bf16[32,3072]{1,0:T(8,128)(2,1)S(1)}, u32[]{:S(2)}, u32[]{:S(2)}) collective-permute-start(bf16[32,3072]{1,0:T(8,128)(2,1)S(1)} %get-tuple-element.72), channel_id=1, source_target_pairs={{0,2},{2,4},{4,6},{6,7},{7,5},{5,3},{3,1},{1,0},{8,10},{10,12},{12... | collective-permute-start | bytes 589832 | tf_op jit(solution)/shard_map/ppermute | solution.py:360
  48.9 7.8 %collective-permute-start.24 = (bf16[32,3072]{1,0:T(8,128)(2,1)S(1)}, bf16[32,3072]{1,0:T(8,128)(2,1)S(1)}, u32[]{:S(2)}, u32[]{:S(2)}) collective-permute-start(bf16[32,3072]{1,0:T(8,128)(2,1)S(1)} %get-tuple-element.68), channel_id=1, source_target_pairs={{2,0},{4,2},{6,4},{7,6},{5,7},{3,5},{1,3},{0,1},{10,8},{12,10},{14... | collective-permute-start | bytes 589832 | tf_op jit(solution)/shard_map/ppermute | solution.py:360
  51.0 10.0 %collective-permute-start.21 = (bf16[32,3072]{1,0:T(8,128)(2,1)S(1)}, bf16[32,3072]{1,0:T(8,128)(2,1)S(1)}, u32[]{:S(2)}, u32[]{:S(2)}) collective-permute-start(bf16[32,3072]{1,0:T(8,128)(2,1)S(1)} %get-tuple-element.64), channel_id=1, source_target_pairs={{2,0},{4,2},{6,4},{7,6},{5,7},{3,5},{1,3},{0,1},{10,8},{12,10},{14... | collective-permute-start | bytes 589832 | tf_op jit(solution)/shard_map/ppermute | solution.py:360
  51.5 10.0 %collective-permute-start.18 = (bf16[32,3072]{1,0:T(8,128)(2,1)S(1)}, bf16[32,3072]{1,0:T(8,128)(2,1)S(1)}, u32[]{:S(2)}, u32[]{:S(2)}) collective-permute-start(bf16[32,3072]{1,0:T(8,128)(2,1)S(1)} %get-tuple-element.61), channel_id=1, source_target_pairs={{0,2},{2,4},{4,6},{6,7},{7,5},{5,3},{3,1},{1,0},{8,10},{10,12},{12... | collective-permute-start | bytes 589832 | tf_op jit(solution)/shard_map/ppermute | solution.py:360
  54.5 9.1 %collective-permute-start.29 = (bf16[32,3072]{1,0:T(8,128)(2,1)S(1)}, bf16[32,3072]{1,0:T(8,128)(2,1)S(1)}, u32[]{:S(2)}, u32[]{:S(2)}) collective-permute-start(bf16[32,3072]{1,0:T(8,128)(2,1)S(1)} %add_step.17), channel_id=1, source_target_pairs={{0,2},{2,4},{4,6},{6,7},{7,5},{5,3},{3,1},{1,0},{8,10},{10,12},{12... | collective-permute-start | bytes 589832 | tf_op jit(solution)/shard_map/ppermute | solution.py:360
  56.8 8.4 %collective-permute-start.25 = (bf16[32,3072]{1,0:T(8,128)(2,1)S(1)}, bf16[32,3072]{1,0:T(8,128)(2,1)S(1)}, u32[]{:S(2)}, u32[]{:S(2)}) collective-permute-start(bf16[32,3072]{1,0:T(8,128)(2,1)S(1)} %add_step.14), channel_id=1, source_target_pairs={{2,0},{4,2},{6,4},{7,6},{5,7},{3,5},{1,3},{0,1},{10,8},{12,10},{14... | collective-permute-start | bytes 589832 | tf_op jit(solution)/shard_map/ppermute | solution.py:360
  61.0 8.4 %collective-permute-start.22 = (bf16[32,3072]{1,0:T(8,128)(2,1)S(1)}, bf16[32,3072]{1,0:T(8,128)(2,1)S(1)}, u32[]{:S(2)}, u32[]{:S(2)}) collective-permute-start(bf16[32,3072]{1,0:T(8,128)(2,1)S(1)} %add_step.12), channel_id=1, source_target_pairs={{2,0},{4,2},{6,4},{7,6},{5,7},{3,5},{1,3},{0,1},{10,8},{12,10},{14... | collective-permute-start | bytes 589832 | tf_op jit(solution)/shard_map/ppermute | solution.py:360
  61.6 8.4 %collective-permute-start.19 = (bf16[32,3072]{1,0:T(8,128)(2,1)S(1)}, bf16[32,3072]{1,0:T(8,128)(2,1)S(1)}, u32[]{:S(2)}, u32[]{:S(2)}) collective-permute-start(bf16[32,3072]{1,0:T(8,128)(2,1)S(1)} %add_step.10), channel_id=1, source_target_pairs={{0,2},{2,4},{4,6},{6,7},{7,5},{5,3},{3,1},{1,0},{8,10},{10,12},{12... | collective-permute-start | bytes 589832 | tf_op jit(solution)/shard_map/ppermute | solution.py:360
  63.6 8.5 %collective-permute-start.30 = (bf16[32,3072]{1,0:T(8,128)(2,1)S(1)}, bf16[32,3072]{1,0:T(8,128)(2,1)S(1)}, u32[]{:S(2)}, u32[]{:S(2)}) collective-permute-start(bf16[32,3072]{1,0:T(8,128)(2,1)S(1)} %add_step.18), channel_id=1, source_target_pairs={{0,2},{2,4},{4,6},{6,7},{7,5},{5,3},{3,1},{1,0},{8,10},{10,12},{12... | collective-permute-start | bytes 589832 | tf_op jit(solution)/shard_map/ppermute | solution.py:360
  65.3 8.5 %collective-permute-start.26 = (bf16[32,3072]{1,0:T(8,128)(2,1)S(1)}, bf16[32,3072]{1,0:T(8,128)(2,1)S(1)}, u32[]{:S(2)}, u32[]{:S(2)}) collective-permute-start(bf16[32,3072]{1,0:T(8,128)(2,1)S(1)} %add_step.15), channel_id=1, source_target_pairs={{2,0},{4,2},{6,4},{7,6},{5,7},{3,5},{1,3},{0,1},{10,8},{12,10},{14... | collective-permute-start | bytes 589832 | tf_op jit(solution)/shard_map/ppermute | solution.py:360
  69.4 8.4 %collective-permute-start.23 = (bf16[32,3072]{1,0:T(8,128)(2,1)S(1)}, bf16[32,3072]{1,0:T(8,128)(2,1)S(1)}, u32[]{:S(2)}, u32[]{:S(2)}) collective-permute-start(bf16[32,3072]{1,0:T(8,128)(2,1)S(1)} %add_step.13), channel_id=1, source_target_pairs={{2,0},{4,2},{6,4},{7,6},{5,7},{3,5},{1,3},{0,1},{10,8},{12,10},{14... | collective-permute-start | bytes 589832 | tf_op jit(solution)/shard_map/ppermute | solution.py:360
  70.0 7.8 %collective-permute-start.20 = (bf16[32,3072]{1,0:T(8,128)(2,1)S(1)}, bf16[32,3072]{1,0:T(8,128)(2,1)S(1)}, u32[]{:S(2)}, u32[]{:S(2)}) collective-permute-start(bf16[32,3072]{1,0:T(8,128)(2,1)S(1)} %add_step.11), channel_id=1, source_target_pairs={{0,2},{2,4},{4,6},{6,7},{7,5},{5,3},{3,1},{1,0},{8,10},{10,12},{12... | collective-permute-start | bytes 589832 | tf_op jit(solution)/shard_map/ppermute | solution.py:360
  72.1 6.7 %collective-permute-start.31 = (bf16[32,3072]{1,0:T(8,128)(2,1)S(1)}, bf16[32,3072]{1,0:T(8,128)(2,1)S(1)}, u32[]{:S(2)}, u32[]{:S(2)}) collective-permute-start(bf16[32,3072]{1,0:T(8,128)(2,1)S(1)} %add_step.19), channel_id=1, source_target_pairs={{0,2},{2,4},{4,6},{6,7},{7,5},{5,3},{3,1},{1,0},{8,10},{10,12},{12... | collective-permute-start | bytes 589832 | tf_op jit(solution)/shard_map/ppermute | solution.py:360
  73.8 6.4 %collective-permute-start.27 = (bf16[32,3072]{1,0:T(8,128)(2,1)S(1)}, bf16[32,3072]{1,0:T(8,128)(2,1)S(1)}, u32[]{:S(2)}, u32[]{:S(2)}) collective-permute-start(bf16[32,3072]{1,0:T(8,128)(2,1)S(1)} %add_step.16), channel_id=1, source_target_pairs={{2,0},{4,2},{6,4},{7,6},{5,7},{3,5},{1,3},{0,1},{10,8},{12,10},{14... | collective-permute-start | bytes 589832 | tf_op jit(solution)/shard_map/ppermute | solution.py:360

commit v11 on v10

--- a/solution.py
+++ b/solution.py
@@ -434,8 +434,8 @@
         feat_q, within, initial_state, exchanged, norm_gain, out_weight, soon, rows, head_dim
     )
     parts = project_rest(normalized, out_weight, n_fsdp - soon, rows) + parts
-    mirrored = [distance if distance == n_fsdp // 2 else -distance for distance in order]
-    return ring_scatter(parts, mirrored, left, right)
+
+    return ring_scatter(parts, order, right, left)
 
 
 def solution(mesh):

time: 81.1 us -> 80 us (0.986)
  waiting for transfers between devices: 34.1 us -> 33 us
    ppermute x7, starting transfers between devices: 11.3 us -> 3.45 us  [hop(): lax.ppermute(to_left, 'fsdp', left)]
    ppermute x7, starting transfers between devices: 3.47 us -> 11.3 us  [hop(): lax.ppermute(to_right, 'fsdp', right)]
    ppermute x7, waiting for transfers between devices: 12.7 us -> 7.43 us  [hop(): lax.ppermute(to_right, 'fsdp', right)]
    ppermute x7, waiting for transfers between devices: 3.12 us -> 7.35 us  [hop(): lax.ppermute(to_left, 'fsdp', left)]
where the time goes in v11:
time: 80 us; the launch traced here: 79.9 us
  starting transfers between devices  33.5 us (42%)
  waiting for transfers between devices  33 us (41%)
  Pallas kernels  12 us (15%)
  local copies, waits for them, and re-layouts  1.09 us (1%)
    ppermute x6, starting transfers between devices, ring_gather(): going_right[part] = lax.ppermute(going_right[part], 'fsdp', right)  13.6 us
    ppermute x7, starting transfers between devices, hop(): lax.ppermute(to_right, 'fsdp', right)  11.3 us
    ppermute x6, waiting for transfers between devices, ring_gather(): going_right[part] = lax.ppermute(going_right[part], 'fsdp', right)  7.63 us
    ppermute x7, waiting for transfers between devices, hop(): lax.ppermute(to_right, 'fsdp', right)  7.43 us
    ppermute x7, waiting for transfers between devices, hop(): lax.ppermute(to_left, 'fsdp', left)  7.35 us
    ppermute x6, waiting for transfers between devices, ring_gather(): going_left[1 - part] = lax.ppermute(going_left[1 - part], 'fsdp', left)  6.17 us
    ppermute x7, starting transfers between devices, hop(): lax.ppermute(to_left, 'fsdp', left)  3.45 us
    ppermute x4, starting transfers between devices, exchange_states(): received[at].append(lax.ppermute(total, 'ctx', pairs))  3.09 us
  transfers between devices with their start and end apart: 32, of which 17 were waited for; matrix products, arithmetic and copies ran while one was open for 0% of the time, Pallas kernels for 10%

profile of v11, /device:TPU:0, one launch (start us, length us, event | category | flops | bytes accessed | tf_op | source)
XLA Modules:
  0.0 79.9 jit_solution(12693641336135160786)
XLA Ops:
  0.0 1.0 %fusion = (bf16[32,3072]{1,0:T(8,128)(2,1)S(1)}, bf16[32,3072]{1,0:T(8,128)(2,1)S(1)}) fusion(bf16[32,6144]{1,0:T(8,128)(2,1)} %param.5), kind=kLoop, calls=%fused_computation | loop fusion | bytes 786432 | tf_op jit(solution)/shard_map/slice | solution.py:68
  1.1 3.1 %collective-permute-start = (bf16[32,3072]{1,0:T(8,128)(2,1)S(1)}, bf16[32,3072]{1,0:T(8,128)(2,1)S(1)}, u32[]{:S(2)}, u32[]{:S(2)}) collective-permute-start(bf16[32,3072]{1,0:T(8,128)(2,1)S(1)} %get-tuple-element.74.refs_0_), channel_id=1, source_target_pairs={{0,2},{2,4},{4,6},{6,7},{7,5},{5,3},{3,1},{1,0},{8,10},{10,12},{12... | collective-permute-start | bytes 589832 | tf_op jit(solution)/shard_map/ppermute | solution.py:73
  4.1 2.0 %collective-permute-start.11 = (bf16[32,3072]{1,0:T(8,128)(2,1)S(1)}, bf16[32,3072]{1,0:T(8,128)(2,1)S(1)}, u32[]{:S(2)}, u32[]{:S(2)}) collective-permute-start(bf16[32,3072]{1,0:T(8,128)(2,1)S(1)} %get-tuple-element.73.refs_5_), channel_id=1, source_target_pairs={{0,2},{2,4},{4,6},{6,7},{7,5},{5,3},{3,1},{1,0},{8,10},{10,12},{12... | collective-permute-start | bytes 589832 | tf_op jit(solution)/shard_map/ppermute | solution.py:73
  6.2 3.6 %collective-permute-done.refs_1_.arrived_ref = bf16[32,3072]{1,0:T(8,128)(2,1)S(1)} collective-permute-done((bf16[32,3072]{1,0:T(8,128)(2,1)S(1)}, bf16[32,3072]{1,0:T(8,128)(2,1)S(1)}, u32[]{:S(2)}, u32[]{:S(2)}) %collective-permute-start) | collective-permute-done | bytes 196640 | tf_op jit(solution)/shard_map/ppermute | solution.py:73
  9.8 2.1 %collective-permute-start.1 = (bf16[32,3072]{1,0:T(8,128)(2,1)S(1)}, bf16[32,3072]{1,0:T(8,128)(2,1)S(1)}, u32[]{:S(2)}, u32[]{:S(2)}) collective-permute-start(bf16[32,3072]{1,0:T(8,128)(2,1)S(1)} %collective-permute-done.refs_1_.arrived_ref), channel_id=1, source_target_pairs={{0,2},{2,4},{4,6},{6,7},{7,5},{5,3},{3,1},{1,0},{8,10},{10,12},{12... | collective-permute-start | bytes 589832 | tf_op jit(solution)/shard_map/ppermute | solution.py:73
  12.0 2.0 %collective-permute-done.11.refs_6_ = bf16[32,3072]{1,0:T(8,128)(2,1)S(1)} collective-permute-done((bf16[32,3072]{1,0:T(8,128)(2,1)S(1)}, bf16[32,3072]{1,0:T(8,128)(2,1)S(1)}, u32[]{:S(2)}, u32[]{:S(2)}) %collective-permute-start.11) | collective-permute-done | bytes 196640 | tf_op jit(solution)/shard_map/ppermute | solution.py:73
  14.0 2.1 %collective-permute-start.12 = (bf16[32,3072]{1,0:T(8,128)(2,1)S(1)}, bf16[32,3072]{1,0:T(8,128)(2,1)S(1)}, u32[]{:S(2)}, u32[]{:S(2)}) collective-permute-start(bf16[32,3072]{1,0:T(8,128)(2,1)S(1)} %collective-permute-done.11.refs_6_), channel_id=1, source_target_pairs={{0,2},{2,4},{4,6},{6,7},{7,5},{5,3},{3,1},{1,0},{8,10},{10,12},{12... | collective-permute-start | bytes 589832 | tf_op jit(solution)/shard_map/ppermute | solution.py:73
  16.2 2.0 %collective-permute-done.1.refs_3_ = bf16[32,3072]{1,0:T(8,128)(2,1)S(1)} collective-permute-done((bf16[32,3072]{1,0:T(8,128)(2,1)S(1)}, bf16[32,3072]{1,0:T(8,128)(2,1)S(1)}, u32[]{:S(2)}, u32[]{:S(2)}) %collective-permute-start.1) | collective-permute-done | bytes 196640 | tf_op jit(solution)/shard_map/ppermute | solution.py:73
  18.2 2.1 %collective-permute-start.2 = (bf16[32,3072]{1,0:T(8,128)(2,1)S(1)}, bf16[32,3072]{1,0:T(8,128)(2,1)S(1)}, u32[]{:S(2)}, u32[]{:S(2)}) collective-permute-start(bf16[32,3072]{1,0:T(8,128)(2,1)S(1)} %collective-permute-done.1.refs_3_), channel_id=1, source_target_pairs={{0,2},{2,4},{4,6},{6,7},{7,5},{5,3},{3,1},{1,0},{8,10},{10,12},{12... | collective-permute-start | bytes 589832 | tf_op jit(solution)/shard_map/ppermute | solution.py:73
  20.4 4.2 %collective-permute-done.9.refs_4_ = bf16[32,3072]{1,0:T(8,128)(2,1)S(1)} collective-permute-done((bf16[32,3072]{1,0:T(8,128)(2,1)S(1)}, bf16[32,3072]{1,0:T(8,128)(2,1)S(1)}, u32[]{:S(2)}, u32[]{:S(2)}) %collective-permute-start.9) | collective-permute-done | bytes 196640 | tf_op jit(solution)/shard_map/ppermute | solution.py:74
  24.6 2.0 %collective-permute-start.13 = (bf16[32,3072]{1,0:T(8,128)(2,1)S(1)}, bf16[32,3072]{1,0:T(8,128)(2,1)S(1)}, u32[]{:S(2)}, u32[]{:S(2)}) collective-permute-start(bf16[32,3072]{1,0:T(8,128)(2,1)S(1)} %collective-permute-done.12.refs_8_), channel_id=1, source_target_pairs={{0,2},{2,4},{4,6},{6,7},{7,5},{5,3},{3,1},{1,0},{8,10},{10,12},{12... | collective-permute-start | bytes 589832 | tf_op jit(solution)/shard_map/ppermute | solution.py:73
  26.7 1.2 %early_keys.1 = (bf16[256,512]{1,0:T(8,128)(2,1)S(1)}, bf16[256,3072]{1,0:T(8,128)(2,1)S(1)}, bf16[256,3072]{1,0:T(8,128)(2,1)S(1)}) custom-call(bf16[32,3072]{1,0:T(8,128)(2,1)S(1)} %get-tuple-element.74.refs_0_, bf16[32,3072]{1,0:T(8,128)(2,1)S(1)} %collective-permute-done.refs_1_.arrived_ref, bf16[32,3072]{1,0:T(8,128)(2,1)S(1)} %collective-permute-done.8.refs_2_, ...), custom_call_target="tpu_custom_call" | custom-call | flops 1006632960 | bytes 6291456 | tf_op jit(solution)/shard_map/early_keys/pallas_call | solution.py:106
  27.9 1.2 %early_values.1.refs_6_ = bf16[256,512]{1,0:T(8,128)(2,1)S(1)} custom-call(bf16[256,3072]{1,0:T(8,128)(2,1)S(1)} %get-tuple-element.39.first_ref.refs_4_, bf16[256,3072]{1,0:T(8,128)(2,1)S(1)} %get-tuple-element.40.second_ref.refs_5_, bf16[3,6144,512]{2,1,0:T(8,128)(2,1)S(1)} %bitcast.2), custom_call_target="tpu_custom_call" | custom-call | flops 1006632960 | bytes 6291456 | tf_op jit(solution)/shard_map/early_values/pallas_call | solution.py:126
  29.1 1.6 %collective-permute-start.3 = (bf16[32,3072]{1,0:T(8,128)(2,1)S(1)}, bf16[32,3072]{1,0:T(8,128)(2,1)S(1)}, u32[]{:S(2)}, u32[]{:S(2)}) collective-permute-start(bf16[32,3072]{1,0:T(8,128)(2,1)S(1)} %collective-permute-done.2.refs_0_), channel_id=1, source_target_pairs={{0,2},{2,4},{4,6},{6,7},{7,5},{5,3},{3,1},{1,0},{8,10},{10,12},{12... | collective-permute-start | bytes 589832 | tf_op jit(solution)/shard_map/ppermute | solution.py:77
  31.2 1.8 %collective-permute-done.10.refs_1_ = bf16[32,3072]{1,0:T(8,128)(2,1)S(1)} collective-permute-done((bf16[32,3072]{1,0:T(8,128)(2,1)S(1)}, bf16[32,3072]{1,0:T(8,128)(2,1)S(1)}, u32[]{:S(2)}, u32[]{:S(2)}) %collective-permute-start.10) | collective-permute-done | bytes 196640 | tf_op jit(solution)/shard_map/ppermute | solution.py:74
  33.1 1.7 %collective-permute-done.3.refs_0_ = bf16[32,3072]{1,0:T(8,128)(2,1)S(1)} collective-permute-done((bf16[32,3072]{1,0:T(8,128)(2,1)S(1)}, bf16[32,3072]{1,0:T(8,128)(2,1)S(1)}, u32[]{:S(2)}, u32[]{:S(2)}) %collective-permute-start.3) | collective-permute-done | bytes 196640 | tf_op jit(solution)/shard_map/ppermute | solution.py:77
  34.8 1.6 %collective-permute-done.7.refs_1_ = bf16[32,3072]{1,0:T(8,128)(2,1)S(1)} collective-permute-done((bf16[32,3072]{1,0:T(8,128)(2,1)S(1)}, bf16[32,3072]{1,0:T(8,128)(2,1)S(1)}, u32[]{:S(2)}, u32[]{:S(2)}) %collective-permute-start.7) | collective-permute-done | bytes 196640 | tf_op jit(solution)/shard_map/ppermute | solution.py:78
  36.4 1.4 %late_keys_and_values.2 = (bf16[256,3072]{1,0:T(8,128)(2,1)S(1)}, bf16[256,3072]{1,0:T(8,128)(2,1)S(1)}, bf16[256,512]{1,0:T(8,128)(2,1)S(1)}, bf16[256,512]{1,0:T(8,128)(2,1)S(1)}, bf16[2,128,128]{2,1,0:T(8,128)(2,1)S(1)}) custom-call(bf16[32,3072]{1,0:T(8,128)(2,1)S(1)} %collective-permute-, ...), custom_call_target="tpu_custom_call", output_to_operand_aliasing={{0}: (2, {}), {1}: (3, {}), {2}: (5, {}), {3}: (6, {})} | custom-call | flops 603979776 | bytes 6291456 | tf_op jit(solution)/shard_map/late_keys_and_values/pallas_call | solution.py:180
  37.8 1.4 %late_keys_and_values.3 = (bf16[256,3072]{1,0:T(8,128)(2,1)S(1)}, bf16[256,3072]{1,0:T(8,128)(2,1)S(1)}, bf16[256,512]{1,0:T(8,128)(2,1)S(1)}, bf16[256,512]{1,0:T(8,128)(2,1)S(1)}, bf16[2,128,128]{2,1,0:T(8,128)(2,1)S(1)}) custom-call(bf16[256,3072]{1,0:T(8,128)(2,1)S(1)} %get-tuple-element., ...), custom_call_target="tpu_custom_call", output_to_operand_aliasing={{0}: (0, {}), {1}: (1, {}), {2}: (3, {}), {3}: (4, {})} | custom-call | flops 5000000000 | bytes 6291456 | tf_op jit(solution)/shard_map/late_keys_and_values/pallas_call | solution.py:180
  39.2 0.6 collective-permute-start.16
  39.8 1.6 %collective-permute-start.15 = (bf16[2,128,128]{2,1,0:T(8,128)(2,1)S(1)}, bf16[2,128,128]{2,1,0:T(8,128)(2,1)S(1)}, u32[]{:S(2)}, u32[]{:S(2)}) collective-permute-start(bf16[2,128,128]{2,1,0:T(8,128)(2,1)S(1)} %add_states.2.refs_0_), channel_id=1, source_target_pairs={{0,16},{8,24},{16,0},{24,8},{1,17},{9,25},{17,1},{25,9},{2,18},{10... | collective-permute-start | bytes 196616 | tf_op jit(solution)/shard_map/ppermute | solution.py:396
  41.4 0.9 %collective-permute-start.17 = (bf16[2,128,128]{2,1,0:T(8,128)(2,1)S(1)}, bf16[2,128,128]{2,1,0:T(8,128)(2,1)S(1)}, u32[]{:S(2)}, u32[]{:S(2)}) collective-permute-start(bf16[2,128,128]{2,1,0:T(8,128)(2,1)S(1)} %add_states.3), channel_id=1, source_target_pairs={{0,16},{8,24},{16,0},{24,8},{1,17},{9,25},{17,1},{25,9},{2,18},{10... | collective-permute-start | bytes 196616 | tf_op jit(solution)/shard_map/ppermute | solution.py:396
  42.3 2.3 %queries_within.1 = (bf16[256,512]{1,0:T(8,128)(2,1)S(1)}, f32[256,512]{1,0:T(8,128)S(1)}) custom-call(bf16[256,3072]{1,0:T(8,128)(2,1)S(1)} %get-tuple-element.48.first_ref, bf16[256,3072]{1,0:T(8,128)(2,1)S(1)} %get-tuple-element.49.second_ref, bf16[3,6144,512]{2,1,0:T(8,128)(2,1)S(1)} %bitcast.2, bf16[256,512]{1,0:T(8,128)(2,1)S(1)} %get-tuple-element.50.k_ref, ...), custom_call_target="tpu_custom_call" | custom-call | flops 1744830464 | bytes 6291456 | tf_op jit(solution)/shard_map/queries_within/pallas_call | solution.py:224
  44.6 1.1 %collective-permute-done.17.refs_3_ = bf16[2,128,128]{2,1,0:T(8,128)(2,1)S(1)} collective-permute-done((bf16[2,128,128]{2,1,0:T(8,128)(2,1)S(1)}, bf16[2,128,128]{2,1,0:T(8,128)(2,1)S(1)}, u32[]{:S(2)}, u32[]{:S(2)}) %collective-permute-start.17) | collective-permute-done | bytes 65568 | tf_op jit(solution)/shard_map/ppermute | solution.py:396
  45.8 1.5 %attend_and_project.1 = (bf16[256,512]{1,0:T(8,128)(2,1)S(1)}, bf16[32,3072]{1,0:T(8,128)(2,1)S(1)}, bf16[32,3072]{1,0:T(8,128)(2,1)S(1)}) custom-call(bf16[256,512]{1,0:T(8,128)(2,1)S(1)} %get-tuple-element.52.q_ref, f32[256,512]{1,0:T(8,128)S(1)} %get-tuple-element.53.within_ref, f32[4,128,128]{2,1,0:T(8,128)S(1)} %copy-done, f32[1,512]{1,0:T(1,128)S(1)} %bitcast.5, ...), custom_call_target="tpu_custom_call" | custom-call | flops 1610612736 | bytes 6291456 | tf_op jit(solution)/shard_map/attend_and_project/pallas_call | solution.py:272
  47.8 1.6 %collective-permute-start.24 = (bf16[32,3072]{1,0:T(8,128)(2,1)S(1)}, bf16[32,3072]{1,0:T(8,128)(2,1)S(1)}, u32[]{:S(2)}, u32[]{:S(2)}) collective-permute-start(bf16[32,3072]{1,0:T(8,128)(2,1)S(1)} %get-tuple-element.68), channel_id=1, source_target_pairs={{0,2},{2,4},{4,6},{6,7},{7,5},{5,3},{3,1},{1,0},{8,10},{10,12},{12... | collective-permute-start | bytes 589832 | tf_op jit(solution)/shard_map/ppermute | solution.py:360
  49.4 1.6 %project_rest.1 = (bf16[32,3072]{1,0:T(8,128)(2,1)S(1)}, bf16[32,3072]{1,0:T(8,128)(2,1)S(1)}, bf16[32,3072]{1,0:T(8,128)(2,1)S(1)}, bf16[32,3072]{1,0:T(8,128)(...) custom-call(bf16[256,512]{1,0:T(8,128)(2,1)S(1)} %get-tuple-element., ...), custom_call_target="tpu_custom_call" | custom-call | flops 5000000000 | bytes 6291456 | tf_op jit(solution)/shard_map/project_rest/pallas_call | solution.py:291
  51.0 1.6 %collective-permute-start.21 = (bf16[32,3072]{1,0:T(8,128)(2,1)S(1)}, bf16[32,3072]{1,0:T(8,128)(2,1)S(1)}, u32[]{:S(2)}, u32[]{:S(2)}) collective-permute-start(bf16[32,3072]{1,0:T(8,128)(2,1)S(1)} %get-tuple-element.64), channel_id=1, source_target_pairs={{0,2},{2,4},{4,6},{6,7},{7,5},{5,3},{3,1},{1,0},{8,10},{10,12},{12... | collective-permute-start | bytes 589832 | tf_op jit(solution)/shard_map/ppermute | solution.py:360
  53.0 0.5 collective-permute-done.28.got_ref
  53.6 0.5 collective-permute-start.29
  54.1 0.9 %collective-permute-done.24.got_ref = bf16[32,3072]{1,0:T(8,128)(2,1)S(1)} collective-permute-done((bf16[32,3072]{1,0:T(8,128)(2,1)S(1)}, bf16[32,3072]{1,0:T(8,128)(2,1)S(1)}, u32[]{:S(2)}, u32[]{:S(2)}) %collective-permute-start.24) | collective-permute-done | bytes 196640 | tf_op jit(solution)/shard_map/ppermute | solution.py:360
  55.1 1.6 %collective-permute-start.25 = (bf16[32,3072]{1,0:T(8,128)(2,1)S(1)}, bf16[32,3072]{1,0:T(8,128)(2,1)S(1)}, u32[]{:S(2)}, u32[]{:S(2)}) collective-permute-start(bf16[32,3072]{1,0:T(8,128)(2,1)S(1)} %add_step.14), channel_id=1, source_target_pairs={{0,2},{2,4},{4,6},{6,7},{7,5},{5,3},{3,1},{1,0},{8,10},{10,12},{12... | collective-permute-start | bytes 589832 | tf_op jit(solution)/shard_map/ppermute | solution.py:360
  56.7 2.5 %collective-permute-done.21.got_ref = bf16[32,3072]{1,0:T(8,128)(2,1)S(1)} collective-permute-done((bf16[32,3072]{1,0:T(8,128)(2,1)S(1)}, bf16[32,3072]{1,0:T(8,128)(2,1)S(1)}, u32[]{:S(2)}, u32[]{:S(2)}) %collective-permute-start.21) | collective-permute-done | bytes 196640 | tf_op jit(solution)/shard_map/ppermute | solution.py:360
  59.3 1.6 %collective-permute-start.22 = (bf16[32,3072]{1,0:T(8,128)(2,1)S(1)}, bf16[32,3072]{1,0:T(8,128)(2,1)S(1)}, u32[]{:S(2)}, u32[]{:S(2)}) collective-permute-start(bf16[32,3072]{1,0:T(8,128)(2,1)S(1)} %add_step.12), channel_id=1, source_target_pairs={{0,2},{2,4},{4,6},{6,7},{7,5},{5,3},{3,1},{1,0},{8,10},{10,12},{12... | collective-permute-start | bytes 589832 | tf_op jit(solution)/shard_map/ppermute | solution.py:360
  60.9 0.5 collective-permute-start.19
  61.5 2.0 %collective-permute-done.29.got_ref = bf16[32,3072]{1,0:T(8,128)(2,1)S(1)} collective-permute-done((bf16[32,3072]{1,0:T(8,128)(2,1)S(1)}, bf16[32,3072]{1,0:T(8,128)(2,1)S(1)}, u32[]{:S(2)}, u32[]{:S(2)}) %collective-permute-start.29) | collective-permute-done | bytes 196640 | tf_op jit(solution)/shard_map/ppermute | solution.py:360
  63.5 0.5 collective-permute-start.30
  64.0 1.6 %collective-permute-start.26 = (bf16[32,3072]{1,0:T(8,128)(2,1)S(1)}, bf16[32,3072]{1,0:T(8,128)(2,1)S(1)}, u32[]{:S(2)}, u32[]{:S(2)}) collective-permute-start(bf16[32,3072]{1,0:T(8,128)(2,1)S(1)} %add_step.15), channel_id=1, source_target_pairs={{0,2},{2,4},{4,6},{6,7},{7,5},{5,3},{3,1},{1,0},{8,10},{10,12},{12... | collective-permute-start | bytes 589832 | tf_op jit(solution)/shard_map/ppermute | solution.py:360
  65.7 2.0 %collective-permute-done.22.got_ref = bf16[32,3072]{1,0:T(8,128)(2,1)S(1)} collective-permute-done((bf16[32,3072]{1,0:T(8,128)(2,1)S(1)}, bf16[32,3072]{1,0:T(8,128)(2,1)S(1)}, u32[]{:S(2)}, u32[]{:S(2)}) %collective-permute-start.22) | collective-permute-done | bytes 196640 | tf_op jit(solution)/shard_map/ppermute | solution.py:360
  67.7 1.6 %collective-permute-start.23 = (bf16[32,3072]{1,0:T(8,128)(2,1)S(1)}, bf16[32,3072]{1,0:T(8,128)(2,1)S(1)}, u32[]{:S(2)}, u32[]{:S(2)}) collective-permute-start(bf16[32,3072]{1,0:T(8,128)(2,1)S(1)} %add_step.13), channel_id=1, source_target_pairs={{0,2},{2,4},{4,6},{6,7},{7,5},{5,3},{3,1},{1,0},{8,10},{10,12},{12... | collective-permute-start | bytes 589832 | tf_op jit(solution)/shard_map/ppermute | solution.py:360
  69.4 0.5 collective-permute-start.20
  69.9 2.0 %collective-permute-done.30.got_ref = bf16[32,3072]{1,0:T(8,128)(2,1)S(1)} collective-permute-done((bf16[32,3072]{1,0:T(8,128)(2,1)S(1)}, bf16[32,3072]{1,0:T(8,128)(2,1)S(1)}, u32[]{:S(2)}, u32[]{:S(2)}) %collective-permute-start.30) | collective-permute-done | bytes 196640 | tf_op jit(solution)/shard_map/ppermute | solution.py:360
  71.9 0.5 collective-permute-start.31
  72.5 1.6 %collective-permute-start.27 = (bf16[32,3072]{1,0:T(8,128)(2,1)S(1)}, bf16[32,3072]{1,0:T(8,128)(2,1)S(1)}, u32[]{:S(2)}, u32[]{:S(2)}) collective-permute-start(bf16[32,3072]{1,0:T(8,128)(2,1)S(1)} %add_step.16), channel_id=1, source_target_pairs={{0,2},{2,4},{4,6},{6,7},{7,5},{5,3},{3,1},{1,0},{8,10},{10,12},{12... | collective-permute-start | bytes 589832 | tf_op jit(solution)/shard_map/ppermute | solution.py:360
  74.1 2.0 %collective-permute-done.23.got_second = bf16[32,3072]{1,0:T(8,128)(2,1)S(1)} collective-permute-done((bf16[32,3072]{1,0:T(8,128)(2,1)S(1)}, bf16[32,3072]{1,0:T(8,128)(2,1)S(1)}, u32[]{:S(2)}, u32[]{:S(2)}) %collective-permute-start.23) | collective-permute-done | bytes 196640 | tf_op jit(solution)/shard_map/ppermute | solution.py:360
  76.1 0.8 %collective-permute-done.20.got_first = bf16[32,3072]{1,0:T(8,128)(2,1)S(1)} collective-permute-done((bf16[32,3072]{1,0:T(8,128)(2,1)S(1)}, bf16[32,3072]{1,0:T(8,128)(2,1)S(1)}, u32[]{:S(2)}, u32[]{:S(2)}) %collective-permute-start.20) | collective-permute-done | bytes 196640 | tf_op jit(solution)/shard_map/ppermute | solution.py:360
  77.0 2.0 %collective-permute-done.31.second = bf16[32,3072]{1,0:T(8,128)(2,1)S(1)} collective-permute-done((bf16[32,3072]{1,0:T(8,128)(2,1)S(1)}, bf16[32,3072]{1,0:T(8,128)(2,1)S(1)}, u32[]{:S(2)}, u32[]{:S(2)}) %collective-permute-start.31) | collective-permute-done | bytes 196640 | tf_op jit(solution)/shard_map/ppermute | solution.py:360
  79.1 0.8 %finish.1 = bf16[32,6144]{1,0:T(8,128)(2,1)} custom-call(f32[2,32,3072]{2,1,0:T(8,128)S(1)} %add_own.1.gathered_ref, bf16[32,3072]{1,0:T(8,128)(2,1)S(1)} %collective-permute-done.27.first, bf16[32,3072]{1,0:T(8,128)(2,1)S(1)} %collective-permute-done.31.second), custom_call_target="tpu_custom_call" | custom-call | bytes 393216 | tf_op jit(solution)/shard_map/finish/pallas_call | solution.py:342
  (61 shorter events, 2.3 us)
Async XLA Ops:
  1.1 8.7 %collective-permute-start = (bf16[32,3072]{1,0:T(8,128)(2,1)S(1)}, bf16[32,3072]{1,0:T(8,128)(2,1)S(1)}, u32[]{:S(2)}, u32[]{:S(2)}) collective-permute-start(bf16[32,3072]{1,0:T(8,128)(2,1)S(1)} %get-tuple-element.74.refs_0_), channel_id=1, source_target_pairs={{0,2},{2,4},{4,6},{6,7},{7,5},{5,3},{3,1},{1,0},{8,10},{10,12},{12... | collective-permute-start | bytes 589832 | tf_op jit(solution)/shard_map/ppermute | solution.py:73
  4.1 7.8 %collective-permute-start.4 = (bf16[32,3072]{1,0:T(8,128)(2,1)S(1)}, bf16[32,3072]{1,0:T(8,128)(2,1)S(1)}, u32[]{:S(2)}, u32[]{:S(2)}) collective-permute-start(bf16[32,3072]{1,0:T(8,128)(2,1)S(1)} %get-tuple-element.73.refs_5_), channel_id=1, source_target_pairs={{2,0},{4,2},{6,4},{7,6},{5,7},{3,5},{1,3},{0,1},{10,8},{12,10},{14... | collective-permute-start | bytes 589832 | tf_op jit(solution)/shard_map/ppermute | solution.py:74
  4.1 9.9 %collective-permute-start.11 = (bf16[32,3072]{1,0:T(8,128)(2,1)S(1)}, bf16[32,3072]{1,0:T(8,128)(2,1)S(1)}, u32[]{:S(2)}, u32[]{:S(2)}) collective-permute-start(bf16[32,3072]{1,0:T(8,128)(2,1)S(1)} %get-tuple-element.73.refs_5_), channel_id=1, source_target_pairs={{0,2},{2,4},{4,6},{6,7},{7,5},{5,3},{3,1},{1,0},{8,10},{10,12},{12... | collective-permute-start | bytes 589832 | tf_op jit(solution)/shard_map/ppermute | solution.py:73
  6.2 10.0 %collective-permute-start.8 = (bf16[32,3072]{1,0:T(8,128)(2,1)S(1)}, bf16[32,3072]{1,0:T(8,128)(2,1)S(1)}, u32[]{:S(2)}, u32[]{:S(2)}) collective-permute-start(bf16[32,3072]{1,0:T(8,128)(2,1)S(1)} %get-tuple-element.74.refs_0_), channel_id=1, source_target_pairs={{2,0},{4,2},{6,4},{7,6},{5,7},{3,5},{1,3},{0,1},{10,8},{12,10},{14... | collective-permute-start | bytes 589832 | tf_op jit(solution)/shard_map/ppermute | solution.py:74
  9.8 8.4 %collective-permute-start.1 = (bf16[32,3072]{1,0:T(8,128)(2,1)S(1)}, bf16[32,3072]{1,0:T(8,128)(2,1)S(1)}, u32[]{:S(2)}, u32[]{:S(2)}) collective-permute-start(bf16[32,3072]{1,0:T(8,128)(2,1)S(1)} %collective-permute-done.refs_1_.arrived_ref), channel_id=1, source_target_pairs={{0,2},{2,4},{4,6},{6,7},{7,5},{5,3},{3,1},{1,0},{8,10},{10,12},{12... | collective-permute-start | bytes 589832 | tf_op jit(solution)/shard_map/ppermute | solution.py:73
  12.0 8.4 %collective-permute-start.5 = (bf16[32,3072]{1,0:T(8,128)(2,1)S(1)}, bf16[32,3072]{1,0:T(8,128)(2,1)S(1)}, u32[]{:S(2)}, u32[]{:S(2)}) collective-permute-start(bf16[32,3072]{1,0:T(8,128)(2,1)S(1)} %collective-permute-done.4.refs_7_.arrived_ref), channel_id=1, source_target_pairs={{2,0},{4,2},{6,4},{7,6},{5,7},{3,5},{1,3},{0,1},{10,8},{12,10},{14... | collective-permute-start | bytes 589832 | tf_op jit(solution)/shard_map/ppermute | solution.py:74
  14.0 10.6 %collective-permute-start.12 = (bf16[32,3072]{1,0:T(8,128)(2,1)S(1)}, bf16[32,3072]{1,0:T(8,128)(2,1)S(1)}, u32[]{:S(2)}, u32[]{:S(2)}) collective-permute-start(bf16[32,3072]{1,0:T(8,128)(2,1)S(1)} %collective-permute-done.11.refs_6_), channel_id=1, source_target_pairs={{0,2},{2,4},{4,6},{6,7},{7,5},{5,3},{3,1},{1,0},{8,10},{10,12},{12... | collective-permute-start | bytes 589832 | tf_op jit(solution)/shard_map/ppermute | solution.py:73
  16.2 8.4 %collective-permute-start.9 = (bf16[32,3072]{1,0:T(8,128)(2,1)S(1)}, bf16[32,3072]{1,0:T(8,128)(2,1)S(1)}, u32[]{:S(2)}, u32[]{:S(2)}) collective-permute-start(bf16[32,3072]{1,0:T(8,128)(2,1)S(1)} %collective-permute-done.8.refs_2_), channel_id=1, source_target_pairs={{2,0},{4,2},{6,4},{7,6},{5,7},{3,5},{1,3},{0,1},{10,8},{12,10},{14... | collective-permute-start | bytes 589832 | tf_op jit(solution)/shard_map/ppermute | solution.py:74
  16.2 10.5 %slice-start = ((s8[18874368]{0:T(1024)(128)(4,1)}), s8[4194304]{0:T(1024)(128)(4,1)S(1)}, s32[]{:S(2)}) async-start(s8[18874368]{0:T(1024)(128)(4,1)} %bitcast.1), calls=%async_computation | async-start | bytes 8388608
  16.2 10.5 %slice-start.1 = ((s8[18874368]{0:T(1024)(128)(4,1)}), s8[4194304]{0:T(1024)(128)(4,1)S(1)}, s32[]{:S(2)}) async-start(s8[18874368]{0:T(1024)(128)(4,1)} %bitcast.1), calls=%async_computation.1 | async-start | bytes 8388608
  16.2 10.5 %slice-start.2 = ((s8[18874368]{0:T(1024)(128)(4,1)}), s8[4194304]{0:T(1024)(128)(4,1)S(1)}, s32[]{:S(2)}) async-start(s8[18874368]{0:T(1024)(128)(4,1)} %bitcast.1), calls=%async_computation.2 | async-start | bytes 8388608
  16.2 10.4 %slice-start.3 = ((s8[18874368]{0:T(1024)(128)(4,1)}), s8[4194304]{0:T(1024)(128)(4,1)S(1)}, s32[]{:S(2)}) async-start(s8[18874368]{0:T(1024)(128)(4,1)} %bitcast.1), calls=%async_computation.3 | async-start | bytes 8388608
  16.2 10.4 %slice-start.4 = ((s8[18874368]{0:T(1024)(128)(4,1)}), s8[2097152]{0:T(1024)(128)(4,1)S(1)}, s32[]{:S(2)}) async-start(s8[18874368]{0:T(1024)(128)(4,1)} %bitcast.1), calls=%async_computation.4 | async-start | bytes 4194304
  18.2 10.9 %collective-permute-start.2 = (bf16[32,3072]{1,0:T(8,128)(2,1)S(1)}, bf16[32,3072]{1,0:T(8,128)(2,1)S(1)}, u32[]{:S(2)}, u32[]{:S(2)}) collective-permute-start(bf16[32,3072]{1,0:T(8,128)(2,1)S(1)} %collective-permute-done.1.refs_3_), channel_id=1, source_target_pairs={{0,2},{2,4},{4,6},{6,7},{7,5},{5,3},{3,1},{1,0},{8,10},{10,12},{12... | collective-permute-start | bytes 589832 | tf_op jit(solution)/shard_map/ppermute | solution.py:73
  20.4 10.3 %collective-permute-start.6 = (bf16[32,3072]{1,0:T(8,128)(2,1)S(1)}, bf16[32,3072]{1,0:T(8,128)(2,1)S(1)}, u32[]{:S(2)}, u32[]{:S(2)}) collective-permute-start(bf16[32,3072]{1,0:T(8,128)(2,1)S(1)} %collective-permute-done.5.refs_9_), channel_id=1, source_target_pairs={{2,0},{4,2},{6,4},{7,6},{5,7},{3,5},{1,3},{0,1},{10,8},{12,10},{14... | collective-permute-start | bytes 589832 | tf_op jit(solution)/shard_map/ppermute | solution.py:74
  24.6 8.4 %collective-permute-start.10 = (bf16[32,3072]{1,0:T(8,128)(2,1)S(1)}, bf16[32,3072]{1,0:T(8,128)(2,1)S(1)}, u32[]{:S(2)}, u32[]{:S(2)}) collective-permute-start(bf16[32,3072]{1,0:T(8,128)(2,1)S(1)} %collective-permute-done.9.refs_4_), channel_id=1, source_target_pairs={{2,0},{4,2},{6,4},{7,6},{5,7},{3,5},{1,3},{0,1},{10,8},{12,10},{14... | collective-permute-start | bytes 589832 | tf_op jit(solution)/shard_map/ppermute | solution.py:74
  24.6 8.4 %collective-permute-start.13 = (bf16[32,3072]{1,0:T(8,128)(2,1)S(1)}, bf16[32,3072]{1,0:T(8,128)(2,1)S(1)}, u32[]{:S(2)}, u32[]{:S(2)}) collective-permute-start(bf16[32,3072]{1,0:T(8,128)(2,1)S(1)} %collective-permute-done.12.refs_8_), channel_id=1, source_target_pairs={{0,2},{2,4},{4,6},{6,7},{7,5},{5,3},{3,1},{1,0},{8,10},{10,12},{12... | collective-permute-start | bytes 589832 | tf_op jit(solution)/shard_map/ppermute | solution.py:73
  29.1 5.7 %collective-permute-start.3 = (bf16[32,3072]{1,0:T(8,128)(2,1)S(1)}, bf16[32,3072]{1,0:T(8,128)(2,1)S(1)}, u32[]{:S(2)}, u32[]{:S(2)}) collective-permute-start(bf16[32,3072]{1,0:T(8,128)(2,1)S(1)} %collective-permute-done.2.refs_0_), channel_id=1, source_target_pairs={{0,2},{2,4},{4,6},{6,7},{7,5},{5,3},{3,1},{1,0},{8,10},{10,12},{12... | collective-permute-start | bytes 589832 | tf_op jit(solution)/shard_map/ppermute | solution.py:77
  30.7 5.7 %collective-permute-start.7 = (bf16[32,3072]{1,0:T(8,128)(2,1)S(1)}, bf16[32,3072]{1,0:T(8,128)(2,1)S(1)}, u32[]{:S(2)}, u32[]{:S(2)}) collective-permute-start(bf16[32,3072]{1,0:T(8,128)(2,1)S(1)} %collective-permute-done.6.refs_3_), channel_id=1, source_target_pairs={{2,0},{4,2},{6,4},{7,6},{5,7},{3,5},{1,3},{0,1},{10,8},{12,10},{14... | collective-permute-start | bytes 589832 | tf_op jit(solution)/shard_map/ppermute | solution.py:78
  37.8 2.0 %collective-permute-start.14 = (bf16[2,128,128]{2,1,0:T(8,128)(2,1)S(1)}, bf16[2,128,128]{2,1,0:T(8,128)(2,1)S(1)}, u32[]{:S(2)}, u32[]{:S(2)}) collective-permute-start(bf16[2,128,128]{2,1,0:T(8,128)(2,1)S(1)} %get-tuple-element.54.one_ref), channel_id=1, source_target_pairs={{0,8},{8,0},{16,24},{24,16},{1,9},{9,1},{17,25},{25,17},{2,10},{10... | collective-permute-start | bytes 196616 | tf_op jit(solution)/shard_map/ppermute | solution.py:396
  39.2 2.2 %collective-permute-start.16 = (bf16[2,128,128]{2,1,0:T(8,128)(2,1)S(1)}, bf16[2,128,128]{2,1,0:T(8,128)(2,1)S(1)}, u32[]{:S(2)}, u32[]{:S(2)}) collective-permute-start(bf16[2,128,128]{2,1,0:T(8,128)(2,1)S(1)} %get-tuple-element.55.one_ref), channel_id=1, source_target_pairs={{0,8},{8,0},{16,24},{24,16},{1,9},{9,1},{17,25},{25,17},{2,10},{10... | collective-permute-start | bytes 196616 | tf_op jit(solution)/shard_map/ppermute | solution.py:396
  39.8 5.9 %collective-permute-start.15 = (bf16[2,128,128]{2,1,0:T(8,128)(2,1)S(1)}, bf16[2,128,128]{2,1,0:T(8,128)(2,1)S(1)}, u32[]{:S(2)}, u32[]{:S(2)}) collective-permute-start(bf16[2,128,128]{2,1,0:T(8,128)(2,1)S(1)} %add_states.2.refs_0_), channel_id=1, source_target_pairs={{0,16},{8,24},{16,0},{24,8},{1,17},{9,25},{17,1},{25,9},{2,18},{10... | collective-permute-start | bytes 196616 | tf_op jit(solution)/shard_map/ppermute | solution.py:396
  41.4 4.3 %collective-permute-start.17 = (bf16[2,128,128]{2,1,0:T(8,128)(2,1)S(1)}, bf16[2,128,128]{2,1,0:T(8,128)(2,1)S(1)}, u32[]{:S(2)}, u32[]{:S(2)}) collective-permute-start(bf16[2,128,128]{2,1,0:T(8,128)(2,1)S(1)} %add_states.3), channel_id=1, source_target_pairs={{0,16},{8,24},{16,0},{24,8},{1,17},{9,25},{17,1},{25,9},{2,18},{10... | collective-permute-start | bytes 196616 | tf_op jit(solution)/shard_map/ppermute | solution.py:396
  42.3 3.5 %slice-start.5 = ((s8[6291456]{0:T(1024)(128)(4,1)}), s8[4194304]{0:T(1024)(128)(4,1)S(1)}, s32[]{:S(2)}) async-start(s8[6291456]{0:T(1024)(128)(4,1)} %bitcast.3), calls=%async_computation.5 | async-start | bytes 8388608
  42.3 3.5 %slice-start.6 = ((s8[6291456]{0:T(1024)(128)(4,1)}), s8[2097152]{0:T(1024)(128)(4,1)S(1)}, s32[]{:S(2)}) async-start(s8[6291456]{0:T(1024)(128)(4,1)} %bitcast.3), calls=%async_computation.6 | async-start | bytes 4194304
  42.3 3.5 %copy-start = (f32[4,128,128]{2,1,0:T(8,128)S(1)}, f32[4,128,128]{2,1,0:T(8,128)}, u32[]{:S(2)}) copy-start(f32[4,128,128]{2,1,0:T(8,128)} %initial_ref.1) | copy-start | bytes 786436
  42.3 3.5 %copy-start.1 = (f32[512]{0:T(512)S(1)}, f32[512]{0:T(512)}, u32[]{:S(2)}) copy-start(f32[512]{0:T(512)} %param.8) | copy-start | bytes 6148
  47.3 6.3 %collective-permute-start.28 = (bf16[32,3072]{1,0:T(8,128)(2,1)S(1)}, bf16[32,3072]{1,0:T(8,128)(2,1)S(1)}, u32[]{:S(2)}, u32[]{:S(2)}) collective-permute-start(bf16[32,3072]{1,0:T(8,128)(2,1)S(1)} %get-tuple-element.72), channel_id=1, source_target_pairs={{2,0},{4,2},{6,4},{7,6},{5,7},{3,5},{1,3},{0,1},{10,8},{12,10},{14... | collective-permute-start | bytes 589832 | tf_op jit(solution)/shard_map/ppermute | solution.py:360
  47.8 7.2 %collective-permute-start.24 = (bf16[32,3072]{1,0:T(8,128)(2,1)S(1)}, bf16[32,3072]{1,0:T(8,128)(2,1)S(1)}, u32[]{:S(2)}, u32[]{:S(2)}) collective-permute-start(bf16[32,3072]{1,0:T(8,128)(2,1)S(1)} %get-tuple-element.68), channel_id=1, source_target_pairs={{0,2},{2,4},{4,6},{6,7},{7,5},{5,3},{3,1},{1,0},{8,10},{10,12},{12... | collective-permute-start | bytes 589832 | tf_op jit(solution)/shard_map/ppermute | solution.py:360
  51.0 8.2 %collective-permute-start.21 = (bf16[32,3072]{1,0:T(8,128)(2,1)S(1)}, bf16[32,3072]{1,0:T(8,128)(2,1)S(1)}, u32[]{:S(2)}, u32[]{:S(2)}) collective-permute-start(bf16[32,3072]{1,0:T(8,128)(2,1)S(1)} %get-tuple-element.64), channel_id=1, source_target_pairs={{0,2},{2,4},{4,6},{6,7},{7,5},{5,3},{3,1},{1,0},{8,10},{10,12},{12... | collective-permute-start | bytes 589832 | tf_op jit(solution)/shard_map/ppermute | solution.py:360
  52.6 8.3 %collective-permute-start.18 = (bf16[32,3072]{1,0:T(8,128)(2,1)S(1)}, bf16[32,3072]{1,0:T(8,128)(2,1)S(1)}, u32[]{:S(2)}, u32[]{:S(2)}) collective-permute-start(bf16[32,3072]{1,0:T(8,128)(2,1)S(1)} %get-tuple-element.61), channel_id=1, source_target_pairs={{2,0},{4,2},{6,4},{7,6},{5,7},{3,5},{1,3},{0,1},{10,8},{12,10},{14... | collective-permute-start | bytes 589832 | tf_op jit(solution)/shard_map/ppermute | solution.py:360
  53.6 9.8 %collective-permute-start.29 = (bf16[32,3072]{1,0:T(8,128)(2,1)S(1)}, bf16[32,3072]{1,0:T(8,128)(2,1)S(1)}, u32[]{:S(2)}, u32[]{:S(2)}) collective-permute-start(bf16[32,3072]{1,0:T(8,128)(2,1)S(1)} %add_step.17), channel_id=1, source_target_pairs={{2,0},{4,2},{6,4},{7,6},{5,7},{3,5},{1,3},{0,1},{10,8},{12,10},{14... | collective-permute-start | bytes 589832 | tf_op jit(solution)/shard_map/ppermute | solution.py:360
  55.1 8.9 %collective-permute-start.25 = (bf16[32,3072]{1,0:T(8,128)(2,1)S(1)}, bf16[32,3072]{1,0:T(8,128)(2,1)S(1)}, u32[]{:S(2)}, u32[]{:S(2)}) collective-permute-start(bf16[32,3072]{1,0:T(8,128)(2,1)S(1)} %add_step.14), channel_id=1, source_target_pairs={{0,2},{2,4},{4,6},{6,7},{7,5},{5,3},{3,1},{1,0},{8,10},{10,12},{12... | collective-permute-start | bytes 589832 | tf_op jit(solution)/shard_map/ppermute | solution.py:360
  59.3 8.4 %collective-permute-start.22 = (bf16[32,3072]{1,0:T(8,128)(2,1)S(1)}, bf16[32,3072]{1,0:T(8,128)(2,1)S(1)}, u32[]{:S(2)}, u32[]{:S(2)}) collective-permute-start(bf16[32,3072]{1,0:T(8,128)(2,1)S(1)} %add_step.12), channel_id=1, source_target_pairs={{0,2},{2,4},{4,6},{6,7},{7,5},{5,3},{3,1},{1,0},{8,10},{10,12},{12... | collective-permute-start | bytes 589832 | tf_op jit(solution)/shard_map/ppermute | solution.py:360
  60.9 8.4 %collective-permute-start.19 = (bf16[32,3072]{1,0:T(8,128)(2,1)S(1)}, bf16[32,3072]{1,0:T(8,128)(2,1)S(1)}, u32[]{:S(2)}, u32[]{:S(2)}) collective-permute-start(bf16[32,3072]{1,0:T(8,128)(2,1)S(1)} %add_step.10), channel_id=1, source_target_pairs={{2,0},{4,2},{6,4},{7,6},{5,7},{3,5},{1,3},{0,1},{10,8},{12,10},{14... | collective-permute-start | bytes 589832 | tf_op jit(solution)/shard_map/ppermute | solution.py:360
  63.5 8.4 %collective-permute-start.30 = (bf16[32,3072]{1,0:T(8,128)(2,1)S(1)}, bf16[32,3072]{1,0:T(8,128)(2,1)S(1)}, u32[]{:S(2)}, u32[]{:S(2)}) collective-permute-start(bf16[32,3072]{1,0:T(8,128)(2,1)S(1)} %add_step.18), channel_id=1, source_target_pairs={{2,0},{4,2},{6,4},{7,6},{5,7},{3,5},{1,3},{0,1},{10,8},{12,10},{14... | collective-permute-start | bytes 589832 | tf_op jit(solution)/shard_map/ppermute | solution.py:360
  64.0 8.4 %collective-permute-start.26 = (bf16[32,3072]{1,0:T(8,128)(2,1)S(1)}, bf16[32,3072]{1,0:T(8,128)(2,1)S(1)}, u32[]{:S(2)}, u32[]{:S(2)}) collective-permute-start(bf16[32,3072]{1,0:T(8,128)(2,1)S(1)} %add_step.15), channel_id=1, source_target_pairs={{0,2},{2,4},{4,6},{6,7},{7,5},{5,3},{3,1},{1,0},{8,10},{10,12},{12... | collective-permute-start | bytes 589832 | tf_op jit(solution)/shard_map/ppermute | solution.py:360
  67.7 8.4 %collective-permute-start.23 = (bf16[32,3072]{1,0:T(8,128)(2,1)S(1)}, bf16[32,3072]{1,0:T(8,128)(2,1)S(1)}, u32[]{:S(2)}, u32[]{:S(2)}) collective-permute-start(bf16[32,3072]{1,0:T(8,128)(2,1)S(1)} %add_step.13), channel_id=1, source_target_pairs={{0,2},{2,4},{4,6},{6,7},{7,5},{5,3},{3,1},{1,0},{8,10},{10,12},{12... | collective-permute-start | bytes 589832 | tf_op jit(solution)/shard_map/ppermute | solution.py:360
  69.4 7.6 %collective-permute-start.20 = (bf16[32,3072]{1,0:T(8,128)(2,1)S(1)}, bf16[32,3072]{1,0:T(8,128)(2,1)S(1)}, u32[]{:S(2)}, u32[]{:S(2)}) collective-permute-start(bf16[32,3072]{1,0:T(8,128)(2,1)S(1)} %add_step.11), channel_id=1, source_target_pairs={{2,0},{4,2},{6,4},{7,6},{5,7},{3,5},{1,3},{0,1},{10,8},{12,10},{14... | collective-permute-start | bytes 589832 | tf_op jit(solution)/shard_map/ppermute | solution.py:360
  71.9 7.2 %collective-permute-start.31 = (bf16[32,3072]{1,0:T(8,128)(2,1)S(1)}, bf16[32,3072]{1,0:T(8,128)(2,1)S(1)}, u32[]{:S(2)}, u32[]{:S(2)}) collective-permute-start(bf16[32,3072]{1,0:T(8,128)(2,1)S(1)} %add_step.19), channel_id=1, source_target_pairs={{2,0},{4,2},{6,4},{7,6},{5,7},{3,5},{1,3},{0,1},{10,8},{12,10},{14... | collective-permute-start | bytes 589832 | tf_op jit(solution)/shard_map/ppermute | solution.py:360
  72.5 6.6 %collective-permute-start.27 = (bf16[32,3072]{1,0:T(8,128)(2,1)S(1)}, bf16[32,3072]{1,0:T(8,128)(2,1)S(1)}, u32[]{:S(2)}, u32[]{:S(2)}) collective-permute-start(bf16[32,3072]{1,0:T(8,128)(2,1)S(1)} %add_step.16), channel_id=1, source_target_pairs={{0,2},{2,4},{4,6},{6,7},{7,5},{5,3},{3,1},{1,0},{8,10},{10,12},{12... | collective-permute-start | bytes 589832 | tf_op jit(solution)/shard_map/ppermute | solution.py:360

commit v12 on v11

--- a/solution.py
+++ b/solution.py
@@ -243,15 +243,17 @@
                 parts[2 * block + which][:, span] = product[block * rows : (block + 1) * rows, :]
 
 
-def attend_and_project(feat_q, within, initial, exchanged, gain, out_weight, blocks, rows, head_dim):
+def attend_and_project(rows, feat_q, within, initial, exchanged, gain, out_weight, block, head_dim, flops, name):
+    columns = feat_q.shape[1]
+    half = out_weight.shape[1] // 2
     per_group = initial.shape[0] // len(exchanged)
     steps = len(exchanged[0])
     others = [other for group in exchanged for other in group]
-    n_rows, columns = feat_q.shape
-    half = out_weight.shape[1] // 2
+    count = rows.stop - rows.start
+    n_parts = 2 * (count // block)
 
     def body(q_ref, within_ref, initial_ref, gain_ref, weight_ref, *refs):
-        other_refs, normalized_ref, parts = refs[: len(others)], refs[len(others)], refs[len(others) + 1 :]
+        other_refs, parts, normalized_ref = refs[: len(others)], refs[len(others) : -1], refs[-1]
         place = lax.axis_index("ctx")
         for head in range(columns // head_dim):
             at = slice(head * head_dim, (head + 1) * head_dim)
@@ -262,42 +264,24 @@
                 prefix = prefix + jnp.where(later, other_ref[within_group].astype(F32), 0.0)
             high = prefix.astype(BF16)
             low = (prefix - high.astype(F32)).astype(BF16)
-            q = q_ref[:, at]
-            attended = within_ref[:, at] + jnp.dot(q, high, preferred_element_type=F32)
+            q = q_ref[rows, at]
+            attended = within_ref[rows, at] + jnp.dot(q, high, preferred_element_type=F32)
             attended = attended + jnp.dot(q, low, preferred_element_type=F32)
             scale = lax.rsqrt(jnp.mean(attended * attended, axis=-1, keepdims=True) + 1e-06)
             normalized_ref[:, at] = (attended * scale * gain_ref[:, at]).astype(BF16)
-        project_out(normalized_ref[n_rows - blocks * rows :, :], weight_ref, parts, rows)
+        project_out(normalized_ref[...], weight_ref, parts, block)
 
     out = call(
         body,
-        [jax.ShapeDtypeStruct((n_rows, columns), BF16)] + [jax.ShapeDtypeStruct((rows, half), BF16)] * (2 * blocks),
+        [jax.ShapeDtypeStruct((block, half), BF16)] * n_parts,
         [VMEM] * (5 + len(others)),
-        [VMEM] * (1 + 2 * blocks),
-        flops=4 * n_rows * half * columns,
+        [VMEM] * n_parts,
+        flops=flops,
         nbytes=4 * half * columns,
-        name="attend_and_project",
+        scratch_shapes=[pltpu.VMEM((count, columns), BF16)],
+        name=name,
     )(feat_q, within, initial, gain.reshape(1, columns), out_weight, *others)
-    return out[0], [out[1 + 2 * block : 3 + 2 * block] for block in range(blocks)]
-
-
-def project_rest(normalized, out_weight, blocks, rows):
-    columns = normalized.shape[1]
-    half = out_weight.shape[1] // 2
-
-    def body(normalized_ref, weight_ref, *parts):
-        project_out(normalized_ref[: blocks * rows, :], weight_ref, parts, rows)
-
-    out = call(
-        body,
-        [jax.ShapeDtypeStruct((rows, half), BF16)] * (2 * blocks),
-        [VMEM] * 2,
-        [VMEM] * (2 * blocks),
-        flops=HOP_FLOPS,
-        nbytes=4 * half * columns,
-        name="project_rest",
-    )(normalized, out_weight)
-    return [out[2 * block : 2 * block + 2] for block in range(blocks)]
+    return [out[2 * at : 2 * at + 2] for at in range(count // block)]
 
 
 def add_step(mine, got):
@@ -429,12 +413,10 @@
         states.append(state)
     feat_q, within = queries_within(halves, qkv_weight, feat_k, values, head_dim, n_fsdp, rows)
     exchanged = exchange_states(states, n_ctx)
-    soon = 1
-    normalized, parts = attend_and_project(
-        feat_q, within, initial_state, exchanged, norm_gain, out_weight, soon, rows, head_dim
-    )
-    parts = project_rest(normalized, out_weight, n_fsdp - soon, rows) + parts
-
+    last = n_rows - rows
+    common = (feat_q, within, initial_state, exchanged, norm_gain, out_weight, rows, head_dim)
+    farthest = attend_and_project(slice(last, n_rows), *common, 2 * rows * columns * width, "attend_farthest")
+    parts = attend_and_project(slice(0, last), *common, HOP_FLOPS, "attend_rest") + farthest
     return ring_scatter(parts, order, right, left)
 
 

time: 80 us -> 80.3 us (level)
  transfers between devices with their start and end apart: 32 -> 32, of which waited for: 17 -> 17; matrix products, arithmetic and copies ran while one was open for 0% -> 0% of each run, Pallas kernels for 10% -> 11%
where the time goes in v12:
time: 80.3 us; the launch traced here: 80.1 us
  starting transfers between devices  33.5 us (42%)
  waiting for transfers between devices  33 us (41%)
  Pallas kernels  12.3 us (15%)
  local copies, waits for them, and re-layouts  1.09 us (1%)
    ppermute x6, starting transfers between devices, ring_gather(): going_right[part] = lax.ppermute(going_right[part], 'fsdp', right)  13.6 us
    ppermute x7, starting transfers between devices, hop(): lax.ppermute(to_right, 'fsdp', right)  11.3 us
    ppermute x7, waiting for transfers between devices, hop(): lax.ppermute(to_left, 'fsdp', left)  8.02 us
    ppermute x6, waiting for transfers between devices, ring_gather(): going_right[part] = lax.ppermute(going_right[part], 'fsdp', right)  7.63 us
    ppermute x7, waiting for transfers between devices, hop(): lax.ppermute(to_right, 'fsdp', right)  6.74 us
    ppermute x6, waiting for transfers between devices, ring_gather(): going_left[1 - part] = lax.ppermute(going_left[1 - part], 'fsdp', left)  6.17 us
    ppermute x7, starting transfers between devices, hop(): lax.ppermute(to_left, 'fsdp', left)  3.43 us
    pallas_call x2, Pallas kernels, attend_and_project(): call(body, [jax.ShapeDtypeStruct((block, half), BF16)] * n_parts, [VMEM]...  3.38 us
  transfers between devices with their start and end apart: 32, of which 17 were waited for; matrix products, arithmetic and copies ran while one was open for 0% of the time, Pallas kernels for 11%

profile of v12, /device:TPU:0, one launch (start us, length us, event | category | flops | bytes accessed | tf_op | source)
XLA Modules:
  0.0 80.1 jit_solution(16889260503684358128)
XLA Ops:
  0.0 1.0 %fusion = (bf16[32,3072]{1,0:T(8,128)(2,1)S(1)}, bf16[32,3072]{1,0:T(8,128)(2,1)S(1)}) fusion(bf16[32,6144]{1,0:T(8,128)(2,1)} %param.5), kind=kLoop, calls=%fused_computation | loop fusion | bytes 786432 | tf_op jit(solution)/shard_map/slice | solution.py:68
  1.1 3.1 %collective-permute-start = (bf16[32,3072]{1,0:T(8,128)(2,1)S(1)}, bf16[32,3072]{1,0:T(8,128)(2,1)S(1)}, u32[]{:S(2)}, u32[]{:S(2)}) collective-permute-start(bf16[32,3072]{1,0:T(8,128)(2,1)S(1)} %get-tuple-element.72.refs_0_), channel_id=1, source_target_pairs={{0,2},{2,4},{4,6},{6,7},{7,5},{5,3},{3,1},{1,0},{8,10},{10,12},{12... | collective-permute-start | bytes 589832 | tf_op jit(solution)/shard_map/ppermute | solution.py:73
  4.1 2.0 %collective-permute-start.11 = (bf16[32,3072]{1,0:T(8,128)(2,1)S(1)}, bf16[32,3072]{1,0:T(8,128)(2,1)S(1)}, u32[]{:S(2)}, u32[]{:S(2)}) collective-permute-start(bf16[32,3072]{1,0:T(8,128)(2,1)S(1)} %get-tuple-element.71.refs_5_), channel_id=1, source_target_pairs={{0,2},{2,4},{4,6},{6,7},{7,5},{5,3},{3,1},{1,0},{8,10},{10,12},{12... | collective-permute-start | bytes 589832 | tf_op jit(solution)/shard_map/ppermute | solution.py:73
  6.2 3.6 %collective-permute-done.refs_1_.arrived_ref = bf16[32,3072]{1,0:T(8,128)(2,1)S(1)} collective-permute-done((bf16[32,3072]{1,0:T(8,128)(2,1)S(1)}, bf16[32,3072]{1,0:T(8,128)(2,1)S(1)}, u32[]{:S(2)}, u32[]{:S(2)}) %collective-permute-start) | collective-permute-done | bytes 196640 | tf_op jit(solution)/shard_map/ppermute | solution.py:73
  9.8 2.1 %collective-permute-start.1 = (bf16[32,3072]{1,0:T(8,128)(2,1)S(1)}, bf16[32,3072]{1,0:T(8,128)(2,1)S(1)}, u32[]{:S(2)}, u32[]{:S(2)}) collective-permute-start(bf16[32,3072]{1,0:T(8,128)(2,1)S(1)} %collective-permute-done.refs_1_.arrived_ref), channel_id=1, source_target_pairs={{0,2},{2,4},{4,6},{6,7},{7,5},{5,3},{3,1},{1,0},{8,10},{10,12},{12... | collective-permute-start | bytes 589832 | tf_op jit(solution)/shard_map/ppermute | solution.py:73
  12.0 2.0 %collective-permute-done.11.refs_6_ = bf16[32,3072]{1,0:T(8,128)(2,1)S(1)} collective-permute-done((bf16[32,3072]{1,0:T(8,128)(2,1)S(1)}, bf16[32,3072]{1,0:T(8,128)(2,1)S(1)}, u32[]{:S(2)}, u32[]{:S(2)}) %collective-permute-start.11) | collective-permute-done | bytes 196640 | tf_op jit(solution)/shard_map/ppermute | solution.py:73
  14.0 2.1 %collective-permute-start.12 = (bf16[32,3072]{1,0:T(8,128)(2,1)S(1)}, bf16[32,3072]{1,0:T(8,128)(2,1)S(1)}, u32[]{:S(2)}, u32[]{:S(2)}) collective-permute-start(bf16[32,3072]{1,0:T(8,128)(2,1)S(1)} %collective-permute-done.11.refs_6_), channel_id=1, source_target_pairs={{0,2},{2,4},{4,6},{6,7},{7,5},{5,3},{3,1},{1,0},{8,10},{10,12},{12... | collective-permute-start | bytes 589832 | tf_op jit(solution)/shard_map/ppermute | solution.py:73
  16.2 2.0 %collective-permute-done.1.refs_3_ = bf16[32,3072]{1,0:T(8,128)(2,1)S(1)} collective-permute-done((bf16[32,3072]{1,0:T(8,128)(2,1)S(1)}, bf16[32,3072]{1,0:T(8,128)(2,1)S(1)}, u32[]{:S(2)}, u32[]{:S(2)}) %collective-permute-start.1) | collective-permute-done | bytes 196640 | tf_op jit(solution)/shard_map/ppermute | solution.py:73
  18.2 2.1 %collective-permute-start.2 = (bf16[32,3072]{1,0:T(8,128)(2,1)S(1)}, bf16[32,3072]{1,0:T(8,128)(2,1)S(1)}, u32[]{:S(2)}, u32[]{:S(2)}) collective-permute-start(bf16[32,3072]{1,0:T(8,128)(2,1)S(1)} %collective-permute-done.1.refs_3_), channel_id=1, source_target_pairs={{0,2},{2,4},{4,6},{6,7},{7,5},{5,3},{3,1},{1,0},{8,10},{10,12},{12... | collective-permute-start | bytes 589832 | tf_op jit(solution)/shard_map/ppermute | solution.py:73
  20.4 4.2 %collective-permute-done.9.refs_4_ = bf16[32,3072]{1,0:T(8,128)(2,1)S(1)} collective-permute-done((bf16[32,3072]{1,0:T(8,128)(2,1)S(1)}, bf16[32,3072]{1,0:T(8,128)(2,1)S(1)}, u32[]{:S(2)}, u32[]{:S(2)}) %collective-permute-start.9) | collective-permute-done | bytes 196640 | tf_op jit(solution)/shard_map/ppermute | solution.py:74
  24.6 2.0 %collective-permute-start.13 = (bf16[32,3072]{1,0:T(8,128)(2,1)S(1)}, bf16[32,3072]{1,0:T(8,128)(2,1)S(1)}, u32[]{:S(2)}, u32[]{:S(2)}) collective-permute-start(bf16[32,3072]{1,0:T(8,128)(2,1)S(1)} %collective-permute-done.12.refs_8_), channel_id=1, source_target_pairs={{0,2},{2,4},{4,6},{6,7},{7,5},{5,3},{3,1},{1,0},{8,10},{10,12},{12... | collective-permute-start | bytes 589832 | tf_op jit(solution)/shard_map/ppermute | solution.py:73
  26.7 1.2 %early_keys.1 = (bf16[256,512]{1,0:T(8,128)(2,1)S(1)}, bf16[256,3072]{1,0:T(8,128)(2,1)S(1)}, bf16[256,3072]{1,0:T(8,128)(2,1)S(1)}) custom-call(bf16[32,3072]{1,0:T(8,128)(2,1)S(1)} %get-tuple-element.72.refs_0_, bf16[32,3072]{1,0:T(8,128)(2,1)S(1)} %collective-permute-done.refs_1_.arrived_ref, bf16[32,3072]{1,0:T(8,128)(2,1)S(1)} %collective-permute-done.8.refs_2_, ...), custom_call_target="tpu_custom_call" | custom-call | flops 1006632960 | bytes 6291456 | tf_op jit(solution)/shard_map/early_keys/pallas_call | solution.py:106
  27.9 1.2 %early_values.1.refs_6_ = bf16[256,512]{1,0:T(8,128)(2,1)S(1)} custom-call(bf16[256,3072]{1,0:T(8,128)(2,1)S(1)} %get-tuple-element.38.first_ref.refs_4_, bf16[256,3072]{1,0:T(8,128)(2,1)S(1)} %get-tuple-element.39.second_ref.refs_5_, bf16[3,6144,512]{2,1,0:T(8,128)(2,1)S(1)} %bitcast.2), custom_call_target="tpu_custom_call" | custom-call | flops 1006632960 | bytes 6291456 | tf_op jit(solution)/shard_map/early_values/pallas_call | solution.py:126
  29.1 1.6 %collective-permute-start.3 = (bf16[32,3072]{1,0:T(8,128)(2,1)S(1)}, bf16[32,3072]{1,0:T(8,128)(2,1)S(1)}, u32[]{:S(2)}, u32[]{:S(2)}) collective-permute-start(bf16[32,3072]{1,0:T(8,128)(2,1)S(1)} %collective-permute-done.2.refs_0_), channel_id=1, source_target_pairs={{0,2},{2,4},{4,6},{6,7},{7,5},{5,3},{3,1},{1,0},{8,10},{10,12},{12... | collective-permute-start | bytes 589832 | tf_op jit(solution)/shard_map/ppermute | solution.py:77
  30.7 0.4 collective-permute-start.7
  31.2 1.8 %collective-permute-done.10.refs_1_ = bf16[32,3072]{1,0:T(8,128)(2,1)S(1)} collective-permute-done((bf16[32,3072]{1,0:T(8,128)(2,1)S(1)}, bf16[32,3072]{1,0:T(8,128)(2,1)S(1)}, u32[]{:S(2)}, u32[]{:S(2)}) %collective-permute-start.10) | collective-permute-done | bytes 196640 | tf_op jit(solution)/shard_map/ppermute | solution.py:74
  33.1 1.7 %collective-permute-done.3.refs_0_ = bf16[32,3072]{1,0:T(8,128)(2,1)S(1)} collective-permute-done((bf16[32,3072]{1,0:T(8,128)(2,1)S(1)}, bf16[32,3072]{1,0:T(8,128)(2,1)S(1)}, u32[]{:S(2)}, u32[]{:S(2)}) %collective-permute-start.3) | collective-permute-done | bytes 196640 | tf_op jit(solution)/shard_map/ppermute | solution.py:77
  34.8 1.6 %collective-permute-done.7.refs_1_ = bf16[32,3072]{1,0:T(8,128)(2,1)S(1)} collective-permute-done((bf16[32,3072]{1,0:T(8,128)(2,1)S(1)}, bf16[32,3072]{1,0:T(8,128)(2,1)S(1)}, u32[]{:S(2)}, u32[]{:S(2)}) %collective-permute-start.7) | collective-permute-done | bytes 196640 | tf_op jit(solution)/shard_map/ppermute | solution.py:78
  36.4 1.4 %late_keys_and_values.2 = (bf16[256,3072]{1,0:T(8,128)(2,1)S(1)}, bf16[256,3072]{1,0:T(8,128)(2,1)S(1)}, bf16[256,512]{1,0:T(8,128)(2,1)S(1)}, bf16[256,512]{1,0:T(8,128)(2,1)S(1)}, bf16[2,128,128]{2,1,0:T(8,128)(2,1)S(1)}) custom-call(bf16[32,3072]{1,0:T(8,128)(2,1)S(1)} %collective-permute-, ...), custom_call_target="tpu_custom_call", output_to_operand_aliasing={{0}: (2, {}), {1}: (3, {}), {2}: (5, {}), {3}: (6, {})} | custom-call | flops 603979776 | bytes 6291456 | tf_op jit(solution)/shard_map/late_keys_and_values/pallas_call | solution.py:180
  37.8 1.4 %late_keys_and_values.3 = (bf16[256,3072]{1,0:T(8,128)(2,1)S(1)}, bf16[256,3072]{1,0:T(8,128)(2,1)S(1)}, bf16[256,512]{1,0:T(8,128)(2,1)S(1)}, bf16[256,512]{1,0:T(8,128)(2,1)S(1)}, bf16[2,128,128]{2,1,0:T(8,128)(2,1)S(1)}) custom-call(bf16[256,3072]{1,0:T(8,128)(2,1)S(1)} %get-tuple-element., ...), custom_call_target="tpu_custom_call", output_to_operand_aliasing={{0}: (0, {}), {1}: (1, {}), {2}: (3, {}), {3}: (4, {})} | custom-call | flops 5000000000 | bytes 6291456 | tf_op jit(solution)/shard_map/late_keys_and_values/pallas_call | solution.py:180
  39.2 0.6 collective-permute-start.16
  39.8 1.6 %collective-permute-start.15 = (bf16[2,128,128]{2,1,0:T(8,128)(2,1)S(1)}, bf16[2,128,128]{2,1,0:T(8,128)(2,1)S(1)}, u32[]{:S(2)}, u32[]{:S(2)}) collective-permute-start(bf16[2,128,128]{2,1,0:T(8,128)(2,1)S(1)} %add_states.2.refs_0_), channel_id=1, source_target_pairs={{0,16},{8,24},{16,0},{24,8},{1,17},{9,25},{17,1},{25,9},{2,18},{10... | collective-permute-start | bytes 196616 | tf_op jit(solution)/shard_map/ppermute | solution.py:380
  41.4 0.9 %collective-permute-start.17 = (bf16[2,128,128]{2,1,0:T(8,128)(2,1)S(1)}, bf16[2,128,128]{2,1,0:T(8,128)(2,1)S(1)}, u32[]{:S(2)}, u32[]{:S(2)}) collective-permute-start(bf16[2,128,128]{2,1,0:T(8,128)(2,1)S(1)} %add_states.3), channel_id=1, source_target_pairs={{0,16},{8,24},{16,0},{24,8},{1,17},{9,25},{17,1},{25,9},{2,18},{10... | collective-permute-start | bytes 196616 | tf_op jit(solution)/shard_map/ppermute | solution.py:380
  42.3 2.3 %queries_within.1 = (bf16[256,512]{1,0:T(8,128)(2,1)S(1)}, f32[256,512]{1,0:T(8,128)S(1)}) custom-call(bf16[256,3072]{1,0:T(8,128)(2,1)S(1)} %get-tuple-element.47.first_ref, bf16[256,3072]{1,0:T(8,128)(2,1)S(1)} %get-tuple-element.48.second_ref, bf16[3,6144,512]{2,1,0:T(8,128)(2,1)S(1)} %bitcast.2, bf16[256,512]{1,0:T(8,128)(2,1)S(1)} %get-tuple-element.49.k_ref, ...), custom_call_target="tpu_custom_call" | custom-call | flops 1744830464 | bytes 6291456 | tf_op jit(solution)/shard_map/queries_within/pallas_call | solution.py:224
  44.6 1.1 %collective-permute-done.17.refs_3_ = bf16[2,128,128]{2,1,0:T(8,128)(2,1)S(1)} collective-permute-done((bf16[2,128,128]{2,1,0:T(8,128)(2,1)S(1)}, bf16[2,128,128]{2,1,0:T(8,128)(2,1)S(1)}, u32[]{:S(2)}, u32[]{:S(2)}) %collective-permute-start.17) | collective-permute-done | bytes 65568 | tf_op jit(solution)/shard_map/ppermute | solution.py:380
  45.8 1.4 %attend_farthest.1 = (bf16[32,3072]{1,0:T(8,128)(2,1)S(1)}, bf16[32,3072]{1,0:T(8,128)(2,1)S(1)}) custom-call(bf16[256,512]{1,0:T(8,128)(2,1)S(1)} %get-tuple-element.51.q_ref, f32[256,512]{1,0:T(8,128)S(1)} %get-tuple-element.52.within_ref, f32[4,128,128]{2,1,0:T(8,128)S(1)} %copy-done, f32[1,512]{1,0:T(1,128)S(1)} %bitcast.5, ...), custom_call_target="tpu_custom_call" | custom-call | flops 201326592 | bytes 6291456 | tf_op jit(solution)/shard_map/attend_farthest/pallas_call | solution.py:274
  47.2 0.5 collective-permute-start.28
  47.7 1.6 %collective-permute-start.24 = (bf16[32,3072]{1,0:T(8,128)(2,1)S(1)}, bf16[32,3072]{1,0:T(8,128)(2,1)S(1)}, u32[]{:S(2)}, u32[]{:S(2)}) collective-permute-start(bf16[32,3072]{1,0:T(8,128)(2,1)S(1)} %get-tuple-element.66), channel_id=1, source_target_pairs={{0,2},{2,4},{4,6},{6,7},{7,5},{5,3},{3,1},{1,0},{8,10},{10,12},{12... | collective-permute-start | bytes 589832 | tf_op jit(solution)/shard_map/ppermute | solution.py:344
  49.3 1.9 %attend_rest.1 = (bf16[32,3072]{1,0:T(8,128)(2,1)S(1)}, bf16[32,3072]{1,0:T(8,128)(2,1)S(1)}, bf16[32,3072]{1,0:T(8,128)(2,1)S(1)}, bf16[32,3072]{1,0:T(8,128)(2...) custom-call(bf16[256,512]{1,0:T(8,128)(2,1)S(1)} %get-tuple-element., ...), custom_call_target="tpu_custom_call" | custom-call | flops 5000000000 | bytes 6291456 | tf_op jit(solution)/shard_map/attend_rest/pallas_call | solution.py:274
  51.2 1.6 %collective-permute-start.21 = (bf16[32,3072]{1,0:T(8,128)(2,1)S(1)}, bf16[32,3072]{1,0:T(8,128)(2,1)S(1)}, u32[]{:S(2)}, u32[]{:S(2)}) collective-permute-start(bf16[32,3072]{1,0:T(8,128)(2,1)S(1)} %get-tuple-element.62), channel_id=1, source_target_pairs={{0,2},{2,4},{4,6},{6,7},{7,5},{5,3},{3,1},{1,0},{8,10},{10,12},{12... | collective-permute-start | bytes 589832 | tf_op jit(solution)/shard_map/ppermute | solution.py:344
  53.5 0.5 collective-permute-start.29
  54.0 0.5 collective-permute-done.24.got_ref
  54.6 1.6 %collective-permute-start.25 = (bf16[32,3072]{1,0:T(8,128)(2,1)S(1)}, bf16[32,3072]{1,0:T(8,128)(2,1)S(1)}, u32[]{:S(2)}, u32[]{:S(2)}) collective-permute-start(bf16[32,3072]{1,0:T(8,128)(2,1)S(1)} %add_step.14), channel_id=1, source_target_pairs={{0,2},{2,4},{4,6},{6,7},{7,5},{5,3},{3,1},{1,0},{8,10},{10,12},{12... | collective-permute-start | bytes 589832 | tf_op jit(solution)/shard_map/ppermute | solution.py:344
  56.2 2.9 %collective-permute-done.21.got_ref = bf16[32,3072]{1,0:T(8,128)(2,1)S(1)} collective-permute-done((bf16[32,3072]{1,0:T(8,128)(2,1)S(1)}, bf16[32,3072]{1,0:T(8,128)(2,1)S(1)}, u32[]{:S(2)}, u32[]{:S(2)}) %collective-permute-start.21) | collective-permute-done | bytes 196640 | tf_op jit(solution)/shard_map/ppermute | solution.py:344
  59.1 1.6 %collective-permute-start.22 = (bf16[32,3072]{1,0:T(8,128)(2,1)S(1)}, bf16[32,3072]{1,0:T(8,128)(2,1)S(1)}, u32[]{:S(2)}, u32[]{:S(2)}) collective-permute-start(bf16[32,3072]{1,0:T(8,128)(2,1)S(1)} %add_step.12), channel_id=1, source_target_pairs={{0,2},{2,4},{4,6},{6,7},{7,5},{5,3},{3,1},{1,0},{8,10},{10,12},{12... | collective-permute-start | bytes 589832 | tf_op jit(solution)/shard_map/ppermute | solution.py:344
  60.8 0.5 collective-permute-start.19
  61.3 2.7 %collective-permute-done.29.got_ref = bf16[32,3072]{1,0:T(8,128)(2,1)S(1)} collective-permute-done((bf16[32,3072]{1,0:T(8,128)(2,1)S(1)}, bf16[32,3072]{1,0:T(8,128)(2,1)S(1)}, u32[]{:S(2)}, u32[]{:S(2)}) %collective-permute-start.29) | collective-permute-done | bytes 196640 | tf_op jit(solution)/shard_map/ppermute | solution.py:344
  64.0 0.5 collective-permute-start.30
  64.6 1.6 %collective-permute-start.26 = (bf16[32,3072]{1,0:T(8,128)(2,1)S(1)}, bf16[32,3072]{1,0:T(8,128)(2,1)S(1)}, u32[]{:S(2)}, u32[]{:S(2)}) collective-permute-start(bf16[32,3072]{1,0:T(8,128)(2,1)S(1)} %add_step.15), channel_id=1, source_target_pairs={{0,2},{2,4},{4,6},{6,7},{7,5},{5,3},{3,1},{1,0},{8,10},{10,12},{12... | collective-permute-start | bytes 589832 | tf_op jit(solution)/shard_map/ppermute | solution.py:344
  66.2 1.3 %collective-permute-done.22.got_ref = bf16[32,3072]{1,0:T(8,128)(2,1)S(1)} collective-permute-done((bf16[32,3072]{1,0:T(8,128)(2,1)S(1)}, bf16[32,3072]{1,0:T(8,128)(2,1)S(1)}, u32[]{:S(2)}, u32[]{:S(2)}) %collective-permute-start.22) | collective-permute-done | bytes 196640 | tf_op jit(solution)/shard_map/ppermute | solution.py:344
  67.6 1.6 %collective-permute-start.23 = (bf16[32,3072]{1,0:T(8,128)(2,1)S(1)}, bf16[32,3072]{1,0:T(8,128)(2,1)S(1)}, u32[]{:S(2)}, u32[]{:S(2)}) collective-permute-start(bf16[32,3072]{1,0:T(8,128)(2,1)S(1)} %add_step.13), channel_id=1, source_target_pairs={{0,2},{2,4},{4,6},{6,7},{7,5},{5,3},{3,1},{1,0},{8,10},{10,12},{12... | collective-permute-start | bytes 589832 | tf_op jit(solution)/shard_map/ppermute | solution.py:344
  69.2 0.5 collective-permute-start.20
  69.8 2.7 %collective-permute-done.30.got_ref = bf16[32,3072]{1,0:T(8,128)(2,1)S(1)} collective-permute-done((bf16[32,3072]{1,0:T(8,128)(2,1)S(1)}, bf16[32,3072]{1,0:T(8,128)(2,1)S(1)}, u32[]{:S(2)}, u32[]{:S(2)}) %collective-permute-start.30) | collective-permute-done | bytes 196640 | tf_op jit(solution)/shard_map/ppermute | solution.py:344
  72.5 0.5 collective-permute-start.31
  73.0 1.6 %collective-permute-start.27 = (bf16[32,3072]{1,0:T(8,128)(2,1)S(1)}, bf16[32,3072]{1,0:T(8,128)(2,1)S(1)}, u32[]{:S(2)}, u32[]{:S(2)}) collective-permute-start(bf16[32,3072]{1,0:T(8,128)(2,1)S(1)} %add_step.16), channel_id=1, source_target_pairs={{0,2},{2,4},{4,6},{6,7},{7,5},{5,3},{3,1},{1,0},{8,10},{10,12},{12... | collective-permute-start | bytes 589832 | tf_op jit(solution)/shard_map/ppermute | solution.py:344
  74.6 2.0 %collective-permute-done.23.got_second = bf16[32,3072]{1,0:T(8,128)(2,1)S(1)} collective-permute-done((bf16[32,3072]{1,0:T(8,128)(2,1)S(1)}, bf16[32,3072]{1,0:T(8,128)(2,1)S(1)}, u32[]{:S(2)}, u32[]{:S(2)}) %collective-permute-start.23) | collective-permute-done | bytes 196640 | tf_op jit(solution)/shard_map/ppermute | solution.py:344
  77.2 2.1 %collective-permute-done.31.second = bf16[32,3072]{1,0:T(8,128)(2,1)S(1)} collective-permute-done((bf16[32,3072]{1,0:T(8,128)(2,1)S(1)}, bf16[32,3072]{1,0:T(8,128)(2,1)S(1)}, u32[]{:S(2)}, u32[]{:S(2)}) %collective-permute-start.31) | collective-permute-done | bytes 196640 | tf_op jit(solution)/shard_map/ppermute | solution.py:344
  79.3 0.8 %finish.1 = bf16[32,6144]{1,0:T(8,128)(2,1)} custom-call(f32[2,32,3072]{2,1,0:T(8,128)S(1)} %add_own.1.gathered_ref, bf16[32,3072]{1,0:T(8,128)(2,1)S(1)} %collective-permute-done.27.first, bf16[32,3072]{1,0:T(8,128)(2,1)S(1)} %collective-permute-done.31.second), custom_call_target="tpu_custom_call" | custom-call | bytes 393216 | tf_op jit(solution)/shard_map/finish/pallas_call | solution.py:326
  (61 shorter events, 2.0 us)
Async XLA Ops:
  1.1 8.7 %collective-permute-start = (bf16[32,3072]{1,0:T(8,128)(2,1)S(1)}, bf16[32,3072]{1,0:T(8,128)(2,1)S(1)}, u32[]{:S(2)}, u32[]{:S(2)}) collective-permute-start(bf16[32,3072]{1,0:T(8,128)(2,1)S(1)} %get-tuple-element.72.refs_0_), channel_id=1, source_target_pairs={{0,2},{2,4},{4,6},{6,7},{7,5},{5,3},{3,1},{1,0},{8,10},{10,12},{12... | collective-permute-start | bytes 589832 | tf_op jit(solution)/shard_map/ppermute | solution.py:73
  4.1 7.8 %collective-permute-start.4 = (bf16[32,3072]{1,0:T(8,128)(2,1)S(1)}, bf16[32,3072]{1,0:T(8,128)(2,1)S(1)}, u32[]{:S(2)}, u32[]{:S(2)}) collective-permute-start(bf16[32,3072]{1,0:T(8,128)(2,1)S(1)} %get-tuple-element.71.refs_5_), channel_id=1, source_target_pairs={{2,0},{4,2},{6,4},{7,6},{5,7},{3,5},{1,3},{0,1},{10,8},{12,10},{14... | collective-permute-start | bytes 589832 | tf_op jit(solution)/shard_map/ppermute | solution.py:74
  4.1 9.9 %collective-permute-start.11 = (bf16[32,3072]{1,0:T(8,128)(2,1)S(1)}, bf16[32,3072]{1,0:T(8,128)(2,1)S(1)}, u32[]{:S(2)}, u32[]{:S(2)}) collective-permute-start(bf16[32,3072]{1,0:T(8,128)(2,1)S(1)} %get-tuple-element.71.refs_5_), channel_id=1, source_target_pairs={{0,2},{2,4},{4,6},{6,7},{7,5},{5,3},{3,1},{1,0},{8,10},{10,12},{12... | collective-permute-start | bytes 589832 | tf_op jit(solution)/shard_map/ppermute | solution.py:73
  6.2 10.0 %collective-permute-start.8 = (bf16[32,3072]{1,0:T(8,128)(2,1)S(1)}, bf16[32,3072]{1,0:T(8,128)(2,1)S(1)}, u32[]{:S(2)}, u32[]{:S(2)}) collective-permute-start(bf16[32,3072]{1,0:T(8,128)(2,1)S(1)} %get-tuple-element.72.refs_0_), channel_id=1, source_target_pairs={{2,0},{4,2},{6,4},{7,6},{5,7},{3,5},{1,3},{0,1},{10,8},{12,10},{14... | collective-permute-start | bytes 589832 | tf_op jit(solution)/shard_map/ppermute | solution.py:74
  9.8 8.4 %collective-permute-start.1 = (bf16[32,3072]{1,0:T(8,128)(2,1)S(1)}, bf16[32,3072]{1,0:T(8,128)(2,1)S(1)}, u32[]{:S(2)}, u32[]{:S(2)}) collective-permute-start(bf16[32,3072]{1,0:T(8,128)(2,1)S(1)} %collective-permute-done.refs_1_.arrived_ref), channel_id=1, source_target_pairs={{0,2},{2,4},{4,6},{6,7},{7,5},{5,3},{3,1},{1,0},{8,10},{10,12},{12... | collective-permute-start | bytes 589832 | tf_op jit(solution)/shard_map/ppermute | solution.py:73
  12.0 8.4 %collective-permute-start.5 = (bf16[32,3072]{1,0:T(8,128)(2,1)S(1)}, bf16[32,3072]{1,0:T(8,128)(2,1)S(1)}, u32[]{:S(2)}, u32[]{:S(2)}) collective-permute-start(bf16[32,3072]{1,0:T(8,128)(2,1)S(1)} %collective-permute-done.4.refs_7_.arrived_ref), channel_id=1, source_target_pairs={{2,0},{4,2},{6,4},{7,6},{5,7},{3,5},{1,3},{0,1},{10,8},{12,10},{14... | collective-permute-start | bytes 589832 | tf_op jit(solution)/shard_map/ppermute | solution.py:74
  14.0 10.6 %collective-permute-start.12 = (bf16[32,3072]{1,0:T(8,128)(2,1)S(1)}, bf16[32,3072]{1,0:T(8,128)(2,1)S(1)}, u32[]{:S(2)}, u32[]{:S(2)}) collective-permute-start(bf16[32,3072]{1,0:T(8,128)(2,1)S(1)} %collective-permute-done.11.refs_6_), channel_id=1, source_target_pairs={{0,2},{2,4},{4,6},{6,7},{7,5},{5,3},{3,1},{1,0},{8,10},{10,12},{12... | collective-permute-start | bytes 589832 | tf_op jit(solution)/shard_map/ppermute | solution.py:73
  16.2 8.4 %collective-permute-start.9 = (bf16[32,3072]{1,0:T(8,128)(2,1)S(1)}, bf16[32,3072]{1,0:T(8,128)(2,1)S(1)}, u32[]{:S(2)}, u32[]{:S(2)}) collective-permute-start(bf16[32,3072]{1,0:T(8,128)(2,1)S(1)} %collective-permute-done.8.refs_2_), channel_id=1, source_target_pairs={{2,0},{4,2},{6,4},{7,6},{5,7},{3,5},{1,3},{0,1},{10,8},{12,10},{14... | collective-permute-start | bytes 589832 | tf_op jit(solution)/shard_map/ppermute | solution.py:74
  16.2 10.5 %slice-start = ((s8[18874368]{0:T(1024)(128)(4,1)}), s8[4194304]{0:T(1024)(128)(4,1)S(1)}, s32[]{:S(2)}) async-start(s8[18874368]{0:T(1024)(128)(4,1)} %bitcast.1), calls=%async_computation | async-start | bytes 8388608
  16.2 10.5 %slice-start.1 = ((s8[18874368]{0:T(1024)(128)(4,1)}), s8[4194304]{0:T(1024)(128)(4,1)S(1)}, s32[]{:S(2)}) async-start(s8[18874368]{0:T(1024)(128)(4,1)} %bitcast.1), calls=%async_computation.1 | async-start | bytes 8388608
  16.2 10.5 %slice-start.2 = ((s8[18874368]{0:T(1024)(128)(4,1)}), s8[4194304]{0:T(1024)(128)(4,1)S(1)}, s32[]{:S(2)}) async-start(s8[18874368]{0:T(1024)(128)(4,1)} %bitcast.1), calls=%async_computation.2 | async-start | bytes 8388608
  16.2 10.4 %slice-start.3 = ((s8[18874368]{0:T(1024)(128)(4,1)}), s8[4194304]{0:T(1024)(128)(4,1)S(1)}, s32[]{:S(2)}) async-start(s8[18874368]{0:T(1024)(128)(4,1)} %bitcast.1), calls=%async_computation.3 | async-start | bytes 8388608
  16.2 10.4 %slice-start.4 = ((s8[18874368]{0:T(1024)(128)(4,1)}), s8[2097152]{0:T(1024)(128)(4,1)S(1)}, s32[]{:S(2)}) async-start(s8[18874368]{0:T(1024)(128)(4,1)} %bitcast.1), calls=%async_computation.4 | async-start | bytes 4194304
  18.2 10.9 %collective-permute-start.2 = (bf16[32,3072]{1,0:T(8,128)(2,1)S(1)}, bf16[32,3072]{1,0:T(8,128)(2,1)S(1)}, u32[]{:S(2)}, u32[]{:S(2)}) collective-permute-start(bf16[32,3072]{1,0:T(8,128)(2,1)S(1)} %collective-permute-done.1.refs_3_), channel_id=1, source_target_pairs={{0,2},{2,4},{4,6},{6,7},{7,5},{5,3},{3,1},{1,0},{8,10},{10,12},{12... | collective-permute-start | bytes 589832 | tf_op jit(solution)/shard_map/ppermute | solution.py:73
  20.4 10.3 %collective-permute-start.6 = (bf16[32,3072]{1,0:T(8,128)(2,1)S(1)}, bf16[32,3072]{1,0:T(8,128)(2,1)S(1)}, u32[]{:S(2)}, u32[]{:S(2)}) collective-permute-start(bf16[32,3072]{1,0:T(8,128)(2,1)S(1)} %collective-permute-done.5.refs_9_), channel_id=1, source_target_pairs={{2,0},{4,2},{6,4},{7,6},{5,7},{3,5},{1,3},{0,1},{10,8},{12,10},{14... | collective-permute-start | bytes 589832 | tf_op jit(solution)/shard_map/ppermute | solution.py:74
  24.6 8.4 %collective-permute-start.10 = (bf16[32,3072]{1,0:T(8,128)(2,1)S(1)}, bf16[32,3072]{1,0:T(8,128)(2,1)S(1)}, u32[]{:S(2)}, u32[]{:S(2)}) collective-permute-start(bf16[32,3072]{1,0:T(8,128)(2,1)S(1)} %collective-permute-done.9.refs_4_), channel_id=1, source_target_pairs={{2,0},{4,2},{6,4},{7,6},{5,7},{3,5},{1,3},{0,1},{10,8},{12,10},{14... | collective-permute-start | bytes 589832 | tf_op jit(solution)/shard_map/ppermute | solution.py:74
  24.6 8.4 %collective-permute-start.13 = (bf16[32,3072]{1,0:T(8,128)(2,1)S(1)}, bf16[32,3072]{1,0:T(8,128)(2,1)S(1)}, u32[]{:S(2)}, u32[]{:S(2)}) collective-permute-start(bf16[32,3072]{1,0:T(8,128)(2,1)S(1)} %collective-permute-done.12.refs_8_), channel_id=1, source_target_pairs={{0,2},{2,4},{4,6},{6,7},{7,5},{5,3},{3,1},{1,0},{8,10},{10,12},{12... | collective-permute-start | bytes 589832 | tf_op jit(solution)/shard_map/ppermute | solution.py:73
  29.1 5.7 %collective-permute-start.3 = (bf16[32,3072]{1,0:T(8,128)(2,1)S(1)}, bf16[32,3072]{1,0:T(8,128)(2,1)S(1)}, u32[]{:S(2)}, u32[]{:S(2)}) collective-permute-start(bf16[32,3072]{1,0:T(8,128)(2,1)S(1)} %collective-permute-done.2.refs_0_), channel_id=1, source_target_pairs={{0,2},{2,4},{4,6},{6,7},{7,5},{5,3},{3,1},{1,0},{8,10},{10,12},{12... | collective-permute-start | bytes 589832 | tf_op jit(solution)/shard_map/ppermute | solution.py:77
  30.7 5.7 %collective-permute-start.7 = (bf16[32,3072]{1,0:T(8,128)(2,1)S(1)}, bf16[32,3072]{1,0:T(8,128)(2,1)S(1)}, u32[]{:S(2)}, u32[]{:S(2)}) collective-permute-start(bf16[32,3072]{1,0:T(8,128)(2,1)S(1)} %collective-permute-done.6.refs_3_), channel_id=1, source_target_pairs={{2,0},{4,2},{6,4},{7,6},{5,7},{3,5},{1,3},{0,1},{10,8},{12,10},{14... | collective-permute-start | bytes 589832 | tf_op jit(solution)/shard_map/ppermute | solution.py:78
  37.8 2.0 %collective-permute-start.14 = (bf16[2,128,128]{2,1,0:T(8,128)(2,1)S(1)}, bf16[2,128,128]{2,1,0:T(8,128)(2,1)S(1)}, u32[]{:S(2)}, u32[]{:S(2)}) collective-permute-start(bf16[2,128,128]{2,1,0:T(8,128)(2,1)S(1)} %get-tuple-element.53.one_ref), channel_id=1, source_target_pairs={{0,8},{8,0},{16,24},{24,16},{1,9},{9,1},{17,25},{25,17},{2,10},{10... | collective-permute-start | bytes 196616 | tf_op jit(solution)/shard_map/ppermute | solution.py:380
  39.2 2.2 %collective-permute-start.16 = (bf16[2,128,128]{2,1,0:T(8,128)(2,1)S(1)}, bf16[2,128,128]{2,1,0:T(8,128)(2,1)S(1)}, u32[]{:S(2)}, u32[]{:S(2)}) collective-permute-start(bf16[2,128,128]{2,1,0:T(8,128)(2,1)S(1)} %get-tuple-element.54.one_ref), channel_id=1, source_target_pairs={{0,8},{8,0},{16,24},{24,16},{1,9},{9,1},{17,25},{25,17},{2,10},{10... | collective-permute-start | bytes 196616 | tf_op jit(solution)/shard_map/ppermute | solution.py:380
  39.8 5.9 %collective-permute-start.15 = (bf16[2,128,128]{2,1,0:T(8,128)(2,1)S(1)}, bf16[2,128,128]{2,1,0:T(8,128)(2,1)S(1)}, u32[]{:S(2)}, u32[]{:S(2)}) collective-permute-start(bf16[2,128,128]{2,1,0:T(8,128)(2,1)S(1)} %add_states.2.refs_0_), channel_id=1, source_target_pairs={{0,16},{8,24},{16,0},{24,8},{1,17},{9,25},{17,1},{25,9},{2,18},{10... | collective-permute-start | bytes 196616 | tf_op jit(solution)/shard_map/ppermute | solution.py:380
  41.4 4.3 %collective-permute-start.17 = (bf16[2,128,128]{2,1,0:T(8,128)(2,1)S(1)}, bf16[2,128,128]{2,1,0:T(8,128)(2,1)S(1)}, u32[]{:S(2)}, u32[]{:S(2)}) collective-permute-start(bf16[2,128,128]{2,1,0:T(8,128)(2,1)S(1)} %add_states.3), channel_id=1, source_target_pairs={{0,16},{8,24},{16,0},{24,8},{1,17},{9,25},{17,1},{25,9},{2,18},{10... | collective-permute-start | bytes 196616 | tf_op jit(solution)/shard_map/ppermute | solution.py:380
  42.3 3.5 %slice-start.5 = ((s8[6291456]{0:T(1024)(128)(4,1)}), s8[4194304]{0:T(1024)(128)(4,1)S(1)}, s32[]{:S(2)}) async-start(s8[6291456]{0:T(1024)(128)(4,1)} %bitcast.3), calls=%async_computation.5 | async-start | bytes 8388608
  42.3 3.5 %slice-start.6 = ((s8[6291456]{0:T(1024)(128)(4,1)}), s8[2097152]{0:T(1024)(128)(4,1)S(1)}, s32[]{:S(2)}) async-start(s8[6291456]{0:T(1024)(128)(4,1)} %bitcast.3), calls=%async_computation.6 | async-start | bytes 4194304
  42.3 3.5 %copy-start = (f32[4,128,128]{2,1,0:T(8,128)S(1)}, f32[4,128,128]{2,1,0:T(8,128)}, u32[]{:S(2)}) copy-start(f32[4,128,128]{2,1,0:T(8,128)} %initial_ref.3) | copy-start | bytes 786436
  42.3 3.5 %copy-start.1 = (f32[512]{0:T(512)S(1)}, f32[512]{0:T(512)}, u32[]{:S(2)}) copy-start(f32[512]{0:T(512)} %param.8) | copy-start | bytes 6148
  47.2 6.3 %collective-permute-start.28 = (bf16[32,3072]{1,0:T(8,128)(2,1)S(1)}, bf16[32,3072]{1,0:T(8,128)(2,1)S(1)}, u32[]{:S(2)}, u32[]{:S(2)}) collective-permute-start(bf16[32,3072]{1,0:T(8,128)(2,1)S(1)} %get-tuple-element.70), channel_id=1, source_target_pairs={{2,0},{4,2},{6,4},{7,6},{5,7},{3,5},{1,3},{0,1},{10,8},{12,10},{14... | collective-permute-start | bytes 589832 | tf_op jit(solution)/shard_map/ppermute | solution.py:344
  47.7 6.8 %collective-permute-start.24 = (bf16[32,3072]{1,0:T(8,128)(2,1)S(1)}, bf16[32,3072]{1,0:T(8,128)(2,1)S(1)}, u32[]{:S(2)}, u32[]{:S(2)}) collective-permute-start(bf16[32,3072]{1,0:T(8,128)(2,1)S(1)} %get-tuple-element.66), channel_id=1, source_target_pairs={{0,2},{2,4},{4,6},{6,7},{7,5},{5,3},{3,1},{1,0},{8,10},{10,12},{12... | collective-permute-start | bytes 589832 | tf_op jit(solution)/shard_map/ppermute | solution.py:344
  51.2 7.9 %collective-permute-start.21 = (bf16[32,3072]{1,0:T(8,128)(2,1)S(1)}, bf16[32,3072]{1,0:T(8,128)(2,1)S(1)}, u32[]{:S(2)}, u32[]{:S(2)}) collective-permute-start(bf16[32,3072]{1,0:T(8,128)(2,1)S(1)} %get-tuple-element.62), channel_id=1, source_target_pairs={{0,2},{2,4},{4,6},{6,7},{7,5},{5,3},{3,1},{1,0},{8,10},{10,12},{12... | collective-permute-start | bytes 589832 | tf_op jit(solution)/shard_map/ppermute | solution.py:344
  52.8 7.9 %collective-permute-start.18 = (bf16[32,3072]{1,0:T(8,128)(2,1)S(1)}, bf16[32,3072]{1,0:T(8,128)(2,1)S(1)}, u32[]{:S(2)}, u32[]{:S(2)}) collective-permute-start(bf16[32,3072]{1,0:T(8,128)(2,1)S(1)} %get-tuple-element.59), channel_id=1, source_target_pairs={{2,0},{4,2},{6,4},{7,6},{5,7},{3,5},{1,3},{0,1},{10,8},{12,10},{14... | collective-permute-start | bytes 589832 | tf_op jit(solution)/shard_map/ppermute | solution.py:344
  53.5 10.5 %collective-permute-start.29 = (bf16[32,3072]{1,0:T(8,128)(2,1)S(1)}, bf16[32,3072]{1,0:T(8,128)(2,1)S(1)}, u32[]{:S(2)}, u32[]{:S(2)}) collective-permute-start(bf16[32,3072]{1,0:T(8,128)(2,1)S(1)} %add_step.17), channel_id=1, source_target_pairs={{2,0},{4,2},{6,4},{7,6},{5,7},{3,5},{1,3},{0,1},{10,8},{12,10},{14... | collective-permute-start | bytes 589832 | tf_op jit(solution)/shard_map/ppermute | solution.py:344
  54.6 10.0 %collective-permute-start.25 = (bf16[32,3072]{1,0:T(8,128)(2,1)S(1)}, bf16[32,3072]{1,0:T(8,128)(2,1)S(1)}, u32[]{:S(2)}, u32[]{:S(2)}) collective-permute-start(bf16[32,3072]{1,0:T(8,128)(2,1)S(1)} %add_step.14), channel_id=1, source_target_pairs={{0,2},{2,4},{4,6},{6,7},{7,5},{5,3},{3,1},{1,0},{8,10},{10,12},{12... | collective-permute-start | bytes 589832 | tf_op jit(solution)/shard_map/ppermute | solution.py:344
  59.1 8.4 %collective-permute-start.22 = (bf16[32,3072]{1,0:T(8,128)(2,1)S(1)}, bf16[32,3072]{1,0:T(8,128)(2,1)S(1)}, u32[]{:S(2)}, u32[]{:S(2)}) collective-permute-start(bf16[32,3072]{1,0:T(8,128)(2,1)S(1)} %add_step.12), channel_id=1, source_target_pairs={{0,2},{2,4},{4,6},{6,7},{7,5},{5,3},{3,1},{1,0},{8,10},{10,12},{12... | collective-permute-start | bytes 589832 | tf_op jit(solution)/shard_map/ppermute | solution.py:344
  60.8 8.4 %collective-permute-start.19 = (bf16[32,3072]{1,0:T(8,128)(2,1)S(1)}, bf16[32,3072]{1,0:T(8,128)(2,1)S(1)}, u32[]{:S(2)}, u32[]{:S(2)}) collective-permute-start(bf16[32,3072]{1,0:T(8,128)(2,1)S(1)} %add_step.10), channel_id=1, source_target_pairs={{2,0},{4,2},{6,4},{7,6},{5,7},{3,5},{1,3},{0,1},{10,8},{12,10},{14... | collective-permute-start | bytes 589832 | tf_op jit(solution)/shard_map/ppermute | solution.py:344
  64.0 8.4 %collective-permute-start.30 = (bf16[32,3072]{1,0:T(8,128)(2,1)S(1)}, bf16[32,3072]{1,0:T(8,128)(2,1)S(1)}, u32[]{:S(2)}, u32[]{:S(2)}) collective-permute-start(bf16[32,3072]{1,0:T(8,128)(2,1)S(1)} %add_step.18), channel_id=1, source_target_pairs={{2,0},{4,2},{6,4},{7,6},{5,7},{3,5},{1,3},{0,1},{10,8},{12,10},{14... | collective-permute-start | bytes 589832 | tf_op jit(solution)/shard_map/ppermute | solution.py:344
  64.6 8.4 %collective-permute-start.26 = (bf16[32,3072]{1,0:T(8,128)(2,1)S(1)}, bf16[32,3072]{1,0:T(8,128)(2,1)S(1)}, u32[]{:S(2)}, u32[]{:S(2)}) collective-permute-start(bf16[32,3072]{1,0:T(8,128)(2,1)S(1)} %add_step.15), channel_id=1, source_target_pairs={{0,2},{2,4},{4,6},{6,7},{7,5},{5,3},{3,1},{1,0},{8,10},{10,12},{12... | collective-permute-start | bytes 589832 | tf_op jit(solution)/shard_map/ppermute | solution.py:344
  67.6 9.1 %collective-permute-start.23 = (bf16[32,3072]{1,0:T(8,128)(2,1)S(1)}, bf16[32,3072]{1,0:T(8,128)(2,1)S(1)}, u32[]{:S(2)}, u32[]{:S(2)}) collective-permute-start(bf16[32,3072]{1,0:T(8,128)(2,1)S(1)} %add_step.13), channel_id=1, source_target_pairs={{0,2},{2,4},{4,6},{6,7},{7,5},{5,3},{3,1},{1,0},{8,10},{10,12},{12... | collective-permute-start | bytes 589832 | tf_op jit(solution)/shard_map/ppermute | solution.py:344
  69.2 7.9 %collective-permute-start.20 = (bf16[32,3072]{1,0:T(8,128)(2,1)S(1)}, bf16[32,3072]{1,0:T(8,128)(2,1)S(1)}, u32[]{:S(2)}, u32[]{:S(2)}) collective-permute-start(bf16[32,3072]{1,0:T(8,128)(2,1)S(1)} %add_step.11), channel_id=1, source_target_pairs={{2,0},{4,2},{6,4},{7,6},{5,7},{3,5},{1,3},{0,1},{10,8},{12,10},{14... | collective-permute-start | bytes 589832 | tf_op jit(solution)/shard_map/ppermute | solution.py:344
  72.5 6.8 %collective-permute-start.31 = (bf16[32,3072]{1,0:T(8,128)(2,1)S(1)}, bf16[32,3072]{1,0:T(8,128)(2,1)S(1)}, u32[]{:S(2)}, u32[]{:S(2)}) collective-permute-start(bf16[32,3072]{1,0:T(8,128)(2,1)S(1)} %add_step.19), channel_id=1, source_target_pairs={{2,0},{4,2},{6,4},{7,6},{5,7},{3,5},{1,3},{0,1},{10,8},{12,10},{14... | collective-permute-start | bytes 589832 | tf_op jit(solution)/shard_map/ppermute | solution.py:344
  73.0 6.3 %collective-permute-start.27 = (bf16[32,3072]{1,0:T(8,128)(2,1)S(1)}, bf16[32,3072]{1,0:T(8,128)(2,1)S(1)}, u32[]{:S(2)}, u32[]{:S(2)}) collective-permute-start(bf16[32,3072]{1,0:T(8,128)(2,1)S(1)} %add_step.16), channel_id=1, source_target_pairs={{0,2},{2,4},{4,6},{6,7},{7,5},{5,3},{3,1},{1,0},{8,10},{10,12},{12... | collective-permute-start | bytes 589832 | tf_op jit(solution)/shard_map/ppermute | solution.py:344

commit v13 on v11

--- a/solution.py
+++ b/solution.py
@@ -153,21 +153,47 @@
     )(*pieces[0], *pieces[1], *halves, *after)
 
 
-def late_keys_and_values(far, halves, weight, feat_k, values, start, count, head_dim, early, after):
-    n_rows, half = halves[0].shape
+def first_pass(far, rows, weight, early, after):
+    n_rows, half = rows.shape
+    columns = weight.shape[2]
+
+    def body(*refs):
+        far_ref, weight_ref, rows_ref, out_ref = refs[0], refs[2], refs[-2], refs[-1]
+        rows_ref[n_rows - far_ref.shape[0] :, :] = far_ref[...]
+        for place in range(2):
+            out_ref[place] = jnp.dot(rows_ref[early:, :], weight_ref[1 + place, :half, :], preferred_element_type=F32)
+
+    return call(
+        body,
+        [
+            jax.ShapeDtypeStruct(rows.shape, BF16),
+            jax.ShapeDtypeStruct((2, n_rows - early, columns), F32),
+        ],
+        [VMEM] * 3 + [ANY] * len(after),
+        [VMEM] * 2,
+        flops=4 * (n_rows - early) * half * columns,
+        nbytes=4 * half * columns,
+        input_output_aliases={1: 0},
+        name="first_pass",
+    )(far, rows, weight, *after)
+
+
+def late_keys_and_values(far, rows, weight, first, feat_k, values, start, count, head_dim, early):
+    n_rows, half = rows.shape
     columns = count * head_dim
     n_far = len(far)
     span = slice(start * head_dim, start * head_dim + columns)
 
     def body(*refs):
-        weight_ref = refs[n_far + 2]
-        rows_refs, (feat_ref, values_ref, state_ref) = refs[-5:-3], refs[-3:]
-        for piece, rows_ref in zip(refs[:n_far], rows_refs):
-            rows_ref[n_rows - piece.shape[0] :, :] = piece[...]
+        weight_ref, first_ref = refs[n_far + 1 : n_far + 3]
+        rows_ref, feat_ref, values_ref, state_ref = refs[-4:]
+        for far_ref in refs[:n_far]:
+            rows_ref[n_rows - far_ref.shape[0] :, :] = far_ref[...]
 
         def product(which):
-            total = jnp.dot(rows_refs[0][early:, :], weight_ref[which, :half, span], preferred_element_type=F32)
-            return total + jnp.dot(rows_refs[1][early:, :], weight_ref[which, half:, span], preferred_element_type=F32)
+            return first_ref[which - 1, :, span] + jnp.dot(
+                rows_ref[early:, :], weight_ref[which, half:, span], preferred_element_type=F32
+            )
 
         feat_ref[early:, span] = feature_map(product(1)).astype(BF16)
         values_ref[early:, span] = product(2).astype(BF16)
@@ -177,18 +203,17 @@
                 feat_ref[:, at], values_ref[:, at], (((0,), (0,)), ((), ())), preferred_element_type=F32
             ).astype(BF16)
 
-    out = call(
-        body,
-        [jax.ShapeDtypeStruct(array.shape, BF16) for array in (*halves, feat_k, values)]
+    return call(
+        body,
+        [jax.ShapeDtypeStruct(array.shape, BF16) for array in (rows, feat_k, values)]
         + [jax.ShapeDtypeStruct((count, head_dim, head_dim), BF16)],
-        [VMEM] * (n_far + 5) + [ANY] * len(after),
-        [VMEM] * 5,
-        flops=8 * (n_rows - early) * half * columns if far else HOP_FLOPS,
-        nbytes=8 * half * columns,
-        input_output_aliases={n_far: 0, n_far + 1: 1, n_far + 3: 2, n_far + 4: 3},
+        [VMEM] * (n_far + 5),
+        [VMEM] * 4,
+        flops=4 * (n_rows - early) * half * columns if far else HOP_FLOPS,
+        nbytes=4 * half * columns,
+        input_output_aliases={n_far: 0, n_far + 3: 1, n_far + 4: 2},
         name="late_keys_and_values",
-    )(*far, *halves, weight, feat_k, values, *after)
-    return out[:2], *out[2:]
+    )(*far, rows, weight, first, feat_k, values)
 
 
 def queries_within(halves, qkv_weight, feat_k, values, head_dim, size, rows):
@@ -417,16 +442,18 @@
     early = blocks * rows
     feat_k, *halves = early_keys(held[0][:blocks], held[1][:blocks], qkv_weight, n_rows)
     values = early_values(*halves, qkv_weight, early)
-    halves = assemble_late([held[0][blocks:-1], held[1][blocks:-1]], halves, early, [values])
+    first_rows, second_rows = assemble_late([held[0][blocks:-1], held[1][blocks:-1]], halves, early, [values])
     marks = [mark(held[0][1]), mark(held[1][2])]
+    first_rows, first = first_pass(held[0][-1], first_rows, qkv_weight, early, marks + [feat_k])
     count = heads_here // 2 if heads_here % 2 == 0 else heads_here
     states = []
     for start in range(0, heads_here, count):
-        far = [held[0][-1], held[1][-1]] if start == 0 else []
-        halves, feat_k, values, state = late_keys_and_values(
-            far, halves, qkv_weight, feat_k, values, start, count, head_dim, early, marks if start == 0 else []
+        far = [held[1][-1]] if start == 0 else []
+        second_rows, feat_k, values, state = late_keys_and_values(
+            far, second_rows, qkv_weight, first, feat_k, values, start, count, head_dim, early
         )
         states.append(state)
+    halves = (first_rows, second_rows)
     feat_q, within = queries_within(halves, qkv_weight, feat_k, values, head_dim, n_fsdp, rows)
     exchanged = exchange_states(states, n_ctx)
     soon = 1

time: 80 us -> 79.7 us (level)
    ppermute x7, starting transfers between devices: 11.3 us -> 4.63 us  [hop(): lax.ppermute(to_right, 'fsdp', right)]
    ppermute x7, starting transfers between devices: 3.45 us -> 9.87 us  [hop(): lax.ppermute(to_left, 'fsdp', left)]
    ppermute x7, waiting for transfers between devices: 7.43 us -> 12.2 us  [hop(): lax.ppermute(to_right, 'fsdp', right)]
    ppermute x6, waiting for transfers between devices: 6.17 us -> 10.4 us  [ring_gather(): going_left[1 - part] = lax.ppermute(going_left[1 - part], 'fsdp', left)]
    ppermute x6, waiting for transfers between devices: 7.63 us -> 3.6 us  [ring_gather(): going_right[part] = lax.ppermute(going_right[part], 'fsdp', right)]
    ppermute x7, waiting for transfers between devices: 7.35 us -> 3.45 us  [hop(): lax.ppermute(to_left, 'fsdp', left)]
    ppermute x6, starting transfers between devices: 13.6 us -> 11.4 us  [ring_gather(): going_right[part] = lax.ppermute(going_right[part], 'fsdp', right)]
    ppermute x6, starting transfers between devices: 0.02 us -> 1.95 us  [ring_gather(): going_left[1 - part] = lax.ppermute(going_left[1 - part], 'fsdp', left)]
  transfers between devices with their start and end apart: 32 -> 32, of which waited for: 17 -> 17; matrix products, arithmetic and copies ran while one was open for 0% -> 0% of each run, Pallas kernels for 10% -> 11%
where the time goes in v13:
time: 79.7 us; the launch traced here: 79.6 us
  waiting for transfers between devices  33.1 us (42%)
  starting transfers between devices  33 us (41%)
  Pallas kernels  12.2 us (15%)
  local copies, waits for them, and re-layouts  1.09 us (1%)
    ppermute x7, waiting for transfers between devices, hop(): lax.ppermute(to_right, 'fsdp', right)  12.2 us
    ppermute x6, starting transfers between devices, ring_gather(): going_right[part] = lax.ppermute(going_right[part], 'fsdp', right)  11.4 us
    ppermute x6, waiting for transfers between devices, ring_gather(): going_left[1 - part] = lax.ppermute(going_left[1 - part], 'fsdp', left)  10.4 us
    ppermute x7, starting transfers between devices, hop(): lax.ppermute(to_left, 'fsdp', left)  9.87 us
    ppermute x7, starting transfers between devices, hop(): lax.ppermute(to_right, 'fsdp', right)  4.63 us
    ppermute x6, waiting for transfers between devices, ring_gather(): going_right[part] = lax.ppermute(going_right[part], 'fsdp', right)  3.6 us
    ppermute x7, waiting for transfers between devices, hop(): lax.ppermute(to_left, 'fsdp', left)  3.45 us
    ppermute x4, starting transfers between devices, exchange_states(): received[at].append(lax.ppermute(total, 'ctx', pairs))  3.09 us
  transfers between devices with their start and end apart: 32, of which 17 were waited for; matrix products, arithmetic and copies ran while one was open for 0% of the time, Pallas kernels for 11%

profile of v13, /device:TPU:0, one launch (start us, length us, event | category | flops | bytes accessed | tf_op | source)
XLA Modules:
  0.0 79.6 jit_solution(663761206433619399)
XLA Ops:
  0.0 1.0 %fusion = (bf16[32,3072]{1,0:T(8,128)(2,1)S(1)}, bf16[32,3072]{1,0:T(8,128)(2,1)S(1)}) fusion(bf16[32,6144]{1,0:T(8,128)(2,1)} %param.5), kind=kLoop, calls=%fused_computation | loop fusion | bytes 786432 | tf_op jit(solution)/shard_map/slice | solution.py:68
  1.1 3.1 %collective-permute-start = (bf16[32,3072]{1,0:T(8,128)(2,1)S(1)}, bf16[32,3072]{1,0:T(8,128)(2,1)S(1)}, u32[]{:S(2)}, u32[]{:S(2)}) collective-permute-start(bf16[32,3072]{1,0:T(8,128)(2,1)S(1)} %get-tuple-element.74.refs_0_), channel_id=1, source_target_pairs={{0,2},{2,4},{4,6},{6,7},{7,5},{5,3},{3,1},{1,0},{8,10},{10,12},{12... | collective-permute-start | bytes 589832 | tf_op jit(solution)/shard_map/ppermute | solution.py:73
  4.1 1.9 %collective-permute-start.4 = (bf16[32,3072]{1,0:T(8,128)(2,1)S(1)}, bf16[32,3072]{1,0:T(8,128)(2,1)S(1)}, u32[]{:S(2)}, u32[]{:S(2)}) collective-permute-start(bf16[32,3072]{1,0:T(8,128)(2,1)S(1)} %get-tuple-element.74.refs_0_), channel_id=1, source_target_pairs={{2,0},{4,2},{6,4},{7,6},{5,7},{3,5},{1,3},{0,1},{10,8},{12,10},{14... | collective-permute-start | bytes 589832 | tf_op jit(solution)/shard_map/ppermute | solution.py:74
  6.2 3.6 %collective-permute-done.refs_1_.arrived_ref = bf16[32,3072]{1,0:T(8,128)(2,1)S(1)} collective-permute-done((bf16[32,3072]{1,0:T(8,128)(2,1)S(1)}, bf16[32,3072]{1,0:T(8,128)(2,1)S(1)}, u32[]{:S(2)}, u32[]{:S(2)}) %collective-permute-start) | collective-permute-done | bytes 196640 | tf_op jit(solution)/shard_map/ppermute | solution.py:73
  9.8 2.1 %collective-permute-start.1 = (bf16[32,3072]{1,0:T(8,128)(2,1)S(1)}, bf16[32,3072]{1,0:T(8,128)(2,1)S(1)}, u32[]{:S(2)}, u32[]{:S(2)}) collective-permute-start(bf16[32,3072]{1,0:T(8,128)(2,1)S(1)} %collective-permute-done.refs_1_.arrived_ref), channel_id=1, source_target_pairs={{0,2},{2,4},{4,6},{6,7},{7,5},{5,3},{3,1},{1,0},{8,10},{10,12},{12... | collective-permute-start | bytes 589832 | tf_op jit(solution)/shard_map/ppermute | solution.py:73
  12.0 4.2 %collective-permute-done.4.refs_2_ = bf16[32,3072]{1,0:T(8,128)(2,1)S(1)} collective-permute-done((bf16[32,3072]{1,0:T(8,128)(2,1)S(1)}, bf16[32,3072]{1,0:T(8,128)(2,1)S(1)}, u32[]{:S(2)}, u32[]{:S(2)}) %collective-permute-start.4) | collective-permute-done | bytes 196640 | tf_op jit(solution)/shard_map/ppermute | solution.py:74
  16.2 2.0 %collective-permute-start.8 = (bf16[32,3072]{1,0:T(8,128)(2,1)S(1)}, bf16[32,3072]{1,0:T(8,128)(2,1)S(1)}, u32[]{:S(2)}, u32[]{:S(2)}) collective-permute-start(bf16[32,3072]{1,0:T(8,128)(2,1)S(1)} %collective-permute-done.7.refs_6_), channel_id=1, source_target_pairs={{0,2},{2,4},{4,6},{6,7},{7,5},{5,3},{3,1},{1,0},{8,10},{10,12},{12... | collective-permute-start | bytes 589832 | tf_op jit(solution)/shard_map/ppermute | solution.py:73
  18.2 2.1 %collective-permute-done.11.refs_9_ = bf16[32,3072]{1,0:T(8,128)(2,1)S(1)} collective-permute-done((bf16[32,3072]{1,0:T(8,128)(2,1)S(1)}, bf16[32,3072]{1,0:T(8,128)(2,1)S(1)}, u32[]{:S(2)}, u32[]{:S(2)}) %collective-permute-start.11) | collective-permute-done | bytes 196640 | tf_op jit(solution)/shard_map/ppermute | solution.py:74
  20.4 2.0 %collective-permute-start.2 = (bf16[32,3072]{1,0:T(8,128)(2,1)S(1)}, bf16[32,3072]{1,0:T(8,128)(2,1)S(1)}, u32[]{:S(2)}, u32[]{:S(2)}) collective-permute-start(bf16[32,3072]{1,0:T(8,128)(2,1)S(1)} %collective-permute-done.1.refs_3_), channel_id=1, source_target_pairs={{0,2},{2,4},{4,6},{6,7},{7,5},{5,3},{3,1},{1,0},{8,10},{10,12},{12... | collective-permute-start | bytes 589832 | tf_op jit(solution)/shard_map/ppermute | solution.py:73
  22.4 2.2 %collective-permute-done.5.refs_4_ = bf16[32,3072]{1,0:T(8,128)(2,1)S(1)} collective-permute-done((bf16[32,3072]{1,0:T(8,128)(2,1)S(1)}, bf16[32,3072]{1,0:T(8,128)(2,1)S(1)}, u32[]{:S(2)}, u32[]{:S(2)}) %collective-permute-start.5) | collective-permute-done | bytes 196640 | tf_op jit(solution)/shard_map/ppermute | solution.py:74
  24.6 2.0 %collective-permute-start.9 = (bf16[32,3072]{1,0:T(8,128)(2,1)S(1)}, bf16[32,3072]{1,0:T(8,128)(2,1)S(1)}, u32[]{:S(2)}, u32[]{:S(2)}) collective-permute-start(bf16[32,3072]{1,0:T(8,128)(2,1)S(1)} %collective-permute-done.8.refs_8_), channel_id=1, source_target_pairs={{0,2},{2,4},{4,6},{6,7},{7,5},{5,3},{3,1},{1,0},{8,10},{10,12},{12... | collective-permute-start | bytes 589832 | tf_op jit(solution)/shard_map/ppermute | solution.py:73
  26.7 1.2 %early_keys.1 = (bf16[256,512]{1,0:T(8,128)(2,1)S(1)}, bf16[256,3072]{1,0:T(8,128)(2,1)S(1)}, bf16[256,3072]{1,0:T(8,128)(2,1)S(1)}) custom-call(bf16[32,3072]{1,0:T(8,128)(2,1)S(1)} %get-tuple-element.74.refs_0_, bf16[32,3072]{1,0:T(8,128)(2,1)S(1)} %collective-permute-done.refs_1_.arrived_ref, bf16[32,3072]{1,0:T(8,128)(2,1)S(1)} %collective-permute-done.4.refs_2_, ...), custom_call_target="tpu_custom_call" | custom-call | flops 1006632960 | bytes 6291456 | tf_op jit(solution)/shard_map/early_keys/pallas_call | solution.py:106
  27.9 1.2 %early_values.1.refs_6_.refs_5_ = bf16[256,512]{1,0:T(8,128)(2,1)S(1)} custom-call(bf16[256,3072]{1,0:T(8,128)(2,1)S(1)} %get-tuple-element.39.first_ref.refs_4_, bf16[256,3072]{1,0:T(8,128)(2,1)S(1)} %get-tuple-element.40.second_ref.refs_5_, bf16[3,6144,512]{2,1,0:T(8,128)(2,1)S(1)} %bitcast.2), custom_call_target="tpu_custom_call" | custom-call | flops 1006632960 | bytes 6291456 | tf_op jit(solution)/shard_map/early_values/pallas_call | solution.py:126
  29.1 1.6 %collective-permute-start.3 = (bf16[32,3072]{1,0:T(8,128)(2,1)S(1)}, bf16[32,3072]{1,0:T(8,128)(2,1)S(1)}, u32[]{:S(2)}, u32[]{:S(2)}) collective-permute-start(bf16[32,3072]{1,0:T(8,128)(2,1)S(1)} %collective-permute-done.2.refs_0_), channel_id=1, source_target_pairs={{0,2},{2,4},{4,6},{6,7},{7,5},{5,3},{3,1},{1,0},{8,10},{10,12},{12... | collective-permute-start | bytes 589832 | tf_op jit(solution)/shard_map/ppermute | solution.py:77
  30.7 0.4 collective-permute-start.13
  31.2 1.8 %collective-permute-done.6.refs_1_ = bf16[32,3072]{1,0:T(8,128)(2,1)S(1)} collective-permute-done((bf16[32,3072]{1,0:T(8,128)(2,1)S(1)}, bf16[32,3072]{1,0:T(8,128)(2,1)S(1)}, u32[]{:S(2)}, u32[]{:S(2)}) %collective-permute-start.6) | collective-permute-done | bytes 196640 | tf_op jit(solution)/shard_map/ppermute | solution.py:74
  33.1 1.7 %collective-permute-done.3.refs_0_ = bf16[32,3072]{1,0:T(8,128)(2,1)S(1)} collective-permute-done((bf16[32,3072]{1,0:T(8,128)(2,1)S(1)}, bf16[32,3072]{1,0:T(8,128)(2,1)S(1)}, u32[]{:S(2)}, u32[]{:S(2)}) %collective-permute-start.3) | collective-permute-done | bytes 196640 | tf_op jit(solution)/shard_map/ppermute | solution.py:77
  34.8 1.1 %first_pass.1 = (bf16[256,3072]{1,0:T(8,128)(2,1)S(1)}, f32[2,96,512]{2,1,0:T(8,128)S(1)}) custom-call(bf16[32,3072]{1,0:T(8,128)(2,1)S(1)} %collective-permute-done.3.refs_0_, bf16[256,3072]{1,0:T(8,128)(2,1)S(1)} %get-tuple-element.41.refs_1_, bf16[3,6144,512]{2,1,0:T(8,128)(2,1)S(1)} %bitcast.2, ...), custom_call_target="tpu_custom_call", output_to_operand_aliasing={{0}: (1, {})} | custom-call | flops 603979776 | bytes 6291456 | tf_op jit(solution)/shard_map/first_pass/pallas_call | solution.py:166
  35.9 0.5 collective-permute-done.13.refs_0_
  36.4 0.9 %late_keys_and_values.2 = (bf16[256,3072]{1,0:T(8,128)(2,1)S(1)}, bf16[256,512]{1,0:T(8,128)(2,1)S(1)}, bf16[256,512]{1,0:T(8,128)(2,1)S(1)}, bf16[2,128,128]{2,1,0:T(8,128)(2,1)S(1)}) custom-call(bf16[32,3072]{1,0:T(8,128)(2,1)S(1)} %collective-permute-done.13.refs_0_, ...), custom_call_target="tpu_custom_call", output_to_operand_aliasing={{0}: (1, {}), {1}: (4, {}), {2}: (5, {})} | custom-call | flops 301989888 | bytes 3145728 | tf_op jit(solution)/shard_map/late_keys_and_values/pallas_call | solution.py:206
  37.3 0.9 %late_keys_and_values.3 = (bf16[256,3072]{1,0:T(8,128)(2,1)S(1)}, bf16[256,512]{1,0:T(8,128)(2,1)S(1)}, bf16[256,512]{1,0:T(8,128)(2,1)S(1)}, bf16[2,128,128]{2,1,0:T(8,128)(2,1)S(1)}) custom-call(bf16[256,3072]{1,0:T(8,128)(2,1)S(1)} %get-tuple-element.46.refs_0_, ...), custom_call_target="tpu_custom_call", output_to_operand_aliasing={{0}: (0, {}), {1}: (3, {}), {2}: (4, {})} | custom-call | flops 5000000000 | bytes 3145728 | tf_op jit(solution)/shard_map/late_keys_and_values/pallas_call | solution.py:206
  38.2 0.6 collective-permute-start.16
  38.8 1.6 %collective-permute-start.15 = (bf16[2,128,128]{2,1,0:T(8,128)(2,1)S(1)}, bf16[2,128,128]{2,1,0:T(8,128)(2,1)S(1)}, u32[]{:S(2)}, u32[]{:S(2)}) collective-permute-start(bf16[2,128,128]{2,1,0:T(8,128)(2,1)S(1)} %add_states.2.refs_0_), channel_id=1, source_target_pairs={{0,16},{8,24},{16,0},{24,8},{1,17},{9,25},{17,1},{25,9},{2,18},{10... | collective-permute-start | bytes 196616 | tf_op jit(solution)/shard_map/ppermute | solution.py:421
  40.4 0.9 %collective-permute-start.17 = (bf16[2,128,128]{2,1,0:T(8,128)(2,1)S(1)}, bf16[2,128,128]{2,1,0:T(8,128)(2,1)S(1)}, u32[]{:S(2)}, u32[]{:S(2)}) collective-permute-start(bf16[2,128,128]{2,1,0:T(8,128)(2,1)S(1)} %add_states.3), channel_id=1, source_target_pairs={{0,16},{8,24},{16,0},{24,8},{1,17},{9,25},{17,1},{25,9},{2,18},{10... | collective-permute-start | bytes 196616 | tf_op jit(solution)/shard_map/ppermute | solution.py:421
  41.3 2.3 %queries_within.1 = (bf16[256,512]{1,0:T(8,128)(2,1)S(1)}, f32[256,512]{1,0:T(8,128)S(1)}) custom-call(bf16[256,3072]{1,0:T(8,128)(2,1)S(1)} %get-tuple-element.43.first_ref, bf16[256,3072]{1,0:T(8,128)(2,1)S(1)} %get-tuple-element.49.second_ref, bf16[3,6144,512]{2,1,0:T(8,128)(2,1)S(1)} %bitcast.2, bf16[256,512]{1,0:T(8,128)(2,1)S(1)} %get-tuple-element.50.k_ref, ...), custom_call_target="tpu_custom_call" | custom-call | flops 1744830464 | bytes 6291456 | tf_op jit(solution)/shard_map/queries_within/pallas_call | solution.py:249
  43.6 1.1 %collective-permute-done.17.refs_3_ = bf16[2,128,128]{2,1,0:T(8,128)(2,1)S(1)} collective-permute-done((bf16[2,128,128]{2,1,0:T(8,128)(2,1)S(1)}, bf16[2,128,128]{2,1,0:T(8,128)(2,1)S(1)}, u32[]{:S(2)}, u32[]{:S(2)}) %collective-permute-start.17) | collective-permute-done | bytes 65568 | tf_op jit(solution)/shard_map/ppermute | solution.py:421
  44.8 1.5 %attend_and_project.1 = (bf16[256,512]{1,0:T(8,128)(2,1)S(1)}, bf16[32,3072]{1,0:T(8,128)(2,1)S(1)}, bf16[32,3072]{1,0:T(8,128)(2,1)S(1)}) custom-call(bf16[256,512]{1,0:T(8,128)(2,1)S(1)} %get-tuple-element.52.q_ref, f32[256,512]{1,0:T(8,128)S(1)} %get-tuple-element.53.within_ref, f32[4,128,128]{2,1,0:T(8,128)S(1)} %copy-done, f32[1,512]{1,0:T(1,128)S(1)} %bitcast.5, ...), custom_call_target="tpu_custom_call" | custom-call | flops 1610612736 | bytes 6291456 | tf_op jit(solution)/shard_map/attend_and_project/pallas_call | solution.py:297
  46.3 1.2 %collective-permute-start.28 = (bf16[32,3072]{1,0:T(8,128)(2,1)S(1)}, bf16[32,3072]{1,0:T(8,128)(2,1)S(1)}, u32[]{:S(2)}, u32[]{:S(2)}) collective-permute-start(bf16[32,3072]{1,0:T(8,128)(2,1)S(1)} %get-tuple-element.72), channel_id=1, source_target_pairs={{2,0},{4,2},{6,4},{7,6},{5,7},{3,5},{1,3},{0,1},{10,8},{12,10},{14... | collective-permute-start | bytes 589832 | tf_op jit(solution)/shard_map/ppermute | solution.py:385
  47.5 0.9 %collective-permute-start.24 = (bf16[32,3072]{1,0:T(8,128)(2,1)S(1)}, bf16[32,3072]{1,0:T(8,128)(2,1)S(1)}, u32[]{:S(2)}, u32[]{:S(2)}) collective-permute-start(bf16[32,3072]{1,0:T(8,128)(2,1)S(1)} %get-tuple-element.68), channel_id=1, source_target_pairs={{0,2},{2,4},{4,6},{6,7},{7,5},{5,3},{3,1},{1,0},{8,10},{10,12},{12... | collective-permute-start | bytes 589832 | tf_op jit(solution)/shard_map/ppermute | solution.py:385
  48.4 1.6 %project_rest.1 = (bf16[32,3072]{1,0:T(8,128)(2,1)S(1)}, bf16[32,3072]{1,0:T(8,128)(2,1)S(1)}, bf16[32,3072]{1,0:T(8,128)(2,1)S(1)}, bf16[32,3072]{1,0:T(8,128)(...) custom-call(bf16[256,512]{1,0:T(8,128)(2,1)S(1)} %get-tuple-element., ...), custom_call_target="tpu_custom_call" | custom-call | flops 5000000000 | bytes 6291456 | tf_op jit(solution)/shard_map/project_rest/pallas_call | solution.py:316
  50.0 1.6 %collective-permute-start.21 = (bf16[32,3072]{1,0:T(8,128)(2,1)S(1)}, bf16[32,3072]{1,0:T(8,128)(2,1)S(1)}, u32[]{:S(2)}, u32[]{:S(2)}) collective-permute-start(bf16[32,3072]{1,0:T(8,128)(2,1)S(1)} %get-tuple-element.64), channel_id=1, source_target_pairs={{0,2},{2,4},{4,6},{6,7},{7,5},{5,3},{3,1},{1,0},{8,10},{10,12},{12... | collective-permute-start | bytes 589832 | tf_op jit(solution)/shard_map/ppermute | solution.py:385
  52.1 0.5 collective-permute-done.28.got_ref
  52.7 1.6 %collective-permute-start.29 = (bf16[32,3072]{1,0:T(8,128)(2,1)S(1)}, bf16[32,3072]{1,0:T(8,128)(2,1)S(1)}, u32[]{:S(2)}, u32[]{:S(2)}) collective-permute-start(bf16[32,3072]{1,0:T(8,128)(2,1)S(1)} %add_step.17), channel_id=1, source_target_pairs={{2,0},{4,2},{6,4},{7,6},{5,7},{3,5},{1,3},{0,1},{10,8},{12,10},{14... | collective-permute-start | bytes 589832 | tf_op jit(solution)/shard_map/ppermute | solution.py:385
  54.3 1.1 %collective-permute-done.24.got_ref = bf16[32,3072]{1,0:T(8,128)(2,1)S(1)} collective-permute-done((bf16[32,3072]{1,0:T(8,128)(2,1)S(1)}, bf16[32,3072]{1,0:T(8,128)(2,1)S(1)}, u32[]{:S(2)}, u32[]{:S(2)}) %collective-permute-start.24) | collective-permute-done | bytes 196640 | tf_op jit(solution)/shard_map/ppermute | solution.py:385
  55.7 3.9 %collective-permute-done.21.got_ref = bf16[32,3072]{1,0:T(8,128)(2,1)S(1)} collective-permute-done((bf16[32,3072]{1,0:T(8,128)(2,1)S(1)}, bf16[32,3072]{1,0:T(8,128)(2,1)S(1)}, u32[]{:S(2)}, u32[]{:S(2)}) %collective-permute-start.21) | collective-permute-done | bytes 196640 | tf_op jit(solution)/shard_map/ppermute | solution.py:385
  59.9 1.9 %collective-permute-start.19 = (bf16[32,3072]{1,0:T(8,128)(2,1)S(1)}, bf16[32,3072]{1,0:T(8,128)(2,1)S(1)}, u32[]{:S(2)}, u32[]{:S(2)}) collective-permute-start(bf16[32,3072]{1,0:T(8,128)(2,1)S(1)} %add_step.10), channel_id=1, source_target_pairs={{2,0},{4,2},{6,4},{7,6},{5,7},{3,5},{1,3},{0,1},{10,8},{12,10},{14... | collective-permute-start | bytes 589832 | tf_op jit(solution)/shard_map/ppermute | solution.py:385
  61.8 0.7 collective-permute-done.29.got_ref
  62.5 1.4 %collective-permute-start.30 = (bf16[32,3072]{1,0:T(8,128)(2,1)S(1)}, bf16[32,3072]{1,0:T(8,128)(2,1)S(1)}, u32[]{:S(2)}, u32[]{:S(2)}) collective-permute-start(bf16[32,3072]{1,0:T(8,128)(2,1)S(1)} %add_step.18), channel_id=1, source_target_pairs={{2,0},{4,2},{6,4},{7,6},{5,7},{3,5},{1,3},{0,1},{10,8},{12,10},{14... | collective-permute-start | bytes 589832 | tf_op jit(solution)/shard_map/ppermute | solution.py:385
  64.0 0.7 collective-permute-start.26
  64.7 3.3 %collective-permute-done.22.got_ref = bf16[32,3072]{1,0:T(8,128)(2,1)S(1)} collective-permute-done((bf16[32,3072]{1,0:T(8,128)(2,1)S(1)}, bf16[32,3072]{1,0:T(8,128)(2,1)S(1)}, u32[]{:S(2)}, u32[]{:S(2)}) %collective-permute-start.22) | collective-permute-done | bytes 196640 | tf_op jit(solution)/shard_map/ppermute | solution.py:385
  68.3 1.9 %collective-permute-start.20 = (bf16[32,3072]{1,0:T(8,128)(2,1)S(1)}, bf16[32,3072]{1,0:T(8,128)(2,1)S(1)}, u32[]{:S(2)}, u32[]{:S(2)}) collective-permute-start(bf16[32,3072]{1,0:T(8,128)(2,1)S(1)} %add_step.11), channel_id=1, source_target_pairs={{2,0},{4,2},{6,4},{7,6},{5,7},{3,5},{1,3},{0,1},{10,8},{12,10},{14... | collective-permute-start | bytes 589832 | tf_op jit(solution)/shard_map/ppermute | solution.py:385
  70.2 0.7 collective-permute-done.30.got_ref
  71.0 1.4 %collective-permute-start.31 = (bf16[32,3072]{1,0:T(8,128)(2,1)S(1)}, bf16[32,3072]{1,0:T(8,128)(2,1)S(1)}, u32[]{:S(2)}, u32[]{:S(2)}) collective-permute-start(bf16[32,3072]{1,0:T(8,128)(2,1)S(1)} %add_step.19), channel_id=1, source_target_pairs={{2,0},{4,2},{6,4},{7,6},{5,7},{3,5},{1,3},{0,1},{10,8},{12,10},{14... | collective-permute-start | bytes 589832 | tf_op jit(solution)/shard_map/ppermute | solution.py:385
  72.4 0.7 collective-permute-start.27
  73.2 3.3 %collective-permute-done.23.got_second = bf16[32,3072]{1,0:T(8,128)(2,1)S(1)} collective-permute-done((bf16[32,3072]{1,0:T(8,128)(2,1)S(1)}, bf16[32,3072]{1,0:T(8,128)(2,1)S(1)}, u32[]{:S(2)}, u32[]{:S(2)}) %collective-permute-start.23) | collective-permute-done | bytes 196640 | tf_op jit(solution)/shard_map/ppermute | solution.py:385
  76.5 1.6 %collective-permute-done.31.second = bf16[32,3072]{1,0:T(8,128)(2,1)S(1)} collective-permute-done((bf16[32,3072]{1,0:T(8,128)(2,1)S(1)}, bf16[32,3072]{1,0:T(8,128)(2,1)S(1)}, u32[]{:S(2)}, u32[]{:S(2)}) %collective-permute-start.31) | collective-permute-done | bytes 196640 | tf_op jit(solution)/shard_map/ppermute | solution.py:385
  78.1 0.6 collective-permute-done.27.first
  78.8 0.8 %finish.1 = bf16[32,6144]{1,0:T(8,128)(2,1)} custom-call(f32[2,32,3072]{2,1,0:T(8,128)S(1)} %add_own.1.gathered_ref, bf16[32,3072]{1,0:T(8,128)(2,1)S(1)} %collective-permute-done.27.first, bf16[32,3072]{1,0:T(8,128)(2,1)S(1)} %collective-permute-done.31.second), custom_call_target="tpu_custom_call" | custom-call | bytes 393216 | tf_op jit(solution)/shard_map/finish/pallas_call | solution.py:367
  (62 shorter events, 2.1 us)
Async XLA Ops:
  1.1 8.7 %collective-permute-start = (bf16[32,3072]{1,0:T(8,128)(2,1)S(1)}, bf16[32,3072]{1,0:T(8,128)(2,1)S(1)}, u32[]{:S(2)}, u32[]{:S(2)}) collective-permute-start(bf16[32,3072]{1,0:T(8,128)(2,1)S(1)} %get-tuple-element.74.refs_0_), channel_id=1, source_target_pairs={{0,2},{2,4},{4,6},{6,7},{7,5},{5,3},{3,1},{1,0},{8,10},{10,12},{12... | collective-permute-start | bytes 589832 | tf_op jit(solution)/shard_map/ppermute | solution.py:73
  4.1 7.8 %collective-permute-start.10 = (bf16[32,3072]{1,0:T(8,128)(2,1)S(1)}, bf16[32,3072]{1,0:T(8,128)(2,1)S(1)}, u32[]{:S(2)}, u32[]{:S(2)}) collective-permute-start(bf16[32,3072]{1,0:T(8,128)(2,1)S(1)} %get-tuple-element.73.refs_5_), channel_id=1, source_target_pairs={{2,0},{4,2},{6,4},{7,6},{5,7},{3,5},{1,3},{0,1},{10,8},{12,10},{14... | collective-permute-start | bytes 589832 | tf_op jit(solution)/shard_map/ppermute | solution.py:74
  4.1 12.0 %collective-permute-start.4 = (bf16[32,3072]{1,0:T(8,128)(2,1)S(1)}, bf16[32,3072]{1,0:T(8,128)(2,1)S(1)}, u32[]{:S(2)}, u32[]{:S(2)}) collective-permute-start(bf16[32,3072]{1,0:T(8,128)(2,1)S(1)} %get-tuple-element.74.refs_0_), channel_id=1, source_target_pairs={{2,0},{4,2},{6,4},{7,6},{5,7},{3,5},{1,3},{0,1},{10,8},{12,10},{14... | collective-permute-start | bytes 589832 | tf_op jit(solution)/shard_map/ppermute | solution.py:74
  6.1 10.1 %collective-permute-start.7 = (bf16[32,3072]{1,0:T(8,128)(2,1)S(1)}, bf16[32,3072]{1,0:T(8,128)(2,1)S(1)}, u32[]{:S(2)}, u32[]{:S(2)}) collective-permute-start(bf16[32,3072]{1,0:T(8,128)(2,1)S(1)} %get-tuple-element.73.refs_5_), channel_id=1, source_target_pairs={{0,2},{2,4},{4,6},{6,7},{7,5},{5,3},{3,1},{1,0},{8,10},{10,12},{12... | collective-permute-start | bytes 589832 | tf_op jit(solution)/shard_map/ppermute | solution.py:73
  9.8 10.6 %collective-permute-start.1 = (bf16[32,3072]{1,0:T(8,128)(2,1)S(1)}, bf16[32,3072]{1,0:T(8,128)(2,1)S(1)}, u32[]{:S(2)}, u32[]{:S(2)}) collective-permute-start(bf16[32,3072]{1,0:T(8,128)(2,1)S(1)} %collective-permute-done.refs_1_.arrived_ref), channel_id=1, source_target_pairs={{0,2},{2,4},{4,6},{6,7},{7,5},{5,3},{3,1},{1,0},{8,10},{10,12},{12... | collective-permute-start | bytes 589832 | tf_op jit(solution)/shard_map/ppermute | solution.py:73
  12.0 8.4 %collective-permute-start.11 = (bf16[32,3072]{1,0:T(8,128)(2,1)S(1)}, bf16[32,3072]{1,0:T(8,128)(2,1)S(1)}, u32[]{:S(2)}, u32[]{:S(2)}) collective-permute-start(bf16[32,3072]{1,0:T(8,128)(2,1)S(1)} %collective-permute-done.10.refs_7_.arrived_ref), channel_id=1, source_target_pairs={{2,0},{4,2},{6,4},{7,6},{5,7},{3,5},{1,3},{0,1},{10,8},{12,10},{14... | collective-permute-start | bytes 589832 | tf_op jit(solution)/shard_map/ppermute | solution.py:74
  16.2 8.4 %collective-permute-start.5 = (bf16[32,3072]{1,0:T(8,128)(2,1)S(1)}, bf16[32,3072]{1,0:T(8,128)(2,1)S(1)}, u32[]{:S(2)}, u32[]{:S(2)}) collective-permute-start(bf16[32,3072]{1,0:T(8,128)(2,1)S(1)} %collective-permute-done.4.refs_2_), channel_id=1, source_target_pairs={{2,0},{4,2},{6,4},{7,6},{5,7},{3,5},{1,3},{0,1},{10,8},{12,10},{14... | collective-permute-start | bytes 589832 | tf_op jit(solution)/shard_map/ppermute | solution.py:74
  16.2 8.4 %collective-permute-start.8 = (bf16[32,3072]{1,0:T(8,128)(2,1)S(1)}, bf16[32,3072]{1,0:T(8,128)(2,1)S(1)}, u32[]{:S(2)}, u32[]{:S(2)}) collective-permute-start(bf16[32,3072]{1,0:T(8,128)(2,1)S(1)} %collective-permute-done.7.refs_6_), channel_id=1, source_target_pairs={{0,2},{2,4},{4,6},{6,7},{7,5},{5,3},{3,1},{1,0},{8,10},{10,12},{12... | collective-permute-start | bytes 589832 | tf_op jit(solution)/shard_map/ppermute | solution.py:73
  18.2 8.4 %slice-start = ((s8[18874368]{0:T(1024)(128)(4,1)}), s8[4194304]{0:T(1024)(128)(4,1)S(1)}, s32[]{:S(2)}) async-start(s8[18874368]{0:T(1024)(128)(4,1)} %bitcast.1), calls=%async_computation | async-start | bytes 8388608
  18.2 8.4 %slice-start.1 = ((s8[18874368]{0:T(1024)(128)(4,1)}), s8[4194304]{0:T(1024)(128)(4,1)S(1)}, s32[]{:S(2)}) async-start(s8[18874368]{0:T(1024)(128)(4,1)} %bitcast.1), calls=%async_computation.1 | async-start | bytes 8388608
  18.2 8.4 %slice-start.2 = ((s8[18874368]{0:T(1024)(128)(4,1)}), s8[4194304]{0:T(1024)(128)(4,1)S(1)}, s32[]{:S(2)}) async-start(s8[18874368]{0:T(1024)(128)(4,1)} %bitcast.1), calls=%async_computation.2 | async-start | bytes 8388608
  18.2 8.4 %slice-start.3 = ((s8[18874368]{0:T(1024)(128)(4,1)}), s8[4194304]{0:T(1024)(128)(4,1)S(1)}, s32[]{:S(2)}) async-start(s8[18874368]{0:T(1024)(128)(4,1)} %bitcast.1), calls=%async_computation.3 | async-start | bytes 8388608
  18.2 8.4 %slice-start.4 = ((s8[18874368]{0:T(1024)(128)(4,1)}), s8[2097152]{0:T(1024)(128)(4,1)S(1)}, s32[]{:S(2)}) async-start(s8[18874368]{0:T(1024)(128)(4,1)} %bitcast.1), calls=%async_computation.4 | async-start | bytes 4194304
  20.4 10.3 %collective-permute-start.12 = (bf16[32,3072]{1,0:T(8,128)(2,1)S(1)}, bf16[32,3072]{1,0:T(8,128)(2,1)S(1)}, u32[]{:S(2)}, u32[]{:S(2)}) collective-permute-start(bf16[32,3072]{1,0:T(8,128)(2,1)S(1)} %collective-permute-done.11.refs_9_), channel_id=1, source_target_pairs={{2,0},{4,2},{6,4},{7,6},{5,7},{3,5},{1,3},{0,1},{10,8},{12,10},{14... | collective-permute-start | bytes 589832 | tf_op jit(solution)/shard_map/ppermute | solution.py:74
  20.4 8.7 %collective-permute-start.2 = (bf16[32,3072]{1,0:T(8,128)(2,1)S(1)}, bf16[32,3072]{1,0:T(8,128)(2,1)S(1)}, u32[]{:S(2)}, u32[]{:S(2)}) collective-permute-start(bf16[32,3072]{1,0:T(8,128)(2,1)S(1)} %collective-permute-done.1.refs_3_), channel_id=1, source_target_pairs={{0,2},{2,4},{4,6},{6,7},{7,5},{5,3},{3,1},{1,0},{8,10},{10,12},{12... | collective-permute-start | bytes 589832 | tf_op jit(solution)/shard_map/ppermute | solution.py:73
  24.6 8.4 %collective-permute-start.6 = (bf16[32,3072]{1,0:T(8,128)(2,1)S(1)}, bf16[32,3072]{1,0:T(8,128)(2,1)S(1)}, u32[]{:S(2)}, u32[]{:S(2)}) collective-permute-start(bf16[32,3072]{1,0:T(8,128)(2,1)S(1)} %collective-permute-done.5.refs_4_), channel_id=1, source_target_pairs={{2,0},{4,2},{6,4},{7,6},{5,7},{3,5},{1,3},{0,1},{10,8},{12,10},{14... | collective-permute-start | bytes 589832 | tf_op jit(solution)/shard_map/ppermute | solution.py:74
  24.6 8.4 %collective-permute-start.9 = (bf16[32,3072]{1,0:T(8,128)(2,1)S(1)}, bf16[32,3072]{1,0:T(8,128)(2,1)S(1)}, u32[]{:S(2)}, u32[]{:S(2)}) collective-permute-start(bf16[32,3072]{1,0:T(8,128)(2,1)S(1)} %collective-permute-done.8.refs_8_), channel_id=1, source_target_pairs={{0,2},{2,4},{4,6},{6,7},{7,5},{5,3},{3,1},{1,0},{8,10},{10,12},{12... | collective-permute-start | bytes 589832 | tf_op jit(solution)/shard_map/ppermute | solution.py:73
  29.1 5.7 %collective-permute-start.3 = (bf16[32,3072]{1,0:T(8,128)(2,1)S(1)}, bf16[32,3072]{1,0:T(8,128)(2,1)S(1)}, u32[]{:S(2)}, u32[]{:S(2)}) collective-permute-start(bf16[32,3072]{1,0:T(8,128)(2,1)S(1)} %collective-permute-done.2.refs_0_), channel_id=1, source_target_pairs={{0,2},{2,4},{4,6},{6,7},{7,5},{5,3},{3,1},{1,0},{8,10},{10,12},{12... | collective-permute-start | bytes 589832 | tf_op jit(solution)/shard_map/ppermute | solution.py:77
  30.7 5.7 %collective-permute-start.13 = (bf16[32,3072]{1,0:T(8,128)(2,1)S(1)}, bf16[32,3072]{1,0:T(8,128)(2,1)S(1)}, u32[]{:S(2)}, u32[]{:S(2)}) collective-permute-start(bf16[32,3072]{1,0:T(8,128)(2,1)S(1)} %collective-permute-done.12.refs_3_), channel_id=1, source_target_pairs={{2,0},{4,2},{6,4},{7,6},{5,7},{3,5},{1,3},{0,1},{10,8},{12,10},{14... | collective-permute-start | bytes 589832 | tf_op jit(solution)/shard_map/ppermute | solution.py:78
  37.3 1.5 %collective-permute-start.14 = (bf16[2,128,128]{2,1,0:T(8,128)(2,1)S(1)}, bf16[2,128,128]{2,1,0:T(8,128)(2,1)S(1)}, u32[]{:S(2)}, u32[]{:S(2)}) collective-permute-start(bf16[2,128,128]{2,1,0:T(8,128)(2,1)S(1)} %get-tuple-element.54.one_ref), channel_id=1, source_target_pairs={{0,8},{8,0},{16,24},{24,16},{1,9},{9,1},{17,25},{25,17},{2,10},{10... | collective-permute-start | bytes 196616 | tf_op jit(solution)/shard_map/ppermute | solution.py:421
  38.2 2.2 %collective-permute-start.16 = (bf16[2,128,128]{2,1,0:T(8,128)(2,1)S(1)}, bf16[2,128,128]{2,1,0:T(8,128)(2,1)S(1)}, u32[]{:S(2)}, u32[]{:S(2)}) collective-permute-start(bf16[2,128,128]{2,1,0:T(8,128)(2,1)S(1)} %get-tuple-element.55.one_ref), channel_id=1, source_target_pairs={{0,8},{8,0},{16,24},{24,16},{1,9},{9,1},{17,25},{25,17},{2,10},{10... | collective-permute-start | bytes 196616 | tf_op jit(solution)/shard_map/ppermute | solution.py:421
  38.8 5.9 %collective-permute-start.15 = (bf16[2,128,128]{2,1,0:T(8,128)(2,1)S(1)}, bf16[2,128,128]{2,1,0:T(8,128)(2,1)S(1)}, u32[]{:S(2)}, u32[]{:S(2)}) collective-permute-start(bf16[2,128,128]{2,1,0:T(8,128)(2,1)S(1)} %add_states.2.refs_0_), channel_id=1, source_target_pairs={{0,16},{8,24},{16,0},{24,8},{1,17},{9,25},{17,1},{25,9},{2,18},{10... | collective-permute-start | bytes 196616 | tf_op jit(solution)/shard_map/ppermute | solution.py:421
  40.4 4.3 %collective-permute-start.17 = (bf16[2,128,128]{2,1,0:T(8,128)(2,1)S(1)}, bf16[2,128,128]{2,1,0:T(8,128)(2,1)S(1)}, u32[]{:S(2)}, u32[]{:S(2)}) collective-permute-start(bf16[2,128,128]{2,1,0:T(8,128)(2,1)S(1)} %add_states.3), channel_id=1, source_target_pairs={{0,16},{8,24},{16,0},{24,8},{1,17},{9,25},{17,1},{25,9},{2,18},{10... | collective-permute-start | bytes 196616 | tf_op jit(solution)/shard_map/ppermute | solution.py:421
  41.3 3.5 %slice-start.5 = ((s8[6291456]{0:T(1024)(128)(4,1)}), s8[4194304]{0:T(1024)(128)(4,1)S(1)}, s32[]{:S(2)}) async-start(s8[6291456]{0:T(1024)(128)(4,1)} %bitcast.3), calls=%async_computation.5 | async-start | bytes 8388608
  41.3 3.5 %slice-start.6 = ((s8[6291456]{0:T(1024)(128)(4,1)}), s8[2097152]{0:T(1024)(128)(4,1)S(1)}, s32[]{:S(2)}) async-start(s8[6291456]{0:T(1024)(128)(4,1)} %bitcast.3), calls=%async_computation.6 | async-start | bytes 4194304
  41.3 3.5 %copy-start = (f32[4,128,128]{2,1,0:T(8,128)S(1)}, f32[4,128,128]{2,1,0:T(8,128)}, u32[]{:S(2)}) copy-start(f32[4,128,128]{2,1,0:T(8,128)} %initial_ref.1) | copy-start | bytes 786436
  41.3 3.5 %copy-start.1 = (f32[512]{0:T(512)S(1)}, f32[512]{0:T(512)}, u32[]{:S(2)}) copy-start(f32[512]{0:T(512)} %param.8) | copy-start | bytes 6148
  46.3 6.3 %collective-permute-start.28 = (bf16[32,3072]{1,0:T(8,128)(2,1)S(1)}, bf16[32,3072]{1,0:T(8,128)(2,1)S(1)}, u32[]{:S(2)}, u32[]{:S(2)}) collective-permute-start(bf16[32,3072]{1,0:T(8,128)(2,1)S(1)} %get-tuple-element.72), channel_id=1, source_target_pairs={{2,0},{4,2},{6,4},{7,6},{5,7},{3,5},{1,3},{0,1},{10,8},{12,10},{14... | collective-permute-start | bytes 589832 | tf_op jit(solution)/shard_map/ppermute | solution.py:385
  47.5 7.8 %collective-permute-start.24 = (bf16[32,3072]{1,0:T(8,128)(2,1)S(1)}, bf16[32,3072]{1,0:T(8,128)(2,1)S(1)}, u32[]{:S(2)}, u32[]{:S(2)}) collective-permute-start(bf16[32,3072]{1,0:T(8,128)(2,1)S(1)} %get-tuple-element.68), channel_id=1, source_target_pairs={{0,2},{2,4},{4,6},{6,7},{7,5},{5,3},{3,1},{1,0},{8,10},{10,12},{12... | collective-permute-start | bytes 589832 | tf_op jit(solution)/shard_map/ppermute | solution.py:385
  50.0 9.6 %collective-permute-start.21 = (bf16[32,3072]{1,0:T(8,128)(2,1)S(1)}, bf16[32,3072]{1,0:T(8,128)(2,1)S(1)}, u32[]{:S(2)}, u32[]{:S(2)}) collective-permute-start(bf16[32,3072]{1,0:T(8,128)(2,1)S(1)} %get-tuple-element.64), channel_id=1, source_target_pairs={{0,2},{2,4},{4,6},{6,7},{7,5},{5,3},{3,1},{1,0},{8,10},{10,12},{12... | collective-permute-start | bytes 589832 | tf_op jit(solution)/shard_map/ppermute | solution.py:385
  51.7 8.2 %collective-permute-start.18 = (bf16[32,3072]{1,0:T(8,128)(2,1)S(1)}, bf16[32,3072]{1,0:T(8,128)(2,1)S(1)}, u32[]{:S(2)}, u32[]{:S(2)}) collective-permute-start(bf16[32,3072]{1,0:T(8,128)(2,1)S(1)} %get-tuple-element.61), channel_id=1, source_target_pairs={{2,0},{4,2},{6,4},{7,6},{5,7},{3,5},{1,3},{0,1},{10,8},{12,10},{14... | collective-permute-start | bytes 589832 | tf_op jit(solution)/shard_map/ppermute | solution.py:385
  52.7 9.8 %collective-permute-start.29 = (bf16[32,3072]{1,0:T(8,128)(2,1)S(1)}, bf16[32,3072]{1,0:T(8,128)(2,1)S(1)}, u32[]{:S(2)}, u32[]{:S(2)}) collective-permute-start(bf16[32,3072]{1,0:T(8,128)(2,1)S(1)} %add_step.17), channel_id=1, source_target_pairs={{2,0},{4,2},{6,4},{7,6},{5,7},{3,5},{1,3},{0,1},{10,8},{12,10},{14... | collective-permute-start | bytes 589832 | tf_op jit(solution)/shard_map/ppermute | solution.py:385
  55.4 8.5 %collective-permute-start.25 = (bf16[32,3072]{1,0:T(8,128)(2,1)S(1)}, bf16[32,3072]{1,0:T(8,128)(2,1)S(1)}, u32[]{:S(2)}, u32[]{:S(2)}) collective-permute-start(bf16[32,3072]{1,0:T(8,128)(2,1)S(1)} %add_step.14), channel_id=1, source_target_pairs={{0,2},{2,4},{4,6},{6,7},{7,5},{5,3},{3,1},{1,0},{8,10},{10,12},{12... | collective-permute-start | bytes 589832 | tf_op jit(solution)/shard_map/ppermute | solution.py:385
  59.6 8.4 %collective-permute-start.22 = (bf16[32,3072]{1,0:T(8,128)(2,1)S(1)}, bf16[32,3072]{1,0:T(8,128)(2,1)S(1)}, u32[]{:S(2)}, u32[]{:S(2)}) collective-permute-start(bf16[32,3072]{1,0:T(8,128)(2,1)S(1)} %add_step.12), channel_id=1, source_target_pairs={{0,2},{2,4},{4,6},{6,7},{7,5},{5,3},{3,1},{1,0},{8,10},{10,12},{12... | collective-permute-start | bytes 589832 | tf_op jit(solution)/shard_map/ppermute | solution.py:385
  59.9 8.4 %collective-permute-start.19 = (bf16[32,3072]{1,0:T(8,128)(2,1)S(1)}, bf16[32,3072]{1,0:T(8,128)(2,1)S(1)}, u32[]{:S(2)}, u32[]{:S(2)}) collective-permute-start(bf16[32,3072]{1,0:T(8,128)(2,1)S(1)} %add_step.10), channel_id=1, source_target_pairs={{2,0},{4,2},{6,4},{7,6},{5,7},{3,5},{1,3},{0,1},{10,8},{12,10},{14... | collective-permute-start | bytes 589832 | tf_op jit(solution)/shard_map/ppermute | solution.py:385
  62.5 8.4 %collective-permute-start.30 = (bf16[32,3072]{1,0:T(8,128)(2,1)S(1)}, bf16[32,3072]{1,0:T(8,128)(2,1)S(1)}, u32[]{:S(2)}, u32[]{:S(2)}) collective-permute-start(bf16[32,3072]{1,0:T(8,128)(2,1)S(1)} %add_step.18), channel_id=1, source_target_pairs={{2,0},{4,2},{6,4},{7,6},{5,7},{3,5},{1,3},{0,1},{10,8},{12,10},{14... | collective-permute-start | bytes 589832 | tf_op jit(solution)/shard_map/ppermute | solution.py:385
  64.0 8.4 %collective-permute-start.26 = (bf16[32,3072]{1,0:T(8,128)(2,1)S(1)}, bf16[32,3072]{1,0:T(8,128)(2,1)S(1)}, u32[]{:S(2)}, u32[]{:S(2)}) collective-permute-start(bf16[32,3072]{1,0:T(8,128)(2,1)S(1)} %add_step.15), channel_id=1, source_target_pairs={{0,2},{2,4},{4,6},{6,7},{7,5},{5,3},{3,1},{1,0},{8,10},{10,12},{12... | collective-permute-start | bytes 589832 | tf_op jit(solution)/shard_map/ppermute | solution.py:385
  68.1 8.4 %collective-permute-start.23 = (bf16[32,3072]{1,0:T(8,128)(2,1)S(1)}, bf16[32,3072]{1,0:T(8,128)(2,1)S(1)}, u32[]{:S(2)}, u32[]{:S(2)}) collective-permute-start(bf16[32,3072]{1,0:T(8,128)(2,1)S(1)} %add_step.13), channel_id=1, source_target_pairs={{0,2},{2,4},{4,6},{6,7},{7,5},{5,3},{3,1},{1,0},{8,10},{10,12},{12... | collective-permute-start | bytes 589832 | tf_op jit(solution)/shard_map/ppermute | solution.py:385
  68.3 8.1 %collective-permute-start.20 = (bf16[32,3072]{1,0:T(8,128)(2,1)S(1)}, bf16[32,3072]{1,0:T(8,128)(2,1)S(1)}, u32[]{:S(2)}, u32[]{:S(2)}) collective-permute-start(bf16[32,3072]{1,0:T(8,128)(2,1)S(1)} %add_step.11), channel_id=1, source_target_pairs={{2,0},{4,2},{6,4},{7,6},{5,7},{3,5},{1,3},{0,1},{10,8},{12,10},{14... | collective-permute-start | bytes 589832 | tf_op jit(solution)/shard_map/ppermute | solution.py:385
  71.0 7.2 %collective-permute-start.31 = (bf16[32,3072]{1,0:T(8,128)(2,1)S(1)}, bf16[32,3072]{1,0:T(8,128)(2,1)S(1)}, u32[]{:S(2)}, u32[]{:S(2)}) collective-permute-start(bf16[32,3072]{1,0:T(8,128)(2,1)S(1)} %add_step.19), channel_id=1, source_target_pairs={{2,0},{4,2},{6,4},{7,6},{5,7},{3,5},{1,3},{0,1},{10,8},{12,10},{14... | collective-permute-start | bytes 589832 | tf_op jit(solution)/shard_map/ppermute | solution.py:385
  72.4 6.4 %collective-permute-start.27 = (bf16[32,3072]{1,0:T(8,128)(2,1)S(1)}, bf16[32,3072]{1,0:T(8,128)(2,1)S(1)}, u32[]{:S(2)}, u32[]{:S(2)}) collective-permute-start(bf16[32,3072]{1,0:T(8,128)(2,1)S(1)} %add_step.16), channel_id=1, source_target_pairs={{0,2},{2,4},{4,6},{6,7},{7,5},{5,3},{3,1},{1,0},{8,10},{10,12},{12... | collective-permute-start | bytes 589832 | tf_op jit(solution)/shard_map/ppermute | solution.py:385

commit v14 on v13

--- a/solution.py
+++ b/solution.py
@@ -462,7 +462,8 @@
     )
     parts = project_rest(normalized, out_weight, n_fsdp - soon, rows) + parts
 
-    return ring_scatter(parts, order, right, left)
+    mirrored = [distance if distance == n_fsdp // 2 else -distance for distance in order]
+    return ring_scatter(parts, mirrored, left, right)
 
 
 def solution(mesh):

time: 79.7 us -> 80.1 us (level)
    ppermute x7, starting transfers between devices: 9.87 us -> 12.1 us  [hop(): lax.ppermute(to_left, 'fsdp', left)]
    ppermute x7, starting transfers between devices: 4.63 us -> 3.19 us  [hop(): lax.ppermute(to_right, 'fsdp', right)]
    ppermute x7, waiting for transfers between devices: 3.45 us -> 2.02 us  [hop(): lax.ppermute(to_left, 'fsdp', left)]
    ppermute x7, waiting for transfers between devices: 12.2 us -> 13.3 us  [hop(): lax.ppermute(to_right, 'fsdp', right)]
where the time goes in v14:
time: 80.1 us; the launch traced here: 80 us
  starting transfers between devices  33.8 us (42%)
  waiting for transfers between devices  32.7 us (41%)
  Pallas kernels  12.2 us (15%)
  local copies, waits for them, and re-layouts  1.09 us (1%)
    ppermute x7, waiting for transfers between devices, hop(): lax.ppermute(to_right, 'fsdp', right)  13.3 us
    ppermute x7, starting transfers between devices, hop(): lax.ppermute(to_left, 'fsdp', left)  12.1 us
    ppermute x6, starting transfers between devices, ring_gather(): going_right[part] = lax.ppermute(going_right[part], 'fsdp', right)  11.4 us
    ppermute x6, waiting for transfers between devices, ring_gather(): going_left[1 - part] = lax.ppermute(going_left[1 - part], 'fsdp', left)  10.4 us
    ppermute x6, waiting for transfers between devices, ring_gather(): going_right[part] = lax.ppermute(going_right[part], 'fsdp', right)  3.6 us
    ppermute x7, starting transfers between devices, hop(): lax.ppermute(to_right, 'fsdp', right)  3.19 us
    ppermute x4, starting transfers between devices, exchange_states(): received[at].append(lax.ppermute(total, 'ctx', pairs))  3.09 us
    pallas_call x1, Pallas kernels, queries_within(): call(body, (jax.ShapeDtypeStruct((n_rows, columns), BF16), jax.ShapeDtype...  2.3 us
  transfers between devices with their start and end apart: 32, of which 17 were waited for; matrix products, arithmetic and copies ran while one was open for 0% of the time, Pallas kernels for 11%

profile of v14, /device:TPU:0, one launch (start us, length us, event | category | flops | bytes accessed | tf_op | source)
XLA Modules:
  0.0 80.0 jit_solution(14063438573800575235)
XLA Ops:
  0.0 1.0 %fusion = (bf16[32,3072]{1,0:T(8,128)(2,1)S(1)}, bf16[32,3072]{1,0:T(8,128)(2,1)S(1)}) fusion(bf16[32,6144]{1,0:T(8,128)(2,1)} %param.5), kind=kLoop, calls=%fused_computation | loop fusion | bytes 786432 | tf_op jit(solution)/shard_map/slice | solution.py:68
  1.1 3.1 %collective-permute-start = (bf16[32,3072]{1,0:T(8,128)(2,1)S(1)}, bf16[32,3072]{1,0:T(8,128)(2,1)S(1)}, u32[]{:S(2)}, u32[]{:S(2)}) collective-permute-start(bf16[32,3072]{1,0:T(8,128)(2,1)S(1)} %get-tuple-element.74.refs_0_), channel_id=1, source_target_pairs={{0,2},{2,4},{4,6},{6,7},{7,5},{5,3},{3,1},{1,0},{8,10},{10,12},{12... | collective-permute-start | bytes 589832 | tf_op jit(solution)/shard_map/ppermute | solution.py:73
  4.1 1.9 %collective-permute-start.4 = (bf16[32,3072]{1,0:T(8,128)(2,1)S(1)}, bf16[32,3072]{1,0:T(8,128)(2,1)S(1)}, u32[]{:S(2)}, u32[]{:S(2)}) collective-permute-start(bf16[32,3072]{1,0:T(8,128)(2,1)S(1)} %get-tuple-element.74.refs_0_), channel_id=1, source_target_pairs={{2,0},{4,2},{6,4},{7,6},{5,7},{3,5},{1,3},{0,1},{10,8},{12,10},{14... | collective-permute-start | bytes 589832 | tf_op jit(solution)/shard_map/ppermute | solution.py:74
  6.2 3.6 %collective-permute-done.refs_1_.arrived_ref = bf16[32,3072]{1,0:T(8,128)(2,1)S(1)} collective-permute-done((bf16[32,3072]{1,0:T(8,128)(2,1)S(1)}, bf16[32,3072]{1,0:T(8,128)(2,1)S(1)}, u32[]{:S(2)}, u32[]{:S(2)}) %collective-permute-start) | collective-permute-done | bytes 196640 | tf_op jit(solution)/shard_map/ppermute | solution.py:73
  9.8 2.1 %collective-permute-start.1 = (bf16[32,3072]{1,0:T(8,128)(2,1)S(1)}, bf16[32,3072]{1,0:T(8,128)(2,1)S(1)}, u32[]{:S(2)}, u32[]{:S(2)}) collective-permute-start(bf16[32,3072]{1,0:T(8,128)(2,1)S(1)} %collective-permute-done.refs_1_.arrived_ref), channel_id=1, source_target_pairs={{0,2},{2,4},{4,6},{6,7},{7,5},{5,3},{3,1},{1,0},{8,10},{10,12},{12... | collective-permute-start | bytes 589832 | tf_op jit(solution)/shard_map/ppermute | solution.py:73
  12.0 4.2 %collective-permute-done.4.refs_2_ = bf16[32,3072]{1,0:T(8,128)(2,1)S(1)} collective-permute-done((bf16[32,3072]{1,0:T(8,128)(2,1)S(1)}, bf16[32,3072]{1,0:T(8,128)(2,1)S(1)}, u32[]{:S(2)}, u32[]{:S(2)}) %collective-permute-start.4) | collective-permute-done | bytes 196640 | tf_op jit(solution)/shard_map/ppermute | solution.py:74
  16.2 2.0 %collective-permute-start.8 = (bf16[32,3072]{1,0:T(8,128)(2,1)S(1)}, bf16[32,3072]{1,0:T(8,128)(2,1)S(1)}, u32[]{:S(2)}, u32[]{:S(2)}) collective-permute-start(bf16[32,3072]{1,0:T(8,128)(2,1)S(1)} %collective-permute-done.7.refs_6_), channel_id=1, source_target_pairs={{0,2},{2,4},{4,6},{6,7},{7,5},{5,3},{3,1},{1,0},{8,10},{10,12},{12... | collective-permute-start | bytes 589832 | tf_op jit(solution)/shard_map/ppermute | solution.py:73
  18.2 2.1 %collective-permute-done.11.refs_9_ = bf16[32,3072]{1,0:T(8,128)(2,1)S(1)} collective-permute-done((bf16[32,3072]{1,0:T(8,128)(2,1)S(1)}, bf16[32,3072]{1,0:T(8,128)(2,1)S(1)}, u32[]{:S(2)}, u32[]{:S(2)}) %collective-permute-start.11) | collective-permute-done | bytes 196640 | tf_op jit(solution)/shard_map/ppermute | solution.py:74
  20.4 2.0 %collective-permute-start.2 = (bf16[32,3072]{1,0:T(8,128)(2,1)S(1)}, bf16[32,3072]{1,0:T(8,128)(2,1)S(1)}, u32[]{:S(2)}, u32[]{:S(2)}) collective-permute-start(bf16[32,3072]{1,0:T(8,128)(2,1)S(1)} %collective-permute-done.1.refs_3_), channel_id=1, source_target_pairs={{0,2},{2,4},{4,6},{6,7},{7,5},{5,3},{3,1},{1,0},{8,10},{10,12},{12... | collective-permute-start | bytes 589832 | tf_op jit(solution)/shard_map/ppermute | solution.py:73
  22.4 2.2 %collective-permute-done.5.refs_4_ = bf16[32,3072]{1,0:T(8,128)(2,1)S(1)} collective-permute-done((bf16[32,3072]{1,0:T(8,128)(2,1)S(1)}, bf16[32,3072]{1,0:T(8,128)(2,1)S(1)}, u32[]{:S(2)}, u32[]{:S(2)}) %collective-permute-start.5) | collective-permute-done | bytes 196640 | tf_op jit(solution)/shard_map/ppermute | solution.py:74
  24.6 2.0 %collective-permute-start.9 = (bf16[32,3072]{1,0:T(8,128)(2,1)S(1)}, bf16[32,3072]{1,0:T(8,128)(2,1)S(1)}, u32[]{:S(2)}, u32[]{:S(2)}) collective-permute-start(bf16[32,3072]{1,0:T(8,128)(2,1)S(1)} %collective-permute-done.8.refs_8_), channel_id=1, source_target_pairs={{0,2},{2,4},{4,6},{6,7},{7,5},{5,3},{3,1},{1,0},{8,10},{10,12},{12... | collective-permute-start | bytes 589832 | tf_op jit(solution)/shard_map/ppermute | solution.py:73
  26.7 1.2 %early_keys.1 = (bf16[256,512]{1,0:T(8,128)(2,1)S(1)}, bf16[256,3072]{1,0:T(8,128)(2,1)S(1)}, bf16[256,3072]{1,0:T(8,128)(2,1)S(1)}) custom-call(bf16[32,3072]{1,0:T(8,128)(2,1)S(1)} %get-tuple-element.74.refs_0_, bf16[32,3072]{1,0:T(8,128)(2,1)S(1)} %collective-permute-done.refs_1_.arrived_ref, bf16[32,3072]{1,0:T(8,128)(2,1)S(1)} %collective-permute-done.4.refs_2_, ...), custom_call_target="tpu_custom_call" | custom-call | flops 1006632960 | bytes 6291456 | tf_op jit(solution)/shard_map/early_keys/pallas_call | solution.py:106
  27.9 1.2 %early_values.1.refs_6_.refs_5_ = bf16[256,512]{1,0:T(8,128)(2,1)S(1)} custom-call(bf16[256,3072]{1,0:T(8,128)(2,1)S(1)} %get-tuple-element.39.first_ref.refs_4_, bf16[256,3072]{1,0:T(8,128)(2,1)S(1)} %get-tuple-element.40.second_ref.refs_5_, bf16[3,6144,512]{2,1,0:T(8,128)(2,1)S(1)} %bitcast.2), custom_call_target="tpu_custom_call" | custom-call | flops 1006632960 | bytes 6291456 | tf_op jit(solution)/shard_map/early_values/pallas_call | solution.py:126
  29.1 1.6 %collective-permute-start.3 = (bf16[32,3072]{1,0:T(8,128)(2,1)S(1)}, bf16[32,3072]{1,0:T(8,128)(2,1)S(1)}, u32[]{:S(2)}, u32[]{:S(2)}) collective-permute-start(bf16[32,3072]{1,0:T(8,128)(2,1)S(1)} %collective-permute-done.2.refs_0_), channel_id=1, source_target_pairs={{0,2},{2,4},{4,6},{6,7},{7,5},{5,3},{3,1},{1,0},{8,10},{10,12},{12... | collective-permute-start | bytes 589832 | tf_op jit(solution)/shard_map/ppermute | solution.py:77
  30.7 0.4 collective-permute-start.13
  31.2 1.8 %collective-permute-done.6.refs_1_ = bf16[32,3072]{1,0:T(8,128)(2,1)S(1)} collective-permute-done((bf16[32,3072]{1,0:T(8,128)(2,1)S(1)}, bf16[32,3072]{1,0:T(8,128)(2,1)S(1)}, u32[]{:S(2)}, u32[]{:S(2)}) %collective-permute-start.6) | collective-permute-done | bytes 196640 | tf_op jit(solution)/shard_map/ppermute | solution.py:74
  33.1 1.7 %collective-permute-done.3.refs_0_ = bf16[32,3072]{1,0:T(8,128)(2,1)S(1)} collective-permute-done((bf16[32,3072]{1,0:T(8,128)(2,1)S(1)}, bf16[32,3072]{1,0:T(8,128)(2,1)S(1)}, u32[]{:S(2)}, u32[]{:S(2)}) %collective-permute-start.3) | collective-permute-done | bytes 196640 | tf_op jit(solution)/shard_map/ppermute | solution.py:77
  34.8 1.1 %first_pass.1 = (bf16[256,3072]{1,0:T(8,128)(2,1)S(1)}, f32[2,96,512]{2,1,0:T(8,128)S(1)}) custom-call(bf16[32,3072]{1,0:T(8,128)(2,1)S(1)} %collective-permute-done.3.refs_0_, bf16[256,3072]{1,0:T(8,128)(2,1)S(1)} %get-tuple-element.41.refs_1_, bf16[3,6144,512]{2,1,0:T(8,128)(2,1)S(1)} %bitcast.2, ...), custom_call_target="tpu_custom_call", output_to_operand_aliasing={{0}: (1, {})} | custom-call | flops 603979776 | bytes 6291456 | tf_op jit(solution)/shard_map/first_pass/pallas_call | solution.py:166
  35.9 0.5 collective-permute-done.13.refs_0_
  36.4 0.9 %late_keys_and_values.2 = (bf16[256,3072]{1,0:T(8,128)(2,1)S(1)}, bf16[256,512]{1,0:T(8,128)(2,1)S(1)}, bf16[256,512]{1,0:T(8,128)(2,1)S(1)}, bf16[2,128,128]{2,1,0:T(8,128)(2,1)S(1)}) custom-call(bf16[32,3072]{1,0:T(8,128)(2,1)S(1)} %collective-permute-done.13.refs_0_, ...), custom_call_target="tpu_custom_call", output_to_operand_aliasing={{0}: (1, {}), {1}: (4, {}), {2}: (5, {})} | custom-call | flops 301989888 | bytes 3145728 | tf_op jit(solution)/shard_map/late_keys_and_values/pallas_call | solution.py:206
  37.3 0.9 %late_keys_and_values.3 = (bf16[256,3072]{1,0:T(8,128)(2,1)S(1)}, bf16[256,512]{1,0:T(8,128)(2,1)S(1)}, bf16[256,512]{1,0:T(8,128)(2,1)S(1)}, bf16[2,128,128]{2,1,0:T(8,128)(2,1)S(1)}) custom-call(bf16[256,3072]{1,0:T(8,128)(2,1)S(1)} %get-tuple-element.46.refs_0_, ...), custom_call_target="tpu_custom_call", output_to_operand_aliasing={{0}: (0, {}), {1}: (3, {}), {2}: (4, {})} | custom-call | flops 5000000000 | bytes 3145728 | tf_op jit(solution)/shard_map/late_keys_and_values/pallas_call | solution.py:206
  38.2 0.6 collective-permute-start.16
  38.8 1.6 %collective-permute-start.15 = (bf16[2,128,128]{2,1,0:T(8,128)(2,1)S(1)}, bf16[2,128,128]{2,1,0:T(8,128)(2,1)S(1)}, u32[]{:S(2)}, u32[]{:S(2)}) collective-permute-start(bf16[2,128,128]{2,1,0:T(8,128)(2,1)S(1)} %add_states.2.refs_0_), channel_id=1, source_target_pairs={{0,16},{8,24},{16,0},{24,8},{1,17},{9,25},{17,1},{25,9},{2,18},{10... | collective-permute-start | bytes 196616 | tf_op jit(solution)/shard_map/ppermute | solution.py:421
  40.4 0.9 %collective-permute-start.17 = (bf16[2,128,128]{2,1,0:T(8,128)(2,1)S(1)}, bf16[2,128,128]{2,1,0:T(8,128)(2,1)S(1)}, u32[]{:S(2)}, u32[]{:S(2)}) collective-permute-start(bf16[2,128,128]{2,1,0:T(8,128)(2,1)S(1)} %add_states.3), channel_id=1, source_target_pairs={{0,16},{8,24},{16,0},{24,8},{1,17},{9,25},{17,1},{25,9},{2,18},{10... | collective-permute-start | bytes 196616 | tf_op jit(solution)/shard_map/ppermute | solution.py:421
  41.3 2.3 %queries_within.1 = (bf16[256,512]{1,0:T(8,128)(2,1)S(1)}, f32[256,512]{1,0:T(8,128)S(1)}) custom-call(bf16[256,3072]{1,0:T(8,128)(2,1)S(1)} %get-tuple-element.43.first_ref, bf16[256,3072]{1,0:T(8,128)(2,1)S(1)} %get-tuple-element.49.second_ref, bf16[3,6144,512]{2,1,0:T(8,128)(2,1)S(1)} %bitcast.2, bf16[256,512]{1,0:T(8,128)(2,1)S(1)} %get-tuple-element.50.k_ref, ...), custom_call_target="tpu_custom_call" | custom-call | flops 1744830464 | bytes 6291456 | tf_op jit(solution)/shard_map/queries_within/pallas_call | solution.py:249
  43.6 1.1 %collective-permute-done.17.refs_3_ = bf16[2,128,128]{2,1,0:T(8,128)(2,1)S(1)} collective-permute-done((bf16[2,128,128]{2,1,0:T(8,128)(2,1)S(1)}, bf16[2,128,128]{2,1,0:T(8,128)(2,1)S(1)}, u32[]{:S(2)}, u32[]{:S(2)}) %collective-permute-start.17) | collective-permute-done | bytes 65568 | tf_op jit(solution)/shard_map/ppermute | solution.py:421
  44.8 1.5 %attend_and_project.1 = (bf16[256,512]{1,0:T(8,128)(2,1)S(1)}, bf16[32,3072]{1,0:T(8,128)(2,1)S(1)}, bf16[32,3072]{1,0:T(8,128)(2,1)S(1)}) custom-call(bf16[256,512]{1,0:T(8,128)(2,1)S(1)} %get-tuple-element.52.q_ref, f32[256,512]{1,0:T(8,128)S(1)} %get-tuple-element.53.within_ref, f32[4,128,128]{2,1,0:T(8,128)S(1)} %copy-done, f32[1,512]{1,0:T(1,128)S(1)} %bitcast.5, ...), custom_call_target="tpu_custom_call" | custom-call | flops 1610612736 | bytes 6291456 | tf_op jit(solution)/shard_map/attend_and_project/pallas_call | solution.py:297
  46.3 1.6 %collective-permute-start.28 = (bf16[32,3072]{1,0:T(8,128)(2,1)S(1)}, bf16[32,3072]{1,0:T(8,128)(2,1)S(1)}, u32[]{:S(2)}, u32[]{:S(2)}) collective-permute-start(bf16[32,3072]{1,0:T(8,128)(2,1)S(1)} %get-tuple-element.72), channel_id=1, source_target_pairs={{0,2},{2,4},{4,6},{6,7},{7,5},{5,3},{3,1},{1,0},{8,10},{10,12},{12... | collective-permute-start | bytes 589832 | tf_op jit(solution)/shard_map/ppermute | solution.py:385
  47.9 0.4 collective-permute-start.24
  48.4 1.6 %project_rest.1 = (bf16[32,3072]{1,0:T(8,128)(2,1)S(1)}, bf16[32,3072]{1,0:T(8,128)(2,1)S(1)}, bf16[32,3072]{1,0:T(8,128)(2,1)S(1)}, bf16[32,3072]{1,0:T(8,128)(...) custom-call(bf16[256,512]{1,0:T(8,128)(2,1)S(1)} %get-tuple-element., ...), custom_call_target="tpu_custom_call" | custom-call | flops 5000000000 | bytes 6291456 | tf_op jit(solution)/shard_map/project_rest/pallas_call | solution.py:316
  50.0 1.2 %collective-permute-start.21 = (bf16[32,3072]{1,0:T(8,128)(2,1)S(1)}, bf16[32,3072]{1,0:T(8,128)(2,1)S(1)}, u32[]{:S(2)}, u32[]{:S(2)}) collective-permute-start(bf16[32,3072]{1,0:T(8,128)(2,1)S(1)} %get-tuple-element.64), channel_id=1, source_target_pairs={{2,0},{4,2},{6,4},{7,6},{5,7},{3,5},{1,3},{0,1},{10,8},{12,10},{14... | collective-permute-start | bytes 589832 | tf_op jit(solution)/shard_map/ppermute | solution.py:385
  51.3 0.9 %collective-permute-start.18 = (bf16[32,3072]{1,0:T(8,128)(2,1)S(1)}, bf16[32,3072]{1,0:T(8,128)(2,1)S(1)}, u32[]{:S(2)}, u32[]{:S(2)}) collective-permute-start(bf16[32,3072]{1,0:T(8,128)(2,1)S(1)} %get-tuple-element.61), channel_id=1, source_target_pairs={{0,2},{2,4},{4,6},{6,7},{7,5},{5,3},{3,1},{1,0},{8,10},{10,12},{12... | collective-permute-start | bytes 589832 | tf_op jit(solution)/shard_map/ppermute | solution.py:385
  52.1 0.6 collective-permute-done.28.got_ref
  52.8 2.3 %collective-permute-start.29 = (bf16[32,3072]{1,0:T(8,128)(2,1)S(1)}, bf16[32,3072]{1,0:T(8,128)(2,1)S(1)}, u32[]{:S(2)}, u32[]{:S(2)}) collective-permute-start(bf16[32,3072]{1,0:T(8,128)(2,1)S(1)} %add_step.17), channel_id=1, source_target_pairs={{0,2},{2,4},{4,6},{6,7},{7,5},{5,3},{3,1},{1,0},{8,10},{10,12},{12... | collective-permute-start | bytes 589832 | tf_op jit(solution)/shard_map/ppermute | solution.py:385
  55.1 0.7 collective-permute-done.24.got_ref
  55.8 0.3 collective-permute-start.25
  56.1 3.9 %collective-permute-done.21.got_ref = bf16[32,3072]{1,0:T(8,128)(2,1)S(1)} collective-permute-done((bf16[32,3072]{1,0:T(8,128)(2,1)S(1)}, bf16[32,3072]{1,0:T(8,128)(2,1)S(1)}, u32[]{:S(2)}, u32[]{:S(2)}) %collective-permute-start.21) | collective-permute-done | bytes 196640 | tf_op jit(solution)/shard_map/ppermute | solution.py:385
  60.0 0.3 collective-permute-start.22
  60.4 1.8 %collective-permute-start.19 = (bf16[32,3072]{1,0:T(8,128)(2,1)S(1)}, bf16[32,3072]{1,0:T(8,128)(2,1)S(1)}, u32[]{:S(2)}, u32[]{:S(2)}) collective-permute-start(bf16[32,3072]{1,0:T(8,128)(2,1)S(1)} %add_step.10), channel_id=1, source_target_pairs={{0,2},{2,4},{4,6},{6,7},{7,5},{5,3},{3,1},{1,0},{8,10},{10,12},{12... | collective-permute-start | bytes 589832 | tf_op jit(solution)/shard_map/ppermute | solution.py:385
  62.5 1.8 %collective-permute-start.30 = (bf16[32,3072]{1,0:T(8,128)(2,1)S(1)}, bf16[32,3072]{1,0:T(8,128)(2,1)S(1)}, u32[]{:S(2)}, u32[]{:S(2)}) collective-permute-start(bf16[32,3072]{1,0:T(8,128)(2,1)S(1)} %add_step.18), channel_id=1, source_target_pairs={{0,2},{2,4},{4,6},{6,7},{7,5},{5,3},{3,1},{1,0},{8,10},{10,12},{12... | collective-permute-start | bytes 589832 | tf_op jit(solution)/shard_map/ppermute | solution.py:385
  64.3 0.4 collective-permute-start.26
  64.7 3.7 %collective-permute-done.22.got_ref = bf16[32,3072]{1,0:T(8,128)(2,1)S(1)} collective-permute-done((bf16[32,3072]{1,0:T(8,128)(2,1)S(1)}, bf16[32,3072]{1,0:T(8,128)(2,1)S(1)}, u32[]{:S(2)}, u32[]{:S(2)}) %collective-permute-start.22) | collective-permute-done | bytes 196640 | tf_op jit(solution)/shard_map/ppermute | solution.py:385
  68.8 1.8 %collective-permute-start.20 = (bf16[32,3072]{1,0:T(8,128)(2,1)S(1)}, bf16[32,3072]{1,0:T(8,128)(2,1)S(1)}, u32[]{:S(2)}, u32[]{:S(2)}) collective-permute-start(bf16[32,3072]{1,0:T(8,128)(2,1)S(1)} %add_step.11), channel_id=1, source_target_pairs={{0,2},{2,4},{4,6},{6,7},{7,5},{5,3},{3,1},{1,0},{8,10},{10,12},{12... | collective-permute-start | bytes 589832 | tf_op jit(solution)/shard_map/ppermute | solution.py:385
  70.9 1.8 %collective-permute-start.31 = (bf16[32,3072]{1,0:T(8,128)(2,1)S(1)}, bf16[32,3072]{1,0:T(8,128)(2,1)S(1)}, u32[]{:S(2)}, u32[]{:S(2)}) collective-permute-start(bf16[32,3072]{1,0:T(8,128)(2,1)S(1)} %add_step.19), channel_id=1, source_target_pairs={{0,2},{2,4},{4,6},{6,7},{7,5},{5,3},{3,1},{1,0},{8,10},{10,12},{12... | collective-permute-start | bytes 589832 | tf_op jit(solution)/shard_map/ppermute | solution.py:385
  73.1 3.7 %collective-permute-done.23.got_second = bf16[32,3072]{1,0:T(8,128)(2,1)S(1)} collective-permute-done((bf16[32,3072]{1,0:T(8,128)(2,1)S(1)}, bf16[32,3072]{1,0:T(8,128)(2,1)S(1)}, u32[]{:S(2)}, u32[]{:S(2)}) %collective-permute-start.23) | collective-permute-done | bytes 196640 | tf_op jit(solution)/shard_map/ppermute | solution.py:385
  76.9 1.0 %collective-permute-done.31.second = bf16[32,3072]{1,0:T(8,128)(2,1)S(1)} collective-permute-done((bf16[32,3072]{1,0:T(8,128)(2,1)S(1)}, bf16[32,3072]{1,0:T(8,128)(2,1)S(1)}, u32[]{:S(2)}, u32[]{:S(2)}) %collective-permute-start.31) | collective-permute-done | bytes 196640 | tf_op jit(solution)/shard_map/ppermute | solution.py:385
  77.9 1.3 %collective-permute-done.27.first = bf16[32,3072]{1,0:T(8,128)(2,1)S(1)} collective-permute-done((bf16[32,3072]{1,0:T(8,128)(2,1)S(1)}, bf16[32,3072]{1,0:T(8,128)(2,1)S(1)}, u32[]{:S(2)}, u32[]{:S(2)}) %collective-permute-start.27) | collective-permute-done | bytes 196640 | tf_op jit(solution)/shard_map/ppermute | solution.py:385
  79.2 0.8 %finish.1 = bf16[32,6144]{1,0:T(8,128)(2,1)} custom-call(f32[2,32,3072]{2,1,0:T(8,128)S(1)} %add_own.1.gathered_ref, bf16[32,3072]{1,0:T(8,128)(2,1)S(1)} %collective-permute-done.27.first, bf16[32,3072]{1,0:T(8,128)(2,1)S(1)} %collective-permute-done.31.second), custom_call_target="tpu_custom_call" | custom-call | bytes 393216 | tf_op jit(solution)/shard_map/finish/pallas_call | solution.py:367
  (62 shorter events, 2.0 us)
Async XLA Ops:
  1.1 8.7 %collective-permute-start = (bf16[32,3072]{1,0:T(8,128)(2,1)S(1)}, bf16[32,3072]{1,0:T(8,128)(2,1)S(1)}, u32[]{:S(2)}, u32[]{:S(2)}) collective-permute-start(bf16[32,3072]{1,0:T(8,128)(2,1)S(1)} %get-tuple-element.74.refs_0_), channel_id=1, source_target_pairs={{0,2},{2,4},{4,6},{6,7},{7,5},{5,3},{3,1},{1,0},{8,10},{10,12},{12... | collective-permute-start | bytes 589832 | tf_op jit(solution)/shard_map/ppermute | solution.py:73
  4.1 7.8 %collective-permute-start.10 = (bf16[32,3072]{1,0:T(8,128)(2,1)S(1)}, bf16[32,3072]{1,0:T(8,128)(2,1)S(1)}, u32[]{:S(2)}, u32[]{:S(2)}) collective-permute-start(bf16[32,3072]{1,0:T(8,128)(2,1)S(1)} %get-tuple-element.73.refs_5_), channel_id=1, source_target_pairs={{2,0},{4,2},{6,4},{7,6},{5,7},{3,5},{1,3},{0,1},{10,8},{12,10},{14... | collective-permute-start | bytes 589832 | tf_op jit(solution)/shard_map/ppermute | solution.py:74
  4.1 12.0 %collective-permute-start.4 = (bf16[32,3072]{1,0:T(8,128)(2,1)S(1)}, bf16[32,3072]{1,0:T(8,128)(2,1)S(1)}, u32[]{:S(2)}, u32[]{:S(2)}) collective-permute-start(bf16[32,3072]{1,0:T(8,128)(2,1)S(1)} %get-tuple-element.74.refs_0_), channel_id=1, source_target_pairs={{2,0},{4,2},{6,4},{7,6},{5,7},{3,5},{1,3},{0,1},{10,8},{12,10},{14... | collective-permute-start | bytes 589832 | tf_op jit(solution)/shard_map/ppermute | solution.py:74
  6.1 10.1 %collective-permute-start.7 = (bf16[32,3072]{1,0:T(8,128)(2,1)S(1)}, bf16[32,3072]{1,0:T(8,128)(2,1)S(1)}, u32[]{:S(2)}, u32[]{:S(2)}) collective-permute-start(bf16[32,3072]{1,0:T(8,128)(2,1)S(1)} %get-tuple-element.73.refs_5_), channel_id=1, source_target_pairs={{0,2},{2,4},{4,6},{6,7},{7,5},{5,3},{3,1},{1,0},{8,10},{10,12},{12... | collective-permute-start | bytes 589832 | tf_op jit(solution)/shard_map/ppermute | solution.py:73
  9.8 10.6 %collective-permute-start.1 = (bf16[32,3072]{1,0:T(8,128)(2,1)S(1)}, bf16[32,3072]{1,0:T(8,128)(2,1)S(1)}, u32[]{:S(2)}, u32[]{:S(2)}) collective-permute-start(bf16[32,3072]{1,0:T(8,128)(2,1)S(1)} %collective-permute-done.refs_1_.arrived_ref), channel_id=1, source_target_pairs={{0,2},{2,4},{4,6},{6,7},{7,5},{5,3},{3,1},{1,0},{8,10},{10,12},{12... | collective-permute-start | bytes 589832 | tf_op jit(solution)/shard_map/ppermute | solution.py:73
  12.0 8.4 %collective-permute-start.11 = (bf16[32,3072]{1,0:T(8,128)(2,1)S(1)}, bf16[32,3072]{1,0:T(8,128)(2,1)S(1)}, u32[]{:S(2)}, u32[]{:S(2)}) collective-permute-start(bf16[32,3072]{1,0:T(8,128)(2,1)S(1)} %collective-permute-done.10.refs_7_.arrived_ref), channel_id=1, source_target_pairs={{2,0},{4,2},{6,4},{7,6},{5,7},{3,5},{1,3},{0,1},{10,8},{12,10},{14... | collective-permute-start | bytes 589832 | tf_op jit(solution)/shard_map/ppermute | solution.py:74
  16.2 8.4 %collective-permute-start.5 = (bf16[32,3072]{1,0:T(8,128)(2,1)S(1)}, bf16[32,3072]{1,0:T(8,128)(2,1)S(1)}, u32[]{:S(2)}, u32[]{:S(2)}) collective-permute-start(bf16[32,3072]{1,0:T(8,128)(2,1)S(1)} %collective-permute-done.4.refs_2_), channel_id=1, source_target_pairs={{2,0},{4,2},{6,4},{7,6},{5,7},{3,5},{1,3},{0,1},{10,8},{12,10},{14... | collective-permute-start | bytes 589832 | tf_op jit(solution)/shard_map/ppermute | solution.py:74
  16.2 8.4 %collective-permute-start.8 = (bf16[32,3072]{1,0:T(8,128)(2,1)S(1)}, bf16[32,3072]{1,0:T(8,128)(2,1)S(1)}, u32[]{:S(2)}, u32[]{:S(2)}) collective-permute-start(bf16[32,3072]{1,0:T(8,128)(2,1)S(1)} %collective-permute-done.7.refs_6_), channel_id=1, source_target_pairs={{0,2},{2,4},{4,6},{6,7},{7,5},{5,3},{3,1},{1,0},{8,10},{10,12},{12... | collective-permute-start | bytes 589832 | tf_op jit(solution)/shard_map/ppermute | solution.py:73
  18.2 8.4 %slice-start = ((s8[18874368]{0:T(1024)(128)(4,1)}), s8[4194304]{0:T(1024)(128)(4,1)S(1)}, s32[]{:S(2)}) async-start(s8[18874368]{0:T(1024)(128)(4,1)} %bitcast.1), calls=%async_computation | async-start | bytes 8388608
  18.2 8.4 %slice-start.1 = ((s8[18874368]{0:T(1024)(128)(4,1)}), s8[4194304]{0:T(1024)(128)(4,1)S(1)}, s32[]{:S(2)}) async-start(s8[18874368]{0:T(1024)(128)(4,1)} %bitcast.1), calls=%async_computation.1 | async-start | bytes 8388608
  18.2 8.4 %slice-start.2 = ((s8[18874368]{0:T(1024)(128)(4,1)}), s8[4194304]{0:T(1024)(128)(4,1)S(1)}, s32[]{:S(2)}) async-start(s8[18874368]{0:T(1024)(128)(4,1)} %bitcast.1), calls=%async_computation.2 | async-start | bytes 8388608
  18.2 8.4 %slice-start.3 = ((s8[18874368]{0:T(1024)(128)(4,1)}), s8[4194304]{0:T(1024)(128)(4,1)S(1)}, s32[]{:S(2)}) async-start(s8[18874368]{0:T(1024)(128)(4,1)} %bitcast.1), calls=%async_computation.3 | async-start | bytes 8388608
  18.2 8.4 %slice-start.4 = ((s8[18874368]{0:T(1024)(128)(4,1)}), s8[2097152]{0:T(1024)(128)(4,1)S(1)}, s32[]{:S(2)}) async-start(s8[18874368]{0:T(1024)(128)(4,1)} %bitcast.1), calls=%async_computation.4 | async-start | bytes 4194304
  20.4 10.3 %collective-permute-start.12 = (bf16[32,3072]{1,0:T(8,128)(2,1)S(1)}, bf16[32,3072]{1,0:T(8,128)(2,1)S(1)}, u32[]{:S(2)}, u32[]{:S(2)}) collective-permute-start(bf16[32,3072]{1,0:T(8,128)(2,1)S(1)} %collective-permute-done.11.refs_9_), channel_id=1, source_target_pairs={{2,0},{4,2},{6,4},{7,6},{5,7},{3,5},{1,3},{0,1},{10,8},{12,10},{14... | collective-permute-start | bytes 589832 | tf_op jit(solution)/shard_map/ppermute | solution.py:74
  20.4 8.7 %collective-permute-start.2 = (bf16[32,3072]{1,0:T(8,128)(2,1)S(1)}, bf16[32,3072]{1,0:T(8,128)(2,1)S(1)}, u32[]{:S(2)}, u32[]{:S(2)}) collective-permute-start(bf16[32,3072]{1,0:T(8,128)(2,1)S(1)} %collective-permute-done.1.refs_3_), channel_id=1, source_target_pairs={{0,2},{2,4},{4,6},{6,7},{7,5},{5,3},{3,1},{1,0},{8,10},{10,12},{12... | collective-permute-start | bytes 589832 | tf_op jit(solution)/shard_map/ppermute | solution.py:73
  24.6 8.4 %collective-permute-start.6 = (bf16[32,3072]{1,0:T(8,128)(2,1)S(1)}, bf16[32,3072]{1,0:T(8,128)(2,1)S(1)}, u32[]{:S(2)}, u32[]{:S(2)}) collective-permute-start(bf16[32,3072]{1,0:T(8,128)(2,1)S(1)} %collective-permute-done.5.refs_4_), channel_id=1, source_target_pairs={{2,0},{4,2},{6,4},{7,6},{5,7},{3,5},{1,3},{0,1},{10,8},{12,10},{14... | collective-permute-start | bytes 589832 | tf_op jit(solution)/shard_map/ppermute | solution.py:74
  24.6 8.4 %collective-permute-start.9 = (bf16[32,3072]{1,0:T(8,128)(2,1)S(1)}, bf16[32,3072]{1,0:T(8,128)(2,1)S(1)}, u32[]{:S(2)}, u32[]{:S(2)}) collective-permute-start(bf16[32,3072]{1,0:T(8,128)(2,1)S(1)} %collective-permute-done.8.refs_8_), channel_id=1, source_target_pairs={{0,2},{2,4},{4,6},{6,7},{7,5},{5,3},{3,1},{1,0},{8,10},{10,12},{12... | collective-permute-start | bytes 589832 | tf_op jit(solution)/shard_map/ppermute | solution.py:73
  29.1 5.7 %collective-permute-start.3 = (bf16[32,3072]{1,0:T(8,128)(2,1)S(1)}, bf16[32,3072]{1,0:T(8,128)(2,1)S(1)}, u32[]{:S(2)}, u32[]{:S(2)}) collective-permute-start(bf16[32,3072]{1,0:T(8,128)(2,1)S(1)} %collective-permute-done.2.refs_0_), channel_id=1, source_target_pairs={{0,2},{2,4},{4,6},{6,7},{7,5},{5,3},{3,1},{1,0},{8,10},{10,12},{12... | collective-permute-start | bytes 589832 | tf_op jit(solution)/shard_map/ppermute | solution.py:77
  30.7 5.7 %collective-permute-start.13 = (bf16[32,3072]{1,0:T(8,128)(2,1)S(1)}, bf16[32,3072]{1,0:T(8,128)(2,1)S(1)}, u32[]{:S(2)}, u32[]{:S(2)}) collective-permute-start(bf16[32,3072]{1,0:T(8,128)(2,1)S(1)} %collective-permute-done.12.refs_3_), channel_id=1, source_target_pairs={{2,0},{4,2},{6,4},{7,6},{5,7},{3,5},{1,3},{0,1},{10,8},{12,10},{14... | collective-permute-start | bytes 589832 | tf_op jit(solution)/shard_map/ppermute | solution.py:78
  37.3 1.5 %collective-permute-start.14 = (bf16[2,128,128]{2,1,0:T(8,128)(2,1)S(1)}, bf16[2,128,128]{2,1,0:T(8,128)(2,1)S(1)}, u32[]{:S(2)}, u32[]{:S(2)}) collective-permute-start(bf16[2,128,128]{2,1,0:T(8,128)(2,1)S(1)} %get-tuple-element.54.one_ref), channel_id=1, source_target_pairs={{0,8},{8,0},{16,24},{24,16},{1,9},{9,1},{17,25},{25,17},{2,10},{10... | collective-permute-start | bytes 196616 | tf_op jit(solution)/shard_map/ppermute | solution.py:421
  38.2 2.2 %collective-permute-start.16 = (bf16[2,128,128]{2,1,0:T(8,128)(2,1)S(1)}, bf16[2,128,128]{2,1,0:T(8,128)(2,1)S(1)}, u32[]{:S(2)}, u32[]{:S(2)}) collective-permute-start(bf16[2,128,128]{2,1,0:T(8,128)(2,1)S(1)} %get-tuple-element.55.one_ref), channel_id=1, source_target_pairs={{0,8},{8,0},{16,24},{24,16},{1,9},{9,1},{17,25},{25,17},{2,10},{10... | collective-permute-start | bytes 196616 | tf_op jit(solution)/shard_map/ppermute | solution.py:421
  38.8 5.9 %collective-permute-start.15 = (bf16[2,128,128]{2,1,0:T(8,128)(2,1)S(1)}, bf16[2,128,128]{2,1,0:T(8,128)(2,1)S(1)}, u32[]{:S(2)}, u32[]{:S(2)}) collective-permute-start(bf16[2,128,128]{2,1,0:T(8,128)(2,1)S(1)} %add_states.2.refs_0_), channel_id=1, source_target_pairs={{0,16},{8,24},{16,0},{24,8},{1,17},{9,25},{17,1},{25,9},{2,18},{10... | collective-permute-start | bytes 196616 | tf_op jit(solution)/shard_map/ppermute | solution.py:421
  40.4 4.3 %collective-permute-start.17 = (bf16[2,128,128]{2,1,0:T(8,128)(2,1)S(1)}, bf16[2,128,128]{2,1,0:T(8,128)(2,1)S(1)}, u32[]{:S(2)}, u32[]{:S(2)}) collective-permute-start(bf16[2,128,128]{2,1,0:T(8,128)(2,1)S(1)} %add_states.3), channel_id=1, source_target_pairs={{0,16},{8,24},{16,0},{24,8},{1,17},{9,25},{17,1},{25,9},{2,18},{10... | collective-permute-start | bytes 196616 | tf_op jit(solution)/shard_map/ppermute | solution.py:421
  41.3 3.5 %slice-start.5 = ((s8[6291456]{0:T(1024)(128)(4,1)}), s8[4194304]{0:T(1024)(128)(4,1)S(1)}, s32[]{:S(2)}) async-start(s8[6291456]{0:T(1024)(128)(4,1)} %bitcast.3), calls=%async_computation.5 | async-start | bytes 8388608
  41.3 3.5 %slice-start.6 = ((s8[6291456]{0:T(1024)(128)(4,1)}), s8[2097152]{0:T(1024)(128)(4,1)S(1)}, s32[]{:S(2)}) async-start(s8[6291456]{0:T(1024)(128)(4,1)} %bitcast.3), calls=%async_computation.6 | async-start | bytes 4194304
  41.3 3.5 %copy-start = (f32[4,128,128]{2,1,0:T(8,128)S(1)}, f32[4,128,128]{2,1,0:T(8,128)}, u32[]{:S(2)}) copy-start(f32[4,128,128]{2,1,0:T(8,128)} %initial_ref.1) | copy-start | bytes 786436
  41.3 3.5 %copy-start.1 = (f32[512]{0:T(512)S(1)}, f32[512]{0:T(512)}, u32[]{:S(2)}) copy-start(f32[512]{0:T(512)} %param.8) | copy-start | bytes 6148
  46.3 6.4 %collective-permute-start.28 = (bf16[32,3072]{1,0:T(8,128)(2,1)S(1)}, bf16[32,3072]{1,0:T(8,128)(2,1)S(1)}, u32[]{:S(2)}, u32[]{:S(2)}) collective-permute-start(bf16[32,3072]{1,0:T(8,128)(2,1)S(1)} %get-tuple-element.72), channel_id=1, source_target_pairs={{0,2},{2,4},{4,6},{6,7},{7,5},{5,3},{3,1},{1,0},{8,10},{10,12},{12... | collective-permute-start | bytes 589832 | tf_op jit(solution)/shard_map/ppermute | solution.py:385
  47.9 7.8 %collective-permute-start.24 = (bf16[32,3072]{1,0:T(8,128)(2,1)S(1)}, bf16[32,3072]{1,0:T(8,128)(2,1)S(1)}, u32[]{:S(2)}, u32[]{:S(2)}) collective-permute-start(bf16[32,3072]{1,0:T(8,128)(2,1)S(1)} %get-tuple-element.68), channel_id=1, source_target_pairs={{2,0},{4,2},{6,4},{7,6},{5,7},{3,5},{1,3},{0,1},{10,8},{12,10},{14... | collective-permute-start | bytes 589832 | tf_op jit(solution)/shard_map/ppermute | solution.py:385
  50.0 10.0 %collective-permute-start.21 = (bf16[32,3072]{1,0:T(8,128)(2,1)S(1)}, bf16[32,3072]{1,0:T(8,128)(2,1)S(1)}, u32[]{:S(2)}, u32[]{:S(2)}) collective-permute-start(bf16[32,3072]{1,0:T(8,128)(2,1)S(1)} %get-tuple-element.64), channel_id=1, source_target_pairs={{2,0},{4,2},{6,4},{7,6},{5,7},{3,5},{1,3},{0,1},{10,8},{12,10},{14... | collective-permute-start | bytes 589832 | tf_op jit(solution)/shard_map/ppermute | solution.py:385
  51.3 9.1 %collective-permute-start.18 = (bf16[32,3072]{1,0:T(8,128)(2,1)S(1)}, bf16[32,3072]{1,0:T(8,128)(2,1)S(1)}, u32[]{:S(2)}, u32[]{:S(2)}) collective-permute-start(bf16[32,3072]{1,0:T(8,128)(2,1)S(1)} %get-tuple-element.61), channel_id=1, source_target_pairs={{0,2},{2,4},{4,6},{6,7},{7,5},{5,3},{3,1},{1,0},{8,10},{10,12},{12... | collective-permute-start | bytes 589832 | tf_op jit(solution)/shard_map/ppermute | solution.py:385
  52.8 9.7 %collective-permute-start.29 = (bf16[32,3072]{1,0:T(8,128)(2,1)S(1)}, bf16[32,3072]{1,0:T(8,128)(2,1)S(1)}, u32[]{:S(2)}, u32[]{:S(2)}) collective-permute-start(bf16[32,3072]{1,0:T(8,128)(2,1)S(1)} %add_step.17), channel_id=1, source_target_pairs={{0,2},{2,4},{4,6},{6,7},{7,5},{5,3},{3,1},{1,0},{8,10},{10,12},{12... | collective-permute-start | bytes 589832 | tf_op jit(solution)/shard_map/ppermute | solution.py:385
  55.8 8.4 %collective-permute-start.25 = (bf16[32,3072]{1,0:T(8,128)(2,1)S(1)}, bf16[32,3072]{1,0:T(8,128)(2,1)S(1)}, u32[]{:S(2)}, u32[]{:S(2)}) collective-permute-start(bf16[32,3072]{1,0:T(8,128)(2,1)S(1)} %add_step.14), channel_id=1, source_target_pairs={{2,0},{4,2},{6,4},{7,6},{5,7},{3,5},{1,3},{0,1},{10,8},{12,10},{14... | collective-permute-start | bytes 589832 | tf_op jit(solution)/shard_map/ppermute | solution.py:385
  60.0 8.4 %collective-permute-start.22 = (bf16[32,3072]{1,0:T(8,128)(2,1)S(1)}, bf16[32,3072]{1,0:T(8,128)(2,1)S(1)}, u32[]{:S(2)}, u32[]{:S(2)}) collective-permute-start(bf16[32,3072]{1,0:T(8,128)(2,1)S(1)} %add_step.12), channel_id=1, source_target_pairs={{2,0},{4,2},{6,4},{7,6},{5,7},{3,5},{1,3},{0,1},{10,8},{12,10},{14... | collective-permute-start | bytes 589832 | tf_op jit(solution)/shard_map/ppermute | solution.py:385
  60.4 8.4 %collective-permute-start.19 = (bf16[32,3072]{1,0:T(8,128)(2,1)S(1)}, bf16[32,3072]{1,0:T(8,128)(2,1)S(1)}, u32[]{:S(2)}, u32[]{:S(2)}) collective-permute-start(bf16[32,3072]{1,0:T(8,128)(2,1)S(1)} %add_step.10), channel_id=1, source_target_pairs={{0,2},{2,4},{4,6},{6,7},{7,5},{5,3},{3,1},{1,0},{8,10},{10,12},{12... | collective-permute-start | bytes 589832 | tf_op jit(solution)/shard_map/ppermute | solution.py:385
  62.5 8.4 %collective-permute-start.30 = (bf16[32,3072]{1,0:T(8,128)(2,1)S(1)}, bf16[32,3072]{1,0:T(8,128)(2,1)S(1)}, u32[]{:S(2)}, u32[]{:S(2)}) collective-permute-start(bf16[32,3072]{1,0:T(8,128)(2,1)S(1)} %add_step.18), channel_id=1, source_target_pairs={{0,2},{2,4},{4,6},{6,7},{7,5},{5,3},{3,1},{1,0},{8,10},{10,12},{12... | collective-permute-start | bytes 589832 | tf_op jit(solution)/shard_map/ppermute | solution.py:385
  64.3 8.5 %collective-permute-start.26 = (bf16[32,3072]{1,0:T(8,128)(2,1)S(1)}, bf16[32,3072]{1,0:T(8,128)(2,1)S(1)}, u32[]{:S(2)}, u32[]{:S(2)}) collective-permute-start(bf16[32,3072]{1,0:T(8,128)(2,1)S(1)} %add_step.15), channel_id=1, source_target_pairs={{2,0},{4,2},{6,4},{7,6},{5,7},{3,5},{1,3},{0,1},{10,8},{12,10},{14... | collective-permute-start | bytes 589832 | tf_op jit(solution)/shard_map/ppermute | solution.py:385
  68.5 8.4 %collective-permute-start.23 = (bf16[32,3072]{1,0:T(8,128)(2,1)S(1)}, bf16[32,3072]{1,0:T(8,128)(2,1)S(1)}, u32[]{:S(2)}, u32[]{:S(2)}) collective-permute-start(bf16[32,3072]{1,0:T(8,128)(2,1)S(1)} %add_step.13), channel_id=1, source_target_pairs={{2,0},{4,2},{6,4},{7,6},{5,7},{3,5},{1,3},{0,1},{10,8},{12,10},{14... | collective-permute-start | bytes 589832 | tf_op jit(solution)/shard_map/ppermute | solution.py:385
  68.8 8.0 %collective-permute-start.20 = (bf16[32,3072]{1,0:T(8,128)(2,1)S(1)}, bf16[32,3072]{1,0:T(8,128)(2,1)S(1)}, u32[]{:S(2)}, u32[]{:S(2)}) collective-permute-start(bf16[32,3072]{1,0:T(8,128)(2,1)S(1)} %add_step.11), channel_id=1, source_target_pairs={{0,2},{2,4},{4,6},{6,7},{7,5},{5,3},{3,1},{1,0},{8,10},{10,12},{12... | collective-permute-start | bytes 589832 | tf_op jit(solution)/shard_map/ppermute | solution.py:385
  70.9 7.0 %collective-permute-start.31 = (bf16[32,3072]{1,0:T(8,128)(2,1)S(1)}, bf16[32,3072]{1,0:T(8,128)(2,1)S(1)}, u32[]{:S(2)}, u32[]{:S(2)}) collective-permute-start(bf16[32,3072]{1,0:T(8,128)(2,1)S(1)} %add_step.19), channel_id=1, source_target_pairs={{0,2},{2,4},{4,6},{6,7},{7,5},{5,3},{3,1},{1,0},{8,10},{10,12},{12... | collective-permute-start | bytes 589832 | tf_op jit(solution)/shard_map/ppermute | solution.py:385
  72.8 6.4 %collective-permute-start.27 = (bf16[32,3072]{1,0:T(8,128)(2,1)S(1)}, bf16[32,3072]{1,0:T(8,128)(2,1)S(1)}, u32[]{:S(2)}, u32[]{:S(2)}) collective-permute-start(bf16[32,3072]{1,0:T(8,128)(2,1)S(1)} %add_step.16), channel_id=1, source_target_pairs={{2,0},{4,2},{6,4},{7,6},{5,7},{3,5},{1,3},{0,1},{10,8},{12,10},{14... | collective-permute-start | bytes 589832 | tf_op jit(solution)/shard_map/ppermute | solution.py:385

commit v15 on v14

--- a/solution.py
+++ b/solution.py
@@ -89,14 +89,14 @@
     return jnp.where(projected > 0.0, projected + 1.0, jnp.exp(jnp.minimum(projected, 0.0)))
 
 
-def early_keys(first_pieces, second_pieces, weight, n_rows):
+def early_keys(first_pieces, second_pieces, weight, n_rows, after):
     _, width, columns = weight.shape
     half = width // 2
     count = len(first_pieces)
     early = count * first_pieces[0].shape[0]
 
     def body(*refs):
-        weight_ref, feat_ref, first_ref, second_ref = refs[2 * count :]
+        weight_ref, (feat_ref, first_ref, second_ref) = refs[2 * count], refs[-3:]
         assemble(refs[:count], first_ref, 0)
         assemble(refs[count : 2 * count], second_ref, 0)
         projected = jnp.dot(first_ref[:early, :], weight_ref[1, :half, :], preferred_element_type=F32)
@@ -106,12 +106,12 @@
     return call(
         body,
         [jax.ShapeDtypeStruct((n_rows, columns), BF16)] + [jax.ShapeDtypeStruct((n_rows, half), BF16)] * 2,
-        [VMEM] * (2 * count + 1),
+        [VMEM] * (2 * count + 1) + [ANY] * len(after),
         [VMEM] * 3,
         flops=2 * early * width * columns,
         nbytes=2 * width * columns,
         name="early_keys",
-    )(*first_pieces, *second_pieces, weight)
+    )(*first_pieces, *second_pieces, weight, *after)
 
 
 def early_values(first_rows, second_rows, weight, early):
@@ -440,7 +440,7 @@
 
     blocks = n_fsdp - 3
     early = blocks * rows
-    feat_k, *halves = early_keys(held[0][:blocks], held[1][:blocks], qkv_weight, n_rows)
+    feat_k, *halves = early_keys(held[0][:blocks], held[1][:blocks], qkv_weight, n_rows, [held[1][-2]])
     values = early_values(*halves, qkv_weight, early)
     first_rows, second_rows = assemble_late([held[0][blocks:-1], held[1][blocks:-1]], halves, early, [values])
     marks = [mark(held[0][1]), mark(held[1][2])]

time: 80.1 us -> 79.5 us (level)
    ppermute x6, starting transfers between devices: 1.95 us -> 12.8 us  [ring_gather(): going_left[1 - part] = lax.ppermute(going_left[1 - part], 'fsdp', left)]
    ppermute x6, starting transfers between devices: 11.4 us -> 0.75 us  [ring_gather(): going_right[part] = lax.ppermute(going_right[part], 'fsdp', right)]
    ppermute x7, starting transfers between devices: 12.1 us -> 4.29 us  [hop(): lax.ppermute(to_left, 'fsdp', left)]
    ppermute x7, starting transfers between devices: 3.19 us -> 10.7 us  [hop(): lax.ppermute(to_right, 'fsdp', right)]
    ppermute x7, waiting for transfers between devices: 13.3 us -> 7.75 us  [hop(): lax.ppermute(to_right, 'fsdp', right)]
    ppermute x7, waiting for transfers between devices: 2.02 us -> 6.8 us  [hop(): lax.ppermute(to_left, 'fsdp', left)]
    ppermute x1, starting transfers between devices: 1.63 us -> 0.11 us  [ring_gather(): held[0].append(lax.ppermute(going_right[0], 'fsdp', right))]
    ppermute x1, starting transfers between devices: 0.45 us -> 1.91 us  [ring_gather(): held[1].append(lax.ppermute(going_left[1], 'fsdp', left))]
  transfers between devices with their start and end apart: 32 -> 32, of which waited for: 17 -> 16; matrix products, arithmetic and copies ran while one was open for 0% -> 0% of each run, Pallas kernels for 11% -> 11%
where the time goes in v15:
time: 79.5 us; the launch traced here: 79.4 us
  starting transfers between devices  33.6 us (42%)
  waiting for transfers between devices  32.2 us (41%)
  Pallas kernels  12.2 us (15%)
  local copies, waits for them, and re-layouts  1.09 us (1%)
    ppermute x6, starting transfers between devices, ring_gather(): going_left[1 - part] = lax.ppermute(going_left[1 - part], 'fsdp', left)  12.8 us
    ppermute x7, starting transfers between devices, hop(): lax.ppermute(to_right, 'fsdp', right)  10.7 us
    ppermute x6, waiting for transfers between devices, ring_gather(): going_left[1 - part] = lax.ppermute(going_left[1 - part], 'fsdp', left)  9.87 us
    ppermute x7, waiting for transfers between devices, hop(): lax.ppermute(to_right, 'fsdp', right)  7.75 us
    ppermute x7, waiting for transfers between devices, hop(): lax.ppermute(to_left, 'fsdp', left)  6.8 us
    ppermute x7, starting transfers between devices, hop(): lax.ppermute(to_left, 'fsdp', left)  4.29 us
    ppermute x6, waiting for transfers between devices, ring_gather(): going_right[part] = lax.ppermute(going_right[part], 'fsdp', right)  4.25 us
    ppermute x4, starting transfers between devices, exchange_states(): received[at].append(lax.ppermute(total, 'ctx', pairs))  3.09 us
  transfers between devices with their start and end apart: 32, of which 16 were waited for; matrix products, arithmetic and copies ran while one was open for 0% of the time, Pallas kernels for 11%

profile of v15, /device:TPU:0, one launch (start us, length us, event | category | flops | bytes accessed | tf_op | source)
XLA Modules:
  0.0 79.4 jit_solution(13796805645792393259)
XLA Ops:
  0.0 1.0 %fusion = (bf16[32,3072]{1,0:T(8,128)(2,1)S(1)}, bf16[32,3072]{1,0:T(8,128)(2,1)S(1)}) fusion(bf16[32,6144]{1,0:T(8,128)(2,1)} %param.5), kind=kLoop, calls=%fused_computation | loop fusion | bytes 786432 | tf_op jit(solution)/shard_map/slice | solution.py:68
  1.1 3.0 %collective-permute-start.10 = (bf16[32,3072]{1,0:T(8,128)(2,1)S(1)}, bf16[32,3072]{1,0:T(8,128)(2,1)S(1)}, u32[]{:S(2)}, u32[]{:S(2)}) collective-permute-start(bf16[32,3072]{1,0:T(8,128)(2,1)S(1)} %get-tuple-element.73.refs_5_), channel_id=1, source_target_pairs={{2,0},{4,2},{6,4},{7,6},{5,7},{3,5},{1,3},{0,1},{10,8},{12,10},{14... | collective-permute-start | bytes 589832 | tf_op jit(solution)/shard_map/ppermute | solution.py:74
  4.2 1.9 %collective-permute-start.4 = (bf16[32,3072]{1,0:T(8,128)(2,1)S(1)}, bf16[32,3072]{1,0:T(8,128)(2,1)S(1)}, u32[]{:S(2)}, u32[]{:S(2)}) collective-permute-start(bf16[32,3072]{1,0:T(8,128)(2,1)S(1)} %get-tuple-element.74.refs_0_), channel_id=1, source_target_pairs={{2,0},{4,2},{6,4},{7,6},{5,7},{3,5},{1,3},{0,1},{10,8},{12,10},{14... | collective-permute-start | bytes 589832 | tf_op jit(solution)/shard_map/ppermute | solution.py:74
  6.2 3.6 %collective-permute-done.10.refs_7_.arrived_ref = bf16[32,3072]{1,0:T(8,128)(2,1)S(1)} collective-permute-done((bf16[32,3072]{1,0:T(8,128)(2,1)S(1)}, bf16[32,3072]{1,0:T(8,128)(2,1)S(1)}, u32[]{:S(2)}, u32[]{:S(2)}) %collective-permute-start.10) | collective-permute-done | bytes 196640 | tf_op jit(solution)/shard_map/ppermute | solution.py:74
  9.9 2.0 %collective-permute-start.11 = (bf16[32,3072]{1,0:T(8,128)(2,1)S(1)}, bf16[32,3072]{1,0:T(8,128)(2,1)S(1)}, u32[]{:S(2)}, u32[]{:S(2)}) collective-permute-start(bf16[32,3072]{1,0:T(8,128)(2,1)S(1)} %collective-permute-done.10.refs_7_.arrived_ref), channel_id=1, source_target_pairs={{2,0},{4,2},{6,4},{7,6},{5,7},{3,5},{1,3},{0,1},{10,8},{12,10},{14... | collective-permute-start | bytes 589832 | tf_op jit(solution)/shard_map/ppermute | solution.py:74
  12.0 2.1 %collective-permute-done.4.refs_2_ = bf16[32,3072]{1,0:T(8,128)(2,1)S(1)} collective-permute-done((bf16[32,3072]{1,0:T(8,128)(2,1)S(1)}, bf16[32,3072]{1,0:T(8,128)(2,1)S(1)}, u32[]{:S(2)}, u32[]{:S(2)}) %collective-permute-start.4) | collective-permute-done | bytes 196640 | tf_op jit(solution)/shard_map/ppermute | solution.py:74
  14.1 2.0 %collective-permute-start.5 = (bf16[32,3072]{1,0:T(8,128)(2,1)S(1)}, bf16[32,3072]{1,0:T(8,128)(2,1)S(1)}, u32[]{:S(2)}, u32[]{:S(2)}) collective-permute-start(bf16[32,3072]{1,0:T(8,128)(2,1)S(1)} %collective-permute-done.4.refs_2_), channel_id=1, source_target_pairs={{2,0},{4,2},{6,4},{7,6},{5,7},{3,5},{1,3},{0,1},{10,8},{12,10},{14... | collective-permute-start | bytes 589832 | tf_op jit(solution)/shard_map/ppermute | solution.py:74
  16.2 2.1 %collective-permute-done.11.refs_9_ = bf16[32,3072]{1,0:T(8,128)(2,1)S(1)} collective-permute-done((bf16[32,3072]{1,0:T(8,128)(2,1)S(1)}, bf16[32,3072]{1,0:T(8,128)(2,1)S(1)}, u32[]{:S(2)}, u32[]{:S(2)}) %collective-permute-start.11) | collective-permute-done | bytes 196640 | tf_op jit(solution)/shard_map/ppermute | solution.py:74
  18.3 2.0 %collective-permute-start.12 = (bf16[32,3072]{1,0:T(8,128)(2,1)S(1)}, bf16[32,3072]{1,0:T(8,128)(2,1)S(1)}, u32[]{:S(2)}, u32[]{:S(2)}) collective-permute-start(bf16[32,3072]{1,0:T(8,128)(2,1)S(1)} %collective-permute-done.11.refs_9_), channel_id=1, source_target_pairs={{2,0},{4,2},{6,4},{7,6},{5,7},{3,5},{1,3},{0,1},{10,8},{12,10},{14... | collective-permute-start | bytes 589832 | tf_op jit(solution)/shard_map/ppermute | solution.py:74
  20.4 2.1 %collective-permute-done.5.refs_4_ = bf16[32,3072]{1,0:T(8,128)(2,1)S(1)} collective-permute-done((bf16[32,3072]{1,0:T(8,128)(2,1)S(1)}, bf16[32,3072]{1,0:T(8,128)(2,1)S(1)}, u32[]{:S(2)}, u32[]{:S(2)}) %collective-permute-start.5) | collective-permute-done | bytes 196640 | tf_op jit(solution)/shard_map/ppermute | solution.py:74
  22.5 2.0 %collective-permute-start.6 = (bf16[32,3072]{1,0:T(8,128)(2,1)S(1)}, bf16[32,3072]{1,0:T(8,128)(2,1)S(1)}, u32[]{:S(2)}, u32[]{:S(2)}) collective-permute-start(bf16[32,3072]{1,0:T(8,128)(2,1)S(1)} %collective-permute-done.5.refs_4_), channel_id=1, source_target_pairs={{2,0},{4,2},{6,4},{7,6},{5,7},{3,5},{1,3},{0,1},{10,8},{12,10},{14... | collective-permute-start | bytes 589832 | tf_op jit(solution)/shard_map/ppermute | solution.py:74
  24.6 4.1 %collective-permute-done.2.refs_0_ = bf16[32,3072]{1,0:T(8,128)(2,1)S(1)} collective-permute-done((bf16[32,3072]{1,0:T(8,128)(2,1)S(1)}, bf16[32,3072]{1,0:T(8,128)(2,1)S(1)}, u32[]{:S(2)}, u32[]{:S(2)}) %collective-permute-start.2) | collective-permute-done | bytes 196640 | tf_op jit(solution)/shard_map/ppermute | solution.py:73
  28.8 1.9 %collective-permute-start.13 = (bf16[32,3072]{1,0:T(8,128)(2,1)S(1)}, bf16[32,3072]{1,0:T(8,128)(2,1)S(1)}, u32[]{:S(2)}, u32[]{:S(2)}) collective-permute-start(bf16[32,3072]{1,0:T(8,128)(2,1)S(1)} %collective-permute-done.12.refs_11_.refs_3_), channel_id=1, source_target_pairs={{2,0},{4,2},{6,4},{7,6},{5,7},{3,5},{1,3},{0,1},{10,8},{12,10},{14... | collective-permute-start | bytes 589832 | tf_op jit(solution)/shard_map/ppermute | solution.py:78
  30.8 1.2 %early_keys.1 = (bf16[256,512]{1,0:T(8,128)(2,1)S(1)}, bf16[256,3072]{1,0:T(8,128)(2,1)S(1)}, bf16[256,3072]{1,0:T(8,128)(2,1)S(1)}) custom-call(bf16[32,3072]{1,0:T(8,128)(2,1)S(1)} %get-tuple-element.74.refs_0_, bf16[32,3072]{1,0:T(8,128)(2,1)S(1)} %collective-permute-done.refs_1_.arrived_ref, bf16[32,3072]{1,0:T(8,128)(2,1)S(1)} %collective-permute-done.4.refs_2_, ...), custom_call_target="tpu_custom_call" | custom-call | flops 1006632960 | bytes 6291456 | tf_op jit(solution)/shard_map/early_keys/pallas_call | solution.py:106
  32.0 1.2 %early_values.1.refs_6_.refs_5_ = bf16[256,512]{1,0:T(8,128)(2,1)S(1)} custom-call(bf16[256,3072]{1,0:T(8,128)(2,1)S(1)} %get-tuple-element.39.first_ref.refs_4_, bf16[256,3072]{1,0:T(8,128)(2,1)S(1)} %get-tuple-element.40.second_ref.refs_5_, bf16[3,6144,512]{2,1,0:T(8,128)(2,1)S(1)} %bitcast.2), custom_call_target="tpu_custom_call" | custom-call | flops 1006632960 | bytes 6291456 | tf_op jit(solution)/shard_map/early_values/pallas_call | solution.py:126
  33.3 2.4 %collective-permute-done.3.refs_0_ = bf16[32,3072]{1,0:T(8,128)(2,1)S(1)} collective-permute-done((bf16[32,3072]{1,0:T(8,128)(2,1)S(1)}, bf16[32,3072]{1,0:T(8,128)(2,1)S(1)}, u32[]{:S(2)}, u32[]{:S(2)}) %collective-permute-start.3) | collective-permute-done | bytes 196640 | tf_op jit(solution)/shard_map/ppermute | solution.py:77
  35.7 1.1 %first_pass.1 = (bf16[256,3072]{1,0:T(8,128)(2,1)S(1)}, f32[2,96,512]{2,1,0:T(8,128)S(1)}) custom-call(bf16[32,3072]{1,0:T(8,128)(2,1)S(1)} %collective-permute-done.3.refs_0_, bf16[256,3072]{1,0:T(8,128)(2,1)S(1)} %get-tuple-element.41.refs_1_, bf16[3,6144,512]{2,1,0:T(8,128)(2,1)S(1)} %bitcast.2, ...), custom_call_target="tpu_custom_call", output_to_operand_aliasing={{0}: (1, {})} | custom-call | flops 603979776 | bytes 6291456 | tf_op jit(solution)/shard_map/first_pass/pallas_call | solution.py:166
  36.8 0.9 %late_keys_and_values.2 = (bf16[256,3072]{1,0:T(8,128)(2,1)S(1)}, bf16[256,512]{1,0:T(8,128)(2,1)S(1)}, bf16[256,512]{1,0:T(8,128)(2,1)S(1)}, bf16[2,128,128]{2,1,0:T(8,128)(2,1)S(1)}) custom-call(bf16[32,3072]{1,0:T(8,128)(2,1)S(1)} %collective-permute-done.13.refs_0_, ...), custom_call_target="tpu_custom_call", output_to_operand_aliasing={{0}: (1, {}), {1}: (4, {}), {2}: (5, {})} | custom-call | flops 301989888 | bytes 3145728 | tf_op jit(solution)/shard_map/late_keys_and_values/pallas_call | solution.py:206
  37.8 0.9 %late_keys_and_values.3 = (bf16[256,3072]{1,0:T(8,128)(2,1)S(1)}, bf16[256,512]{1,0:T(8,128)(2,1)S(1)}, bf16[256,512]{1,0:T(8,128)(2,1)S(1)}, bf16[2,128,128]{2,1,0:T(8,128)(2,1)S(1)}) custom-call(bf16[256,3072]{1,0:T(8,128)(2,1)S(1)} %get-tuple-element.46.refs_0_, ...), custom_call_target="tpu_custom_call", output_to_operand_aliasing={{0}: (0, {}), {1}: (3, {}), {2}: (4, {})} | custom-call | flops 5000000000 | bytes 3145728 | tf_op jit(solution)/shard_map/late_keys_and_values/pallas_call | solution.py:206
  38.7 0.6 collective-permute-start.16
  39.2 1.6 %collective-permute-start.15 = (bf16[2,128,128]{2,1,0:T(8,128)(2,1)S(1)}, bf16[2,128,128]{2,1,0:T(8,128)(2,1)S(1)}, u32[]{:S(2)}, u32[]{:S(2)}) collective-permute-start(bf16[2,128,128]{2,1,0:T(8,128)(2,1)S(1)} %add_states.2.refs_0_), channel_id=1, source_target_pairs={{0,16},{8,24},{16,0},{24,8},{1,17},{9,25},{17,1},{25,9},{2,18},{10... | collective-permute-start | bytes 196616 | tf_op jit(solution)/shard_map/ppermute | solution.py:421
  40.8 0.9 %collective-permute-start.17 = (bf16[2,128,128]{2,1,0:T(8,128)(2,1)S(1)}, bf16[2,128,128]{2,1,0:T(8,128)(2,1)S(1)}, u32[]{:S(2)}, u32[]{:S(2)}) collective-permute-start(bf16[2,128,128]{2,1,0:T(8,128)(2,1)S(1)} %add_states.3), channel_id=1, source_target_pairs={{0,16},{8,24},{16,0},{24,8},{1,17},{9,25},{17,1},{25,9},{2,18},{10... | collective-permute-start | bytes 196616 | tf_op jit(solution)/shard_map/ppermute | solution.py:421
  41.7 2.3 %queries_within.1 = (bf16[256,512]{1,0:T(8,128)(2,1)S(1)}, f32[256,512]{1,0:T(8,128)S(1)}) custom-call(bf16[256,3072]{1,0:T(8,128)(2,1)S(1)} %get-tuple-element.43.first_ref, bf16[256,3072]{1,0:T(8,128)(2,1)S(1)} %get-tuple-element.49.second_ref, bf16[3,6144,512]{2,1,0:T(8,128)(2,1)S(1)} %bitcast.2, bf16[256,512]{1,0:T(8,128)(2,1)S(1)} %get-tuple-element.50.k_ref, ...), custom_call_target="tpu_custom_call" | custom-call | flops 1744830464 | bytes 6291456 | tf_op jit(solution)/shard_map/queries_within/pallas_call | solution.py:249
  44.0 1.1 %collective-permute-done.17.refs_3_ = bf16[2,128,128]{2,1,0:T(8,128)(2,1)S(1)} collective-permute-done((bf16[2,128,128]{2,1,0:T(8,128)(2,1)S(1)}, bf16[2,128,128]{2,1,0:T(8,128)(2,1)S(1)}, u32[]{:S(2)}, u32[]{:S(2)}) %collective-permute-start.17) | collective-permute-done | bytes 65568 | tf_op jit(solution)/shard_map/ppermute | solution.py:421
  45.2 1.6 %attend_and_project.1 = (bf16[256,512]{1,0:T(8,128)(2,1)S(1)}, bf16[32,3072]{1,0:T(8,128)(2,1)S(1)}, bf16[32,3072]{1,0:T(8,128)(2,1)S(1)}) custom-call(bf16[256,512]{1,0:T(8,128)(2,1)S(1)} %get-tuple-element.52.q_ref, f32[256,512]{1,0:T(8,128)S(1)} %get-tuple-element.53.within_ref, f32[4,128,128]{2,1,0:T(8,128)S(1)} %copy-done, f32[1,512]{1,0:T(1,128)S(1)} %bitcast.5, ...), custom_call_target="tpu_custom_call" | custom-call | flops 1610612736 | bytes 6291456 | tf_op jit(solution)/shard_map/attend_and_project/pallas_call | solution.py:297
  46.8 0.6 collective-permute-start.28
  47.3 1.5 %collective-permute-start.24 = (bf16[32,3072]{1,0:T(8,128)(2,1)S(1)}, bf16[32,3072]{1,0:T(8,128)(2,1)S(1)}, u32[]{:S(2)}, u32[]{:S(2)}) collective-permute-start(bf16[32,3072]{1,0:T(8,128)(2,1)S(1)} %get-tuple-element.68), channel_id=1, source_target_pairs={{2,0},{4,2},{6,4},{7,6},{5,7},{3,5},{1,3},{0,1},{10,8},{12,10},{14... | collective-permute-start | bytes 589832 | tf_op jit(solution)/shard_map/ppermute | solution.py:385
  48.8 1.6 %project_rest.1 = (bf16[32,3072]{1,0:T(8,128)(2,1)S(1)}, bf16[32,3072]{1,0:T(8,128)(2,1)S(1)}, bf16[32,3072]{1,0:T(8,128)(2,1)S(1)}, bf16[32,3072]{1,0:T(8,128)(...) custom-call(bf16[256,512]{1,0:T(8,128)(2,1)S(1)} %get-tuple-element., ...), custom_call_target="tpu_custom_call" | custom-call | flops 5000000000 | bytes 6291456 | tf_op jit(solution)/shard_map/project_rest/pallas_call | solution.py:316
  50.5 1.6 %collective-permute-start.21 = (bf16[32,3072]{1,0:T(8,128)(2,1)S(1)}, bf16[32,3072]{1,0:T(8,128)(2,1)S(1)}, u32[]{:S(2)}, u32[]{:S(2)}) collective-permute-start(bf16[32,3072]{1,0:T(8,128)(2,1)S(1)} %get-tuple-element.64), channel_id=1, source_target_pairs={{2,0},{4,2},{6,4},{7,6},{5,7},{3,5},{1,3},{0,1},{10,8},{12,10},{14... | collective-permute-start | bytes 589832 | tf_op jit(solution)/shard_map/ppermute | solution.py:385
  53.1 0.6 collective-permute-start.29
  53.7 0.9 %collective-permute-done.24.got_ref = bf16[32,3072]{1,0:T(8,128)(2,1)S(1)} collective-permute-done((bf16[32,3072]{1,0:T(8,128)(2,1)S(1)}, bf16[32,3072]{1,0:T(8,128)(2,1)S(1)}, u32[]{:S(2)}, u32[]{:S(2)}) %collective-permute-start.24) | collective-permute-done | bytes 196640 | tf_op jit(solution)/shard_map/ppermute | solution.py:385
  54.6 1.4 %collective-permute-start.25 = (bf16[32,3072]{1,0:T(8,128)(2,1)S(1)}, bf16[32,3072]{1,0:T(8,128)(2,1)S(1)}, u32[]{:S(2)}, u32[]{:S(2)}) collective-permute-start(bf16[32,3072]{1,0:T(8,128)(2,1)S(1)} %add_step.14), channel_id=1, source_target_pairs={{2,0},{4,2},{6,4},{7,6},{5,7},{3,5},{1,3},{0,1},{10,8},{12,10},{14... | collective-permute-start | bytes 589832 | tf_op jit(solution)/shard_map/ppermute | solution.py:385
  56.1 2.7 %collective-permute-done.21.got_ref = bf16[32,3072]{1,0:T(8,128)(2,1)S(1)} collective-permute-done((bf16[32,3072]{1,0:T(8,128)(2,1)S(1)}, bf16[32,3072]{1,0:T(8,128)(2,1)S(1)}, u32[]{:S(2)}, u32[]{:S(2)}) %collective-permute-start.21) | collective-permute-done | bytes 196640 | tf_op jit(solution)/shard_map/ppermute | solution.py:385
  58.8 1.4 %collective-permute-start.22 = (bf16[32,3072]{1,0:T(8,128)(2,1)S(1)}, bf16[32,3072]{1,0:T(8,128)(2,1)S(1)}, u32[]{:S(2)}, u32[]{:S(2)}) collective-permute-start(bf16[32,3072]{1,0:T(8,128)(2,1)S(1)} %add_step.12), channel_id=1, source_target_pairs={{2,0},{4,2},{6,4},{7,6},{5,7},{3,5},{1,3},{0,1},{10,8},{12,10},{14... | collective-permute-start | bytes 589832 | tf_op jit(solution)/shard_map/ppermute | solution.py:385
  60.3 0.8 %collective-permute-start.19 = (bf16[32,3072]{1,0:T(8,128)(2,1)S(1)}, bf16[32,3072]{1,0:T(8,128)(2,1)S(1)}, u32[]{:S(2)}, u32[]{:S(2)}) collective-permute-start(bf16[32,3072]{1,0:T(8,128)(2,1)S(1)} %add_step.10), channel_id=1, source_target_pairs={{0,2},{2,4},{4,6},{6,7},{7,5},{5,3},{3,1},{1,0},{8,10},{10,12},{12... | collective-permute-start | bytes 589832 | tf_op jit(solution)/shard_map/ppermute | solution.py:385
  61.2 1.7 %collective-permute-done.29.got_ref = bf16[32,3072]{1,0:T(8,128)(2,1)S(1)} collective-permute-done((bf16[32,3072]{1,0:T(8,128)(2,1)S(1)}, bf16[32,3072]{1,0:T(8,128)(2,1)S(1)}, u32[]{:S(2)}, u32[]{:S(2)}) %collective-permute-start.29) | collective-permute-done | bytes 196640 | tf_op jit(solution)/shard_map/ppermute | solution.py:385
  63.0 0.5 collective-permute-start.30
  63.5 1.6 %collective-permute-start.26 = (bf16[32,3072]{1,0:T(8,128)(2,1)S(1)}, bf16[32,3072]{1,0:T(8,128)(2,1)S(1)}, u32[]{:S(2)}, u32[]{:S(2)}) collective-permute-start(bf16[32,3072]{1,0:T(8,128)(2,1)S(1)} %add_step.15), channel_id=1, source_target_pairs={{2,0},{4,2},{6,4},{7,6},{5,7},{3,5},{1,3},{0,1},{10,8},{12,10},{14... | collective-permute-start | bytes 589832 | tf_op jit(solution)/shard_map/ppermute | solution.py:385
  65.2 2.1 %collective-permute-done.22.got_ref = bf16[32,3072]{1,0:T(8,128)(2,1)S(1)} collective-permute-done((bf16[32,3072]{1,0:T(8,128)(2,1)S(1)}, bf16[32,3072]{1,0:T(8,128)(2,1)S(1)}, u32[]{:S(2)}, u32[]{:S(2)}) %collective-permute-start.22) | collective-permute-done | bytes 196640 | tf_op jit(solution)/shard_map/ppermute | solution.py:385
  67.3 1.4 %collective-permute-start.23 = (bf16[32,3072]{1,0:T(8,128)(2,1)S(1)}, bf16[32,3072]{1,0:T(8,128)(2,1)S(1)}, u32[]{:S(2)}, u32[]{:S(2)}) collective-permute-start(bf16[32,3072]{1,0:T(8,128)(2,1)S(1)} %add_step.13), channel_id=1, source_target_pairs={{2,0},{4,2},{6,4},{7,6},{5,7},{3,5},{1,3},{0,1},{10,8},{12,10},{14... | collective-permute-start | bytes 589832 | tf_op jit(solution)/shard_map/ppermute | solution.py:385
  68.8 0.8 %collective-permute-start.20 = (bf16[32,3072]{1,0:T(8,128)(2,1)S(1)}, bf16[32,3072]{1,0:T(8,128)(2,1)S(1)}, u32[]{:S(2)}, u32[]{:S(2)}) collective-permute-start(bf16[32,3072]{1,0:T(8,128)(2,1)S(1)} %add_step.11), channel_id=1, source_target_pairs={{0,2},{2,4},{4,6},{6,7},{7,5},{5,3},{3,1},{1,0},{8,10},{10,12},{12... | collective-permute-start | bytes 589832 | tf_op jit(solution)/shard_map/ppermute | solution.py:385
  69.6 1.7 %collective-permute-done.30.got_ref = bf16[32,3072]{1,0:T(8,128)(2,1)S(1)} collective-permute-done((bf16[32,3072]{1,0:T(8,128)(2,1)S(1)}, bf16[32,3072]{1,0:T(8,128)(2,1)S(1)}, u32[]{:S(2)}, u32[]{:S(2)}) %collective-permute-start.30) | collective-permute-done | bytes 196640 | tf_op jit(solution)/shard_map/ppermute | solution.py:385
  71.4 0.5 collective-permute-start.31
  72.0 1.6 %collective-permute-start.27 = (bf16[32,3072]{1,0:T(8,128)(2,1)S(1)}, bf16[32,3072]{1,0:T(8,128)(2,1)S(1)}, u32[]{:S(2)}, u32[]{:S(2)}) collective-permute-start(bf16[32,3072]{1,0:T(8,128)(2,1)S(1)} %add_step.16), channel_id=1, source_target_pairs={{2,0},{4,2},{6,4},{7,6},{5,7},{3,5},{1,3},{0,1},{10,8},{12,10},{14... | collective-permute-start | bytes 589832 | tf_op jit(solution)/shard_map/ppermute | solution.py:385
  73.6 2.1 %collective-permute-done.23.got_second = bf16[32,3072]{1,0:T(8,128)(2,1)S(1)} collective-permute-done((bf16[32,3072]{1,0:T(8,128)(2,1)S(1)}, bf16[32,3072]{1,0:T(8,128)(2,1)S(1)}, u32[]{:S(2)}, u32[]{:S(2)}) %collective-permute-start.23) | collective-permute-done | bytes 196640 | tf_op jit(solution)/shard_map/ppermute | solution.py:385
  75.6 0.8 %collective-permute-done.20.got_first = bf16[32,3072]{1,0:T(8,128)(2,1)S(1)} collective-permute-done((bf16[32,3072]{1,0:T(8,128)(2,1)S(1)}, bf16[32,3072]{1,0:T(8,128)(2,1)S(1)}, u32[]{:S(2)}, u32[]{:S(2)}) %collective-permute-start.20) | collective-permute-done | bytes 196640 | tf_op jit(solution)/shard_map/ppermute | solution.py:385
  76.5 2.0 %collective-permute-done.31.second = bf16[32,3072]{1,0:T(8,128)(2,1)S(1)} collective-permute-done((bf16[32,3072]{1,0:T(8,128)(2,1)S(1)}, bf16[32,3072]{1,0:T(8,128)(2,1)S(1)}, u32[]{:S(2)}, u32[]{:S(2)}) %collective-permute-start.31) | collective-permute-done | bytes 196640 | tf_op jit(solution)/shard_map/ppermute | solution.py:385
  78.6 0.8 %finish.1 = bf16[32,6144]{1,0:T(8,128)(2,1)} custom-call(f32[2,32,3072]{2,1,0:T(8,128)S(1)} %add_own.1.gathered_ref, bf16[32,3072]{1,0:T(8,128)(2,1)S(1)} %collective-permute-done.27.first, bf16[32,3072]{1,0:T(8,128)(2,1)S(1)} %collective-permute-done.31.second), custom_call_target="tpu_custom_call" | custom-call | bytes 393216 | tf_op jit(solution)/shard_map/finish/pallas_call | solution.py:367
  (62 shorter events, 2.7 us)
Async XLA Ops:
  1.1 8.8 %collective-permute-start.10 = (bf16[32,3072]{1,0:T(8,128)(2,1)S(1)}, bf16[32,3072]{1,0:T(8,128)(2,1)S(1)}, u32[]{:S(2)}, u32[]{:S(2)}) collective-permute-start(bf16[32,3072]{1,0:T(8,128)(2,1)S(1)} %get-tuple-element.73.refs_5_), channel_id=1, source_target_pairs={{2,0},{4,2},{6,4},{7,6},{5,7},{3,5},{1,3},{0,1},{10,8},{12,10},{14... | collective-permute-start | bytes 589832 | tf_op jit(solution)/shard_map/ppermute | solution.py:74
  4.0 7.8 %collective-permute-start = (bf16[32,3072]{1,0:T(8,128)(2,1)S(1)}, bf16[32,3072]{1,0:T(8,128)(2,1)S(1)}, u32[]{:S(2)}, u32[]{:S(2)}) collective-permute-start(bf16[32,3072]{1,0:T(8,128)(2,1)S(1)} %get-tuple-element.74.refs_0_), channel_id=1, source_target_pairs={{0,2},{2,4},{4,6},{6,7},{7,5},{5,3},{3,1},{1,0},{8,10},{10,12},{12... | collective-permute-start | bytes 589832 | tf_op jit(solution)/shard_map/ppermute | solution.py:73
  4.2 9.9 %collective-permute-start.4 = (bf16[32,3072]{1,0:T(8,128)(2,1)S(1)}, bf16[32,3072]{1,0:T(8,128)(2,1)S(1)}, u32[]{:S(2)}, u32[]{:S(2)}) collective-permute-start(bf16[32,3072]{1,0:T(8,128)(2,1)S(1)} %get-tuple-element.74.refs_0_), channel_id=1, source_target_pairs={{2,0},{4,2},{6,4},{7,6},{5,7},{3,5},{1,3},{0,1},{10,8},{12,10},{14... | collective-permute-start | bytes 589832 | tf_op jit(solution)/shard_map/ppermute | solution.py:74
  6.1 10.0 %collective-permute-start.7 = (bf16[32,3072]{1,0:T(8,128)(2,1)S(1)}, bf16[32,3072]{1,0:T(8,128)(2,1)S(1)}, u32[]{:S(2)}, u32[]{:S(2)}) collective-permute-start(bf16[32,3072]{1,0:T(8,128)(2,1)S(1)} %get-tuple-element.73.refs_5_), channel_id=1, source_target_pairs={{0,2},{2,4},{4,6},{6,7},{7,5},{5,3},{3,1},{1,0},{8,10},{10,12},{12... | collective-permute-start | bytes 589832 | tf_op jit(solution)/shard_map/ppermute | solution.py:73
  9.9 8.4 %collective-permute-start.11 = (bf16[32,3072]{1,0:T(8,128)(2,1)S(1)}, bf16[32,3072]{1,0:T(8,128)(2,1)S(1)}, u32[]{:S(2)}, u32[]{:S(2)}) collective-permute-start(bf16[32,3072]{1,0:T(8,128)(2,1)S(1)} %collective-permute-done.10.refs_7_.arrived_ref), channel_id=1, source_target_pairs={{2,0},{4,2},{6,4},{7,6},{5,7},{3,5},{1,3},{0,1},{10,8},{12,10},{14... | collective-permute-start | bytes 589832 | tf_op jit(solution)/shard_map/ppermute | solution.py:74
  11.9 8.4 %collective-permute-start.1 = (bf16[32,3072]{1,0:T(8,128)(2,1)S(1)}, bf16[32,3072]{1,0:T(8,128)(2,1)S(1)}, u32[]{:S(2)}, u32[]{:S(2)}) collective-permute-start(bf16[32,3072]{1,0:T(8,128)(2,1)S(1)} %collective-permute-done.refs_1_.arrived_ref), channel_id=1, source_target_pairs={{0,2},{2,4},{4,6},{6,7},{7,5},{5,3},{3,1},{1,0},{8,10},{10,12},{12... | collective-permute-start | bytes 589832 | tf_op jit(solution)/shard_map/ppermute | solution.py:73
  14.1 8.4 %collective-permute-start.5 = (bf16[32,3072]{1,0:T(8,128)(2,1)S(1)}, bf16[32,3072]{1,0:T(8,128)(2,1)S(1)}, u32[]{:S(2)}, u32[]{:S(2)}) collective-permute-start(bf16[32,3072]{1,0:T(8,128)(2,1)S(1)} %collective-permute-done.4.refs_2_), channel_id=1, source_target_pairs={{2,0},{4,2},{6,4},{7,6},{5,7},{3,5},{1,3},{0,1},{10,8},{12,10},{14... | collective-permute-start | bytes 589832 | tf_op jit(solution)/shard_map/ppermute | solution.py:74
  16.1 8.4 %collective-permute-start.8 = (bf16[32,3072]{1,0:T(8,128)(2,1)S(1)}, bf16[32,3072]{1,0:T(8,128)(2,1)S(1)}, u32[]{:S(2)}, u32[]{:S(2)}) collective-permute-start(bf16[32,3072]{1,0:T(8,128)(2,1)S(1)} %collective-permute-done.7.refs_6_), channel_id=1, source_target_pairs={{0,2},{2,4},{4,6},{6,7},{7,5},{5,3},{3,1},{1,0},{8,10},{10,12},{12... | collective-permute-start | bytes 589832 | tf_op jit(solution)/shard_map/ppermute | solution.py:73
  16.2 14.6 %slice-start = ((s8[18874368]{0:T(1024)(128)(4,1)}), s8[4194304]{0:T(1024)(128)(4,1)S(1)}, s32[]{:S(2)}) async-start(s8[18874368]{0:T(1024)(128)(4,1)} %bitcast.1), calls=%async_computation | async-start | bytes 8388608
  16.2 14.6 %slice-start.1 = ((s8[18874368]{0:T(1024)(128)(4,1)}), s8[4194304]{0:T(1024)(128)(4,1)S(1)}, s32[]{:S(2)}) async-start(s8[18874368]{0:T(1024)(128)(4,1)} %bitcast.1), calls=%async_computation.1 | async-start | bytes 8388608
  16.2 14.6 %slice-start.2 = ((s8[18874368]{0:T(1024)(128)(4,1)}), s8[4194304]{0:T(1024)(128)(4,1)S(1)}, s32[]{:S(2)}) async-start(s8[18874368]{0:T(1024)(128)(4,1)} %bitcast.1), calls=%async_computation.2 | async-start | bytes 8388608
  16.2 14.6 %slice-start.3 = ((s8[18874368]{0:T(1024)(128)(4,1)}), s8[4194304]{0:T(1024)(128)(4,1)S(1)}, s32[]{:S(2)}) async-start(s8[18874368]{0:T(1024)(128)(4,1)} %bitcast.1), calls=%async_computation.3 | async-start | bytes 8388608
  16.2 14.5 %slice-start.4 = ((s8[18874368]{0:T(1024)(128)(4,1)}), s8[2097152]{0:T(1024)(128)(4,1)S(1)}, s32[]{:S(2)}) async-start(s8[18874368]{0:T(1024)(128)(4,1)} %bitcast.1), calls=%async_computation.4 | async-start | bytes 4194304
  18.3 10.6 %collective-permute-start.12 = (bf16[32,3072]{1,0:T(8,128)(2,1)S(1)}, bf16[32,3072]{1,0:T(8,128)(2,1)S(1)}, u32[]{:S(2)}, u32[]{:S(2)}) collective-permute-start(bf16[32,3072]{1,0:T(8,128)(2,1)S(1)} %collective-permute-done.11.refs_9_), channel_id=1, source_target_pairs={{2,0},{4,2},{6,4},{7,6},{5,7},{3,5},{1,3},{0,1},{10,8},{12,10},{14... | collective-permute-start | bytes 589832 | tf_op jit(solution)/shard_map/ppermute | solution.py:74
  20.3 8.4 %collective-permute-start.2 = (bf16[32,3072]{1,0:T(8,128)(2,1)S(1)}, bf16[32,3072]{1,0:T(8,128)(2,1)S(1)}, u32[]{:S(2)}, u32[]{:S(2)}) collective-permute-start(bf16[32,3072]{1,0:T(8,128)(2,1)S(1)} %collective-permute-done.1.refs_3_), channel_id=1, source_target_pairs={{0,2},{2,4},{4,6},{6,7},{7,5},{5,3},{3,1},{1,0},{8,10},{10,12},{12... | collective-permute-start | bytes 589832 | tf_op jit(solution)/shard_map/ppermute | solution.py:73
  22.5 10.7 %collective-permute-start.6 = (bf16[32,3072]{1,0:T(8,128)(2,1)S(1)}, bf16[32,3072]{1,0:T(8,128)(2,1)S(1)}, u32[]{:S(2)}, u32[]{:S(2)}) collective-permute-start(bf16[32,3072]{1,0:T(8,128)(2,1)S(1)} %collective-permute-done.5.refs_4_), channel_id=1, source_target_pairs={{2,0},{4,2},{6,4},{7,6},{5,7},{3,5},{1,3},{0,1},{10,8},{12,10},{14... | collective-permute-start | bytes 589832 | tf_op jit(solution)/shard_map/ppermute | solution.py:74
  24.5 8.7 %collective-permute-start.9 = (bf16[32,3072]{1,0:T(8,128)(2,1)S(1)}, bf16[32,3072]{1,0:T(8,128)(2,1)S(1)}, u32[]{:S(2)}, u32[]{:S(2)}) collective-permute-start(bf16[32,3072]{1,0:T(8,128)(2,1)S(1)} %collective-permute-done.8.refs_8_), channel_id=1, source_target_pairs={{0,2},{2,4},{4,6},{6,7},{7,5},{5,3},{3,1},{1,0},{8,10},{10,12},{12... | collective-permute-start | bytes 589832 | tf_op jit(solution)/shard_map/ppermute | solution.py:73
  28.7 7.0 %collective-permute-start.3 = (bf16[32,3072]{1,0:T(8,128)(2,1)S(1)}, bf16[32,3072]{1,0:T(8,128)(2,1)S(1)}, u32[]{:S(2)}, u32[]{:S(2)}) collective-permute-start(bf16[32,3072]{1,0:T(8,128)(2,1)S(1)} %collective-permute-done.2.refs_0_), channel_id=1, source_target_pairs={{0,2},{2,4},{4,6},{6,7},{7,5},{5,3},{3,1},{1,0},{8,10},{10,12},{12... | collective-permute-start | bytes 589832 | tf_op jit(solution)/shard_map/ppermute | solution.py:77
  28.8 8.0 %collective-permute-start.13 = (bf16[32,3072]{1,0:T(8,128)(2,1)S(1)}, bf16[32,3072]{1,0:T(8,128)(2,1)S(1)}, u32[]{:S(2)}, u32[]{:S(2)}) collective-permute-start(bf16[32,3072]{1,0:T(8,128)(2,1)S(1)} %collective-permute-done.12.refs_11_.refs_3_), channel_id=1, source_target_pairs={{2,0},{4,2},{6,4},{7,6},{5,7},{3,5},{1,3},{0,1},{10,8},{12,10},{14... | collective-permute-start | bytes 589832 | tf_op jit(solution)/shard_map/ppermute | solution.py:78
  37.7 1.5 %collective-permute-start.14 = (bf16[2,128,128]{2,1,0:T(8,128)(2,1)S(1)}, bf16[2,128,128]{2,1,0:T(8,128)(2,1)S(1)}, u32[]{:S(2)}, u32[]{:S(2)}) collective-permute-start(bf16[2,128,128]{2,1,0:T(8,128)(2,1)S(1)} %get-tuple-element.54.one_ref), channel_id=1, source_target_pairs={{0,8},{8,0},{16,24},{24,16},{1,9},{9,1},{17,25},{25,17},{2,10},{10... | collective-permute-start | bytes 196616 | tf_op jit(solution)/shard_map/ppermute | solution.py:421
  38.7 2.2 %collective-permute-start.16 = (bf16[2,128,128]{2,1,0:T(8,128)(2,1)S(1)}, bf16[2,128,128]{2,1,0:T(8,128)(2,1)S(1)}, u32[]{:S(2)}, u32[]{:S(2)}) collective-permute-start(bf16[2,128,128]{2,1,0:T(8,128)(2,1)S(1)} %get-tuple-element.55.one_ref), channel_id=1, source_target_pairs={{0,8},{8,0},{16,24},{24,16},{1,9},{9,1},{17,25},{25,17},{2,10},{10... | collective-permute-start | bytes 196616 | tf_op jit(solution)/shard_map/ppermute | solution.py:421
  39.2 5.9 %collective-permute-start.15 = (bf16[2,128,128]{2,1,0:T(8,128)(2,1)S(1)}, bf16[2,128,128]{2,1,0:T(8,128)(2,1)S(1)}, u32[]{:S(2)}, u32[]{:S(2)}) collective-permute-start(bf16[2,128,128]{2,1,0:T(8,128)(2,1)S(1)} %add_states.2.refs_0_), channel_id=1, source_target_pairs={{0,16},{8,24},{16,0},{24,8},{1,17},{9,25},{17,1},{25,9},{2,18},{10... | collective-permute-start | bytes 196616 | tf_op jit(solution)/shard_map/ppermute | solution.py:421
  40.8 4.3 %collective-permute-start.17 = (bf16[2,128,128]{2,1,0:T(8,128)(2,1)S(1)}, bf16[2,128,128]{2,1,0:T(8,128)(2,1)S(1)}, u32[]{:S(2)}, u32[]{:S(2)}) collective-permute-start(bf16[2,128,128]{2,1,0:T(8,128)(2,1)S(1)} %add_states.3), channel_id=1, source_target_pairs={{0,16},{8,24},{16,0},{24,8},{1,17},{9,25},{17,1},{25,9},{2,18},{10... | collective-permute-start | bytes 196616 | tf_op jit(solution)/shard_map/ppermute | solution.py:421
  41.7 3.5 %slice-start.5 = ((s8[6291456]{0:T(1024)(128)(4,1)}), s8[4194304]{0:T(1024)(128)(4,1)S(1)}, s32[]{:S(2)}) async-start(s8[6291456]{0:T(1024)(128)(4,1)} %bitcast.3), calls=%async_computation.5 | async-start | bytes 8388608
  41.7 3.5 %slice-start.6 = ((s8[6291456]{0:T(1024)(128)(4,1)}), s8[2097152]{0:T(1024)(128)(4,1)S(1)}, s32[]{:S(2)}) async-start(s8[6291456]{0:T(1024)(128)(4,1)} %bitcast.3), calls=%async_computation.6 | async-start | bytes 4194304
  41.7 3.5 %copy-start = (f32[4,128,128]{2,1,0:T(8,128)S(1)}, f32[4,128,128]{2,1,0:T(8,128)}, u32[]{:S(2)}) copy-start(f32[4,128,128]{2,1,0:T(8,128)} %initial_ref.1) | copy-start | bytes 786436
  41.7 3.5 %copy-start.1 = (f32[512]{0:T(512)S(1)}, f32[512]{0:T(512)}, u32[]{:S(2)}) copy-start(f32[512]{0:T(512)} %param.8) | copy-start | bytes 6148
  46.8 6.3 %collective-permute-start.28 = (bf16[32,3072]{1,0:T(8,128)(2,1)S(1)}, bf16[32,3072]{1,0:T(8,128)(2,1)S(1)}, u32[]{:S(2)}, u32[]{:S(2)}) collective-permute-start(bf16[32,3072]{1,0:T(8,128)(2,1)S(1)} %get-tuple-element.72), channel_id=1, source_target_pairs={{0,2},{2,4},{4,6},{6,7},{7,5},{5,3},{3,1},{1,0},{8,10},{10,12},{12... | collective-permute-start | bytes 589832 | tf_op jit(solution)/shard_map/ppermute | solution.py:385
  47.3 7.3 %collective-permute-start.24 = (bf16[32,3072]{1,0:T(8,128)(2,1)S(1)}, bf16[32,3072]{1,0:T(8,128)(2,1)S(1)}, u32[]{:S(2)}, u32[]{:S(2)}) collective-permute-start(bf16[32,3072]{1,0:T(8,128)(2,1)S(1)} %get-tuple-element.68), channel_id=1, source_target_pairs={{2,0},{4,2},{6,4},{7,6},{5,7},{3,5},{1,3},{0,1},{10,8},{12,10},{14... | collective-permute-start | bytes 589832 | tf_op jit(solution)/shard_map/ppermute | solution.py:385
  50.5 8.3 %collective-permute-start.21 = (bf16[32,3072]{1,0:T(8,128)(2,1)S(1)}, bf16[32,3072]{1,0:T(8,128)(2,1)S(1)}, u32[]{:S(2)}, u32[]{:S(2)}) collective-permute-start(bf16[32,3072]{1,0:T(8,128)(2,1)S(1)} %get-tuple-element.64), channel_id=1, source_target_pairs={{2,0},{4,2},{6,4},{7,6},{5,7},{3,5},{1,3},{0,1},{10,8},{12,10},{14... | collective-permute-start | bytes 589832 | tf_op jit(solution)/shard_map/ppermute | solution.py:385
  52.1 8.2 %collective-permute-start.18 = (bf16[32,3072]{1,0:T(8,128)(2,1)S(1)}, bf16[32,3072]{1,0:T(8,128)(2,1)S(1)}, u32[]{:S(2)}, u32[]{:S(2)}) collective-permute-start(bf16[32,3072]{1,0:T(8,128)(2,1)S(1)} %get-tuple-element.61), channel_id=1, source_target_pairs={{0,2},{2,4},{4,6},{6,7},{7,5},{5,3},{3,1},{1,0},{8,10},{10,12},{12... | collective-permute-start | bytes 589832 | tf_op jit(solution)/shard_map/ppermute | solution.py:385
  53.1 9.8 %collective-permute-start.29 = (bf16[32,3072]{1,0:T(8,128)(2,1)S(1)}, bf16[32,3072]{1,0:T(8,128)(2,1)S(1)}, u32[]{:S(2)}, u32[]{:S(2)}) collective-permute-start(bf16[32,3072]{1,0:T(8,128)(2,1)S(1)} %add_step.17), channel_id=1, source_target_pairs={{0,2},{2,4},{4,6},{6,7},{7,5},{5,3},{3,1},{1,0},{8,10},{10,12},{12... | collective-permute-start | bytes 589832 | tf_op jit(solution)/shard_map/ppermute | solution.py:385
  54.6 8.9 %collective-permute-start.25 = (bf16[32,3072]{1,0:T(8,128)(2,1)S(1)}, bf16[32,3072]{1,0:T(8,128)(2,1)S(1)}, u32[]{:S(2)}, u32[]{:S(2)}) collective-permute-start(bf16[32,3072]{1,0:T(8,128)(2,1)S(1)} %add_step.14), channel_id=1, source_target_pairs={{2,0},{4,2},{6,4},{7,6},{5,7},{3,5},{1,3},{0,1},{10,8},{12,10},{14... | collective-permute-start | bytes 589832 | tf_op jit(solution)/shard_map/ppermute | solution.py:385
  58.8 8.4 %collective-permute-start.22 = (bf16[32,3072]{1,0:T(8,128)(2,1)S(1)}, bf16[32,3072]{1,0:T(8,128)(2,1)S(1)}, u32[]{:S(2)}, u32[]{:S(2)}) collective-permute-start(bf16[32,3072]{1,0:T(8,128)(2,1)S(1)} %add_step.12), channel_id=1, source_target_pairs={{2,0},{4,2},{6,4},{7,6},{5,7},{3,5},{1,3},{0,1},{10,8},{12,10},{14... | collective-permute-start | bytes 589832 | tf_op jit(solution)/shard_map/ppermute | solution.py:385
  60.3 8.4 %collective-permute-start.19 = (bf16[32,3072]{1,0:T(8,128)(2,1)S(1)}, bf16[32,3072]{1,0:T(8,128)(2,1)S(1)}, u32[]{:S(2)}, u32[]{:S(2)}) collective-permute-start(bf16[32,3072]{1,0:T(8,128)(2,1)S(1)} %add_step.10), channel_id=1, source_target_pairs={{0,2},{2,4},{4,6},{6,7},{7,5},{5,3},{3,1},{1,0},{8,10},{10,12},{12... | collective-permute-start | bytes 589832 | tf_op jit(solution)/shard_map/ppermute | solution.py:385
  63.0 8.4 %collective-permute-start.30 = (bf16[32,3072]{1,0:T(8,128)(2,1)S(1)}, bf16[32,3072]{1,0:T(8,128)(2,1)S(1)}, u32[]{:S(2)}, u32[]{:S(2)}) collective-permute-start(bf16[32,3072]{1,0:T(8,128)(2,1)S(1)} %add_step.18), channel_id=1, source_target_pairs={{0,2},{2,4},{4,6},{6,7},{7,5},{5,3},{3,1},{1,0},{8,10},{10,12},{12... | collective-permute-start | bytes 589832 | tf_op jit(solution)/shard_map/ppermute | solution.py:385
  63.5 8.4 %collective-permute-start.26 = (bf16[32,3072]{1,0:T(8,128)(2,1)S(1)}, bf16[32,3072]{1,0:T(8,128)(2,1)S(1)}, u32[]{:S(2)}, u32[]{:S(2)}) collective-permute-start(bf16[32,3072]{1,0:T(8,128)(2,1)S(1)} %add_step.15), channel_id=1, source_target_pairs={{2,0},{4,2},{6,4},{7,6},{5,7},{3,5},{1,3},{0,1},{10,8},{12,10},{14... | collective-permute-start | bytes 589832 | tf_op jit(solution)/shard_map/ppermute | solution.py:385
  67.3 8.4 %collective-permute-start.23 = (bf16[32,3072]{1,0:T(8,128)(2,1)S(1)}, bf16[32,3072]{1,0:T(8,128)(2,1)S(1)}, u32[]{:S(2)}, u32[]{:S(2)}) collective-permute-start(bf16[32,3072]{1,0:T(8,128)(2,1)S(1)} %add_step.13), channel_id=1, source_target_pairs={{2,0},{4,2},{6,4},{7,6},{5,7},{3,5},{1,3},{0,1},{10,8},{12,10},{14... | collective-permute-start | bytes 589832 | tf_op jit(solution)/shard_map/ppermute | solution.py:385
  68.8 7.7 %collective-permute-start.20 = (bf16[32,3072]{1,0:T(8,128)(2,1)S(1)}, bf16[32,3072]{1,0:T(8,128)(2,1)S(1)}, u32[]{:S(2)}, u32[]{:S(2)}) collective-permute-start(bf16[32,3072]{1,0:T(8,128)(2,1)S(1)} %add_step.11), channel_id=1, source_target_pairs={{0,2},{2,4},{4,6},{6,7},{7,5},{5,3},{3,1},{1,0},{8,10},{10,12},{12... | collective-permute-start | bytes 589832 | tf_op jit(solution)/shard_map/ppermute | solution.py:385
  71.4 7.2 %collective-permute-start.31 = (bf16[32,3072]{1,0:T(8,128)(2,1)S(1)}, bf16[32,3072]{1,0:T(8,128)(2,1)S(1)}, u32[]{:S(2)}, u32[]{:S(2)}) collective-permute-start(bf16[32,3072]{1,0:T(8,128)(2,1)S(1)} %add_step.19), channel_id=1, source_target_pairs={{0,2},{2,4},{4,6},{6,7},{7,5},{5,3},{3,1},{1,0},{8,10},{10,12},{12... | collective-permute-start | bytes 589832 | tf_op jit(solution)/shard_map/ppermute | solution.py:385
  72.0 6.6 %collective-permute-start.27 = (bf16[32,3072]{1,0:T(8,128)(2,1)S(1)}, bf16[32,3072]{1,0:T(8,128)(2,1)S(1)}, u32[]{:S(2)}, u32[]{:S(2)}) collective-permute-start(bf16[32,3072]{1,0:T(8,128)(2,1)S(1)} %add_step.16), channel_id=1, source_target_pairs={{2,0},{4,2},{6,4},{7,6},{5,7},{3,5},{1,3},{0,1},{10,8},{12,10},{14... | collective-permute-start | bytes 589832 | tf_op jit(solution)/shard_map/ppermute | solution.py:385

commit v16 on v15

--- a/solution.py
+++ b/solution.py
@@ -462,8 +462,7 @@
     )
     parts = project_rest(normalized, out_weight, n_fsdp - soon, rows) + parts
 
-    mirrored = [distance if distance == n_fsdp // 2 else -distance for distance in order]
-    return ring_scatter(parts, mirrored, left, right)
+    return ring_scatter(parts, order, right, left)
 
 
 def solution(mesh):

time: 79.5 us -> 80.6 us (1.014)
  waiting for transfers between devices: 32.2 us -> 33.4 us
    ppermute x7, starting transfers between devices: 10.7 us -> 3.59 us  [hop(): lax.ppermute(to_right, 'fsdp', right)]
    ppermute x7, starting transfers between devices: 4.29 us -> 11.3 us  [hop(): lax.ppermute(to_left, 'fsdp', left)]
    ppermute x7, waiting for transfers between devices: 7.75 us -> 12.7 us  [hop(): lax.ppermute(to_right, 'fsdp', right)]
    ppermute x7, waiting for transfers between devices: 6.8 us -> 3.04 us  [hop(): lax.ppermute(to_left, 'fsdp', left)]
where the time goes in v16:
time: 80.6 us; the launch traced here: 80.4 us
  starting transfers between devices  33.5 us (42%)
  waiting for transfers between devices  33.4 us (41%)
  Pallas kernels  12.2 us (15%)
  local copies, waits for them, and re-layouts  1.09 us (1%)
    ppermute x6, starting transfers between devices, ring_gather(): going_left[1 - part] = lax.ppermute(going_left[1 - part], 'fsdp', left)  12.8 us
    ppermute x7, waiting for transfers between devices, hop(): lax.ppermute(to_right, 'fsdp', right)  12.7 us
    ppermute x7, starting transfers between devices, hop(): lax.ppermute(to_left, 'fsdp', left)  11.3 us
    ppermute x6, waiting for transfers between devices, ring_gather(): going_left[1 - part] = lax.ppermute(going_left[1 - part], 'fsdp', left)  9.87 us
    ppermute x6, waiting for transfers between devices, ring_gather(): going_right[part] = lax.ppermute(going_right[part], 'fsdp', right)  4.25 us
    ppermute x7, starting transfers between devices, hop(): lax.ppermute(to_right, 'fsdp', right)  3.59 us
    ppermute x4, starting transfers between devices, exchange_states(): received[at].append(lax.ppermute(total, 'ctx', pairs))  3.09 us
    ppermute x7, waiting for transfers between devices, hop(): lax.ppermute(to_left, 'fsdp', left)  3.04 us
  transfers between devices with their start and end apart: 32, of which 16 were waited for; matrix products, arithmetic and copies ran while one was open for 0% of the time, Pallas kernels for 11%

profile of v16, /device:TPU:0, one launch (start us, length us, event | category | flops | bytes accessed | tf_op | source)
XLA Modules:
  0.0 80.4 jit_solution(17406854588143465180)
XLA Ops:
  0.0 1.0 %fusion = (bf16[32,3072]{1,0:T(8,128)(2,1)S(1)}, bf16[32,3072]{1,0:T(8,128)(2,1)S(1)}) fusion(bf16[32,6144]{1,0:T(8,128)(2,1)} %param.5), kind=kLoop, calls=%fused_computation | loop fusion | bytes 786432 | tf_op jit(solution)/shard_map/slice | solution.py:68
  1.1 3.0 %collective-permute-start.10 = (bf16[32,3072]{1,0:T(8,128)(2,1)S(1)}, bf16[32,3072]{1,0:T(8,128)(2,1)S(1)}, u32[]{:S(2)}, u32[]{:S(2)}) collective-permute-start(bf16[32,3072]{1,0:T(8,128)(2,1)S(1)} %get-tuple-element.73.refs_5_), channel_id=1, source_target_pairs={{2,0},{4,2},{6,4},{7,6},{5,7},{3,5},{1,3},{0,1},{10,8},{12,10},{14... | collective-permute-start | bytes 589832 | tf_op jit(solution)/shard_map/ppermute | solution.py:74
  4.2 1.9 %collective-permute-start.4 = (bf16[32,3072]{1,0:T(8,128)(2,1)S(1)}, bf16[32,3072]{1,0:T(8,128)(2,1)S(1)}, u32[]{:S(2)}, u32[]{:S(2)}) collective-permute-start(bf16[32,3072]{1,0:T(8,128)(2,1)S(1)} %get-tuple-element.74.refs_0_), channel_id=1, source_target_pairs={{2,0},{4,2},{6,4},{7,6},{5,7},{3,5},{1,3},{0,1},{10,8},{12,10},{14... | collective-permute-start | bytes 589832 | tf_op jit(solution)/shard_map/ppermute | solution.py:74
  6.2 3.6 %collective-permute-done.10.refs_7_.arrived_ref = bf16[32,3072]{1,0:T(8,128)(2,1)S(1)} collective-permute-done((bf16[32,3072]{1,0:T(8,128)(2,1)S(1)}, bf16[32,3072]{1,0:T(8,128)(2,1)S(1)}, u32[]{:S(2)}, u32[]{:S(2)}) %collective-permute-start.10) | collective-permute-done | bytes 196640 | tf_op jit(solution)/shard_map/ppermute | solution.py:74
  9.9 2.0 %collective-permute-start.11 = (bf16[32,3072]{1,0:T(8,128)(2,1)S(1)}, bf16[32,3072]{1,0:T(8,128)(2,1)S(1)}, u32[]{:S(2)}, u32[]{:S(2)}) collective-permute-start(bf16[32,3072]{1,0:T(8,128)(2,1)S(1)} %collective-permute-done.10.refs_7_.arrived_ref), channel_id=1, source_target_pairs={{2,0},{4,2},{6,4},{7,6},{5,7},{3,5},{1,3},{0,1},{10,8},{12,10},{14... | collective-permute-start | bytes 589832 | tf_op jit(solution)/shard_map/ppermute | solution.py:74
  12.0 2.1 %collective-permute-done.4.refs_2_ = bf16[32,3072]{1,0:T(8,128)(2,1)S(1)} collective-permute-done((bf16[32,3072]{1,0:T(8,128)(2,1)S(1)}, bf16[32,3072]{1,0:T(8,128)(2,1)S(1)}, u32[]{:S(2)}, u32[]{:S(2)}) %collective-permute-start.4) | collective-permute-done | bytes 196640 | tf_op jit(solution)/shard_map/ppermute | solution.py:74
  14.1 2.0 %collective-permute-start.5 = (bf16[32,3072]{1,0:T(8,128)(2,1)S(1)}, bf16[32,3072]{1,0:T(8,128)(2,1)S(1)}, u32[]{:S(2)}, u32[]{:S(2)}) collective-permute-start(bf16[32,3072]{1,0:T(8,128)(2,1)S(1)} %collective-permute-done.4.refs_2_), channel_id=1, source_target_pairs={{2,0},{4,2},{6,4},{7,6},{5,7},{3,5},{1,3},{0,1},{10,8},{12,10},{14... | collective-permute-start | bytes 589832 | tf_op jit(solution)/shard_map/ppermute | solution.py:74
  16.2 2.1 %collective-permute-done.11.refs_9_ = bf16[32,3072]{1,0:T(8,128)(2,1)S(1)} collective-permute-done((bf16[32,3072]{1,0:T(8,128)(2,1)S(1)}, bf16[32,3072]{1,0:T(8,128)(2,1)S(1)}, u32[]{:S(2)}, u32[]{:S(2)}) %collective-permute-start.11) | collective-permute-done | bytes 196640 | tf_op jit(solution)/shard_map/ppermute | solution.py:74
  18.3 2.0 %collective-permute-start.12 = (bf16[32,3072]{1,0:T(8,128)(2,1)S(1)}, bf16[32,3072]{1,0:T(8,128)(2,1)S(1)}, u32[]{:S(2)}, u32[]{:S(2)}) collective-permute-start(bf16[32,3072]{1,0:T(8,128)(2,1)S(1)} %collective-permute-done.11.refs_9_), channel_id=1, source_target_pairs={{2,0},{4,2},{6,4},{7,6},{5,7},{3,5},{1,3},{0,1},{10,8},{12,10},{14... | collective-permute-start | bytes 589832 | tf_op jit(solution)/shard_map/ppermute | solution.py:74
  20.4 2.1 %collective-permute-done.5.refs_4_ = bf16[32,3072]{1,0:T(8,128)(2,1)S(1)} collective-permute-done((bf16[32,3072]{1,0:T(8,128)(2,1)S(1)}, bf16[32,3072]{1,0:T(8,128)(2,1)S(1)}, u32[]{:S(2)}, u32[]{:S(2)}) %collective-permute-start.5) | collective-permute-done | bytes 196640 | tf_op jit(solution)/shard_map/ppermute | solution.py:74
  22.5 2.0 %collective-permute-start.6 = (bf16[32,3072]{1,0:T(8,128)(2,1)S(1)}, bf16[32,3072]{1,0:T(8,128)(2,1)S(1)}, u32[]{:S(2)}, u32[]{:S(2)}) collective-permute-start(bf16[32,3072]{1,0:T(8,128)(2,1)S(1)} %collective-permute-done.5.refs_4_), channel_id=1, source_target_pairs={{2,0},{4,2},{6,4},{7,6},{5,7},{3,5},{1,3},{0,1},{10,8},{12,10},{14... | collective-permute-start | bytes 589832 | tf_op jit(solution)/shard_map/ppermute | solution.py:74
  24.6 4.1 %collective-permute-done.2.refs_0_ = bf16[32,3072]{1,0:T(8,128)(2,1)S(1)} collective-permute-done((bf16[32,3072]{1,0:T(8,128)(2,1)S(1)}, bf16[32,3072]{1,0:T(8,128)(2,1)S(1)}, u32[]{:S(2)}, u32[]{:S(2)}) %collective-permute-start.2) | collective-permute-done | bytes 196640 | tf_op jit(solution)/shard_map/ppermute | solution.py:73
  28.8 1.9 %collective-permute-start.13 = (bf16[32,3072]{1,0:T(8,128)(2,1)S(1)}, bf16[32,3072]{1,0:T(8,128)(2,1)S(1)}, u32[]{:S(2)}, u32[]{:S(2)}) collective-permute-start(bf16[32,3072]{1,0:T(8,128)(2,1)S(1)} %collective-permute-done.12.refs_11_.refs_3_), channel_id=1, source_target_pairs={{2,0},{4,2},{6,4},{7,6},{5,7},{3,5},{1,3},{0,1},{10,8},{12,10},{14... | collective-permute-start | bytes 589832 | tf_op jit(solution)/shard_map/ppermute | solution.py:78
  30.8 1.2 %early_keys.1 = (bf16[256,512]{1,0:T(8,128)(2,1)S(1)}, bf16[256,3072]{1,0:T(8,128)(2,1)S(1)}, bf16[256,3072]{1,0:T(8,128)(2,1)S(1)}) custom-call(bf16[32,3072]{1,0:T(8,128)(2,1)S(1)} %get-tuple-element.74.refs_0_, bf16[32,3072]{1,0:T(8,128)(2,1)S(1)} %collective-permute-done.refs_1_.arrived_ref, bf16[32,3072]{1,0:T(8,128)(2,1)S(1)} %collective-permute-done.4.refs_2_, ...), custom_call_target="tpu_custom_call" | custom-call | flops 1006632960 | bytes 6291456 | tf_op jit(solution)/shard_map/early_keys/pallas_call | solution.py:106
  32.0 1.2 %early_values.1.refs_6_.refs_5_ = bf16[256,512]{1,0:T(8,128)(2,1)S(1)} custom-call(bf16[256,3072]{1,0:T(8,128)(2,1)S(1)} %get-tuple-element.39.first_ref.refs_4_, bf16[256,3072]{1,0:T(8,128)(2,1)S(1)} %get-tuple-element.40.second_ref.refs_5_, bf16[3,6144,512]{2,1,0:T(8,128)(2,1)S(1)} %bitcast.2), custom_call_target="tpu_custom_call" | custom-call | flops 1006632960 | bytes 6291456 | tf_op jit(solution)/shard_map/early_values/pallas_call | solution.py:126
  33.3 2.4 %collective-permute-done.3.refs_0_ = bf16[32,3072]{1,0:T(8,128)(2,1)S(1)} collective-permute-done((bf16[32,3072]{1,0:T(8,128)(2,1)S(1)}, bf16[32,3072]{1,0:T(8,128)(2,1)S(1)}, u32[]{:S(2)}, u32[]{:S(2)}) %collective-permute-start.3) | collective-permute-done | bytes 196640 | tf_op jit(solution)/shard_map/ppermute | solution.py:77
  35.7 1.1 %first_pass.1 = (bf16[256,3072]{1,0:T(8,128)(2,1)S(1)}, f32[2,96,512]{2,1,0:T(8,128)S(1)}) custom-call(bf16[32,3072]{1,0:T(8,128)(2,1)S(1)} %collective-permute-done.3.refs_0_, bf16[256,3072]{1,0:T(8,128)(2,1)S(1)} %get-tuple-element.41.refs_1_, bf16[3,6144,512]{2,1,0:T(8,128)(2,1)S(1)} %bitcast.2, ...), custom_call_target="tpu_custom_call", output_to_operand_aliasing={{0}: (1, {})} | custom-call | flops 603979776 | bytes 6291456 | tf_op jit(solution)/shard_map/first_pass/pallas_call | solution.py:166
  36.8 0.9 %late_keys_and_values.2 = (bf16[256,3072]{1,0:T(8,128)(2,1)S(1)}, bf16[256,512]{1,0:T(8,128)(2,1)S(1)}, bf16[256,512]{1,0:T(8,128)(2,1)S(1)}, bf16[2,128,128]{2,1,0:T(8,128)(2,1)S(1)}) custom-call(bf16[32,3072]{1,0:T(8,128)(2,1)S(1)} %collective-permute-done.13.refs_0_, ...), custom_call_target="tpu_custom_call", output_to_operand_aliasing={{0}: (1, {}), {1}: (4, {}), {2}: (5, {})} | custom-call | flops 301989888 | bytes 3145728 | tf_op jit(solution)/shard_map/late_keys_and_values/pallas_call | solution.py:206
  37.8 0.9 %late_keys_and_values.3 = (bf16[256,3072]{1,0:T(8,128)(2,1)S(1)}, bf16[256,512]{1,0:T(8,128)(2,1)S(1)}, bf16[256,512]{1,0:T(8,128)(2,1)S(1)}, bf16[2,128,128]{2,1,0:T(8,128)(2,1)S(1)}) custom-call(bf16[256,3072]{1,0:T(8,128)(2,1)S(1)} %get-tuple-element.46.refs_0_, ...), custom_call_target="tpu_custom_call", output_to_operand_aliasing={{0}: (0, {}), {1}: (3, {}), {2}: (4, {})} | custom-call | flops 5000000000 | bytes 3145728 | tf_op jit(solution)/shard_map/late_keys_and_values/pallas_call | solution.py:206
  38.7 0.6 collective-permute-start.16
  39.2 1.6 %collective-permute-start.15 = (bf16[2,128,128]{2,1,0:T(8,128)(2,1)S(1)}, bf16[2,128,128]{2,1,0:T(8,128)(2,1)S(1)}, u32[]{:S(2)}, u32[]{:S(2)}) collective-permute-start(bf16[2,128,128]{2,1,0:T(8,128)(2,1)S(1)} %add_states.2.refs_0_), channel_id=1, source_target_pairs={{0,16},{8,24},{16,0},{24,8},{1,17},{9,25},{17,1},{25,9},{2,18},{10... | collective-permute-start | bytes 196616 | tf_op jit(solution)/shard_map/ppermute | solution.py:421
  40.8 0.9 %collective-permute-start.17 = (bf16[2,128,128]{2,1,0:T(8,128)(2,1)S(1)}, bf16[2,128,128]{2,1,0:T(8,128)(2,1)S(1)}, u32[]{:S(2)}, u32[]{:S(2)}) collective-permute-start(bf16[2,128,128]{2,1,0:T(8,128)(2,1)S(1)} %add_states.3), channel_id=1, source_target_pairs={{0,16},{8,24},{16,0},{24,8},{1,17},{9,25},{17,1},{25,9},{2,18},{10... | collective-permute-start | bytes 196616 | tf_op jit(solution)/shard_map/ppermute | solution.py:421
  41.7 2.3 %queries_within.1 = (bf16[256,512]{1,0:T(8,128)(2,1)S(1)}, f32[256,512]{1,0:T(8,128)S(1)}) custom-call(bf16[256,3072]{1,0:T(8,128)(2,1)S(1)} %get-tuple-element.43.first_ref, bf16[256,3072]{1,0:T(8,128)(2,1)S(1)} %get-tuple-element.49.second_ref, bf16[3,6144,512]{2,1,0:T(8,128)(2,1)S(1)} %bitcast.2, bf16[256,512]{1,0:T(8,128)(2,1)S(1)} %get-tuple-element.50.k_ref, ...), custom_call_target="tpu_custom_call" | custom-call | flops 1744830464 | bytes 6291456 | tf_op jit(solution)/shard_map/queries_within/pallas_call | solution.py:249
  44.0 1.1 %collective-permute-done.17.refs_3_ = bf16[2,128,128]{2,1,0:T(8,128)(2,1)S(1)} collective-permute-done((bf16[2,128,128]{2,1,0:T(8,128)(2,1)S(1)}, bf16[2,128,128]{2,1,0:T(8,128)(2,1)S(1)}, u32[]{:S(2)}, u32[]{:S(2)}) %collective-permute-start.17) | collective-permute-done | bytes 65568 | tf_op jit(solution)/shard_map/ppermute | solution.py:421
  45.2 1.6 %attend_and_project.1 = (bf16[256,512]{1,0:T(8,128)(2,1)S(1)}, bf16[32,3072]{1,0:T(8,128)(2,1)S(1)}, bf16[32,3072]{1,0:T(8,128)(2,1)S(1)}) custom-call(bf16[256,512]{1,0:T(8,128)(2,1)S(1)} %get-tuple-element.52.q_ref, f32[256,512]{1,0:T(8,128)S(1)} %get-tuple-element.53.within_ref, f32[4,128,128]{2,1,0:T(8,128)S(1)} %copy-done, f32[1,512]{1,0:T(1,128)S(1)} %bitcast.5, ...), custom_call_target="tpu_custom_call" | custom-call | flops 1610612736 | bytes 6291456 | tf_op jit(solution)/shard_map/attend_and_project/pallas_call | solution.py:297
  46.8 1.6 %collective-permute-start.28 = (bf16[32,3072]{1,0:T(8,128)(2,1)S(1)}, bf16[32,3072]{1,0:T(8,128)(2,1)S(1)}, u32[]{:S(2)}, u32[]{:S(2)}) collective-permute-start(bf16[32,3072]{1,0:T(8,128)(2,1)S(1)} %get-tuple-element.72), channel_id=1, source_target_pairs={{2,0},{4,2},{6,4},{7,6},{5,7},{3,5},{1,3},{0,1},{10,8},{12,10},{14... | collective-permute-start | bytes 589832 | tf_op jit(solution)/shard_map/ppermute | solution.py:385
  48.4 0.4 collective-permute-start.24
  48.8 1.6 %project_rest.1 = (bf16[32,3072]{1,0:T(8,128)(2,1)S(1)}, bf16[32,3072]{1,0:T(8,128)(2,1)S(1)}, bf16[32,3072]{1,0:T(8,128)(2,1)S(1)}, bf16[32,3072]{1,0:T(8,128)(...) custom-call(bf16[256,512]{1,0:T(8,128)(2,1)S(1)} %get-tuple-element., ...), custom_call_target="tpu_custom_call" | custom-call | flops 5000000000 | bytes 6291456 | tf_op jit(solution)/shard_map/project_rest/pallas_call | solution.py:316
  50.5 0.6 collective-permute-start.21
  51.0 1.5 %collective-permute-start.18 = (bf16[32,3072]{1,0:T(8,128)(2,1)S(1)}, bf16[32,3072]{1,0:T(8,128)(2,1)S(1)}, u32[]{:S(2)}, u32[]{:S(2)}) collective-permute-start(bf16[32,3072]{1,0:T(8,128)(2,1)S(1)} %get-tuple-element.61), channel_id=1, source_target_pairs={{2,0},{4,2},{6,4},{7,6},{5,7},{3,5},{1,3},{0,1},{10,8},{12,10},{14... | collective-permute-start | bytes 589832 | tf_op jit(solution)/shard_map/ppermute | solution.py:385
  52.5 1.2 %collective-permute-done.28.got_ref = bf16[32,3072]{1,0:T(8,128)(2,1)S(1)} collective-permute-done((bf16[32,3072]{1,0:T(8,128)(2,1)S(1)}, bf16[32,3072]{1,0:T(8,128)(2,1)S(1)}, u32[]{:S(2)}, u32[]{:S(2)}) %collective-permute-start.28) | collective-permute-done | bytes 196640 | tf_op jit(solution)/shard_map/ppermute | solution.py:385
  53.8 1.7 %collective-permute-start.29 = (bf16[32,3072]{1,0:T(8,128)(2,1)S(1)}, bf16[32,3072]{1,0:T(8,128)(2,1)S(1)}, u32[]{:S(2)}, u32[]{:S(2)}) collective-permute-start(bf16[32,3072]{1,0:T(8,128)(2,1)S(1)} %add_step.17), channel_id=1, source_target_pairs={{2,0},{4,2},{6,4},{7,6},{5,7},{3,5},{1,3},{0,1},{10,8},{12,10},{14... | collective-permute-start | bytes 589832 | tf_op jit(solution)/shard_map/ppermute | solution.py:385
  55.5 0.7 collective-permute-done.24.got_ref
  56.3 0.5 collective-permute-start.25
  56.8 3.7 %collective-permute-done.21.got_ref = bf16[32,3072]{1,0:T(8,128)(2,1)S(1)} collective-permute-done((bf16[32,3072]{1,0:T(8,128)(2,1)S(1)}, bf16[32,3072]{1,0:T(8,128)(2,1)S(1)}, u32[]{:S(2)}, u32[]{:S(2)}) %collective-permute-start.21) | collective-permute-done | bytes 196640 | tf_op jit(solution)/shard_map/ppermute | solution.py:385
  60.5 0.5 collective-permute-start.22
  61.0 1.6 %collective-permute-start.19 = (bf16[32,3072]{1,0:T(8,128)(2,1)S(1)}, bf16[32,3072]{1,0:T(8,128)(2,1)S(1)}, u32[]{:S(2)}, u32[]{:S(2)}) collective-permute-start(bf16[32,3072]{1,0:T(8,128)(2,1)S(1)} %add_step.10), channel_id=1, source_target_pairs={{2,0},{4,2},{6,4},{7,6},{5,7},{3,5},{1,3},{0,1},{10,8},{12,10},{14... | collective-permute-start | bytes 589832 | tf_op jit(solution)/shard_map/ppermute | solution.py:385
  63.1 1.5 %collective-permute-start.30 = (bf16[32,3072]{1,0:T(8,128)(2,1)S(1)}, bf16[32,3072]{1,0:T(8,128)(2,1)S(1)}, u32[]{:S(2)}, u32[]{:S(2)}) collective-permute-start(bf16[32,3072]{1,0:T(8,128)(2,1)S(1)} %add_step.18), channel_id=1, source_target_pairs={{2,0},{4,2},{6,4},{7,6},{5,7},{3,5},{1,3},{0,1},{10,8},{12,10},{14... | collective-permute-start | bytes 589832 | tf_op jit(solution)/shard_map/ppermute | solution.py:385
  64.7 0.6 collective-permute-start.26
  65.3 3.5 %collective-permute-done.22.got_ref = bf16[32,3072]{1,0:T(8,128)(2,1)S(1)} collective-permute-done((bf16[32,3072]{1,0:T(8,128)(2,1)S(1)}, bf16[32,3072]{1,0:T(8,128)(2,1)S(1)}, u32[]{:S(2)}, u32[]{:S(2)}) %collective-permute-start.22) | collective-permute-done | bytes 196640 | tf_op jit(solution)/shard_map/ppermute | solution.py:385
  68.9 0.5 collective-permute-start.23
  69.5 1.6 %collective-permute-start.20 = (bf16[32,3072]{1,0:T(8,128)(2,1)S(1)}, bf16[32,3072]{1,0:T(8,128)(2,1)S(1)}, u32[]{:S(2)}, u32[]{:S(2)}) collective-permute-start(bf16[32,3072]{1,0:T(8,128)(2,1)S(1)} %add_step.11), channel_id=1, source_target_pairs={{2,0},{4,2},{6,4},{7,6},{5,7},{3,5},{1,3},{0,1},{10,8},{12,10},{14... | collective-permute-start | bytes 589832 | tf_op jit(solution)/shard_map/ppermute | solution.py:385
  71.6 1.6 %collective-permute-start.31 = (bf16[32,3072]{1,0:T(8,128)(2,1)S(1)}, bf16[32,3072]{1,0:T(8,128)(2,1)S(1)}, u32[]{:S(2)}, u32[]{:S(2)}) collective-permute-start(bf16[32,3072]{1,0:T(8,128)(2,1)S(1)} %add_step.19), channel_id=1, source_target_pairs={{2,0},{4,2},{6,4},{7,6},{5,7},{3,5},{1,3},{0,1},{10,8},{12,10},{14... | collective-permute-start | bytes 589832 | tf_op jit(solution)/shard_map/ppermute | solution.py:385
  73.3 0.5 collective-permute-start.27
  73.8 3.5 %collective-permute-done.23.got_second = bf16[32,3072]{1,0:T(8,128)(2,1)S(1)} collective-permute-done((bf16[32,3072]{1,0:T(8,128)(2,1)S(1)}, bf16[32,3072]{1,0:T(8,128)(2,1)S(1)}, u32[]{:S(2)}, u32[]{:S(2)}) %collective-permute-start.23) | collective-permute-done | bytes 196640 | tf_op jit(solution)/shard_map/ppermute | solution.py:385
  77.4 0.9 %collective-permute-done.31.second = bf16[32,3072]{1,0:T(8,128)(2,1)S(1)} collective-permute-done((bf16[32,3072]{1,0:T(8,128)(2,1)S(1)}, bf16[32,3072]{1,0:T(8,128)(2,1)S(1)}, u32[]{:S(2)}, u32[]{:S(2)}) %collective-permute-start.31) | collective-permute-done | bytes 196640 | tf_op jit(solution)/shard_map/ppermute | solution.py:385
  78.3 1.3 %collective-permute-done.27.first = bf16[32,3072]{1,0:T(8,128)(2,1)S(1)} collective-permute-done((bf16[32,3072]{1,0:T(8,128)(2,1)S(1)}, bf16[32,3072]{1,0:T(8,128)(2,1)S(1)}, u32[]{:S(2)}, u32[]{:S(2)}) %collective-permute-start.27) | collective-permute-done | bytes 196640 | tf_op jit(solution)/shard_map/ppermute | solution.py:385
  79.6 0.8 %finish.1 = bf16[32,6144]{1,0:T(8,128)(2,1)} custom-call(f32[2,32,3072]{2,1,0:T(8,128)S(1)} %add_own.1.gathered_ref, bf16[32,3072]{1,0:T(8,128)(2,1)S(1)} %collective-permute-done.27.first, bf16[32,3072]{1,0:T(8,128)(2,1)S(1)} %collective-permute-done.31.second), custom_call_target="tpu_custom_call" | custom-call | bytes 393216 | tf_op jit(solution)/shard_map/finish/pallas_call | solution.py:367
  (62 shorter events, 2.7 us)
Async XLA Ops:
  1.1 8.8 %collective-permute-start.10 = (bf16[32,3072]{1,0:T(8,128)(2,1)S(1)}, bf16[32,3072]{1,0:T(8,128)(2,1)S(1)}, u32[]{:S(2)}, u32[]{:S(2)}) collective-permute-start(bf16[32,3072]{1,0:T(8,128)(2,1)S(1)} %get-tuple-element.73.refs_5_), channel_id=1, source_target_pairs={{2,0},{4,2},{6,4},{7,6},{5,7},{3,5},{1,3},{0,1},{10,8},{12,10},{14... | collective-permute-start | bytes 589832 | tf_op jit(solution)/shard_map/ppermute | solution.py:74
  4.0 7.8 %collective-permute-start = (bf16[32,3072]{1,0:T(8,128)(2,1)S(1)}, bf16[32,3072]{1,0:T(8,128)(2,1)S(1)}, u32[]{:S(2)}, u32[]{:S(2)}) collective-permute-start(bf16[32,3072]{1,0:T(8,128)(2,1)S(1)} %get-tuple-element.74.refs_0_), channel_id=1, source_target_pairs={{0,2},{2,4},{4,6},{6,7},{7,5},{5,3},{3,1},{1,0},{8,10},{10,12},{12... | collective-permute-start | bytes 589832 | tf_op jit(solution)/shard_map/ppermute | solution.py:73
  4.2 9.9 %collective-permute-start.4 = (bf16[32,3072]{1,0:T(8,128)(2,1)S(1)}, bf16[32,3072]{1,0:T(8,128)(2,1)S(1)}, u32[]{:S(2)}, u32[]{:S(2)}) collective-permute-start(bf16[32,3072]{1,0:T(8,128)(2,1)S(1)} %get-tuple-element.74.refs_0_), channel_id=1, source_target_pairs={{2,0},{4,2},{6,4},{7,6},{5,7},{3,5},{1,3},{0,1},{10,8},{12,10},{14... | collective-permute-start | bytes 589832 | tf_op jit(solution)/shard_map/ppermute | solution.py:74
  6.1 10.0 %collective-permute-start.7 = (bf16[32,3072]{1,0:T(8,128)(2,1)S(1)}, bf16[32,3072]{1,0:T(8,128)(2,1)S(1)}, u32[]{:S(2)}, u32[]{:S(2)}) collective-permute-start(bf16[32,3072]{1,0:T(8,128)(2,1)S(1)} %get-tuple-element.73.refs_5_), channel_id=1, source_target_pairs={{0,2},{2,4},{4,6},{6,7},{7,5},{5,3},{3,1},{1,0},{8,10},{10,12},{12... | collective-permute-start | bytes 589832 | tf_op jit(solution)/shard_map/ppermute | solution.py:73
  9.9 8.4 %collective-permute-start.11 = (bf16[32,3072]{1,0:T(8,128)(2,1)S(1)}, bf16[32,3072]{1,0:T(8,128)(2,1)S(1)}, u32[]{:S(2)}, u32[]{:S(2)}) collective-permute-start(bf16[32,3072]{1,0:T(8,128)(2,1)S(1)} %collective-permute-done.10.refs_7_.arrived_ref), channel_id=1, source_target_pairs={{2,0},{4,2},{6,4},{7,6},{5,7},{3,5},{1,3},{0,1},{10,8},{12,10},{14... | collective-permute-start | bytes 589832 | tf_op jit(solution)/shard_map/ppermute | solution.py:74
  11.9 8.4 %collective-permute-start.1 = (bf16[32,3072]{1,0:T(8,128)(2,1)S(1)}, bf16[32,3072]{1,0:T(8,128)(2,1)S(1)}, u32[]{:S(2)}, u32[]{:S(2)}) collective-permute-start(bf16[32,3072]{1,0:T(8,128)(2,1)S(1)} %collective-permute-done.refs_1_.arrived_ref), channel_id=1, source_target_pairs={{0,2},{2,4},{4,6},{6,7},{7,5},{5,3},{3,1},{1,0},{8,10},{10,12},{12... | collective-permute-start | bytes 589832 | tf_op jit(solution)/shard_map/ppermute | solution.py:73
  14.1 8.4 %collective-permute-start.5 = (bf16[32,3072]{1,0:T(8,128)(2,1)S(1)}, bf16[32,3072]{1,0:T(8,128)(2,1)S(1)}, u32[]{:S(2)}, u32[]{:S(2)}) collective-permute-start(bf16[32,3072]{1,0:T(8,128)(2,1)S(1)} %collective-permute-done.4.refs_2_), channel_id=1, source_target_pairs={{2,0},{4,2},{6,4},{7,6},{5,7},{3,5},{1,3},{0,1},{10,8},{12,10},{14... | collective-permute-start | bytes 589832 | tf_op jit(solution)/shard_map/ppermute | solution.py:74
  16.1 8.4 %collective-permute-start.8 = (bf16[32,3072]{1,0:T(8,128)(2,1)S(1)}, bf16[32,3072]{1,0:T(8,128)(2,1)S(1)}, u32[]{:S(2)}, u32[]{:S(2)}) collective-permute-start(bf16[32,3072]{1,0:T(8,128)(2,1)S(1)} %collective-permute-done.7.refs_6_), channel_id=1, source_target_pairs={{0,2},{2,4},{4,6},{6,7},{7,5},{5,3},{3,1},{1,0},{8,10},{10,12},{12... | collective-permute-start | bytes 589832 | tf_op jit(solution)/shard_map/ppermute | solution.py:73
  16.2 14.6 %slice-start = ((s8[18874368]{0:T(1024)(128)(4,1)}), s8[4194304]{0:T(1024)(128)(4,1)S(1)}, s32[]{:S(2)}) async-start(s8[18874368]{0:T(1024)(128)(4,1)} %bitcast.1), calls=%async_computation | async-start | bytes 8388608
  16.2 14.6 %slice-start.1 = ((s8[18874368]{0:T(1024)(128)(4,1)}), s8[4194304]{0:T(1024)(128)(4,1)S(1)}, s32[]{:S(2)}) async-start(s8[18874368]{0:T(1024)(128)(4,1)} %bitcast.1), calls=%async_computation.1 | async-start | bytes 8388608
  16.2 14.6 %slice-start.2 = ((s8[18874368]{0:T(1024)(128)(4,1)}), s8[4194304]{0:T(1024)(128)(4,1)S(1)}, s32[]{:S(2)}) async-start(s8[18874368]{0:T(1024)(128)(4,1)} %bitcast.1), calls=%async_computation.2 | async-start | bytes 8388608
  16.2 14.6 %slice-start.3 = ((s8[18874368]{0:T(1024)(128)(4,1)}), s8[4194304]{0:T(1024)(128)(4,1)S(1)}, s32[]{:S(2)}) async-start(s8[18874368]{0:T(1024)(128)(4,1)} %bitcast.1), calls=%async_computation.3 | async-start | bytes 8388608
  16.2 14.5 %slice-start.4 = ((s8[18874368]{0:T(1024)(128)(4,1)}), s8[2097152]{0:T(1024)(128)(4,1)S(1)}, s32[]{:S(2)}) async-start(s8[18874368]{0:T(1024)(128)(4,1)} %bitcast.1), calls=%async_computation.4 | async-start | bytes 4194304
  18.3 10.6 %collective-permute-start.12 = (bf16[32,3072]{1,0:T(8,128)(2,1)S(1)}, bf16[32,3072]{1,0:T(8,128)(2,1)S(1)}, u32[]{:S(2)}, u32[]{:S(2)}) collective-permute-start(bf16[32,3072]{1,0:T(8,128)(2,1)S(1)} %collective-permute-done.11.refs_9_), channel_id=1, source_target_pairs={{2,0},{4,2},{6,4},{7,6},{5,7},{3,5},{1,3},{0,1},{10,8},{12,10},{14... | collective-permute-start | bytes 589832 | tf_op jit(solution)/shard_map/ppermute | solution.py:74
  20.3 8.4 %collective-permute-start.2 = (bf16[32,3072]{1,0:T(8,128)(2,1)S(1)}, bf16[32,3072]{1,0:T(8,128)(2,1)S(1)}, u32[]{:S(2)}, u32[]{:S(2)}) collective-permute-start(bf16[32,3072]{1,0:T(8,128)(2,1)S(1)} %collective-permute-done.1.refs_3_), channel_id=1, source_target_pairs={{0,2},{2,4},{4,6},{6,7},{7,5},{5,3},{3,1},{1,0},{8,10},{10,12},{12... | collective-permute-start | bytes 589832 | tf_op jit(solution)/shard_map/ppermute | solution.py:73
  22.5 10.7 %collective-permute-start.6 = (bf16[32,3072]{1,0:T(8,128)(2,1)S(1)}, bf16[32,3072]{1,0:T(8,128)(2,1)S(1)}, u32[]{:S(2)}, u32[]{:S(2)}) collective-permute-start(bf16[32,3072]{1,0:T(8,128)(2,1)S(1)} %collective-permute-done.5.refs_4_), channel_id=1, source_target_pairs={{2,0},{4,2},{6,4},{7,6},{5,7},{3,5},{1,3},{0,1},{10,8},{12,10},{14... | collective-permute-start | bytes 589832 | tf_op jit(solution)/shard_map/ppermute | solution.py:74
  24.5 8.7 %collective-permute-start.9 = (bf16[32,3072]{1,0:T(8,128)(2,1)S(1)}, bf16[32,3072]{1,0:T(8,128)(2,1)S(1)}, u32[]{:S(2)}, u32[]{:S(2)}) collective-permute-start(bf16[32,3072]{1,0:T(8,128)(2,1)S(1)} %collective-permute-done.8.refs_8_), channel_id=1, source_target_pairs={{0,2},{2,4},{4,6},{6,7},{7,5},{5,3},{3,1},{1,0},{8,10},{10,12},{12... | collective-permute-start | bytes 589832 | tf_op jit(solution)/shard_map/ppermute | solution.py:73
  28.7 7.0 %collective-permute-start.3 = (bf16[32,3072]{1,0:T(8,128)(2,1)S(1)}, bf16[32,3072]{1,0:T(8,128)(2,1)S(1)}, u32[]{:S(2)}, u32[]{:S(2)}) collective-permute-start(bf16[32,3072]{1,0:T(8,128)(2,1)S(1)} %collective-permute-done.2.refs_0_), channel_id=1, source_target_pairs={{0,2},{2,4},{4,6},{6,7},{7,5},{5,3},{3,1},{1,0},{8,10},{10,12},{12... | collective-permute-start | bytes 589832 | tf_op jit(solution)/shard_map/ppermute | solution.py:77
  28.8 8.0 %collective-permute-start.13 = (bf16[32,3072]{1,0:T(8,128)(2,1)S(1)}, bf16[32,3072]{1,0:T(8,128)(2,1)S(1)}, u32[]{:S(2)}, u32[]{:S(2)}) collective-permute-start(bf16[32,3072]{1,0:T(8,128)(2,1)S(1)} %collective-permute-done.12.refs_11_.refs_3_), channel_id=1, source_target_pairs={{2,0},{4,2},{6,4},{7,6},{5,7},{3,5},{1,3},{0,1},{10,8},{12,10},{14... | collective-permute-start | bytes 589832 | tf_op jit(solution)/shard_map/ppermute | solution.py:78
  37.7 1.5 %collective-permute-start.14 = (bf16[2,128,128]{2,1,0:T(8,128)(2,1)S(1)}, bf16[2,128,128]{2,1,0:T(8,128)(2,1)S(1)}, u32[]{:S(2)}, u32[]{:S(2)}) collective-permute-start(bf16[2,128,128]{2,1,0:T(8,128)(2,1)S(1)} %get-tuple-element.54.one_ref), channel_id=1, source_target_pairs={{0,8},{8,0},{16,24},{24,16},{1,9},{9,1},{17,25},{25,17},{2,10},{10... | collective-permute-start | bytes 196616 | tf_op jit(solution)/shard_map/ppermute | solution.py:421
  38.7 2.2 %collective-permute-start.16 = (bf16[2,128,128]{2,1,0:T(8,128)(2,1)S(1)}, bf16[2,128,128]{2,1,0:T(8,128)(2,1)S(1)}, u32[]{:S(2)}, u32[]{:S(2)}) collective-permute-start(bf16[2,128,128]{2,1,0:T(8,128)(2,1)S(1)} %get-tuple-element.55.one_ref), channel_id=1, source_target_pairs={{0,8},{8,0},{16,24},{24,16},{1,9},{9,1},{17,25},{25,17},{2,10},{10... | collective-permute-start | bytes 196616 | tf_op jit(solution)/shard_map/ppermute | solution.py:421
  39.2 5.9 %collective-permute-start.15 = (bf16[2,128,128]{2,1,0:T(8,128)(2,1)S(1)}, bf16[2,128,128]{2,1,0:T(8,128)(2,1)S(1)}, u32[]{:S(2)}, u32[]{:S(2)}) collective-permute-start(bf16[2,128,128]{2,1,0:T(8,128)(2,1)S(1)} %add_states.2.refs_0_), channel_id=1, source_target_pairs={{0,16},{8,24},{16,0},{24,8},{1,17},{9,25},{17,1},{25,9},{2,18},{10... | collective-permute-start | bytes 196616 | tf_op jit(solution)/shard_map/ppermute | solution.py:421
  40.8 4.3 %collective-permute-start.17 = (bf16[2,128,128]{2,1,0:T(8,128)(2,1)S(1)}, bf16[2,128,128]{2,1,0:T(8,128)(2,1)S(1)}, u32[]{:S(2)}, u32[]{:S(2)}) collective-permute-start(bf16[2,128,128]{2,1,0:T(8,128)(2,1)S(1)} %add_states.3), channel_id=1, source_target_pairs={{0,16},{8,24},{16,0},{24,8},{1,17},{9,25},{17,1},{25,9},{2,18},{10... | collective-permute-start | bytes 196616 | tf_op jit(solution)/shard_map/ppermute | solution.py:421
  41.7 3.5 %slice-start.5 = ((s8[6291456]{0:T(1024)(128)(4,1)}), s8[4194304]{0:T(1024)(128)(4,1)S(1)}, s32[]{:S(2)}) async-start(s8[6291456]{0:T(1024)(128)(4,1)} %bitcast.3), calls=%async_computation.5 | async-start | bytes 8388608
  41.7 3.5 %slice-start.6 = ((s8[6291456]{0:T(1024)(128)(4,1)}), s8[2097152]{0:T(1024)(128)(4,1)S(1)}, s32[]{:S(2)}) async-start(s8[6291456]{0:T(1024)(128)(4,1)} %bitcast.3), calls=%async_computation.6 | async-start | bytes 4194304
  41.7 3.5 %copy-start = (f32[4,128,128]{2,1,0:T(8,128)S(1)}, f32[4,128,128]{2,1,0:T(8,128)}, u32[]{:S(2)}) copy-start(f32[4,128,128]{2,1,0:T(8,128)} %initial_ref.1) | copy-start | bytes 786436
  41.7 3.5 %copy-start.1 = (f32[512]{0:T(512)S(1)}, f32[512]{0:T(512)}, u32[]{:S(2)}) copy-start(f32[512]{0:T(512)} %param.8) | copy-start | bytes 6148
  46.8 7.0 %collective-permute-start.28 = (bf16[32,3072]{1,0:T(8,128)(2,1)S(1)}, bf16[32,3072]{1,0:T(8,128)(2,1)S(1)}, u32[]{:S(2)}, u32[]{:S(2)}) collective-permute-start(bf16[32,3072]{1,0:T(8,128)(2,1)S(1)} %get-tuple-element.72), channel_id=1, source_target_pairs={{2,0},{4,2},{6,4},{7,6},{5,7},{3,5},{1,3},{0,1},{10,8},{12,10},{14... | collective-permute-start | bytes 589832 | tf_op jit(solution)/shard_map/ppermute | solution.py:385
  48.4 7.8 %collective-permute-start.24 = (bf16[32,3072]{1,0:T(8,128)(2,1)S(1)}, bf16[32,3072]{1,0:T(8,128)(2,1)S(1)}, u32[]{:S(2)}, u32[]{:S(2)}) collective-permute-start(bf16[32,3072]{1,0:T(8,128)(2,1)S(1)} %get-tuple-element.68), channel_id=1, source_target_pairs={{0,2},{2,4},{4,6},{6,7},{7,5},{5,3},{3,1},{1,0},{8,10},{10,12},{12... | collective-permute-start | bytes 589832 | tf_op jit(solution)/shard_map/ppermute | solution.py:385
  50.5 10.0 %collective-permute-start.21 = (bf16[32,3072]{1,0:T(8,128)(2,1)S(1)}, bf16[32,3072]{1,0:T(8,128)(2,1)S(1)}, u32[]{:S(2)}, u32[]{:S(2)}) collective-permute-start(bf16[32,3072]{1,0:T(8,128)(2,1)S(1)} %get-tuple-element.64), channel_id=1, source_target_pairs={{0,2},{2,4},{4,6},{6,7},{7,5},{5,3},{3,1},{1,0},{8,10},{10,12},{12... | collective-permute-start | bytes 589832 | tf_op jit(solution)/shard_map/ppermute | solution.py:385
  51.0 9.9 %collective-permute-start.18 = (bf16[32,3072]{1,0:T(8,128)(2,1)S(1)}, bf16[32,3072]{1,0:T(8,128)(2,1)S(1)}, u32[]{:S(2)}, u32[]{:S(2)}) collective-permute-start(bf16[32,3072]{1,0:T(8,128)(2,1)S(1)} %get-tuple-element.61), channel_id=1, source_target_pairs={{2,0},{4,2},{6,4},{7,6},{5,7},{3,5},{1,3},{0,1},{10,8},{12,10},{14... | collective-permute-start | bytes 589832 | tf_op jit(solution)/shard_map/ppermute | solution.py:385
  53.8 9.3 %collective-permute-start.29 = (bf16[32,3072]{1,0:T(8,128)(2,1)S(1)}, bf16[32,3072]{1,0:T(8,128)(2,1)S(1)}, u32[]{:S(2)}, u32[]{:S(2)}) collective-permute-start(bf16[32,3072]{1,0:T(8,128)(2,1)S(1)} %add_step.17), channel_id=1, source_target_pairs={{2,0},{4,2},{6,4},{7,6},{5,7},{3,5},{1,3},{0,1},{10,8},{12,10},{14... | collective-permute-start | bytes 589832 | tf_op jit(solution)/shard_map/ppermute | solution.py:385
  56.3 8.4 %collective-permute-start.25 = (bf16[32,3072]{1,0:T(8,128)(2,1)S(1)}, bf16[32,3072]{1,0:T(8,128)(2,1)S(1)}, u32[]{:S(2)}, u32[]{:S(2)}) collective-permute-start(bf16[32,3072]{1,0:T(8,128)(2,1)S(1)} %add_step.14), channel_id=1, source_target_pairs={{0,2},{2,4},{4,6},{6,7},{7,5},{5,3},{3,1},{1,0},{8,10},{10,12},{12... | collective-permute-start | bytes 589832 | tf_op jit(solution)/shard_map/ppermute | solution.py:385
  60.5 8.4 %collective-permute-start.22 = (bf16[32,3072]{1,0:T(8,128)(2,1)S(1)}, bf16[32,3072]{1,0:T(8,128)(2,1)S(1)}, u32[]{:S(2)}, u32[]{:S(2)}) collective-permute-start(bf16[32,3072]{1,0:T(8,128)(2,1)S(1)} %add_step.12), channel_id=1, source_target_pairs={{0,2},{2,4},{4,6},{6,7},{7,5},{5,3},{3,1},{1,0},{8,10},{10,12},{12... | collective-permute-start | bytes 589832 | tf_op jit(solution)/shard_map/ppermute | solution.py:385
  61.0 8.4 %collective-permute-start.19 = (bf16[32,3072]{1,0:T(8,128)(2,1)S(1)}, bf16[32,3072]{1,0:T(8,128)(2,1)S(1)}, u32[]{:S(2)}, u32[]{:S(2)}) collective-permute-start(bf16[32,3072]{1,0:T(8,128)(2,1)S(1)} %add_step.10), channel_id=1, source_target_pairs={{2,0},{4,2},{6,4},{7,6},{5,7},{3,5},{1,3},{0,1},{10,8},{12,10},{14... | collective-permute-start | bytes 589832 | tf_op jit(solution)/shard_map/ppermute | solution.py:385
  63.1 8.4 %collective-permute-start.30 = (bf16[32,3072]{1,0:T(8,128)(2,1)S(1)}, bf16[32,3072]{1,0:T(8,128)(2,1)S(1)}, u32[]{:S(2)}, u32[]{:S(2)}) collective-permute-start(bf16[32,3072]{1,0:T(8,128)(2,1)S(1)} %add_step.18), channel_id=1, source_target_pairs={{2,0},{4,2},{6,4},{7,6},{5,7},{3,5},{1,3},{0,1},{10,8},{12,10},{14... | collective-permute-start | bytes 589832 | tf_op jit(solution)/shard_map/ppermute | solution.py:385
  64.7 8.5 %collective-permute-start.26 = (bf16[32,3072]{1,0:T(8,128)(2,1)S(1)}, bf16[32,3072]{1,0:T(8,128)(2,1)S(1)}, u32[]{:S(2)}, u32[]{:S(2)}) collective-permute-start(bf16[32,3072]{1,0:T(8,128)(2,1)S(1)} %add_step.15), channel_id=1, source_target_pairs={{0,2},{2,4},{4,6},{6,7},{7,5},{5,3},{3,1},{1,0},{8,10},{10,12},{12... | collective-permute-start | bytes 589832 | tf_op jit(solution)/shard_map/ppermute | solution.py:385
  68.9 8.4 %collective-permute-start.23 = (bf16[32,3072]{1,0:T(8,128)(2,1)S(1)}, bf16[32,3072]{1,0:T(8,128)(2,1)S(1)}, u32[]{:S(2)}, u32[]{:S(2)}) collective-permute-start(bf16[32,3072]{1,0:T(8,128)(2,1)S(1)} %add_step.13), channel_id=1, source_target_pairs={{0,2},{2,4},{4,6},{6,7},{7,5},{5,3},{3,1},{1,0},{8,10},{10,12},{12... | collective-permute-start | bytes 589832 | tf_op jit(solution)/shard_map/ppermute | solution.py:385
  69.5 7.8 %collective-permute-start.20 = (bf16[32,3072]{1,0:T(8,128)(2,1)S(1)}, bf16[32,3072]{1,0:T(8,128)(2,1)S(1)}, u32[]{:S(2)}, u32[]{:S(2)}) collective-permute-start(bf16[32,3072]{1,0:T(8,128)(2,1)S(1)} %add_step.11), channel_id=1, source_target_pairs={{2,0},{4,2},{6,4},{7,6},{5,7},{3,5},{1,3},{0,1},{10,8},{12,10},{14... | collective-permute-start | bytes 589832 | tf_op jit(solution)/shard_map/ppermute | solution.py:385
  71.6 6.7 %collective-permute-start.31 = (bf16[32,3072]{1,0:T(8,128)(2,1)S(1)}, bf16[32,3072]{1,0:T(8,128)(2,1)S(1)}, u32[]{:S(2)}, u32[]{:S(2)}) collective-permute-start(bf16[32,3072]{1,0:T(8,128)(2,1)S(1)} %add_step.19), channel_id=1, source_target_pairs={{2,0},{4,2},{6,4},{7,6},{5,7},{3,5},{1,3},{0,1},{10,8},{12,10},{14... | collective-permute-start | bytes 589832 | tf_op jit(solution)/shard_map/ppermute | solution.py:385
  73.3 6.3 %collective-permute-start.27 = (bf16[32,3072]{1,0:T(8,128)(2,1)S(1)}, bf16[32,3072]{1,0:T(8,128)(2,1)S(1)}, u32[]{:S(2)}, u32[]{:S(2)}) collective-permute-start(bf16[32,3072]{1,0:T(8,128)(2,1)S(1)} %add_step.16), channel_id=1, source_target_pairs={{0,2},{2,4},{4,6},{6,7},{7,5},{5,3},{3,1},{1,0},{8,10},{10,12},{12... | collective-permute-start | bytes 589832 | tf_op jit(solution)/shard_map/ppermute | solution.py:385

commit v17 on v15

--- a/solution.py
+++ b/solution.py
@@ -268,15 +268,17 @@
                 parts[2 * block + which][:, span] = product[block * rows : (block + 1) * rows, :]
 
 
-def attend_and_project(feat_q, within, initial, exchanged, gain, out_weight, blocks, rows, head_dim):
+def attend_and_project(rows, feat_q, within, initial, exchanged, gain, out_weight, block, head_dim, flops, name):
+    columns = feat_q.shape[1]
+    half = out_weight.shape[1] // 2
     per_group = initial.shape[0] // len(exchanged)
     steps = len(exchanged[0])
     others = [other for group in exchanged for other in group]
-    n_rows, columns = feat_q.shape
-    half = out_weight.shape[1] // 2
+    count = rows.stop - rows.start
+    n_parts = 2 * (count // block)
 
     def body(q_ref, within_ref, initial_ref, gain_ref, weight_ref, *refs):
-        other_refs, normalized_ref, parts = refs[: len(others)], refs[len(others)], refs[len(others) + 1 :]
+        other_refs, parts, normalized_ref = refs[: len(others)], refs[len(others) : -1], refs[-1]
         place = lax.axis_index("ctx")
         for head in range(columns // head_dim):
             at = slice(head * head_dim, (head + 1) * head_dim)
@@ -287,42 +289,24 @@
                 prefix = prefix + jnp.where(later, other_ref[within_group].astype(F32), 0.0)
             high = prefix.astype(BF16)
             low = (prefix - high.astype(F32)).astype(BF16)
-            q = q_ref[:, at]
-            attended = within_ref[:, at] + jnp.dot(q, high, preferred_element_type=F32)
+            q = q_ref[rows, at]
+            attended = within_ref[rows, at] + jnp.dot(q, high, preferred_element_type=F32)
             attended = attended + jnp.dot(q, low, preferred_element_type=F32)
             scale = lax.rsqrt(jnp.mean(attended * attended, axis=-1, keepdims=True) + 1e-06)
             normalized_ref[:, at] = (attended * scale * gain_ref[:, at]).astype(BF16)
-        project_out(normalized_ref[n_rows - blocks * rows :, :], weight_ref, parts, rows)
+        project_out(normalized_ref[...], weight_ref, parts, block)
 
     out = call(
         body,
-        [jax.ShapeDtypeStruct((n_rows, columns), BF16)] + [jax.ShapeDtypeStruct((rows, half), BF16)] * (2 * blocks),
+        [jax.ShapeDtypeStruct((block, half), BF16)] * n_parts,
         [VMEM] * (5 + len(others)),
-        [VMEM] * (1 + 2 * blocks),
-        flops=4 * n_rows * half * columns,
+        [VMEM] * n_parts,
+        flops=flops,
         nbytes=4 * half * columns,
-        name="attend_and_project",
+        scratch_shapes=[pltpu.VMEM((count, columns), BF16)],
+        name=name,
     )(feat_q, within, initial, gain.reshape(1, columns), out_weight, *others)
-    return out[0], [out[1 + 2 * block : 3 + 2 * block] for block in range(blocks)]
-
-
-def project_rest(normalized, out_weight, blocks, rows):
-    columns = normalized.shape[1]
-    half = out_weight.shape[1] // 2
-
-    def body(normalized_ref, weight_ref, *parts):
-        project_out(normalized_ref[: blocks * rows, :], weight_ref, parts, rows)
-
-    out = call(
-        body,
-        [jax.ShapeDtypeStruct((rows, half), BF16)] * (2 * blocks),
-        [VMEM] * 2,
-        [VMEM] * (2 * blocks),
-        flops=HOP_FLOPS,
-        nbytes=4 * half * columns,
-        name="project_rest",
-    )(normalized, out_weight)
-    return [out[2 * block : 2 * block + 2] for block in range(blocks)]
+    return [out[2 * at : 2 * at + 2] for at in range(count // block)]
 
 
 def add_step(mine, got):
@@ -456,12 +440,10 @@
     halves = (first_rows, second_rows)
     feat_q, within = queries_within(halves, qkv_weight, feat_k, values, head_dim, n_fsdp, rows)
     exchanged = exchange_states(states, n_ctx)
-    soon = 1
-    normalized, parts = attend_and_project(
-        feat_q, within, initial_state, exchanged, norm_gain, out_weight, soon, rows, head_dim
-    )
-    parts = project_rest(normalized, out_weight, n_fsdp - soon, rows) + parts
-
+    last = n_rows - rows
+    common = (feat_q, within, initial_state, exchanged, norm_gain, out_weight, rows, head_dim)
+    farthest = attend_and_project(slice(last, n_rows), *common, 2 * rows * columns * width, "attend_farthest")
+    parts = attend_and_project(slice(0, last), *common, HOP_FLOPS, "attend_rest") + farthest
     mirrored = [distance if distance == n_fsdp // 2 else -distance for distance in order]
     return ring_scatter(parts, mirrored, left, right)
 

time: 79.5 us -> 79.7 us (level)
    ppermute x7, waiting for transfers between devices: 7.75 us -> 6.62 us  [hop(): lax.ppermute(to_right, 'fsdp', right)]
    ppermute x7, waiting for transfers between devices: 6.8 us -> 7.63 us  [hop(): lax.ppermute(to_left, 'fsdp', left)]
  transfers between devices with their start and end apart: 32 -> 32, of which waited for: 16 -> 16; matrix products, arithmetic and copies ran while one was open for 0% -> 0% of each run, Pallas kernels for 11% -> 12%
where the time goes in v17:
time: 79.7 us; the launch traced here: 79.6 us
  starting transfers between devices  33.9 us (43%)
  waiting for transfers between devices  31.9 us (40%)
  Pallas kernels  12.4 us (16%)
  local copies, waits for them, and re-layouts  1.09 us (1%)
    ppermute x6, starting transfers between devices, ring_gather(): going_left[1 - part] = lax.ppermute(going_left[1 - part], 'fsdp', left)  12.8 us
    ppermute x7, starting transfers between devices, hop(): lax.ppermute(to_right, 'fsdp', right)  11.5 us
    ppermute x6, waiting for transfers between devices, ring_gather(): going_left[1 - part] = lax.ppermute(going_left[1 - part], 'fsdp', left)  9.87 us
    ppermute x7, waiting for transfers between devices, hop(): lax.ppermute(to_left, 'fsdp', left)  7.63 us
    ppermute x7, waiting for transfers between devices, hop(): lax.ppermute(to_right, 'fsdp', right)  6.62 us
    ppermute x6, waiting for transfers between devices, ring_gather(): going_right[part] = lax.ppermute(going_right[part], 'fsdp', right)  4.25 us
    ppermute x7, starting transfers between devices, hop(): lax.ppermute(to_left, 'fsdp', left)  3.82 us
    pallas_call x2, Pallas kernels, attend_and_project(): call(body, [jax.ShapeDtypeStruct((block, half), BF16)] * n_parts, [VMEM]...  3.36 us
  transfers between devices with their start and end apart: 32, of which 16 were waited for; matrix products, arithmetic and copies ran while one was open for 0% of the time, Pallas kernels for 12%

profile of v17, /device:TPU:0, one launch (start us, length us, event | category | flops | bytes accessed | tf_op | source)
XLA Modules:
  0.0 79.6 jit_solution(10088139281781889043)
XLA Ops:
  0.0 1.0 %fusion = (bf16[32,3072]{1,0:T(8,128)(2,1)S(1)}, bf16[32,3072]{1,0:T(8,128)(2,1)S(1)}) fusion(bf16[32,6144]{1,0:T(8,128)(2,1)} %param.5), kind=kLoop, calls=%fused_computation | loop fusion | bytes 786432 | tf_op jit(solution)/shard_map/slice | solution.py:68
  1.1 3.0 %collective-permute-start.10 = (bf16[32,3072]{1,0:T(8,128)(2,1)S(1)}, bf16[32,3072]{1,0:T(8,128)(2,1)S(1)}, u32[]{:S(2)}, u32[]{:S(2)}) collective-permute-start(bf16[32,3072]{1,0:T(8,128)(2,1)S(1)} %get-tuple-element.71.refs_5_), channel_id=1, source_target_pairs={{2,0},{4,2},{6,4},{7,6},{5,7},{3,5},{1,3},{0,1},{10,8},{12,10},{14... | collective-permute-start | bytes 589832 | tf_op jit(solution)/shard_map/ppermute | solution.py:74
  4.2 1.9 %collective-permute-start.4 = (bf16[32,3072]{1,0:T(8,128)(2,1)S(1)}, bf16[32,3072]{1,0:T(8,128)(2,1)S(1)}, u32[]{:S(2)}, u32[]{:S(2)}) collective-permute-start(bf16[32,3072]{1,0:T(8,128)(2,1)S(1)} %get-tuple-element.72.refs_0_), channel_id=1, source_target_pairs={{2,0},{4,2},{6,4},{7,6},{5,7},{3,5},{1,3},{0,1},{10,8},{12,10},{14... | collective-permute-start | bytes 589832 | tf_op jit(solution)/shard_map/ppermute | solution.py:74
  6.2 3.6 %collective-permute-done.10.refs_7_.arrived_ref = bf16[32,3072]{1,0:T(8,128)(2,1)S(1)} collective-permute-done((bf16[32,3072]{1,0:T(8,128)(2,1)S(1)}, bf16[32,3072]{1,0:T(8,128)(2,1)S(1)}, u32[]{:S(2)}, u32[]{:S(2)}) %collective-permute-start.10) | collective-permute-done | bytes 196640 | tf_op jit(solution)/shard_map/ppermute | solution.py:74
  9.9 2.0 %collective-permute-start.11 = (bf16[32,3072]{1,0:T(8,128)(2,1)S(1)}, bf16[32,3072]{1,0:T(8,128)(2,1)S(1)}, u32[]{:S(2)}, u32[]{:S(2)}) collective-permute-start(bf16[32,3072]{1,0:T(8,128)(2,1)S(1)} %collective-permute-done.10.refs_7_.arrived_ref), channel_id=1, source_target_pairs={{2,0},{4,2},{6,4},{7,6},{5,7},{3,5},{1,3},{0,1},{10,8},{12,10},{14... | collective-permute-start | bytes 589832 | tf_op jit(solution)/shard_map/ppermute | solution.py:74
  12.0 2.1 %collective-permute-done.4.refs_2_ = bf16[32,3072]{1,0:T(8,128)(2,1)S(1)} collective-permute-done((bf16[32,3072]{1,0:T(8,128)(2,1)S(1)}, bf16[32,3072]{1,0:T(8,128)(2,1)S(1)}, u32[]{:S(2)}, u32[]{:S(2)}) %collective-permute-start.4) | collective-permute-done | bytes 196640 | tf_op jit(solution)/shard_map/ppermute | solution.py:74
  14.1 2.0 %collective-permute-start.5 = (bf16[32,3072]{1,0:T(8,128)(2,1)S(1)}, bf16[32,3072]{1,0:T(8,128)(2,1)S(1)}, u32[]{:S(2)}, u32[]{:S(2)}) collective-permute-start(bf16[32,3072]{1,0:T(8,128)(2,1)S(1)} %collective-permute-done.4.refs_2_), channel_id=1, source_target_pairs={{2,0},{4,2},{6,4},{7,6},{5,7},{3,5},{1,3},{0,1},{10,8},{12,10},{14... | collective-permute-start | bytes 589832 | tf_op jit(solution)/shard_map/ppermute | solution.py:74
  16.2 2.1 %collective-permute-done.11.refs_9_ = bf16[32,3072]{1,0:T(8,128)(2,1)S(1)} collective-permute-done((bf16[32,3072]{1,0:T(8,128)(2,1)S(1)}, bf16[32,3072]{1,0:T(8,128)(2,1)S(1)}, u32[]{:S(2)}, u32[]{:S(2)}) %collective-permute-start.11) | collective-permute-done | bytes 196640 | tf_op jit(solution)/shard_map/ppermute | solution.py:74
  18.3 2.0 %collective-permute-start.12 = (bf16[32,3072]{1,0:T(8,128)(2,1)S(1)}, bf16[32,3072]{1,0:T(8,128)(2,1)S(1)}, u32[]{:S(2)}, u32[]{:S(2)}) collective-permute-start(bf16[32,3072]{1,0:T(8,128)(2,1)S(1)} %collective-permute-done.11.refs_9_), channel_id=1, source_target_pairs={{2,0},{4,2},{6,4},{7,6},{5,7},{3,5},{1,3},{0,1},{10,8},{12,10},{14... | collective-permute-start | bytes 589832 | tf_op jit(solution)/shard_map/ppermute | solution.py:74
  20.4 2.1 %collective-permute-done.5.refs_4_ = bf16[32,3072]{1,0:T(8,128)(2,1)S(1)} collective-permute-done((bf16[32,3072]{1,0:T(8,128)(2,1)S(1)}, bf16[32,3072]{1,0:T(8,128)(2,1)S(1)}, u32[]{:S(2)}, u32[]{:S(2)}) %collective-permute-start.5) | collective-permute-done | bytes 196640 | tf_op jit(solution)/shard_map/ppermute | solution.py:74
  22.5 2.0 %collective-permute-start.6 = (bf16[32,3072]{1,0:T(8,128)(2,1)S(1)}, bf16[32,3072]{1,0:T(8,128)(2,1)S(1)}, u32[]{:S(2)}, u32[]{:S(2)}) collective-permute-start(bf16[32,3072]{1,0:T(8,128)(2,1)S(1)} %collective-permute-done.5.refs_4_), channel_id=1, source_target_pairs={{2,0},{4,2},{6,4},{7,6},{5,7},{3,5},{1,3},{0,1},{10,8},{12,10},{14... | collective-permute-start | bytes 589832 | tf_op jit(solution)/shard_map/ppermute | solution.py:74
  24.6 4.1 %collective-permute-done.2.refs_0_ = bf16[32,3072]{1,0:T(8,128)(2,1)S(1)} collective-permute-done((bf16[32,3072]{1,0:T(8,128)(2,1)S(1)}, bf16[32,3072]{1,0:T(8,128)(2,1)S(1)}, u32[]{:S(2)}, u32[]{:S(2)}) %collective-permute-start.2) | collective-permute-done | bytes 196640 | tf_op jit(solution)/shard_map/ppermute | solution.py:73
  28.8 1.9 %collective-permute-start.13 = (bf16[32,3072]{1,0:T(8,128)(2,1)S(1)}, bf16[32,3072]{1,0:T(8,128)(2,1)S(1)}, u32[]{:S(2)}, u32[]{:S(2)}) collective-permute-start(bf16[32,3072]{1,0:T(8,128)(2,1)S(1)} %collective-permute-done.12.refs_11_.refs_3_), channel_id=1, source_target_pairs={{2,0},{4,2},{6,4},{7,6},{5,7},{3,5},{1,3},{0,1},{10,8},{12,10},{14... | collective-permute-start | bytes 589832 | tf_op jit(solution)/shard_map/ppermute | solution.py:78
  30.8 1.2 %early_keys.1 = (bf16[256,512]{1,0:T(8,128)(2,1)S(1)}, bf16[256,3072]{1,0:T(8,128)(2,1)S(1)}, bf16[256,3072]{1,0:T(8,128)(2,1)S(1)}) custom-call(bf16[32,3072]{1,0:T(8,128)(2,1)S(1)} %get-tuple-element.72.refs_0_, bf16[32,3072]{1,0:T(8,128)(2,1)S(1)} %collective-permute-done.refs_1_.arrived_ref, bf16[32,3072]{1,0:T(8,128)(2,1)S(1)} %collective-permute-done.4.refs_2_, ...), custom_call_target="tpu_custom_call" | custom-call | flops 1006632960 | bytes 6291456 | tf_op jit(solution)/shard_map/early_keys/pallas_call | solution.py:106
  32.0 1.2 %early_values.1.refs_6_.refs_5_ = bf16[256,512]{1,0:T(8,128)(2,1)S(1)} custom-call(bf16[256,3072]{1,0:T(8,128)(2,1)S(1)} %get-tuple-element.38.first_ref.refs_4_, bf16[256,3072]{1,0:T(8,128)(2,1)S(1)} %get-tuple-element.39.second_ref.refs_5_, bf16[3,6144,512]{2,1,0:T(8,128)(2,1)S(1)} %bitcast.2), custom_call_target="tpu_custom_call" | custom-call | flops 1006632960 | bytes 6291456 | tf_op jit(solution)/shard_map/early_values/pallas_call | solution.py:126
  33.3 2.4 %collective-permute-done.3.refs_0_ = bf16[32,3072]{1,0:T(8,128)(2,1)S(1)} collective-permute-done((bf16[32,3072]{1,0:T(8,128)(2,1)S(1)}, bf16[32,3072]{1,0:T(8,128)(2,1)S(1)}, u32[]{:S(2)}, u32[]{:S(2)}) %collective-permute-start.3) | collective-permute-done | bytes 196640 | tf_op jit(solution)/shard_map/ppermute | solution.py:77
  35.7 1.1 %first_pass.1 = (bf16[256,3072]{1,0:T(8,128)(2,1)S(1)}, f32[2,96,512]{2,1,0:T(8,128)S(1)}) custom-call(bf16[32,3072]{1,0:T(8,128)(2,1)S(1)} %collective-permute-done.3.refs_0_, bf16[256,3072]{1,0:T(8,128)(2,1)S(1)} %get-tuple-element.40.refs_1_, bf16[3,6144,512]{2,1,0:T(8,128)(2,1)S(1)} %bitcast.2, ...), custom_call_target="tpu_custom_call", output_to_operand_aliasing={{0}: (1, {})} | custom-call | flops 603979776 | bytes 6291456 | tf_op jit(solution)/shard_map/first_pass/pallas_call | solution.py:166
  36.8 0.9 %late_keys_and_values.2 = (bf16[256,3072]{1,0:T(8,128)(2,1)S(1)}, bf16[256,512]{1,0:T(8,128)(2,1)S(1)}, bf16[256,512]{1,0:T(8,128)(2,1)S(1)}, bf16[2,128,128]{2,1,0:T(8,128)(2,1)S(1)}) custom-call(bf16[32,3072]{1,0:T(8,128)(2,1)S(1)} %collective-permute-done.13.refs_0_, ...), custom_call_target="tpu_custom_call", output_to_operand_aliasing={{0}: (1, {}), {1}: (4, {}), {2}: (5, {})} | custom-call | flops 301989888 | bytes 3145728 | tf_op jit(solution)/shard_map/late_keys_and_values/pallas_call | solution.py:206
  37.8 0.9 %late_keys_and_values.3 = (bf16[256,3072]{1,0:T(8,128)(2,1)S(1)}, bf16[256,512]{1,0:T(8,128)(2,1)S(1)}, bf16[256,512]{1,0:T(8,128)(2,1)S(1)}, bf16[2,128,128]{2,1,0:T(8,128)(2,1)S(1)}) custom-call(bf16[256,3072]{1,0:T(8,128)(2,1)S(1)} %get-tuple-element.45.refs_0_, ...), custom_call_target="tpu_custom_call", output_to_operand_aliasing={{0}: (0, {}), {1}: (3, {}), {2}: (4, {})} | custom-call | flops 5000000000 | bytes 3145728 | tf_op jit(solution)/shard_map/late_keys_and_values/pallas_call | solution.py:206
  38.7 0.6 collective-permute-start.16
  39.2 1.6 %collective-permute-start.15 = (bf16[2,128,128]{2,1,0:T(8,128)(2,1)S(1)}, bf16[2,128,128]{2,1,0:T(8,128)(2,1)S(1)}, u32[]{:S(2)}, u32[]{:S(2)}) collective-permute-start(bf16[2,128,128]{2,1,0:T(8,128)(2,1)S(1)} %add_states.2.refs_0_), channel_id=1, source_target_pairs={{0,16},{8,24},{16,0},{24,8},{1,17},{9,25},{17,1},{25,9},{2,18},{10... | collective-permute-start | bytes 196616 | tf_op jit(solution)/shard_map/ppermute | solution.py:405
  40.8 0.9 %collective-permute-start.17 = (bf16[2,128,128]{2,1,0:T(8,128)(2,1)S(1)}, bf16[2,128,128]{2,1,0:T(8,128)(2,1)S(1)}, u32[]{:S(2)}, u32[]{:S(2)}) collective-permute-start(bf16[2,128,128]{2,1,0:T(8,128)(2,1)S(1)} %add_states.3), channel_id=1, source_target_pairs={{0,16},{8,24},{16,0},{24,8},{1,17},{9,25},{17,1},{25,9},{2,18},{10... | collective-permute-start | bytes 196616 | tf_op jit(solution)/shard_map/ppermute | solution.py:405
  41.7 2.3 %queries_within.1 = (bf16[256,512]{1,0:T(8,128)(2,1)S(1)}, f32[256,512]{1,0:T(8,128)S(1)}) custom-call(bf16[256,3072]{1,0:T(8,128)(2,1)S(1)} %get-tuple-element.42.first_ref, bf16[256,3072]{1,0:T(8,128)(2,1)S(1)} %get-tuple-element.48.second_ref, bf16[3,6144,512]{2,1,0:T(8,128)(2,1)S(1)} %bitcast.2, bf16[256,512]{1,0:T(8,128)(2,1)S(1)} %get-tuple-element.49.k_ref, ...), custom_call_target="tpu_custom_call" | custom-call | flops 1744830464 | bytes 6291456 | tf_op jit(solution)/shard_map/queries_within/pallas_call | solution.py:249
  44.0 1.1 %collective-permute-done.17.refs_3_ = bf16[2,128,128]{2,1,0:T(8,128)(2,1)S(1)} collective-permute-done((bf16[2,128,128]{2,1,0:T(8,128)(2,1)S(1)}, bf16[2,128,128]{2,1,0:T(8,128)(2,1)S(1)}, u32[]{:S(2)}, u32[]{:S(2)}) %collective-permute-start.17) | collective-permute-done | bytes 65568 | tf_op jit(solution)/shard_map/ppermute | solution.py:405
  45.2 1.4 %attend_farthest.1 = (bf16[32,3072]{1,0:T(8,128)(2,1)S(1)}, bf16[32,3072]{1,0:T(8,128)(2,1)S(1)}) custom-call(bf16[256,512]{1,0:T(8,128)(2,1)S(1)} %get-tuple-element.51.q_ref, f32[256,512]{1,0:T(8,128)S(1)} %get-tuple-element.52.within_ref, f32[4,128,128]{2,1,0:T(8,128)S(1)} %copy-done, f32[1,512]{1,0:T(1,128)S(1)} %bitcast.5, ...), custom_call_target="tpu_custom_call" | custom-call | flops 201326592 | bytes 6291456 | tf_op jit(solution)/shard_map/attend_farthest/pallas_call | solution.py:299
  46.7 0.6 collective-permute-start.28
  47.2 1.5 %collective-permute-start.24 = (bf16[32,3072]{1,0:T(8,128)(2,1)S(1)}, bf16[32,3072]{1,0:T(8,128)(2,1)S(1)}, u32[]{:S(2)}, u32[]{:S(2)}) collective-permute-start(bf16[32,3072]{1,0:T(8,128)(2,1)S(1)} %get-tuple-element.66), channel_id=1, source_target_pairs={{2,0},{4,2},{6,4},{7,6},{5,7},{3,5},{1,3},{0,1},{10,8},{12,10},{14... | collective-permute-start | bytes 589832 | tf_op jit(solution)/shard_map/ppermute | solution.py:369
  48.7 1.9 %attend_rest.1 = (bf16[32,3072]{1,0:T(8,128)(2,1)S(1)}, bf16[32,3072]{1,0:T(8,128)(2,1)S(1)}, bf16[32,3072]{1,0:T(8,128)(2,1)S(1)}, bf16[32,3072]{1,0:T(8,128)(2...) custom-call(bf16[256,512]{1,0:T(8,128)(2,1)S(1)} %get-tuple-element., ...), custom_call_target="tpu_custom_call" | custom-call | flops 5000000000 | bytes 6291456 | tf_op jit(solution)/shard_map/attend_rest/pallas_call | solution.py:299
  50.6 1.6 %collective-permute-start.21 = (bf16[32,3072]{1,0:T(8,128)(2,1)S(1)}, bf16[32,3072]{1,0:T(8,128)(2,1)S(1)}, u32[]{:S(2)}, u32[]{:S(2)}) collective-permute-start(bf16[32,3072]{1,0:T(8,128)(2,1)S(1)} %get-tuple-element.62), channel_id=1, source_target_pairs={{2,0},{4,2},{6,4},{7,6},{5,7},{3,5},{1,3},{0,1},{10,8},{12,10},{14... | collective-permute-start | bytes 589832 | tf_op jit(solution)/shard_map/ppermute | solution.py:369
  52.3 0.4 collective-permute-start.18
  53.0 0.6 collective-permute-start.29
  53.6 0.6 collective-permute-done.24.got_ref
  54.2 1.4 %collective-permute-start.25 = (bf16[32,3072]{1,0:T(8,128)(2,1)S(1)}, bf16[32,3072]{1,0:T(8,128)(2,1)S(1)}, u32[]{:S(2)}, u32[]{:S(2)}) collective-permute-start(bf16[32,3072]{1,0:T(8,128)(2,1)S(1)} %add_step.14), channel_id=1, source_target_pairs={{2,0},{4,2},{6,4},{7,6},{5,7},{3,5},{1,3},{0,1},{10,8},{12,10},{14... | collective-permute-start | bytes 589832 | tf_op jit(solution)/shard_map/ppermute | solution.py:369
  55.6 2.9 %collective-permute-done.21.got_ref = bf16[32,3072]{1,0:T(8,128)(2,1)S(1)} collective-permute-done((bf16[32,3072]{1,0:T(8,128)(2,1)S(1)}, bf16[32,3072]{1,0:T(8,128)(2,1)S(1)}, u32[]{:S(2)}, u32[]{:S(2)}) %collective-permute-start.21) | collective-permute-done | bytes 196640 | tf_op jit(solution)/shard_map/ppermute | solution.py:369
  58.6 1.6 %collective-permute-start.22 = (bf16[32,3072]{1,0:T(8,128)(2,1)S(1)}, bf16[32,3072]{1,0:T(8,128)(2,1)S(1)}, u32[]{:S(2)}, u32[]{:S(2)}) collective-permute-start(bf16[32,3072]{1,0:T(8,128)(2,1)S(1)} %add_step.12), channel_id=1, source_target_pairs={{2,0},{4,2},{6,4},{7,6},{5,7},{3,5},{1,3},{0,1},{10,8},{12,10},{14... | collective-permute-start | bytes 589832 | tf_op jit(solution)/shard_map/ppermute | solution.py:369
  60.3 0.8 %collective-permute-start.19 = (bf16[32,3072]{1,0:T(8,128)(2,1)S(1)}, bf16[32,3072]{1,0:T(8,128)(2,1)S(1)}, u32[]{:S(2)}, u32[]{:S(2)}) collective-permute-start(bf16[32,3072]{1,0:T(8,128)(2,1)S(1)} %add_step.10), channel_id=1, source_target_pairs={{0,2},{2,4},{4,6},{6,7},{7,5},{5,3},{3,1},{1,0},{8,10},{10,12},{12... | collective-permute-start | bytes 589832 | tf_op jit(solution)/shard_map/ppermute | solution.py:369
  61.1 2.3 %collective-permute-done.29.got_ref = bf16[32,3072]{1,0:T(8,128)(2,1)S(1)} collective-permute-done((bf16[32,3072]{1,0:T(8,128)(2,1)S(1)}, bf16[32,3072]{1,0:T(8,128)(2,1)S(1)}, u32[]{:S(2)}, u32[]{:S(2)}) %collective-permute-start.29) | collective-permute-done | bytes 196640 | tf_op jit(solution)/shard_map/ppermute | solution.py:369
  63.5 0.3 collective-permute-start.30
  63.8 1.8 %collective-permute-start.26 = (bf16[32,3072]{1,0:T(8,128)(2,1)S(1)}, bf16[32,3072]{1,0:T(8,128)(2,1)S(1)}, u32[]{:S(2)}, u32[]{:S(2)}) collective-permute-start(bf16[32,3072]{1,0:T(8,128)(2,1)S(1)} %add_step.15), channel_id=1, source_target_pairs={{2,0},{4,2},{6,4},{7,6},{5,7},{3,5},{1,3},{0,1},{10,8},{12,10},{14... | collective-permute-start | bytes 589832 | tf_op jit(solution)/shard_map/ppermute | solution.py:369
  65.7 1.3 %collective-permute-done.22.got_ref = bf16[32,3072]{1,0:T(8,128)(2,1)S(1)} collective-permute-done((bf16[32,3072]{1,0:T(8,128)(2,1)S(1)}, bf16[32,3072]{1,0:T(8,128)(2,1)S(1)}, u32[]{:S(2)}, u32[]{:S(2)}) %collective-permute-start.22) | collective-permute-done | bytes 196640 | tf_op jit(solution)/shard_map/ppermute | solution.py:369
  67.0 1.6 %collective-permute-start.23 = (bf16[32,3072]{1,0:T(8,128)(2,1)S(1)}, bf16[32,3072]{1,0:T(8,128)(2,1)S(1)}, u32[]{:S(2)}, u32[]{:S(2)}) collective-permute-start(bf16[32,3072]{1,0:T(8,128)(2,1)S(1)} %add_step.13), channel_id=1, source_target_pairs={{2,0},{4,2},{6,4},{7,6},{5,7},{3,5},{1,3},{0,1},{10,8},{12,10},{14... | collective-permute-start | bytes 589832 | tf_op jit(solution)/shard_map/ppermute | solution.py:369
  68.7 0.8 %collective-permute-start.20 = (bf16[32,3072]{1,0:T(8,128)(2,1)S(1)}, bf16[32,3072]{1,0:T(8,128)(2,1)S(1)}, u32[]{:S(2)}, u32[]{:S(2)}) collective-permute-start(bf16[32,3072]{1,0:T(8,128)(2,1)S(1)} %add_step.11), channel_id=1, source_target_pairs={{0,2},{2,4},{4,6},{6,7},{7,5},{5,3},{3,1},{1,0},{8,10},{10,12},{12... | collective-permute-start | bytes 589832 | tf_op jit(solution)/shard_map/ppermute | solution.py:369
  69.5 2.3 %collective-permute-done.30.got_ref = bf16[32,3072]{1,0:T(8,128)(2,1)S(1)} collective-permute-done((bf16[32,3072]{1,0:T(8,128)(2,1)S(1)}, bf16[32,3072]{1,0:T(8,128)(2,1)S(1)}, u32[]{:S(2)}, u32[]{:S(2)}) %collective-permute-start.30) | collective-permute-done | bytes 196640 | tf_op jit(solution)/shard_map/ppermute | solution.py:369
  72.3 1.8 %collective-permute-start.27 = (bf16[32,3072]{1,0:T(8,128)(2,1)S(1)}, bf16[32,3072]{1,0:T(8,128)(2,1)S(1)}, u32[]{:S(2)}, u32[]{:S(2)}) collective-permute-start(bf16[32,3072]{1,0:T(8,128)(2,1)S(1)} %add_step.16), channel_id=1, source_target_pairs={{2,0},{4,2},{6,4},{7,6},{5,7},{3,5},{1,3},{0,1},{10,8},{12,10},{14... | collective-permute-start | bytes 589832 | tf_op jit(solution)/shard_map/ppermute | solution.py:369
  74.1 1.9 %collective-permute-done.23.got_second = bf16[32,3072]{1,0:T(8,128)(2,1)S(1)} collective-permute-done((bf16[32,3072]{1,0:T(8,128)(2,1)S(1)}, bf16[32,3072]{1,0:T(8,128)(2,1)S(1)}, u32[]{:S(2)}, u32[]{:S(2)}) %collective-permute-start.23) | collective-permute-done | bytes 196640 | tf_op jit(solution)/shard_map/ppermute | solution.py:369
  75.9 0.6 collective-permute-done.20.got_first
  76.7 2.1 %collective-permute-done.31.second = bf16[32,3072]{1,0:T(8,128)(2,1)S(1)} collective-permute-done((bf16[32,3072]{1,0:T(8,128)(2,1)S(1)}, bf16[32,3072]{1,0:T(8,128)(2,1)S(1)}, u32[]{:S(2)}, u32[]{:S(2)}) %collective-permute-start.31) | collective-permute-done | bytes 196640 | tf_op jit(solution)/shard_map/ppermute | solution.py:369
  78.8 0.8 %finish.1 = bf16[32,6144]{1,0:T(8,128)(2,1)} custom-call(f32[2,32,3072]{2,1,0:T(8,128)S(1)} %add_own.1.gathered_ref, bf16[32,3072]{1,0:T(8,128)(2,1)S(1)} %collective-permute-done.27.first, bf16[32,3072]{1,0:T(8,128)(2,1)S(1)} %collective-permute-done.31.second), custom_call_target="tpu_custom_call" | custom-call | bytes 393216 | tf_op jit(solution)/shard_map/finish/pallas_call | solution.py:351
  (62 shorter events, 2.3 us)
Async XLA Ops:
  1.1 8.8 %collective-permute-start.10 = (bf16[32,3072]{1,0:T(8,128)(2,1)S(1)}, bf16[32,3072]{1,0:T(8,128)(2,1)S(1)}, u32[]{:S(2)}, u32[]{:S(2)}) collective-permute-start(bf16[32,3072]{1,0:T(8,128)(2,1)S(1)} %get-tuple-element.71.refs_5_), channel_id=1, source_target_pairs={{2,0},{4,2},{6,4},{7,6},{5,7},{3,5},{1,3},{0,1},{10,8},{12,10},{14... | collective-permute-start | bytes 589832 | tf_op jit(solution)/shard_map/ppermute | solution.py:74
  4.0 7.8 %collective-permute-start = (bf16[32,3072]{1,0:T(8,128)(2,1)S(1)}, bf16[32,3072]{1,0:T(8,128)(2,1)S(1)}, u32[]{:S(2)}, u32[]{:S(2)}) collective-permute-start(bf16[32,3072]{1,0:T(8,128)(2,1)S(1)} %get-tuple-element.72.refs_0_), channel_id=1, source_target_pairs={{0,2},{2,4},{4,6},{6,7},{7,5},{5,3},{3,1},{1,0},{8,10},{10,12},{12... | collective-permute-start | bytes 589832 | tf_op jit(solution)/shard_map/ppermute | solution.py:73
  4.2 9.9 %collective-permute-start.4 = (bf16[32,3072]{1,0:T(8,128)(2,1)S(1)}, bf16[32,3072]{1,0:T(8,128)(2,1)S(1)}, u32[]{:S(2)}, u32[]{:S(2)}) collective-permute-start(bf16[32,3072]{1,0:T(8,128)(2,1)S(1)} %get-tuple-element.72.refs_0_), channel_id=1, source_target_pairs={{2,0},{4,2},{6,4},{7,6},{5,7},{3,5},{1,3},{0,1},{10,8},{12,10},{14... | collective-permute-start | bytes 589832 | tf_op jit(solution)/shard_map/ppermute | solution.py:74
  6.1 10.0 %collective-permute-start.7 = (bf16[32,3072]{1,0:T(8,128)(2,1)S(1)}, bf16[32,3072]{1,0:T(8,128)(2,1)S(1)}, u32[]{:S(2)}, u32[]{:S(2)}) collective-permute-start(bf16[32,3072]{1,0:T(8,128)(2,1)S(1)} %get-tuple-element.71.refs_5_), channel_id=1, source_target_pairs={{0,2},{2,4},{4,6},{6,7},{7,5},{5,3},{3,1},{1,0},{8,10},{10,12},{12... | collective-permute-start | bytes 589832 | tf_op jit(solution)/shard_map/ppermute | solution.py:73
  9.9 8.4 %collective-permute-start.11 = (bf16[32,3072]{1,0:T(8,128)(2,1)S(1)}, bf16[32,3072]{1,0:T(8,128)(2,1)S(1)}, u32[]{:S(2)}, u32[]{:S(2)}) collective-permute-start(bf16[32,3072]{1,0:T(8,128)(2,1)S(1)} %collective-permute-done.10.refs_7_.arrived_ref), channel_id=1, source_target_pairs={{2,0},{4,2},{6,4},{7,6},{5,7},{3,5},{1,3},{0,1},{10,8},{12,10},{14... | collective-permute-start | bytes 589832 | tf_op jit(solution)/shard_map/ppermute | solution.py:74
  11.9 8.4 %collective-permute-start.1 = (bf16[32,3072]{1,0:T(8,128)(2,1)S(1)}, bf16[32,3072]{1,0:T(8,128)(2,1)S(1)}, u32[]{:S(2)}, u32[]{:S(2)}) collective-permute-start(bf16[32,3072]{1,0:T(8,128)(2,1)S(1)} %collective-permute-done.refs_1_.arrived_ref), channel_id=1, source_target_pairs={{0,2},{2,4},{4,6},{6,7},{7,5},{5,3},{3,1},{1,0},{8,10},{10,12},{12... | collective-permute-start | bytes 589832 | tf_op jit(solution)/shard_map/ppermute | solution.py:73
  14.1 8.4 %collective-permute-start.5 = (bf16[32,3072]{1,0:T(8,128)(2,1)S(1)}, bf16[32,3072]{1,0:T(8,128)(2,1)S(1)}, u32[]{:S(2)}, u32[]{:S(2)}) collective-permute-start(bf16[32,3072]{1,0:T(8,128)(2,1)S(1)} %collective-permute-done.4.refs_2_), channel_id=1, source_target_pairs={{2,0},{4,2},{6,4},{7,6},{5,7},{3,5},{1,3},{0,1},{10,8},{12,10},{14... | collective-permute-start | bytes 589832 | tf_op jit(solution)/shard_map/ppermute | solution.py:74
  16.1 8.4 %collective-permute-start.8 = (bf16[32,3072]{1,0:T(8,128)(2,1)S(1)}, bf16[32,3072]{1,0:T(8,128)(2,1)S(1)}, u32[]{:S(2)}, u32[]{:S(2)}) collective-permute-start(bf16[32,3072]{1,0:T(8,128)(2,1)S(1)} %collective-permute-done.7.refs_6_), channel_id=1, source_target_pairs={{0,2},{2,4},{4,6},{6,7},{7,5},{5,3},{3,1},{1,0},{8,10},{10,12},{12... | collective-permute-start | bytes 589832 | tf_op jit(solution)/shard_map/ppermute | solution.py:73
  16.2 14.6 %slice-start = ((s8[18874368]{0:T(1024)(128)(4,1)}), s8[4194304]{0:T(1024)(128)(4,1)S(1)}, s32[]{:S(2)}) async-start(s8[18874368]{0:T(1024)(128)(4,1)} %bitcast.1), calls=%async_computation | async-start | bytes 8388608
  16.2 14.6 %slice-start.1 = ((s8[18874368]{0:T(1024)(128)(4,1)}), s8[4194304]{0:T(1024)(128)(4,1)S(1)}, s32[]{:S(2)}) async-start(s8[18874368]{0:T(1024)(128)(4,1)} %bitcast.1), calls=%async_computation.1 | async-start | bytes 8388608
  16.2 14.6 %slice-start.2 = ((s8[18874368]{0:T(1024)(128)(4,1)}), s8[4194304]{0:T(1024)(128)(4,1)S(1)}, s32[]{:S(2)}) async-start(s8[18874368]{0:T(1024)(128)(4,1)} %bitcast.1), calls=%async_computation.2 | async-start | bytes 8388608
  16.2 14.6 %slice-start.3 = ((s8[18874368]{0:T(1024)(128)(4,1)}), s8[4194304]{0:T(1024)(128)(4,1)S(1)}, s32[]{:S(2)}) async-start(s8[18874368]{0:T(1024)(128)(4,1)} %bitcast.1), calls=%async_computation.3 | async-start | bytes 8388608
  16.2 14.5 %slice-start.4 = ((s8[18874368]{0:T(1024)(128)(4,1)}), s8[2097152]{0:T(1024)(128)(4,1)S(1)}, s32[]{:S(2)}) async-start(s8[18874368]{0:T(1024)(128)(4,1)} %bitcast.1), calls=%async_computation.4 | async-start | bytes 4194304
  18.3 10.6 %collective-permute-start.12 = (bf16[32,3072]{1,0:T(8,128)(2,1)S(1)}, bf16[32,3072]{1,0:T(8,128)(2,1)S(1)}, u32[]{:S(2)}, u32[]{:S(2)}) collective-permute-start(bf16[32,3072]{1,0:T(8,128)(2,1)S(1)} %collective-permute-done.11.refs_9_), channel_id=1, source_target_pairs={{2,0},{4,2},{6,4},{7,6},{5,7},{3,5},{1,3},{0,1},{10,8},{12,10},{14... | collective-permute-start | bytes 589832 | tf_op jit(solution)/shard_map/ppermute | solution.py:74
  20.3 8.4 %collective-permute-start.2 = (bf16[32,3072]{1,0:T(8,128)(2,1)S(1)}, bf16[32,3072]{1,0:T(8,128)(2,1)S(1)}, u32[]{:S(2)}, u32[]{:S(2)}) collective-permute-start(bf16[32,3072]{1,0:T(8,128)(2,1)S(1)} %collective-permute-done.1.refs_3_), channel_id=1, source_target_pairs={{0,2},{2,4},{4,6},{6,7},{7,5},{5,3},{3,1},{1,0},{8,10},{10,12},{12... | collective-permute-start | bytes 589832 | tf_op jit(solution)/shard_map/ppermute | solution.py:73
  22.5 10.7 %collective-permute-start.6 = (bf16[32,3072]{1,0:T(8,128)(2,1)S(1)}, bf16[32,3072]{1,0:T(8,128)(2,1)S(1)}, u32[]{:S(2)}, u32[]{:S(2)}) collective-permute-start(bf16[32,3072]{1,0:T(8,128)(2,1)S(1)} %collective-permute-done.5.refs_4_), channel_id=1, source_target_pairs={{2,0},{4,2},{6,4},{7,6},{5,7},{3,5},{1,3},{0,1},{10,8},{12,10},{14... | collective-permute-start | bytes 589832 | tf_op jit(solution)/shard_map/ppermute | solution.py:74
  24.5 8.7 %collective-permute-start.9 = (bf16[32,3072]{1,0:T(8,128)(2,1)S(1)}, bf16[32,3072]{1,0:T(8,128)(2,1)S(1)}, u32[]{:S(2)}, u32[]{:S(2)}) collective-permute-start(bf16[32,3072]{1,0:T(8,128)(2,1)S(1)} %collective-permute-done.8.refs_8_), channel_id=1, source_target_pairs={{0,2},{2,4},{4,6},{6,7},{7,5},{5,3},{3,1},{1,0},{8,10},{10,12},{12... | collective-permute-start | bytes 589832 | tf_op jit(solution)/shard_map/ppermute | solution.py:73
  28.7 7.0 %collective-permute-start.3 = (bf16[32,3072]{1,0:T(8,128)(2,1)S(1)}, bf16[32,3072]{1,0:T(8,128)(2,1)S(1)}, u32[]{:S(2)}, u32[]{:S(2)}) collective-permute-start(bf16[32,3072]{1,0:T(8,128)(2,1)S(1)} %collective-permute-done.2.refs_0_), channel_id=1, source_target_pairs={{0,2},{2,4},{4,6},{6,7},{7,5},{5,3},{3,1},{1,0},{8,10},{10,12},{12... | collective-permute-start | bytes 589832 | tf_op jit(solution)/shard_map/ppermute | solution.py:77
  28.8 8.0 %collective-permute-start.13 = (bf16[32,3072]{1,0:T(8,128)(2,1)S(1)}, bf16[32,3072]{1,0:T(8,128)(2,1)S(1)}, u32[]{:S(2)}, u32[]{:S(2)}) collective-permute-start(bf16[32,3072]{1,0:T(8,128)(2,1)S(1)} %collective-permute-done.12.refs_11_.refs_3_), channel_id=1, source_target_pairs={{2,0},{4,2},{6,4},{7,6},{5,7},{3,5},{1,3},{0,1},{10,8},{12,10},{14... | collective-permute-start | bytes 589832 | tf_op jit(solution)/shard_map/ppermute | solution.py:78
  37.7 1.5 %collective-permute-start.14 = (bf16[2,128,128]{2,1,0:T(8,128)(2,1)S(1)}, bf16[2,128,128]{2,1,0:T(8,128)(2,1)S(1)}, u32[]{:S(2)}, u32[]{:S(2)}) collective-permute-start(bf16[2,128,128]{2,1,0:T(8,128)(2,1)S(1)} %get-tuple-element.53.one_ref), channel_id=1, source_target_pairs={{0,8},{8,0},{16,24},{24,16},{1,9},{9,1},{17,25},{25,17},{2,10},{10... | collective-permute-start | bytes 196616 | tf_op jit(solution)/shard_map/ppermute | solution.py:405
  38.7 2.2 %collective-permute-start.16 = (bf16[2,128,128]{2,1,0:T(8,128)(2,1)S(1)}, bf16[2,128,128]{2,1,0:T(8,128)(2,1)S(1)}, u32[]{:S(2)}, u32[]{:S(2)}) collective-permute-start(bf16[2,128,128]{2,1,0:T(8,128)(2,1)S(1)} %get-tuple-element.54.one_ref), channel_id=1, source_target_pairs={{0,8},{8,0},{16,24},{24,16},{1,9},{9,1},{17,25},{25,17},{2,10},{10... | collective-permute-start | bytes 196616 | tf_op jit(solution)/shard_map/ppermute | solution.py:405
  39.2 5.9 %collective-permute-start.15 = (bf16[2,128,128]{2,1,0:T(8,128)(2,1)S(1)}, bf16[2,128,128]{2,1,0:T(8,128)(2,1)S(1)}, u32[]{:S(2)}, u32[]{:S(2)}) collective-permute-start(bf16[2,128,128]{2,1,0:T(8,128)(2,1)S(1)} %add_states.2.refs_0_), channel_id=1, source_target_pairs={{0,16},{8,24},{16,0},{24,8},{1,17},{9,25},{17,1},{25,9},{2,18},{10... | collective-permute-start | bytes 196616 | tf_op jit(solution)/shard_map/ppermute | solution.py:405
  40.8 4.3 %collective-permute-start.17 = (bf16[2,128,128]{2,1,0:T(8,128)(2,1)S(1)}, bf16[2,128,128]{2,1,0:T(8,128)(2,1)S(1)}, u32[]{:S(2)}, u32[]{:S(2)}) collective-permute-start(bf16[2,128,128]{2,1,0:T(8,128)(2,1)S(1)} %add_states.3), channel_id=1, source_target_pairs={{0,16},{8,24},{16,0},{24,8},{1,17},{9,25},{17,1},{25,9},{2,18},{10... | collective-permute-start | bytes 196616 | tf_op jit(solution)/shard_map/ppermute | solution.py:405
  41.7 3.5 %slice-start.5 = ((s8[6291456]{0:T(1024)(128)(4,1)}), s8[4194304]{0:T(1024)(128)(4,1)S(1)}, s32[]{:S(2)}) async-start(s8[6291456]{0:T(1024)(128)(4,1)} %bitcast.3), calls=%async_computation.5 | async-start | bytes 8388608
  41.7 3.5 %slice-start.6 = ((s8[6291456]{0:T(1024)(128)(4,1)}), s8[2097152]{0:T(1024)(128)(4,1)S(1)}, s32[]{:S(2)}) async-start(s8[6291456]{0:T(1024)(128)(4,1)} %bitcast.3), calls=%async_computation.6 | async-start | bytes 4194304
  41.7 3.5 %copy-start = (f32[4,128,128]{2,1,0:T(8,128)S(1)}, f32[4,128,128]{2,1,0:T(8,128)}, u32[]{:S(2)}) copy-start(f32[4,128,128]{2,1,0:T(8,128)} %initial_ref.3) | copy-start | bytes 786436
  41.7 3.5 %copy-start.1 = (f32[512]{0:T(512)S(1)}, f32[512]{0:T(512)}, u32[]{:S(2)}) copy-start(f32[512]{0:T(512)} %param.8) | copy-start | bytes 6148
  46.7 6.3 %collective-permute-start.28 = (bf16[32,3072]{1,0:T(8,128)(2,1)S(1)}, bf16[32,3072]{1,0:T(8,128)(2,1)S(1)}, u32[]{:S(2)}, u32[]{:S(2)}) collective-permute-start(bf16[32,3072]{1,0:T(8,128)(2,1)S(1)} %get-tuple-element.70), channel_id=1, source_target_pairs={{0,2},{2,4},{4,6},{6,7},{7,5},{5,3},{3,1},{1,0},{8,10},{10,12},{12... | collective-permute-start | bytes 589832 | tf_op jit(solution)/shard_map/ppermute | solution.py:369
  47.2 6.9 %collective-permute-start.24 = (bf16[32,3072]{1,0:T(8,128)(2,1)S(1)}, bf16[32,3072]{1,0:T(8,128)(2,1)S(1)}, u32[]{:S(2)}, u32[]{:S(2)}) collective-permute-start(bf16[32,3072]{1,0:T(8,128)(2,1)S(1)} %get-tuple-element.66), channel_id=1, source_target_pairs={{2,0},{4,2},{6,4},{7,6},{5,7},{3,5},{1,3},{0,1},{10,8},{12,10},{14... | collective-permute-start | bytes 589832 | tf_op jit(solution)/shard_map/ppermute | solution.py:369
  50.6 7.9 %collective-permute-start.21 = (bf16[32,3072]{1,0:T(8,128)(2,1)S(1)}, bf16[32,3072]{1,0:T(8,128)(2,1)S(1)}, u32[]{:S(2)}, u32[]{:S(2)}) collective-permute-start(bf16[32,3072]{1,0:T(8,128)(2,1)S(1)} %get-tuple-element.62), channel_id=1, source_target_pairs={{2,0},{4,2},{6,4},{7,6},{5,7},{3,5},{1,3},{0,1},{10,8},{12,10},{14... | collective-permute-start | bytes 589832 | tf_op jit(solution)/shard_map/ppermute | solution.py:369
  52.3 7.9 %collective-permute-start.18 = (bf16[32,3072]{1,0:T(8,128)(2,1)S(1)}, bf16[32,3072]{1,0:T(8,128)(2,1)S(1)}, u32[]{:S(2)}, u32[]{:S(2)}) collective-permute-start(bf16[32,3072]{1,0:T(8,128)(2,1)S(1)} %get-tuple-element.59), channel_id=1, source_target_pairs={{0,2},{2,4},{4,6},{6,7},{7,5},{5,3},{3,1},{1,0},{8,10},{10,12},{12... | collective-permute-start | bytes 589832 | tf_op jit(solution)/shard_map/ppermute | solution.py:369
  53.0 10.4 %collective-permute-start.29 = (bf16[32,3072]{1,0:T(8,128)(2,1)S(1)}, bf16[32,3072]{1,0:T(8,128)(2,1)S(1)}, u32[]{:S(2)}, u32[]{:S(2)}) collective-permute-start(bf16[32,3072]{1,0:T(8,128)(2,1)S(1)} %add_step.17), channel_id=1, source_target_pairs={{0,2},{2,4},{4,6},{6,7},{7,5},{5,3},{3,1},{1,0},{8,10},{10,12},{12... | collective-permute-start | bytes 589832 | tf_op jit(solution)/shard_map/ppermute | solution.py:369
  54.2 9.6 %collective-permute-start.25 = (bf16[32,3072]{1,0:T(8,128)(2,1)S(1)}, bf16[32,3072]{1,0:T(8,128)(2,1)S(1)}, u32[]{:S(2)}, u32[]{:S(2)}) collective-permute-start(bf16[32,3072]{1,0:T(8,128)(2,1)S(1)} %add_step.14), channel_id=1, source_target_pairs={{2,0},{4,2},{6,4},{7,6},{5,7},{3,5},{1,3},{0,1},{10,8},{12,10},{14... | collective-permute-start | bytes 589832 | tf_op jit(solution)/shard_map/ppermute | solution.py:369
  58.6 8.4 %collective-permute-start.22 = (bf16[32,3072]{1,0:T(8,128)(2,1)S(1)}, bf16[32,3072]{1,0:T(8,128)(2,1)S(1)}, u32[]{:S(2)}, u32[]{:S(2)}) collective-permute-start(bf16[32,3072]{1,0:T(8,128)(2,1)S(1)} %add_step.12), channel_id=1, source_target_pairs={{2,0},{4,2},{6,4},{7,6},{5,7},{3,5},{1,3},{0,1},{10,8},{12,10},{14... | collective-permute-start | bytes 589832 | tf_op jit(solution)/shard_map/ppermute | solution.py:369
  60.3 8.4 %collective-permute-start.19 = (bf16[32,3072]{1,0:T(8,128)(2,1)S(1)}, bf16[32,3072]{1,0:T(8,128)(2,1)S(1)}, u32[]{:S(2)}, u32[]{:S(2)}) collective-permute-start(bf16[32,3072]{1,0:T(8,128)(2,1)S(1)} %add_step.10), channel_id=1, source_target_pairs={{0,2},{2,4},{4,6},{6,7},{7,5},{5,3},{3,1},{1,0},{8,10},{10,12},{12... | collective-permute-start | bytes 589832 | tf_op jit(solution)/shard_map/ppermute | solution.py:369
  63.5 8.4 %collective-permute-start.30 = (bf16[32,3072]{1,0:T(8,128)(2,1)S(1)}, bf16[32,3072]{1,0:T(8,128)(2,1)S(1)}, u32[]{:S(2)}, u32[]{:S(2)}) collective-permute-start(bf16[32,3072]{1,0:T(8,128)(2,1)S(1)} %add_step.18), channel_id=1, source_target_pairs={{0,2},{2,4},{4,6},{6,7},{7,5},{5,3},{3,1},{1,0},{8,10},{10,12},{12... | collective-permute-start | bytes 589832 | tf_op jit(solution)/shard_map/ppermute | solution.py:369
  63.8 8.4 %collective-permute-start.26 = (bf16[32,3072]{1,0:T(8,128)(2,1)S(1)}, bf16[32,3072]{1,0:T(8,128)(2,1)S(1)}, u32[]{:S(2)}, u32[]{:S(2)}) collective-permute-start(bf16[32,3072]{1,0:T(8,128)(2,1)S(1)} %add_step.15), channel_id=1, source_target_pairs={{2,0},{4,2},{6,4},{7,6},{5,7},{3,5},{1,3},{0,1},{10,8},{12,10},{14... | collective-permute-start | bytes 589832 | tf_op jit(solution)/shard_map/ppermute | solution.py:369
  67.0 8.9 %collective-permute-start.23 = (bf16[32,3072]{1,0:T(8,128)(2,1)S(1)}, bf16[32,3072]{1,0:T(8,128)(2,1)S(1)}, u32[]{:S(2)}, u32[]{:S(2)}) collective-permute-start(bf16[32,3072]{1,0:T(8,128)(2,1)S(1)} %add_step.13), channel_id=1, source_target_pairs={{2,0},{4,2},{6,4},{7,6},{5,7},{3,5},{1,3},{0,1},{10,8},{12,10},{14... | collective-permute-start | bytes 589832 | tf_op jit(solution)/shard_map/ppermute | solution.py:369
  68.7 7.9 %collective-permute-start.20 = (bf16[32,3072]{1,0:T(8,128)(2,1)S(1)}, bf16[32,3072]{1,0:T(8,128)(2,1)S(1)}, u32[]{:S(2)}, u32[]{:S(2)}) collective-permute-start(bf16[32,3072]{1,0:T(8,128)(2,1)S(1)} %add_step.11), channel_id=1, source_target_pairs={{0,2},{2,4},{4,6},{6,7},{7,5},{5,3},{3,1},{1,0},{8,10},{10,12},{12... | collective-permute-start | bytes 589832 | tf_op jit(solution)/shard_map/ppermute | solution.py:369
  71.9 6.8 %collective-permute-start.31 = (bf16[32,3072]{1,0:T(8,128)(2,1)S(1)}, bf16[32,3072]{1,0:T(8,128)(2,1)S(1)}, u32[]{:S(2)}, u32[]{:S(2)}) collective-permute-start(bf16[32,3072]{1,0:T(8,128)(2,1)S(1)} %add_step.19), channel_id=1, source_target_pairs={{0,2},{2,4},{4,6},{6,7},{7,5},{5,3},{3,1},{1,0},{8,10},{10,12},{12... | collective-permute-start | bytes 589832 | tf_op jit(solution)/shard_map/ppermute | solution.py:369
  72.3 6.5 %collective-permute-start.27 = (bf16[32,3072]{1,0:T(8,128)(2,1)S(1)}, bf16[32,3072]{1,0:T(8,128)(2,1)S(1)}, u32[]{:S(2)}, u32[]{:S(2)}) collective-permute-start(bf16[32,3072]{1,0:T(8,128)(2,1)S(1)} %add_step.16), channel_id=1, source_target_pairs={{2,0},{4,2},{6,4},{7,6},{5,7},{3,5},{1,3},{0,1},{10,8},{12,10},{14... | collective-permute-start | bytes 589832 | tf_op jit(solution)/shard_map/ppermute | solution.py:369
